TPU v7x, 32 devices: a whole 2x2x4 slice. The times are simulated.
32 devices in a mesh: groups: 2 (over x), wide: 8 (over z, y), narrow: 2 (over core).
Axes of the slice: x: 2, y: 2, z: 4, core: 2. Of those that a mesh axis runs over, the one named last changes fastest.
Arguments:
- tokens: bfloat16 [256, 8192], P(('groups', 'wide'), 'narrow'), parts along dimension 0, may hold values from -6 to 6
- gate_weight: bfloat16 [8192, 4096], P('narrow', 'wide'), may hold values from -0.0625 to 0.0625
- up_weight: bfloat16 [8192, 4096], P('narrow', 'wide'), may hold values from -0.0625 to 0.0625
- down_weight: bfloat16 [4096, 8192], P('wide', 'narrow'), may hold values from -0.09375 to 0.09375
Outputs:
- mixed: bfloat16 [256, 8192], P(('groups', 'wide'), 'narrow'), parts along dimension 0
There are 2 independent parts, one for each index of `groups`. A program takes and returns all parts, laid end to end along the dimension named above; an argument that names none is the same for every part. Nothing has to cross between parts.
All inputs are finite; a program needn't handle non-finite values.
Results may differ from a plain program's by a relative error of at most 0.0049.
Values may be sent and summed in bfloat16 or wider, within the bound.
No kernel may reach another device: no remote copies, remote signals or barrier semaphores. Data moves between devices by JAX's collectives and lax.ppermute only.
A program may use at most 64 MiB of HBM per device.

v0:
```python
import jax
import jax.numpy as jnp
from jax import lax
from jax.sharding import PartitionSpec as P


def local(tokens, gate_weight, up_weight, down_weight):
    rows_piece = lax.all_gather(tokens, "wide", axis=0, tiled=True)
    gate_part = jnp.dot(rows_piece, gate_weight, preferred_element_type=jnp.float32)
    up_part = jnp.dot(rows_piece, up_weight, preferred_element_type=jnp.float32)
    partial_value = jnp.stack([gate_part, up_part], axis=1)
    summed = lax.psum(partial_value, "narrow")
    hidden = (jax.nn.silu(summed[:, 0]) * summed[:, 1]).astype(jnp.bfloat16)
    mixed_out = lax.psum_scatter(
        jnp.dot(hidden, down_weight, preferred_element_type=jnp.float32),
        "wide",
        scatter_dimension=0,
        tiled=True,
    )
    return mixed_out.astype(jnp.bfloat16)


def solution(mesh):
    return jax.shard_map(
        local,
        mesh=mesh,
        in_specs=(
            P(("groups", "wide"), "narrow"),
            P("narrow", "wide"),
            P("narrow", "wide"),
            P("wide", "narrow"),
        ),
        out_specs=P(("groups", "wide"), "narrow"),
        check_vma=False,
    )
```

profile of v0, /device:TPU:0, one launch (start us, length us, event | category | flops | bytes accessed | tf_op | source)
XLA Modules:
  0.0 157.4 jit_solution(6204122818148850296)
XLA Ops:
  6.5 0.0 all-gather.2.cloned.1.call-start
  6.5 0.7 all-gather.2.cloned.1.call-update
  7.3 0.0 all-reduce.2.cloned.1.call-start
  7.3 45.1 %all-gather.2.cloned.1.call-done = bf16[128,4096]{1,0:T(8,128)(2,1)} async-done(((bf16[16,4096]{1,0:T(8,128)(2,1)}), bf16[128,4096]{1,0:T(8,128)(2,1)}) %all-gather.2.cloned.1.call-update) | async-done | bytes 1048592 | tf_op jit(solution)/shard_map/all_gather | solution.py:8
  52.4 0.0 copy-start
  52.4 0.0 copy-start.1
  52.4 3.4 %convolution_bitcast_fusion = f32[128,1,512]{2,0,1:T(8,128)S(1)} fusion(bf16[128,4096]{1,0:T(8,128)(2,1)} %all-gather.2.cloned.1.call-done, bf16[4096,512]{1,0:T(8,128)(2,1)} %param.6), kind=kOutput, calls=%fused_computation | convolution fusion | flops 536870912 | bytes 5505024 | tf_op jit(solution)/shard_map/dot_general | solution.py:10
  55.7 0.4 copy-done
  56.1 0.3 copy-done.1
  56.4 0.7 convolution_bitcast_fusion.1
  57.1 0.8 pad_maximum_fusion
  58.0 0.0 all-reduce.2.cloned.1.call-update
  58.0 0.0 reduce-scatter.2.cloned.1.call-start
  58.0 17.6 %all-reduce.2.cloned.1.call-done = f32[128,2,512]{2,0,1:T(8,128)} async-done(((f32[128,2,512]{2,0,1:T(8,128)}), f32[128,2,512]{2,0,1:T(8,128)}) %all-reduce.2.cloned.1.call-update) | async-done | bytes 524304 | tf_op jit(solution)/shard_map/psum | solution.py:12
  75.6 4.4 %fusion.2 = f32[128,4096]{1,0:T(8,128)} fusion(bf16[512,4096]{1,0:T(8,128)(2,1)} %param.7, f32[128,2,512]{2,0,1:T(8,128)} %all-reduce.2.cloned.1.call-done), kind=kOutput, calls=%fused_computation.7 | convolution fusion | flops 537264128 | bytes 6815744 | tf_op jit(solution)/shard_map/dot_general | solution.py:15
  80.1 0.0 reduce-scatter.2.cloned.1.call-update
  80.1 69.2 %reduce-scatter.2.cloned.1.call-done = f32[16,4096]{1,0:T(8,128)} async-done(((f32[128,4096]{1,0:T(8,128)}), f32[16,4096]{1,0:T(8,128)}) %reduce-scatter.2.cloned.1.call-update) | async-done | bytes 262160 | tf_op jit(solution)/shard_map/reduce_scatter | solution.py:14
  149.3 1.6 %convert_element_type.7 = bf16[16,4096]{1,0:T(8,128)(2,1)} convert(f32[16,4096]{1,0:T(8,128)} %reduce-scatter.2.cloned.1.call-done) | non-fusion elementwise | flops 65536 | bytes 393216 | tf_op jit(solution)/shard_map/convert_element_type | solution.py:20
Async XLA Ops:
  6.5 45.8 %all-gather.2.cloned.1.call-start = ((), (), s32[]{:S(2)}) async-start(), calls=%async_computation.1 | async-start | bytes 1179648 | tf_op jit(solution)/shard_map/all_gather | solution.py:8
  7.3 68.4 %all-reduce.2.cloned.1.call-start = ((), (), s32[]{:S(2)}) async-start(), calls=%async_computation.2 | async-start | bytes 1048576 | tf_op jit(solution)/shard_map/psum | solution.py:12
  52.4 3.7 %copy-start = (bf16[4096,512]{1,0:T(8,128)(2,1)S(1)}, bf16[4096,512]{1,0:T(8,128)(2,1)}, u32[]{:S(2)}) copy-start(bf16[4096,512]{1,0:T(8,128)(2,1)} %param.5) | copy-start | bytes 12582916
  52.4 4.0 %copy-start.1 = (bf16[128,4096]{1,0:T(8,128)(2,1)S(1)}, bf16[128,4096]{1,0:T(8,128)(2,1)}, u32[]{:S(2)}) copy-start(bf16[128,4096]{1,0:T(8,128)(2,1)} %all-gather.2.cloned.1.call-done) | copy-start | bytes 3145732
  58.0 91.3 %reduce-scatter.2.cloned.1.call-start = ((), (), s32[]{:S(2)}) async-start(), calls=%async_computation.3 | async-start | bytes 2359296 | tf_op jit(solution)/shard_map/reduce_scatter | solution.py:14
Sparse Core Ops, SparseCore 0:
  9.5 42.8 all-gather.1
  58.1 17.4 all-reduce.1
  80.2 69.0 reduce-scatter.1
where the time goes:
time: 158 us; the launch traced here: 157 us
  waiting for transfers between devices  133 us (84%)
  between operations  13.1 us (8%)
  matrix products  8.52 us (5%)
  other arithmetic  2.44 us (2%)
    reduce_scatter x1, waiting for transfers between devices, local(): lax.psum_scatter(jnp.dot(hidden, down_weight, preferred_element_type=jnp....  69.2 us
    all_gather x1, waiting for transfers between devices, local(): rows_piece = lax.all_gather(tokens, 'wide', axis=0, tiled=True)  45.1 us
    psum x1, waiting for transfers between devices, local(): summed = lax.psum(partial_value, 'narrow')  17.6 us
    dot_general x1, matrix products, local(): jnp.dot(hidden, down_weight, preferred_element_type=jnp.float32)  4.44 us
    dot_general x1, matrix products, local(): up_part = jnp.dot(rows_piece, up_weight, preferred_element_type=jnp.float32)  3.37 us
  transfers between devices with their start and end apart: 3, of which 3 were waited for; matrix products, arithmetic and copies ran while one was open for 0% of the time, Pallas kernels for 0%

commit v1 on v0

v1 whole, which is shorter than its diff:
```python
import jax
import jax.numpy as jnp
from jax import lax
from jax.sharding import PartitionSpec as P

F32 = jnp.float32
BF16 = jnp.bfloat16


def make_local(wide, narrow):
    inner = 2 if wide % 2 == 0 else 1
    outer = wide // inner

    def along_outer(value, step):
        pairs = [(i, (i + step * inner) % wide) for i in range(wide)]
        return lax.ppermute(value, "wide", pairs)

    def along_inner(value):
        pairs = [(i, i ^ 1) for i in range(wide)]
        return lax.ppermute(value, "wide", pairs)

    def across_cores(value):
        pairs = [(i, (i + 1) % narrow) for i in range(narrow)]
        return lax.ppermute(value, "narrow", pairs)

    def local(tokens, gate_weight, up_weight, down_weight):
        rows = tokens.shape[0]
        mine = [tokens] + [along_outer(tokens, k) for k in range(1, outer)]
        theirs = [along_inner(block) for block in mine] if inner == 2 else []
        all_rows = jnp.concatenate(mine + theirs, axis=0)
        gate_part = jnp.dot(all_rows, gate_weight, preferred_element_type=F32)
        up_part = jnp.dot(all_rows, up_weight, preferred_element_type=F32)
        gate_sum = gate_part + across_cores(gate_part)
        up_sum = up_part + across_cores(up_part)
        hidden = (jax.nn.silu(gate_sum) * up_sum).astype(BF16)
        partial = jnp.dot(hidden, down_weight, preferred_element_type=F32)
        blocks = [partial[k * rows:(k + 1) * rows] for k in range(wide)]
        if inner == 2:
            paired = [
                blocks[k] + along_inner(blocks[outer + k].astype(BF16)).astype(F32)
                for k in range(outer)
            ]
        else:
            paired = blocks
        total = paired[0]
        for k in range(1, outer):
            total = total + along_outer(paired[k].astype(BF16), -k).astype(F32)
        return total.astype(BF16)

    return local


def solution(mesh):
    return jax.shard_map(
        make_local(mesh.shape["wide"], mesh.shape["narrow"]),
        mesh=mesh,
        in_specs=(
            P(("groups", "wide"), "narrow"),
            P("narrow", "wide"),
            P("narrow", "wide"),
            P("wide", "narrow"),
        ),
        out_specs=P(("groups", "wide"), "narrow"),
        check_vma=False,
    )
```

time: 158 us -> 55.7 us (0.35)
  waiting for transfers between devices: 133 us -> 31 us
  starting transfers between devices: 0.08 us -> 17.9 us
  between operations: 13.1 us -> 0.15 us
  matrix products: 8.52 us -> 4.58 us
  other arithmetic: 2.44 us -> 0.84 us
    reduce_scatter x1 -> x0, waiting for transfers between devices: 69.2 us -> none  [local(): lax.psum_scatter(jnp.dot(hidden, down_weight, preferred_element_type=jnp....]
    all_gather x1 -> x0, waiting for transfers between devices: 45.1 us -> none  [local(): rows_piece = lax.all_gather(tokens, 'wide', axis=0, tiled=True)]
    ppermute x0 -> x16, waiting for transfers between devices: none -> 31 us  [the longest x6 16.3 us: along_outer(): return lax.ppermute(value, 'wide', pairs)]
    ppermute x0 -> x16, starting transfers between devices: none -> 17.9 us  [the longest x8 9.18 us: along_inner(): return lax.ppermute(value, 'wide', pairs)]
    psum x1 -> x0, waiting for transfers between devices: 17.6 us -> none  [local(): summed = lax.psum(partial_value, 'narrow')]
    dot_general x3, matrix products: 8.52 us -> 4.58 us  [the longest x1 3.12 us: local(): up_part = jnp.dot(all_rows, up_weight, preferred_element_type=F32)]
  transfers between devices with their start and end apart: 3 -> 16, of which waited for: 3 -> 11; matrix products, arithmetic and copies ran while one was open for 0% -> 2% of each run, Pallas kernels for 0% -> 0%
where the time goes in v1:
time: 55.7 us; the launch traced here: 55.6 us
  waiting for transfers between devices  31 us (56%)
  starting transfers between devices  17.9 us (32%)
  matrix products  4.58 us (8%)
  local copies, waits for them, and re-layouts  1.07 us (2%)
  other arithmetic  0.84 us (2%)
    ppermute x6, waiting for transfers between devices, along_outer(): return lax.ppermute(value, 'wide', pairs)  16.3 us
    ppermute x8, waiting for transfers between devices, along_inner(): return lax.ppermute(value, 'wide', pairs)  13.4 us
    ppermute x8, starting transfers between devices, along_inner(): return lax.ppermute(value, 'wide', pairs)  9.18 us
    ppermute x6, starting transfers between devices, along_outer(): return lax.ppermute(value, 'wide', pairs)  8.18 us
    dot_general x1, matrix products, local(): up_part = jnp.dot(all_rows, up_weight, preferred_element_type=F32)  3.12 us
    ppermute x2, waiting for transfers between devices, across_cores(): return lax.ppermute(value, 'narrow', pairs)  1.4 us
  transfers between devices with their start and end apart: 16, of which 11 were waited for; matrix products, arithmetic and copies ran while one was open for 2% of the time, Pallas kernels for 0%

profile of v1, /device:TPU:0, one launch (start us, length us, event | category | flops | bytes accessed | tf_op | source)
XLA Modules:
  0.0 55.6 jit_solution(16849230729330915145)
XLA Ops:
  0.0 0.0 copy-start
  0.0 5.0 %collective-permute-start.2 = (bf16[16,4096]{1,0:T(8,128)(2,1)}, bf16[16,4096]{1,0:T(8,128)(2,1)S(1)}, u32[]{:S(2)}, u32[]{:S(2)}) collective-permute-start(bf16[16,4096]{1,0:T(8,128)(2,1)} %param.4), channel_id=1, source_target_pairs={{0,12},{2,14},{4,0},{6,2},{8,4},{10,6},{12,8},{14,10},{1,13},{3,15... | collective-permute-start | bytes 393224 | tf_op jit(solution)/shard_map/ppermute | solution.py:16
  5.1 0.0 collective-permute-start.1
  5.1 1.0 %collective-permute-start = (bf16[16,4096]{1,0:T(8,128)(2,1)}, bf16[16,4096]{1,0:T(8,128)(2,1)S(1)}, u32[]{:S(2)}, u32[]{:S(2)}) collective-permute-start(bf16[16,4096]{1,0:T(8,128)(2,1)} %param.4), channel_id=1, source_target_pairs={{0,4},{2,6},{4,8},{6,10},{8,12},{10,14},{12,0},{14,2},{1,5},{3,7},... | collective-permute-start | bytes 393224 | tf_op jit(solution)/shard_map/ppermute | solution.py:16
  6.1 1.5 %collective-permute-start.3 = (bf16[16,4096]{1,0:T(8,128)(2,1)}, bf16[16,4096]{1,0:T(8,128)(2,1)S(1)}, u32[]{:S(2)}, u32[]{:S(2)}) collective-permute-start(bf16[16,4096]{1,0:T(8,128)(2,1)} %param.4), channel_id=1, source_target_pairs={{0,2},{2,0},{4,6},{6,4},{8,10},{10,8},{12,14},{14,12},{1,3},{3,1},... | collective-permute-start | bytes 393224 | tf_op jit(solution)/shard_map/ppermute | solution.py:20
  7.6 0.9 %constant_dynamic-update-slice_fusion.7 = bf16[128,4096]{1,0:T(8,128)(2,1)S(1)} fusion(bf16[16,4096]{1,0:T(8,128)(2,1)} %param.4), kind=kLoop, calls=%fused_computation.21 | loop fusion | bytes 262144
  8.5 0.7 %collective-permute-done.2 = bf16[16,4096]{1,0:T(8,128)(2,1)S(1)} collective-permute-done((bf16[16,4096]{1,0:T(8,128)(2,1)}, bf16[16,4096]{1,0:T(8,128)(2,1)S(1)}, u32[]{:S(2)}, u32[]{:S(2)}) %collective-permute-start.2) | collective-permute-done | bytes 131104 | tf_op jit(solution)/shard_map/ppermute | solution.py:16
  9.3 1.5 %collective-permute-start.6 = (bf16[16,4096]{1,0:T(8,128)(2,1)S(1)}, bf16[16,4096]{1,0:T(8,128)(2,1)S(1)}, u32[]{:S(2)}, u32[]{:S(2)}) collective-permute-start(bf16[16,4096]{1,0:T(8,128)(2,1)S(1)} %collective-permute-done.2), channel_id=1, source_target_pairs={{0,2},{2,0},{4,6},{6,4},{8,10},{10,8},{12,14},{14,12},{1,3},{3,1},... | collective-permute-start | bytes 393224 | tf_op jit(solution)/shard_map/ppermute | solution.py:20
  10.8 5.7 %collective-permute-done.1 = bf16[16,4096]{1,0:T(8,128)(2,1)S(1)} collective-permute-done((bf16[16,4096]{1,0:T(8,128)(2,1)}, bf16[16,4096]{1,0:T(8,128)(2,1)S(1)}, u32[]{:S(2)}, u32[]{:S(2)}) %collective-permute-start.1) | collective-permute-done | bytes 131104 | tf_op jit(solution)/shard_map/ppermute | solution.py:16
  16.5 1.5 %collective-permute-start.5 = (bf16[16,4096]{1,0:T(8,128)(2,1)S(1)}, bf16[16,4096]{1,0:T(8,128)(2,1)S(1)}, u32[]{:S(2)}, u32[]{:S(2)}) collective-permute-start(bf16[16,4096]{1,0:T(8,128)(2,1)S(1)} %collective-permute-done.1), channel_id=1, source_target_pairs={{0,2},{2,0},{4,6},{6,4},{8,10},{10,8},{12,14},{14,12},{1,3},{3,1},... | collective-permute-start | bytes 393224 | tf_op jit(solution)/shard_map/ppermute | solution.py:20
  18.0 0.0 collective-permute-done
  18.0 0.5 collective-permute-start.4
  18.5 0.0 collective-permute-done.3
  18.6 5.5 %collective-permute-done.4 = bf16[16,4096]{1,0:T(8,128)(2,1)S(1)} collective-permute-done((bf16[16,4096]{1,0:T(8,128)(2,1)S(1)}, bf16[16,4096]{1,0:T(8,128)(2,1)S(1)}, u32[]{:S(2)}, u32[]{:S(2)}) %collective-permute-start.4) | collective-permute-done | bytes 131104 | tf_op jit(solution)/shard_map/ppermute | solution.py:20
  24.0 0.0 collective-permute-done.5
  24.1 0.0 collective-permute-done.6
  24.1 0.0 copy-start.1
  24.1 3.1 %fusion.13 = f32[128,512]{1,0:T(8,128)S(1)} fusion(bf16[128,4096]{1,0:T(8,128)(2,1)S(1)} %constant_dynamic-update-slice_fusion, bf16[4096,512]{1,0:T(8,128)(2,1)} %param.6), kind=kOutput, calls=%fused_computation.26 | convolution fusion | flops 536870912 | bytes 5505024 | tf_op jit(solution)/shard_map/dot_general | solution.py:32
  27.2 0.0 copy-done
  27.2 0.7 %fusion.12 = f32[128,512]{1,0:T(8,128)S(1)} fusion(bf16[128,4096]{1,0:T(8,128)(2,1)S(1)} %constant_dynamic-update-slice_fusion, bf16[4096,512]{1,0:T(8,128)(2,1)S(1)} %copy-done), kind=kOutput, calls=%fused_computation.25 | convolution fusion | flops 536870912 | bytes 5505024 | tf_op jit(solution)/shard_map/dot_general | solution.py:31
  28.0 0.1 collective-permute-start.7
  28.1 0.5 collective-permute-start.8
  28.5 1.0 %collective-permute-done.7 = f32[128,512]{1,0:T(8,128)S(1)} collective-permute-done((f32[128,512]{1,0:T(8,128)S(1)}, f32[128,512]{1,0:T(8,128)S(1)}, u32[]{:S(2)}, u32[]{:S(2)}) %collective-permute-start.7) | collective-permute-done | bytes 262176 | tf_op jit(solution)/shard_map/ppermute | solution.py:24
  29.6 0.4 collective-permute-done.8
  29.9 0.0 copy-done.1
  30.0 0.7 %fusion.11 = (bf16[128,4096]{1,0:T(8,128)(2,1)S(1)}, f32[128,4096]{1,0:T(8,128)S(1)}) fusion(bf16[512,4096]{1,0:T(8,128)(2,1)S(1)} %copy-done.1, f32[128,512]{1,0:T(8,128)S(1)} %fusion.13, f32[128,512]{1,0:T(8,128)S(1)} %collective-permute-done.8, f32[128,512]{1,0:T(8,128)S(1)} %fusion.12, f32[128,512]{1,0:T(8,128)S(1)} %collective-permute-done.7), kind=kOutput, calls=%fused_computation.24 | convolution fusion | flops 537919488 | bytes 8388608 | tf_op jit(solution)/shard_map/dot_general | solution.py:36
  30.8 1.6 %collective-permute-start.14 = (bf16[16,4096]{1,0:T(8,128)(2,1)S(1)}, bf16[16,4096]{1,0:T(8,128)(2,1)S(1)}, u32[]{:S(2)}, u32[]{:S(2)}) collective-permute-start(bf16[16,4096]{1,0:T(8,128)(2,1)S(1)} %get-tuple-element.9), channel_id=1, source_target_pairs={{0,2},{2,0},{4,6},{6,4},{8,10},{10,8},{12,14},{14,12},{1,3},{3,1},... | collective-permute-start | bytes 393224 | tf_op jit(solution)/shard_map/ppermute | solution.py:20
  32.3 0.5 collective-permute-start.12
  32.8 1.5 %collective-permute-start.10 = (bf16[16,4096]{1,0:T(8,128)(2,1)S(1)}, bf16[16,4096]{1,0:T(8,128)(2,1)S(1)}, u32[]{:S(2)}, u32[]{:S(2)}) collective-permute-start(bf16[16,4096]{1,0:T(8,128)(2,1)S(1)} %get-tuple-element.11), channel_id=1, source_target_pairs={{0,2},{2,0},{4,6},{6,4},{8,10},{10,8},{12,14},{14,12},{1,3},{3,1},... | collective-permute-start | bytes 393224 | tf_op jit(solution)/shard_map/ppermute | solution.py:20
  34.4 0.5 collective-permute-start.9
  34.9 2.3 %collective-permute-done.14 = bf16[16,4096]{1,0:T(8,128)(2,1)S(1)} collective-permute-done((bf16[16,4096]{1,0:T(8,128)(2,1)S(1)}, bf16[16,4096]{1,0:T(8,128)(2,1)S(1)}, u32[]{:S(2)}, u32[]{:S(2)}) %collective-permute-start.14) | collective-permute-done | bytes 131104 | tf_op jit(solution)/shard_map/ppermute | solution.py:20
  37.2 2.8 %collective-permute-done.12 = bf16[16,4096]{1,0:T(8,128)(2,1)S(1)} collective-permute-done((bf16[16,4096]{1,0:T(8,128)(2,1)S(1)}, bf16[16,4096]{1,0:T(8,128)(2,1)S(1)}, u32[]{:S(2)}, u32[]{:S(2)}) %collective-permute-start.12) | collective-permute-done | bytes 131104 | tf_op jit(solution)/shard_map/ppermute | solution.py:20
  40.0 2.8 %collective-permute-done.10 = bf16[16,4096]{1,0:T(8,128)(2,1)S(1)} collective-permute-done((bf16[16,4096]{1,0:T(8,128)(2,1)S(1)}, bf16[16,4096]{1,0:T(8,128)(2,1)S(1)}, u32[]{:S(2)}, u32[]{:S(2)}) %collective-permute-start.10) | collective-permute-done | bytes 131104 | tf_op jit(solution)/shard_map/ppermute | solution.py:20
  42.8 0.1 fusion.2
  42.9 0.7 %collective-permute-start.11 = (bf16[16,4096]{1,0:T(8,128)(2,1)S(1)}, bf16[16,4096]{1,0:T(8,128)(2,1)S(1)}, u32[]{:S(2)}, u32[]{:S(2)}) collective-permute-start(bf16[16,4096]{1,0:T(8,128)(2,1)S(1)} %get-tuple-element.5), channel_id=1, source_target_pairs={{0,12},{2,14},{4,0},{6,2},{8,4},{10,6},{12,8},{14,10},{1,13},{3,15... | collective-permute-start | bytes 393224 | tf_op jit(solution)/shard_map/ppermute | solution.py:16
  43.5 1.4 %collective-permute-start.15 = (bf16[16,4096]{1,0:T(8,128)(2,1)S(1)}, bf16[16,4096]{1,0:T(8,128)(2,1)S(1)}, u32[]{:S(2)}, u32[]{:S(2)}) collective-permute-start(bf16[16,4096]{1,0:T(8,128)(2,1)S(1)} %get-tuple-element.6), channel_id=1, source_target_pairs={{0,4},{2,6},{4,8},{6,10},{8,12},{10,14},{12,0},{14,2},{1,5},{3,7},... | collective-permute-start | bytes 393224 | tf_op jit(solution)/shard_map/ppermute | solution.py:16
  45.0 0.0 collective-permute-start.13
  45.0 0.0 collective-permute-done.9
  45.0 6.3 %collective-permute-done.11 = bf16[16,4096]{1,0:T(8,128)(2,1)S(1)} collective-permute-done((bf16[16,4096]{1,0:T(8,128)(2,1)S(1)}, bf16[16,4096]{1,0:T(8,128)(2,1)S(1)}, u32[]{:S(2)}, u32[]{:S(2)}) %collective-permute-start.11) | collective-permute-done | bytes 131104 | tf_op jit(solution)/shard_map/ppermute | solution.py:16
  51.3 0.4 collective-permute-done.15
  51.7 3.2 %collective-permute-done.13 = bf16[16,4096]{1,0:T(8,128)(2,1)S(1)} collective-permute-done((bf16[16,4096]{1,0:T(8,128)(2,1)S(1)}, bf16[16,4096]{1,0:T(8,128)(2,1)S(1)}, u32[]{:S(2)}, u32[]{:S(2)}) %collective-permute-start.13) | collective-permute-done | bytes 131104 | tf_op jit(solution)/shard_map/ppermute | solution.py:16
  54.9 0.7 %fusion.6 = bf16[16,4096]{1,0:T(8,128)(2,1)} fusion(f32[128,4096]{1,0:T(8,128)S(1)} %get-tuple-element.13, bf16[16,4096]{1,0:T(8,128)(2,1)S(1)} %collective-permute-done.15, bf16[16,4096]{1,0:T(8,128)(2,1)S(1)} %collective-permute-done.13, bf16[16,4096]{1,0:T(8,128)(2,1)S(1)} %collective-permute-done.11, bf16[16,4096]{1,0:T(8,128)(2,1)S(1)} %collective-permute-done.9), kind=kLoop, calls=%fused_computation.10 | loop fusion | flops 589824 | bytes 917504 | tf_op jit(solution)/shard_map/convert_element_type | solution.py:48
  (8 shorter events, 0.1 us)
Async XLA Ops:
  0.0 27.2 %copy-start = (bf16[4096,512]{1,0:T(8,128)(2,1)S(1)}, bf16[4096,512]{1,0:T(8,128)(2,1)}, u32[]{:S(2)}) copy-start(bf16[4096,512]{1,0:T(8,128)(2,1)} %param.5) | copy-start | bytes 12582916
  0.0 9.3 %collective-permute-start.2 = (bf16[16,4096]{1,0:T(8,128)(2,1)}, bf16[16,4096]{1,0:T(8,128)(2,1)S(1)}, u32[]{:S(2)}, u32[]{:S(2)}) collective-permute-start(bf16[16,4096]{1,0:T(8,128)(2,1)} %param.4), channel_id=1, source_target_pairs={{0,12},{2,14},{4,0},{6,2},{8,4},{10,6},{12,8},{14,10},{1,13},{3,15... | collective-permute-start | bytes 393224 | tf_op jit(solution)/shard_map/ppermute | solution.py:16
  5.1 11.4 %collective-permute-start.1 = (bf16[16,4096]{1,0:T(8,128)(2,1)}, bf16[16,4096]{1,0:T(8,128)(2,1)S(1)}, u32[]{:S(2)}, u32[]{:S(2)}) collective-permute-start(bf16[16,4096]{1,0:T(8,128)(2,1)} %param.4), channel_id=1, source_target_pairs={{0,8},{2,10},{4,12},{6,14},{8,0},{10,2},{12,4},{14,6},{1,9},{3,11}... | collective-permute-start | bytes 393224 | tf_op jit(solution)/shard_map/ppermute | solution.py:16
  5.1 12.9 %collective-permute-start = (bf16[16,4096]{1,0:T(8,128)(2,1)}, bf16[16,4096]{1,0:T(8,128)(2,1)S(1)}, u32[]{:S(2)}, u32[]{:S(2)}) collective-permute-start(bf16[16,4096]{1,0:T(8,128)(2,1)} %param.4), channel_id=1, source_target_pairs={{0,4},{2,6},{4,8},{6,10},{8,12},{10,14},{12,0},{14,2},{1,5},{3,7},... | collective-permute-start | bytes 393224 | tf_op jit(solution)/shard_map/ppermute | solution.py:16
  6.1 12.5 %collective-permute-start.3 = (bf16[16,4096]{1,0:T(8,128)(2,1)}, bf16[16,4096]{1,0:T(8,128)(2,1)S(1)}, u32[]{:S(2)}, u32[]{:S(2)}) collective-permute-start(bf16[16,4096]{1,0:T(8,128)(2,1)} %param.4), channel_id=1, source_target_pairs={{0,2},{2,0},{4,6},{6,4},{8,10},{10,8},{12,14},{14,12},{1,3},{3,1},... | collective-permute-start | bytes 393224 | tf_op jit(solution)/shard_map/ppermute | solution.py:20
  9.3 14.8 %collective-permute-start.6 = (bf16[16,4096]{1,0:T(8,128)(2,1)S(1)}, bf16[16,4096]{1,0:T(8,128)(2,1)S(1)}, u32[]{:S(2)}, u32[]{:S(2)}) collective-permute-start(bf16[16,4096]{1,0:T(8,128)(2,1)S(1)} %collective-permute-done.2), channel_id=1, source_target_pairs={{0,2},{2,0},{4,6},{6,4},{8,10},{10,8},{12,14},{14,12},{1,3},{3,1},... | collective-permute-start | bytes 393224 | tf_op jit(solution)/shard_map/ppermute | solution.py:20
  16.5 7.6 %collective-permute-start.5 = (bf16[16,4096]{1,0:T(8,128)(2,1)S(1)}, bf16[16,4096]{1,0:T(8,128)(2,1)S(1)}, u32[]{:S(2)}, u32[]{:S(2)}) collective-permute-start(bf16[16,4096]{1,0:T(8,128)(2,1)S(1)} %collective-permute-done.1), channel_id=1, source_target_pairs={{0,2},{2,0},{4,6},{6,4},{8,10},{10,8},{12,14},{14,12},{1,3},{3,1},... | collective-permute-start | bytes 393224 | tf_op jit(solution)/shard_map/ppermute | solution.py:20
  18.0 6.0 %collective-permute-start.4 = (bf16[16,4096]{1,0:T(8,128)(2,1)S(1)}, bf16[16,4096]{1,0:T(8,128)(2,1)S(1)}, u32[]{:S(2)}, u32[]{:S(2)}) collective-permute-start(bf16[16,4096]{1,0:T(8,128)(2,1)S(1)} %collective-permute-done), channel_id=1, source_target_pairs={{0,2},{2,0},{4,6},{6,4},{8,10},{10,8},{12,14},{14,12},{1,3},{3,1},... | collective-permute-start | bytes 393224 | tf_op jit(solution)/shard_map/ppermute | solution.py:20
  24.1 5.8 %copy-start.1 = (bf16[512,4096]{1,0:T(8,128)(2,1)S(1)}, bf16[512,4096]{1,0:T(8,128)(2,1)}, u32[]{:S(2)}) copy-start(bf16[512,4096]{1,0:T(8,128)(2,1)} %param.7) | copy-start | bytes 12582916
  28.0 1.6 %collective-permute-start.7 = (f32[128,512]{1,0:T(8,128)S(1)}, f32[128,512]{1,0:T(8,128)S(1)}, u32[]{:S(2)}, u32[]{:S(2)}) collective-permute-start(f32[128,512]{1,0:T(8,128)S(1)} %fusion.12), channel_id=1, source_target_pairs={{0,1},{1,0},{2,3},{3,2},{4,5},{5,4},{6,7},{7,6},{8,9},{9,8},{10,11... | collective-permute-start | bytes 786440 | tf_op jit(solution)/shard_map/ppermute | solution.py:24
  28.1 1.9 %collective-permute-start.8 = (f32[128,512]{1,0:T(8,128)S(1)}, f32[128,512]{1,0:T(8,128)S(1)}, u32[]{:S(2)}, u32[]{:S(2)}) collective-permute-start(f32[128,512]{1,0:T(8,128)S(1)} %fusion.13), channel_id=1, source_target_pairs={{0,1},{1,0},{2,3},{3,2},{4,5},{5,4},{6,7},{7,6},{8,9},{9,8},{10,11... | collective-permute-start | bytes 786440 | tf_op jit(solution)/shard_map/ppermute | solution.py:24
  30.8 6.4 %collective-permute-start.14 = (bf16[16,4096]{1,0:T(8,128)(2,1)S(1)}, bf16[16,4096]{1,0:T(8,128)(2,1)S(1)}, u32[]{:S(2)}, u32[]{:S(2)}) collective-permute-start(bf16[16,4096]{1,0:T(8,128)(2,1)S(1)} %get-tuple-element.9), channel_id=1, source_target_pairs={{0,2},{2,0},{4,6},{6,4},{8,10},{10,8},{12,14},{14,12},{1,3},{3,1},... | collective-permute-start | bytes 393224 | tf_op jit(solution)/shard_map/ppermute | solution.py:20
  32.3 7.6 %collective-permute-start.12 = (bf16[16,4096]{1,0:T(8,128)(2,1)S(1)}, bf16[16,4096]{1,0:T(8,128)(2,1)S(1)}, u32[]{:S(2)}, u32[]{:S(2)}) collective-permute-start(bf16[16,4096]{1,0:T(8,128)(2,1)S(1)} %get-tuple-element.10), channel_id=1, source_target_pairs={{0,2},{2,0},{4,6},{6,4},{8,10},{10,8},{12,14},{14,12},{1,3},{3,1},... | collective-permute-start | bytes 393224 | tf_op jit(solution)/shard_map/ppermute | solution.py:20
  32.8 9.9 %collective-permute-start.10 = (bf16[16,4096]{1,0:T(8,128)(2,1)S(1)}, bf16[16,4096]{1,0:T(8,128)(2,1)S(1)}, u32[]{:S(2)}, u32[]{:S(2)}) collective-permute-start(bf16[16,4096]{1,0:T(8,128)(2,1)S(1)} %get-tuple-element.11), channel_id=1, source_target_pairs={{0,2},{2,0},{4,6},{6,4},{8,10},{10,8},{12,14},{14,12},{1,3},{3,1},... | collective-permute-start | bytes 393224 | tf_op jit(solution)/shard_map/ppermute | solution.py:20
  34.4 10.6 %collective-permute-start.9 = (bf16[16,4096]{1,0:T(8,128)(2,1)S(1)}, bf16[16,4096]{1,0:T(8,128)(2,1)S(1)}, u32[]{:S(2)}, u32[]{:S(2)}) collective-permute-start(bf16[16,4096]{1,0:T(8,128)(2,1)S(1)} %get-tuple-element.8), channel_id=1, source_target_pairs={{0,2},{2,0},{4,6},{6,4},{8,10},{10,8},{12,14},{14,12},{1,3},{3,1},... | collective-permute-start | bytes 393224 | tf_op jit(solution)/shard_map/ppermute | solution.py:20
  42.9 8.4 %collective-permute-start.11 = (bf16[16,4096]{1,0:T(8,128)(2,1)S(1)}, bf16[16,4096]{1,0:T(8,128)(2,1)S(1)}, u32[]{:S(2)}, u32[]{:S(2)}) collective-permute-start(bf16[16,4096]{1,0:T(8,128)(2,1)S(1)} %get-tuple-element.5), channel_id=1, source_target_pairs={{0,12},{2,14},{4,0},{6,2},{8,4},{10,6},{12,8},{14,10},{1,13},{3,15... | collective-permute-start | bytes 393224 | tf_op jit(solution)/shard_map/ppermute | solution.py:16
  43.5 8.2 %collective-permute-start.15 = (bf16[16,4096]{1,0:T(8,128)(2,1)S(1)}, bf16[16,4096]{1,0:T(8,128)(2,1)S(1)}, u32[]{:S(2)}, u32[]{:S(2)}) collective-permute-start(bf16[16,4096]{1,0:T(8,128)(2,1)S(1)} %get-tuple-element.6), channel_id=1, source_target_pairs={{0,4},{2,6},{4,8},{6,10},{8,12},{10,14},{12,0},{14,2},{1,5},{3,7},... | collective-permute-start | bytes 393224 | tf_op jit(solution)/shard_map/ppermute | solution.py:16
  45.0 9.9 %collective-permute-start.13 = (bf16[16,4096]{1,0:T(8,128)(2,1)S(1)}, bf16[16,4096]{1,0:T(8,128)(2,1)S(1)}, u32[]{:S(2)}, u32[]{:S(2)}) collective-permute-start(bf16[16,4096]{1,0:T(8,128)(2,1)S(1)} %get-tuple-element.7), channel_id=1, source_target_pairs={{0,8},{2,10},{4,12},{6,14},{8,0},{10,2},{12,4},{14,6},{1,9},{3,11}... | collective-permute-start | bytes 393224 | tf_op jit(solution)/shard_map/ppermute | solution.py:16

commit v2 on v1

--- a/solution.py
+++ b/solution.py
@@ -1,10 +1,25 @@
 import jax
 import jax.numpy as jnp
 from jax import lax
+from jax.experimental import pallas as pl
+from jax.experimental.pallas import tpu as pltpu
 from jax.sharding import PartitionSpec as P
 
 F32 = jnp.float32
 BF16 = jnp.bfloat16
+
+
+def pair_kernel(arrived_ref, own_ref, out_ref):
+    out_ref[...] = (own_ref[...] + arrived_ref[...].astype(F32)).astype(out_ref.dtype)
+
+
+def add_pair(arrived, own, dtype, flops):
+    return pl.pallas_call(
+        pair_kernel,
+        out_shape=jax.ShapeDtypeStruct(own.shape, dtype),
+        cost_estimate=pl.CostEstimate(flops=flops, bytes_accessed=0, transcendentals=0),
+        name="add_pair",
+    )(arrived, own)
 
 
 def make_local(wide, narrow):
@@ -35,17 +50,22 @@
         hidden = (jax.nn.silu(gate_sum) * up_sum).astype(BF16)
         partial = jnp.dot(hidden, down_weight, preferred_element_type=F32)
         blocks = [partial[k * rows:(k + 1) * rows] for k in range(wide)]
-        if inner == 2:
-            paired = [
-                blocks[k] + along_inner(blocks[outer + k].astype(BF16)).astype(F32)
-                for k in range(outer)
-            ]
-        else:
-            paired = blocks
-        total = paired[0]
-        for k in range(1, outer):
-            total = total + along_outer(paired[k].astype(BF16), -k).astype(F32)
-        return total.astype(BF16)
+        order = sorted(range(1, outer), key=lambda k: -min(k, outer - k)) + [0]
+        give = [blocks[outer + k].astype(BF16) for k in range(outer)] if inner == 2 else []
+        sent = []
+        for k in order:
+            if inner == 2 and k == 0 and sent:
+                give[0], sent[0] = lax.optimization_barrier((give[0], sent[0]))
+            pair = blocks[k]
+            if inner == 2:
+                pair = add_pair(along_inner(give[k]), blocks[k], BF16 if k else F32, 1000000)
+            if k:
+                sent.append(pair.astype(BF16))
+            else:
+                total = pair
+        for k, value in zip(order, sent):
+            total = add_pair(along_outer(value, -k), total, BF16 if k == order[-2] else F32, 1500000000)
+        return total
 
     return local
 

time: 55.7 us -> 57.6 us (1.034)
  waiting for transfers between devices: 31 us -> 15.1 us
  Pallas kernels: 0 us -> 12 us
  local copies, waits for them, and re-layouts: 1.07 us -> 6.67 us
  starting transfers between devices: 17.9 us -> 18.9 us
  other arithmetic: 0.84 us -> 0 us
    pallas_call x0 -> x7, Pallas kernels: none -> 12 us  [add_pair(): pl.pallas_call(pair_kernel, out_shape=jax.ShapeDtypeStruct(own.shape, dty...]
    ppermute x6, waiting for transfers between devices: 16.3 us -> 6.42 us  [along_outer(): return lax.ppermute(value, 'wide', pairs)]
    ppermute x8, waiting for transfers between devices: 13.4 us -> 7.23 us  [along_inner(): return lax.ppermute(value, 'wide', pairs)]
    unnamed x11 -> x25, local copies, waits for them, and re-layouts: 1.02 us -> 5.6 us
    slice x1 -> x2, local copies, waits for them, and re-layouts: 0.04 us -> 1.06 us  [local(): blocks = [partial[k * rows:(k + 1) * rows] for k in range(wide)]]
    ppermute x8, starting transfers between devices: 9.18 us -> 10.2 us  [along_inner(): return lax.ppermute(value, 'wide', pairs)]
    convert_element_type x2 -> x0, other arithmetic: 0.84 us -> none  [the longest x1 0.74 us: local(): return total.astype(BF16)]
  transfers between devices with their start and end apart: 16 -> 16, of which waited for: 11 -> 6; matrix products, arithmetic and copies ran while one was open for 2% -> 4% of each run, Pallas kernels for 0% -> 18%
where the time goes in v2:
time: 57.6 us; the launch traced here: 57.4 us
  starting transfers between devices  18.9 us (33%)
  waiting for transfers between devices  15.1 us (26%)
  Pallas kernels  12 us (21%)
  local copies, waits for them, and re-layouts  6.67 us (12%)
  matrix products  4.58 us (8%)
    pallas_call x7, Pallas kernels, add_pair(): pl.pallas_call(pair_kernel, out_shape=jax.ShapeDtypeStruct(own.shape, dty...  12 us
    ppermute x8, starting transfers between devices, along_inner(): return lax.ppermute(value, 'wide', pairs)  10.2 us
    ppermute x6, starting transfers between devices, along_outer(): return lax.ppermute(value, 'wide', pairs)  8.13 us
    ppermute x8, waiting for transfers between devices, along_inner(): return lax.ppermute(value, 'wide', pairs)  7.23 us
    ppermute x6, waiting for transfers between devices, along_outer(): return lax.ppermute(value, 'wide', pairs)  6.42 us
    unnamed x25, local copies, waits for them, and re-layouts  5.6 us
    dot_general x1, matrix products, local(): up_part = jnp.dot(all_rows, up_weight, preferred_element_type=F32)  3.12 us
    ppermute x2, waiting for transfers between devices, across_cores(): return lax.ppermute(value, 'narrow', pairs)  1.4 us
  transfers between devices with their start and end apart: 16, of which 6 were waited for; matrix products, arithmetic and copies ran while one was open for 4% of the time, Pallas kernels for 18%

profile of v2, /device:TPU:0, one launch (start us, length us, event | category | flops | bytes accessed | tf_op | source)
XLA Modules:
  0.0 57.4 jit_solution(896498503929675820)
XLA Ops:
  0.0 5.0 %collective-permute-start.2 = (bf16[16,4096]{1,0:T(8,128)(2,1)}, bf16[16,4096]{1,0:T(8,128)(2,1)S(1)}, u32[]{:S(2)}, u32[]{:S(2)}) collective-permute-start(bf16[16,4096]{1,0:T(8,128)(2,1)} %param.4), channel_id=1, source_target_pairs={{0,12},{2,14},{4,0},{6,2},{8,4},{10,6},{12,8},{14,10},{1,13},{3,15... | collective-permute-start | bytes 393224 | tf_op jit(solution)/shard_map/ppermute | solution.py:31
  5.1 0.0 collective-permute-start.1
  5.1 1.0 %collective-permute-start = (bf16[16,4096]{1,0:T(8,128)(2,1)}, bf16[16,4096]{1,0:T(8,128)(2,1)S(1)}, u32[]{:S(2)}, u32[]{:S(2)}) collective-permute-start(bf16[16,4096]{1,0:T(8,128)(2,1)} %param.4), channel_id=1, source_target_pairs={{0,4},{2,6},{4,8},{6,10},{8,12},{10,14},{12,0},{14,2},{1,5},{3,7},... | collective-permute-start | bytes 393224 | tf_op jit(solution)/shard_map/ppermute | solution.py:31
  6.1 1.5 %collective-permute-start.3 = (bf16[16,4096]{1,0:T(8,128)(2,1)}, bf16[16,4096]{1,0:T(8,128)(2,1)S(1)}, u32[]{:S(2)}, u32[]{:S(2)}) collective-permute-start(bf16[16,4096]{1,0:T(8,128)(2,1)} %param.4), channel_id=1, source_target_pairs={{0,2},{2,0},{4,6},{6,4},{8,10},{10,8},{12,14},{14,12},{1,3},{3,1},... | collective-permute-start | bytes 393224 | tf_op jit(solution)/shard_map/ppermute | solution.py:35
  7.6 0.9 %constant_dynamic-update-slice_fusion.7 = bf16[128,4096]{1,0:T(8,128)(2,1)S(1)} fusion(bf16[16,4096]{1,0:T(8,128)(2,1)} %param.4), kind=kLoop, calls=%fused_computation.10 | loop fusion | bytes 262144
  8.5 0.7 %collective-permute-done.2 = bf16[16,4096]{1,0:T(8,128)(2,1)S(1)} collective-permute-done((bf16[16,4096]{1,0:T(8,128)(2,1)}, bf16[16,4096]{1,0:T(8,128)(2,1)S(1)}, u32[]{:S(2)}, u32[]{:S(2)}) %collective-permute-start.2) | collective-permute-done | bytes 131104 | tf_op jit(solution)/shard_map/ppermute | solution.py:31
  9.3 1.5 %collective-permute-start.6 = (bf16[16,4096]{1,0:T(8,128)(2,1)S(1)}, bf16[16,4096]{1,0:T(8,128)(2,1)S(1)}, u32[]{:S(2)}, u32[]{:S(2)}) collective-permute-start(bf16[16,4096]{1,0:T(8,128)(2,1)S(1)} %collective-permute-done.2), channel_id=1, source_target_pairs={{0,2},{2,0},{4,6},{6,4},{8,10},{10,8},{12,14},{14,12},{1,3},{3,1},... | collective-permute-start | bytes 393224 | tf_op jit(solution)/shard_map/ppermute | solution.py:35
  10.8 5.7 %collective-permute-done.1 = bf16[16,4096]{1,0:T(8,128)(2,1)S(1)} collective-permute-done((bf16[16,4096]{1,0:T(8,128)(2,1)}, bf16[16,4096]{1,0:T(8,128)(2,1)S(1)}, u32[]{:S(2)}, u32[]{:S(2)}) %collective-permute-start.1) | collective-permute-done | bytes 131104 | tf_op jit(solution)/shard_map/ppermute | solution.py:31
  16.5 1.5 %collective-permute-start.5 = (bf16[16,4096]{1,0:T(8,128)(2,1)S(1)}, bf16[16,4096]{1,0:T(8,128)(2,1)S(1)}, u32[]{:S(2)}, u32[]{:S(2)}) collective-permute-start(bf16[16,4096]{1,0:T(8,128)(2,1)S(1)} %collective-permute-done.1), channel_id=1, source_target_pairs={{0,2},{2,0},{4,6},{6,4},{8,10},{10,8},{12,14},{14,12},{1,3},{3,1},... | collective-permute-start | bytes 393224 | tf_op jit(solution)/shard_map/ppermute | solution.py:35
  18.0 0.0 collective-permute-done
  18.0 0.5 collective-permute-start.4
  18.5 0.0 collective-permute-done.3
  18.6 5.5 %collective-permute-done.4 = bf16[16,4096]{1,0:T(8,128)(2,1)S(1)} collective-permute-done((bf16[16,4096]{1,0:T(8,128)(2,1)S(1)}, bf16[16,4096]{1,0:T(8,128)(2,1)S(1)}, u32[]{:S(2)}, u32[]{:S(2)}) %collective-permute-start.4) | collective-permute-done | bytes 131104 | tf_op jit(solution)/shard_map/ppermute | solution.py:35
  24.1 0.0 copy-start.1
  24.1 3.1 %fusion.7 = f32[128,512]{1,0:T(8,128)S(1)} fusion(bf16[128,4096]{1,0:T(8,128)(2,1)S(1)} %constant_dynamic-update-slice_fusion, bf16[4096,512]{1,0:T(8,128)(2,1)} %param.6), kind=kOutput, calls=%fused_computation.16 | convolution fusion | flops 536870912 | bytes 5505024 | tf_op jit(solution)/shard_map/dot_general | solution.py:47
  27.2 0.7 %fusion.6 = f32[128,512]{1,0:T(8,128)S(1)} fusion(bf16[128,4096]{1,0:T(8,128)(2,1)S(1)} %constant_dynamic-update-slice_fusion, bf16[4096,512]{1,0:T(8,128)(2,1)S(1)} %copy-done), kind=kOutput, calls=%fused_computation.15 | convolution fusion | flops 536870912 | bytes 5505024 | tf_op jit(solution)/shard_map/dot_general | solution.py:46
  28.0 0.1 collective-permute-start.7
  28.1 0.5 collective-permute-start.8
  28.5 1.0 %collective-permute-done.7 = f32[128,512]{1,0:T(8,128)S(1)} collective-permute-done((f32[128,512]{1,0:T(8,128)S(1)}, f32[128,512]{1,0:T(8,128)S(1)}, u32[]{:S(2)}, u32[]{:S(2)}) %collective-permute-start.7) | collective-permute-done | bytes 262176 | tf_op jit(solution)/shard_map/ppermute | solution.py:39
  29.6 0.4 collective-permute-done.8
  30.0 0.7 %fusion.5 = (bf16[128,4096]{1,0:T(8,128)(2,1)S(1)}, f32[128,4096]{1,0:T(8,128)S(1)}) fusion(bf16[512,4096]{1,0:T(8,128)(2,1)S(1)} %copy-done.1, f32[128,512]{1,0:T(8,128)S(1)} %fusion.7, f32[128,512]{1,0:T(8,128)S(1)} %collective-permute-done.8, f32[128,512]{1,0:T(8,128)S(1)} %fusion.6, f32[128,512]{1,0:T(8,128)S(1)} %collective-permute-done.7), kind=kOutput, calls=%fused_computation.14 | convolution fusion | flops 537919488 | bytes 8388608 | tf_op jit(solution)/shard_map/dot_general | solution.py:51
  30.8 1.6 %collective-permute-start.13 = (bf16[16,4096]{1,0:T(8,128)(2,1)S(1)}, bf16[16,4096]{1,0:T(8,128)(2,1)S(1)}, u32[]{:S(2)}, u32[]{:S(2)}) collective-permute-start(bf16[16,4096]{1,0:T(8,128)(2,1)S(1)} %get-tuple-element.13), channel_id=1, source_target_pairs={{0,2},{2,0},{4,6},{6,4},{8,10},{10,8},{12,14},{14,12},{1,3},{3,1},... | collective-permute-start | bytes 393224 | tf_op jit(solution)/shard_map/ppermute | solution.py:35
  32.3 0.5 collective-permute-start.11
  32.8 1.5 %collective-permute-start.9 = (bf16[16,4096]{1,0:T(8,128)(2,1)S(1)}, bf16[16,4096]{1,0:T(8,128)(2,1)S(1)}, u32[]{:S(2)}, u32[]{:S(2)}) collective-permute-start(bf16[16,4096]{1,0:T(8,128)(2,1)S(1)} %get-tuple-element.16), channel_id=1, source_target_pairs={{0,2},{2,0},{4,6},{6,4},{8,10},{10,8},{12,14},{14,12},{1,3},{3,1},... | collective-permute-start | bytes 393224 | tf_op jit(solution)/shard_map/ppermute | solution.py:35
  34.4 1.0 %fusion.3 = (f32[16,4096]{1,0:T(8,128)}, f32[16,4096]{1,0:T(8,128)}, f32[16,4096]{1,0:T(8,128)}, f32[16,4096]{1,0:T(8,128)}) fusion(f32[128,4096]{1,0:T(8,128)S(1)} %get-tuple-element.18), kind=kLoop, calls=%fused_computation.12 | loop fusion | bytes 2097152 | tf_op jit(solution)/shard_map/slice | solution.py:52
  35.4 1.8 %collective-permute-done.13.arrived_ref = bf16[16,4096]{1,0:T(8,128)(2,1)S(1)} collective-permute-done((bf16[16,4096]{1,0:T(8,128)(2,1)S(1)}, bf16[16,4096]{1,0:T(8,128)(2,1)S(1)}, u32[]{:S(2)}, u32[]{:S(2)}) %collective-permute-start.13) | collective-permute-done | bytes 131104 | tf_op jit(solution)/shard_map/ppermute | solution.py:35
  37.2 0.7 %copy-done.5 = bf16[16,4096]{1,0:T(8,128)(2,1)} copy-done((bf16[16,4096]{1,0:T(8,128)(2,1)}, bf16[16,4096]{1,0:T(8,128)(2,1)S(1)}, u32[]{:S(2)}) %copy-start.5) | copy-done | bytes 131096
  37.8 1.7 %add_pair.9 = bf16[16,4096]{1,0:T(8,128)(2,1)} custom-call(bf16[16,4096]{1,0:T(8,128)(2,1)} %copy-done.5, f32[16,4096]{1,0:T(8,128)} %get-tuple-element.10.own_ref), custom_call_target="tpu_custom_call" | custom-call | flops 1000000 | tf_op jit(solution)/shard_map/add_pair/pallas_call | solution.py:17
  39.5 1.5 %collective-permute-start.15 = (bf16[16,4096]{1,0:T(8,128)(2,1)S(1)}, bf16[16,4096]{1,0:T(8,128)(2,1)S(1)}, u32[]{:S(2)}, u32[]{:S(2)}) collective-permute-start(bf16[16,4096]{1,0:T(8,128)(2,1)S(1)} %get-tuple-element.8), channel_id=1, source_target_pairs={{0,2},{2,0},{4,6},{6,4},{8,10},{10,8},{12,14},{14,12},{1,3},{3,1},... | collective-permute-start | bytes 393224 | tf_op jit(solution)/shard_map/ppermute | solution.py:35
  41.0 0.0 collective-permute-start.14
  41.1 0.7 %copy-done.4 = bf16[16,4096]{1,0:T(8,128)(2,1)} copy-done((bf16[16,4096]{1,0:T(8,128)(2,1)}, bf16[16,4096]{1,0:T(8,128)(2,1)S(1)}, u32[]{:S(2)}) %copy-start.4) | copy-done | bytes 131096
  41.7 1.7 %add_pair.8 = bf16[16,4096]{1,0:T(8,128)(2,1)} custom-call(bf16[16,4096]{1,0:T(8,128)(2,1)} %copy-done.4, f32[16,4096]{1,0:T(8,128)} %get-tuple-element.11.own_ref), custom_call_target="tpu_custom_call" | custom-call | flops 1000000 | tf_op jit(solution)/shard_map/add_pair/pallas_call | solution.py:17
  43.4 1.4 %collective-permute-start.12 = (bf16[16,4096]{1,0:T(8,128)(2,1)}, bf16[16,4096]{1,0:T(8,128)(2,1)S(1)}, u32[]{:S(2)}, u32[]{:S(2)}) collective-permute-start(bf16[16,4096]{1,0:T(8,128)(2,1)} %add_pair.8), channel_id=1, source_target_pairs={{0,12},{2,14},{4,0},{6,2},{8,4},{10,6},{12,8},{14,10},{1,13},{3,15... | collective-permute-start | bytes 393224 | tf_op jit(solution)/shard_map/ppermute | solution.py:31
  44.8 0.0 collective-permute-done.9.arrived_ref
  44.8 0.7 %copy-done.3 = bf16[16,4096]{1,0:T(8,128)(2,1)} copy-done((bf16[16,4096]{1,0:T(8,128)(2,1)}, bf16[16,4096]{1,0:T(8,128)(2,1)S(1)}, u32[]{:S(2)}) %copy-start.3) | copy-done | bytes 131096
  45.5 1.7 %add_pair.7 = bf16[16,4096]{1,0:T(8,128)(2,1)} custom-call(bf16[16,4096]{1,0:T(8,128)(2,1)} %copy-done.3, f32[16,4096]{1,0:T(8,128)} %get-tuple-element.12.own_ref), custom_call_target="tpu_custom_call" | custom-call | flops 1000000 | tf_op jit(solution)/shard_map/add_pair/pallas_call | solution.py:17
  47.2 0.6 %collective-permute-start.10 = (bf16[16,4096]{1,0:T(8,128)(2,1)}, bf16[16,4096]{1,0:T(8,128)(2,1)S(1)}, u32[]{:S(2)}, u32[]{:S(2)}) collective-permute-start(bf16[16,4096]{1,0:T(8,128)(2,1)} %add_pair.7), channel_id=1, source_target_pairs={{0,4},{2,6},{4,8},{6,10},{8,12},{10,14},{12,0},{14,2},{1,5},{3,7},... | collective-permute-start | bytes 393224 | tf_op jit(solution)/shard_map/ppermute | solution.py:31
  47.8 0.0 collective-permute-done.15.arrived_ref
  47.8 0.7 %copy-done.2 = bf16[16,4096]{1,0:T(8,128)(2,1)} copy-done((bf16[16,4096]{1,0:T(8,128)(2,1)}, bf16[16,4096]{1,0:T(8,128)(2,1)S(1)}, u32[]{:S(2)}) %copy-start.2) | copy-done | bytes 131096
  48.5 1.7 %add_pair.10.own_ref = f32[16,4096]{1,0:T(8,128)} custom-call(bf16[16,4096]{1,0:T(8,128)(2,1)} %copy-done.2, f32[16,4096]{1,0:T(8,128)} %get-tuple-element.9.own_ref), custom_call_target="tpu_custom_call" | custom-call | flops 1000000 | tf_op jit(solution)/shard_map/add_pair/pallas_call | solution.py:17
  50.2 0.0 collective-permute-done.14.arrived_ref
  50.2 0.7 %copy-done.6 = bf16[16,4096]{1,0:T(8,128)(2,1)} copy-done((bf16[16,4096]{1,0:T(8,128)(2,1)}, bf16[16,4096]{1,0:T(8,128)(2,1)S(1)}, u32[]{:S(2)}) %copy-start.6) | copy-done | bytes 131096
  50.9 1.7 %add_pair.11.own_ref = f32[16,4096]{1,0:T(8,128)} custom-call(bf16[16,4096]{1,0:T(8,128)(2,1)} %copy-done.6, f32[16,4096]{1,0:T(8,128)} %add_pair.10.own_ref), custom_call_target="tpu_custom_call" | custom-call | flops 1500000000 | tf_op jit(solution)/shard_map/add_pair/pallas_call | solution.py:17
  52.6 0.0 collective-permute-done.12.arrived_ref
  52.6 0.7 %copy-done.7 = bf16[16,4096]{1,0:T(8,128)(2,1)} copy-done((bf16[16,4096]{1,0:T(8,128)(2,1)}, bf16[16,4096]{1,0:T(8,128)(2,1)S(1)}, u32[]{:S(2)}) %copy-start.7) | copy-done | bytes 131096
  53.3 1.7 %add_pair.12.own_ref = f32[16,4096]{1,0:T(8,128)} custom-call(bf16[16,4096]{1,0:T(8,128)(2,1)} %copy-done.7, f32[16,4096]{1,0:T(8,128)} %add_pair.11.own_ref), custom_call_target="tpu_custom_call" | custom-call | flops 1500000000 | tf_op jit(solution)/shard_map/add_pair/pallas_call | solution.py:17
  55.0 0.6 %copy-done.8 = bf16[16,4096]{1,0:T(8,128)(2,1)} copy-done((bf16[16,4096]{1,0:T(8,128)(2,1)}, bf16[16,4096]{1,0:T(8,128)(2,1)S(1)}, u32[]{:S(2)}) %copy-start.8) | copy-done | bytes 131096
  55.7 1.7 %add_pair.13 = bf16[16,4096]{1,0:T(8,128)(2,1)} custom-call(bf16[16,4096]{1,0:T(8,128)(2,1)} %copy-done.8, f32[16,4096]{1,0:T(8,128)} %add_pair.12.own_ref), custom_call_target="tpu_custom_call" | custom-call | flops 1500000000 | tf_op jit(solution)/shard_map/add_pair/pallas_call | solution.py:17
  (22 shorter events, 0.1 us)
Async XLA Ops:
  0.0 27.2 %copy-start = (bf16[4096,512]{1,0:T(8,128)(2,1)S(1)}, bf16[4096,512]{1,0:T(8,128)(2,1)}, u32[]{:S(2)}) copy-start(bf16[4096,512]{1,0:T(8,128)(2,1)} %param.5) | copy-start | bytes 12582916
  0.0 9.3 %collective-permute-start.2 = (bf16[16,4096]{1,0:T(8,128)(2,1)}, bf16[16,4096]{1,0:T(8,128)(2,1)S(1)}, u32[]{:S(2)}, u32[]{:S(2)}) collective-permute-start(bf16[16,4096]{1,0:T(8,128)(2,1)} %param.4), channel_id=1, source_target_pairs={{0,12},{2,14},{4,0},{6,2},{8,4},{10,6},{12,8},{14,10},{1,13},{3,15... | collective-permute-start | bytes 393224 | tf_op jit(solution)/shard_map/ppermute | solution.py:31
  5.1 11.4 %collective-permute-start.1 = (bf16[16,4096]{1,0:T(8,128)(2,1)}, bf16[16,4096]{1,0:T(8,128)(2,1)S(1)}, u32[]{:S(2)}, u32[]{:S(2)}) collective-permute-start(bf16[16,4096]{1,0:T(8,128)(2,1)} %param.4), channel_id=1, source_target_pairs={{0,8},{2,10},{4,12},{6,14},{8,0},{10,2},{12,4},{14,6},{1,9},{3,11}... | collective-permute-start | bytes 393224 | tf_op jit(solution)/shard_map/ppermute | solution.py:31
  5.1 12.9 %collective-permute-start = (bf16[16,4096]{1,0:T(8,128)(2,1)}, bf16[16,4096]{1,0:T(8,128)(2,1)S(1)}, u32[]{:S(2)}, u32[]{:S(2)}) collective-permute-start(bf16[16,4096]{1,0:T(8,128)(2,1)} %param.4), channel_id=1, source_target_pairs={{0,4},{2,6},{4,8},{6,10},{8,12},{10,14},{12,0},{14,2},{1,5},{3,7},... | collective-permute-start | bytes 393224 | tf_op jit(solution)/shard_map/ppermute | solution.py:31
  6.1 12.5 %collective-permute-start.3 = (bf16[16,4096]{1,0:T(8,128)(2,1)}, bf16[16,4096]{1,0:T(8,128)(2,1)S(1)}, u32[]{:S(2)}, u32[]{:S(2)}) collective-permute-start(bf16[16,4096]{1,0:T(8,128)(2,1)} %param.4), channel_id=1, source_target_pairs={{0,2},{2,0},{4,6},{6,4},{8,10},{10,8},{12,14},{14,12},{1,3},{3,1},... | collective-permute-start | bytes 393224 | tf_op jit(solution)/shard_map/ppermute | solution.py:35
  9.3 14.8 %collective-permute-start.6 = (bf16[16,4096]{1,0:T(8,128)(2,1)S(1)}, bf16[16,4096]{1,0:T(8,128)(2,1)S(1)}, u32[]{:S(2)}, u32[]{:S(2)}) collective-permute-start(bf16[16,4096]{1,0:T(8,128)(2,1)S(1)} %collective-permute-done.2), channel_id=1, source_target_pairs={{0,2},{2,0},{4,6},{6,4},{8,10},{10,8},{12,14},{14,12},{1,3},{3,1},... | collective-permute-start | bytes 393224 | tf_op jit(solution)/shard_map/ppermute | solution.py:35
  16.5 7.6 %collective-permute-start.5 = (bf16[16,4096]{1,0:T(8,128)(2,1)S(1)}, bf16[16,4096]{1,0:T(8,128)(2,1)S(1)}, u32[]{:S(2)}, u32[]{:S(2)}) collective-permute-start(bf16[16,4096]{1,0:T(8,128)(2,1)S(1)} %collective-permute-done.1), channel_id=1, source_target_pairs={{0,2},{2,0},{4,6},{6,4},{8,10},{10,8},{12,14},{14,12},{1,3},{3,1},... | collective-permute-start | bytes 393224 | tf_op jit(solution)/shard_map/ppermute | solution.py:35
  18.0 6.0 %collective-permute-start.4 = (bf16[16,4096]{1,0:T(8,128)(2,1)S(1)}, bf16[16,4096]{1,0:T(8,128)(2,1)S(1)}, u32[]{:S(2)}, u32[]{:S(2)}) collective-permute-start(bf16[16,4096]{1,0:T(8,128)(2,1)S(1)} %collective-permute-done), channel_id=1, source_target_pairs={{0,2},{2,0},{4,6},{6,4},{8,10},{10,8},{12,14},{14,12},{1,3},{3,1},... | collective-permute-start | bytes 393224 | tf_op jit(solution)/shard_map/ppermute | solution.py:35
  24.1 5.8 %copy-start.1 = (bf16[512,4096]{1,0:T(8,128)(2,1)S(1)}, bf16[512,4096]{1,0:T(8,128)(2,1)}, u32[]{:S(2)}) copy-start(bf16[512,4096]{1,0:T(8,128)(2,1)} %param.7) | copy-start | bytes 12582916
  28.0 1.6 %collective-permute-start.7 = (f32[128,512]{1,0:T(8,128)S(1)}, f32[128,512]{1,0:T(8,128)S(1)}, u32[]{:S(2)}, u32[]{:S(2)}) collective-permute-start(f32[128,512]{1,0:T(8,128)S(1)} %fusion.6), channel_id=1, source_target_pairs={{0,1},{1,0},{2,3},{3,2},{4,5},{5,4},{6,7},{7,6},{8,9},{9,8},{10,11... | collective-permute-start | bytes 786440 | tf_op jit(solution)/shard_map/ppermute | solution.py:39
  28.1 1.9 %collective-permute-start.8 = (f32[128,512]{1,0:T(8,128)S(1)}, f32[128,512]{1,0:T(8,128)S(1)}, u32[]{:S(2)}, u32[]{:S(2)}) collective-permute-start(f32[128,512]{1,0:T(8,128)S(1)} %fusion.7), channel_id=1, source_target_pairs={{0,1},{1,0},{2,3},{3,2},{4,5},{5,4},{6,7},{7,6},{8,9},{9,8},{10,11... | collective-permute-start | bytes 786440 | tf_op jit(solution)/shard_map/ppermute | solution.py:39
  30.8 6.4 %collective-permute-start.13 = (bf16[16,4096]{1,0:T(8,128)(2,1)S(1)}, bf16[16,4096]{1,0:T(8,128)(2,1)S(1)}, u32[]{:S(2)}, u32[]{:S(2)}) collective-permute-start(bf16[16,4096]{1,0:T(8,128)(2,1)S(1)} %get-tuple-element.13), channel_id=1, source_target_pairs={{0,2},{2,0},{4,6},{6,4},{8,10},{10,8},{12,14},{14,12},{1,3},{3,1},... | collective-permute-start | bytes 393224 | tf_op jit(solution)/shard_map/ppermute | solution.py:35
  32.3 8.7 %collective-permute-start.11 = (bf16[16,4096]{1,0:T(8,128)(2,1)S(1)}, bf16[16,4096]{1,0:T(8,128)(2,1)S(1)}, u32[]{:S(2)}, u32[]{:S(2)}) collective-permute-start(bf16[16,4096]{1,0:T(8,128)(2,1)S(1)} %get-tuple-element.15), channel_id=1, source_target_pairs={{0,2},{2,0},{4,6},{6,4},{8,10},{10,8},{12,14},{14,12},{1,3},{3,1},... | collective-permute-start | bytes 393224 | tf_op jit(solution)/shard_map/ppermute | solution.py:35
  32.8 12.0 %collective-permute-start.9 = (bf16[16,4096]{1,0:T(8,128)(2,1)S(1)}, bf16[16,4096]{1,0:T(8,128)(2,1)S(1)}, u32[]{:S(2)}, u32[]{:S(2)}) collective-permute-start(bf16[16,4096]{1,0:T(8,128)(2,1)S(1)} %get-tuple-element.16), channel_id=1, source_target_pairs={{0,2},{2,0},{4,6},{6,4},{8,10},{10,8},{12,14},{14,12},{1,3},{3,1},... | collective-permute-start | bytes 393224 | tf_op jit(solution)/shard_map/ppermute | solution.py:35
  37.2 0.7 %copy-start.5 = (bf16[16,4096]{1,0:T(8,128)(2,1)}, bf16[16,4096]{1,0:T(8,128)(2,1)S(1)}, u32[]{:S(2)}) copy-start(bf16[16,4096]{1,0:T(8,128)(2,1)S(1)} %collective-permute-done.13.arrived_ref) | copy-start | bytes 393220
  39.5 8.3 %collective-permute-start.15 = (bf16[16,4096]{1,0:T(8,128)(2,1)S(1)}, bf16[16,4096]{1,0:T(8,128)(2,1)S(1)}, u32[]{:S(2)}, u32[]{:S(2)}) collective-permute-start(bf16[16,4096]{1,0:T(8,128)(2,1)S(1)} %get-tuple-element.8), channel_id=1, source_target_pairs={{0,2},{2,0},{4,6},{6,4},{8,10},{10,8},{12,14},{14,12},{1,3},{3,1},... | collective-permute-start | bytes 393224 | tf_op jit(solution)/shard_map/ppermute | solution.py:35
  41.0 9.2 %collective-permute-start.14 = (bf16[16,4096]{1,0:T(8,128)(2,1)}, bf16[16,4096]{1,0:T(8,128)(2,1)S(1)}, u32[]{:S(2)}, u32[]{:S(2)}) collective-permute-start(bf16[16,4096]{1,0:T(8,128)(2,1)} %add_pair.9), channel_id=1, source_target_pairs={{0,8},{2,10},{4,12},{6,14},{8,0},{10,2},{12,4},{14,6},{1,9},{3,11}... | collective-permute-start | bytes 393224 | tf_op jit(solution)/shard_map/ppermute | solution.py:31
  41.1 0.7 %copy-start.4 = (bf16[16,4096]{1,0:T(8,128)(2,1)}, bf16[16,4096]{1,0:T(8,128)(2,1)S(1)}, u32[]{:S(2)}) copy-start(bf16[16,4096]{1,0:T(8,128)(2,1)S(1)} %collective-permute-done.11.arrived_ref) | copy-start | bytes 393220
  43.4 9.2 %collective-permute-start.12 = (bf16[16,4096]{1,0:T(8,128)(2,1)}, bf16[16,4096]{1,0:T(8,128)(2,1)S(1)}, u32[]{:S(2)}, u32[]{:S(2)}) collective-permute-start(bf16[16,4096]{1,0:T(8,128)(2,1)} %add_pair.8), channel_id=1, source_target_pairs={{0,12},{2,14},{4,0},{6,2},{8,4},{10,6},{12,8},{14,10},{1,13},{3,15... | collective-permute-start | bytes 393224 | tf_op jit(solution)/shard_map/ppermute | solution.py:31
  44.8 0.7 %copy-start.3 = (bf16[16,4096]{1,0:T(8,128)(2,1)}, bf16[16,4096]{1,0:T(8,128)(2,1)S(1)}, u32[]{:S(2)}) copy-start(bf16[16,4096]{1,0:T(8,128)(2,1)S(1)} %collective-permute-done.9.arrived_ref) | copy-start | bytes 393220
  47.2 7.8 %collective-permute-start.10 = (bf16[16,4096]{1,0:T(8,128)(2,1)}, bf16[16,4096]{1,0:T(8,128)(2,1)S(1)}, u32[]{:S(2)}, u32[]{:S(2)}) collective-permute-start(bf16[16,4096]{1,0:T(8,128)(2,1)} %add_pair.7), channel_id=1, source_target_pairs={{0,4},{2,6},{4,8},{6,10},{8,12},{10,14},{12,0},{14,2},{1,5},{3,7},... | collective-permute-start | bytes 393224 | tf_op jit(solution)/shard_map/ppermute | solution.py:31
  47.8 0.7 %copy-start.2 = (bf16[16,4096]{1,0:T(8,128)(2,1)}, bf16[16,4096]{1,0:T(8,128)(2,1)S(1)}, u32[]{:S(2)}) copy-start(bf16[16,4096]{1,0:T(8,128)(2,1)S(1)} %collective-permute-done.15.arrived_ref) | copy-start | bytes 393220
  50.2 0.7 %copy-start.6 = (bf16[16,4096]{1,0:T(8,128)(2,1)}, bf16[16,4096]{1,0:T(8,128)(2,1)S(1)}, u32[]{:S(2)}) copy-start(bf16[16,4096]{1,0:T(8,128)(2,1)S(1)} %collective-permute-done.14.arrived_ref) | copy-start | bytes 393220
  52.6 0.7 %copy-start.7 = (bf16[16,4096]{1,0:T(8,128)(2,1)}, bf16[16,4096]{1,0:T(8,128)(2,1)S(1)}, u32[]{:S(2)}) copy-start(bf16[16,4096]{1,0:T(8,128)(2,1)S(1)} %collective-permute-done.12.arrived_ref) | copy-start | bytes 393220
  55.0 0.6 %copy-start.8 = (bf16[16,4096]{1,0:T(8,128)(2,1)}, bf16[16,4096]{1,0:T(8,128)(2,1)S(1)}, u32[]{:S(2)}) copy-start(bf16[16,4096]{1,0:T(8,128)(2,1)S(1)} %collective-permute-done.10.arrived_ref) | copy-start | bytes 393220

commit v3 on v2

--- a/solution.py
+++ b/solution.py
@@ -17,6 +17,7 @@
     return pl.pallas_call(
         pair_kernel,
         out_shape=jax.ShapeDtypeStruct(own.shape, dtype),
+        compiler_params=pltpu.CompilerParams(vmem_limit_bytes=2 << 20),
         cost_estimate=pl.CostEstimate(flops=flops, bytes_accessed=0, transcendentals=0),
         name="add_pair",
     )(arrived, own)

time: 57.6 us -> 50.5 us (0.88)
  Pallas kernels: 12 us -> 0.83 us
  waiting for transfers between devices: 15.1 us -> 26 us
  local copies, waits for them, and re-layouts: 6.67 us -> 1.14 us
  starting transfers between devices: 18.9 us -> 17.7 us
    pallas_call x7, Pallas kernels: 12 us -> 0.83 us  [add_pair(): pl.pallas_call(pair_kernel, out_shape=jax.ShapeDtypeStruct(own.shape, dty...]
    ppermute x8, waiting for transfers between devices: 7.23 us -> 13.4 us  [along_inner(): return lax.ppermute(value, 'wide', pairs)]
    ppermute x6, waiting for transfers between devices: 6.42 us -> 11.3 us  [along_outer(): return lax.ppermute(value, 'wide', pairs)]
    unnamed x25 -> x11, local copies, waits for them, and re-layouts: 5.6 us -> 1.02 us
    ppermute x6, starting transfers between devices: 8.13 us -> 6.82 us  [along_outer(): return lax.ppermute(value, 'wide', pairs)]
    slice x2, local copies, waits for them, and re-layouts: 1.06 us -> 0.11 us  [local(): blocks = [partial[k * rows:(k + 1) * rows] for k in range(wide)]]
  transfers between devices with their start and end apart: 16 -> 16, of which waited for: 6 -> 12; matrix products, arithmetic and copies ran while one was open for 4% -> 2% of each run, Pallas kernels for 18% -> 0%
where the time goes in v3:
time: 50.5 us; the launch traced here: 50.4 us
  waiting for transfers between devices  26 us (51%)
  starting transfers between devices  17.7 us (35%)
  matrix products  4.58 us (9%)
  local copies, waits for them, and re-layouts  1.14 us (2%)
  Pallas kernels  0.83 us (2%)
    ppermute x8, waiting for transfers between devices, along_inner(): return lax.ppermute(value, 'wide', pairs)  13.4 us
    ppermute x6, waiting for transfers between devices, along_outer(): return lax.ppermute(value, 'wide', pairs)  11.3 us
    ppermute x8, starting transfers between devices, along_inner(): return lax.ppermute(value, 'wide', pairs)  10.3 us
    ppermute x6, starting transfers between devices, along_outer(): return lax.ppermute(value, 'wide', pairs)  6.82 us
    dot_general x1, matrix products, local(): up_part = jnp.dot(all_rows, up_weight, preferred_element_type=F32)  3.12 us
    ppermute x2, waiting for transfers between devices, across_cores(): return lax.ppermute(value, 'narrow', pairs)  1.4 us
    unnamed x11, local copies, waits for them, and re-layouts  1.02 us
  transfers between devices with their start and end apart: 16, of which 12 were waited for; matrix products, arithmetic and copies ran while one was open for 2% of the time, Pallas kernels for 0%

profile of v3, /device:TPU:0, one launch (start us, length us, event | category | flops | bytes accessed | tf_op | source)
XLA Modules:
  0.0 50.4 jit_solution(9911107637630004786)
XLA Ops:
  0.0 0.0 copy-start
  0.0 5.0 %collective-permute-start.2 = (bf16[16,4096]{1,0:T(8,128)(2,1)}, bf16[16,4096]{1,0:T(8,128)(2,1)S(1)}, u32[]{:S(2)}, u32[]{:S(2)}) collective-permute-start(bf16[16,4096]{1,0:T(8,128)(2,1)} %param.4), channel_id=1, source_target_pairs={{0,12},{2,14},{4,0},{6,2},{8,4},{10,6},{12,8},{14,10},{1,13},{3,15... | collective-permute-start | bytes 393224 | tf_op jit(solution)/shard_map/ppermute | solution.py:32
  5.1 0.0 collective-permute-start.1
  5.1 1.0 %collective-permute-start = (bf16[16,4096]{1,0:T(8,128)(2,1)}, bf16[16,4096]{1,0:T(8,128)(2,1)S(1)}, u32[]{:S(2)}, u32[]{:S(2)}) collective-permute-start(bf16[16,4096]{1,0:T(8,128)(2,1)} %param.4), channel_id=1, source_target_pairs={{0,4},{2,6},{4,8},{6,10},{8,12},{10,14},{12,0},{14,2},{1,5},{3,7},... | collective-permute-start | bytes 393224 | tf_op jit(solution)/shard_map/ppermute | solution.py:32
  6.1 1.5 %collective-permute-start.3 = (bf16[16,4096]{1,0:T(8,128)(2,1)}, bf16[16,4096]{1,0:T(8,128)(2,1)S(1)}, u32[]{:S(2)}, u32[]{:S(2)}) collective-permute-start(bf16[16,4096]{1,0:T(8,128)(2,1)} %param.4), channel_id=1, source_target_pairs={{0,2},{2,0},{4,6},{6,4},{8,10},{10,8},{12,14},{14,12},{1,3},{3,1},... | collective-permute-start | bytes 393224 | tf_op jit(solution)/shard_map/ppermute | solution.py:36
  7.6 0.9 %constant_dynamic-update-slice_fusion.7 = bf16[128,4096]{1,0:T(8,128)(2,1)S(1)} fusion(bf16[16,4096]{1,0:T(8,128)(2,1)} %param.4), kind=kLoop, calls=%fused_computation.10 | loop fusion | bytes 262144
  8.5 0.7 %collective-permute-done.2 = bf16[16,4096]{1,0:T(8,128)(2,1)S(1)} collective-permute-done((bf16[16,4096]{1,0:T(8,128)(2,1)}, bf16[16,4096]{1,0:T(8,128)(2,1)S(1)}, u32[]{:S(2)}, u32[]{:S(2)}) %collective-permute-start.2) | collective-permute-done | bytes 131104 | tf_op jit(solution)/shard_map/ppermute | solution.py:32
  9.3 1.5 %collective-permute-start.6 = (bf16[16,4096]{1,0:T(8,128)(2,1)S(1)}, bf16[16,4096]{1,0:T(8,128)(2,1)S(1)}, u32[]{:S(2)}, u32[]{:S(2)}) collective-permute-start(bf16[16,4096]{1,0:T(8,128)(2,1)S(1)} %collective-permute-done.2), channel_id=1, source_target_pairs={{0,2},{2,0},{4,6},{6,4},{8,10},{10,8},{12,14},{14,12},{1,3},{3,1},... | collective-permute-start | bytes 393224 | tf_op jit(solution)/shard_map/ppermute | solution.py:36
  10.8 5.7 %collective-permute-done.1 = bf16[16,4096]{1,0:T(8,128)(2,1)S(1)} collective-permute-done((bf16[16,4096]{1,0:T(8,128)(2,1)}, bf16[16,4096]{1,0:T(8,128)(2,1)S(1)}, u32[]{:S(2)}, u32[]{:S(2)}) %collective-permute-start.1) | collective-permute-done | bytes 131104 | tf_op jit(solution)/shard_map/ppermute | solution.py:32
  16.5 1.5 %collective-permute-start.5 = (bf16[16,4096]{1,0:T(8,128)(2,1)S(1)}, bf16[16,4096]{1,0:T(8,128)(2,1)S(1)}, u32[]{:S(2)}, u32[]{:S(2)}) collective-permute-start(bf16[16,4096]{1,0:T(8,128)(2,1)S(1)} %collective-permute-done.1), channel_id=1, source_target_pairs={{0,2},{2,0},{4,6},{6,4},{8,10},{10,8},{12,14},{14,12},{1,3},{3,1},... | collective-permute-start | bytes 393224 | tf_op jit(solution)/shard_map/ppermute | solution.py:36
  18.0 0.0 collective-permute-done
  18.0 0.5 %collective-permute-start.4 = (bf16[16,4096]{1,0:T(8,128)(2,1)S(1)}, bf16[16,4096]{1,0:T(8,128)(2,1)S(1)}, u32[]{:S(2)}, u32[]{:S(2)}) collective-permute-start(bf16[16,4096]{1,0:T(8,128)(2,1)S(1)} %collective-permute-done), channel_id=1, source_target_pairs={{0,2},{2,0},{4,6},{6,4},{8,10},{10,8},{12,14},{14,12},{1,3},{3,1},... | collective-permute-start | bytes 393224 | tf_op jit(solution)/shard_map/ppermute | solution.py:36
  18.5 0.0 collective-permute-done.3
  18.6 5.5 %collective-permute-done.4 = bf16[16,4096]{1,0:T(8,128)(2,1)S(1)} collective-permute-done((bf16[16,4096]{1,0:T(8,128)(2,1)S(1)}, bf16[16,4096]{1,0:T(8,128)(2,1)S(1)}, u32[]{:S(2)}, u32[]{:S(2)}) %collective-permute-start.4) | collective-permute-done | bytes 131104 | tf_op jit(solution)/shard_map/ppermute | solution.py:36
  24.0 0.0 collective-permute-done.5
  24.1 0.0 collective-permute-done.6
  24.1 0.0 copy-start.1
  24.1 3.1 %fusion.7 = f32[128,512]{1,0:T(8,128)S(1)} fusion(bf16[128,4096]{1,0:T(8,128)(2,1)S(1)} %constant_dynamic-update-slice_fusion, bf16[4096,512]{1,0:T(8,128)(2,1)} %param.6), kind=kOutput, calls=%fused_computation.16 | convolution fusion | flops 536870912 | bytes 5505024 | tf_op jit(solution)/shard_map/dot_general | solution.py:48
  27.2 0.0 copy-done
  27.2 0.7 %fusion.6 = f32[128,512]{1,0:T(8,128)S(1)} fusion(bf16[128,4096]{1,0:T(8,128)(2,1)S(1)} %constant_dynamic-update-slice_fusion, bf16[4096,512]{1,0:T(8,128)(2,1)S(1)} %copy-done), kind=kOutput, calls=%fused_computation.15 | convolution fusion | flops 536870912 | bytes 5505024 | tf_op jit(solution)/shard_map/dot_general | solution.py:47
  28.0 0.1 collective-permute-start.7
  28.1 0.5 collective-permute-start.8
  28.5 1.0 %collective-permute-done.7 = f32[128,512]{1,0:T(8,128)S(1)} collective-permute-done((f32[128,512]{1,0:T(8,128)S(1)}, f32[128,512]{1,0:T(8,128)S(1)}, u32[]{:S(2)}, u32[]{:S(2)}) %collective-permute-start.7) | collective-permute-done | bytes 262176 | tf_op jit(solution)/shard_map/ppermute | solution.py:40
  29.6 0.4 collective-permute-done.8
  29.9 0.0 copy-done.1
  30.0 0.7 %fusion.5 = (bf16[128,4096]{1,0:T(8,128)(2,1)S(1)}, f32[128,4096]{1,0:T(8,128)S(1)}) fusion(bf16[512,4096]{1,0:T(8,128)(2,1)S(1)} %copy-done.1, f32[128,512]{1,0:T(8,128)S(1)} %fusion.7, f32[128,512]{1,0:T(8,128)S(1)} %collective-permute-done.8, f32[128,512]{1,0:T(8,128)S(1)} %fusion.6, f32[128,512]{1,0:T(8,128)S(1)} %collective-permute-done.7), kind=kOutput, calls=%fused_computation.14 | convolution fusion | flops 537919488 | bytes 8388608 | tf_op jit(solution)/shard_map/dot_general | solution.py:52
  30.8 1.6 %collective-permute-start.13 = (bf16[16,4096]{1,0:T(8,128)(2,1)S(1)}, bf16[16,4096]{1,0:T(8,128)(2,1)S(1)}, u32[]{:S(2)}, u32[]{:S(2)}) collective-permute-start(bf16[16,4096]{1,0:T(8,128)(2,1)S(1)} %get-tuple-element.13), channel_id=1, source_target_pairs={{0,2},{2,0},{4,6},{6,4},{8,10},{10,8},{12,14},{14,12},{1,3},{3,1},... | collective-permute-start | bytes 393224 | tf_op jit(solution)/shard_map/ppermute | solution.py:36
  32.3 0.5 %collective-permute-start.11 = (bf16[16,4096]{1,0:T(8,128)(2,1)S(1)}, bf16[16,4096]{1,0:T(8,128)(2,1)S(1)}, u32[]{:S(2)}, u32[]{:S(2)}) collective-permute-start(bf16[16,4096]{1,0:T(8,128)(2,1)S(1)} %get-tuple-element.15), channel_id=1, source_target_pairs={{0,2},{2,0},{4,6},{6,4},{8,10},{10,8},{12,14},{14,12},{1,3},{3,1},... | collective-permute-start | bytes 393224 | tf_op jit(solution)/shard_map/ppermute | solution.py:36
  32.8 1.5 %collective-permute-start.9 = (bf16[16,4096]{1,0:T(8,128)(2,1)S(1)}, bf16[16,4096]{1,0:T(8,128)(2,1)S(1)}, u32[]{:S(2)}, u32[]{:S(2)}) collective-permute-start(bf16[16,4096]{1,0:T(8,128)(2,1)S(1)} %get-tuple-element.16), channel_id=1, source_target_pairs={{0,2},{2,0},{4,6},{6,4},{8,10},{10,8},{12,14},{14,12},{1,3},{3,1},... | collective-permute-start | bytes 393224 | tf_op jit(solution)/shard_map/ppermute | solution.py:36
  34.4 0.1 fusion.3
  34.4 2.7 %collective-permute-done.13.arrived_ref = bf16[16,4096]{1,0:T(8,128)(2,1)S(1)} collective-permute-done((bf16[16,4096]{1,0:T(8,128)(2,1)S(1)}, bf16[16,4096]{1,0:T(8,128)(2,1)S(1)}, u32[]{:S(2)}, u32[]{:S(2)}) %collective-permute-start.13) | collective-permute-done | bytes 131104 | tf_op jit(solution)/shard_map/ppermute | solution.py:36
  37.2 1.6 %collective-permute-start.15 = (bf16[16,4096]{1,0:T(8,128)(2,1)S(1)}, bf16[16,4096]{1,0:T(8,128)(2,1)S(1)}, u32[]{:S(2)}, u32[]{:S(2)}) collective-permute-start(bf16[16,4096]{1,0:T(8,128)(2,1)S(1)} %get-tuple-element.8), channel_id=1, source_target_pairs={{0,2},{2,0},{4,6},{6,4},{8,10},{10,8},{12,14},{14,12},{1,3},{3,1},... | collective-permute-start | bytes 393224 | tf_op jit(solution)/shard_map/ppermute | solution.py:36
  38.8 0.0 collective-permute-start.14
  38.8 1.1 %collective-permute-done.11.arrived_ref = bf16[16,4096]{1,0:T(8,128)(2,1)S(1)} collective-permute-done((bf16[16,4096]{1,0:T(8,128)(2,1)S(1)}, bf16[16,4096]{1,0:T(8,128)(2,1)S(1)}, u32[]{:S(2)}, u32[]{:S(2)}) %collective-permute-start.11) | collective-permute-done | bytes 131104 | tf_op jit(solution)/shard_map/ppermute | solution.py:36
  40.0 0.7 %collective-permute-start.12 = (bf16[16,4096]{1,0:T(8,128)(2,1)S(1)}, bf16[16,4096]{1,0:T(8,128)(2,1)S(1)}, u32[]{:S(2)}, u32[]{:S(2)}) collective-permute-start(bf16[16,4096]{1,0:T(8,128)(2,1)S(1)} %add_pair.8), channel_id=1, source_target_pairs={{0,12},{2,14},{4,0},{6,2},{8,4},{10,6},{12,8},{14,10},{1,13},{3,15... | collective-permute-start | bytes 393224 | tf_op jit(solution)/shard_map/ppermute | solution.py:32
  40.6 2.1 %collective-permute-done.9.arrived_ref = bf16[16,4096]{1,0:T(8,128)(2,1)S(1)} collective-permute-done((bf16[16,4096]{1,0:T(8,128)(2,1)S(1)}, bf16[16,4096]{1,0:T(8,128)(2,1)S(1)}, u32[]{:S(2)}, u32[]{:S(2)}) %collective-permute-start.9) | collective-permute-done | bytes 131104 | tf_op jit(solution)/shard_map/ppermute | solution.py:36
  42.8 0.1 collective-permute-start.10
  42.9 1.9 %collective-permute-done.15.arrived_ref = bf16[16,4096]{1,0:T(8,128)(2,1)S(1)} collective-permute-done((bf16[16,4096]{1,0:T(8,128)(2,1)S(1)}, bf16[16,4096]{1,0:T(8,128)(2,1)S(1)}, u32[]{:S(2)}, u32[]{:S(2)}) %collective-permute-start.15) | collective-permute-done | bytes 131104 | tf_op jit(solution)/shard_map/ppermute | solution.py:36
  44.8 1.7 %collective-permute-done.14.arrived_ref = bf16[16,4096]{1,0:T(8,128)(2,1)S(1)} collective-permute-done((bf16[16,4096]{1,0:T(8,128)(2,1)S(1)}, bf16[16,4096]{1,0:T(8,128)(2,1)S(1)}, u32[]{:S(2)}, u32[]{:S(2)}) %collective-permute-start.14) | collective-permute-done | bytes 131104 | tf_op jit(solution)/shard_map/ppermute | solution.py:32
  46.6 1.2 %collective-permute-done.12.arrived_ref = bf16[16,4096]{1,0:T(8,128)(2,1)S(1)} collective-permute-done((bf16[16,4096]{1,0:T(8,128)(2,1)S(1)}, bf16[16,4096]{1,0:T(8,128)(2,1)S(1)}, u32[]{:S(2)}, u32[]{:S(2)}) %collective-permute-start.12) | collective-permute-done | bytes 131104 | tf_op jit(solution)/shard_map/ppermute | solution.py:32
  47.8 1.9 %collective-permute-done.10.arrived_ref = bf16[16,4096]{1,0:T(8,128)(2,1)S(1)} collective-permute-done((bf16[16,4096]{1,0:T(8,128)(2,1)S(1)}, bf16[16,4096]{1,0:T(8,128)(2,1)S(1)}, u32[]{:S(2)}, u32[]{:S(2)}) %collective-permute-start.10) | collective-permute-done | bytes 131104 | tf_op jit(solution)/shard_map/ppermute | solution.py:32
  49.7 0.7 %add_pair.13 = bf16[16,4096]{1,0:T(8,128)(2,1)} custom-call(bf16[16,4096]{1,0:T(8,128)(2,1)S(1)} %collective-permute-done.10.arrived_ref, f32[16,4096]{1,0:T(8,128)S(1)} %add_pair.12.own_ref), custom_call_target="tpu_custom_call" | custom-call | flops 1500000000 | tf_op jit(solution)/shard_map/add_pair/pallas_call | solution.py:17
  (14 shorter events, 0.3 us)
Async XLA Ops:
  0.0 27.2 %copy-start = (bf16[4096,512]{1,0:T(8,128)(2,1)S(1)}, bf16[4096,512]{1,0:T(8,128)(2,1)}, u32[]{:S(2)}) copy-start(bf16[4096,512]{1,0:T(8,128)(2,1)} %param.5) | copy-start | bytes 12582916
  0.0 9.3 %collective-permute-start.2 = (bf16[16,4096]{1,0:T(8,128)(2,1)}, bf16[16,4096]{1,0:T(8,128)(2,1)S(1)}, u32[]{:S(2)}, u32[]{:S(2)}) collective-permute-start(bf16[16,4096]{1,0:T(8,128)(2,1)} %param.4), channel_id=1, source_target_pairs={{0,12},{2,14},{4,0},{6,2},{8,4},{10,6},{12,8},{14,10},{1,13},{3,15... | collective-permute-start | bytes 393224 | tf_op jit(solution)/shard_map/ppermute | solution.py:32
  5.1 11.4 %collective-permute-start.1 = (bf16[16,4096]{1,0:T(8,128)(2,1)}, bf16[16,4096]{1,0:T(8,128)(2,1)S(1)}, u32[]{:S(2)}, u32[]{:S(2)}) collective-permute-start(bf16[16,4096]{1,0:T(8,128)(2,1)} %param.4), channel_id=1, source_target_pairs={{0,8},{2,10},{4,12},{6,14},{8,0},{10,2},{12,4},{14,6},{1,9},{3,11}... | collective-permute-start | bytes 393224 | tf_op jit(solution)/shard_map/ppermute | solution.py:32
  5.1 12.9 %collective-permute-start = (bf16[16,4096]{1,0:T(8,128)(2,1)}, bf16[16,4096]{1,0:T(8,128)(2,1)S(1)}, u32[]{:S(2)}, u32[]{:S(2)}) collective-permute-start(bf16[16,4096]{1,0:T(8,128)(2,1)} %param.4), channel_id=1, source_target_pairs={{0,4},{2,6},{4,8},{6,10},{8,12},{10,14},{12,0},{14,2},{1,5},{3,7},... | collective-permute-start | bytes 393224 | tf_op jit(solution)/shard_map/ppermute | solution.py:32
  6.1 12.5 %collective-permute-start.3 = (bf16[16,4096]{1,0:T(8,128)(2,1)}, bf16[16,4096]{1,0:T(8,128)(2,1)S(1)}, u32[]{:S(2)}, u32[]{:S(2)}) collective-permute-start(bf16[16,4096]{1,0:T(8,128)(2,1)} %param.4), channel_id=1, source_target_pairs={{0,2},{2,0},{4,6},{6,4},{8,10},{10,8},{12,14},{14,12},{1,3},{3,1},... | collective-permute-start | bytes 393224 | tf_op jit(solution)/shard_map/ppermute | solution.py:36
  9.3 14.8 %collective-permute-start.6 = (bf16[16,4096]{1,0:T(8,128)(2,1)S(1)}, bf16[16,4096]{1,0:T(8,128)(2,1)S(1)}, u32[]{:S(2)}, u32[]{:S(2)}) collective-permute-start(bf16[16,4096]{1,0:T(8,128)(2,1)S(1)} %collective-permute-done.2), channel_id=1, source_target_pairs={{0,2},{2,0},{4,6},{6,4},{8,10},{10,8},{12,14},{14,12},{1,3},{3,1},... | collective-permute-start | bytes 393224 | tf_op jit(solution)/shard_map/ppermute | solution.py:36
  16.5 7.6 %collective-permute-start.5 = (bf16[16,4096]{1,0:T(8,128)(2,1)S(1)}, bf16[16,4096]{1,0:T(8,128)(2,1)S(1)}, u32[]{:S(2)}, u32[]{:S(2)}) collective-permute-start(bf16[16,4096]{1,0:T(8,128)(2,1)S(1)} %collective-permute-done.1), channel_id=1, source_target_pairs={{0,2},{2,0},{4,6},{6,4},{8,10},{10,8},{12,14},{14,12},{1,3},{3,1},... | collective-permute-start | bytes 393224 | tf_op jit(solution)/shard_map/ppermute | solution.py:36
  18.0 6.0 %collective-permute-start.4 = (bf16[16,4096]{1,0:T(8,128)(2,1)S(1)}, bf16[16,4096]{1,0:T(8,128)(2,1)S(1)}, u32[]{:S(2)}, u32[]{:S(2)}) collective-permute-start(bf16[16,4096]{1,0:T(8,128)(2,1)S(1)} %collective-permute-done), channel_id=1, source_target_pairs={{0,2},{2,0},{4,6},{6,4},{8,10},{10,8},{12,14},{14,12},{1,3},{3,1},... | collective-permute-start | bytes 393224 | tf_op jit(solution)/shard_map/ppermute | solution.py:36
  24.1 5.8 %copy-start.1 = (bf16[512,4096]{1,0:T(8,128)(2,1)S(1)}, bf16[512,4096]{1,0:T(8,128)(2,1)}, u32[]{:S(2)}) copy-start(bf16[512,4096]{1,0:T(8,128)(2,1)} %param.7) | copy-start | bytes 12582916
  28.0 1.6 %collective-permute-start.7 = (f32[128,512]{1,0:T(8,128)S(1)}, f32[128,512]{1,0:T(8,128)S(1)}, u32[]{:S(2)}, u32[]{:S(2)}) collective-permute-start(f32[128,512]{1,0:T(8,128)S(1)} %fusion.6), channel_id=1, source_target_pairs={{0,1},{1,0},{2,3},{3,2},{4,5},{5,4},{6,7},{7,6},{8,9},{9,8},{10,11... | collective-permute-start | bytes 786440 | tf_op jit(solution)/shard_map/ppermute | solution.py:40
  28.1 1.9 %collective-permute-start.8 = (f32[128,512]{1,0:T(8,128)S(1)}, f32[128,512]{1,0:T(8,128)S(1)}, u32[]{:S(2)}, u32[]{:S(2)}) collective-permute-start(f32[128,512]{1,0:T(8,128)S(1)} %fusion.7), channel_id=1, source_target_pairs={{0,1},{1,0},{2,3},{3,2},{4,5},{5,4},{6,7},{7,6},{8,9},{9,8},{10,11... | collective-permute-start | bytes 786440 | tf_op jit(solution)/shard_map/ppermute | solution.py:40
  30.8 6.4 %collective-permute-start.13 = (bf16[16,4096]{1,0:T(8,128)(2,1)S(1)}, bf16[16,4096]{1,0:T(8,128)(2,1)S(1)}, u32[]{:S(2)}, u32[]{:S(2)}) collective-permute-start(bf16[16,4096]{1,0:T(8,128)(2,1)S(1)} %get-tuple-element.13), channel_id=1, source_target_pairs={{0,2},{2,0},{4,6},{6,4},{8,10},{10,8},{12,14},{14,12},{1,3},{3,1},... | collective-permute-start | bytes 393224 | tf_op jit(solution)/shard_map/ppermute | solution.py:36
  32.3 7.6 %collective-permute-start.11 = (bf16[16,4096]{1,0:T(8,128)(2,1)S(1)}, bf16[16,4096]{1,0:T(8,128)(2,1)S(1)}, u32[]{:S(2)}, u32[]{:S(2)}) collective-permute-start(bf16[16,4096]{1,0:T(8,128)(2,1)S(1)} %get-tuple-element.15), channel_id=1, source_target_pairs={{0,2},{2,0},{4,6},{6,4},{8,10},{10,8},{12,14},{14,12},{1,3},{3,1},... | collective-permute-start | bytes 393224 | tf_op jit(solution)/shard_map/ppermute | solution.py:36
  32.8 9.9 %collective-permute-start.9 = (bf16[16,4096]{1,0:T(8,128)(2,1)S(1)}, bf16[16,4096]{1,0:T(8,128)(2,1)S(1)}, u32[]{:S(2)}, u32[]{:S(2)}) collective-permute-start(bf16[16,4096]{1,0:T(8,128)(2,1)S(1)} %get-tuple-element.16), channel_id=1, source_target_pairs={{0,2},{2,0},{4,6},{6,4},{8,10},{10,8},{12,14},{14,12},{1,3},{3,1},... | collective-permute-start | bytes 393224 | tf_op jit(solution)/shard_map/ppermute | solution.py:36
  37.2 7.6 %collective-permute-start.15 = (bf16[16,4096]{1,0:T(8,128)(2,1)S(1)}, bf16[16,4096]{1,0:T(8,128)(2,1)S(1)}, u32[]{:S(2)}, u32[]{:S(2)}) collective-permute-start(bf16[16,4096]{1,0:T(8,128)(2,1)S(1)} %get-tuple-element.8), channel_id=1, source_target_pairs={{0,2},{2,0},{4,6},{6,4},{8,10},{10,8},{12,14},{14,12},{1,3},{3,1},... | collective-permute-start | bytes 393224 | tf_op jit(solution)/shard_map/ppermute | solution.py:36
  38.8 7.8 %collective-permute-start.14 = (bf16[16,4096]{1,0:T(8,128)(2,1)S(1)}, bf16[16,4096]{1,0:T(8,128)(2,1)S(1)}, u32[]{:S(2)}, u32[]{:S(2)}) collective-permute-start(bf16[16,4096]{1,0:T(8,128)(2,1)S(1)} %add_pair.9), channel_id=1, source_target_pairs={{0,8},{2,10},{4,12},{6,14},{8,0},{10,2},{12,4},{14,6},{1,9},{3,11}... | collective-permute-start | bytes 393224 | tf_op jit(solution)/shard_map/ppermute | solution.py:32
  40.0 7.8 %collective-permute-start.12 = (bf16[16,4096]{1,0:T(8,128)(2,1)S(1)}, bf16[16,4096]{1,0:T(8,128)(2,1)S(1)}, u32[]{:S(2)}, u32[]{:S(2)}) collective-permute-start(bf16[16,4096]{1,0:T(8,128)(2,1)S(1)} %add_pair.8), channel_id=1, source_target_pairs={{0,12},{2,14},{4,0},{6,2},{8,4},{10,6},{12,8},{14,10},{1,13},{3,15... | collective-permute-start | bytes 393224 | tf_op jit(solution)/shard_map/ppermute | solution.py:32
  42.8 6.9 %collective-permute-start.10 = (bf16[16,4096]{1,0:T(8,128)(2,1)S(1)}, bf16[16,4096]{1,0:T(8,128)(2,1)S(1)}, u32[]{:S(2)}, u32[]{:S(2)}) collective-permute-start(bf16[16,4096]{1,0:T(8,128)(2,1)S(1)} %add_pair.7), channel_id=1, source_target_pairs={{0,4},{2,6},{4,8},{6,10},{8,12},{10,14},{12,0},{14,2},{1,5},{3,7},... | collective-permute-start | bytes 393224 | tf_op jit(solution)/shard_map/ppermute | solution.py:32

commit v4 on v2

v4 whole, which is shorter than its diff:
```python
import functools

import jax
import jax.numpy as jnp
from jax import lax
from jax.experimental import pallas as pl
from jax.experimental.pallas import tpu as pltpu
from jax.sharding import PartitionSpec as P

F32 = jnp.float32
BF16 = jnp.bfloat16


def call(kernel, name, out_shape, flops, vmem, *operands):
    return pl.pallas_call(
        kernel,
        out_shape=out_shape,
        compiler_params=pltpu.CompilerParams(vmem_limit_bytes=vmem),
        cost_estimate=pl.CostEstimate(flops=flops, bytes_accessed=0, transcendentals=0),
        name=name,
    )(*operands)


def fetch_kernel(pieces, *refs):
    count = (len(refs) - 1) // 2
    sems = refs[-1]
    copies = []
    for n in range(count):
        source, target = refs[n], refs[count + n]
        step = source.shape[0] // pieces
        for i in range(pieces):
            part = pl.ds(i * step, step)
            copies.append(pltpu.make_async_copy(source.at[part], target.at[part], sems.at[n, i]))
    for copy in copies:
        copy.start()
    for copy in copies:
        copy.wait()


def fetch(weights, pieces=4):
    return pl.pallas_call(
        functools.partial(fetch_kernel, pieces),
        in_specs=[pl.BlockSpec(memory_space=pl.ANY)] * len(weights),
        out_specs=[pl.BlockSpec(memory_space=pltpu.VMEM)] * len(weights),
        out_shape=[jax.ShapeDtypeStruct(w.shape, w.dtype) for w in weights],
        scratch_shapes=[pltpu.SemaphoreType.DMA((len(weights), pieces))],
        compiler_params=pltpu.CompilerParams(vmem_limit_bytes=43 << 20),
        cost_estimate=pl.CostEstimate(flops=1000000000, bytes_accessed=0, transcendentals=0),
        name="fetch",
    )(*weights)


def project_kernel(*refs):
    *block_refs, weight_ref, out_ref = refs
    rows = jnp.concatenate([ref[...] for ref in block_refs], axis=0)
    out_ref[...] = jnp.dot(rows, weight_ref[...], preferred_element_type=F32)


def project(blocks, weight):
    rows = sum(block.shape[0] for block in blocks)
    out = jax.ShapeDtypeStruct((rows, weight.shape[1]), F32)
    flops = 2 * rows * weight.shape[0] * weight.shape[1]
    return call(project_kernel, "project", out, flops, 4 << 20, *blocks, weight)


def down_kernel(give, keep, gate_ref, gate_other_ref, up_ref, up_other_ref, weight_ref, *out_refs):
    gate_sum = gate_ref[...] + gate_other_ref[...]
    up_sum = up_ref[...] + up_other_ref[...]
    hidden = (jax.nn.silu(gate_sum) * up_sum).astype(BF16)
    width = weight_ref.shape[1]
    tile = min(512, width)
    rows = out_refs[0].shape[0]

    def column_tile(step, carry):
        columns = pl.ds(pl.multiple_of(step * tile, tile), tile)
        partial = jnp.dot(hidden, weight_ref[:, columns], preferred_element_type=F32)
        for k in range(keep + give):
            piece = partial[k * rows:(k + 1) * rows]
            out_refs[k][:, columns] = piece.astype(out_refs[k].dtype)
        return carry

    lax.fori_loop(0, width // tile, column_tile, 0, unroll=True)


def down(gate, gate_other, up, up_other, weight, rows, keep, give):
    width = weight.shape[1]
    outs = [jax.ShapeDtypeStruct((rows, width), F32)] * keep
    outs += [jax.ShapeDtypeStruct((rows, width), BF16)] * give
    flops = 2 * gate.shape[0] * weight.shape[0] * width
    return call(
        functools.partial(down_kernel, give, keep), "down", outs, flops, 4 << 20,
        gate, gate_other, up, up_other, weight,
    )


def pair_kernel(arrived_ref, own_ref, out_ref):
    out_ref[...] = (own_ref[...] + arrived_ref[...].astype(F32)).astype(out_ref.dtype)


def add_pair(arrived, own, dtype, flops):
    out = jax.ShapeDtypeStruct(own.shape, dtype)
    return call(pair_kernel, "add_pair", out, flops, 2 << 20, arrived, own)


def make_local(wide, narrow):
    inner = 2 if wide % 2 == 0 else 1
    outer = wide // inner

    def along_outer(value, step):
        pairs = [(i, (i + step * inner) % wide) for i in range(wide)]
        return lax.ppermute(value, "wide", pairs)

    def along_inner(value):
        pairs = [(i, i ^ 1) for i in range(wide)]
        return lax.ppermute(value, "wide", pairs)

    def across_cores(value):
        pairs = [(i, (i + 1) % narrow) for i in range(narrow)]
        return lax.ppermute(value, "narrow", pairs)

    def local(tokens, gate_weight, up_weight, down_weight):
        rows = tokens.shape[0]
        mine = [tokens] + [along_outer(tokens, k) for k in range(1, outer)]
        theirs = [along_inner(block) for block in mine] if inner == 2 else []
        gate_held, up_held = fetch([gate_weight, up_weight])
        gate_part = project(mine + theirs, gate_held)
        up_part = project(mine + theirs, up_held)
        blocks = down(
            gate_part, across_cores(gate_part), up_part, across_cores(up_part),
            down_weight, rows, len(mine), len(theirs),
        )
        order = sorted(range(1, outer), key=lambda k: -min(k, outer - k)) + [0]
        keep, give = list(blocks[:outer]), list(blocks[outer:])
        sent = []
        for k in order:
            if give and k == 0 and sent:
                give[0], sent[0] = lax.optimization_barrier((give[0], sent[0]))
            pair = keep[k]
            if give:
                pair = add_pair(along_inner(give[k]), keep[k], BF16 if k else F32, 1000000)
            if k:
                sent.append(pair.astype(BF16))
            else:
                total = pair
        for k, value in zip(order, sent):
            last = k == order[-2]
            total = add_pair(along_outer(value, -k), total, BF16 if last else F32, 1500000000)
        return total.astype(BF16)

    return local


def solution(mesh):
    return jax.shard_map(
        make_local(mesh.shape["wide"], mesh.shape["narrow"]),
        mesh=mesh,
        in_specs=(
            P(("groups", "wide"), "narrow"),
            P("narrow", "wide"),
            P("narrow", "wide"),
            P("wide", "narrow"),
        ),
        out_specs=P(("groups", "wide"), "narrow"),
        check_vma=False,
    )
```

time: 57.6 us -> 48.9 us (0.85)
  waiting for transfers between devices: 15.1 us -> 24 us
  local copies, waits for them, and re-layouts: 6.67 us -> 0.01 us
  Pallas kernels: 12 us -> 6.46 us
  matrix products: 4.58 us -> 0 us
  starting transfers between devices: 18.9 us -> 18.2 us
    ppermute x6, waiting for transfers between devices: 6.42 us -> 13.1 us  [along_outer(): return lax.ppermute(value, 'wide', pairs)]
    unnamed x25 -> x4, local copies, waits for them, and re-layouts: 5.6 us -> 0.01 us
    pallas_call x7 -> x11, Pallas kernels: 12 us -> 6.46 us  [the longest x1 3.47 us: fetch(): pl.pallas_call(functools.partial(fetch_kernel, pieces), in_specs=[pl.Bloc...]
    dot_general x3 -> x0, matrix products: 4.58 us -> none  [the longest x1 3.12 us: local(): up_part = jnp.dot(all_rows, up_weight, preferred_element_type=F32)]
    ppermute x8, waiting for transfers between devices: 7.23 us -> 9.75 us  [along_inner(): return lax.ppermute(value, 'wide', pairs)]
    slice x2 -> x0, local copies, waits for them, and re-layouts: 1.06 us -> none  [local(): blocks = [partial[k * rows:(k + 1) * rows] for k in range(wide)]]
    ppermute x6, starting transfers between devices: 8.13 us -> 7.3 us  [along_outer(): return lax.ppermute(value, 'wide', pairs)]
  transfers between devices with their start and end apart: 16 -> 16, of which waited for: 6 -> 12; matrix products, arithmetic and copies ran while one was open for 4% -> 0% of each run, Pallas kernels for 18% -> 9%
where the time goes in v4:
time: 48.9 us; the launch traced here: 48.8 us
  waiting for transfers between devices  24 us (49%)
  starting transfers between devices  18.2 us (37%)
  Pallas kernels  6.46 us (13%)
    ppermute x6, waiting for transfers between devices, along_outer(): return lax.ppermute(value, 'wide', pairs)  13.1 us
    ppermute x8, starting transfers between devices, along_inner(): return lax.ppermute(value, 'wide', pairs)  10.3 us
    ppermute x8, waiting for transfers between devices, along_inner(): return lax.ppermute(value, 'wide', pairs)  9.75 us
    ppermute x6, starting transfers between devices, along_outer(): return lax.ppermute(value, 'wide', pairs)  7.3 us
    pallas_call x1, Pallas kernels, fetch(): pl.pallas_call(functools.partial(fetch_kernel, pieces), in_specs=[pl.Bloc...  3.47 us
    pallas_call x10, Pallas kernels, call(): pl.pallas_call(kernel, out_shape=out_shape, compiler_params=pltpu.Compile...  2.99 us
    ppermute x2, waiting for transfers between devices, across_cores(): return lax.ppermute(value, 'narrow', pairs)  1.16 us
  transfers between devices with their start and end apart: 16, of which 12 were waited for; matrix products, arithmetic and copies ran while one was open for 0% of the time, Pallas kernels for 9%

profile of v4, /device:TPU:0, one launch (start us, length us, event | category | flops | bytes accessed | tf_op | source)
XLA Modules:
  0.0 48.8 jit_solution(11631485503674739931)
XLA Ops:
  0.0 0.0 copy-start.1
  0.0 5.0 %collective-permute-start.2 = (bf16[16,4096]{1,0:T(8,128)(2,1)}, bf16[16,4096]{1,0:T(8,128)(2,1)S(1)}, u32[]{:S(2)}, u32[]{:S(2)}) collective-permute-start(bf16[16,4096]{1,0:T(8,128)(2,1)} %refs_0_.5), channel_id=1, source_target_pairs={{0,12},{2,14},{4,0},{6,2},{8,4},{10,6},{12,8},{14,10},{1,13},{3,15... | collective-permute-start | bytes 393224 | tf_op jit(solution)/shard_map/ppermute | solution.py:111
  5.1 0.0 collective-permute-start.1
  5.1 1.0 %collective-permute-start = (bf16[16,4096]{1,0:T(8,128)(2,1)}, bf16[16,4096]{1,0:T(8,128)(2,1)S(1)}, u32[]{:S(2)}, u32[]{:S(2)}) collective-permute-start(bf16[16,4096]{1,0:T(8,128)(2,1)} %refs_0_.5), channel_id=1, source_target_pairs={{0,4},{2,6},{4,8},{6,10},{8,12},{10,14},{12,0},{14,2},{1,5},{3,7},... | collective-permute-start | bytes 393224 | tf_op jit(solution)/shard_map/ppermute | solution.py:111
  6.1 1.5 %collective-permute-start.3 = (bf16[16,4096]{1,0:T(8,128)(2,1)}, bf16[16,4096]{1,0:T(8,128)(2,1)S(1)}, u32[]{:S(2)}, u32[]{:S(2)}) collective-permute-start(bf16[16,4096]{1,0:T(8,128)(2,1)} %refs_0_.5), channel_id=1, source_target_pairs={{0,2},{2,0},{4,6},{6,4},{8,10},{10,8},{12,14},{14,12},{1,3},{3,1},... | collective-permute-start | bytes 393224 | tf_op jit(solution)/shard_map/ppermute | solution.py:115
  7.6 1.7 %collective-permute-done.2.refs_3_ = bf16[16,4096]{1,0:T(8,128)(2,1)S(1)} collective-permute-done((bf16[16,4096]{1,0:T(8,128)(2,1)}, bf16[16,4096]{1,0:T(8,128)(2,1)S(1)}, u32[]{:S(2)}, u32[]{:S(2)}) %collective-permute-start.2) | collective-permute-done | bytes 131104 | tf_op jit(solution)/shard_map/ppermute | solution.py:111
  9.3 1.5 %collective-permute-start.6 = (bf16[16,4096]{1,0:T(8,128)(2,1)S(1)}, bf16[16,4096]{1,0:T(8,128)(2,1)S(1)}, u32[]{:S(2)}, u32[]{:S(2)}) collective-permute-start(bf16[16,4096]{1,0:T(8,128)(2,1)S(1)} %collective-permute-done.2.refs_3_), channel_id=1, source_target_pairs={{0,2},{2,0},{4,6},{6,4},{8,10},{10,8},{12,14},{14,12},{1,3},{3,1},... | collective-permute-start | bytes 393224 | tf_op jit(solution)/shard_map/ppermute | solution.py:115
  10.8 5.7 %collective-permute-done.1.refs_2_ = bf16[16,4096]{1,0:T(8,128)(2,1)S(1)} collective-permute-done((bf16[16,4096]{1,0:T(8,128)(2,1)}, bf16[16,4096]{1,0:T(8,128)(2,1)S(1)}, u32[]{:S(2)}, u32[]{:S(2)}) %collective-permute-start.1) | collective-permute-done | bytes 131104 | tf_op jit(solution)/shard_map/ppermute | solution.py:111
  16.5 1.5 %collective-permute-start.5 = (bf16[16,4096]{1,0:T(8,128)(2,1)S(1)}, bf16[16,4096]{1,0:T(8,128)(2,1)S(1)}, u32[]{:S(2)}, u32[]{:S(2)}) collective-permute-start(bf16[16,4096]{1,0:T(8,128)(2,1)S(1)} %collective-permute-done.1.refs_2_), channel_id=1, source_target_pairs={{0,2},{2,0},{4,6},{6,4},{8,10},{10,8},{12,14},{14,12},{1,3},{3,1},... | collective-permute-start | bytes 393224 | tf_op jit(solution)/shard_map/ppermute | solution.py:115
  18.0 0.0 collective-permute-done.refs_1_
  18.0 0.5 %collective-permute-start.4 = (bf16[16,4096]{1,0:T(8,128)(2,1)S(1)}, bf16[16,4096]{1,0:T(8,128)(2,1)S(1)}, u32[]{:S(2)}, u32[]{:S(2)}) collective-permute-start(bf16[16,4096]{1,0:T(8,128)(2,1)S(1)} %collective-permute-done.refs_1_), channel_id=1, source_target_pairs={{0,2},{2,0},{4,6},{6,4},{8,10},{10,8},{12,14},{14,12},{1,3},{3,1},... | collective-permute-start | bytes 393224 | tf_op jit(solution)/shard_map/ppermute | solution.py:115
  18.5 3.5 %fetch.1 = (bf16[4096,512]{1,0:T(8,128)(2,1)S(1)}, bf16[4096,512]{1,0:T(8,128)(2,1)S(1)}) custom-call(bf16[4096,512]{1,0:T(8,128)(2,1)} %refs_0_.3, bf16[4096,512]{1,0:T(8,128)(2,1)} %refs_1_.1), custom_call_target="tpu_custom_call" | custom-call | flops 1000000000 | tf_op jit(solution)/shard_map/fetch/pallas_call | solution.py:41
  22.0 0.0 collective-permute-done.3.refs_4_
  22.0 0.0 collective-permute-done.6.refs_7_
  22.0 0.6 %collective-permute-done.5.refs_6_ = bf16[16,4096]{1,0:T(8,128)(2,1)S(1)} collective-permute-done((bf16[16,4096]{1,0:T(8,128)(2,1)S(1)}, bf16[16,4096]{1,0:T(8,128)(2,1)S(1)}, u32[]{:S(2)}, u32[]{:S(2)}) %collective-permute-start.5) | collective-permute-done | bytes 131104 | tf_op jit(solution)/shard_map/ppermute | solution.py:115
  22.6 1.4 %collective-permute-done.4.refs_5_ = bf16[16,4096]{1,0:T(8,128)(2,1)S(1)} collective-permute-done((bf16[16,4096]{1,0:T(8,128)(2,1)S(1)}, bf16[16,4096]{1,0:T(8,128)(2,1)S(1)}, u32[]{:S(2)}, u32[]{:S(2)}) %collective-permute-start.4) | collective-permute-done | bytes 131104 | tf_op jit(solution)/shard_map/ppermute | solution.py:115
  24.0 0.0 copy-done.1
  24.0 0.0 copy-start
  24.0 0.7 %project.3.up_ref = f32[128,512]{1,0:T(8,128)S(1)} custom-call(bf16[16,4096]{1,0:T(8,128)(2,1)S(1)} %copy-done.1, bf16[16,4096]{1,0:T(8,128)(2,1)S(1)} %collective-permute-done.refs_1_, bf16[16,4096]{1,0:T(8,128)(2,1)S(1)} %collective-permute-done.1.refs_2_, bf16[16,4096]{1,0:T(8,128)(2,1)S(1)} %collective-permute-done.2.refs_3_, ...), custom_call_target="tpu_custom_call" | custom-call | flops 536870912 | tf_op jit(solution)/shard_map/project/pallas_call | solution.py:15
  24.8 0.1 collective-permute-start.8
  24.8 0.7 %project.2.gate_ref = f32[128,512]{1,0:T(8,128)S(1)} custom-call(bf16[16,4096]{1,0:T(8,128)(2,1)S(1)} %copy-done.1, bf16[16,4096]{1,0:T(8,128)(2,1)S(1)} %collective-permute-done.refs_1_, bf16[16,4096]{1,0:T(8,128)(2,1)S(1)} %collective-permute-done.1.refs_2_, bf16[16,4096]{1,0:T(8,128)(2,1)S(1)} %collective-permute-done.2.refs_3_, ...), custom_call_target="tpu_custom_call" | custom-call | flops 536870912 | tf_op jit(solution)/shard_map/project/pallas_call | solution.py:15
  25.6 0.6 %collective-permute-start.7 = (f32[128,512]{1,0:T(8,128)S(1)}, f32[128,512]{1,0:T(8,128)S(1)}, u32[]{:S(2)}, u32[]{:S(2)}) collective-permute-start(f32[128,512]{1,0:T(8,128)S(1)} %project.2.gate_ref), channel_id=1, source_target_pairs={{0,1},{1,0},{2,3},{3,2},{4,5},{5,4},{6,7},{7,6},{8,9},{9,8},{10,11... | collective-permute-start | bytes 786440 | tf_op jit(solution)/shard_map/ppermute | solution.py:119
  26.1 0.2 collective-permute-done.8.up_other_ref
  26.4 0.9 %collective-permute-done.7.gate_other_ref = f32[128,512]{1,0:T(8,128)S(1)} collective-permute-done((f32[128,512]{1,0:T(8,128)S(1)}, f32[128,512]{1,0:T(8,128)S(1)}, u32[]{:S(2)}, u32[]{:S(2)}) %collective-permute-start.7) | collective-permute-done | bytes 262176 | tf_op jit(solution)/shard_map/ppermute | solution.py:119
  27.3 0.0 copy-done
  27.3 0.7 %down.1 = (f32[16,4096]{1,0:T(8,128)S(1)}, f32[16,4096]{1,0:T(8,128)S(1)}, f32[16,4096]{1,0:T(8,128)S(1)}, f32[16,4096]{1,0:T(8,128)S(1)}, bf16[16,4096]{1,0:T(8...) custom-call(f32[128,512]{1,0:T(8,128)S(1)} %project.2.gate_ref, ...), custom_call_target="tpu_custom_call" | custom-call | flops 536870912 | tf_op jit(solution)/shard_map/down/pallas_call | solution.py:15
  28.0 1.6 %collective-permute-start.13 = (bf16[16,4096]{1,0:T(8,128)(2,1)S(1)}, bf16[16,4096]{1,0:T(8,128)(2,1)S(1)}, u32[]{:S(2)}, u32[]{:S(2)}) collective-permute-start(bf16[16,4096]{1,0:T(8,128)(2,1)S(1)} %get-tuple-element.24), channel_id=1, source_target_pairs={{0,2},{2,0},{4,6},{6,4},{8,10},{10,8},{12,14},{14,12},{1,3},{3,1},... | collective-permute-start | bytes 393224 | tf_op jit(solution)/shard_map/ppermute | solution.py:115
  29.6 0.5 %collective-permute-start.9 = (bf16[16,4096]{1,0:T(8,128)(2,1)S(1)}, bf16[16,4096]{1,0:T(8,128)(2,1)S(1)}, u32[]{:S(2)}, u32[]{:S(2)}) collective-permute-start(bf16[16,4096]{1,0:T(8,128)(2,1)S(1)} %get-tuple-element.19), channel_id=1, source_target_pairs={{0,2},{2,0},{4,6},{6,4},{8,10},{10,8},{12,14},{14,12},{1,3},{3,1},... | collective-permute-start | bytes 393224 | tf_op jit(solution)/shard_map/ppermute | solution.py:115
  30.1 1.5 %collective-permute-start.11 = (bf16[16,4096]{1,0:T(8,128)(2,1)S(1)}, bf16[16,4096]{1,0:T(8,128)(2,1)S(1)}, u32[]{:S(2)}, u32[]{:S(2)}) collective-permute-start(bf16[16,4096]{1,0:T(8,128)(2,1)S(1)} %get-tuple-element.21), channel_id=1, source_target_pairs={{0,2},{2,0},{4,6},{6,4},{8,10},{10,8},{12,14},{14,12},{1,3},{3,1},... | collective-permute-start | bytes 393224 | tf_op jit(solution)/shard_map/ppermute | solution.py:115
  31.7 2.8 %collective-permute-done.13.arrived_ref = bf16[16,4096]{1,0:T(8,128)(2,1)S(1)} collective-permute-done((bf16[16,4096]{1,0:T(8,128)(2,1)S(1)}, bf16[16,4096]{1,0:T(8,128)(2,1)S(1)}, u32[]{:S(2)}, u32[]{:S(2)}) %collective-permute-start.13) | collective-permute-done | bytes 131104 | tf_op jit(solution)/shard_map/ppermute | solution.py:115
  34.5 1.6 %collective-permute-start.15 = (bf16[16,4096]{1,0:T(8,128)(2,1)S(1)}, bf16[16,4096]{1,0:T(8,128)(2,1)S(1)}, u32[]{:S(2)}, u32[]{:S(2)}) collective-permute-start(bf16[16,4096]{1,0:T(8,128)(2,1)S(1)} %get-tuple-element.27), channel_id=1, source_target_pairs={{0,2},{2,0},{4,6},{6,4},{8,10},{10,8},{12,14},{14,12},{1,3},{3,1},... | collective-permute-start | bytes 393224 | tf_op jit(solution)/shard_map/ppermute | solution.py:115
  36.0 0.0 collective-permute-start.14
  36.1 1.2 %collective-permute-done.9.arrived_ref = bf16[16,4096]{1,0:T(8,128)(2,1)S(1)} collective-permute-done((bf16[16,4096]{1,0:T(8,128)(2,1)S(1)}, bf16[16,4096]{1,0:T(8,128)(2,1)S(1)}, u32[]{:S(2)}, u32[]{:S(2)}) %collective-permute-start.9) | collective-permute-done | bytes 131104 | tf_op jit(solution)/shard_map/ppermute | solution.py:115
  37.3 0.1 collective-permute-start.10
  37.3 2.7 %collective-permute-done.11.arrived_ref = bf16[16,4096]{1,0:T(8,128)(2,1)S(1)} collective-permute-done((bf16[16,4096]{1,0:T(8,128)(2,1)S(1)}, bf16[16,4096]{1,0:T(8,128)(2,1)S(1)}, u32[]{:S(2)}, u32[]{:S(2)}) %collective-permute-start.11) | collective-permute-done | bytes 131104 | tf_op jit(solution)/shard_map/ppermute | solution.py:115
  40.1 1.2 %collective-permute-start.12 = (bf16[16,4096]{1,0:T(8,128)(2,1)S(1)}, bf16[16,4096]{1,0:T(8,128)(2,1)S(1)}, u32[]{:S(2)}, u32[]{:S(2)}) collective-permute-start(bf16[16,4096]{1,0:T(8,128)(2,1)S(1)} %add_pair.8), channel_id=1, source_target_pairs={{0,12},{2,14},{4,0},{6,2},{8,4},{10,6},{12,8},{14,10},{1,13},{3,15... | collective-permute-start | bytes 393224 | tf_op jit(solution)/shard_map/ppermute | solution.py:111
  41.2 1.1 %collective-permute-done.15.arrived_ref = bf16[16,4096]{1,0:T(8,128)(2,1)S(1)} collective-permute-done((bf16[16,4096]{1,0:T(8,128)(2,1)S(1)}, bf16[16,4096]{1,0:T(8,128)(2,1)S(1)}, u32[]{:S(2)}, u32[]{:S(2)}) %collective-permute-start.15) | collective-permute-done | bytes 131104 | tf_op jit(solution)/shard_map/ppermute | solution.py:115
  42.3 3.9 %collective-permute-done.14.arrived_ref = bf16[16,4096]{1,0:T(8,128)(2,1)S(1)} collective-permute-done((bf16[16,4096]{1,0:T(8,128)(2,1)S(1)}, bf16[16,4096]{1,0:T(8,128)(2,1)S(1)}, u32[]{:S(2)}, u32[]{:S(2)}) %collective-permute-start.14) | collective-permute-done | bytes 131104 | tf_op jit(solution)/shard_map/ppermute | solution.py:111
  46.2 1.8 %collective-permute-done.12.arrived_ref = bf16[16,4096]{1,0:T(8,128)(2,1)S(1)} collective-permute-done((bf16[16,4096]{1,0:T(8,128)(2,1)S(1)}, bf16[16,4096]{1,0:T(8,128)(2,1)S(1)}, u32[]{:S(2)}, u32[]{:S(2)}) %collective-permute-start.12) | collective-permute-done | bytes 131104 | tf_op jit(solution)/shard_map/ppermute | solution.py:111
  48.1 0.0 collective-permute-done.10.arrived_ref
  48.1 0.7 %add_pair.13 = bf16[16,4096]{1,0:T(8,128)(2,1)} custom-call(bf16[16,4096]{1,0:T(8,128)(2,1)S(1)} %collective-permute-done.10.arrived_ref, f32[16,4096]{1,0:T(8,128)S(1)} %add_pair.12.own_ref), custom_call_target="tpu_custom_call" | custom-call | flops 1500000000 | tf_op jit(solution)/shard_map/add_pair/pallas_call | solution.py:15
  (6 shorter events, 0.1 us)
Async XLA Ops:
  0.0 24.0 %copy-start.1 = (bf16[16,4096]{1,0:T(8,128)(2,1)S(1)}, bf16[16,4096]{1,0:T(8,128)(2,1)}, u32[]{:S(2)}) copy-start(bf16[16,4096]{1,0:T(8,128)(2,1)} %refs_0_.5) | copy-start | bytes 393220
  0.0 9.3 %collective-permute-start.2 = (bf16[16,4096]{1,0:T(8,128)(2,1)}, bf16[16,4096]{1,0:T(8,128)(2,1)S(1)}, u32[]{:S(2)}, u32[]{:S(2)}) collective-permute-start(bf16[16,4096]{1,0:T(8,128)(2,1)} %refs_0_.5), channel_id=1, source_target_pairs={{0,12},{2,14},{4,0},{6,2},{8,4},{10,6},{12,8},{14,10},{1,13},{3,15... | collective-permute-start | bytes 393224 | tf_op jit(solution)/shard_map/ppermute | solution.py:111
  5.1 11.4 %collective-permute-start.1 = (bf16[16,4096]{1,0:T(8,128)(2,1)}, bf16[16,4096]{1,0:T(8,128)(2,1)S(1)}, u32[]{:S(2)}, u32[]{:S(2)}) collective-permute-start(bf16[16,4096]{1,0:T(8,128)(2,1)} %refs_0_.5), channel_id=1, source_target_pairs={{0,8},{2,10},{4,12},{6,14},{8,0},{10,2},{12,4},{14,6},{1,9},{3,11}... | collective-permute-start | bytes 393224 | tf_op jit(solution)/shard_map/ppermute | solution.py:111
  5.1 12.9 %collective-permute-start = (bf16[16,4096]{1,0:T(8,128)(2,1)}, bf16[16,4096]{1,0:T(8,128)(2,1)S(1)}, u32[]{:S(2)}, u32[]{:S(2)}) collective-permute-start(bf16[16,4096]{1,0:T(8,128)(2,1)} %refs_0_.5), channel_id=1, source_target_pairs={{0,4},{2,6},{4,8},{6,10},{8,12},{10,14},{12,0},{14,2},{1,5},{3,7},... | collective-permute-start | bytes 393224 | tf_op jit(solution)/shard_map/ppermute | solution.py:111
  6.1 15.9 %collective-permute-start.3 = (bf16[16,4096]{1,0:T(8,128)(2,1)}, bf16[16,4096]{1,0:T(8,128)(2,1)S(1)}, u32[]{:S(2)}, u32[]{:S(2)}) collective-permute-start(bf16[16,4096]{1,0:T(8,128)(2,1)} %refs_0_.5), channel_id=1, source_target_pairs={{0,2},{2,0},{4,6},{6,4},{8,10},{10,8},{12,14},{14,12},{1,3},{3,1},... | collective-permute-start | bytes 393224 | tf_op jit(solution)/shard_map/ppermute | solution.py:115
  9.3 12.7 %collective-permute-start.6 = (bf16[16,4096]{1,0:T(8,128)(2,1)S(1)}, bf16[16,4096]{1,0:T(8,128)(2,1)S(1)}, u32[]{:S(2)}, u32[]{:S(2)}) collective-permute-start(bf16[16,4096]{1,0:T(8,128)(2,1)S(1)} %collective-permute-done.2.refs_3_), channel_id=1, source_target_pairs={{0,2},{2,0},{4,6},{6,4},{8,10},{10,8},{12,14},{14,12},{1,3},{3,1},... | collective-permute-start | bytes 393224 | tf_op jit(solution)/shard_map/ppermute | solution.py:115
  16.5 6.2 %collective-permute-start.5 = (bf16[16,4096]{1,0:T(8,128)(2,1)S(1)}, bf16[16,4096]{1,0:T(8,128)(2,1)S(1)}, u32[]{:S(2)}, u32[]{:S(2)}) collective-permute-start(bf16[16,4096]{1,0:T(8,128)(2,1)S(1)} %collective-permute-done.1.refs_2_), channel_id=1, source_target_pairs={{0,2},{2,0},{4,6},{6,4},{8,10},{10,8},{12,14},{14,12},{1,3},{3,1},... | collective-permute-start | bytes 393224 | tf_op jit(solution)/shard_map/ppermute | solution.py:115
  18.0 6.0 %collective-permute-start.4 = (bf16[16,4096]{1,0:T(8,128)(2,1)S(1)}, bf16[16,4096]{1,0:T(8,128)(2,1)S(1)}, u32[]{:S(2)}, u32[]{:S(2)}) collective-permute-start(bf16[16,4096]{1,0:T(8,128)(2,1)S(1)} %collective-permute-done.refs_1_), channel_id=1, source_target_pairs={{0,2},{2,0},{4,6},{6,4},{8,10},{10,8},{12,14},{14,12},{1,3},{3,1},... | collective-permute-start | bytes 393224 | tf_op jit(solution)/shard_map/ppermute | solution.py:115
  24.0 3.2 %copy-start = (bf16[512,4096]{1,0:T(8,128)(2,1)S(1)}, bf16[512,4096]{1,0:T(8,128)(2,1)}, u32[]{:S(2)}) copy-start(bf16[512,4096]{1,0:T(8,128)(2,1)} %weight_ref.1) | copy-start | bytes 12582916
  24.8 1.6 %collective-permute-start.8 = (f32[128,512]{1,0:T(8,128)S(1)}, f32[128,512]{1,0:T(8,128)S(1)}, u32[]{:S(2)}, u32[]{:S(2)}) collective-permute-start(f32[128,512]{1,0:T(8,128)S(1)} %project.3.up_ref), channel_id=1, source_target_pairs={{0,1},{1,0},{2,3},{3,2},{4,5},{5,4},{6,7},{7,6},{8,9},{9,8},{10,11... | collective-permute-start | bytes 786440 | tf_op jit(solution)/shard_map/ppermute | solution.py:119
  25.6 1.7 %collective-permute-start.7 = (f32[128,512]{1,0:T(8,128)S(1)}, f32[128,512]{1,0:T(8,128)S(1)}, u32[]{:S(2)}, u32[]{:S(2)}) collective-permute-start(f32[128,512]{1,0:T(8,128)S(1)} %project.2.gate_ref), channel_id=1, source_target_pairs={{0,1},{1,0},{2,3},{3,2},{4,5},{5,4},{6,7},{7,6},{8,9},{9,8},{10,11... | collective-permute-start | bytes 786440 | tf_op jit(solution)/shard_map/ppermute | solution.py:119
  28.0 6.4 %collective-permute-start.13 = (bf16[16,4096]{1,0:T(8,128)(2,1)S(1)}, bf16[16,4096]{1,0:T(8,128)(2,1)S(1)}, u32[]{:S(2)}, u32[]{:S(2)}) collective-permute-start(bf16[16,4096]{1,0:T(8,128)(2,1)S(1)} %get-tuple-element.24), channel_id=1, source_target_pairs={{0,2},{2,0},{4,6},{6,4},{8,10},{10,8},{12,14},{14,12},{1,3},{3,1},... | collective-permute-start | bytes 393224 | tf_op jit(solution)/shard_map/ppermute | solution.py:115
  29.6 7.6 %collective-permute-start.9 = (bf16[16,4096]{1,0:T(8,128)(2,1)S(1)}, bf16[16,4096]{1,0:T(8,128)(2,1)S(1)}, u32[]{:S(2)}, u32[]{:S(2)}) collective-permute-start(bf16[16,4096]{1,0:T(8,128)(2,1)S(1)} %get-tuple-element.19), channel_id=1, source_target_pairs={{0,2},{2,0},{4,6},{6,4},{8,10},{10,8},{12,14},{14,12},{1,3},{3,1},... | collective-permute-start | bytes 393224 | tf_op jit(solution)/shard_map/ppermute | solution.py:115
  30.1 9.9 %collective-permute-start.11 = (bf16[16,4096]{1,0:T(8,128)(2,1)S(1)}, bf16[16,4096]{1,0:T(8,128)(2,1)S(1)}, u32[]{:S(2)}, u32[]{:S(2)}) collective-permute-start(bf16[16,4096]{1,0:T(8,128)(2,1)S(1)} %get-tuple-element.21), channel_id=1, source_target_pairs={{0,2},{2,0},{4,6},{6,4},{8,10},{10,8},{12,14},{14,12},{1,3},{3,1},... | collective-permute-start | bytes 393224 | tf_op jit(solution)/shard_map/ppermute | solution.py:115
  34.5 7.8 %collective-permute-start.15 = (bf16[16,4096]{1,0:T(8,128)(2,1)S(1)}, bf16[16,4096]{1,0:T(8,128)(2,1)S(1)}, u32[]{:S(2)}, u32[]{:S(2)}) collective-permute-start(bf16[16,4096]{1,0:T(8,128)(2,1)S(1)} %get-tuple-element.27), channel_id=1, source_target_pairs={{0,2},{2,0},{4,6},{6,4},{8,10},{10,8},{12,14},{14,12},{1,3},{3,1},... | collective-permute-start | bytes 393224 | tf_op jit(solution)/shard_map/ppermute | solution.py:115
  36.0 10.2 %collective-permute-start.14 = (bf16[16,4096]{1,0:T(8,128)(2,1)S(1)}, bf16[16,4096]{1,0:T(8,128)(2,1)S(1)}, u32[]{:S(2)}, u32[]{:S(2)}) collective-permute-start(bf16[16,4096]{1,0:T(8,128)(2,1)S(1)} %add_pair.9), channel_id=1, source_target_pairs={{0,8},{2,10},{4,12},{6,14},{8,0},{10,2},{12,4},{14,6},{1,9},{3,11}... | collective-permute-start | bytes 393224 | tf_op jit(solution)/shard_map/ppermute | solution.py:111
  37.3 10.9 %collective-permute-start.10 = (bf16[16,4096]{1,0:T(8,128)(2,1)S(1)}, bf16[16,4096]{1,0:T(8,128)(2,1)S(1)}, u32[]{:S(2)}, u32[]{:S(2)}) collective-permute-start(bf16[16,4096]{1,0:T(8,128)(2,1)S(1)} %add_pair.7), channel_id=1, source_target_pairs={{0,4},{2,6},{4,8},{6,10},{8,12},{10,14},{12,0},{14,2},{1,5},{3,7},... | collective-permute-start | bytes 393224 | tf_op jit(solution)/shard_map/ppermute | solution.py:111
  40.1 8.0 %collective-permute-start.12 = (bf16[16,4096]{1,0:T(8,128)(2,1)S(1)}, bf16[16,4096]{1,0:T(8,128)(2,1)S(1)}, u32[]{:S(2)}, u32[]{:S(2)}) collective-permute-start(bf16[16,4096]{1,0:T(8,128)(2,1)S(1)} %add_pair.8), channel_id=1, source_target_pairs={{0,12},{2,14},{4,0},{6,2},{8,4},{10,6},{12,8},{14,10},{1,13},{3,15... | collective-permute-start | bytes 393224 | tf_op jit(solution)/shard_map/ppermute | solution.py:111

commit v5 on v4

--- a/solution.py
+++ b/solution.py
@@ -118,33 +118,40 @@
         pairs = [(i, (i + 1) % narrow) for i in range(narrow)]
         return lax.ppermute(value, "narrow", pairs)
 
+    shifts = sorted(range(outer), key=lambda k: (min(k, outer - k), k))
+    near = [k for k in shifts if min(k, outer - k) <= outer // 4]
+    waves = [near, [k for k in shifts if k not in near]]
+
     def local(tokens, gate_weight, up_weight, down_weight):
         rows = tokens.shape[0]
-        mine = [tokens] + [along_outer(tokens, k) for k in range(1, outer)]
-        theirs = [along_inner(block) for block in mine] if inner == 2 else []
+        mine = {k: along_outer(tokens, k) if k else tokens for k in shifts}
+        theirs = {k: along_inner(mine[k]) for k in shifts} if inner == 2 else {}
         gate_held, up_held = fetch([gate_weight, up_weight])
-        gate_part = project(mine + theirs, gate_held)
-        up_part = project(mine + theirs, up_held)
-        blocks = down(
-            gate_part, across_cores(gate_part), up_part, across_cores(up_part),
-            down_weight, rows, len(mine), len(theirs),
-        )
-        order = sorted(range(1, outer), key=lambda k: -min(k, outer - k)) + [0]
-        keep, give = list(blocks[:outer]), list(blocks[outer:])
-        sent = []
-        for k in order:
-            if give and k == 0 and sent:
-                give[0], sent[0] = lax.optimization_barrier((give[0], sent[0]))
+        keep, give = {}, {}
+        for wave in waves:
+            if not wave:
+                continue
+            blocks = [mine[k] for k in wave] + [theirs[k] for k in wave if theirs]
+            gate_part = project(blocks, gate_held)
+            up_part = project(blocks, up_held)
+            outs = down(
+                gate_part, across_cores(gate_part), up_part, across_cores(up_part),
+                down_weight, rows, len(wave), len(blocks) - len(wave),
+            )
+            keep.update(zip(wave, outs[:len(wave)]))
+            give.update(zip(wave, outs[len(wave):]))
+        total = None
+        for k in shifts:
+            last = k == shifts[-1]
             pair = keep[k]
             if give:
                 pair = add_pair(along_inner(give[k]), keep[k], BF16 if k else F32, 1000000)
             if k:
-                sent.append(pair.astype(BF16))
+                arrived = along_outer(pair.astype(BF16), -k)
+                hint = 100000000 if k == shifts[1] else 5000000000
+                total = add_pair(arrived, total, BF16 if last else F32, hint)
             else:
                 total = pair
-        for k, value in zip(order, sent):
-            last = k == order[-2]
-            total = add_pair(along_outer(value, -k), total, BF16 if last else F32, 1500000000)
         return total.astype(BF16)
 
     return local

time: 48.9 us -> 47.8 us (0.978)
  waiting for transfers between devices: 24 us -> 18.3 us
  Pallas kernels: 6.46 us -> 9.14 us
  starting transfers between devices: 18.2 us -> 20.1 us
    ppermute x8, waiting for transfers between devices: 9.75 us -> 6.03 us  [along_inner(): return lax.ppermute(value, 'wide', pairs)]
    pallas_call x10 -> x13, Pallas kernels: 2.99 us -> 5.66 us  [call(): pl.pallas_call(kernel, out_shape=out_shape, compiler_params=pltpu.Compile...]
    ppermute x6, starting transfers between devices: 7.3 us -> 9.56 us  [along_outer(): return lax.ppermute(value, 'wide', pairs)]
    ppermute x6, waiting for transfers between devices: 13.1 us -> 11.4 us  [along_outer(): return lax.ppermute(value, 'wide', pairs)]
    ppermute x8, starting transfers between devices: 10.3 us -> 9.41 us  [along_inner(): return lax.ppermute(value, 'wide', pairs)]
    ppermute x2 -> x4, starting transfers between devices: 0.63 us -> 1.16 us  [across_cores(): return lax.ppermute(value, 'narrow', pairs)]
    ppermute x2 -> x4, waiting for transfers between devices: 1.16 us -> 0.91 us  [across_cores(): return lax.ppermute(value, 'narrow', pairs)]
  transfers between devices with their start and end apart: 16 -> 18, of which waited for: 12 -> 8; matrix products, arithmetic and copies ran while one was open for 0% -> 0% of each run, Pallas kernels for 9% -> 18%
where the time goes in v5:
time: 47.8 us; the launch traced here: 47.7 us
  starting transfers between devices  20.1 us (42%)
  waiting for transfers between devices  18.3 us (38%)
  Pallas kernels  9.14 us (19%)
    ppermute x6, waiting for transfers between devices, along_outer(): return lax.ppermute(value, 'wide', pairs)  11.4 us
    ppermute x6, starting transfers between devices, along_outer(): return lax.ppermute(value, 'wide', pairs)  9.56 us
    ppermute x8, starting transfers between devices, along_inner(): return lax.ppermute(value, 'wide', pairs)  9.41 us
    ppermute x8, waiting for transfers between devices, along_inner(): return lax.ppermute(value, 'wide', pairs)  6.03 us
    pallas_call x13, Pallas kernels, call(): pl.pallas_call(kernel, out_shape=out_shape, compiler_params=pltpu.Compile...  5.66 us
    pallas_call x1, Pallas kernels, fetch(): pl.pallas_call(functools.partial(fetch_kernel, pieces), in_specs=[pl.Bloc...  3.47 us
    ppermute x4, starting transfers between devices, across_cores(): return lax.ppermute(value, 'narrow', pairs)  1.16 us
  transfers between devices with their start and end apart: 18, of which 8 were waited for; matrix products, arithmetic and copies ran while one was open for 0% of the time, Pallas kernels for 18%

profile of v5, /device:TPU:0, one launch (start us, length us, event | category | flops | bytes accessed | tf_op | source)
XLA Modules:
  0.0 47.7 jit_solution(16191774501129828454)
XLA Ops:
  0.0 0.0 copy-start.1
  0.0 3.0 %collective-permute-start.6 = (bf16[16,4096]{1,0:T(8,128)(2,1)}, bf16[16,4096]{1,0:T(8,128)(2,1)S(1)}, u32[]{:S(2)}, u32[]{:S(2)}) collective-permute-start(bf16[16,4096]{1,0:T(8,128)(2,1)} %refs_0_.5), channel_id=1, source_target_pairs={{0,4},{2,6},{4,8},{6,10},{8,12},{10,14},{12,0},{14,2},{1,5},{3,7},... | collective-permute-start | bytes 393224 | tf_op jit(solution)/shard_map/ppermute | solution.py:111
  3.0 2.1 %collective-permute-start.7 = (bf16[16,4096]{1,0:T(8,128)(2,1)}, bf16[16,4096]{1,0:T(8,128)(2,1)S(1)}, u32[]{:S(2)}, u32[]{:S(2)}) collective-permute-start(bf16[16,4096]{1,0:T(8,128)(2,1)} %refs_0_.5), channel_id=1, source_target_pairs={{0,12},{2,14},{4,0},{6,2},{8,4},{10,6},{12,8},{14,10},{1,13},{3,15... | collective-permute-start | bytes 393224 | tf_op jit(solution)/shard_map/ppermute | solution.py:111
  5.1 1.7 %collective-permute-start.8 = (bf16[16,4096]{1,0:T(8,128)(2,1)}, bf16[16,4096]{1,0:T(8,128)(2,1)S(1)}, u32[]{:S(2)}, u32[]{:S(2)}) collective-permute-start(bf16[16,4096]{1,0:T(8,128)(2,1)} %refs_0_.5), channel_id=1, source_target_pairs={{0,2},{2,0},{4,6},{6,4},{8,10},{10,8},{12,14},{14,12},{1,3},{3,1},... | collective-permute-start | bytes 393224 | tf_op jit(solution)/shard_map/ppermute | solution.py:115
  6.8 2.9 %collective-permute-done.6.refs_1_ = bf16[16,4096]{1,0:T(8,128)(2,1)S(1)} collective-permute-done((bf16[16,4096]{1,0:T(8,128)(2,1)}, bf16[16,4096]{1,0:T(8,128)(2,1)S(1)}, u32[]{:S(2)}, u32[]{:S(2)}) %collective-permute-start.6) | collective-permute-done | bytes 131104 | tf_op jit(solution)/shard_map/ppermute | solution.py:111
  9.7 1.7 %collective-permute-start.9 = (bf16[16,4096]{1,0:T(8,128)(2,1)S(1)}, bf16[16,4096]{1,0:T(8,128)(2,1)S(1)}, u32[]{:S(2)}, u32[]{:S(2)}) collective-permute-start(bf16[16,4096]{1,0:T(8,128)(2,1)S(1)} %collective-permute-done.6.refs_1_), channel_id=1, source_target_pairs={{0,2},{2,0},{4,6},{6,4},{8,10},{10,8},{12,14},{14,12},{1,3},{3,1},... | collective-permute-start | bytes 393224 | tf_op jit(solution)/shard_map/ppermute | solution.py:115
  11.3 0.0 collective-permute-done.7.refs_2_
  11.4 1.2 %collective-permute-start.10 = (bf16[16,4096]{1,0:T(8,128)(2,1)S(1)}, bf16[16,4096]{1,0:T(8,128)(2,1)S(1)}, u32[]{:S(2)}, u32[]{:S(2)}) collective-permute-start(bf16[16,4096]{1,0:T(8,128)(2,1)S(1)} %collective-permute-done.7.refs_2_), channel_id=1, source_target_pairs={{0,2},{2,0},{4,6},{6,4},{8,10},{10,8},{12,14},{14,12},{1,3},{3,1},... | collective-permute-start | bytes 393224 | tf_op jit(solution)/shard_map/ppermute | solution.py:115
  12.5 1.8 %collective-permute-start = (bf16[16,4096]{1,0:T(8,128)(2,1)}, bf16[16,4096]{1,0:T(8,128)(2,1)S(1)}, u32[]{:S(2)}, u32[]{:S(2)}) collective-permute-start(bf16[16,4096]{1,0:T(8,128)(2,1)} %refs_0_.5), channel_id=1, source_target_pairs={{0,8},{2,10},{4,12},{6,14},{8,0},{10,2},{12,4},{14,6},{1,9},{3,11}... | collective-permute-start | bytes 393224 | tf_op jit(solution)/shard_map/ppermute | solution.py:111
  14.3 3.5 %fetch.1 = (bf16[4096,512]{1,0:T(8,128)(2,1)S(1)}, bf16[4096,512]{1,0:T(8,128)(2,1)S(1)}) custom-call(bf16[4096,512]{1,0:T(8,128)(2,1)} %refs_0_.3, bf16[4096,512]{1,0:T(8,128)(2,1)} %refs_1_.1), custom_call_target="tpu_custom_call" | custom-call | flops 1000000000 | tf_op jit(solution)/shard_map/fetch/pallas_call | solution.py:41
  17.8 0.0 collective-permute-done.8.refs_3_
  17.8 0.0 collective-permute-done.9.refs_4_
  17.8 0.0 collective-permute-done.10.refs_5_
  17.8 0.0 copy-done.1
  17.8 0.0 copy-start
  17.9 0.8 %project.6.gate_ref = f32[96,512]{1,0:T(8,128)S(1)} custom-call(bf16[16,4096]{1,0:T(8,128)(2,1)S(1)} %copy-done.1, bf16[16,4096]{1,0:T(8,128)(2,1)S(1)} %collective-permute-done.6.refs_1_, bf16[16,4096]{1,0:T(8,128)(2,1)S(1)} %collective-permute-done.7.refs_2_, bf16[16,4096]{1,0:T(8,128)(2,1)S(1)} %collective-permute-done.8.refs_3_, ...), custom_call_target="tpu_custom_call" | custom-call | flops 402653184 | tf_op jit(solution)/shard_map/project/pallas_call | solution.py:15
  18.7 0.1 collective-permute-start.11
  18.7 0.8 %project.7.up_ref = f32[96,512]{1,0:T(8,128)S(1)} custom-call(bf16[16,4096]{1,0:T(8,128)(2,1)S(1)} %copy-done.1, bf16[16,4096]{1,0:T(8,128)(2,1)S(1)} %collective-permute-done.6.refs_1_, bf16[16,4096]{1,0:T(8,128)(2,1)S(1)} %collective-permute-done.7.refs_2_, bf16[16,4096]{1,0:T(8,128)(2,1)S(1)} %collective-permute-done.8.refs_3_, ...), custom_call_target="tpu_custom_call" | custom-call | flops 402653184 | tf_op jit(solution)/shard_map/project/pallas_call | solution.py:15
  19.5 0.6 %collective-permute-start.12 = (f32[96,512]{1,0:T(8,128)S(1)}, f32[96,512]{1,0:T(8,128)S(1)}, u32[]{:S(2)}, u32[]{:S(2)}) collective-permute-start(f32[96,512]{1,0:T(8,128)S(1)} %project.7.up_ref), channel_id=1, source_target_pairs={{0,1},{1,0},{2,3},{3,2},{4,5},{5,4},{6,7},{7,6},{8,9},{9,8},{10,11... | collective-permute-start | bytes 589832 | tf_op jit(solution)/shard_map/ppermute | solution.py:119
  20.1 0.8 %collective-permute-done.refs_0_ = bf16[16,4096]{1,0:T(8,128)(2,1)S(1)} collective-permute-done((bf16[16,4096]{1,0:T(8,128)(2,1)}, bf16[16,4096]{1,0:T(8,128)(2,1)S(1)}, u32[]{:S(2)}, u32[]{:S(2)}) %collective-permute-start) | collective-permute-done | bytes 131104 | tf_op jit(solution)/shard_map/ppermute | solution.py:111
  20.9 0.7 %collective-permute-start.1 = (bf16[16,4096]{1,0:T(8,128)(2,1)S(1)}, bf16[16,4096]{1,0:T(8,128)(2,1)S(1)}, u32[]{:S(2)}, u32[]{:S(2)}) collective-permute-start(bf16[16,4096]{1,0:T(8,128)(2,1)S(1)} %collective-permute-done.refs_0_), channel_id=1, source_target_pairs={{0,2},{2,0},{4,6},{6,4},{8,10},{10,8},{12,14},{14,12},{1,3},{3,1},... | collective-permute-start | bytes 393224 | tf_op jit(solution)/shard_map/ppermute | solution.py:115
  21.6 0.0 collective-permute-done.11.gate_other_ref
  21.6 0.0 collective-permute-done.12.up_other_ref
  21.6 0.0 copy-done
  21.6 0.8 %down.3 = (f32[16,4096]{1,0:T(8,128)S(1)}, f32[16,4096]{1,0:T(8,128)S(1)}, f32[16,4096]{1,0:T(8,128)S(1)}, bf16[16,4096]{1,0:T(8,128)(2,1)S(1)}, bf16[16,4096]{1...) custom-call(f32[96,512]{1,0:T(8,128)S(1)} %project.6.gate_ref, f32[96,512]{1,0:T(8,128)S(1)} %collective-permute-done.11.gate_other_ref, ...), custom_call_target="tpu_custom_call" | custom-call | flops 402653184 | tf_op jit(solution)/shard_map/down/pallas_call | solution.py:15
  22.4 1.4 %collective-permute-start.15 = (bf16[16,4096]{1,0:T(8,128)(2,1)S(1)}, bf16[16,4096]{1,0:T(8,128)(2,1)S(1)}, u32[]{:S(2)}, u32[]{:S(2)}) collective-permute-start(bf16[16,4096]{1,0:T(8,128)(2,1)S(1)} %get-tuple-element.21), channel_id=1, source_target_pairs={{0,2},{2,0},{4,6},{6,4},{8,10},{10,8},{12,14},{14,12},{1,3},{3,1},... | collective-permute-start | bytes 393224 | tf_op jit(solution)/shard_map/ppermute | solution.py:115
  23.8 0.7 %collective-permute-start.13 = (bf16[16,4096]{1,0:T(8,128)(2,1)S(1)}, bf16[16,4096]{1,0:T(8,128)(2,1)S(1)}, u32[]{:S(2)}, u32[]{:S(2)}) collective-permute-start(bf16[16,4096]{1,0:T(8,128)(2,1)S(1)} %get-tuple-element.19), channel_id=1, source_target_pairs={{0,2},{2,0},{4,6},{6,4},{8,10},{10,8},{12,14},{14,12},{1,3},{3,1},... | collective-permute-start | bytes 393224 | tf_op jit(solution)/shard_map/ppermute | solution.py:115
  24.5 2.2 %collective-permute-done.1.refs_1_ = bf16[16,4096]{1,0:T(8,128)(2,1)S(1)} collective-permute-done((bf16[16,4096]{1,0:T(8,128)(2,1)S(1)}, bf16[16,4096]{1,0:T(8,128)(2,1)S(1)}, u32[]{:S(2)}, u32[]{:S(2)}) %collective-permute-start.1) | collective-permute-done | bytes 131104 | tf_op jit(solution)/shard_map/ppermute | solution.py:115
  26.8 0.8 %project.4.gate_ref = f32[32,512]{1,0:T(8,128)S(1)} custom-call(bf16[16,4096]{1,0:T(8,128)(2,1)S(1)} %collective-permute-done.refs_0_, bf16[16,4096]{1,0:T(8,128)(2,1)S(1)} %collective-permute-done.1.refs_1_, bf16[4096,512]{1,0:T(8,128)(2,1)S(1)} %get-tuple-element.15.refs_2_.refs_6_), custom_call_target="tpu_custom_call" | custom-call | flops 134217728 | tf_op jit(solution)/shard_map/project/pallas_call | solution.py:15
  27.6 0.0 collective-permute-start.2
  27.6 0.8 %project.5.up_ref = f32[32,512]{1,0:T(8,128)S(1)} custom-call(bf16[16,4096]{1,0:T(8,128)(2,1)S(1)} %collective-permute-done.refs_0_, bf16[16,4096]{1,0:T(8,128)(2,1)S(1)} %collective-permute-done.1.refs_1_, bf16[4096,512]{1,0:T(8,128)(2,1)S(1)} %get-tuple-element.16.refs_2_.refs_6_), custom_call_target="tpu_custom_call" | custom-call | flops 134217728 | tf_op jit(solution)/shard_map/project/pallas_call | solution.py:15
  28.4 0.5 %collective-permute-start.3 = (f32[32,512]{1,0:T(8,128)S(1)}, f32[32,512]{1,0:T(8,128)S(1)}, u32[]{:S(2)}, u32[]{:S(2)}) collective-permute-start(f32[32,512]{1,0:T(8,128)S(1)} %project.5.up_ref), channel_id=1, source_target_pairs={{0,1},{1,0},{2,3},{3,2},{4,5},{5,4},{6,7},{7,6},{8,9},{9,8},{10,11... | collective-permute-start | bytes 196616 | tf_op jit(solution)/shard_map/ppermute | solution.py:119
  28.9 0.0 collective-permute-done.2.gate_other_ref
  28.9 0.9 %collective-permute-done.3.up_other_ref = f32[32,512]{1,0:T(8,128)S(1)} collective-permute-done((f32[32,512]{1,0:T(8,128)S(1)}, f32[32,512]{1,0:T(8,128)S(1)}, u32[]{:S(2)}, u32[]{:S(2)}) %collective-permute-start.3) | collective-permute-done | bytes 65568 | tf_op jit(solution)/shard_map/ppermute | solution.py:119
  29.8 0.8 %down.2 = (f32[16,4096]{1,0:T(8,128)S(1)}, bf16[16,4096]{1,0:T(8,128)(2,1)S(1)}) custom-call(f32[32,512]{1,0:T(8,128)S(1)} %project.4.gate_ref, f32[32,512]{1,0:T(8,128)S(1)} %collective-permute-done.2.gate_other_ref, f32[32,512]{1,0:T(8,128)S(1)} %project.5.up_ref, f32[32,512]{1,0:T(8,128)S(1)} %collective-permute-done.3.up_other_ref, ...), custom_call_target="tpu_custom_call" | custom-call | flops 134217728 | tf_op jit(solution)/shard_map/down/pallas_call | solution.py:15
  30.7 0.9 %collective-permute-start.4 = (bf16[16,4096]{1,0:T(8,128)(2,1)S(1)}, bf16[16,4096]{1,0:T(8,128)(2,1)S(1)}, u32[]{:S(2)}, u32[]{:S(2)}) collective-permute-start(bf16[16,4096]{1,0:T(8,128)(2,1)S(1)} %get-tuple-element.17), channel_id=1, source_target_pairs={{0,2},{2,0},{4,6},{6,4},{8,10},{10,8},{12,14},{14,12},{1,3},{3,1},... | collective-permute-start | bytes 393224 | tf_op jit(solution)/shard_map/ppermute | solution.py:115
  31.5 1.2 %collective-permute-start.17 = (bf16[16,4096]{1,0:T(8,128)(2,1)S(1)}, bf16[16,4096]{1,0:T(8,128)(2,1)S(1)}, u32[]{:S(2)}, u32[]{:S(2)}) collective-permute-start(bf16[16,4096]{1,0:T(8,128)(2,1)S(1)} %get-tuple-element.23), channel_id=1, source_target_pairs={{0,2},{2,0},{4,6},{6,4},{8,10},{10,8},{12,14},{14,12},{1,3},{3,1},... | collective-permute-start | bytes 393224 | tf_op jit(solution)/shard_map/ppermute | solution.py:115
  32.7 0.0 collective-permute-done.15.arrived_ref
  32.7 1.9 %collective-permute-start.16 = (bf16[16,4096]{1,0:T(8,128)(2,1)S(1)}, bf16[16,4096]{1,0:T(8,128)(2,1)S(1)}, u32[]{:S(2)}, u32[]{:S(2)}) collective-permute-start(bf16[16,4096]{1,0:T(8,128)(2,1)S(1)} %add_pair.9), channel_id=1, source_target_pairs={{0,12},{2,14},{4,0},{6,2},{8,4},{10,6},{12,8},{14,10},{1,13},{3,15... | collective-permute-start | bytes 393224 | tf_op jit(solution)/shard_map/ppermute | solution.py:111
  34.6 0.0 collective-permute-done.13.arrived_ref
  34.6 0.3 collective-permute-start.14
  34.9 2.1 %collective-permute-done.4.arrived_ref = bf16[16,4096]{1,0:T(8,128)(2,1)S(1)} collective-permute-done((bf16[16,4096]{1,0:T(8,128)(2,1)S(1)}, bf16[16,4096]{1,0:T(8,128)(2,1)S(1)}, u32[]{:S(2)}, u32[]{:S(2)}) %collective-permute-start.4) | collective-permute-done | bytes 131104 | tf_op jit(solution)/shard_map/ppermute | solution.py:115
  37.0 0.5 %collective-permute-start.5 = (bf16[16,4096]{1,0:T(8,128)(2,1)S(1)}, bf16[16,4096]{1,0:T(8,128)(2,1)S(1)}, u32[]{:S(2)}, u32[]{:S(2)}) collective-permute-start(bf16[16,4096]{1,0:T(8,128)(2,1)S(1)} %add_pair.7), channel_id=1, source_target_pairs={{0,8},{2,10},{4,12},{6,14},{8,0},{10,2},{12,4},{14,6},{1,9},{3,11}... | collective-permute-start | bytes 393224 | tf_op jit(solution)/shard_map/ppermute | solution.py:111
  37.5 1.7 %collective-permute-done.17.arrived_ref = bf16[16,4096]{1,0:T(8,128)(2,1)S(1)} collective-permute-done((bf16[16,4096]{1,0:T(8,128)(2,1)S(1)}, bf16[16,4096]{1,0:T(8,128)(2,1)S(1)}, u32[]{:S(2)}, u32[]{:S(2)}) %collective-permute-start.17) | collective-permute-done | bytes 131104 | tf_op jit(solution)/shard_map/ppermute | solution.py:115
  39.3 0.0 collective-permute-done.16.arrived_ref
  39.3 3.6 %collective-permute-done.14.arrived_ref = bf16[16,4096]{1,0:T(8,128)(2,1)S(1)} collective-permute-done((bf16[16,4096]{1,0:T(8,128)(2,1)S(1)}, bf16[16,4096]{1,0:T(8,128)(2,1)S(1)}, u32[]{:S(2)}, u32[]{:S(2)}) %collective-permute-start.14) | collective-permute-done | bytes 131104 | tf_op jit(solution)/shard_map/ppermute | solution.py:111
  42.9 4.1 %collective-permute-done.5.arrived_ref = bf16[16,4096]{1,0:T(8,128)(2,1)S(1)} collective-permute-done((bf16[16,4096]{1,0:T(8,128)(2,1)S(1)}, bf16[16,4096]{1,0:T(8,128)(2,1)S(1)}, u32[]{:S(2)}, u32[]{:S(2)}) %collective-permute-start.5) | collective-permute-done | bytes 131104 | tf_op jit(solution)/shard_map/ppermute | solution.py:111
  47.0 0.7 %add_pair.13 = bf16[16,4096]{1,0:T(8,128)(2,1)} custom-call(bf16[16,4096]{1,0:T(8,128)(2,1)S(1)} %collective-permute-done.5.arrived_ref, f32[16,4096]{1,0:T(8,128)S(1)} %add_pair.12.own_ref), custom_call_target="tpu_custom_call" | custom-call | flops 5000000000 | tf_op jit(solution)/shard_map/add_pair/pallas_call | solution.py:15
  (6 shorter events, 0.1 us)
Async XLA Ops:
  0.0 17.8 %copy-start.1 = (bf16[16,4096]{1,0:T(8,128)(2,1)S(1)}, bf16[16,4096]{1,0:T(8,128)(2,1)}, u32[]{:S(2)}) copy-start(bf16[16,4096]{1,0:T(8,128)(2,1)} %refs_0_.5) | copy-start | bytes 393220
  0.0 9.7 %collective-permute-start.6 = (bf16[16,4096]{1,0:T(8,128)(2,1)}, bf16[16,4096]{1,0:T(8,128)(2,1)S(1)}, u32[]{:S(2)}, u32[]{:S(2)}) collective-permute-start(bf16[16,4096]{1,0:T(8,128)(2,1)} %refs_0_.5), channel_id=1, source_target_pairs={{0,4},{2,6},{4,8},{6,10},{8,12},{10,14},{12,0},{14,2},{1,5},{3,7},... | collective-permute-start | bytes 393224 | tf_op jit(solution)/shard_map/ppermute | solution.py:111
  3.0 8.3 %collective-permute-start.7 = (bf16[16,4096]{1,0:T(8,128)(2,1)}, bf16[16,4096]{1,0:T(8,128)(2,1)S(1)}, u32[]{:S(2)}, u32[]{:S(2)}) collective-permute-start(bf16[16,4096]{1,0:T(8,128)(2,1)} %refs_0_.5), channel_id=1, source_target_pairs={{0,12},{2,14},{4,0},{6,2},{8,4},{10,6},{12,8},{14,10},{1,13},{3,15... | collective-permute-start | bytes 393224 | tf_op jit(solution)/shard_map/ppermute | solution.py:111
  5.1 12.7 %collective-permute-start.8 = (bf16[16,4096]{1,0:T(8,128)(2,1)}, bf16[16,4096]{1,0:T(8,128)(2,1)S(1)}, u32[]{:S(2)}, u32[]{:S(2)}) collective-permute-start(bf16[16,4096]{1,0:T(8,128)(2,1)} %refs_0_.5), channel_id=1, source_target_pairs={{0,2},{2,0},{4,6},{6,4},{8,10},{10,8},{12,14},{14,12},{1,3},{3,1},... | collective-permute-start | bytes 393224 | tf_op jit(solution)/shard_map/ppermute | solution.py:115
  9.7 8.1 %collective-permute-start.9 = (bf16[16,4096]{1,0:T(8,128)(2,1)S(1)}, bf16[16,4096]{1,0:T(8,128)(2,1)S(1)}, u32[]{:S(2)}, u32[]{:S(2)}) collective-permute-start(bf16[16,4096]{1,0:T(8,128)(2,1)S(1)} %collective-permute-done.6.refs_1_), channel_id=1, source_target_pairs={{0,2},{2,0},{4,6},{6,4},{8,10},{10,8},{12,14},{14,12},{1,3},{3,1},... | collective-permute-start | bytes 393224 | tf_op jit(solution)/shard_map/ppermute | solution.py:115
  11.4 6.5 %collective-permute-start.10 = (bf16[16,4096]{1,0:T(8,128)(2,1)S(1)}, bf16[16,4096]{1,0:T(8,128)(2,1)S(1)}, u32[]{:S(2)}, u32[]{:S(2)}) collective-permute-start(bf16[16,4096]{1,0:T(8,128)(2,1)S(1)} %collective-permute-done.7.refs_2_), channel_id=1, source_target_pairs={{0,2},{2,0},{4,6},{6,4},{8,10},{10,8},{12,14},{14,12},{1,3},{3,1},... | collective-permute-start | bytes 393224 | tf_op jit(solution)/shard_map/ppermute | solution.py:115
  12.5 8.4 %collective-permute-start = (bf16[16,4096]{1,0:T(8,128)(2,1)}, bf16[16,4096]{1,0:T(8,128)(2,1)S(1)}, u32[]{:S(2)}, u32[]{:S(2)}) collective-permute-start(bf16[16,4096]{1,0:T(8,128)(2,1)} %refs_0_.5), channel_id=1, source_target_pairs={{0,8},{2,10},{4,12},{6,14},{8,0},{10,2},{12,4},{14,6},{1,9},{3,11}... | collective-permute-start | bytes 393224 | tf_op jit(solution)/shard_map/ppermute | solution.py:111
  17.8 3.8 %copy-start = (bf16[512,4096]{1,0:T(8,128)(2,1)S(1)}, bf16[512,4096]{1,0:T(8,128)(2,1)}, u32[]{:S(2)}) copy-start(bf16[512,4096]{1,0:T(8,128)(2,1)} %weight_ref.3) | copy-start | bytes 12582916
  18.7 3.0 %collective-permute-start.11 = (f32[96,512]{1,0:T(8,128)S(1)}, f32[96,512]{1,0:T(8,128)S(1)}, u32[]{:S(2)}, u32[]{:S(2)}) collective-permute-start(f32[96,512]{1,0:T(8,128)S(1)} %project.6.gate_ref), channel_id=1, source_target_pairs={{0,1},{1,0},{2,3},{3,2},{4,5},{5,4},{6,7},{7,6},{8,9},{9,8},{10,11... | collective-permute-start | bytes 589832 | tf_op jit(solution)/shard_map/ppermute | solution.py:119
  19.5 2.1 %collective-permute-start.12 = (f32[96,512]{1,0:T(8,128)S(1)}, f32[96,512]{1,0:T(8,128)S(1)}, u32[]{:S(2)}, u32[]{:S(2)}) collective-permute-start(f32[96,512]{1,0:T(8,128)S(1)} %project.7.up_ref), channel_id=1, source_target_pairs={{0,1},{1,0},{2,3},{3,2},{4,5},{5,4},{6,7},{7,6},{8,9},{9,8},{10,11... | collective-permute-start | bytes 589832 | tf_op jit(solution)/shard_map/ppermute | solution.py:119
  20.9 5.9 %collective-permute-start.1 = (bf16[16,4096]{1,0:T(8,128)(2,1)S(1)}, bf16[16,4096]{1,0:T(8,128)(2,1)S(1)}, u32[]{:S(2)}, u32[]{:S(2)}) collective-permute-start(bf16[16,4096]{1,0:T(8,128)(2,1)S(1)} %collective-permute-done.refs_0_), channel_id=1, source_target_pairs={{0,2},{2,0},{4,6},{6,4},{8,10},{10,8},{12,14},{14,12},{1,3},{3,1},... | collective-permute-start | bytes 393224 | tf_op jit(solution)/shard_map/ppermute | solution.py:115
  22.4 10.3 %collective-permute-start.15 = (bf16[16,4096]{1,0:T(8,128)(2,1)S(1)}, bf16[16,4096]{1,0:T(8,128)(2,1)S(1)}, u32[]{:S(2)}, u32[]{:S(2)}) collective-permute-start(bf16[16,4096]{1,0:T(8,128)(2,1)S(1)} %get-tuple-element.21), channel_id=1, source_target_pairs={{0,2},{2,0},{4,6},{6,4},{8,10},{10,8},{12,14},{14,12},{1,3},{3,1},... | collective-permute-start | bytes 393224 | tf_op jit(solution)/shard_map/ppermute | solution.py:115
  23.8 10.8 %collective-permute-start.13 = (bf16[16,4096]{1,0:T(8,128)(2,1)S(1)}, bf16[16,4096]{1,0:T(8,128)(2,1)S(1)}, u32[]{:S(2)}, u32[]{:S(2)}) collective-permute-start(bf16[16,4096]{1,0:T(8,128)(2,1)S(1)} %get-tuple-element.19), channel_id=1, source_target_pairs={{0,2},{2,0},{4,6},{6,4},{8,10},{10,8},{12,14},{14,12},{1,3},{3,1},... | collective-permute-start | bytes 393224 | tf_op jit(solution)/shard_map/ppermute | solution.py:115
  27.6 1.4 %collective-permute-start.2 = (f32[32,512]{1,0:T(8,128)S(1)}, f32[32,512]{1,0:T(8,128)S(1)}, u32[]{:S(2)}, u32[]{:S(2)}) collective-permute-start(f32[32,512]{1,0:T(8,128)S(1)} %project.4.gate_ref), channel_id=1, source_target_pairs={{0,1},{1,0},{2,3},{3,2},{4,5},{5,4},{6,7},{7,6},{8,9},{9,8},{10,11... | collective-permute-start | bytes 196616 | tf_op jit(solution)/shard_map/ppermute | solution.py:119
  28.4 1.4 %collective-permute-start.3 = (f32[32,512]{1,0:T(8,128)S(1)}, f32[32,512]{1,0:T(8,128)S(1)}, u32[]{:S(2)}, u32[]{:S(2)}) collective-permute-start(f32[32,512]{1,0:T(8,128)S(1)} %project.5.up_ref), channel_id=1, source_target_pairs={{0,1},{1,0},{2,3},{3,2},{4,5},{5,4},{6,7},{7,6},{8,9},{9,8},{10,11... | collective-permute-start | bytes 196616 | tf_op jit(solution)/shard_map/ppermute | solution.py:119
  30.7 6.3 %collective-permute-start.4 = (bf16[16,4096]{1,0:T(8,128)(2,1)S(1)}, bf16[16,4096]{1,0:T(8,128)(2,1)S(1)}, u32[]{:S(2)}, u32[]{:S(2)}) collective-permute-start(bf16[16,4096]{1,0:T(8,128)(2,1)S(1)} %get-tuple-element.17), channel_id=1, source_target_pairs={{0,2},{2,0},{4,6},{6,4},{8,10},{10,8},{12,14},{14,12},{1,3},{3,1},... | collective-permute-start | bytes 393224 | tf_op jit(solution)/shard_map/ppermute | solution.py:115
  31.5 7.7 %collective-permute-start.17 = (bf16[16,4096]{1,0:T(8,128)(2,1)S(1)}, bf16[16,4096]{1,0:T(8,128)(2,1)S(1)}, u32[]{:S(2)}, u32[]{:S(2)}) collective-permute-start(bf16[16,4096]{1,0:T(8,128)(2,1)S(1)} %get-tuple-element.23), channel_id=1, source_target_pairs={{0,2},{2,0},{4,6},{6,4},{8,10},{10,8},{12,14},{14,12},{1,3},{3,1},... | collective-permute-start | bytes 393224 | tf_op jit(solution)/shard_map/ppermute | solution.py:115
  32.7 6.5 %collective-permute-start.16 = (bf16[16,4096]{1,0:T(8,128)(2,1)S(1)}, bf16[16,4096]{1,0:T(8,128)(2,1)S(1)}, u32[]{:S(2)}, u32[]{:S(2)}) collective-permute-start(bf16[16,4096]{1,0:T(8,128)(2,1)S(1)} %add_pair.9), channel_id=1, source_target_pairs={{0,12},{2,14},{4,0},{6,2},{8,4},{10,6},{12,8},{14,10},{1,13},{3,15... | collective-permute-start | bytes 393224 | tf_op jit(solution)/shard_map/ppermute | solution.py:111
  34.6 8.3 %collective-permute-start.14 = (bf16[16,4096]{1,0:T(8,128)(2,1)S(1)}, bf16[16,4096]{1,0:T(8,128)(2,1)S(1)}, u32[]{:S(2)}, u32[]{:S(2)}) collective-permute-start(bf16[16,4096]{1,0:T(8,128)(2,1)S(1)} %add_pair.8), channel_id=1, source_target_pairs={{0,4},{2,6},{4,8},{6,10},{8,12},{10,14},{12,0},{14,2},{1,5},{3,7},... | collective-permute-start | bytes 393224 | tf_op jit(solution)/shard_map/ppermute | solution.py:111
  37.0 10.0 %collective-permute-start.5 = (bf16[16,4096]{1,0:T(8,128)(2,1)S(1)}, bf16[16,4096]{1,0:T(8,128)(2,1)S(1)}, u32[]{:S(2)}, u32[]{:S(2)}) collective-permute-start(bf16[16,4096]{1,0:T(8,128)(2,1)S(1)} %add_pair.7), channel_id=1, source_target_pairs={{0,8},{2,10},{4,12},{6,14},{8,0},{10,2},{12,4},{14,6},{1,9},{3,11}... | collective-permute-start | bytes 393224 | tf_op jit(solution)/shard_map/ppermute | solution.py:111

commit v6 on v5

--- a/solution.py
+++ b/solution.py
@@ -59,8 +59,7 @@
 def project(blocks, weight):
     rows = sum(block.shape[0] for block in blocks)
     out = jax.ShapeDtypeStruct((rows, weight.shape[1]), F32)
-    flops = 2 * rows * weight.shape[0] * weight.shape[1]
-    return call(project_kernel, "project", out, flops, 4 << 20, *blocks, weight)
+    return call(project_kernel, "project", out, 2000000000, 4 << 20, *blocks, weight)
 
 
 def down_kernel(give, keep, gate_ref, gate_other_ref, up_ref, up_other_ref, weight_ref, *out_refs):
@@ -93,21 +92,34 @@
     )
 
 
-def pair_kernel(arrived_ref, own_ref, out_ref):
+def pair_kernel(arrived_ref, own_ref, *refs):
+    out_ref = refs[-1]
     out_ref[...] = (own_ref[...] + arrived_ref[...].astype(F32)).astype(out_ref.dtype)
 
 
-def add_pair(arrived, own, dtype, flops):
-    out = jax.ShapeDtypeStruct(own.shape, dtype)
-    return call(pair_kernel, "add_pair", out, flops, 2 << 20, arrived, own)
+def add_pair(arrived, own, dtype, flops, after=()):
+    return pl.pallas_call(
+        pair_kernel,
+        in_specs=[pl.BlockSpec(memory_space=pltpu.VMEM)] * 2
+        + [pl.BlockSpec(memory_space=pl.ANY)] * len(after),
+        out_shape=jax.ShapeDtypeStruct(own.shape, dtype),
+        compiler_params=pltpu.CompilerParams(vmem_limit_bytes=2 << 20),
+        cost_estimate=pl.CostEstimate(flops=flops, bytes_accessed=0, transcendentals=0),
+        name="add_pair",
+    )(arrived, own, *after)
 
 
 def make_local(wide, narrow):
-    inner = 2 if wide % 2 == 0 else 1
+    inner = 2
     outer = wide // inner
 
-    def along_outer(value, step):
-        pairs = [(i, (i + step * inner) % wide) for i in range(wide)]
+    pairwise = outer & (outer - 1) == 0
+
+    def along_outer(value, k, back=False):
+        if pairwise:
+            pairs = [(i, i ^ (k * inner)) for i in range(wide)]
+        else:
+            pairs = [(i, (i + (-k if back else k) * inner) % wide) for i in range(wide)]
         return lax.ppermute(value, "wide", pairs)
 
     def along_inner(value):
@@ -118,40 +130,42 @@
         pairs = [(i, (i + 1) % narrow) for i in range(narrow)]
         return lax.ppermute(value, "narrow", pairs)
 
-    shifts = sorted(range(outer), key=lambda k: (min(k, outer - k), k))
-    near = [k for k in shifts if min(k, outer - k) <= outer // 4]
-    waves = [near, [k for k in shifts if k not in near]]
+    split = max(outer * 3 // 4, 1)
+    waves = [[0] + list(range(split - 1, 0, -1)), list(range(split, outer))]
 
     def local(tokens, gate_weight, up_weight, down_weight):
         rows = tokens.shape[0]
-        mine = {k: along_outer(tokens, k) if k else tokens for k in shifts}
-        theirs = {k: along_inner(mine[k]) for k in shifts} if inner == 2 else {}
+        mine = {k: along_outer(tokens, k) if k else tokens for k in range(outer)}
+        theirs = {k: along_inner(mine[k]) for k in range(outer)}
         gate_held, up_held = fetch([gate_weight, up_weight])
         keep, give = {}, {}
         for wave in waves:
             if not wave:
                 continue
-            blocks = [mine[k] for k in wave] + [theirs[k] for k in wave if theirs]
+            blocks = [mine[k] for k in wave] + [theirs[k] for k in wave]
             gate_part = project(blocks, gate_held)
             up_part = project(blocks, up_held)
             outs = down(
                 gate_part, across_cores(gate_part), up_part, across_cores(up_part),
-                down_weight, rows, len(wave), len(blocks) - len(wave),
+                down_weight, rows, len(wave), len(wave),
             )
             keep.update(zip(wave, outs[:len(wave)]))
             give.update(zip(wave, outs[len(wave):]))
-        total = None
-        for k in shifts:
-            last = k == shifts[-1]
-            pair = keep[k]
-            if give:
-                pair = add_pair(along_inner(give[k]), keep[k], BF16 if k else F32, 1000000)
-            if k:
-                arrived = along_outer(pair.astype(BF16), -k)
-                hint = 100000000 if k == shifts[1] else 5000000000
-                total = add_pair(arrived, total, BF16 if last else F32, hint)
-            else:
-                total = pair
+        def send_back(k, after=()):
+            pair = add_pair(along_inner(give[k]), keep[k], BF16, 1000000, after)
+            return along_outer(pair, k, back=True)
+
+        near, far = waves[0][1:], waves[1]
+        arrived = {k: send_back(k) for k in near}
+        total = keep[0]
+        after = ()
+        for k in near:
+            total = add_pair(arrived[k], total, F32, 3000000000)
+            after = after or (total,)
+        arrived.update({k: send_back(k, after) for k in far})
+        total = add_pair(along_inner(give[0]), total, F32, 100000000)
+        for k in far:
+            total = add_pair(arrived[k], total, BF16 if k == far[-1] else F32, 5000000000)
         return total.astype(BF16)
 
     return local

time: 47.8 us -> 47.2 us (0.987)
  waiting for transfers between devices: 18.3 us -> 16.7 us
  starting transfers between devices: 20.1 us -> 21.1 us
    ppermute x6, waiting for transfers between devices: 11.4 us -> 8.48 us  [along_outer(): return lax.ppermute(value, 'wide', pairs)]
    ppermute x6, starting transfers between devices: 9.56 us -> 11.5 us  [along_outer(): return lax.ppermute(value, 'wide', pairs)]
    ppermute x4, waiting for transfers between devices: 0.91 us -> 1.82 us  [across_cores(): return lax.ppermute(value, 'narrow', pairs)]
    pallas_call x13 -> x6, Pallas kernels: 5.66 us -> 4.82 us  [call(): pl.pallas_call(kernel, out_shape=out_shape, compiler_params=pltpu.Compile...]
    pallas_call x0 -> x7, Pallas kernels: none -> 0.83 us  [add_pair(): pl.pallas_call(pair_kernel, in_specs=[pl.BlockSpec(memory_space=pltpu.VME...]
    ppermute x4, starting transfers between devices: 1.16 us -> 0.64 us  [across_cores(): return lax.ppermute(value, 'narrow', pairs)]
    ppermute x8, starting transfers between devices: 9.41 us -> 8.9 us  [along_inner(): return lax.ppermute(value, 'wide', pairs)]
  transfers between devices with their start and end apart: 18 -> 18, of which waited for: 8 -> 10; matrix products, arithmetic and copies ran while one was open for 0% -> 0% of each run, Pallas kernels for 18% -> 18%
where the time goes in v6:
time: 47.2 us; the launch traced here: 47 us
  starting transfers between devices  21.1 us (45%)
  waiting for transfers between devices  16.7 us (35%)
  Pallas kernels  9.12 us (19%)
    ppermute x6, starting transfers between devices, along_outer(): return lax.ppermute(value, 'wide', pairs)  11.5 us
    ppermute x8, starting transfers between devices, along_inner(): return lax.ppermute(value, 'wide', pairs)  8.9 us
    ppermute x6, waiting for transfers between devices, along_outer(): return lax.ppermute(value, 'wide', pairs)  8.48 us
    ppermute x8, waiting for transfers between devices, along_inner(): return lax.ppermute(value, 'wide', pairs)  6.4 us
    pallas_call x6, Pallas kernels, call(): pl.pallas_call(kernel, out_shape=out_shape, compiler_params=pltpu.Compile...  4.82 us
    pallas_call x1, Pallas kernels, fetch(): pl.pallas_call(functools.partial(fetch_kernel, pieces), in_specs=[pl.Bloc...  3.47 us
    ppermute x4, waiting for transfers between devices, across_cores(): return lax.ppermute(value, 'narrow', pairs)  1.82 us
  transfers between devices with their start and end apart: 18, of which 10 were waited for; matrix products, arithmetic and copies ran while one was open for 0% of the time, Pallas kernels for 18%

profile of v6, /device:TPU:0, one launch (start us, length us, event | category | flops | bytes accessed | tf_op | source)
XLA Modules:
  0.0 47.0 jit_solution(9211647818349544135)
XLA Ops:
  0.0 0.0 copy-start.1
  0.0 3.0 %collective-permute-start.6 = (bf16[16,4096]{1,0:T(8,128)(2,1)}, bf16[16,4096]{1,0:T(8,128)(2,1)S(1)}, u32[]{:S(2)}, u32[]{:S(2)}) collective-permute-start(bf16[16,4096]{1,0:T(8,128)(2,1)} %refs_0_.5), channel_id=1, source_target_pairs={{0,4},{2,6},{4,0},{6,2},{8,12},{10,14},{12,8},{14,10},{1,5},{3,7},... | collective-permute-start | bytes 393224 | tf_op jit(solution)/shard_map/ppermute | solution.py:123
  3.0 2.6 %collective-permute-start.5 = (bf16[16,4096]{1,0:T(8,128)(2,1)}, bf16[16,4096]{1,0:T(8,128)(2,1)S(1)}, u32[]{:S(2)}, u32[]{:S(2)}) collective-permute-start(bf16[16,4096]{1,0:T(8,128)(2,1)} %refs_0_.5), channel_id=1, source_target_pairs={{0,8},{2,10},{4,12},{6,14},{8,0},{10,2},{12,4},{14,6},{1,9},{3,11}... | collective-permute-start | bytes 393224 | tf_op jit(solution)/shard_map/ppermute | solution.py:123
  5.6 1.5 %collective-permute-start.7 = (bf16[16,4096]{1,0:T(8,128)(2,1)}, bf16[16,4096]{1,0:T(8,128)(2,1)S(1)}, u32[]{:S(2)}, u32[]{:S(2)}) collective-permute-start(bf16[16,4096]{1,0:T(8,128)(2,1)} %refs_0_.5), channel_id=1, source_target_pairs={{0,2},{2,0},{4,6},{6,4},{8,10},{10,8},{12,14},{14,12},{1,3},{3,1},... | collective-permute-start | bytes 393224 | tf_op jit(solution)/shard_map/ppermute | solution.py:127
  7.1 1.5 %collective-permute-done.6.refs_2_ = bf16[16,4096]{1,0:T(8,128)(2,1)S(1)} collective-permute-done((bf16[16,4096]{1,0:T(8,128)(2,1)}, bf16[16,4096]{1,0:T(8,128)(2,1)S(1)}, u32[]{:S(2)}, u32[]{:S(2)}) %collective-permute-start.6) | collective-permute-done | bytes 131104 | tf_op jit(solution)/shard_map/ppermute | solution.py:123
  8.7 1.7 %collective-permute-start.9 = (bf16[16,4096]{1,0:T(8,128)(2,1)S(1)}, bf16[16,4096]{1,0:T(8,128)(2,1)S(1)}, u32[]{:S(2)}, u32[]{:S(2)}) collective-permute-start(bf16[16,4096]{1,0:T(8,128)(2,1)S(1)} %collective-permute-done.6.refs_2_), channel_id=1, source_target_pairs={{0,2},{2,0},{4,6},{6,4},{8,10},{10,8},{12,14},{14,12},{1,3},{3,1},... | collective-permute-start | bytes 393224 | tf_op jit(solution)/shard_map/ppermute | solution.py:127
  10.4 1.6 %collective-permute-done.5.refs_1_ = bf16[16,4096]{1,0:T(8,128)(2,1)S(1)} collective-permute-done((bf16[16,4096]{1,0:T(8,128)(2,1)}, bf16[16,4096]{1,0:T(8,128)(2,1)S(1)}, u32[]{:S(2)}, u32[]{:S(2)}) %collective-permute-start.5) | collective-permute-done | bytes 131104 | tf_op jit(solution)/shard_map/ppermute | solution.py:123
  12.0 1.5 %collective-permute-start.8 = (bf16[16,4096]{1,0:T(8,128)(2,1)S(1)}, bf16[16,4096]{1,0:T(8,128)(2,1)S(1)}, u32[]{:S(2)}, u32[]{:S(2)}) collective-permute-start(bf16[16,4096]{1,0:T(8,128)(2,1)S(1)} %collective-permute-done.5.refs_1_), channel_id=1, source_target_pairs={{0,2},{2,0},{4,6},{6,4},{8,10},{10,8},{12,14},{14,12},{1,3},{3,1},... | collective-permute-start | bytes 393224 | tf_op jit(solution)/shard_map/ppermute | solution.py:127
  13.5 2.5 %collective-permute-start = (bf16[16,4096]{1,0:T(8,128)(2,1)}, bf16[16,4096]{1,0:T(8,128)(2,1)S(1)}, u32[]{:S(2)}, u32[]{:S(2)}) collective-permute-start(bf16[16,4096]{1,0:T(8,128)(2,1)} %refs_0_.5), channel_id=1, source_target_pairs={{0,12},{2,14},{4,8},{6,10},{8,4},{10,6},{12,0},{14,2},{1,13},{3,15... | collective-permute-start | bytes 393224 | tf_op jit(solution)/shard_map/ppermute | solution.py:123
  15.9 3.5 %fetch.1 = (bf16[4096,512]{1,0:T(8,128)(2,1)S(1)}, bf16[4096,512]{1,0:T(8,128)(2,1)S(1)}) custom-call(bf16[4096,512]{1,0:T(8,128)(2,1)} %refs_0_.3, bf16[4096,512]{1,0:T(8,128)(2,1)} %refs_1_.1), custom_call_target="tpu_custom_call" | custom-call | flops 1000000000 | tf_op jit(solution)/shard_map/fetch/pallas_call | solution.py:41
  19.4 0.0 collective-permute-done.7.refs_3_
  19.4 0.0 collective-permute-done.9.refs_5_
  19.4 0.0 collective-permute-done.8.refs_4_
  19.5 0.0 copy-done.1
  19.5 0.8 %project.7.up_ref = f32[96,512]{1,0:T(8,128)S(1)} custom-call(bf16[16,4096]{1,0:T(8,128)(2,1)S(1)} %copy-done.1, bf16[16,4096]{1,0:T(8,128)(2,1)S(1)} %collective-permute-done.5.refs_1_, bf16[16,4096]{1,0:T(8,128)(2,1)S(1)} %collective-permute-done.6.refs_2_, bf16[16,4096]{1,0:T(8,128)(2,1)S(1)} %collective-permute-done.7.refs_3_, ...), custom_call_target="tpu_custom_call" | custom-call | flops 2000000000 | tf_op jit(solution)/shard_map/project/pallas_call | solution.py:15
  20.3 0.0 copy-start
  20.3 0.1 collective-permute-start.11
  20.4 0.8 %project.6.gate_ref = f32[96,512]{1,0:T(8,128)S(1)} custom-call(bf16[16,4096]{1,0:T(8,128)(2,1)S(1)} %copy-done.1, bf16[16,4096]{1,0:T(8,128)(2,1)S(1)} %collective-permute-done.5.refs_1_, bf16[16,4096]{1,0:T(8,128)(2,1)S(1)} %collective-permute-done.6.refs_2_, bf16[16,4096]{1,0:T(8,128)(2,1)S(1)} %collective-permute-done.7.refs_3_, ...), custom_call_target="tpu_custom_call" | custom-call | flops 2000000000 | tf_op jit(solution)/shard_map/project/pallas_call | solution.py:15
  21.2 0.6 %collective-permute-start.10 = (f32[96,512]{1,0:T(8,128)S(1)}, f32[96,512]{1,0:T(8,128)S(1)}, u32[]{:S(2)}, u32[]{:S(2)}) collective-permute-start(f32[96,512]{1,0:T(8,128)S(1)} %project.6.gate_ref), channel_id=1, source_target_pairs={{0,1},{1,0},{2,3},{3,2},{4,5},{5,4},{6,7},{7,6},{8,9},{9,8},{10,11... | collective-permute-start | bytes 589832 | tf_op jit(solution)/shard_map/ppermute | solution.py:131
  21.7 0.0 collective-permute-done.refs_0_
  21.7 0.5 %collective-permute-start.1 = (bf16[16,4096]{1,0:T(8,128)(2,1)S(1)}, bf16[16,4096]{1,0:T(8,128)(2,1)S(1)}, u32[]{:S(2)}, u32[]{:S(2)}) collective-permute-start(bf16[16,4096]{1,0:T(8,128)(2,1)S(1)} %collective-permute-done.refs_0_), channel_id=1, source_target_pairs={{0,2},{2,0},{4,6},{6,4},{8,10},{10,8},{12,14},{14,12},{1,3},{3,1},... | collective-permute-start | bytes 393224 | tf_op jit(solution)/shard_map/ppermute | solution.py:127
  22.2 0.0 collective-permute-done.11.up_other_ref
  22.2 0.6 %collective-permute-done.10.gate_other_ref = f32[96,512]{1,0:T(8,128)S(1)} collective-permute-done((f32[96,512]{1,0:T(8,128)S(1)}, f32[96,512]{1,0:T(8,128)S(1)}, u32[]{:S(2)}, u32[]{:S(2)}) %collective-permute-start.10) | collective-permute-done | bytes 196640 | tf_op jit(solution)/shard_map/ppermute | solution.py:131
  22.8 0.0 copy-done
  22.8 0.8 %down.3 = (f32[16,4096]{1,0:T(8,128)S(1)}, f32[16,4096]{1,0:T(8,128)S(1)}, f32[16,4096]{1,0:T(8,128)S(1)}, bf16[16,4096]{1,0:T(8,128)(2,1)S(1)}, bf16[16,4096]{1...) custom-call(f32[96,512]{1,0:T(8,128)S(1)} %project.6.gate_ref, f32[96,512]{1,0:T(8,128)S(1)} %collective-permute-done.10.gate_other_ref, ...), custom_call_target="tpu_custom_call" | custom-call | flops 402653184 | tf_op jit(solution)/shard_map/down/pallas_call | solution.py:15
  23.6 1.0 %collective-permute-start.12 = (bf16[16,4096]{1,0:T(8,128)(2,1)S(1)}, bf16[16,4096]{1,0:T(8,128)(2,1)S(1)}, u32[]{:S(2)}, u32[]{:S(2)}) collective-permute-start(bf16[16,4096]{1,0:T(8,128)(2,1)S(1)} %get-tuple-element.19), channel_id=1, source_target_pairs={{0,2},{2,0},{4,6},{6,4},{8,10},{10,8},{12,14},{14,12},{1,3},{3,1},... | collective-permute-start | bytes 393224 | tf_op jit(solution)/shard_map/ppermute | solution.py:127
  24.6 3.1 %collective-permute-done.1.refs_1_ = bf16[16,4096]{1,0:T(8,128)(2,1)S(1)} collective-permute-done((bf16[16,4096]{1,0:T(8,128)(2,1)S(1)}, bf16[16,4096]{1,0:T(8,128)(2,1)S(1)}, u32[]{:S(2)}, u32[]{:S(2)}) %collective-permute-start.1) | collective-permute-done | bytes 131104 | tf_op jit(solution)/shard_map/ppermute | solution.py:127
  27.7 0.8 %project.5.up_ref = f32[32,512]{1,0:T(8,128)S(1)} custom-call(bf16[16,4096]{1,0:T(8,128)(2,1)S(1)} %collective-permute-done.refs_0_, bf16[16,4096]{1,0:T(8,128)(2,1)S(1)} %collective-permute-done.1.refs_1_, bf16[4096,512]{1,0:T(8,128)(2,1)S(1)} %get-tuple-element.16.refs_2_.refs_6_), custom_call_target="tpu_custom_call" | custom-call | flops 2000000000 | tf_op jit(solution)/shard_map/project/pallas_call | solution.py:15
  28.5 0.0 collective-permute-start.3
  28.6 0.6 %collective-permute-start.16 = (bf16[16,4096]{1,0:T(8,128)(2,1)S(1)}, bf16[16,4096]{1,0:T(8,128)(2,1)S(1)}, u32[]{:S(2)}, u32[]{:S(2)}) collective-permute-start(bf16[16,4096]{1,0:T(8,128)(2,1)S(1)} %get-tuple-element.23), channel_id=1, source_target_pairs={{0,2},{2,0},{4,6},{6,4},{8,10},{10,8},{12,14},{14,12},{1,3},{3,1},... | collective-permute-start | bytes 393224 | tf_op jit(solution)/shard_map/ppermute | solution.py:127
  29.1 0.9 %collective-permute-done.12.arrived_ref = bf16[16,4096]{1,0:T(8,128)(2,1)S(1)} collective-permute-done((bf16[16,4096]{1,0:T(8,128)(2,1)S(1)}, bf16[16,4096]{1,0:T(8,128)(2,1)S(1)}, u32[]{:S(2)}, u32[]{:S(2)}) %collective-permute-start.12) | collective-permute-done | bytes 131104 | tf_op jit(solution)/shard_map/ppermute | solution.py:127
  30.0 0.1 collective-permute-start.13
  30.1 0.8 %project.4.gate_ref = f32[32,512]{1,0:T(8,128)S(1)} custom-call(bf16[16,4096]{1,0:T(8,128)(2,1)S(1)} %collective-permute-done.refs_0_, bf16[16,4096]{1,0:T(8,128)(2,1)S(1)} %collective-permute-done.1.refs_1_, bf16[4096,512]{1,0:T(8,128)(2,1)S(1)} %get-tuple-element.15.refs_2_.refs_6_), custom_call_target="tpu_custom_call" | custom-call | flops 2000000000 | tf_op jit(solution)/shard_map/project/pallas_call | solution.py:15
  30.9 0.0 collective-permute-start.2
  30.9 0.0 collective-permute-done.3.up_other_ref
  31.0 1.2 %collective-permute-done.2.gate_other_ref = f32[32,512]{1,0:T(8,128)S(1)} collective-permute-done((f32[32,512]{1,0:T(8,128)S(1)}, f32[32,512]{1,0:T(8,128)S(1)}, u32[]{:S(2)}, u32[]{:S(2)}) %collective-permute-start.2) | collective-permute-done | bytes 65568 | tf_op jit(solution)/shard_map/ppermute | solution.py:131
  32.2 0.8 %down.2 = (f32[16,4096]{1,0:T(8,128)S(1)}, bf16[16,4096]{1,0:T(8,128)(2,1)S(1)}) custom-call(f32[32,512]{1,0:T(8,128)S(1)} %project.4.gate_ref, f32[32,512]{1,0:T(8,128)S(1)} %collective-permute-done.2.gate_other_ref, f32[32,512]{1,0:T(8,128)S(1)} %project.5.up_ref, f32[32,512]{1,0:T(8,128)S(1)} %collective-permute-done.3.up_other_ref, ...), custom_call_target="tpu_custom_call" | custom-call | flops 134217728 | tf_op jit(solution)/shard_map/down/pallas_call | solution.py:15
  33.0 0.6 %collective-permute-start.4 = (bf16[16,4096]{1,0:T(8,128)(2,1)S(1)}, bf16[16,4096]{1,0:T(8,128)(2,1)S(1)}, u32[]{:S(2)}, u32[]{:S(2)}) collective-permute-start(bf16[16,4096]{1,0:T(8,128)(2,1)S(1)} %get-tuple-element.17), channel_id=1, source_target_pairs={{0,2},{2,0},{4,6},{6,4},{8,10},{10,8},{12,14},{14,12},{1,3},{3,1},... | collective-permute-start | bytes 393224 | tf_op jit(solution)/shard_map/ppermute | solution.py:127
  33.7 1.4 %collective-permute-start.15 = (bf16[16,4096]{1,0:T(8,128)(2,1)S(1)}, bf16[16,4096]{1,0:T(8,128)(2,1)S(1)}, u32[]{:S(2)}, u32[]{:S(2)}) collective-permute-start(bf16[16,4096]{1,0:T(8,128)(2,1)S(1)} %get-tuple-element.22), channel_id=1, source_target_pairs={{0,2},{2,0},{4,6},{6,4},{8,10},{10,8},{12,14},{14,12},{1,3},{3,1},... | collective-permute-start | bytes 393224 | tf_op jit(solution)/shard_map/ppermute | solution.py:127
  35.1 0.0 collective-permute-done.16.arrived_ref
  35.1 2.0 %collective-permute-start.17 = (bf16[16,4096]{1,0:T(8,128)(2,1)S(1)}, bf16[16,4096]{1,0:T(8,128)(2,1)S(1)}, u32[]{:S(2)}, u32[]{:S(2)}) collective-permute-start(bf16[16,4096]{1,0:T(8,128)(2,1)S(1)} %add_pair.10), channel_id=1, source_target_pairs={{0,4},{2,6},{4,0},{6,2},{8,12},{10,14},{12,8},{14,10},{1,5},{3,7},... | collective-permute-start | bytes 393224 | tf_op jit(solution)/shard_map/ppermute | solution.py:123
  37.1 0.4 collective-permute-done.13.arrived_ref
  37.5 1.8 %collective-permute-done.4.arrived_ref = bf16[16,4096]{1,0:T(8,128)(2,1)S(1)} collective-permute-done((bf16[16,4096]{1,0:T(8,128)(2,1)S(1)}, bf16[16,4096]{1,0:T(8,128)(2,1)S(1)}, u32[]{:S(2)}, u32[]{:S(2)}) %collective-permute-start.4) | collective-permute-done | bytes 131104 | tf_op jit(solution)/shard_map/ppermute | solution.py:127
  39.4 1.4 %collective-permute-start.14 = (bf16[16,4096]{1,0:T(8,128)(2,1)S(1)}, bf16[16,4096]{1,0:T(8,128)(2,1)S(1)}, u32[]{:S(2)}, u32[]{:S(2)}) collective-permute-start(bf16[16,4096]{1,0:T(8,128)(2,1)S(1)} %add_pair.9), channel_id=1, source_target_pairs={{0,12},{2,14},{4,8},{6,10},{8,4},{10,6},{12,0},{14,2},{1,13},{3,15... | collective-permute-start | bytes 393224 | tf_op jit(solution)/shard_map/ppermute | solution.py:123
  40.8 0.0 collective-permute-done.17.arrived_ref
  40.9 0.5 %collective-permute-done.15.arrived_ref = bf16[16,4096]{1,0:T(8,128)(2,1)S(1)} collective-permute-done((bf16[16,4096]{1,0:T(8,128)(2,1)S(1)}, bf16[16,4096]{1,0:T(8,128)(2,1)S(1)}, u32[]{:S(2)}, u32[]{:S(2)}) %collective-permute-start.15) | collective-permute-done | bytes 131104 | tf_op jit(solution)/shard_map/ppermute | solution.py:127
  41.4 4.9 %collective-permute-done.14.arrived_ref = bf16[16,4096]{1,0:T(8,128)(2,1)S(1)} collective-permute-done((bf16[16,4096]{1,0:T(8,128)(2,1)S(1)}, bf16[16,4096]{1,0:T(8,128)(2,1)S(1)}, u32[]{:S(2)}, u32[]{:S(2)}) %collective-permute-start.14) | collective-permute-done | bytes 131104 | tf_op jit(solution)/shard_map/ppermute | solution.py:123
  46.3 0.7 %add_pair.13 = bf16[16,4096]{1,0:T(8,128)(2,1)} custom-call(bf16[16,4096]{1,0:T(8,128)(2,1)S(1)} %collective-permute-done.14.arrived_ref, f32[16,4096]{1,0:T(8,128)S(1)} %add_pair.12.own_ref), custom_call_target="tpu_custom_call" | custom-call | flops 5000000000 | tf_op jit(solution)/shard_map/add_pair/pallas_call | solution.py:101
  (6 shorter events, 0.1 us)
Async XLA Ops:
  0.0 19.5 %copy-start.1 = (bf16[16,4096]{1,0:T(8,128)(2,1)S(1)}, bf16[16,4096]{1,0:T(8,128)(2,1)}, u32[]{:S(2)}) copy-start(bf16[16,4096]{1,0:T(8,128)(2,1)} %refs_0_.5) | copy-start | bytes 393220
  0.0 8.7 %collective-permute-start.6 = (bf16[16,4096]{1,0:T(8,128)(2,1)}, bf16[16,4096]{1,0:T(8,128)(2,1)S(1)}, u32[]{:S(2)}, u32[]{:S(2)}) collective-permute-start(bf16[16,4096]{1,0:T(8,128)(2,1)} %refs_0_.5), channel_id=1, source_target_pairs={{0,4},{2,6},{4,0},{6,2},{8,12},{10,14},{12,8},{14,10},{1,5},{3,7},... | collective-permute-start | bytes 393224 | tf_op jit(solution)/shard_map/ppermute | solution.py:123
  3.0 8.9 %collective-permute-start.5 = (bf16[16,4096]{1,0:T(8,128)(2,1)}, bf16[16,4096]{1,0:T(8,128)(2,1)S(1)}, u32[]{:S(2)}, u32[]{:S(2)}) collective-permute-start(bf16[16,4096]{1,0:T(8,128)(2,1)} %refs_0_.5), channel_id=1, source_target_pairs={{0,8},{2,10},{4,12},{6,14},{8,0},{10,2},{12,4},{14,6},{1,9},{3,11}... | collective-permute-start | bytes 393224 | tf_op jit(solution)/shard_map/ppermute | solution.py:123
  5.6 13.8 %collective-permute-start.7 = (bf16[16,4096]{1,0:T(8,128)(2,1)}, bf16[16,4096]{1,0:T(8,128)(2,1)S(1)}, u32[]{:S(2)}, u32[]{:S(2)}) collective-permute-start(bf16[16,4096]{1,0:T(8,128)(2,1)} %refs_0_.5), channel_id=1, source_target_pairs={{0,2},{2,0},{4,6},{6,4},{8,10},{10,8},{12,14},{14,12},{1,3},{3,1},... | collective-permute-start | bytes 393224 | tf_op jit(solution)/shard_map/ppermute | solution.py:127
  8.7 10.8 %collective-permute-start.9 = (bf16[16,4096]{1,0:T(8,128)(2,1)S(1)}, bf16[16,4096]{1,0:T(8,128)(2,1)S(1)}, u32[]{:S(2)}, u32[]{:S(2)}) collective-permute-start(bf16[16,4096]{1,0:T(8,128)(2,1)S(1)} %collective-permute-done.6.refs_2_), channel_id=1, source_target_pairs={{0,2},{2,0},{4,6},{6,4},{8,10},{10,8},{12,14},{14,12},{1,3},{3,1},... | collective-permute-start | bytes 393224 | tf_op jit(solution)/shard_map/ppermute | solution.py:127
  12.0 7.5 %collective-permute-start.8 = (bf16[16,4096]{1,0:T(8,128)(2,1)S(1)}, bf16[16,4096]{1,0:T(8,128)(2,1)S(1)}, u32[]{:S(2)}, u32[]{:S(2)}) collective-permute-start(bf16[16,4096]{1,0:T(8,128)(2,1)S(1)} %collective-permute-done.5.refs_1_), channel_id=1, source_target_pairs={{0,2},{2,0},{4,6},{6,4},{8,10},{10,8},{12,14},{14,12},{1,3},{3,1},... | collective-permute-start | bytes 393224 | tf_op jit(solution)/shard_map/ppermute | solution.py:127
  13.5 8.2 %collective-permute-start = (bf16[16,4096]{1,0:T(8,128)(2,1)}, bf16[16,4096]{1,0:T(8,128)(2,1)S(1)}, u32[]{:S(2)}, u32[]{:S(2)}) collective-permute-start(bf16[16,4096]{1,0:T(8,128)(2,1)} %refs_0_.5), channel_id=1, source_target_pairs={{0,12},{2,14},{4,8},{6,10},{8,4},{10,6},{12,0},{14,2},{1,13},{3,15... | collective-permute-start | bytes 393224 | tf_op jit(solution)/shard_map/ppermute | solution.py:123
  20.3 2.5 %copy-start = (bf16[512,4096]{1,0:T(8,128)(2,1)S(1)}, bf16[512,4096]{1,0:T(8,128)(2,1)}, u32[]{:S(2)}) copy-start(bf16[512,4096]{1,0:T(8,128)(2,1)} %weight_ref.3) | copy-start | bytes 12582916
  20.3 2.0 %collective-permute-start.11 = (f32[96,512]{1,0:T(8,128)S(1)}, f32[96,512]{1,0:T(8,128)S(1)}, u32[]{:S(2)}, u32[]{:S(2)}) collective-permute-start(f32[96,512]{1,0:T(8,128)S(1)} %project.7.up_ref), channel_id=1, source_target_pairs={{0,1},{1,0},{2,3},{3,2},{4,5},{5,4},{6,7},{7,6},{8,9},{9,8},{10,11... | collective-permute-start | bytes 589832 | tf_op jit(solution)/shard_map/ppermute | solution.py:131
  21.2 1.6 %collective-permute-start.10 = (f32[96,512]{1,0:T(8,128)S(1)}, f32[96,512]{1,0:T(8,128)S(1)}, u32[]{:S(2)}, u32[]{:S(2)}) collective-permute-start(f32[96,512]{1,0:T(8,128)S(1)} %project.6.gate_ref), channel_id=1, source_target_pairs={{0,1},{1,0},{2,3},{3,2},{4,5},{5,4},{6,7},{7,6},{8,9},{9,8},{10,11... | collective-permute-start | bytes 589832 | tf_op jit(solution)/shard_map/ppermute | solution.py:131
  21.7 6.0 %collective-permute-start.1 = (bf16[16,4096]{1,0:T(8,128)(2,1)S(1)}, bf16[16,4096]{1,0:T(8,128)(2,1)S(1)}, u32[]{:S(2)}, u32[]{:S(2)}) collective-permute-start(bf16[16,4096]{1,0:T(8,128)(2,1)S(1)} %collective-permute-done.refs_0_), channel_id=1, source_target_pairs={{0,2},{2,0},{4,6},{6,4},{8,10},{10,8},{12,14},{14,12},{1,3},{3,1},... | collective-permute-start | bytes 393224 | tf_op jit(solution)/shard_map/ppermute | solution.py:127
  23.6 6.4 %collective-permute-start.12 = (bf16[16,4096]{1,0:T(8,128)(2,1)S(1)}, bf16[16,4096]{1,0:T(8,128)(2,1)S(1)}, u32[]{:S(2)}, u32[]{:S(2)}) collective-permute-start(bf16[16,4096]{1,0:T(8,128)(2,1)S(1)} %get-tuple-element.19), channel_id=1, source_target_pairs={{0,2},{2,0},{4,6},{6,4},{8,10},{10,8},{12,14},{14,12},{1,3},{3,1},... | collective-permute-start | bytes 393224 | tf_op jit(solution)/shard_map/ppermute | solution.py:127
  28.5 2.4 %collective-permute-start.3 = (f32[32,512]{1,0:T(8,128)S(1)}, f32[32,512]{1,0:T(8,128)S(1)}, u32[]{:S(2)}, u32[]{:S(2)}) collective-permute-start(f32[32,512]{1,0:T(8,128)S(1)} %project.5.up_ref), channel_id=1, source_target_pairs={{0,1},{1,0},{2,3},{3,2},{4,5},{5,4},{6,7},{7,6},{8,9},{9,8},{10,11... | collective-permute-start | bytes 196616 | tf_op jit(solution)/shard_map/ppermute | solution.py:131
  28.6 6.5 %collective-permute-start.16 = (bf16[16,4096]{1,0:T(8,128)(2,1)S(1)}, bf16[16,4096]{1,0:T(8,128)(2,1)S(1)}, u32[]{:S(2)}, u32[]{:S(2)}) collective-permute-start(bf16[16,4096]{1,0:T(8,128)(2,1)S(1)} %get-tuple-element.23), channel_id=1, source_target_pairs={{0,2},{2,0},{4,6},{6,4},{8,10},{10,8},{12,14},{14,12},{1,3},{3,1},... | collective-permute-start | bytes 393224 | tf_op jit(solution)/shard_map/ppermute | solution.py:127
  30.0 7.5 %collective-permute-start.13 = (bf16[16,4096]{1,0:T(8,128)(2,1)S(1)}, bf16[16,4096]{1,0:T(8,128)(2,1)S(1)}, u32[]{:S(2)}, u32[]{:S(2)}) collective-permute-start(bf16[16,4096]{1,0:T(8,128)(2,1)S(1)} %add_pair.7), channel_id=1, source_target_pairs={{0,8},{2,10},{4,12},{6,14},{8,0},{10,2},{12,4},{14,6},{1,9},{3,11}... | collective-permute-start | bytes 393224 | tf_op jit(solution)/shard_map/ppermute | solution.py:123
  30.9 1.3 %collective-permute-start.2 = (f32[32,512]{1,0:T(8,128)S(1)}, f32[32,512]{1,0:T(8,128)S(1)}, u32[]{:S(2)}, u32[]{:S(2)}) collective-permute-start(f32[32,512]{1,0:T(8,128)S(1)} %project.4.gate_ref), channel_id=1, source_target_pairs={{0,1},{1,0},{2,3},{3,2},{4,5},{5,4},{6,7},{7,6},{8,9},{9,8},{10,11... | collective-permute-start | bytes 196616 | tf_op jit(solution)/shard_map/ppermute | solution.py:131
  33.0 6.4 %collective-permute-start.4 = (bf16[16,4096]{1,0:T(8,128)(2,1)S(1)}, bf16[16,4096]{1,0:T(8,128)(2,1)S(1)}, u32[]{:S(2)}, u32[]{:S(2)}) collective-permute-start(bf16[16,4096]{1,0:T(8,128)(2,1)S(1)} %get-tuple-element.17), channel_id=1, source_target_pairs={{0,2},{2,0},{4,6},{6,4},{8,10},{10,8},{12,14},{14,12},{1,3},{3,1},... | collective-permute-start | bytes 393224 | tf_op jit(solution)/shard_map/ppermute | solution.py:127
  33.7 7.7 %collective-permute-start.15 = (bf16[16,4096]{1,0:T(8,128)(2,1)S(1)}, bf16[16,4096]{1,0:T(8,128)(2,1)S(1)}, u32[]{:S(2)}, u32[]{:S(2)}) collective-permute-start(bf16[16,4096]{1,0:T(8,128)(2,1)S(1)} %get-tuple-element.22), channel_id=1, source_target_pairs={{0,2},{2,0},{4,6},{6,4},{8,10},{10,8},{12,14},{14,12},{1,3},{3,1},... | collective-permute-start | bytes 393224 | tf_op jit(solution)/shard_map/ppermute | solution.py:127
  35.1 5.7 %collective-permute-start.17 = (bf16[16,4096]{1,0:T(8,128)(2,1)S(1)}, bf16[16,4096]{1,0:T(8,128)(2,1)S(1)}, u32[]{:S(2)}, u32[]{:S(2)}) collective-permute-start(bf16[16,4096]{1,0:T(8,128)(2,1)S(1)} %add_pair.10), channel_id=1, source_target_pairs={{0,4},{2,6},{4,0},{6,2},{8,12},{10,14},{12,8},{14,10},{1,5},{3,7},... | collective-permute-start | bytes 393224 | tf_op jit(solution)/shard_map/ppermute | solution.py:123
  39.4 6.9 %collective-permute-start.14 = (bf16[16,4096]{1,0:T(8,128)(2,1)S(1)}, bf16[16,4096]{1,0:T(8,128)(2,1)S(1)}, u32[]{:S(2)}, u32[]{:S(2)}) collective-permute-start(bf16[16,4096]{1,0:T(8,128)(2,1)S(1)} %add_pair.9), channel_id=1, source_target_pairs={{0,12},{2,14},{4,8},{6,10},{8,4},{10,6},{12,0},{14,2},{1,13},{3,15... | collective-permute-start | bytes 393224 | tf_op jit(solution)/shard_map/ppermute | solution.py:123

commit v7 on v4

v7 whole, which is shorter than its diff:
```python
import functools

import jax
import jax.numpy as jnp
from jax import lax
from jax.experimental import pallas as pl
from jax.experimental.pallas import tpu as pltpu
from jax.sharding import PartitionSpec as P

F32 = jnp.float32
BF16 = jnp.bfloat16


def call(kernel, name, out_shape, flops, vmem, *operands):
    return pl.pallas_call(
        kernel,
        out_shape=out_shape,
        compiler_params=pltpu.CompilerParams(vmem_limit_bytes=vmem),
        cost_estimate=pl.CostEstimate(flops=flops, bytes_accessed=0, transcendentals=0),
        name=name,
    )(*operands)


def fetch_kernel(pieces, count, *refs):
    sources, targets, sems = refs[:count], refs[-1 - count:-1], refs[-1]
    copies = []
    for n, (source, target) in enumerate(zip(sources, targets)):
        step = source.shape[0] // pieces
        for i in range(pieces):
            part = pl.ds(i * step, step)
            copies.append(pltpu.make_async_copy(source.at[part], target.at[part], sems.at[n, i]))
    for copy in copies:
        copy.start()
    for copy in copies:
        copy.wait()


def fetch(weights, after, pieces=4):
    count = len(weights)
    return pl.pallas_call(
        functools.partial(fetch_kernel, pieces, count),
        in_specs=[pl.BlockSpec(memory_space=pl.ANY)] * (count + len(after)),
        out_specs=[pl.BlockSpec(memory_space=pltpu.VMEM)] * count,
        out_shape=[jax.ShapeDtypeStruct(w.shape, w.dtype) for w in weights],
        scratch_shapes=[pltpu.SemaphoreType.DMA((count, pieces))],
        compiler_params=pltpu.CompilerParams(vmem_limit_bytes=43 << 20),
        cost_estimate=pl.CostEstimate(flops=4000000000, bytes_accessed=0, transcendentals=0),
        name="fetch",
    )(*weights, *after)


def project_kernel(*refs):
    *block_refs, weight_ref, out_ref = refs
    rows = jnp.concatenate([ref[...] for ref in block_refs], axis=0)
    out_ref[...] = jnp.dot(rows, weight_ref[...], preferred_element_type=F32)


def project(blocks, weight):
    rows = sum(block.shape[0] for block in blocks)
    out = jax.ShapeDtypeStruct((rows, weight.shape[1]), F32)
    return call(project_kernel, "project", out, 400000000, 4 << 20, *blocks, weight)


def down_kernel(give, keep, gate_ref, gate_other_ref, up_ref, up_other_ref, weight_ref, *out_refs):
    gate_sum = gate_ref[...] + gate_other_ref[...]
    up_sum = up_ref[...] + up_other_ref[...]
    hidden = (jax.nn.silu(gate_sum) * up_sum).astype(BF16)
    width = weight_ref.shape[1]
    tile = min(512, width)
    rows = out_refs[0].shape[0]

    def column_tile(step, carry):
        columns = pl.ds(pl.multiple_of(step * tile, tile), tile)
        partial = jnp.dot(hidden, weight_ref[:, columns], preferred_element_type=F32)
        for k in range(keep + give):
            piece = partial[k * rows:(k + 1) * rows]
            out_refs[k][:, columns] = piece.astype(out_refs[k].dtype)
        return carry

    lax.fori_loop(0, width // tile, column_tile, 0, unroll=True)


def down(gate, gate_other, up, up_other, weight, rows, keep, give):
    width = weight.shape[1]
    outs = [jax.ShapeDtypeStruct((rows, width), F32)] * keep
    outs += [jax.ShapeDtypeStruct((rows, width), BF16)] * give
    flops = 2 * gate.shape[0] * weight.shape[0] * width
    return call(
        functools.partial(down_kernel, give, keep), "down", outs, flops, 4 << 20,
        gate, gate_other, up, up_other, weight,
    )


def add_kernel(count, own_ref, *refs):
    total = own_ref[...]
    for ref in refs[:count]:
        total = total + ref[...].astype(F32)
    refs[-1][...] = total.astype(refs[-1].dtype)


def add(own, arrived, dtype, hint=1000000, after=()):
    count = len(arrived)
    return pl.pallas_call(
        functools.partial(add_kernel, count),
        in_specs=[pl.BlockSpec(memory_space=pltpu.VMEM)] * (1 + count)
        + [pl.BlockSpec(memory_space=pl.ANY)] * len(after),
        out_shape=jax.ShapeDtypeStruct(own.shape, dtype),
        compiler_params=pltpu.CompilerParams(vmem_limit_bytes=2 << 20),
        cost_estimate=pl.CostEstimate(flops=hint, bytes_accessed=0, transcendentals=0),
        name="add",
    )(own, *arrived, *after)


def make_local(wide, narrow):
    fars = list(range(4, wide, 4))

    def swap(value, bits):
        return lax.ppermute(value, "wide", [(i, i ^ bits) for i in range(wide)])

    def across_cores(value):
        return lax.ppermute(value, "narrow", [(i, (i + 1) % narrow) for i in range(narrow)])

    def local(tokens, gate_weight, up_weight, down_weight):
        rows = tokens.shape[0]
        block = {0: tokens}
        for far in fars:
            block[far] = swap(tokens, far)
        block[2] = swap(tokens, 2)
        block[1] = swap(tokens, 1)
        block[2], block[1] = lax.optimization_barrier((block[2], block[1]))
        block[3] = swap(block[2], 1)
        for far in fars:
            for near in (2, 3, 1):
                block[far + near] = swap(block[far], near)
        gate_held, up_held = fetch([gate_weight, up_weight], [block[3]])
        stay = [0, 2] + fars
        away = [b for b in range(wide) if b not in stay]
        blocks = [block[b] for b in stay + away]
        gate_part = project(blocks, gate_held)
        up_part = project(blocks, up_held)
        outs = down(
            gate_part, across_cores(gate_part), up_part, across_cores(up_part),
            down_weight, rows, len(stay), len(away),
        )
        part = dict(zip(stay + away, outs))
        sums = []
        for far in fars:
            quad = [swap(part[far + near], near) for near in (2, 3, 1)]
            sums.append(add(part[far], quad, BF16))
        arrived = [swap(value, far) for value, far in zip(sums, fars)]
        pair = add(part[2], [swap(part[3], 1)], BF16, after=sums)
        total = add(part[0], arrived, F32, 1500000000)
        return add(total, [swap(part[1], 1), swap(pair, 2)], BF16)

    return local


def solution(mesh):
    return jax.shard_map(
        make_local(mesh.shape["wide"], mesh.shape["narrow"]),
        mesh=mesh,
        in_specs=(
            P(("groups", "wide"), "narrow"),
            P("narrow", "wide"),
            P("narrow", "wide"),
            P("wide", "narrow"),
        ),
        out_specs=P(("groups", "wide"), "narrow"),
        check_vma=False,
    )
```

time: 48.9 us -> 47.3 us (0.967)
  waiting for transfers between devices: 24 us -> 19 us
  starting transfers between devices: 18.2 us -> 21.6 us
    ppermute x16, waiting for transfers between devices: 24 us -> 19 us  [the longest x14 17.8 us: swap(): return lax.ppermute(value, 'wide', [(i, i ^ bits) for i in range(wide)])]
    ppermute x16, starting transfers between devices: 18.2 us -> 21.6 us  [the longest x14 21 us: swap(): return lax.ppermute(value, 'wide', [(i, i ^ bits) for i in range(wide)])]
    pallas_call x10 -> x3, Pallas kernels: 2.99 us -> 2.17 us  [call(): pl.pallas_call(kernel, out_shape=out_shape, compiler_params=pltpu.Compile...]
    pallas_call x1 -> x5, Pallas kernels: 3.47 us -> 4.28 us  [the longest x1 3.47 us: fetch(): pl.pallas_call(functools.partial(fetch_kernel, pieces, count), in_specs=[...]
  transfers between devices with their start and end apart: 16 -> 16, of which waited for: 12 -> 11; matrix products, arithmetic and copies ran while one was open for 0% -> 0% of each run, Pallas kernels for 9% -> 9%
where the time goes in v7:
time: 47.3 us; the launch traced here: 47.1 us
  starting transfers between devices  21.6 us (46%)
  waiting for transfers between devices  19 us (40%)
  Pallas kernels  6.44 us (14%)
    ppermute x14, starting transfers between devices, swap(): return lax.ppermute(value, 'wide', [(i, i ^ bits) for i in range(wide)])  21 us
    ppermute x14, waiting for transfers between devices, swap(): return lax.ppermute(value, 'wide', [(i, i ^ bits) for i in range(wide)])  17.8 us
    pallas_call x1, Pallas kernels, fetch(): pl.pallas_call(functools.partial(fetch_kernel, pieces, count), in_specs=[...  3.47 us
    pallas_call x3, Pallas kernels, call(): pl.pallas_call(kernel, out_shape=out_shape, compiler_params=pltpu.Compile...  2.17 us
    ppermute x2, waiting for transfers between devices, across_cores(): lax.ppermute(value, 'narrow', [(i, (i + 1) % narrow) for i in range(narro...  1.16 us
  transfers between devices with their start and end apart: 16, of which 11 were waited for; matrix products, arithmetic and copies ran while one was open for 0% of the time, Pallas kernels for 9%

profile of v7, /device:TPU:0, one launch (start us, length us, event | category | flops | bytes accessed | tf_op | source)
XLA Modules:
  0.0 47.1 jit_solution(3402284429864381695)
XLA Ops:
  0.0 0.0 copy-start.1
  0.0 3.0 %collective-permute-start.1 = (bf16[16,4096]{1,0:T(8,128)(2,1)}, bf16[16,4096]{1,0:T(8,128)(2,1)S(1)}, u32[]{:S(2)}, u32[]{:S(2)}) collective-permute-start(bf16[16,4096]{1,0:T(8,128)(2,1)} %refs_0_.5), channel_id=1, source_target_pairs={{0,2},{2,0},{4,6},{6,4},{8,10},{10,8},{12,14},{14,12},{1,3},{3,1},... | collective-permute-start | bytes 393224 | tf_op jit(solution)/shard_map/ppermute | solution.py:118
  3.0 1.6 %collective-permute-start = (bf16[16,4096]{1,0:T(8,128)(2,1)}, bf16[16,4096]{1,0:T(8,128)(2,1)S(1)}, u32[]{:S(2)}, u32[]{:S(2)}) collective-permute-start(bf16[16,4096]{1,0:T(8,128)(2,1)} %refs_0_.5), channel_id=1, source_target_pairs={{0,4},{2,6},{4,0},{6,2},{8,12},{10,14},{12,8},{14,10},{1,5},{3,7},... | collective-permute-start | bytes 393224 | tf_op jit(solution)/shard_map/ppermute | solution.py:118
  4.5 2.6 %collective-permute-start.2 = (bf16[16,4096]{1,0:T(8,128)(2,1)}, bf16[16,4096]{1,0:T(8,128)(2,1)S(1)}, u32[]{:S(2)}, u32[]{:S(2)}) collective-permute-start(bf16[16,4096]{1,0:T(8,128)(2,1)} %refs_0_.5), channel_id=1, source_target_pairs={{0,8},{2,10},{4,12},{6,14},{8,0},{10,2},{12,4},{14,6},{1,9},{3,11}... | collective-permute-start | bytes 393224 | tf_op jit(solution)/shard_map/ppermute | solution.py:118
  7.1 0.0 collective-permute-done.1.refs_3_
  7.1 2.7 %collective-permute-done.refs_1_ = bf16[16,4096]{1,0:T(8,128)(2,1)S(1)} collective-permute-done((bf16[16,4096]{1,0:T(8,128)(2,1)}, bf16[16,4096]{1,0:T(8,128)(2,1)S(1)}, u32[]{:S(2)}, u32[]{:S(2)}) %collective-permute-start) | collective-permute-done | bytes 131104 | tf_op jit(solution)/shard_map/ppermute | solution.py:118
  9.8 0.2 collective-permute-start.3
  10.0 3.3 %collective-permute-done.2.refs_2_ = bf16[16,4096]{1,0:T(8,128)(2,1)S(1)} collective-permute-done((bf16[16,4096]{1,0:T(8,128)(2,1)}, bf16[16,4096]{1,0:T(8,128)(2,1)S(1)}, u32[]{:S(2)}, u32[]{:S(2)}) %collective-permute-start.2) | collective-permute-done | bytes 131104 | tf_op jit(solution)/shard_map/ppermute | solution.py:118
  13.3 0.2 collective-permute-start.6
  13.5 1.8 %collective-permute-start.5 = (bf16[16,4096]{1,0:T(8,128)(2,1)S(1)}, bf16[16,4096]{1,0:T(8,128)(2,1)S(1)}, u32[]{:S(2)}, u32[]{:S(2)}) collective-permute-start(bf16[16,4096]{1,0:T(8,128)(2,1)S(1)} %collective-permute-done.2.refs_2_), channel_id=1, source_target_pairs={{0,4},{2,6},{4,0},{6,2},{8,12},{10,14},{12,8},{14,10},{1,5},{3,7},... | collective-permute-start | bytes 393224 | tf_op jit(solution)/shard_map/ppermute | solution.py:118
  15.3 1.5 %collective-permute-start.4 = (bf16[16,4096]{1,0:T(8,128)(2,1)S(1)}, bf16[16,4096]{1,0:T(8,128)(2,1)S(1)}, u32[]{:S(2)}, u32[]{:S(2)}) collective-permute-start(bf16[16,4096]{1,0:T(8,128)(2,1)S(1)} %collective-permute-done.2.refs_2_), channel_id=1, source_target_pairs={{0,2},{2,0},{4,6},{6,4},{8,10},{10,8},{12,14},{14,12},{1,3},{3,1},... | collective-permute-start | bytes 393224 | tf_op jit(solution)/shard_map/ppermute | solution.py:118
  16.8 0.2 collective-permute-done.3.refs_2_.refs_4_
  17.0 3.5 %fetch.1 = (bf16[4096,512]{1,0:T(8,128)(2,1)S(1)}, bf16[4096,512]{1,0:T(8,128)(2,1)S(1)}) custom-call(bf16[4096,512]{1,0:T(8,128)(2,1)} %refs_0_.3, bf16[4096,512]{1,0:T(8,128)(2,1)} %refs_1_.1, bf16[16,4096]{1,0:T(8,128)(2,1)S(1)} %collective-permute-done.3.refs_2_.refs_4_), custom_call_target="tpu_custom_call" | custom-call | flops 4000000000 | tf_op jit(solution)/shard_map/fetch/pallas_call | solution.py:40
  20.5 0.0 collective-permute-done.6.refs_7_
  20.5 0.0 collective-permute-done.5.refs_6_
  20.5 0.0 collective-permute-done.4.refs_5_
  20.6 0.0 copy-done.1
  20.6 0.0 copy-start
  20.6 0.7 %project.3.up_ref = f32[128,512]{1,0:T(8,128)S(1)} custom-call(bf16[16,4096]{1,0:T(8,128)(2,1)S(1)} %copy-done.1, bf16[16,4096]{1,0:T(8,128)(2,1)S(1)} %collective-permute-done.refs_1_, bf16[16,4096]{1,0:T(8,128)(2,1)S(1)} %collective-permute-done.2.refs_2_, bf16[16,4096]{1,0:T(8,128)(2,1)S(1)} %collective-permute-done.1.refs_3_, ...), custom_call_target="tpu_custom_call" | custom-call | flops 400000000 | tf_op jit(solution)/shard_map/project/pallas_call | solution.py:15
  21.3 0.1 collective-permute-start.8
  21.4 0.7 %project.2.gate_ref = f32[128,512]{1,0:T(8,128)S(1)} custom-call(bf16[16,4096]{1,0:T(8,128)(2,1)S(1)} %copy-done.1, bf16[16,4096]{1,0:T(8,128)(2,1)S(1)} %collective-permute-done.refs_1_, bf16[16,4096]{1,0:T(8,128)(2,1)S(1)} %collective-permute-done.2.refs_2_, bf16[16,4096]{1,0:T(8,128)(2,1)S(1)} %collective-permute-done.1.refs_3_, ...), custom_call_target="tpu_custom_call" | custom-call | flops 400000000 | tf_op jit(solution)/shard_map/project/pallas_call | solution.py:15
  22.1 0.6 %collective-permute-start.7 = (f32[128,512]{1,0:T(8,128)S(1)}, f32[128,512]{1,0:T(8,128)S(1)}, u32[]{:S(2)}, u32[]{:S(2)}) collective-permute-start(f32[128,512]{1,0:T(8,128)S(1)} %project.2.gate_ref), channel_id=1, source_target_pairs={{0,1},{1,0},{2,3},{3,2},{4,5},{5,4},{6,7},{7,6},{8,9},{9,8},{10,11... | collective-permute-start | bytes 786440 | tf_op jit(solution)/shard_map/ppermute | solution.py:121
  22.7 0.2 collective-permute-done.8.up_other_ref
  22.9 0.9 %collective-permute-done.7.gate_other_ref = f32[128,512]{1,0:T(8,128)S(1)} collective-permute-done((f32[128,512]{1,0:T(8,128)S(1)}, f32[128,512]{1,0:T(8,128)S(1)}, u32[]{:S(2)}, u32[]{:S(2)}) %collective-permute-start.7) | collective-permute-done | bytes 262176 | tf_op jit(solution)/shard_map/ppermute | solution.py:121
  23.8 0.0 copy-done
  23.8 0.7 %down.1 = (f32[16,4096]{1,0:T(8,128)S(1)}, f32[16,4096]{1,0:T(8,128)S(1)}, f32[16,4096]{1,0:T(8,128)S(1)}, bf16[16,4096]{1,0:T(8,128)(2,1)S(1)}, bf16[16,4096]{1...) custom-call(f32[128,512]{1,0:T(8,128)S(1)} %project.2.gate_ref, ...), custom_call_target="tpu_custom_call" | custom-call | flops 536870912 | tf_op jit(solution)/shard_map/down/pallas_call | solution.py:15
  24.6 0.5 %collective-permute-start.9 = (bf16[16,4096]{1,0:T(8,128)(2,1)S(1)}, bf16[16,4096]{1,0:T(8,128)(2,1)S(1)}, u32[]{:S(2)}, u32[]{:S(2)}) collective-permute-start(bf16[16,4096]{1,0:T(8,128)(2,1)S(1)} %get-tuple-element.23), channel_id=1, source_target_pairs={{0,4},{2,6},{4,0},{6,2},{8,12},{10,14},{12,8},{14,10},{1,5},{3,7},... | collective-permute-start | bytes 393224 | tf_op jit(solution)/shard_map/ppermute | solution.py:118
  25.1 2.2 %collective-permute-start.10 = (bf16[16,4096]{1,0:T(8,128)(2,1)S(1)}, bf16[16,4096]{1,0:T(8,128)(2,1)S(1)}, u32[]{:S(2)}, u32[]{:S(2)}) collective-permute-start(bf16[16,4096]{1,0:T(8,128)(2,1)S(1)} %get-tuple-element.24), channel_id=1, source_target_pairs={{0,6},{2,4},{4,2},{6,0},{8,14},{10,12},{12,10},{14,8},{1,7},{3,5},... | collective-permute-start | bytes 393224 | tf_op jit(solution)/shard_map/ppermute | solution.py:118
  27.3 0.8 %collective-permute-start.11 = (bf16[16,4096]{1,0:T(8,128)(2,1)S(1)}, bf16[16,4096]{1,0:T(8,128)(2,1)S(1)}, u32[]{:S(2)}, u32[]{:S(2)}) collective-permute-start(bf16[16,4096]{1,0:T(8,128)(2,1)S(1)} %get-tuple-element.25), channel_id=1, source_target_pairs={{0,2},{2,0},{4,6},{6,4},{8,10},{10,8},{12,14},{14,12},{1,3},{3,1},... | collective-permute-start | bytes 393224 | tf_op jit(solution)/shard_map/ppermute | solution.py:118
  28.1 1.2 %collective-permute-start.14 = (bf16[16,4096]{1,0:T(8,128)(2,1)S(1)}, bf16[16,4096]{1,0:T(8,128)(2,1)S(1)}, u32[]{:S(2)}, u32[]{:S(2)}) collective-permute-start(bf16[16,4096]{1,0:T(8,128)(2,1)S(1)} %get-tuple-element.28), channel_id=1, source_target_pairs={{0,2},{2,0},{4,6},{6,4},{8,10},{10,8},{12,14},{14,12},{1,3},{3,1},... | collective-permute-start | bytes 393224 | tf_op jit(solution)/shard_map/ppermute | solution.py:118
  29.3 1.6 %collective-permute-done.9.refs_0_ = bf16[16,4096]{1,0:T(8,128)(2,1)S(1)} collective-permute-done((bf16[16,4096]{1,0:T(8,128)(2,1)S(1)}, bf16[16,4096]{1,0:T(8,128)(2,1)S(1)}, u32[]{:S(2)}, u32[]{:S(2)}) %collective-permute-start.9) | collective-permute-done | bytes 131104 | tf_op jit(solution)/shard_map/ppermute | solution.py:118
  31.0 3.0 %collective-permute-done.10.refs_1_ = bf16[16,4096]{1,0:T(8,128)(2,1)S(1)} collective-permute-done((bf16[16,4096]{1,0:T(8,128)(2,1)S(1)}, bf16[16,4096]{1,0:T(8,128)(2,1)S(1)}, u32[]{:S(2)}, u32[]{:S(2)}) %collective-permute-start.10) | collective-permute-done | bytes 131104 | tf_op jit(solution)/shard_map/ppermute | solution.py:118
  34.0 2.4 %collective-permute-done.11.refs_2_ = bf16[16,4096]{1,0:T(8,128)(2,1)S(1)} collective-permute-done((bf16[16,4096]{1,0:T(8,128)(2,1)S(1)}, bf16[16,4096]{1,0:T(8,128)(2,1)S(1)}, u32[]{:S(2)}, u32[]{:S(2)}) %collective-permute-start.11) | collective-permute-done | bytes 131104 | tf_op jit(solution)/shard_map/ppermute | solution.py:118
  36.3 0.1 add.4.refs_1_
  36.4 3.4 %collective-permute-start.12 = (bf16[16,4096]{1,0:T(8,128)(2,1)S(1)}, bf16[16,4096]{1,0:T(8,128)(2,1)S(1)}, u32[]{:S(2)}, u32[]{:S(2)}) collective-permute-start(bf16[16,4096]{1,0:T(8,128)(2,1)S(1)} %add.4.refs_1_), channel_id=1, source_target_pairs={{0,8},{2,10},{4,12},{6,14},{8,0},{10,2},{12,4},{14,6},{1,9},{3,11}... | collective-permute-start | bytes 393224 | tf_op jit(solution)/shard_map/ppermute | solution.py:118
  39.8 1.5 %collective-permute-start.13 = (bf16[16,4096]{1,0:T(8,128)(2,1)S(1)}, bf16[16,4096]{1,0:T(8,128)(2,1)S(1)}, u32[]{:S(2)}, u32[]{:S(2)}) collective-permute-start(bf16[16,4096]{1,0:T(8,128)(2,1)S(1)} %get-tuple-element.26), channel_id=1, source_target_pairs={{0,2},{2,0},{4,6},{6,4},{8,10},{10,8},{12,14},{14,12},{1,3},{3,1},... | collective-permute-start | bytes 393224 | tf_op jit(solution)/shard_map/ppermute | solution.py:118
  41.4 0.0 collective-permute-done.14.refs_0_
  41.4 0.4 collective-permute-start.15
  41.8 2.3 %collective-permute-done.12.refs_0_ = bf16[16,4096]{1,0:T(8,128)(2,1)S(1)} collective-permute-done((bf16[16,4096]{1,0:T(8,128)(2,1)S(1)}, bf16[16,4096]{1,0:T(8,128)(2,1)S(1)}, u32[]{:S(2)}, u32[]{:S(2)}) %collective-permute-start.12) | collective-permute-done | bytes 131104 | tf_op jit(solution)/shard_map/ppermute | solution.py:118
  44.1 0.7 %collective-permute-done.13.refs_0_ = bf16[16,4096]{1,0:T(8,128)(2,1)S(1)} collective-permute-done((bf16[16,4096]{1,0:T(8,128)(2,1)S(1)}, bf16[16,4096]{1,0:T(8,128)(2,1)S(1)}, u32[]{:S(2)}, u32[]{:S(2)}) %collective-permute-start.13) | collective-permute-done | bytes 131104 | tf_op jit(solution)/shard_map/ppermute | solution.py:118
  44.8 1.6 %collective-permute-done.15.refs_1_ = bf16[16,4096]{1,0:T(8,128)(2,1)S(1)} collective-permute-done((bf16[16,4096]{1,0:T(8,128)(2,1)S(1)}, bf16[16,4096]{1,0:T(8,128)(2,1)S(1)}, u32[]{:S(2)}, u32[]{:S(2)}) %collective-permute-start.15) | collective-permute-done | bytes 131104 | tf_op jit(solution)/shard_map/ppermute | solution.py:118
  46.4 0.7 %add.7 = bf16[16,4096]{1,0:T(8,128)(2,1)} custom-call(f32[16,4096]{1,0:T(8,128)S(1)} %add.5.own_ref, bf16[16,4096]{1,0:T(8,128)(2,1)S(1)} %collective-permute-done.13.refs_0_, bf16[16,4096]{1,0:T(8,128)(2,1)S(1)} %collective-permute-done.15.refs_1_), custom_call_target="tpu_custom_call" | custom-call | flops 1000000 | tf_op jit(solution)/shard_map/add/pallas_call | solution.py:103
  (2 shorter events, 0.0 us)
Async XLA Ops:
  0.0 20.6 %copy-start.1 = (bf16[16,4096]{1,0:T(8,128)(2,1)S(1)}, bf16[16,4096]{1,0:T(8,128)(2,1)}, u32[]{:S(2)}) copy-start(bf16[16,4096]{1,0:T(8,128)(2,1)} %refs_0_.5) | copy-start | bytes 393220
  0.0 7.1 %collective-permute-start.1 = (bf16[16,4096]{1,0:T(8,128)(2,1)}, bf16[16,4096]{1,0:T(8,128)(2,1)S(1)}, u32[]{:S(2)}, u32[]{:S(2)}) collective-permute-start(bf16[16,4096]{1,0:T(8,128)(2,1)} %refs_0_.5), channel_id=1, source_target_pairs={{0,2},{2,0},{4,6},{6,4},{8,10},{10,8},{12,14},{14,12},{1,3},{3,1},... | collective-permute-start | bytes 393224 | tf_op jit(solution)/shard_map/ppermute | solution.py:118
  3.0 6.8 %collective-permute-start = (bf16[16,4096]{1,0:T(8,128)(2,1)}, bf16[16,4096]{1,0:T(8,128)(2,1)S(1)}, u32[]{:S(2)}, u32[]{:S(2)}) collective-permute-start(bf16[16,4096]{1,0:T(8,128)(2,1)} %refs_0_.5), channel_id=1, source_target_pairs={{0,4},{2,6},{4,0},{6,2},{8,12},{10,14},{12,8},{14,10},{1,5},{3,7},... | collective-permute-start | bytes 393224 | tf_op jit(solution)/shard_map/ppermute | solution.py:118
  4.5 8.8 %collective-permute-start.2 = (bf16[16,4096]{1,0:T(8,128)(2,1)}, bf16[16,4096]{1,0:T(8,128)(2,1)S(1)}, u32[]{:S(2)}, u32[]{:S(2)}) collective-permute-start(bf16[16,4096]{1,0:T(8,128)(2,1)} %refs_0_.5), channel_id=1, source_target_pairs={{0,8},{2,10},{4,12},{6,14},{8,0},{10,2},{12,4},{14,6},{1,9},{3,11}... | collective-permute-start | bytes 393224 | tf_op jit(solution)/shard_map/ppermute | solution.py:118
  9.8 7.2 %collective-permute-start.3 = (bf16[16,4096]{1,0:T(8,128)(2,1)S(1)}, bf16[16,4096]{1,0:T(8,128)(2,1)S(1)}, u32[]{:S(2)}, u32[]{:S(2)}) collective-permute-start(bf16[16,4096]{1,0:T(8,128)(2,1)S(1)} %collective-permute-done.refs_1_), channel_id=1, source_target_pairs={{0,2},{2,0},{4,6},{6,4},{8,10},{10,8},{12,14},{14,12},{1,3},{3,1},... | collective-permute-start | bytes 393224 | tf_op jit(solution)/shard_map/ppermute | solution.py:118
  13.3 7.2 %collective-permute-start.6 = (bf16[16,4096]{1,0:T(8,128)(2,1)S(1)}, bf16[16,4096]{1,0:T(8,128)(2,1)S(1)}, u32[]{:S(2)}, u32[]{:S(2)}) collective-permute-start(bf16[16,4096]{1,0:T(8,128)(2,1)S(1)} %collective-permute-done.2.refs_2_), channel_id=1, source_target_pairs={{0,6},{2,4},{4,2},{6,0},{8,14},{10,12},{12,10},{14,8},{1,7},{3,5},... | collective-permute-start | bytes 393224 | tf_op jit(solution)/shard_map/ppermute | solution.py:118
  13.5 7.1 %collective-permute-start.5 = (bf16[16,4096]{1,0:T(8,128)(2,1)S(1)}, bf16[16,4096]{1,0:T(8,128)(2,1)S(1)}, u32[]{:S(2)}, u32[]{:S(2)}) collective-permute-start(bf16[16,4096]{1,0:T(8,128)(2,1)S(1)} %collective-permute-done.2.refs_2_), channel_id=1, source_target_pairs={{0,4},{2,6},{4,0},{6,2},{8,12},{10,14},{12,8},{14,10},{1,5},{3,7},... | collective-permute-start | bytes 393224 | tf_op jit(solution)/shard_map/ppermute | solution.py:118
  15.3 5.3 %collective-permute-start.4 = (bf16[16,4096]{1,0:T(8,128)(2,1)S(1)}, bf16[16,4096]{1,0:T(8,128)(2,1)S(1)}, u32[]{:S(2)}, u32[]{:S(2)}) collective-permute-start(bf16[16,4096]{1,0:T(8,128)(2,1)S(1)} %collective-permute-done.2.refs_2_), channel_id=1, source_target_pairs={{0,2},{2,0},{4,6},{6,4},{8,10},{10,8},{12,14},{14,12},{1,3},{3,1},... | collective-permute-start | bytes 393224 | tf_op jit(solution)/shard_map/ppermute | solution.py:118
  20.6 3.2 %copy-start = (bf16[512,4096]{1,0:T(8,128)(2,1)S(1)}, bf16[512,4096]{1,0:T(8,128)(2,1)}, u32[]{:S(2)}) copy-start(bf16[512,4096]{1,0:T(8,128)(2,1)} %weight_ref.1) | copy-start | bytes 12582916
  21.3 1.6 %collective-permute-start.8 = (f32[128,512]{1,0:T(8,128)S(1)}, f32[128,512]{1,0:T(8,128)S(1)}, u32[]{:S(2)}, u32[]{:S(2)}) collective-permute-start(f32[128,512]{1,0:T(8,128)S(1)} %project.3.up_ref), channel_id=1, source_target_pairs={{0,1},{1,0},{2,3},{3,2},{4,5},{5,4},{6,7},{7,6},{8,9},{9,8},{10,11... | collective-permute-start | bytes 786440 | tf_op jit(solution)/shard_map/ppermute | solution.py:121
  22.1 1.7 %collective-permute-start.7 = (f32[128,512]{1,0:T(8,128)S(1)}, f32[128,512]{1,0:T(8,128)S(1)}, u32[]{:S(2)}, u32[]{:S(2)}) collective-permute-start(f32[128,512]{1,0:T(8,128)S(1)} %project.2.gate_ref), channel_id=1, source_target_pairs={{0,1},{1,0},{2,3},{3,2},{4,5},{5,4},{6,7},{7,6},{8,9},{9,8},{10,11... | collective-permute-start | bytes 786440 | tf_op jit(solution)/shard_map/ppermute | solution.py:121
  24.6 6.4 %collective-permute-start.9 = (bf16[16,4096]{1,0:T(8,128)(2,1)S(1)}, bf16[16,4096]{1,0:T(8,128)(2,1)S(1)}, u32[]{:S(2)}, u32[]{:S(2)}) collective-permute-start(bf16[16,4096]{1,0:T(8,128)(2,1)S(1)} %get-tuple-element.23), channel_id=1, source_target_pairs={{0,4},{2,6},{4,0},{6,2},{8,12},{10,14},{12,8},{14,10},{1,5},{3,7},... | collective-permute-start | bytes 393224 | tf_op jit(solution)/shard_map/ppermute | solution.py:118
  25.1 8.9 %collective-permute-start.10 = (bf16[16,4096]{1,0:T(8,128)(2,1)S(1)}, bf16[16,4096]{1,0:T(8,128)(2,1)S(1)}, u32[]{:S(2)}, u32[]{:S(2)}) collective-permute-start(bf16[16,4096]{1,0:T(8,128)(2,1)S(1)} %get-tuple-element.24), channel_id=1, source_target_pairs={{0,6},{2,4},{4,2},{6,0},{8,14},{10,12},{12,10},{14,8},{1,7},{3,5},... | collective-permute-start | bytes 393224 | tf_op jit(solution)/shard_map/ppermute | solution.py:118
  27.3 9.0 %collective-permute-start.11 = (bf16[16,4096]{1,0:T(8,128)(2,1)S(1)}, bf16[16,4096]{1,0:T(8,128)(2,1)S(1)}, u32[]{:S(2)}, u32[]{:S(2)}) collective-permute-start(bf16[16,4096]{1,0:T(8,128)(2,1)S(1)} %get-tuple-element.25), channel_id=1, source_target_pairs={{0,2},{2,0},{4,6},{6,4},{8,10},{10,8},{12,14},{14,12},{1,3},{3,1},... | collective-permute-start | bytes 393224 | tf_op jit(solution)/shard_map/ppermute | solution.py:118
  28.1 13.2 %collective-permute-start.14 = (bf16[16,4096]{1,0:T(8,128)(2,1)S(1)}, bf16[16,4096]{1,0:T(8,128)(2,1)S(1)}, u32[]{:S(2)}, u32[]{:S(2)}) collective-permute-start(bf16[16,4096]{1,0:T(8,128)(2,1)S(1)} %get-tuple-element.28), channel_id=1, source_target_pairs={{0,2},{2,0},{4,6},{6,4},{8,10},{10,8},{12,14},{14,12},{1,3},{3,1},... | collective-permute-start | bytes 393224 | tf_op jit(solution)/shard_map/ppermute | solution.py:118
  36.4 7.7 %collective-permute-start.12 = (bf16[16,4096]{1,0:T(8,128)(2,1)S(1)}, bf16[16,4096]{1,0:T(8,128)(2,1)S(1)}, u32[]{:S(2)}, u32[]{:S(2)}) collective-permute-start(bf16[16,4096]{1,0:T(8,128)(2,1)S(1)} %add.4.refs_1_), channel_id=1, source_target_pairs={{0,8},{2,10},{4,12},{6,14},{8,0},{10,2},{12,4},{14,6},{1,9},{3,11}... | collective-permute-start | bytes 393224 | tf_op jit(solution)/shard_map/ppermute | solution.py:118
  39.8 5.0 %collective-permute-start.13 = (bf16[16,4096]{1,0:T(8,128)(2,1)S(1)}, bf16[16,4096]{1,0:T(8,128)(2,1)S(1)}, u32[]{:S(2)}, u32[]{:S(2)}) collective-permute-start(bf16[16,4096]{1,0:T(8,128)(2,1)S(1)} %get-tuple-element.26), channel_id=1, source_target_pairs={{0,2},{2,0},{4,6},{6,4},{8,10},{10,8},{12,14},{14,12},{1,3},{3,1},... | collective-permute-start | bytes 393224 | tf_op jit(solution)/shard_map/ppermute | solution.py:118
  41.4 5.0 %collective-permute-start.15 = (bf16[16,4096]{1,0:T(8,128)(2,1)S(1)}, bf16[16,4096]{1,0:T(8,128)(2,1)S(1)}, u32[]{:S(2)}, u32[]{:S(2)}) collective-permute-start(bf16[16,4096]{1,0:T(8,128)(2,1)S(1)} %add.6), channel_id=1, source_target_pairs={{0,4},{2,6},{4,0},{6,2},{8,12},{10,14},{12,8},{14,10},{1,5},{3,7},... | collective-permute-start | bytes 393224 | tf_op jit(solution)/shard_map/ppermute | solution.py:118

commit v8 on v7

--- a/solution.py
+++ b/solution.py
@@ -22,9 +22,10 @@
 
 
 def fetch_kernel(pieces, count, *refs):
-    sources, targets, sems = refs[:count], refs[-1 - count:-1], refs[-1]
+    sems = refs[-1]
     copies = []
-    for n, (source, target) in enumerate(zip(sources, targets)):
+    for n in range(count):
+        source, target = refs[n], refs[count + n]
         step = source.shape[0] // pieces
         for i in range(pieces):
             part = pl.ds(i * step, step)
@@ -35,18 +36,31 @@
         copy.wait()
 
 
-def fetch(weights, after, pieces=4):
+def fetch(weights, pieces=4):
     count = len(weights)
     return pl.pallas_call(
         functools.partial(fetch_kernel, pieces, count),
-        in_specs=[pl.BlockSpec(memory_space=pl.ANY)] * (count + len(after)),
+        in_specs=[pl.BlockSpec(memory_space=pl.ANY)] * count,
         out_specs=[pl.BlockSpec(memory_space=pltpu.VMEM)] * count,
         out_shape=[jax.ShapeDtypeStruct(w.shape, w.dtype) for w in weights],
         scratch_shapes=[pltpu.SemaphoreType.DMA((count, pieces))],
         compiler_params=pltpu.CompilerParams(vmem_limit_bytes=43 << 20),
         cost_estimate=pl.CostEstimate(flops=4000000000, bytes_accessed=0, transcendentals=0),
         name="fetch",
-    )(*weights, *after)
+    )(*weights)
+
+
+def pack_kernel(*refs):
+    *block_refs, out_ref = refs
+    rows = block_refs[0].shape[0]
+    for k, ref in enumerate(block_refs):
+        out_ref[k * rows:(k + 1) * rows, :] = ref[...]
+
+
+def pack(blocks):
+    rows, width = blocks[0].shape
+    out = jax.ShapeDtypeStruct((len(blocks) * rows, width), BF16)
+    return call(pack_kernel, "pack", out, 4000000000, 2 << 20, *blocks)
 
 
 def project_kernel(*refs):
@@ -61,7 +75,7 @@
     return call(project_kernel, "project", out, 400000000, 4 << 20, *blocks, weight)
 
 
-def down_kernel(give, keep, gate_ref, gate_other_ref, up_ref, up_other_ref, weight_ref, *out_refs):
+def down_kernel(gate_ref, gate_other_ref, up_ref, up_other_ref, weight_ref, *out_refs):
     gate_sum = gate_ref[...] + gate_other_ref[...]
     up_sum = up_ref[...] + up_other_ref[...]
     hidden = (jax.nn.silu(gate_sum) * up_sum).astype(BF16)
@@ -72,22 +86,19 @@
     def column_tile(step, carry):
         columns = pl.ds(pl.multiple_of(step * tile, tile), tile)
         partial = jnp.dot(hidden, weight_ref[:, columns], preferred_element_type=F32)
-        for k in range(keep + give):
-            piece = partial[k * rows:(k + 1) * rows]
-            out_refs[k][:, columns] = piece.astype(out_refs[k].dtype)
+        for k, out_ref in enumerate(out_refs):
+            out_ref[:, columns] = partial[k * rows:(k + 1) * rows].astype(out_ref.dtype)
         return carry
 
     lax.fori_loop(0, width // tile, column_tile, 0, unroll=True)
 
 
-def down(gate, gate_other, up, up_other, weight, rows, keep, give):
+def down(gate, gate_other, up, up_other, weight, rows, dtypes):
     width = weight.shape[1]
-    outs = [jax.ShapeDtypeStruct((rows, width), F32)] * keep
-    outs += [jax.ShapeDtypeStruct((rows, width), BF16)] * give
+    outs = [jax.ShapeDtypeStruct((rows, width), dtype) for dtype in dtypes]
     flops = 2 * gate.shape[0] * weight.shape[0] * width
     return call(
-        functools.partial(down_kernel, give, keep), "down", outs, flops, 4 << 20,
-        gate, gate_other, up, up_other, weight,
+        down_kernel, "down", outs, flops, 4 << 20, gate, gate_other, up, up_other, weight
     )
 
 
@@ -127,28 +138,32 @@
             block[far] = swap(tokens, far)
         block[2] = swap(tokens, 2)
         block[1] = swap(tokens, 1)
-        block[2], block[1] = lax.optimization_barrier((block[2], block[1]))
+        gate_held, up_held = fetch([gate_weight, up_weight])
+        block[1], block[2], gate_held, up_held = lax.optimization_barrier(
+            (block[1], block[2], gate_held, up_held)
+        )
         block[3] = swap(block[2], 1)
         for far in fars:
             for near in (2, 3, 1):
                 block[far + near] = swap(block[far], near)
-        gate_held, up_held = fetch([gate_weight, up_weight], [block[3]])
         stay = [0, 2] + fars
-        away = [b for b in range(wide) if b not in stay]
-        blocks = [block[b] for b in stay + away]
-        gate_part = project(blocks, gate_held)
-        up_part = project(blocks, up_held)
+        near_blocks = pack([block[b] for b in (0, 2, 1, 3)])
+        order = [0, 2, 1, 3] + [far + near for far in fars for near in (0, 3, 2, 1)]
+        far_blocks = [block[b] for b in order[4:]]
+        gate_part = project([near_blocks] + far_blocks, gate_held)
+        up_part = project([near_blocks] + far_blocks, up_held)
         outs = down(
             gate_part, across_cores(gate_part), up_part, across_cores(up_part),
-            down_weight, rows, len(stay), len(away),
+            down_weight, rows, [F32 if b in stay else BF16 for b in order],
         )
-        part = dict(zip(stay + away, outs))
+        part = dict(zip(order, outs))
         sums = []
         for far in fars:
             quad = [swap(part[far + near], near) for near in (2, 3, 1)]
             sums.append(add(part[far], quad, BF16))
         arrived = [swap(value, far) for value, far in zip(sums, fars)]
-        pair = add(part[2], [swap(part[3], 1)], BF16, after=sums)
+        part[3], sums[0] = lax.optimization_barrier((part[3], sums[0]))
+        pair = add(part[2], [swap(part[3], 1)], BF16)
         total = add(part[0], arrived, F32, 1500000000)
         return add(total, [swap(part[1], 1), swap(pair, 2)], BF16)
 

time: 47.3 us -> 47.4 us (level)
  starting transfers between devices: 21.6 us -> 21 us
  waiting for transfers between devices: 19 us -> 19.6 us
    ppermute x14, waiting for transfers between devices: 17.8 us -> 18.5 us  [swap(): return lax.ppermute(value, 'wide', [(i, i ^ bits) for i in range(wide)])]
    ppermute x14, starting transfers between devices: 21 us -> 20.4 us  [swap(): return lax.ppermute(value, 'wide', [(i, i ^ bits) for i in range(wide)])]
    pallas_call x3 -> x4, Pallas kernels: 2.17 us -> 2.2 us  [call(): pl.pallas_call(kernel, out_shape=out_shape, compiler_params=pltpu.Compile...]
where the time goes in v8:
time: 47.4 us; the launch traced here: 47.2 us
  starting transfers between devices  21 us (44%)
  waiting for transfers between devices  19.6 us (41%)
  Pallas kernels  6.48 us (14%)
    ppermute x14, starting transfers between devices, swap(): return lax.ppermute(value, 'wide', [(i, i ^ bits) for i in range(wide)])  20.4 us
    ppermute x14, waiting for transfers between devices, swap(): return lax.ppermute(value, 'wide', [(i, i ^ bits) for i in range(wide)])  18.5 us
    pallas_call x1, Pallas kernels, fetch(): pl.pallas_call(functools.partial(fetch_kernel, pieces, count), in_specs=[...  3.47 us
    pallas_call x4, Pallas kernels, call(): pl.pallas_call(kernel, out_shape=out_shape, compiler_params=pltpu.Compile...  2.2 us
    ppermute x2, waiting for transfers between devices, across_cores(): lax.ppermute(value, 'narrow', [(i, (i + 1) % narrow) for i in range(narro...  1.16 us
  transfers between devices with their start and end apart: 16, of which 11 were waited for; matrix products, arithmetic and copies ran while one was open for 0% of the time, Pallas kernels for 9%

profile of v8, /device:TPU:0, one launch (start us, length us, event | category | flops | bytes accessed | tf_op | source)
XLA Modules:
  0.0 47.2 jit_solution(582414621618121611)
XLA Ops:
  0.0 0.0 copy-start.1
  0.0 3.0 %collective-permute-start = (bf16[16,4096]{1,0:T(8,128)(2,1)}, bf16[16,4096]{1,0:T(8,128)(2,1)S(1)}, u32[]{:S(2)}, u32[]{:S(2)}) collective-permute-start(bf16[16,4096]{1,0:T(8,128)(2,1)} %refs_0_.3), channel_id=1, source_target_pairs={{0,2},{2,0},{4,6},{6,4},{8,10},{10,8},{12,14},{14,12},{1,3},{3,1},... | collective-permute-start | bytes 393224 | tf_op jit(solution)/shard_map/ppermute | solution.py:129
  3.0 1.6 %collective-permute-start.1 = (bf16[16,4096]{1,0:T(8,128)(2,1)}, bf16[16,4096]{1,0:T(8,128)(2,1)S(1)}, u32[]{:S(2)}, u32[]{:S(2)}) collective-permute-start(bf16[16,4096]{1,0:T(8,128)(2,1)} %refs_0_.3), channel_id=1, source_target_pairs={{0,4},{2,6},{4,0},{6,2},{8,12},{10,14},{12,8},{14,10},{1,5},{3,7},... | collective-permute-start | bytes 393224 | tf_op jit(solution)/shard_map/ppermute | solution.py:129
  4.5 2.6 %collective-permute-start.3 = (bf16[16,4096]{1,0:T(8,128)(2,1)}, bf16[16,4096]{1,0:T(8,128)(2,1)S(1)}, u32[]{:S(2)}, u32[]{:S(2)}) collective-permute-start(bf16[16,4096]{1,0:T(8,128)(2,1)} %refs_0_.3), channel_id=1, source_target_pairs={{0,8},{2,10},{4,12},{6,14},{8,0},{10,2},{12,4},{14,6},{1,9},{3,11}... | collective-permute-start | bytes 393224 | tf_op jit(solution)/shard_map/ppermute | solution.py:129
  7.1 3.5 %fetch.1 = (bf16[4096,512]{1,0:T(8,128)(2,1)S(1)}, bf16[4096,512]{1,0:T(8,128)(2,1)S(1)}) custom-call(bf16[4096,512]{1,0:T(8,128)(2,1)} %refs_0_.2, bf16[4096,512]{1,0:T(8,128)(2,1)} %refs_1_.1), custom_call_target="tpu_custom_call" | custom-call | flops 4000000000 | tf_op jit(solution)/shard_map/fetch/pallas_call | solution.py:41
  10.6 0.0 collective-permute-done.refs_2_
  10.6 0.0 collective-permute-done.1.refs_1_
  10.6 0.6 %collective-permute-start.2 = (bf16[16,4096]{1,0:T(8,128)(2,1)S(1)}, bf16[16,4096]{1,0:T(8,128)(2,1)S(1)}, u32[]{:S(2)}, u32[]{:S(2)}) collective-permute-start(bf16[16,4096]{1,0:T(8,128)(2,1)S(1)} %collective-permute-done.1.refs_1_), channel_id=1, source_target_pairs={{0,2},{2,0},{4,6},{6,4},{8,10},{10,8},{12,14},{14,12},{1,3},{3,1},... | collective-permute-start | bytes 393224 | tf_op jit(solution)/shard_map/ppermute | solution.py:129
  11.2 2.0 %collective-permute-done.3.refs_1_ = bf16[16,4096]{1,0:T(8,128)(2,1)S(1)} collective-permute-done((bf16[16,4096]{1,0:T(8,128)(2,1)}, bf16[16,4096]{1,0:T(8,128)(2,1)S(1)}, u32[]{:S(2)}, u32[]{:S(2)}) %collective-permute-start.3) | collective-permute-done | bytes 131104 | tf_op jit(solution)/shard_map/ppermute | solution.py:129
  13.2 0.3 collective-permute-start.4
  13.5 1.7 %collective-permute-start.5 = (bf16[16,4096]{1,0:T(8,128)(2,1)S(1)}, bf16[16,4096]{1,0:T(8,128)(2,1)S(1)}, u32[]{:S(2)}, u32[]{:S(2)}) collective-permute-start(bf16[16,4096]{1,0:T(8,128)(2,1)S(1)} %collective-permute-done.3.refs_1_), channel_id=1, source_target_pairs={{0,4},{2,6},{4,0},{6,2},{8,12},{10,14},{12,8},{14,10},{1,5},{3,7},... | collective-permute-start | bytes 393224 | tf_op jit(solution)/shard_map/ppermute | solution.py:129
  15.2 1.5 %collective-permute-start.6 = (bf16[16,4096]{1,0:T(8,128)(2,1)S(1)}, bf16[16,4096]{1,0:T(8,128)(2,1)S(1)}, u32[]{:S(2)}, u32[]{:S(2)}) collective-permute-start(bf16[16,4096]{1,0:T(8,128)(2,1)S(1)} %collective-permute-done.3.refs_1_), channel_id=1, source_target_pairs={{0,2},{2,0},{4,6},{6,4},{8,10},{10,8},{12,14},{14,12},{1,3},{3,1},... | collective-permute-start | bytes 393224 | tf_op jit(solution)/shard_map/ppermute | solution.py:129
  16.7 2.5 %collective-permute-done.2.refs_3_ = bf16[16,4096]{1,0:T(8,128)(2,1)S(1)} collective-permute-done((bf16[16,4096]{1,0:T(8,128)(2,1)S(1)}, bf16[16,4096]{1,0:T(8,128)(2,1)S(1)}, u32[]{:S(2)}, u32[]{:S(2)}) %collective-permute-start.2) | collective-permute-done | bytes 131104 | tf_op jit(solution)/shard_map/ppermute | solution.py:129
  19.2 0.0 copy-done.1
  19.2 0.0 copy-start
  19.3 0.0 collective-permute-done.4.refs_2_
  19.3 0.3 collective-permute-done.5.refs_3_
  19.6 1.2 %collective-permute-done.6.refs_4_ = bf16[16,4096]{1,0:T(8,128)(2,1)S(1)} collective-permute-done((bf16[16,4096]{1,0:T(8,128)(2,1)S(1)}, bf16[16,4096]{1,0:T(8,128)(2,1)S(1)}, u32[]{:S(2)}, u32[]{:S(2)}) %collective-permute-start.6) | collective-permute-done | bytes 131104 | tf_op jit(solution)/shard_map/ppermute | solution.py:129
  20.7 0.7 %project.3.up_ref = f32[128,512]{1,0:T(8,128)S(1)} custom-call(bf16[64,4096]{1,0:T(8,128)(2,1)S(1)} %pack.1.refs_0_, bf16[16,4096]{1,0:T(8,128)(2,1)S(1)} %collective-permute-done.3.refs_1_, bf16[16,4096]{1,0:T(8,128)(2,1)S(1)} %collective-permute-done.4.refs_2_, bf16[16,4096]{1,0:T(8,128)(2,1)S(1)} %collective-permute-done.5.refs_3_, ...), custom_call_target="tpu_custom_call" | custom-call | flops 400000000 | tf_op jit(solution)/shard_map/project/pallas_call | solution.py:15
  21.4 0.1 collective-permute-start.8
  21.5 0.7 %project.2.gate_ref = f32[128,512]{1,0:T(8,128)S(1)} custom-call(bf16[64,4096]{1,0:T(8,128)(2,1)S(1)} %pack.1.refs_0_, bf16[16,4096]{1,0:T(8,128)(2,1)S(1)} %collective-permute-done.3.refs_1_, bf16[16,4096]{1,0:T(8,128)(2,1)S(1)} %collective-permute-done.4.refs_2_, bf16[16,4096]{1,0:T(8,128)(2,1)S(1)} %collective-permute-done.5.refs_3_, ...), custom_call_target="tpu_custom_call" | custom-call | flops 400000000 | tf_op jit(solution)/shard_map/project/pallas_call | solution.py:15
  22.2 0.6 %collective-permute-start.7 = (f32[128,512]{1,0:T(8,128)S(1)}, f32[128,512]{1,0:T(8,128)S(1)}, u32[]{:S(2)}, u32[]{:S(2)}) collective-permute-start(f32[128,512]{1,0:T(8,128)S(1)} %project.2.gate_ref), channel_id=1, source_target_pairs={{0,1},{1,0},{2,3},{3,2},{4,5},{5,4},{6,7},{7,6},{8,9},{9,8},{10,11... | collective-permute-start | bytes 786440 | tf_op jit(solution)/shard_map/ppermute | solution.py:132
  22.8 0.2 collective-permute-done.8.up_other_ref
  23.0 0.9 %collective-permute-done.7.gate_other_ref = f32[128,512]{1,0:T(8,128)S(1)} collective-permute-done((f32[128,512]{1,0:T(8,128)S(1)}, f32[128,512]{1,0:T(8,128)S(1)}, u32[]{:S(2)}, u32[]{:S(2)}) %collective-permute-start.7) | collective-permute-done | bytes 262176 | tf_op jit(solution)/shard_map/ppermute | solution.py:132
  24.0 0.0 copy-done
  24.0 0.7 %down.1 = (f32[16,4096]{1,0:T(8,128)S(1)}, f32[16,4096]{1,0:T(8,128)S(1)}, bf16[16,4096]{1,0:T(8,128)(2,1)S(1)}, bf16[16,4096]{1,0:T(8,128)(2,1)S(1)}, f32[16,40...) custom-call(f32[128,512]{1,0:T(8,128)S(1)} %project.2.gate_ref, ...), custom_call_target="tpu_custom_call" | custom-call | flops 536870912 | tf_op jit(solution)/shard_map/down/pallas_call | solution.py:15
  24.7 1.0 %collective-permute-start.10 = (bf16[16,4096]{1,0:T(8,128)(2,1)S(1)}, bf16[16,4096]{1,0:T(8,128)(2,1)S(1)}, u32[]{:S(2)}, u32[]{:S(2)}) collective-permute-start(bf16[16,4096]{1,0:T(8,128)(2,1)S(1)} %get-tuple-element.29), channel_id=1, source_target_pairs={{0,6},{2,4},{4,2},{6,0},{8,14},{10,12},{12,10},{14,8},{1,7},{3,5},... | collective-permute-start | bytes 393224 | tf_op jit(solution)/shard_map/ppermute | solution.py:129
  25.8 1.5 %collective-permute-start.11 = (bf16[16,4096]{1,0:T(8,128)(2,1)S(1)}, bf16[16,4096]{1,0:T(8,128)(2,1)S(1)}, u32[]{:S(2)}, u32[]{:S(2)}) collective-permute-start(bf16[16,4096]{1,0:T(8,128)(2,1)S(1)} %get-tuple-element.30), channel_id=1, source_target_pairs={{0,2},{2,0},{4,6},{6,4},{8,10},{10,8},{12,14},{14,12},{1,3},{3,1},... | collective-permute-start | bytes 393224 | tf_op jit(solution)/shard_map/ppermute | solution.py:129
  27.3 1.0 %collective-permute-start.9 = (bf16[16,4096]{1,0:T(8,128)(2,1)S(1)}, bf16[16,4096]{1,0:T(8,128)(2,1)S(1)}, u32[]{:S(2)}, u32[]{:S(2)}) collective-permute-start(bf16[16,4096]{1,0:T(8,128)(2,1)S(1)} %get-tuple-element.28), channel_id=1, source_target_pairs={{0,4},{2,6},{4,0},{6,2},{8,12},{10,14},{12,8},{14,10},{1,5},{3,7},... | collective-permute-start | bytes 393224 | tf_op jit(solution)/shard_map/ppermute | solution.py:129
  28.3 3.8 %collective-permute-done.10.refs_1_ = bf16[16,4096]{1,0:T(8,128)(2,1)S(1)} collective-permute-done((bf16[16,4096]{1,0:T(8,128)(2,1)S(1)}, bf16[16,4096]{1,0:T(8,128)(2,1)S(1)}, u32[]{:S(2)}, u32[]{:S(2)}) %collective-permute-start.10) | collective-permute-done | bytes 131104 | tf_op jit(solution)/shard_map/ppermute | solution.py:129
  32.0 2.0 %collective-permute-done.11.refs_2_ = bf16[16,4096]{1,0:T(8,128)(2,1)S(1)} collective-permute-done((bf16[16,4096]{1,0:T(8,128)(2,1)S(1)}, bf16[16,4096]{1,0:T(8,128)(2,1)S(1)}, u32[]{:S(2)}, u32[]{:S(2)}) %collective-permute-start.11) | collective-permute-done | bytes 131104 | tf_op jit(solution)/shard_map/ppermute | solution.py:129
  34.0 0.0 collective-permute-done.9.refs_0_
  34.0 0.1 add.4
  34.1 1.4 %collective-permute-start.14 = (bf16[16,4096]{1,0:T(8,128)(2,1)S(1)}, bf16[16,4096]{1,0:T(8,128)(2,1)S(1)}, u32[]{:S(2)}, u32[]{:S(2)}) collective-permute-start(bf16[16,4096]{1,0:T(8,128)(2,1)S(1)} %get-tuple-element.34), channel_id=1, source_target_pairs={{0,2},{2,0},{4,6},{6,4},{8,10},{10,8},{12,14},{14,12},{1,3},{3,1},... | collective-permute-start | bytes 393224 | tf_op jit(solution)/shard_map/ppermute | solution.py:129
  35.5 1.5 %collective-permute-start.12 = (bf16[16,4096]{1,0:T(8,128)(2,1)S(1)}, bf16[16,4096]{1,0:T(8,128)(2,1)S(1)}, u32[]{:S(2)}, u32[]{:S(2)}) collective-permute-start(bf16[16,4096]{1,0:T(8,128)(2,1)S(1)} %add.4), channel_id=1, source_target_pairs={{0,8},{2,10},{4,12},{6,14},{8,0},{10,2},{12,4},{14,6},{1,9},{3,11}... | collective-permute-start | bytes 393224 | tf_op jit(solution)/shard_map/ppermute | solution.py:129
  37.0 1.4 %collective-permute-start.13 = (bf16[16,4096]{1,0:T(8,128)(2,1)S(1)}, bf16[16,4096]{1,0:T(8,128)(2,1)S(1)}, u32[]{:S(2)}, u32[]{:S(2)}) collective-permute-start(bf16[16,4096]{1,0:T(8,128)(2,1)S(1)} %get-tuple-element.31), channel_id=1, source_target_pairs={{0,2},{2,0},{4,6},{6,4},{8,10},{10,8},{12,14},{14,12},{1,3},{3,1},... | collective-permute-start | bytes 393224 | tf_op jit(solution)/shard_map/ppermute | solution.py:129
  38.4 1.4 %collective-permute-done.14.refs_0_ = bf16[16,4096]{1,0:T(8,128)(2,1)S(1)} collective-permute-done((bf16[16,4096]{1,0:T(8,128)(2,1)S(1)}, bf16[16,4096]{1,0:T(8,128)(2,1)S(1)}, u32[]{:S(2)}, u32[]{:S(2)}) %collective-permute-start.14) | collective-permute-done | bytes 131104 | tf_op jit(solution)/shard_map/ppermute | solution.py:129
  39.8 1.3 %collective-permute-start.15 = (bf16[16,4096]{1,0:T(8,128)(2,1)S(1)}, bf16[16,4096]{1,0:T(8,128)(2,1)S(1)}, u32[]{:S(2)}, u32[]{:S(2)}) collective-permute-start(bf16[16,4096]{1,0:T(8,128)(2,1)S(1)} %add.6), channel_id=1, source_target_pairs={{0,4},{2,6},{4,0},{6,2},{8,12},{10,14},{12,8},{14,10},{1,5},{3,7},... | collective-permute-start | bytes 393224 | tf_op jit(solution)/shard_map/ppermute | solution.py:129
  41.1 3.2 %collective-permute-done.12.refs_0_ = bf16[16,4096]{1,0:T(8,128)(2,1)S(1)} collective-permute-done((bf16[16,4096]{1,0:T(8,128)(2,1)S(1)}, bf16[16,4096]{1,0:T(8,128)(2,1)S(1)}, u32[]{:S(2)}, u32[]{:S(2)}) %collective-permute-start.12) | collective-permute-done | bytes 131104 | tf_op jit(solution)/shard_map/ppermute | solution.py:129
  44.3 0.0 collective-permute-done.13.refs_0_
  44.4 2.2 %collective-permute-done.15.refs_1_ = bf16[16,4096]{1,0:T(8,128)(2,1)S(1)} collective-permute-done((bf16[16,4096]{1,0:T(8,128)(2,1)S(1)}, bf16[16,4096]{1,0:T(8,128)(2,1)S(1)}, u32[]{:S(2)}, u32[]{:S(2)}) %collective-permute-start.15) | collective-permute-done | bytes 131104 | tf_op jit(solution)/shard_map/ppermute | solution.py:129
  46.5 0.7 %add.7 = bf16[16,4096]{1,0:T(8,128)(2,1)} custom-call(f32[16,4096]{1,0:T(8,128)S(1)} %add.5.own_ref, bf16[16,4096]{1,0:T(8,128)(2,1)S(1)} %collective-permute-done.13.refs_0_, bf16[16,4096]{1,0:T(8,128)(2,1)S(1)} %collective-permute-done.15.refs_1_), custom_call_target="tpu_custom_call" | custom-call | flops 1000000 | tf_op jit(solution)/shard_map/add/pallas_call | solution.py:114
  (3 shorter events, 0.1 us)
Async XLA Ops:
  0.0 19.2 %copy-start.1 = (bf16[16,4096]{1,0:T(8,128)(2,1)S(1)}, bf16[16,4096]{1,0:T(8,128)(2,1)}, u32[]{:S(2)}) copy-start(bf16[16,4096]{1,0:T(8,128)(2,1)} %refs_0_.3) | copy-start | bytes 393220
  0.0 10.6 %collective-permute-start = (bf16[16,4096]{1,0:T(8,128)(2,1)}, bf16[16,4096]{1,0:T(8,128)(2,1)S(1)}, u32[]{:S(2)}, u32[]{:S(2)}) collective-permute-start(bf16[16,4096]{1,0:T(8,128)(2,1)} %refs_0_.3), channel_id=1, source_target_pairs={{0,2},{2,0},{4,6},{6,4},{8,10},{10,8},{12,14},{14,12},{1,3},{3,1},... | collective-permute-start | bytes 393224 | tf_op jit(solution)/shard_map/ppermute | solution.py:129
  3.0 7.7 %collective-permute-start.1 = (bf16[16,4096]{1,0:T(8,128)(2,1)}, bf16[16,4096]{1,0:T(8,128)(2,1)S(1)}, u32[]{:S(2)}, u32[]{:S(2)}) collective-permute-start(bf16[16,4096]{1,0:T(8,128)(2,1)} %refs_0_.3), channel_id=1, source_target_pairs={{0,4},{2,6},{4,0},{6,2},{8,12},{10,14},{12,8},{14,10},{1,5},{3,7},... | collective-permute-start | bytes 393224 | tf_op jit(solution)/shard_map/ppermute | solution.py:129
  4.5 8.7 %collective-permute-start.3 = (bf16[16,4096]{1,0:T(8,128)(2,1)}, bf16[16,4096]{1,0:T(8,128)(2,1)S(1)}, u32[]{:S(2)}, u32[]{:S(2)}) collective-permute-start(bf16[16,4096]{1,0:T(8,128)(2,1)} %refs_0_.3), channel_id=1, source_target_pairs={{0,8},{2,10},{4,12},{6,14},{8,0},{10,2},{12,4},{14,6},{1,9},{3,11}... | collective-permute-start | bytes 393224 | tf_op jit(solution)/shard_map/ppermute | solution.py:129
  10.6 8.6 %collective-permute-start.2 = (bf16[16,4096]{1,0:T(8,128)(2,1)S(1)}, bf16[16,4096]{1,0:T(8,128)(2,1)S(1)}, u32[]{:S(2)}, u32[]{:S(2)}) collective-permute-start(bf16[16,4096]{1,0:T(8,128)(2,1)S(1)} %collective-permute-done.1.refs_1_), channel_id=1, source_target_pairs={{0,2},{2,0},{4,6},{6,4},{8,10},{10,8},{12,14},{14,12},{1,3},{3,1},... | collective-permute-start | bytes 393224 | tf_op jit(solution)/shard_map/ppermute | solution.py:129
  13.2 6.0 %collective-permute-start.4 = (bf16[16,4096]{1,0:T(8,128)(2,1)S(1)}, bf16[16,4096]{1,0:T(8,128)(2,1)S(1)}, u32[]{:S(2)}, u32[]{:S(2)}) collective-permute-start(bf16[16,4096]{1,0:T(8,128)(2,1)S(1)} %collective-permute-done.3.refs_1_), channel_id=1, source_target_pairs={{0,6},{2,4},{4,2},{6,0},{8,14},{10,12},{12,10},{14,8},{1,7},{3,5},... | collective-permute-start | bytes 393224 | tf_op jit(solution)/shard_map/ppermute | solution.py:129
  13.5 6.1 %collective-permute-start.5 = (bf16[16,4096]{1,0:T(8,128)(2,1)S(1)}, bf16[16,4096]{1,0:T(8,128)(2,1)S(1)}, u32[]{:S(2)}, u32[]{:S(2)}) collective-permute-start(bf16[16,4096]{1,0:T(8,128)(2,1)S(1)} %collective-permute-done.3.refs_1_), channel_id=1, source_target_pairs={{0,4},{2,6},{4,0},{6,2},{8,12},{10,14},{12,8},{14,10},{1,5},{3,7},... | collective-permute-start | bytes 393224 | tf_op jit(solution)/shard_map/ppermute | solution.py:129
  15.2 5.5 %collective-permute-start.6 = (bf16[16,4096]{1,0:T(8,128)(2,1)S(1)}, bf16[16,4096]{1,0:T(8,128)(2,1)S(1)}, u32[]{:S(2)}, u32[]{:S(2)}) collective-permute-start(bf16[16,4096]{1,0:T(8,128)(2,1)S(1)} %collective-permute-done.3.refs_1_), channel_id=1, source_target_pairs={{0,2},{2,0},{4,6},{6,4},{8,10},{10,8},{12,14},{14,12},{1,3},{3,1},... | collective-permute-start | bytes 393224 | tf_op jit(solution)/shard_map/ppermute | solution.py:129
  19.2 4.7 %copy-start = (bf16[512,4096]{1,0:T(8,128)(2,1)S(1)}, bf16[512,4096]{1,0:T(8,128)(2,1)}, u32[]{:S(2)}) copy-start(bf16[512,4096]{1,0:T(8,128)(2,1)} %weight_ref.1) | copy-start | bytes 12582916
  21.4 1.6 %collective-permute-start.8 = (f32[128,512]{1,0:T(8,128)S(1)}, f32[128,512]{1,0:T(8,128)S(1)}, u32[]{:S(2)}, u32[]{:S(2)}) collective-permute-start(f32[128,512]{1,0:T(8,128)S(1)} %project.3.up_ref), channel_id=1, source_target_pairs={{0,1},{1,0},{2,3},{3,2},{4,5},{5,4},{6,7},{7,6},{8,9},{9,8},{10,11... | collective-permute-start | bytes 786440 | tf_op jit(solution)/shard_map/ppermute | solution.py:132
  22.2 1.7 %collective-permute-start.7 = (f32[128,512]{1,0:T(8,128)S(1)}, f32[128,512]{1,0:T(8,128)S(1)}, u32[]{:S(2)}, u32[]{:S(2)}) collective-permute-start(f32[128,512]{1,0:T(8,128)S(1)} %project.2.gate_ref), channel_id=1, source_target_pairs={{0,1},{1,0},{2,3},{3,2},{4,5},{5,4},{6,7},{7,6},{8,9},{9,8},{10,11... | collective-permute-start | bytes 786440 | tf_op jit(solution)/shard_map/ppermute | solution.py:132
  24.7 7.3 %collective-permute-start.10 = (bf16[16,4096]{1,0:T(8,128)(2,1)S(1)}, bf16[16,4096]{1,0:T(8,128)(2,1)S(1)}, u32[]{:S(2)}, u32[]{:S(2)}) collective-permute-start(bf16[16,4096]{1,0:T(8,128)(2,1)S(1)} %get-tuple-element.29), channel_id=1, source_target_pairs={{0,6},{2,4},{4,2},{6,0},{8,14},{10,12},{12,10},{14,8},{1,7},{3,5},... | collective-permute-start | bytes 393224 | tf_op jit(solution)/shard_map/ppermute | solution.py:129
  25.8 8.3 %collective-permute-start.11 = (bf16[16,4096]{1,0:T(8,128)(2,1)S(1)}, bf16[16,4096]{1,0:T(8,128)(2,1)S(1)}, u32[]{:S(2)}, u32[]{:S(2)}) collective-permute-start(bf16[16,4096]{1,0:T(8,128)(2,1)S(1)} %get-tuple-element.30), channel_id=1, source_target_pairs={{0,2},{2,0},{4,6},{6,4},{8,10},{10,8},{12,14},{14,12},{1,3},{3,1},... | collective-permute-start | bytes 393224 | tf_op jit(solution)/shard_map/ppermute | solution.py:129
  27.3 6.8 %collective-permute-start.9 = (bf16[16,4096]{1,0:T(8,128)(2,1)S(1)}, bf16[16,4096]{1,0:T(8,128)(2,1)S(1)}, u32[]{:S(2)}, u32[]{:S(2)}) collective-permute-start(bf16[16,4096]{1,0:T(8,128)(2,1)S(1)} %get-tuple-element.28), channel_id=1, source_target_pairs={{0,4},{2,6},{4,0},{6,2},{8,12},{10,14},{12,8},{14,10},{1,5},{3,7},... | collective-permute-start | bytes 393224 | tf_op jit(solution)/shard_map/ppermute | solution.py:129
  34.1 5.7 %collective-permute-start.14 = (bf16[16,4096]{1,0:T(8,128)(2,1)S(1)}, bf16[16,4096]{1,0:T(8,128)(2,1)S(1)}, u32[]{:S(2)}, u32[]{:S(2)}) collective-permute-start(bf16[16,4096]{1,0:T(8,128)(2,1)S(1)} %get-tuple-element.34), channel_id=1, source_target_pairs={{0,2},{2,0},{4,6},{6,4},{8,10},{10,8},{12,14},{14,12},{1,3},{3,1},... | collective-permute-start | bytes 393224 | tf_op jit(solution)/shard_map/ppermute | solution.py:129
  35.5 8.8 %collective-permute-start.12 = (bf16[16,4096]{1,0:T(8,128)(2,1)S(1)}, bf16[16,4096]{1,0:T(8,128)(2,1)S(1)}, u32[]{:S(2)}, u32[]{:S(2)}) collective-permute-start(bf16[16,4096]{1,0:T(8,128)(2,1)S(1)} %add.4), channel_id=1, source_target_pairs={{0,8},{2,10},{4,12},{6,14},{8,0},{10,2},{12,4},{14,6},{1,9},{3,11}... | collective-permute-start | bytes 393224 | tf_op jit(solution)/shard_map/ppermute | solution.py:129
  37.0 7.4 %collective-permute-start.13 = (bf16[16,4096]{1,0:T(8,128)(2,1)S(1)}, bf16[16,4096]{1,0:T(8,128)(2,1)S(1)}, u32[]{:S(2)}, u32[]{:S(2)}) collective-permute-start(bf16[16,4096]{1,0:T(8,128)(2,1)S(1)} %get-tuple-element.31), channel_id=1, source_target_pairs={{0,2},{2,0},{4,6},{6,4},{8,10},{10,8},{12,14},{14,12},{1,3},{3,1},... | collective-permute-start | bytes 393224 | tf_op jit(solution)/shard_map/ppermute | solution.py:129
  39.8 6.7 %collective-permute-start.15 = (bf16[16,4096]{1,0:T(8,128)(2,1)S(1)}, bf16[16,4096]{1,0:T(8,128)(2,1)S(1)}, u32[]{:S(2)}, u32[]{:S(2)}) collective-permute-start(bf16[16,4096]{1,0:T(8,128)(2,1)S(1)} %add.6), channel_id=1, source_target_pairs={{0,4},{2,6},{4,0},{6,2},{8,12},{10,14},{12,8},{14,10},{1,5},{3,7},... | collective-permute-start | bytes 393224 | tf_op jit(solution)/shard_map/ppermute | solution.py:129

commit v9 on v8

--- a/solution.py
+++ b/solution.py
@@ -162,8 +162,7 @@
             quad = [swap(part[far + near], near) for near in (2, 3, 1)]
             sums.append(add(part[far], quad, BF16))
         arrived = [swap(value, far) for value, far in zip(sums, fars)]
-        part[3], sums[0] = lax.optimization_barrier((part[3], sums[0]))
-        pair = add(part[2], [swap(part[3], 1)], BF16)
+        pair = add(part[2], [swap(part[3], 1)], BF16, after=sums)
         total = add(part[0], arrived, F32, 1500000000)
         return add(total, [swap(part[1], 1), swap(pair, 2)], BF16)
 

time: 47.4 us -> 44.8 us (0.945)
  waiting for transfers between devices: 19.6 us -> 17.3 us
    ppermute x14, waiting for transfers between devices: 18.5 us -> 16.2 us  [swap(): return lax.ppermute(value, 'wide', [(i, i ^ bits) for i in range(wide)])]
  transfers between devices with their start and end apart: 16 -> 16, of which waited for: 11 -> 10; matrix products, arithmetic and copies ran while one was open for 0% -> 0% of each run, Pallas kernels for 9% -> 10%
where the time goes in v9:
time: 44.8 us; the launch traced here: 44.7 us
  starting transfers between devices  20.8 us (46%)
  waiting for transfers between devices  17.3 us (39%)
  Pallas kernels  6.48 us (14%)
    ppermute x14, starting transfers between devices, swap(): return lax.ppermute(value, 'wide', [(i, i ^ bits) for i in range(wide)])  20.1 us
    ppermute x14, waiting for transfers between devices, swap(): return lax.ppermute(value, 'wide', [(i, i ^ bits) for i in range(wide)])  16.2 us
    pallas_call x1, Pallas kernels, fetch(): pl.pallas_call(functools.partial(fetch_kernel, pieces, count), in_specs=[...  3.47 us
    pallas_call x4, Pallas kernels, call(): pl.pallas_call(kernel, out_shape=out_shape, compiler_params=pltpu.Compile...  2.2 us
    ppermute x2, waiting for transfers between devices, across_cores(): lax.ppermute(value, 'narrow', [(i, (i + 1) % narrow) for i in range(narro...  1.16 us
  transfers between devices with their start and end apart: 16, of which 10 were waited for; matrix products, arithmetic and copies ran while one was open for 0% of the time, Pallas kernels for 10%

profile of v9, /device:TPU:0, one launch (start us, length us, event | category | flops | bytes accessed | tf_op | source)
XLA Modules:
  0.0 44.7 jit_solution(7667214595474256618)
XLA Ops:
  0.0 0.0 copy-start.1
  0.0 3.0 %collective-permute-start = (bf16[16,4096]{1,0:T(8,128)(2,1)}, bf16[16,4096]{1,0:T(8,128)(2,1)S(1)}, u32[]{:S(2)}, u32[]{:S(2)}) collective-permute-start(bf16[16,4096]{1,0:T(8,128)(2,1)} %refs_0_.3), channel_id=1, source_target_pairs={{0,2},{2,0},{4,6},{6,4},{8,10},{10,8},{12,14},{14,12},{1,3},{3,1},... | collective-permute-start | bytes 393224 | tf_op jit(solution)/shard_map/ppermute | solution.py:129
  3.0 1.6 %collective-permute-start.1 = (bf16[16,4096]{1,0:T(8,128)(2,1)}, bf16[16,4096]{1,0:T(8,128)(2,1)S(1)}, u32[]{:S(2)}, u32[]{:S(2)}) collective-permute-start(bf16[16,4096]{1,0:T(8,128)(2,1)} %refs_0_.3), channel_id=1, source_target_pairs={{0,4},{2,6},{4,0},{6,2},{8,12},{10,14},{12,8},{14,10},{1,5},{3,7},... | collective-permute-start | bytes 393224 | tf_op jit(solution)/shard_map/ppermute | solution.py:129
  4.5 2.6 %collective-permute-start.3 = (bf16[16,4096]{1,0:T(8,128)(2,1)}, bf16[16,4096]{1,0:T(8,128)(2,1)S(1)}, u32[]{:S(2)}, u32[]{:S(2)}) collective-permute-start(bf16[16,4096]{1,0:T(8,128)(2,1)} %refs_0_.3), channel_id=1, source_target_pairs={{0,8},{2,10},{4,12},{6,14},{8,0},{10,2},{12,4},{14,6},{1,9},{3,11}... | collective-permute-start | bytes 393224 | tf_op jit(solution)/shard_map/ppermute | solution.py:129
  7.1 3.5 %fetch.1 = (bf16[4096,512]{1,0:T(8,128)(2,1)S(1)}, bf16[4096,512]{1,0:T(8,128)(2,1)S(1)}) custom-call(bf16[4096,512]{1,0:T(8,128)(2,1)} %refs_0_.2, bf16[4096,512]{1,0:T(8,128)(2,1)} %refs_1_.1), custom_call_target="tpu_custom_call" | custom-call | flops 4000000000 | tf_op jit(solution)/shard_map/fetch/pallas_call | solution.py:41
  10.6 0.0 collective-permute-done.refs_2_
  10.6 0.0 collective-permute-done.1.refs_1_
  10.6 0.6 %collective-permute-start.2 = (bf16[16,4096]{1,0:T(8,128)(2,1)S(1)}, bf16[16,4096]{1,0:T(8,128)(2,1)S(1)}, u32[]{:S(2)}, u32[]{:S(2)}) collective-permute-start(bf16[16,4096]{1,0:T(8,128)(2,1)S(1)} %collective-permute-done.1.refs_1_), channel_id=1, source_target_pairs={{0,2},{2,0},{4,6},{6,4},{8,10},{10,8},{12,14},{14,12},{1,3},{3,1},... | collective-permute-start | bytes 393224 | tf_op jit(solution)/shard_map/ppermute | solution.py:129
  11.2 2.0 %collective-permute-done.3.refs_1_ = bf16[16,4096]{1,0:T(8,128)(2,1)S(1)} collective-permute-done((bf16[16,4096]{1,0:T(8,128)(2,1)}, bf16[16,4096]{1,0:T(8,128)(2,1)S(1)}, u32[]{:S(2)}, u32[]{:S(2)}) %collective-permute-start.3) | collective-permute-done | bytes 131104 | tf_op jit(solution)/shard_map/ppermute | solution.py:129
  13.2 0.3 collective-permute-start.4
  13.5 1.7 %collective-permute-start.5 = (bf16[16,4096]{1,0:T(8,128)(2,1)S(1)}, bf16[16,4096]{1,0:T(8,128)(2,1)S(1)}, u32[]{:S(2)}, u32[]{:S(2)}) collective-permute-start(bf16[16,4096]{1,0:T(8,128)(2,1)S(1)} %collective-permute-done.3.refs_1_), channel_id=1, source_target_pairs={{0,4},{2,6},{4,0},{6,2},{8,12},{10,14},{12,8},{14,10},{1,5},{3,7},... | collective-permute-start | bytes 393224 | tf_op jit(solution)/shard_map/ppermute | solution.py:129
  15.2 1.5 %collective-permute-start.6 = (bf16[16,4096]{1,0:T(8,128)(2,1)S(1)}, bf16[16,4096]{1,0:T(8,128)(2,1)S(1)}, u32[]{:S(2)}, u32[]{:S(2)}) collective-permute-start(bf16[16,4096]{1,0:T(8,128)(2,1)S(1)} %collective-permute-done.3.refs_1_), channel_id=1, source_target_pairs={{0,2},{2,0},{4,6},{6,4},{8,10},{10,8},{12,14},{14,12},{1,3},{3,1},... | collective-permute-start | bytes 393224 | tf_op jit(solution)/shard_map/ppermute | solution.py:129
  16.7 2.5 %collective-permute-done.2.refs_3_ = bf16[16,4096]{1,0:T(8,128)(2,1)S(1)} collective-permute-done((bf16[16,4096]{1,0:T(8,128)(2,1)S(1)}, bf16[16,4096]{1,0:T(8,128)(2,1)S(1)}, u32[]{:S(2)}, u32[]{:S(2)}) %collective-permute-start.2) | collective-permute-done | bytes 131104 | tf_op jit(solution)/shard_map/ppermute | solution.py:129
  19.2 0.0 copy-done.1
  19.2 0.0 copy-start
  19.3 0.0 collective-permute-done.4.refs_2_
  19.3 0.3 collective-permute-done.5.refs_3_
  19.6 1.2 %collective-permute-done.6.refs_4_ = bf16[16,4096]{1,0:T(8,128)(2,1)S(1)} collective-permute-done((bf16[16,4096]{1,0:T(8,128)(2,1)S(1)}, bf16[16,4096]{1,0:T(8,128)(2,1)S(1)}, u32[]{:S(2)}, u32[]{:S(2)}) %collective-permute-start.6) | collective-permute-done | bytes 131104 | tf_op jit(solution)/shard_map/ppermute | solution.py:129
  20.7 0.7 %project.3.up_ref = f32[128,512]{1,0:T(8,128)S(1)} custom-call(bf16[64,4096]{1,0:T(8,128)(2,1)S(1)} %pack.1.refs_0_, bf16[16,4096]{1,0:T(8,128)(2,1)S(1)} %collective-permute-done.3.refs_1_, bf16[16,4096]{1,0:T(8,128)(2,1)S(1)} %collective-permute-done.4.refs_2_, bf16[16,4096]{1,0:T(8,128)(2,1)S(1)} %collective-permute-done.5.refs_3_, ...), custom_call_target="tpu_custom_call" | custom-call | flops 400000000 | tf_op jit(solution)/shard_map/project/pallas_call | solution.py:15
  21.4 0.1 collective-permute-start.8
  21.5 0.7 %project.2.gate_ref = f32[128,512]{1,0:T(8,128)S(1)} custom-call(bf16[64,4096]{1,0:T(8,128)(2,1)S(1)} %pack.1.refs_0_, bf16[16,4096]{1,0:T(8,128)(2,1)S(1)} %collective-permute-done.3.refs_1_, bf16[16,4096]{1,0:T(8,128)(2,1)S(1)} %collective-permute-done.4.refs_2_, bf16[16,4096]{1,0:T(8,128)(2,1)S(1)} %collective-permute-done.5.refs_3_, ...), custom_call_target="tpu_custom_call" | custom-call | flops 400000000 | tf_op jit(solution)/shard_map/project/pallas_call | solution.py:15
  22.2 0.6 %collective-permute-start.7 = (f32[128,512]{1,0:T(8,128)S(1)}, f32[128,512]{1,0:T(8,128)S(1)}, u32[]{:S(2)}, u32[]{:S(2)}) collective-permute-start(f32[128,512]{1,0:T(8,128)S(1)} %project.2.gate_ref), channel_id=1, source_target_pairs={{0,1},{1,0},{2,3},{3,2},{4,5},{5,4},{6,7},{7,6},{8,9},{9,8},{10,11... | collective-permute-start | bytes 786440 | tf_op jit(solution)/shard_map/ppermute | solution.py:132
  22.8 0.2 collective-permute-done.8.up_other_ref
  23.0 0.9 %collective-permute-done.7.gate_other_ref = f32[128,512]{1,0:T(8,128)S(1)} collective-permute-done((f32[128,512]{1,0:T(8,128)S(1)}, f32[128,512]{1,0:T(8,128)S(1)}, u32[]{:S(2)}, u32[]{:S(2)}) %collective-permute-start.7) | collective-permute-done | bytes 262176 | tf_op jit(solution)/shard_map/ppermute | solution.py:132
  24.0 0.0 copy-done
  24.0 0.7 %down.1 = (f32[16,4096]{1,0:T(8,128)S(1)}, f32[16,4096]{1,0:T(8,128)S(1)}, bf16[16,4096]{1,0:T(8,128)(2,1)S(1)}, bf16[16,4096]{1,0:T(8,128)(2,1)S(1)}, f32[16,40...) custom-call(f32[128,512]{1,0:T(8,128)S(1)} %project.2.gate_ref, ...), custom_call_target="tpu_custom_call" | custom-call | flops 536870912 | tf_op jit(solution)/shard_map/down/pallas_call | solution.py:15
  24.7 1.0 %collective-permute-start.10 = (bf16[16,4096]{1,0:T(8,128)(2,1)S(1)}, bf16[16,4096]{1,0:T(8,128)(2,1)S(1)}, u32[]{:S(2)}, u32[]{:S(2)}) collective-permute-start(bf16[16,4096]{1,0:T(8,128)(2,1)S(1)} %get-tuple-element.28), channel_id=1, source_target_pairs={{0,6},{2,4},{4,2},{6,0},{8,14},{10,12},{12,10},{14,8},{1,7},{3,5},... | collective-permute-start | bytes 393224 | tf_op jit(solution)/shard_map/ppermute | solution.py:129
  25.8 1.5 %collective-permute-start.11 = (bf16[16,4096]{1,0:T(8,128)(2,1)S(1)}, bf16[16,4096]{1,0:T(8,128)(2,1)S(1)}, u32[]{:S(2)}, u32[]{:S(2)}) collective-permute-start(bf16[16,4096]{1,0:T(8,128)(2,1)S(1)} %get-tuple-element.29), channel_id=1, source_target_pairs={{0,2},{2,0},{4,6},{6,4},{8,10},{10,8},{12,14},{14,12},{1,3},{3,1},... | collective-permute-start | bytes 393224 | tf_op jit(solution)/shard_map/ppermute | solution.py:129
  27.3 1.0 %collective-permute-start.9 = (bf16[16,4096]{1,0:T(8,128)(2,1)S(1)}, bf16[16,4096]{1,0:T(8,128)(2,1)S(1)}, u32[]{:S(2)}, u32[]{:S(2)}) collective-permute-start(bf16[16,4096]{1,0:T(8,128)(2,1)S(1)} %get-tuple-element.27), channel_id=1, source_target_pairs={{0,4},{2,6},{4,0},{6,2},{8,12},{10,14},{12,8},{14,10},{1,5},{3,7},... | collective-permute-start | bytes 393224 | tf_op jit(solution)/shard_map/ppermute | solution.py:129
  28.3 1.1 %collective-permute-start.14 = (bf16[16,4096]{1,0:T(8,128)(2,1)S(1)}, bf16[16,4096]{1,0:T(8,128)(2,1)S(1)}, u32[]{:S(2)}, u32[]{:S(2)}) collective-permute-start(bf16[16,4096]{1,0:T(8,128)(2,1)S(1)} %get-tuple-element.32), channel_id=1, source_target_pairs={{0,2},{2,0},{4,6},{6,4},{8,10},{10,8},{12,14},{14,12},{1,3},{3,1},... | collective-permute-start | bytes 393224 | tf_op jit(solution)/shard_map/ppermute | solution.py:129
  29.4 2.7 %collective-permute-done.10.refs_1_ = bf16[16,4096]{1,0:T(8,128)(2,1)S(1)} collective-permute-done((bf16[16,4096]{1,0:T(8,128)(2,1)S(1)}, bf16[16,4096]{1,0:T(8,128)(2,1)S(1)}, u32[]{:S(2)}, u32[]{:S(2)}) %collective-permute-start.10) | collective-permute-done | bytes 131104 | tf_op jit(solution)/shard_map/ppermute | solution.py:129
  32.0 2.3 %collective-permute-done.11.refs_2_ = bf16[16,4096]{1,0:T(8,128)(2,1)S(1)} collective-permute-done((bf16[16,4096]{1,0:T(8,128)(2,1)S(1)}, bf16[16,4096]{1,0:T(8,128)(2,1)S(1)}, u32[]{:S(2)}, u32[]{:S(2)}) %collective-permute-start.11) | collective-permute-done | bytes 131104 | tf_op jit(solution)/shard_map/ppermute | solution.py:129
  34.4 0.0 collective-permute-done.9.refs_0_
  34.4 0.1 add.4.refs_1_
  34.4 2.1 %collective-permute-start.12 = (bf16[16,4096]{1,0:T(8,128)(2,1)S(1)}, bf16[16,4096]{1,0:T(8,128)(2,1)S(1)}, u32[]{:S(2)}, u32[]{:S(2)}) collective-permute-start(bf16[16,4096]{1,0:T(8,128)(2,1)S(1)} %add.4.refs_1_), channel_id=1, source_target_pairs={{0,8},{2,10},{4,12},{6,14},{8,0},{10,2},{12,4},{14,6},{1,9},{3,11}... | collective-permute-start | bytes 393224 | tf_op jit(solution)/shard_map/ppermute | solution.py:129
  36.5 0.5 %collective-permute-start.13 = (bf16[16,4096]{1,0:T(8,128)(2,1)S(1)}, bf16[16,4096]{1,0:T(8,128)(2,1)S(1)}, u32[]{:S(2)}, u32[]{:S(2)}) collective-permute-start(bf16[16,4096]{1,0:T(8,128)(2,1)S(1)} %get-tuple-element.30), channel_id=1, source_target_pairs={{0,2},{2,0},{4,6},{6,4},{8,10},{10,8},{12,14},{14,12},{1,3},{3,1},... | collective-permute-start | bytes 393224 | tf_op jit(solution)/shard_map/ppermute | solution.py:129
  37.0 0.0 collective-permute-done.14.refs_0_
  37.0 1.7 %collective-permute-start.15 = (bf16[16,4096]{1,0:T(8,128)(2,1)S(1)}, bf16[16,4096]{1,0:T(8,128)(2,1)S(1)}, u32[]{:S(2)}, u32[]{:S(2)}) collective-permute-start(bf16[16,4096]{1,0:T(8,128)(2,1)S(1)} %add.6), channel_id=1, source_target_pairs={{0,4},{2,6},{4,0},{6,2},{8,12},{10,14},{12,8},{14,10},{1,5},{3,7},... | collective-permute-start | bytes 393224 | tf_op jit(solution)/shard_map/ppermute | solution.py:129
  38.7 4.5 %collective-permute-done.12.refs_0_ = bf16[16,4096]{1,0:T(8,128)(2,1)S(1)} collective-permute-done((bf16[16,4096]{1,0:T(8,128)(2,1)S(1)}, bf16[16,4096]{1,0:T(8,128)(2,1)S(1)}, u32[]{:S(2)}, u32[]{:S(2)}) %collective-permute-start.12) | collective-permute-done | bytes 131104 | tf_op jit(solution)/shard_map/ppermute | solution.py:129
  43.2 0.0 collective-permute-done.13.refs_0_
  43.2 0.7 %collective-permute-done.15.refs_1_ = bf16[16,4096]{1,0:T(8,128)(2,1)S(1)} collective-permute-done((bf16[16,4096]{1,0:T(8,128)(2,1)S(1)}, bf16[16,4096]{1,0:T(8,128)(2,1)S(1)}, u32[]{:S(2)}, u32[]{:S(2)}) %collective-permute-start.15) | collective-permute-done | bytes 131104 | tf_op jit(solution)/shard_map/ppermute | solution.py:129
  44.0 0.7 %add.7 = bf16[16,4096]{1,0:T(8,128)(2,1)} custom-call(f32[16,4096]{1,0:T(8,128)S(1)} %add.5.own_ref, bf16[16,4096]{1,0:T(8,128)(2,1)S(1)} %collective-permute-done.13.refs_0_, bf16[16,4096]{1,0:T(8,128)(2,1)S(1)} %collective-permute-done.15.refs_1_), custom_call_target="tpu_custom_call" | custom-call | flops 1000000 | tf_op jit(solution)/shard_map/add/pallas_call | solution.py:114
  (3 shorter events, 0.1 us)
Async XLA Ops:
  0.0 19.2 %copy-start.1 = (bf16[16,4096]{1,0:T(8,128)(2,1)S(1)}, bf16[16,4096]{1,0:T(8,128)(2,1)}, u32[]{:S(2)}) copy-start(bf16[16,4096]{1,0:T(8,128)(2,1)} %refs_0_.3) | copy-start | bytes 393220
  0.0 10.6 %collective-permute-start = (bf16[16,4096]{1,0:T(8,128)(2,1)}, bf16[16,4096]{1,0:T(8,128)(2,1)S(1)}, u32[]{:S(2)}, u32[]{:S(2)}) collective-permute-start(bf16[16,4096]{1,0:T(8,128)(2,1)} %refs_0_.3), channel_id=1, source_target_pairs={{0,2},{2,0},{4,6},{6,4},{8,10},{10,8},{12,14},{14,12},{1,3},{3,1},... | collective-permute-start | bytes 393224 | tf_op jit(solution)/shard_map/ppermute | solution.py:129
  3.0 7.7 %collective-permute-start.1 = (bf16[16,4096]{1,0:T(8,128)(2,1)}, bf16[16,4096]{1,0:T(8,128)(2,1)S(1)}, u32[]{:S(2)}, u32[]{:S(2)}) collective-permute-start(bf16[16,4096]{1,0:T(8,128)(2,1)} %refs_0_.3), channel_id=1, source_target_pairs={{0,4},{2,6},{4,0},{6,2},{8,12},{10,14},{12,8},{14,10},{1,5},{3,7},... | collective-permute-start | bytes 393224 | tf_op jit(solution)/shard_map/ppermute | solution.py:129
  4.5 8.7 %collective-permute-start.3 = (bf16[16,4096]{1,0:T(8,128)(2,1)}, bf16[16,4096]{1,0:T(8,128)(2,1)S(1)}, u32[]{:S(2)}, u32[]{:S(2)}) collective-permute-start(bf16[16,4096]{1,0:T(8,128)(2,1)} %refs_0_.3), channel_id=1, source_target_pairs={{0,8},{2,10},{4,12},{6,14},{8,0},{10,2},{12,4},{14,6},{1,9},{3,11}... | collective-permute-start | bytes 393224 | tf_op jit(solution)/shard_map/ppermute | solution.py:129
  10.6 8.6 %collective-permute-start.2 = (bf16[16,4096]{1,0:T(8,128)(2,1)S(1)}, bf16[16,4096]{1,0:T(8,128)(2,1)S(1)}, u32[]{:S(2)}, u32[]{:S(2)}) collective-permute-start(bf16[16,4096]{1,0:T(8,128)(2,1)S(1)} %collective-permute-done.1.refs_1_), channel_id=1, source_target_pairs={{0,2},{2,0},{4,6},{6,4},{8,10},{10,8},{12,14},{14,12},{1,3},{3,1},... | collective-permute-start | bytes 393224 | tf_op jit(solution)/shard_map/ppermute | solution.py:129
  13.2 6.0 %collective-permute-start.4 = (bf16[16,4096]{1,0:T(8,128)(2,1)S(1)}, bf16[16,4096]{1,0:T(8,128)(2,1)S(1)}, u32[]{:S(2)}, u32[]{:S(2)}) collective-permute-start(bf16[16,4096]{1,0:T(8,128)(2,1)S(1)} %collective-permute-done.3.refs_1_), channel_id=1, source_target_pairs={{0,6},{2,4},{4,2},{6,0},{8,14},{10,12},{12,10},{14,8},{1,7},{3,5},... | collective-permute-start | bytes 393224 | tf_op jit(solution)/shard_map/ppermute | solution.py:129
  13.5 6.1 %collective-permute-start.5 = (bf16[16,4096]{1,0:T(8,128)(2,1)S(1)}, bf16[16,4096]{1,0:T(8,128)(2,1)S(1)}, u32[]{:S(2)}, u32[]{:S(2)}) collective-permute-start(bf16[16,4096]{1,0:T(8,128)(2,1)S(1)} %collective-permute-done.3.refs_1_), channel_id=1, source_target_pairs={{0,4},{2,6},{4,0},{6,2},{8,12},{10,14},{12,8},{14,10},{1,5},{3,7},... | collective-permute-start | bytes 393224 | tf_op jit(solution)/shard_map/ppermute | solution.py:129
  15.2 5.5 %collective-permute-start.6 = (bf16[16,4096]{1,0:T(8,128)(2,1)S(1)}, bf16[16,4096]{1,0:T(8,128)(2,1)S(1)}, u32[]{:S(2)}, u32[]{:S(2)}) collective-permute-start(bf16[16,4096]{1,0:T(8,128)(2,1)S(1)} %collective-permute-done.3.refs_1_), channel_id=1, source_target_pairs={{0,2},{2,0},{4,6},{6,4},{8,10},{10,8},{12,14},{14,12},{1,3},{3,1},... | collective-permute-start | bytes 393224 | tf_op jit(solution)/shard_map/ppermute | solution.py:129
  19.2 4.7 %copy-start = (bf16[512,4096]{1,0:T(8,128)(2,1)S(1)}, bf16[512,4096]{1,0:T(8,128)(2,1)}, u32[]{:S(2)}) copy-start(bf16[512,4096]{1,0:T(8,128)(2,1)} %weight_ref.1) | copy-start | bytes 12582916
  21.4 1.6 %collective-permute-start.8 = (f32[128,512]{1,0:T(8,128)S(1)}, f32[128,512]{1,0:T(8,128)S(1)}, u32[]{:S(2)}, u32[]{:S(2)}) collective-permute-start(f32[128,512]{1,0:T(8,128)S(1)} %project.3.up_ref), channel_id=1, source_target_pairs={{0,1},{1,0},{2,3},{3,2},{4,5},{5,4},{6,7},{7,6},{8,9},{9,8},{10,11... | collective-permute-start | bytes 786440 | tf_op jit(solution)/shard_map/ppermute | solution.py:132
  22.2 1.7 %collective-permute-start.7 = (f32[128,512]{1,0:T(8,128)S(1)}, f32[128,512]{1,0:T(8,128)S(1)}, u32[]{:S(2)}, u32[]{:S(2)}) collective-permute-start(f32[128,512]{1,0:T(8,128)S(1)} %project.2.gate_ref), channel_id=1, source_target_pairs={{0,1},{1,0},{2,3},{3,2},{4,5},{5,4},{6,7},{7,6},{8,9},{9,8},{10,11... | collective-permute-start | bytes 786440 | tf_op jit(solution)/shard_map/ppermute | solution.py:132
  24.7 7.3 %collective-permute-start.10 = (bf16[16,4096]{1,0:T(8,128)(2,1)S(1)}, bf16[16,4096]{1,0:T(8,128)(2,1)S(1)}, u32[]{:S(2)}, u32[]{:S(2)}) collective-permute-start(bf16[16,4096]{1,0:T(8,128)(2,1)S(1)} %get-tuple-element.28), channel_id=1, source_target_pairs={{0,6},{2,4},{4,2},{6,0},{8,14},{10,12},{12,10},{14,8},{1,7},{3,5},... | collective-permute-start | bytes 393224 | tf_op jit(solution)/shard_map/ppermute | solution.py:129
  25.8 8.6 %collective-permute-start.11 = (bf16[16,4096]{1,0:T(8,128)(2,1)S(1)}, bf16[16,4096]{1,0:T(8,128)(2,1)S(1)}, u32[]{:S(2)}, u32[]{:S(2)}) collective-permute-start(bf16[16,4096]{1,0:T(8,128)(2,1)S(1)} %get-tuple-element.29), channel_id=1, source_target_pairs={{0,2},{2,0},{4,6},{6,4},{8,10},{10,8},{12,14},{14,12},{1,3},{3,1},... | collective-permute-start | bytes 393224 | tf_op jit(solution)/shard_map/ppermute | solution.py:129
  27.3 7.1 %collective-permute-start.9 = (bf16[16,4096]{1,0:T(8,128)(2,1)S(1)}, bf16[16,4096]{1,0:T(8,128)(2,1)S(1)}, u32[]{:S(2)}, u32[]{:S(2)}) collective-permute-start(bf16[16,4096]{1,0:T(8,128)(2,1)S(1)} %get-tuple-element.27), channel_id=1, source_target_pairs={{0,4},{2,6},{4,0},{6,2},{8,12},{10,14},{12,8},{14,10},{1,5},{3,7},... | collective-permute-start | bytes 393224 | tf_op jit(solution)/shard_map/ppermute | solution.py:129
  28.3 8.7 %collective-permute-start.14 = (bf16[16,4096]{1,0:T(8,128)(2,1)S(1)}, bf16[16,4096]{1,0:T(8,128)(2,1)S(1)}, u32[]{:S(2)}, u32[]{:S(2)}) collective-permute-start(bf16[16,4096]{1,0:T(8,128)(2,1)S(1)} %get-tuple-element.32), channel_id=1, source_target_pairs={{0,2},{2,0},{4,6},{6,4},{8,10},{10,8},{12,14},{14,12},{1,3},{3,1},... | collective-permute-start | bytes 393224 | tf_op jit(solution)/shard_map/ppermute | solution.py:129
  34.4 8.8 %collective-permute-start.12 = (bf16[16,4096]{1,0:T(8,128)(2,1)S(1)}, bf16[16,4096]{1,0:T(8,128)(2,1)S(1)}, u32[]{:S(2)}, u32[]{:S(2)}) collective-permute-start(bf16[16,4096]{1,0:T(8,128)(2,1)S(1)} %add.4.refs_1_), channel_id=1, source_target_pairs={{0,8},{2,10},{4,12},{6,14},{8,0},{10,2},{12,4},{14,6},{1,9},{3,11}... | collective-permute-start | bytes 393224 | tf_op jit(solution)/shard_map/ppermute | solution.py:129
  36.5 6.8 %collective-permute-start.13 = (bf16[16,4096]{1,0:T(8,128)(2,1)S(1)}, bf16[16,4096]{1,0:T(8,128)(2,1)S(1)}, u32[]{:S(2)}, u32[]{:S(2)}) collective-permute-start(bf16[16,4096]{1,0:T(8,128)(2,1)S(1)} %get-tuple-element.30), channel_id=1, source_target_pairs={{0,2},{2,0},{4,6},{6,4},{8,10},{10,8},{12,14},{14,12},{1,3},{3,1},... | collective-permute-start | bytes 393224 | tf_op jit(solution)/shard_map/ppermute | solution.py:129
  37.0 6.9 %collective-permute-start.15 = (bf16[16,4096]{1,0:T(8,128)(2,1)S(1)}, bf16[16,4096]{1,0:T(8,128)(2,1)S(1)}, u32[]{:S(2)}, u32[]{:S(2)}) collective-permute-start(bf16[16,4096]{1,0:T(8,128)(2,1)S(1)} %add.6), channel_id=1, source_target_pairs={{0,4},{2,6},{4,0},{6,2},{8,12},{10,14},{12,8},{14,10},{1,5},{3,7},... | collective-permute-start | bytes 393224 | tf_op jit(solution)/shard_map/ppermute | solution.py:129

commit v10 on v9

--- a/solution.py
+++ b/solution.py
@@ -50,17 +50,16 @@
     )(*weights)
 
 
-def pack_kernel(*refs):
-    *block_refs, out_ref = refs
-    rows = block_refs[0].shape[0]
-    for k, ref in enumerate(block_refs):
-        out_ref[k * rows:(k + 1) * rows, :] = ref[...]
+def spread_kernel(count, block_ref, out_ref):
+    rows = block_ref.shape[0]
+    for k in range(count):
+        out_ref[k * rows:(k + 1) * rows, :] = block_ref[...]
 
 
-def pack(blocks):
-    rows, width = blocks[0].shape
-    out = jax.ShapeDtypeStruct((len(blocks) * rows, width), BF16)
-    return call(pack_kernel, "pack", out, 4000000000, 2 << 20, *blocks)
+def spread(block, count):
+    rows, width = block.shape
+    out = jax.ShapeDtypeStruct((count * rows, width), BF16)
+    return call(functools.partial(spread_kernel, count), "spread", out, 1000000, 2 << 20, block)
 
 
 def project_kernel(*refs):
@@ -102,28 +101,35 @@
     )
 
 
-def add_kernel(count, own_ref, *refs):
-    total = own_ref[...]
-    for ref in refs[:count]:
+def add_kernel(own_ref, *refs):
+    total = own_ref[...].astype(F32)
+    for ref in refs[:-1]:
         total = total + ref[...].astype(F32)
     refs[-1][...] = total.astype(refs[-1].dtype)
 
 
-def add(own, arrived, dtype, hint=1000000, after=()):
-    count = len(arrived)
-    return pl.pallas_call(
-        functools.partial(add_kernel, count),
-        in_specs=[pl.BlockSpec(memory_space=pltpu.VMEM)] * (1 + count)
-        + [pl.BlockSpec(memory_space=pl.ANY)] * len(after),
-        out_shape=jax.ShapeDtypeStruct(own.shape, dtype),
-        compiler_params=pltpu.CompilerParams(vmem_limit_bytes=2 << 20),
-        cost_estimate=pl.CostEstimate(flops=hint, bytes_accessed=0, transcendentals=0),
-        name="add",
-    )(own, *arrived, *after)
+def add(own, arrived, dtype, hint=1000000):
+    out = jax.ShapeDtypeStruct(own.shape, dtype)
+    return call(add_kernel, "add", out, hint, 2 << 20, own, *arrived)
+
+
+def fold_kernel(count, chunks_ref, out_ref):
+    rows = out_ref.shape[0]
+    total = chunks_ref[:rows, :].astype(F32)
+    for k in range(1, count):
+        total = total + chunks_ref[k * rows:(k + 1) * rows, :].astype(F32)
+    out_ref[...] = total.astype(out_ref.dtype)
+
+
+def fold(chunks, count, dtype, hint=1000000):
+    rows, width = chunks.shape
+    out = jax.ShapeDtypeStruct((rows // count, width), dtype)
+    return call(functools.partial(fold_kernel, count), "fold", out, hint, 2 << 20, chunks)
 
 
 def make_local(wide, narrow):
     fars = list(range(4, wide, 4))
+    quads = [list(range(first, first + 4)) for first in range(0, wide, 4)]
 
     def swap(value, bits):
         return lax.ppermute(value, "wide", [(i, i ^ bits) for i in range(wide)])
@@ -131,40 +137,25 @@
     def across_cores(value):
         return lax.ppermute(value, "narrow", [(i, (i + 1) % narrow) for i in range(narrow)])
 
+    def in_quad(value):
+        return lax.all_to_all(value, "wide", 0, 0, axis_index_groups=quads, tiled=True)
+
     def local(tokens, gate_weight, up_weight, down_weight):
         rows = tokens.shape[0]
-        block = {0: tokens}
-        for far in fars:
-            block[far] = swap(tokens, far)
-        block[2] = swap(tokens, 2)
-        block[1] = swap(tokens, 1)
+        away = [swap(tokens, far) for far in fars]
+        near = in_quad(spread(tokens, 4))
         gate_held, up_held = fetch([gate_weight, up_weight])
-        block[1], block[2], gate_held, up_held = lax.optimization_barrier(
-            (block[1], block[2], gate_held, up_held)
+        groups = [near] + [in_quad(spread(value, 4)) for value in away]
+        gate_part = project(groups, gate_held)
+        up_part = project(groups, up_held)
+        parts = down(
+            gate_part, across_cores(gate_part), up_part, across_cores(up_part),
+            down_weight, 4 * rows, [BF16] * len(groups),
         )
-        block[3] = swap(block[2], 1)
-        for far in fars:
-            for near in (2, 3, 1):
-                block[far + near] = swap(block[far], near)
-        stay = [0, 2] + fars
-        near_blocks = pack([block[b] for b in (0, 2, 1, 3)])
-        order = [0, 2, 1, 3] + [far + near for far in fars for near in (0, 3, 2, 1)]
-        far_blocks = [block[b] for b in order[4:]]
-        gate_part = project([near_blocks] + far_blocks, gate_held)
-        up_part = project([near_blocks] + far_blocks, up_held)
-        outs = down(
-            gate_part, across_cores(gate_part), up_part, across_cores(up_part),
-            down_weight, rows, [F32 if b in stay else BF16 for b in order],
-        )
-        part = dict(zip(order, outs))
-        sums = []
-        for far in fars:
-            quad = [swap(part[far + near], near) for near in (2, 3, 1)]
-            sums.append(add(part[far], quad, BF16))
+        sums = [fold(in_quad(part), 4, BF16) for part in parts[1:]]
         arrived = [swap(value, far) for value, far in zip(sums, fars)]
-        pair = add(part[2], [swap(part[3], 1)], BF16, after=sums)
-        total = add(part[0], arrived, F32, 1500000000)
-        return add(total, [swap(part[1], 1), swap(pair, 2)], BF16)
+        total = fold(in_quad(parts[0]), 4, F32)
+        return add(total, arrived, BF16)
 
     return local
 

time: 44.8 us -> 65.6 us (1.46)
  blocking collectives: 0 us -> 12.8 us
  local copies, waits for them, and re-layouts: 0.01 us -> 7.57 us
  starting transfers between devices: 20.8 us -> 17.6 us
  Pallas kernels: 6.48 us -> 8.92 us
  waiting for transfers between devices: 17.3 us -> 18.3 us
    ppermute x14 -> x2, starting transfers between devices: 20.1 us -> 2.66 us  [swap(): return lax.ppermute(value, 'wide', [(i, i ^ bits) for i in range(wide)])]
    all_to_all x0 -> x3, starting transfers between devices: none -> 14.4 us  [in_quad(): lax.all_to_all(value, 'wide', 0, 0, axis_index_groups=quads, tiled=True)]
    all_to_all x0 -> x1, blocking collectives: none -> 12.8 us  [in_quad(): lax.all_to_all(value, 'wide', 0, 0, axis_index_groups=quads, tiled=True)]
    all_to_all x0 -> x3, waiting for transfers between devices: none -> 10.8 us  [in_quad(): lax.all_to_all(value, 'wide', 0, 0, axis_index_groups=quads, tiled=True)]
    ppermute x14 -> x2, waiting for transfers between devices: 16.2 us -> 6.12 us  [swap(): return lax.ppermute(value, 'wide', [(i, i ^ bits) for i in range(wide)])]
    unnamed x4 -> x12, local copies, waits for them, and re-layouts: 0.01 us -> 7.57 us
    pallas_call x4 -> x8, Pallas kernels: 2.2 us -> 5.45 us  [call(): pl.pallas_call(kernel, out_shape=out_shape, compiler_params=pltpu.Compile...]
    pallas_call x4 -> x0, Pallas kernels: 0.81 us -> none  [add(): pl.pallas_call(functools.partial(add_kernel, count), in_specs=[pl.BlockSp...]
  transfers between devices with their start and end apart: 16 -> 7, of which waited for: 10 -> 5; matrix products, arithmetic and copies ran while one was open for 0% -> 0% of each run, Pallas kernels for 10% -> 7%
where the time goes in v10:
time: 65.6 us; the launch traced here: 65.3 us
  waiting for transfers between devices  18.3 us (28%)
  starting transfers between devices  17.6 us (27%)
  blocking collectives  12.8 us (20%)
  Pallas kernels  8.92 us (14%)
  local copies, waits for them, and re-layouts  7.57 us (12%)
    all_to_all x3, starting transfers between devices, in_quad(): lax.all_to_all(value, 'wide', 0, 0, axis_index_groups=quads, tiled=True)  14.4 us
    all_to_all x1, blocking collectives, in_quad(): lax.all_to_all(value, 'wide', 0, 0, axis_index_groups=quads, tiled=True)  12.8 us
    all_to_all x3, waiting for transfers between devices, in_quad(): lax.all_to_all(value, 'wide', 0, 0, axis_index_groups=quads, tiled=True)  10.8 us
    unnamed x12, local copies, waits for them, and re-layouts  7.57 us
    ppermute x2, waiting for transfers between devices, swap(): return lax.ppermute(value, 'wide', [(i, i ^ bits) for i in range(wide)])  6.12 us
    pallas_call x8, Pallas kernels, call(): pl.pallas_call(kernel, out_shape=out_shape, compiler_params=pltpu.Compile...  5.45 us
    pallas_call x1, Pallas kernels, fetch(): pl.pallas_call(functools.partial(fetch_kernel, pieces, count), in_specs=[...  3.47 us
    ppermute x2, starting transfers between devices, swap(): return lax.ppermute(value, 'wide', [(i, i ^ bits) for i in range(wide)])  2.66 us
  transfers between devices with their start and end apart: 7, of which 5 were waited for; matrix products, arithmetic and copies ran while one was open for 0% of the time, Pallas kernels for 7%

profile of v10, /device:TPU:0, one launch (start us, length us, event | category | flops | bytes accessed | tf_op | source)
XLA Modules:
  0.0 65.3 jit_solution(6482604330654846744)
XLA Ops:
  0.0 0.0 copy-start.5
  0.0 0.9 %copy-done.5 = bf16[16,4096]{1,0:T(8,128)(2,1)S(1)} copy-done((bf16[16,4096]{1,0:T(8,128)(2,1)S(1)}, bf16[16,4096]{1,0:T(8,128)(2,1)}, u32[]{:S(2)}) %copy-start.5) | copy-done | bytes 131096
  0.9 0.8 %spread.2 = bf16[64,4096]{1,0:T(8,128)(2,1)} custom-call(bf16[16,4096]{1,0:T(8,128)(2,1)S(1)} %copy-done.5), custom_call_target="tpu_custom_call" | custom-call | flops 1000000 | tf_op jit(solution)/shard_map/spread/pallas_call | solution.py:15
  1.7 5.2 %all-to-all-start = ((bf16[4,16,4096]{2,1,0:T(8,128)(2,1)}), bf16[4,16,4096]{2,1,0:T(8,128)(2,1)S(1)}, u32[]{:S(2)}, u32[]{:S(2)}) async-start(bf16[4,16,4096]{2,1,0:T(8,128)(2,1)} %bitcast), calls=%async_computation | async-start | bytes 1048576 | tf_op jit(solution)/shard_map/all_to_all | solution.py:141
  7.0 2.6 %collective-permute-start = (bf16[16,4096]{1,0:T(8,128)(2,1)}, bf16[16,4096]{1,0:T(8,128)(2,1)S(1)}, u32[]{:S(2)}, u32[]{:S(2)}) collective-permute-start(bf16[16,4096]{1,0:T(8,128)(2,1)} %block_ref.1), channel_id=1, source_target_pairs={{0,8},{2,10},{4,12},{6,14},{8,0},{10,2},{12,4},{14,6},{1,9},{3,11}... | collective-permute-start | bytes 393224 | tf_op jit(solution)/shard_map/ppermute | solution.py:135
  9.6 6.1 %collective-permute-done.block_ref = bf16[16,4096]{1,0:T(8,128)(2,1)S(1)} collective-permute-done((bf16[16,4096]{1,0:T(8,128)(2,1)}, bf16[16,4096]{1,0:T(8,128)(2,1)S(1)}, u32[]{:S(2)}, u32[]{:S(2)}) %collective-permute-start) | collective-permute-done | bytes 131104 | tf_op jit(solution)/shard_map/ppermute | solution.py:135
  15.7 0.9 %spread.3 = bf16[64,4096]{1,0:T(8,128)(2,1)} custom-call(bf16[16,4096]{1,0:T(8,128)(2,1)S(1)} %collective-permute-done.block_ref), custom_call_target="tpu_custom_call" | custom-call | flops 1000000 | tf_op jit(solution)/shard_map/spread/pallas_call | solution.py:15
  16.6 1.2 %all-to-all-done = bf16[4,16,4096]{2,1,0:T(8,128)(2,1)S(1)} async-done(((bf16[4,16,4096]{2,1,0:T(8,128)(2,1)}), bf16[4,16,4096]{2,1,0:T(8,128)(2,1)S(1)}, u32[]{:S(2)}, u32[]{:S(2)}) %all-to-all-start) | async-done | bytes 524320 | tf_op jit(solution)/shard_map/all_to_all | solution.py:141
  17.8 5.7 %all-to-all-start.1 = ((bf16[4,16,4096]{2,1,0:T(8,128)(2,1)}), bf16[4,16,4096]{2,1,0:T(8,128)(2,1)S(1)}, u32[]{:S(2)}, u32[]{:S(2)}) async-start(bf16[4,16,4096]{2,1,0:T(8,128)(2,1)} %bitcast.2), calls=%async_computation.1 | async-start | bytes 1048576 | tf_op jit(solution)/shard_map/all_to_all | solution.py:141
  23.4 3.5 %fetch.1 = (bf16[4096,512]{1,0:T(8,128)(2,1)S(1)}, bf16[4096,512]{1,0:T(8,128)(2,1)S(1)}) custom-call(bf16[4096,512]{1,0:T(8,128)(2,1)} %refs_0_.1, bf16[4096,512]{1,0:T(8,128)(2,1)} %refs_1_.1), custom_call_target="tpu_custom_call" | custom-call | flops 4000000000 | tf_op jit(solution)/shard_map/fetch/pallas_call | solution.py:41
  26.9 0.0 copy-start.1
  26.9 2.0 %copy-done.1 = bf16[4096,512]{1,0:T(8,128)(2,1)} copy-done((bf16[4096,512]{1,0:T(8,128)(2,1)}, bf16[4096,512]{1,0:T(8,128)(2,1)S(1)}, u32[]{:S(2)}) %copy-start.1) | copy-done | bytes 4194328
  28.9 0.0 copy-start.3
  28.9 2.0 %copy-done.3 = bf16[4096,512]{1,0:T(8,128)(2,1)} copy-done((bf16[4096,512]{1,0:T(8,128)(2,1)}, bf16[4096,512]{1,0:T(8,128)(2,1)S(1)}, u32[]{:S(2)}) %copy-start.3) | copy-done | bytes 4194328
  30.9 0.0 all-to-all-done.1
  30.9 0.0 copy-start.2
  30.9 0.0 copy-start.4
  30.9 2.3 %copy-done.4 = bf16[4096,512]{1,0:T(8,128)(2,1)S(1)} copy-done((bf16[4096,512]{1,0:T(8,128)(2,1)S(1)}, bf16[4096,512]{1,0:T(8,128)(2,1)}, u32[]{:S(2)}) %copy-start.4) | copy-done | bytes 4194328
  33.2 0.0 copy-start
  33.2 0.7 %project.2.gate_ref = f32[128,512]{1,0:T(8,128)S(1)} custom-call(bf16[64,4096]{1,0:T(8,128)(2,1)S(1)} %bitcast.8, bf16[64,4096]{1,0:T(8,128)(2,1)S(1)} %bitcast.10, bf16[4096,512]{1,0:T(8,128)(2,1)S(1)} %copy-done.4), custom_call_target="tpu_custom_call" | custom-call | flops 400000000 | tf_op jit(solution)/shard_map/project/pallas_call | solution.py:15
  33.9 0.4 copy-done.2
  34.3 0.7 %project.3.up_ref = f32[128,512]{1,0:T(8,128)S(1)} custom-call(bf16[64,4096]{1,0:T(8,128)(2,1)S(1)} %bitcast.9, bf16[64,4096]{1,0:T(8,128)(2,1)S(1)} %bitcast.11, bf16[4096,512]{1,0:T(8,128)(2,1)S(1)} %copy-done.2), custom_call_target="tpu_custom_call" | custom-call | flops 400000000 | tf_op jit(solution)/shard_map/project/pallas_call | solution.py:15
  35.0 0.1 collective-permute-start.2
  35.1 0.5 collective-permute-start.1
  35.6 1.0 %collective-permute-done.2.up_other_ref = f32[128,512]{1,0:T(8,128)S(1)} collective-permute-done((f32[128,512]{1,0:T(8,128)S(1)}, f32[128,512]{1,0:T(8,128)S(1)}, u32[]{:S(2)}, u32[]{:S(2)}) %collective-permute-start.2) | collective-permute-done | bytes 262176 | tf_op jit(solution)/shard_map/ppermute | solution.py:138
  36.6 0.4 collective-permute-done.1.gate_other_ref
  37.0 0.0 copy-done
  37.0 1.5 %down.1 = (bf16[64,4096]{1,0:T(8,128)(2,1)}, bf16[64,4096]{1,0:T(8,128)(2,1)S(1)}) custom-call(f32[128,512]{1,0:T(8,128)S(1)} %project.2.gate_ref, f32[128,512]{1,0:T(8,128)S(1)} %collective-permute-done.1.gate_other_ref, f32[128,512]{1,0:T(8,128)S(1)} %project.3.up_ref, f32[128,512]{1,0:T(8,128)S(1)} %collective-permute-done.2.up_other_ref, ...), custom_call_target="tpu_custom_call" | custom-call | flops 536870912 | tf_op jit(solution)/shard_map/down/pallas_call | solution.py:15
  38.5 12.8 %all_to_all.44 = bf16[4,16,4096]{2,1,0:T(8,128)(2,1)S(1)} all-to-all(bf16[4,16,4096]{2,1,0:T(8,128)(2,1)S(1)} %bitcast.14), channel_id=1, replica_groups={{0,2,4,6},{8,10,12,14},{1,3,5,7},{9,11,13,15},{16,18,20,22},{24,26,28,3..., dimensions={0} | all-to-all | bytes 1048576 | tf_op jit(solution)/shard_map/all_to_all | solution.py:141
  51.3 3.5 %all-to-all-start.2 = ((bf16[4,16,4096]{2,1,0:T(8,128)(2,1)}), bf16[4,16,4096]{2,1,0:T(8,128)(2,1)S(1)}, u32[]{:S(2)}, u32[]{:S(2)}) async-start(bf16[4,16,4096]{2,1,0:T(8,128)(2,1)} %bitcast.4), calls=%async_computation.2 | async-start | bytes 1048576 | tf_op jit(solution)/shard_map/all_to_all | solution.py:141
  54.8 0.1 fold.3
  54.9 0.1 collective-permute-start.3
  55.0 9.6 %all-to-all-done.2 = bf16[4,16,4096]{2,1,0:T(8,128)(2,1)S(1)} async-done(((bf16[4,16,4096]{2,1,0:T(8,128)(2,1)}), bf16[4,16,4096]{2,1,0:T(8,128)(2,1)S(1)}, u32[]{:S(2)}, u32[]{:S(2)}) %all-to-all-start.2) | async-done | bytes 524320 | tf_op jit(solution)/shard_map/all_to_all | solution.py:141
  64.5 0.1 fold.2.own_ref
  64.6 0.0 collective-permute-done.3.refs_0_
  64.6 0.7 %add.1 = bf16[16,4096]{1,0:T(8,128)(2,1)} custom-call(f32[16,4096]{1,0:T(8,128)S(1)} %fold.2.own_ref, bf16[16,4096]{1,0:T(8,128)(2,1)S(1)} %collective-permute-done.3.refs_0_), custom_call_target="tpu_custom_call" | custom-call | flops 1000000 | tf_op jit(solution)/shard_map/add/pallas_call | solution.py:15
Async XLA Ops:
  0.0 0.9 %copy-start.5 = (bf16[16,4096]{1,0:T(8,128)(2,1)S(1)}, bf16[16,4096]{1,0:T(8,128)(2,1)}, u32[]{:S(2)}) copy-start(bf16[16,4096]{1,0:T(8,128)(2,1)} %block_ref.1) | copy-start | bytes 393220
  1.7 16.0 %all-to-all-start = ((bf16[4,16,4096]{2,1,0:T(8,128)(2,1)}), bf16[4,16,4096]{2,1,0:T(8,128)(2,1)S(1)}, u32[]{:S(2)}, u32[]{:S(2)}) async-start(bf16[4,16,4096]{2,1,0:T(8,128)(2,1)} %bitcast), calls=%async_computation | async-start | bytes 1048576 | tf_op jit(solution)/shard_map/all_to_all | solution.py:141
  7.0 8.7 %collective-permute-start = (bf16[16,4096]{1,0:T(8,128)(2,1)}, bf16[16,4096]{1,0:T(8,128)(2,1)S(1)}, u32[]{:S(2)}, u32[]{:S(2)}) collective-permute-start(bf16[16,4096]{1,0:T(8,128)(2,1)} %block_ref.1), channel_id=1, source_target_pairs={{0,8},{2,10},{4,12},{6,14},{8,0},{10,2},{12,4},{14,6},{1,9},{3,11}... | collective-permute-start | bytes 393224 | tf_op jit(solution)/shard_map/ppermute | solution.py:135
  17.8 13.1 %all-to-all-start.1 = ((bf16[4,16,4096]{2,1,0:T(8,128)(2,1)}), bf16[4,16,4096]{2,1,0:T(8,128)(2,1)S(1)}, u32[]{:S(2)}, u32[]{:S(2)}) async-start(bf16[4,16,4096]{2,1,0:T(8,128)(2,1)} %bitcast.2), calls=%async_computation.1 | async-start | bytes 1048576 | tf_op jit(solution)/shard_map/all_to_all | solution.py:141
  26.9 2.0 %copy-start.1 = (bf16[4096,512]{1,0:T(8,128)(2,1)}, bf16[4096,512]{1,0:T(8,128)(2,1)S(1)}, u32[]{:S(2)}) copy-start(bf16[4096,512]{1,0:T(8,128)(2,1)S(1)} %get-tuple-element.10.refs_2_) | copy-start | bytes 12582916
  28.9 2.0 %copy-start.3 = (bf16[4096,512]{1,0:T(8,128)(2,1)}, bf16[4096,512]{1,0:T(8,128)(2,1)S(1)}, u32[]{:S(2)}) copy-start(bf16[4096,512]{1,0:T(8,128)(2,1)S(1)} %get-tuple-element.9.refs_2_) | copy-start | bytes 12582916
  30.9 3.5 %copy-start.2 = (bf16[4096,512]{1,0:T(8,128)(2,1)S(1)}, bf16[4096,512]{1,0:T(8,128)(2,1)}, u32[]{:S(2)}) copy-start(bf16[4096,512]{1,0:T(8,128)(2,1)} %copy-done.1) | copy-start | bytes 12582916
  30.9 2.3 %copy-start.4 = (bf16[4096,512]{1,0:T(8,128)(2,1)S(1)}, bf16[4096,512]{1,0:T(8,128)(2,1)}, u32[]{:S(2)}) copy-start(bf16[4096,512]{1,0:T(8,128)(2,1)} %copy-done.3) | copy-start | bytes 12582916
  33.2 3.8 %copy-start = (bf16[512,4096]{1,0:T(8,128)(2,1)S(1)}, bf16[512,4096]{1,0:T(8,128)(2,1)}, u32[]{:S(2)}) copy-start(bf16[512,4096]{1,0:T(8,128)(2,1)} %weight_ref.1) | copy-start | bytes 12582916
  35.0 1.6 %collective-permute-start.2 = (f32[128,512]{1,0:T(8,128)S(1)}, f32[128,512]{1,0:T(8,128)S(1)}, u32[]{:S(2)}, u32[]{:S(2)}) collective-permute-start(f32[128,512]{1,0:T(8,128)S(1)} %project.3.up_ref), channel_id=1, source_target_pairs={{0,1},{1,0},{2,3},{3,2},{4,5},{5,4},{6,7},{7,6},{8,9},{9,8},{10,11... | collective-permute-start | bytes 786440 | tf_op jit(solution)/shard_map/ppermute | solution.py:138
  35.1 1.9 %collective-permute-start.1 = (f32[128,512]{1,0:T(8,128)S(1)}, f32[128,512]{1,0:T(8,128)S(1)}, u32[]{:S(2)}, u32[]{:S(2)}) collective-permute-start(f32[128,512]{1,0:T(8,128)S(1)} %project.2.gate_ref), channel_id=1, source_target_pairs={{0,1},{1,0},{2,3},{3,2},{4,5},{5,4},{6,7},{7,6},{8,9},{9,8},{10,11... | collective-permute-start | bytes 786440 | tf_op jit(solution)/shard_map/ppermute | solution.py:138
  51.3 13.2 %all-to-all-start.2 = ((bf16[4,16,4096]{2,1,0:T(8,128)(2,1)}), bf16[4,16,4096]{2,1,0:T(8,128)(2,1)S(1)}, u32[]{:S(2)}, u32[]{:S(2)}) async-start(bf16[4,16,4096]{2,1,0:T(8,128)(2,1)} %bitcast.4), calls=%async_computation.2 | async-start | bytes 1048576 | tf_op jit(solution)/shard_map/all_to_all | solution.py:141
  54.9 9.7 %collective-permute-start.3 = (bf16[16,4096]{1,0:T(8,128)(2,1)S(1)}, bf16[16,4096]{1,0:T(8,128)(2,1)S(1)}, u32[]{:S(2)}, u32[]{:S(2)}) collective-permute-start(bf16[16,4096]{1,0:T(8,128)(2,1)S(1)} %fold.3), channel_id=1, source_target_pairs={{0,8},{2,10},{4,12},{6,14},{8,0},{10,2},{12,4},{14,6},{1,9},{3,11}... | collective-permute-start | bytes 393224 | tf_op jit(solution)/shard_map/ppermute | solution.py:135

commit v11 on v9

--- a/solution.py
+++ b/solution.py
@@ -11,14 +11,16 @@
 BF16 = jnp.bfloat16
 
 
-def call(kernel, name, out_shape, flops, vmem, *operands):
+def call(kernel, name, out_shape, hint, vmem, *operands, after=()):
     return pl.pallas_call(
         kernel,
+        in_specs=[pl.BlockSpec(memory_space=pltpu.VMEM)] * len(operands)
+        + [pl.BlockSpec(memory_space=pl.ANY)] * len(after),
         out_shape=out_shape,
         compiler_params=pltpu.CompilerParams(vmem_limit_bytes=vmem),
-        cost_estimate=pl.CostEstimate(flops=flops, bytes_accessed=0, transcendentals=0),
+        cost_estimate=pl.CostEstimate(flops=hint, bytes_accessed=0, transcendentals=0),
         name=name,
-    )(*operands)
+    )(*operands, *after)
 
 
 def fetch_kernel(pieces, count, *refs):
@@ -50,32 +52,20 @@
     )(*weights)
 
 
-def pack_kernel(*refs):
-    *block_refs, out_ref = refs
-    rows = block_refs[0].shape[0]
-    for k, ref in enumerate(block_refs):
-        out_ref[k * rows:(k + 1) * rows, :] = ref[...]
-
-
-def pack(blocks):
-    rows, width = blocks[0].shape
-    out = jax.ShapeDtypeStruct((len(blocks) * rows, width), BF16)
-    return call(pack_kernel, "pack", out, 4000000000, 2 << 20, *blocks)
-
-
 def project_kernel(*refs):
     *block_refs, weight_ref, out_ref = refs
     rows = jnp.concatenate([ref[...] for ref in block_refs], axis=0)
     out_ref[...] = jnp.dot(rows, weight_ref[...], preferred_element_type=F32)
 
 
-def project(blocks, weight):
+def project(blocks, weight, hint):
     rows = sum(block.shape[0] for block in blocks)
     out = jax.ShapeDtypeStruct((rows, weight.shape[1]), F32)
-    return call(project_kernel, "project", out, 400000000, 4 << 20, *blocks, weight)
+    return call(project_kernel, "project", out, hint, 4 << 20, *blocks, weight)
 
 
-def down_kernel(gate_ref, gate_other_ref, up_ref, up_other_ref, weight_ref, *out_refs):
+def down_kernel(blocks, gate_ref, gate_other_ref, up_ref, up_other_ref, weight_ref, *refs):
+    out_refs = refs[-blocks:]
     gate_sum = gate_ref[...] + gate_other_ref[...]
     up_sum = up_ref[...] + up_other_ref[...]
     hidden = (jax.nn.silu(gate_sum) * up_sum).astype(BF16)
@@ -93,12 +83,13 @@
     lax.fori_loop(0, width // tile, column_tile, 0, unroll=True)
 
 
-def down(gate, gate_other, up, up_other, weight, rows, dtypes):
+def down(gate, gate_other, up, up_other, weight, rows, dtypes, after):
     width = weight.shape[1]
     outs = [jax.ShapeDtypeStruct((rows, width), dtype) for dtype in dtypes]
-    flops = 2 * gate.shape[0] * weight.shape[0] * width
+    hint = 2 * gate.shape[0] * weight.shape[0] * width
     return call(
-        down_kernel, "down", outs, flops, 4 << 20, gate, gate_other, up, up_other, weight
+        functools.partial(down_kernel, len(outs)), "down", outs, hint, 4 << 20,
+        gate, gate_other, up, up_other, weight, after=after,
     )
 
 
@@ -110,16 +101,9 @@
 
 
 def add(own, arrived, dtype, hint=1000000, after=()):
-    count = len(arrived)
-    return pl.pallas_call(
-        functools.partial(add_kernel, count),
-        in_specs=[pl.BlockSpec(memory_space=pltpu.VMEM)] * (1 + count)
-        + [pl.BlockSpec(memory_space=pl.ANY)] * len(after),
-        out_shape=jax.ShapeDtypeStruct(own.shape, dtype),
-        compiler_params=pltpu.CompilerParams(vmem_limit_bytes=2 << 20),
-        cost_estimate=pl.CostEstimate(flops=hint, bytes_accessed=0, transcendentals=0),
-        name="add",
-    )(own, *arrived, *after)
+    out = jax.ShapeDtypeStruct(own.shape, dtype)
+    kernel = functools.partial(add_kernel, len(arrived))
+    return call(kernel, "add", out, hint, 2 << 20, own, *arrived, after=after)
 
 
 def make_local(wide, narrow):
@@ -146,25 +130,29 @@
         for far in fars:
             for near in (2, 3, 1):
                 block[far + near] = swap(block[far], near)
-        stay = [0, 2] + fars
-        near_blocks = pack([block[b] for b in (0, 2, 1, 3)])
-        order = [0, 2, 1, 3] + [far + near for far in fars for near in (0, 3, 2, 1)]
-        far_blocks = [block[b] for b in order[4:]]
-        gate_part = project([near_blocks] + far_blocks, gate_held)
-        up_part = project([near_blocks] + far_blocks, up_held)
-        outs = down(
-            gate_part, across_cores(gate_part), up_part, across_cores(up_part),
-            down_weight, rows, [F32 if b in stay else BF16 for b in order],
-        )
-        part = dict(zip(order, outs))
+
+        def partials(order, gate_held, up_held, hint, after=()):
+            blocks = [block[b] for b in order]
+            gate_part = project(blocks, gate_held, hint)
+            up_part = project(blocks, up_held, hint)
+            outs = down(
+                gate_part, across_cores(gate_part), up_part, across_cores(up_part),
+                down_weight, rows, [F32 if b in stay else BF16 for b in order], after,
+            )
+            return dict(zip(order, outs))
+
+        stay = [0] + fars
+        part = partials([0, 1, 2], gate_held, up_held, 100000000)
+        gate_held, up_held, part[1] = lax.optimization_barrier((gate_held, up_held, part[1]))
+        total = add(part[0], [swap(part[1], 1), swap(part[2], 2)], F32, 1000000000)
+        late = [3] + [far + near for far in fars for near in (0, 3, 2, 1)]
+        part.update(partials(late, gate_held, up_held, 400000000, [total]))
         sums = []
         for far in fars:
             quad = [swap(part[far + near], near) for near in (2, 3, 1)]
             sums.append(add(part[far], quad, BF16))
         arrived = [swap(value, far) for value, far in zip(sums, fars)]
-        pair = add(part[2], [swap(part[3], 1)], BF16, after=sums)
-        total = add(part[0], arrived, F32, 1500000000)
-        return add(total, [swap(part[1], 1), swap(pair, 2)], BF16)
+        return add(total, [swap(part[3], 3)] + arrived, BF16)
 
     return local
 

time: 44.8 us -> 49.7 us (1.11)
  waiting for transfers between devices: 17.3 us -> 21.6 us
  Pallas kernels: 6.48 us -> 9.24 us
  starting transfers between devices: 20.8 us -> 18.5 us
    ppermute x14, waiting for transfers between devices: 16.2 us -> 19.5 us  [swap(): return lax.ppermute(value, 'wide', [(i, i ^ bits) for i in range(wide)])]
    pallas_call x8 -> x9, Pallas kernels: 3 us -> 5.77 us  [call(): pl.pallas_call(kernel, in_specs=[pl.BlockSpec(memory_space=pltpu.VMEM)] *...]
    ppermute x14, starting transfers between devices: 20.1 us -> 17.8 us  [swap(): return lax.ppermute(value, 'wide', [(i, i ^ bits) for i in range(wide)])]
    ppermute x2 -> x4, waiting for transfers between devices: 1.16 us -> 2.19 us  [across_cores(): lax.ppermute(value, 'narrow', [(i, (i + 1) % narrow) for i in range(narro...]
  transfers between devices with their start and end apart: 16 -> 18, of which waited for: 10 -> 11; matrix products, arithmetic and copies ran while one was open for 0% -> 0% of each run, Pallas kernels for 10% -> 16%
where the time goes in v11:
time: 49.7 us; the launch traced here: 49.5 us
  waiting for transfers between devices  21.6 us (43%)
  starting transfers between devices  18.5 us (37%)
  Pallas kernels  9.24 us (19%)
    ppermute x14, waiting for transfers between devices, swap(): return lax.ppermute(value, 'wide', [(i, i ^ bits) for i in range(wide)])  19.5 us
    ppermute x14, starting transfers between devices, swap(): return lax.ppermute(value, 'wide', [(i, i ^ bits) for i in range(wide)])  17.8 us
    pallas_call x9, Pallas kernels, call(): pl.pallas_call(kernel, in_specs=[pl.BlockSpec(memory_space=pltpu.VMEM)] *...  5.77 us
    pallas_call x1, Pallas kernels, fetch(): pl.pallas_call(functools.partial(fetch_kernel, pieces, count), in_specs=[...  3.47 us
    ppermute x4, waiting for transfers between devices, across_cores(): lax.ppermute(value, 'narrow', [(i, (i + 1) % narrow) for i in range(narro...  2.19 us
  transfers between devices with their start and end apart: 18, of which 11 were waited for; matrix products, arithmetic and copies ran while one was open for 0% of the time, Pallas kernels for 16%

profile of v11, /device:TPU:0, one launch (start us, length us, event | category | flops | bytes accessed | tf_op | source)
XLA Modules:
  0.0 49.5 jit_solution(5559377018883648689)
XLA Ops:
  0.0 3.0 %collective-permute-start = (bf16[16,4096]{1,0:T(8,128)(2,1)}, bf16[16,4096]{1,0:T(8,128)(2,1)S(1)}, u32[]{:S(2)}, u32[]{:S(2)}) collective-permute-start(bf16[16,4096]{1,0:T(8,128)(2,1)} %refs_0_.5), channel_id=1, source_target_pairs={{0,2},{2,0},{4,6},{6,4},{8,10},{10,8},{12,14},{14,12},{1,3},{3,1},... | collective-permute-start | bytes 393224 | tf_op jit(solution)/shard_map/ppermute | solution.py:113
  3.0 1.6 %collective-permute-start.1 = (bf16[16,4096]{1,0:T(8,128)(2,1)}, bf16[16,4096]{1,0:T(8,128)(2,1)S(1)}, u32[]{:S(2)}, u32[]{:S(2)}) collective-permute-start(bf16[16,4096]{1,0:T(8,128)(2,1)} %refs_0_.5), channel_id=1, source_target_pairs={{0,4},{2,6},{4,0},{6,2},{8,12},{10,14},{12,8},{14,10},{1,5},{3,7},... | collective-permute-start | bytes 393224 | tf_op jit(solution)/shard_map/ppermute | solution.py:113
  4.5 2.6 %collective-permute-start.7 = (bf16[16,4096]{1,0:T(8,128)(2,1)}, bf16[16,4096]{1,0:T(8,128)(2,1)S(1)}, u32[]{:S(2)}, u32[]{:S(2)}) collective-permute-start(bf16[16,4096]{1,0:T(8,128)(2,1)} %refs_0_.5), channel_id=1, source_target_pairs={{0,8},{2,10},{4,12},{6,14},{8,0},{10,2},{12,4},{14,6},{1,9},{3,11}... | collective-permute-start | bytes 393224 | tf_op jit(solution)/shard_map/ppermute | solution.py:113
  7.1 3.5 %fetch.1 = (bf16[4096,512]{1,0:T(8,128)(2,1)S(1)}, bf16[4096,512]{1,0:T(8,128)(2,1)S(1)}) custom-call(bf16[4096,512]{1,0:T(8,128)(2,1)} %refs_0_.3, bf16[4096,512]{1,0:T(8,128)(2,1)} %refs_1_.1), custom_call_target="tpu_custom_call" | custom-call | flops 4000000000 | tf_op jit(solution)/shard_map/fetch/pallas_call | solution.py:43
  10.6 0.0 collective-permute-done.refs_1_
  10.6 0.0 collective-permute-done.1.refs_2_
  10.6 0.0 copy-done.1
  10.6 0.0 copy-start
  10.7 0.8 %project.4.gate_ref = f32[48,512]{1,0:T(8,128)S(1)} custom-call(bf16[16,4096]{1,0:T(8,128)(2,1)S(1)} %copy-done.1, bf16[16,4096]{1,0:T(8,128)(2,1)S(1)} %collective-permute-done.refs_1_, bf16[16,4096]{1,0:T(8,128)(2,1)S(1)} %collective-permute-done.1.refs_2_, bf16[4096,512]{1,0:T(8,128)(2,1)S(1)} %get-tuple-element.32.refs_3_.refs_5_), custom_call_target="tpu_custom_call" | custom-call | flops 100000000 | tf_op jit(solution)/shard_map/project/pallas_call | solution.py:15
  11.5 0.0 collective-permute-start.2
  11.5 0.6 %collective-permute-start.6 = (bf16[16,4096]{1,0:T(8,128)(2,1)S(1)}, bf16[16,4096]{1,0:T(8,128)(2,1)S(1)}, u32[]{:S(2)}, u32[]{:S(2)}) collective-permute-start(bf16[16,4096]{1,0:T(8,128)(2,1)S(1)} %collective-permute-done.1.refs_2_), channel_id=1, source_target_pairs={{0,2},{2,0},{4,6},{6,4},{8,10},{10,8},{12,14},{14,12},{1,3},{3,1},... | collective-permute-start | bytes 393224 | tf_op jit(solution)/shard_map/ppermute | solution.py:113
  12.1 1.1 %collective-permute-done.7.refs_1_ = bf16[16,4096]{1,0:T(8,128)(2,1)S(1)} collective-permute-done((bf16[16,4096]{1,0:T(8,128)(2,1)}, bf16[16,4096]{1,0:T(8,128)(2,1)S(1)}, u32[]{:S(2)}, u32[]{:S(2)}) %collective-permute-start.7) | collective-permute-done | bytes 131104 | tf_op jit(solution)/shard_map/ppermute | solution.py:113
  13.2 0.3 collective-permute-start.8
  13.5 1.7 %collective-permute-start.9 = (bf16[16,4096]{1,0:T(8,128)(2,1)S(1)}, bf16[16,4096]{1,0:T(8,128)(2,1)S(1)}, u32[]{:S(2)}, u32[]{:S(2)}) collective-permute-start(bf16[16,4096]{1,0:T(8,128)(2,1)S(1)} %collective-permute-done.7.refs_1_), channel_id=1, source_target_pairs={{0,4},{2,6},{4,0},{6,2},{8,12},{10,14},{12,8},{14,10},{1,5},{3,7},... | collective-permute-start | bytes 393224 | tf_op jit(solution)/shard_map/ppermute | solution.py:113
  15.2 1.5 %collective-permute-start.10 = (bf16[16,4096]{1,0:T(8,128)(2,1)S(1)}, bf16[16,4096]{1,0:T(8,128)(2,1)S(1)}, u32[]{:S(2)}, u32[]{:S(2)}) collective-permute-start(bf16[16,4096]{1,0:T(8,128)(2,1)S(1)} %collective-permute-done.7.refs_1_), channel_id=1, source_target_pairs={{0,2},{2,0},{4,6},{6,4},{8,10},{10,8},{12,14},{14,12},{1,3},{3,1},... | collective-permute-start | bytes 393224 | tf_op jit(solution)/shard_map/ppermute | solution.py:113
  16.7 0.8 %project.5.up_ref = f32[48,512]{1,0:T(8,128)S(1)} custom-call(bf16[16,4096]{1,0:T(8,128)(2,1)S(1)} %copy-done.1, bf16[16,4096]{1,0:T(8,128)(2,1)S(1)} %collective-permute-done.refs_1_, bf16[16,4096]{1,0:T(8,128)(2,1)S(1)} %collective-permute-done.1.refs_2_, bf16[4096,512]{1,0:T(8,128)(2,1)S(1)} %get-tuple-element.33.refs_3_.refs_5_), custom_call_target="tpu_custom_call" | custom-call | flops 100000000 | tf_op jit(solution)/shard_map/project/pallas_call | solution.py:15
  17.5 0.0 collective-permute-done.2.gate_other_ref
  17.5 0.1 collective-permute-start.3
  17.6 1.3 %collective-permute-done.3.up_other_ref = f32[48,512]{1,0:T(8,128)S(1)} collective-permute-done((f32[48,512]{1,0:T(8,128)S(1)}, f32[48,512]{1,0:T(8,128)S(1)}, u32[]{:S(2)}, u32[]{:S(2)}) %collective-permute-start.3) | collective-permute-done | bytes 98336 | tf_op jit(solution)/shard_map/ppermute | solution.py:116
  18.9 0.0 copy-done
  18.9 0.8 %down.2 = (f32[16,4096]{1,0:T(8,128)S(1)}, bf16[16,4096]{1,0:T(8,128)(2,1)S(1)}, bf16[16,4096]{1,0:T(8,128)(2,1)S(1)}) custom-call(f32[48,512]{1,0:T(8,128)S(1)} %project.4.gate_ref, f32[48,512]{1,0:T(8,128)S(1)} %collective-permute-done.2.gate_other_ref, f32[48,512]{1,0:T(8,128)S(1)} %project.5.up_ref, f32[48,512]{1,0:T(8,128)S(1)} %collective-permute-done.3.up_other_ref, ...), custom_call_target="tpu_custom_call" | custom-call | flops 201326592 | tf_op jit(solution)/shard_map/down/pallas_call | solution.py:15
  19.7 0.6 %collective-permute-start.4 = (bf16[16,4096]{1,0:T(8,128)(2,1)S(1)}, bf16[16,4096]{1,0:T(8,128)(2,1)S(1)}, u32[]{:S(2)}, u32[]{:S(2)}) collective-permute-start(bf16[16,4096]{1,0:T(8,128)(2,1)S(1)} %get-tuple-element.30), channel_id=1, source_target_pairs={{0,2},{2,0},{4,6},{6,4},{8,10},{10,8},{12,14},{14,12},{1,3},{3,1},... | collective-permute-start | bytes 393224 | tf_op jit(solution)/shard_map/ppermute | solution.py:113
  20.3 0.4 collective-permute-done.6.refs_0_
  20.7 0.4 collective-permute-start.5
  21.1 0.0 collective-permute-done.8.refs_2_
  21.1 0.3 collective-permute-done.9.refs_3_
  21.4 2.0 %collective-permute-done.10.refs_4_ = bf16[16,4096]{1,0:T(8,128)(2,1)S(1)} collective-permute-done((bf16[16,4096]{1,0:T(8,128)(2,1)S(1)}, bf16[16,4096]{1,0:T(8,128)(2,1)S(1)}, u32[]{:S(2)}, u32[]{:S(2)}) %collective-permute-start.10) | collective-permute-done | bytes 131104 | tf_op jit(solution)/shard_map/ppermute | solution.py:113
  23.4 0.8 %project.6.gate_ref = f32[80,512]{1,0:T(8,128)S(1)} custom-call(bf16[16,4096]{1,0:T(8,128)(2,1)S(1)} %collective-permute-done.6.refs_0_, bf16[16,4096]{1,0:T(8,128)(2,1)S(1)} %collective-permute-done.7.refs_1_, bf16[16,4096]{1,0:T(8,128)(2,1)S(1)} %collective-permute-done.8.refs_2_, bf16[16,4096]{1,0:T(8,128)(2,1)S(1)} %collective-permute-done.9.refs_3_, ...), custom_call_target="tpu_custom_call" | custom-call | flops 400000000 | tf_op jit(solution)/shard_map/project/pallas_call | solution.py:15
  24.3 0.1 collective-permute-start.11
  24.3 0.8 %project.7.up_ref = f32[80,512]{1,0:T(8,128)S(1)} custom-call(bf16[16,4096]{1,0:T(8,128)(2,1)S(1)} %collective-permute-done.6.refs_0_, bf16[16,4096]{1,0:T(8,128)(2,1)S(1)} %collective-permute-done.7.refs_1_, bf16[16,4096]{1,0:T(8,128)(2,1)S(1)} %collective-permute-done.8.refs_2_, bf16[16,4096]{1,0:T(8,128)(2,1)S(1)} %collective-permute-done.9.refs_3_, ...), custom_call_target="tpu_custom_call" | custom-call | flops 400000000 | tf_op jit(solution)/shard_map/project/pallas_call | solution.py:15
  25.2 0.6 %collective-permute-start.12 = (f32[80,512]{1,0:T(8,128)S(1)}, f32[80,512]{1,0:T(8,128)S(1)}, u32[]{:S(2)}, u32[]{:S(2)}) collective-permute-start(f32[80,512]{1,0:T(8,128)S(1)} %project.7.up_ref), channel_id=1, source_target_pairs={{0,1},{1,0},{2,3},{3,2},{4,5},{5,4},{6,7},{7,6},{8,9},{9,8},{10,11... | collective-permute-start | bytes 491528 | tf_op jit(solution)/shard_map/ppermute | solution.py:116
  25.7 0.1 collective-permute-done.4.refs_0_
  25.8 0.0 collective-permute-done.5.refs_1_
  25.9 0.0 collective-permute-done.11.gate_other_ref
  25.9 0.9 %collective-permute-done.12.up_other_ref = f32[80,512]{1,0:T(8,128)S(1)} collective-permute-done((f32[80,512]{1,0:T(8,128)S(1)}, f32[80,512]{1,0:T(8,128)S(1)}, u32[]{:S(2)}, u32[]{:S(2)}) %collective-permute-start.12) | collective-permute-done | bytes 163872 | tf_op jit(solution)/shard_map/ppermute | solution.py:116
  26.8 0.8 %down.3 = (bf16[16,4096]{1,0:T(8,128)(2,1)S(1)}, f32[16,4096]{1,0:T(8,128)S(1)}, bf16[16,4096]{1,0:T(8,128)(2,1)S(1)}, bf16[16,4096]{1,0:T(8,128)(2,1)S(1)}, bf16[16,4096]{1,0:T(8,128)(2,1)S(1)}) custom-call(f32[80,512]{1,0:T(8,128)S(1)} %project.6.gate_ref, f32[80,512]{1,0:T(8,128)S(1)} %collective-permute-done.11.gate_other_ref, ...), custom_call_target="tpu_custom_call" | custom-call | flops 335544320 | tf_op jit(solution)/shard_map/down/pallas_call | solution.py:15
  27.6 0.6 %collective-permute-start.14 = (bf16[16,4096]{1,0:T(8,128)(2,1)S(1)}, bf16[16,4096]{1,0:T(8,128)(2,1)S(1)}, u32[]{:S(2)}, u32[]{:S(2)}) collective-permute-start(bf16[16,4096]{1,0:T(8,128)(2,1)S(1)} %get-tuple-element.36), channel_id=1, source_target_pairs={{0,4},{2,6},{4,0},{6,2},{8,12},{10,14},{12,8},{14,10},{1,5},{3,7},... | collective-permute-start | bytes 393224 | tf_op jit(solution)/shard_map/ppermute | solution.py:113
  28.2 1.5 %collective-permute-start.15 = (bf16[16,4096]{1,0:T(8,128)(2,1)S(1)}, bf16[16,4096]{1,0:T(8,128)(2,1)S(1)}, u32[]{:S(2)}, u32[]{:S(2)}) collective-permute-start(bf16[16,4096]{1,0:T(8,128)(2,1)S(1)} %get-tuple-element.37), channel_id=1, source_target_pairs={{0,6},{2,4},{4,2},{6,0},{8,14},{10,12},{12,10},{14,8},{1,7},{3,5},... | collective-permute-start | bytes 393224 | tf_op jit(solution)/shard_map/ppermute | solution.py:113
  29.7 1.5 %collective-permute-start.16 = (bf16[16,4096]{1,0:T(8,128)(2,1)S(1)}, bf16[16,4096]{1,0:T(8,128)(2,1)S(1)}, u32[]{:S(2)}, u32[]{:S(2)}) collective-permute-start(bf16[16,4096]{1,0:T(8,128)(2,1)S(1)} %get-tuple-element.38), channel_id=1, source_target_pairs={{0,2},{2,0},{4,6},{6,4},{8,10},{10,8},{12,14},{14,12},{1,3},{3,1},... | collective-permute-start | bytes 393224 | tf_op jit(solution)/shard_map/ppermute | solution.py:113
  31.2 0.5 collective-permute-start.13
  31.6 2.4 %collective-permute-done.14.refs_0_ = bf16[16,4096]{1,0:T(8,128)(2,1)S(1)} collective-permute-done((bf16[16,4096]{1,0:T(8,128)(2,1)S(1)}, bf16[16,4096]{1,0:T(8,128)(2,1)S(1)}, u32[]{:S(2)}, u32[]{:S(2)}) %collective-permute-start.14) | collective-permute-done | bytes 131104 | tf_op jit(solution)/shard_map/ppermute | solution.py:113
  34.0 2.9 %collective-permute-done.15.refs_1_ = bf16[16,4096]{1,0:T(8,128)(2,1)S(1)} collective-permute-done((bf16[16,4096]{1,0:T(8,128)(2,1)S(1)}, bf16[16,4096]{1,0:T(8,128)(2,1)S(1)}, u32[]{:S(2)}, u32[]{:S(2)}) %collective-permute-start.15) | collective-permute-done | bytes 131104 | tf_op jit(solution)/shard_map/ppermute | solution.py:113
  36.9 3.6 %collective-permute-done.16.refs_2_ = bf16[16,4096]{1,0:T(8,128)(2,1)S(1)} collective-permute-done((bf16[16,4096]{1,0:T(8,128)(2,1)S(1)}, bf16[16,4096]{1,0:T(8,128)(2,1)S(1)}, u32[]{:S(2)}, u32[]{:S(2)}) %collective-permute-start.16) | collective-permute-done | bytes 131104 | tf_op jit(solution)/shard_map/ppermute | solution.py:113
  40.5 0.1 add.4
  40.6 1.5 %collective-permute-start.17 = (bf16[16,4096]{1,0:T(8,128)(2,1)S(1)}, bf16[16,4096]{1,0:T(8,128)(2,1)S(1)}, u32[]{:S(2)}, u32[]{:S(2)}) collective-permute-start(bf16[16,4096]{1,0:T(8,128)(2,1)S(1)} %add.4), channel_id=1, source_target_pairs={{0,8},{2,10},{4,12},{6,14},{8,0},{10,2},{12,4},{14,6},{1,9},{3,11}... | collective-permute-start | bytes 393224 | tf_op jit(solution)/shard_map/ppermute | solution.py:113
  42.1 0.0 collective-permute-done.13.refs_0_
  42.1 6.7 %collective-permute-done.17.refs_1_ = bf16[16,4096]{1,0:T(8,128)(2,1)S(1)} collective-permute-done((bf16[16,4096]{1,0:T(8,128)(2,1)S(1)}, bf16[16,4096]{1,0:T(8,128)(2,1)S(1)}, u32[]{:S(2)}, u32[]{:S(2)}) %collective-permute-start.17) | collective-permute-done | bytes 131104 | tf_op jit(solution)/shard_map/ppermute | solution.py:113
  48.8 0.7 %add.5 = bf16[16,4096]{1,0:T(8,128)(2,1)} custom-call(f32[16,4096]{1,0:T(8,128)S(1)} %add.3.refs_0_.own_ref, bf16[16,4096]{1,0:T(8,128)(2,1)S(1)} %collective-permute-done.13.refs_0_, bf16[16,4096]{1,0:T(8,128)(2,1)S(1)} %collective-permute-done.17.refs_1_), custom_call_target="tpu_custom_call" | custom-call | flops 1000000 | tf_op jit(solution)/shard_map/add/pallas_call | solution.py:15
  (2 shorter events, 0.0 us)
Async XLA Ops:
  0.0 10.6 %copy-start.1 = (bf16[16,4096]{1,0:T(8,128)(2,1)S(1)}, bf16[16,4096]{1,0:T(8,128)(2,1)}, u32[]{:S(2)}) copy-start(bf16[16,4096]{1,0:T(8,128)(2,1)} %refs_0_.5) | copy-start | bytes 393220
  0.0 10.6 %collective-permute-start = (bf16[16,4096]{1,0:T(8,128)(2,1)}, bf16[16,4096]{1,0:T(8,128)(2,1)S(1)}, u32[]{:S(2)}, u32[]{:S(2)}) collective-permute-start(bf16[16,4096]{1,0:T(8,128)(2,1)} %refs_0_.5), channel_id=1, source_target_pairs={{0,2},{2,0},{4,6},{6,4},{8,10},{10,8},{12,14},{14,12},{1,3},{3,1},... | collective-permute-start | bytes 393224 | tf_op jit(solution)/shard_map/ppermute | solution.py:113
  3.0 7.7 %collective-permute-start.1 = (bf16[16,4096]{1,0:T(8,128)(2,1)}, bf16[16,4096]{1,0:T(8,128)(2,1)S(1)}, u32[]{:S(2)}, u32[]{:S(2)}) collective-permute-start(bf16[16,4096]{1,0:T(8,128)(2,1)} %refs_0_.5), channel_id=1, source_target_pairs={{0,4},{2,6},{4,0},{6,2},{8,12},{10,14},{12,8},{14,10},{1,5},{3,7},... | collective-permute-start | bytes 393224 | tf_op jit(solution)/shard_map/ppermute | solution.py:113
  4.5 8.7 %collective-permute-start.7 = (bf16[16,4096]{1,0:T(8,128)(2,1)}, bf16[16,4096]{1,0:T(8,128)(2,1)S(1)}, u32[]{:S(2)}, u32[]{:S(2)}) collective-permute-start(bf16[16,4096]{1,0:T(8,128)(2,1)} %refs_0_.5), channel_id=1, source_target_pairs={{0,8},{2,10},{4,12},{6,14},{8,0},{10,2},{12,4},{14,6},{1,9},{3,11}... | collective-permute-start | bytes 393224 | tf_op jit(solution)/shard_map/ppermute | solution.py:113
  10.6 8.2 %copy-start = (bf16[512,4096]{1,0:T(8,128)(2,1)S(1)}, bf16[512,4096]{1,0:T(8,128)(2,1)}, u32[]{:S(2)}) copy-start(bf16[512,4096]{1,0:T(8,128)(2,1)} %weight_ref.3) | copy-start | bytes 12582916
  11.5 6.0 %collective-permute-start.2 = (f32[48,512]{1,0:T(8,128)S(1)}, f32[48,512]{1,0:T(8,128)S(1)}, u32[]{:S(2)}, u32[]{:S(2)}) collective-permute-start(f32[48,512]{1,0:T(8,128)S(1)} %project.4.gate_ref), channel_id=1, source_target_pairs={{0,1},{1,0},{2,3},{3,2},{4,5},{5,4},{6,7},{7,6},{8,9},{9,8},{10,11... | collective-permute-start | bytes 294920 | tf_op jit(solution)/shard_map/ppermute | solution.py:116
  11.5 9.2 %collective-permute-start.6 = (bf16[16,4096]{1,0:T(8,128)(2,1)S(1)}, bf16[16,4096]{1,0:T(8,128)(2,1)S(1)}, u32[]{:S(2)}, u32[]{:S(2)}) collective-permute-start(bf16[16,4096]{1,0:T(8,128)(2,1)S(1)} %collective-permute-done.1.refs_2_), channel_id=1, source_target_pairs={{0,2},{2,0},{4,6},{6,4},{8,10},{10,8},{12,14},{14,12},{1,3},{3,1},... | collective-permute-start | bytes 393224 | tf_op jit(solution)/shard_map/ppermute | solution.py:113
  13.2 7.9 %collective-permute-start.8 = (bf16[16,4096]{1,0:T(8,128)(2,1)S(1)}, bf16[16,4096]{1,0:T(8,128)(2,1)S(1)}, u32[]{:S(2)}, u32[]{:S(2)}) collective-permute-start(bf16[16,4096]{1,0:T(8,128)(2,1)S(1)} %collective-permute-done.7.refs_1_), channel_id=1, source_target_pairs={{0,6},{2,4},{4,2},{6,0},{8,14},{10,12},{12,10},{14,8},{1,7},{3,5},... | collective-permute-start | bytes 393224 | tf_op jit(solution)/shard_map/ppermute | solution.py:113
  13.5 8.0 %collective-permute-start.9 = (bf16[16,4096]{1,0:T(8,128)(2,1)S(1)}, bf16[16,4096]{1,0:T(8,128)(2,1)S(1)}, u32[]{:S(2)}, u32[]{:S(2)}) collective-permute-start(bf16[16,4096]{1,0:T(8,128)(2,1)S(1)} %collective-permute-done.7.refs_1_), channel_id=1, source_target_pairs={{0,4},{2,6},{4,0},{6,2},{8,12},{10,14},{12,8},{14,10},{1,5},{3,7},... | collective-permute-start | bytes 393224 | tf_op jit(solution)/shard_map/ppermute | solution.py:113
  15.2 8.2 %collective-permute-start.10 = (bf16[16,4096]{1,0:T(8,128)(2,1)S(1)}, bf16[16,4096]{1,0:T(8,128)(2,1)S(1)}, u32[]{:S(2)}, u32[]{:S(2)}) collective-permute-start(bf16[16,4096]{1,0:T(8,128)(2,1)S(1)} %collective-permute-done.7.refs_1_), channel_id=1, source_target_pairs={{0,2},{2,0},{4,6},{6,4},{8,10},{10,8},{12,14},{14,12},{1,3},{3,1},... | collective-permute-start | bytes 393224 | tf_op jit(solution)/shard_map/ppermute | solution.py:113
  17.5 1.4 %collective-permute-start.3 = (f32[48,512]{1,0:T(8,128)S(1)}, f32[48,512]{1,0:T(8,128)S(1)}, u32[]{:S(2)}, u32[]{:S(2)}) collective-permute-start(f32[48,512]{1,0:T(8,128)S(1)} %project.5.up_ref), channel_id=1, source_target_pairs={{0,1},{1,0},{2,3},{3,2},{4,5},{5,4},{6,7},{7,6},{8,9},{9,8},{10,11... | collective-permute-start | bytes 294920 | tf_op jit(solution)/shard_map/ppermute | solution.py:116
  19.7 6.1 %collective-permute-start.4 = (bf16[16,4096]{1,0:T(8,128)(2,1)S(1)}, bf16[16,4096]{1,0:T(8,128)(2,1)S(1)}, u32[]{:S(2)}, u32[]{:S(2)}) collective-permute-start(bf16[16,4096]{1,0:T(8,128)(2,1)S(1)} %get-tuple-element.30), channel_id=1, source_target_pairs={{0,2},{2,0},{4,6},{6,4},{8,10},{10,8},{12,14},{14,12},{1,3},{3,1},... | collective-permute-start | bytes 393224 | tf_op jit(solution)/shard_map/ppermute | solution.py:113
  20.7 5.2 %collective-permute-start.5 = (bf16[16,4096]{1,0:T(8,128)(2,1)S(1)}, bf16[16,4096]{1,0:T(8,128)(2,1)S(1)}, u32[]{:S(2)}, u32[]{:S(2)}) collective-permute-start(bf16[16,4096]{1,0:T(8,128)(2,1)S(1)} %get-tuple-element.31), channel_id=1, source_target_pairs={{0,4},{2,6},{4,0},{6,2},{8,12},{10,14},{12,8},{14,10},{1,5},{3,7},... | collective-permute-start | bytes 393224 | tf_op jit(solution)/shard_map/ppermute | solution.py:113
  24.3 1.6 %collective-permute-start.11 = (f32[80,512]{1,0:T(8,128)S(1)}, f32[80,512]{1,0:T(8,128)S(1)}, u32[]{:S(2)}, u32[]{:S(2)}) collective-permute-start(f32[80,512]{1,0:T(8,128)S(1)} %project.6.gate_ref), channel_id=1, source_target_pairs={{0,1},{1,0},{2,3},{3,2},{4,5},{5,4},{6,7},{7,6},{8,9},{9,8},{10,11... | collective-permute-start | bytes 491528 | tf_op jit(solution)/shard_map/ppermute | solution.py:116
  25.2 1.6 %collective-permute-start.12 = (f32[80,512]{1,0:T(8,128)S(1)}, f32[80,512]{1,0:T(8,128)S(1)}, u32[]{:S(2)}, u32[]{:S(2)}) collective-permute-start(f32[80,512]{1,0:T(8,128)S(1)} %project.7.up_ref), channel_id=1, source_target_pairs={{0,1},{1,0},{2,3},{3,2},{4,5},{5,4},{6,7},{7,6},{8,9},{9,8},{10,11... | collective-permute-start | bytes 491528 | tf_op jit(solution)/shard_map/ppermute | solution.py:116
  27.6 6.4 %collective-permute-start.14 = (bf16[16,4096]{1,0:T(8,128)(2,1)S(1)}, bf16[16,4096]{1,0:T(8,128)(2,1)S(1)}, u32[]{:S(2)}, u32[]{:S(2)}) collective-permute-start(bf16[16,4096]{1,0:T(8,128)(2,1)S(1)} %get-tuple-element.36), channel_id=1, source_target_pairs={{0,4},{2,6},{4,0},{6,2},{8,12},{10,14},{12,8},{14,10},{1,5},{3,7},... | collective-permute-start | bytes 393224 | tf_op jit(solution)/shard_map/ppermute | solution.py:113
  28.2 8.7 %collective-permute-start.15 = (bf16[16,4096]{1,0:T(8,128)(2,1)S(1)}, bf16[16,4096]{1,0:T(8,128)(2,1)S(1)}, u32[]{:S(2)}, u32[]{:S(2)}) collective-permute-start(bf16[16,4096]{1,0:T(8,128)(2,1)S(1)} %get-tuple-element.37), channel_id=1, source_target_pairs={{0,6},{2,4},{4,2},{6,0},{8,14},{10,12},{12,10},{14,8},{1,7},{3,5},... | collective-permute-start | bytes 393224 | tf_op jit(solution)/shard_map/ppermute | solution.py:113
  29.7 10.8 %collective-permute-start.16 = (bf16[16,4096]{1,0:T(8,128)(2,1)S(1)}, bf16[16,4096]{1,0:T(8,128)(2,1)S(1)}, u32[]{:S(2)}, u32[]{:S(2)}) collective-permute-start(bf16[16,4096]{1,0:T(8,128)(2,1)S(1)} %get-tuple-element.38), channel_id=1, source_target_pairs={{0,2},{2,0},{4,6},{6,4},{8,10},{10,8},{12,14},{14,12},{1,3},{3,1},... | collective-permute-start | bytes 393224 | tf_op jit(solution)/shard_map/ppermute | solution.py:113
  31.2 11.0 %collective-permute-start.13 = (bf16[16,4096]{1,0:T(8,128)(2,1)S(1)}, bf16[16,4096]{1,0:T(8,128)(2,1)S(1)}, u32[]{:S(2)}, u32[]{:S(2)}) collective-permute-start(bf16[16,4096]{1,0:T(8,128)(2,1)S(1)} %get-tuple-element.34), channel_id=1, source_target_pairs={{0,6},{2,4},{4,2},{6,0},{8,14},{10,12},{12,10},{14,8},{1,7},{3,5},... | collective-permute-start | bytes 393224 | tf_op jit(solution)/shard_map/ppermute | solution.py:113
  40.6 8.2 %collective-permute-start.17 = (bf16[16,4096]{1,0:T(8,128)(2,1)S(1)}, bf16[16,4096]{1,0:T(8,128)(2,1)S(1)}, u32[]{:S(2)}, u32[]{:S(2)}) collective-permute-start(bf16[16,4096]{1,0:T(8,128)(2,1)S(1)} %add.4), channel_id=1, source_target_pairs={{0,8},{2,10},{4,12},{6,14},{8,0},{10,2},{12,4},{14,6},{1,9},{3,11}... | collective-permute-start | bytes 393224 | tf_op jit(solution)/shard_map/ppermute | solution.py:113

commit v12 on v11

--- a/solution.py
+++ b/solution.py
@@ -142,17 +142,19 @@
             return dict(zip(order, outs))
 
         stay = [0] + fars
-        part = partials([0, 1, 2], gate_held, up_held, 100000000)
+        part = partials([0, 1, 2], gate_held, up_held, 2000000000)
         gate_held, up_held, part[1] = lax.optimization_barrier((gate_held, up_held, part[1]))
-        total = add(part[0], [swap(part[1], 1), swap(part[2], 2)], F32, 1000000000)
+        total = add(part[0], [swap(part[1], 1), swap(part[2], 2)], F32, 3000000000)
         late = [3] + [far + near for far in fars for near in (0, 3, 2, 1)]
-        part.update(partials(late, gate_held, up_held, 400000000, [total]))
+        part.update(partials(late, gate_held, up_held, 400000000))
         sums = []
         for far in fars:
             quad = [swap(part[far + near], near) for near in (2, 3, 1)]
-            sums.append(add(part[far], quad, BF16))
+            sums.append(add(part[far], quad, BF16, after=[total]))
         arrived = [swap(value, far) for value, far in zip(sums, fars)]
-        return add(total, [swap(part[3], 3)] + arrived, BF16)
+        part[3], sums[-1] = lax.optimization_barrier((part[3], sums[-1]))
+        total = add(total, arrived, F32, 3000000000)
+        return add(total, [swap(part[3], 3)], BF16)
 
     return local
 

time: 49.7 us -> 46.8 us (0.942)
  waiting for transfers between devices: 21.6 us -> 16.2 us
  starting transfers between devices: 18.5 us -> 21 us
    ppermute x14, waiting for transfers between devices: 19.5 us -> 14.9 us  [swap(): return lax.ppermute(value, 'wide', [(i, i ^ bits) for i in range(wide)])]
    ppermute x14, starting transfers between devices: 17.8 us -> 20.3 us  [swap(): return lax.ppermute(value, 'wide', [(i, i ^ bits) for i in range(wide)])]
    ppermute x4, waiting for transfers between devices: 2.19 us -> 1.31 us  [across_cores(): lax.ppermute(value, 'narrow', [(i, (i + 1) % narrow) for i in range(narro...]
    pallas_call x9 -> x10, Pallas kernels: 5.77 us -> 5.78 us  [call(): pl.pallas_call(kernel, in_specs=[pl.BlockSpec(memory_space=pltpu.VMEM)] *...]
  transfers between devices with their start and end apart: 18 -> 18, of which waited for: 11 -> 10; matrix products, arithmetic and copies ran while one was open for 0% -> 0% of each run, Pallas kernels for 16% -> 16%
where the time goes in v12:
time: 46.8 us; the launch traced here: 46.6 us
  starting transfers between devices  21 us (45%)
  waiting for transfers between devices  16.2 us (35%)
  Pallas kernels  9.25 us (20%)
    ppermute x14, starting transfers between devices, swap(): return lax.ppermute(value, 'wide', [(i, i ^ bits) for i in range(wide)])  20.3 us
    ppermute x14, waiting for transfers between devices, swap(): return lax.ppermute(value, 'wide', [(i, i ^ bits) for i in range(wide)])  14.9 us
    pallas_call x10, Pallas kernels, call(): pl.pallas_call(kernel, in_specs=[pl.BlockSpec(memory_space=pltpu.VMEM)] *...  5.78 us
    pallas_call x1, Pallas kernels, fetch(): pl.pallas_call(functools.partial(fetch_kernel, pieces, count), in_specs=[...  3.47 us
    ppermute x4, waiting for transfers between devices, across_cores(): lax.ppermute(value, 'narrow', [(i, (i + 1) % narrow) for i in range(narro...  1.31 us
  transfers between devices with their start and end apart: 18, of which 10 were waited for; matrix products, arithmetic and copies ran while one was open for 0% of the time, Pallas kernels for 16%

profile of v12, /device:TPU:0, one launch (start us, length us, event | category | flops | bytes accessed | tf_op | source)
XLA Modules:
  0.0 46.6 jit_solution(14746053000091835466)
XLA Ops:
  0.0 3.0 %collective-permute-start = (bf16[16,4096]{1,0:T(8,128)(2,1)}, bf16[16,4096]{1,0:T(8,128)(2,1)S(1)}, u32[]{:S(2)}, u32[]{:S(2)}) collective-permute-start(bf16[16,4096]{1,0:T(8,128)(2,1)} %refs_0_.5), channel_id=1, source_target_pairs={{0,2},{2,0},{4,6},{6,4},{8,10},{10,8},{12,14},{14,12},{1,3},{3,1},... | collective-permute-start | bytes 393224 | tf_op jit(solution)/shard_map/ppermute | solution.py:113
  3.0 1.6 %collective-permute-start.1 = (bf16[16,4096]{1,0:T(8,128)(2,1)}, bf16[16,4096]{1,0:T(8,128)(2,1)S(1)}, u32[]{:S(2)}, u32[]{:S(2)}) collective-permute-start(bf16[16,4096]{1,0:T(8,128)(2,1)} %refs_0_.5), channel_id=1, source_target_pairs={{0,4},{2,6},{4,0},{6,2},{8,12},{10,14},{12,8},{14,10},{1,5},{3,7},... | collective-permute-start | bytes 393224 | tf_op jit(solution)/shard_map/ppermute | solution.py:113
  4.5 2.6 %collective-permute-start.7 = (bf16[16,4096]{1,0:T(8,128)(2,1)}, bf16[16,4096]{1,0:T(8,128)(2,1)S(1)}, u32[]{:S(2)}, u32[]{:S(2)}) collective-permute-start(bf16[16,4096]{1,0:T(8,128)(2,1)} %refs_0_.5), channel_id=1, source_target_pairs={{0,8},{2,10},{4,12},{6,14},{8,0},{10,2},{12,4},{14,6},{1,9},{3,11}... | collective-permute-start | bytes 393224 | tf_op jit(solution)/shard_map/ppermute | solution.py:113
  7.1 3.5 %fetch.1 = (bf16[4096,512]{1,0:T(8,128)(2,1)S(1)}, bf16[4096,512]{1,0:T(8,128)(2,1)S(1)}) custom-call(bf16[4096,512]{1,0:T(8,128)(2,1)} %refs_0_.3, bf16[4096,512]{1,0:T(8,128)(2,1)} %refs_1_.1), custom_call_target="tpu_custom_call" | custom-call | flops 4000000000 | tf_op jit(solution)/shard_map/fetch/pallas_call | solution.py:43
  10.6 0.0 collective-permute-done.refs_1_
  10.6 0.0 collective-permute-done.1.refs_2_
  10.6 0.6 %collective-permute-start.6 = (bf16[16,4096]{1,0:T(8,128)(2,1)S(1)}, bf16[16,4096]{1,0:T(8,128)(2,1)S(1)}, u32[]{:S(2)}, u32[]{:S(2)}) collective-permute-start(bf16[16,4096]{1,0:T(8,128)(2,1)S(1)} %collective-permute-done.1.refs_2_), channel_id=1, source_target_pairs={{0,2},{2,0},{4,6},{6,4},{8,10},{10,8},{12,14},{14,12},{1,3},{3,1},... | collective-permute-start | bytes 393224 | tf_op jit(solution)/shard_map/ppermute | solution.py:113
  11.2 0.0 copy-done.1
  11.2 0.8 %project.4.gate_ref = f32[48,512]{1,0:T(8,128)S(1)} custom-call(bf16[16,4096]{1,0:T(8,128)(2,1)S(1)} %copy-done.1, bf16[16,4096]{1,0:T(8,128)(2,1)S(1)} %collective-permute-done.refs_1_, bf16[16,4096]{1,0:T(8,128)(2,1)S(1)} %collective-permute-done.1.refs_2_, bf16[4096,512]{1,0:T(8,128)(2,1)S(1)} %get-tuple-element.33.refs_3_.refs_5_), custom_call_target="tpu_custom_call" | custom-call | flops 2000000000 | tf_op jit(solution)/shard_map/project/pallas_call | solution.py:15
  12.0 0.0 copy-start
  12.0 0.1 collective-permute-start.2
  12.1 1.1 %collective-permute-done.7.refs_1_ = bf16[16,4096]{1,0:T(8,128)(2,1)S(1)} collective-permute-done((bf16[16,4096]{1,0:T(8,128)(2,1)}, bf16[16,4096]{1,0:T(8,128)(2,1)S(1)}, u32[]{:S(2)}, u32[]{:S(2)}) %collective-permute-start.7) | collective-permute-done | bytes 131104 | tf_op jit(solution)/shard_map/ppermute | solution.py:113
  13.2 0.4 collective-permute-start.8
  13.6 1.6 %collective-permute-start.9 = (bf16[16,4096]{1,0:T(8,128)(2,1)S(1)}, bf16[16,4096]{1,0:T(8,128)(2,1)S(1)}, u32[]{:S(2)}, u32[]{:S(2)}) collective-permute-start(bf16[16,4096]{1,0:T(8,128)(2,1)S(1)} %collective-permute-done.7.refs_1_), channel_id=1, source_target_pairs={{0,4},{2,6},{4,0},{6,2},{8,12},{10,14},{12,8},{14,10},{1,5},{3,7},... | collective-permute-start | bytes 393224 | tf_op jit(solution)/shard_map/ppermute | solution.py:113
  15.2 1.5 %collective-permute-start.10 = (bf16[16,4096]{1,0:T(8,128)(2,1)S(1)}, bf16[16,4096]{1,0:T(8,128)(2,1)S(1)}, u32[]{:S(2)}, u32[]{:S(2)}) collective-permute-start(bf16[16,4096]{1,0:T(8,128)(2,1)S(1)} %collective-permute-done.7.refs_1_), channel_id=1, source_target_pairs={{0,2},{2,0},{4,6},{6,4},{8,10},{10,8},{12,14},{14,12},{1,3},{3,1},... | collective-permute-start | bytes 393224 | tf_op jit(solution)/shard_map/ppermute | solution.py:113
  16.7 0.8 %project.5.up_ref = f32[48,512]{1,0:T(8,128)S(1)} custom-call(bf16[16,4096]{1,0:T(8,128)(2,1)S(1)} %copy-done.1, bf16[16,4096]{1,0:T(8,128)(2,1)S(1)} %collective-permute-done.refs_1_, bf16[16,4096]{1,0:T(8,128)(2,1)S(1)} %collective-permute-done.1.refs_2_, bf16[4096,512]{1,0:T(8,128)(2,1)S(1)} %get-tuple-element.34.refs_3_.refs_5_), custom_call_target="tpu_custom_call" | custom-call | flops 2000000000 | tf_op jit(solution)/shard_map/project/pallas_call | solution.py:15
  17.5 0.0 collective-permute-done.2.gate_other_ref
  17.5 0.1 collective-permute-start.3
  17.6 1.3 %collective-permute-done.3.up_other_ref = f32[48,512]{1,0:T(8,128)S(1)} collective-permute-done((f32[48,512]{1,0:T(8,128)S(1)}, f32[48,512]{1,0:T(8,128)S(1)}, u32[]{:S(2)}, u32[]{:S(2)}) %collective-permute-start.3) | collective-permute-done | bytes 98336 | tf_op jit(solution)/shard_map/ppermute | solution.py:116
  18.9 0.0 copy-done
  18.9 0.8 %down.2 = (f32[16,4096]{1,0:T(8,128)S(1)}, bf16[16,4096]{1,0:T(8,128)(2,1)S(1)}, bf16[16,4096]{1,0:T(8,128)(2,1)S(1)}) custom-call(f32[48,512]{1,0:T(8,128)S(1)} %project.4.gate_ref, f32[48,512]{1,0:T(8,128)S(1)} %collective-permute-done.2.gate_other_ref, f32[48,512]{1,0:T(8,128)S(1)} %project.5.up_ref, f32[48,512]{1,0:T(8,128)S(1)} %collective-permute-done.3.up_other_ref, ...), custom_call_target="tpu_custom_call" | custom-call | flops 201326592 | tf_op jit(solution)/shard_map/down/pallas_call | solution.py:15
  19.7 0.0 collective-permute-done.6.refs_0_
  19.8 0.7 %collective-permute-done.8.refs_2_ = bf16[16,4096]{1,0:T(8,128)(2,1)S(1)} collective-permute-done((bf16[16,4096]{1,0:T(8,128)(2,1)S(1)}, bf16[16,4096]{1,0:T(8,128)(2,1)S(1)}, u32[]{:S(2)}, u32[]{:S(2)}) %collective-permute-start.8) | collective-permute-done | bytes 131104 | tf_op jit(solution)/shard_map/ppermute | solution.py:113
  20.4 1.4 %collective-permute-done.9.refs_3_ = bf16[16,4096]{1,0:T(8,128)(2,1)S(1)} collective-permute-done((bf16[16,4096]{1,0:T(8,128)(2,1)S(1)}, bf16[16,4096]{1,0:T(8,128)(2,1)S(1)}, u32[]{:S(2)}, u32[]{:S(2)}) %collective-permute-start.9) | collective-permute-done | bytes 131104 | tf_op jit(solution)/shard_map/ppermute | solution.py:113
  21.8 0.0 collective-permute-done.10.refs_4_
  21.9 0.8 %project.6.gate_ref = f32[80,512]{1,0:T(8,128)S(1)} custom-call(bf16[16,4096]{1,0:T(8,128)(2,1)S(1)} %collective-permute-done.6.refs_0_, bf16[16,4096]{1,0:T(8,128)(2,1)S(1)} %collective-permute-done.7.refs_1_, bf16[16,4096]{1,0:T(8,128)(2,1)S(1)} %collective-permute-done.8.refs_2_, bf16[16,4096]{1,0:T(8,128)(2,1)S(1)} %collective-permute-done.9.refs_3_, ...), custom_call_target="tpu_custom_call" | custom-call | flops 400000000 | tf_op jit(solution)/shard_map/project/pallas_call | solution.py:15
  22.7 0.1 collective-permute-start.11
  22.8 0.8 %project.7.up_ref = f32[80,512]{1,0:T(8,128)S(1)} custom-call(bf16[16,4096]{1,0:T(8,128)(2,1)S(1)} %collective-permute-done.6.refs_0_, bf16[16,4096]{1,0:T(8,128)(2,1)S(1)} %collective-permute-done.7.refs_1_, bf16[16,4096]{1,0:T(8,128)(2,1)S(1)} %collective-permute-done.8.refs_2_, bf16[16,4096]{1,0:T(8,128)(2,1)S(1)} %collective-permute-done.9.refs_3_, ...), custom_call_target="tpu_custom_call" | custom-call | flops 400000000 | tf_op jit(solution)/shard_map/project/pallas_call | solution.py:15
  23.6 0.6 %collective-permute-start.12 = (f32[80,512]{1,0:T(8,128)S(1)}, f32[80,512]{1,0:T(8,128)S(1)}, u32[]{:S(2)}, u32[]{:S(2)}) collective-permute-start(f32[80,512]{1,0:T(8,128)S(1)} %project.7.up_ref), channel_id=1, source_target_pairs={{0,1},{1,0},{2,3},{3,2},{4,5},{5,4},{6,7},{7,6},{8,9},{9,8},{10,11... | collective-permute-start | bytes 491528 | tf_op jit(solution)/shard_map/ppermute | solution.py:116
  24.2 1.4 %collective-permute-start.4 = (bf16[16,4096]{1,0:T(8,128)(2,1)S(1)}, bf16[16,4096]{1,0:T(8,128)(2,1)S(1)}, u32[]{:S(2)}, u32[]{:S(2)}) collective-permute-start(bf16[16,4096]{1,0:T(8,128)(2,1)S(1)} %get-tuple-element.31), channel_id=1, source_target_pairs={{0,2},{2,0},{4,6},{6,4},{8,10},{10,8},{12,14},{14,12},{1,3},{3,1},... | collective-permute-start | bytes 393224 | tf_op jit(solution)/shard_map/ppermute | solution.py:113
  25.6 0.4 collective-permute-start.5
  26.0 0.0 collective-permute-done.11.gate_other_ref
  26.0 0.0 collective-permute-done.12.up_other_ref
  26.0 0.8 %down.3 = (bf16[16,4096]{1,0:T(8,128)(2,1)S(1)}, f32[16,4096]{1,0:T(8,128)S(1)}, bf16[16,4096]{1,0:T(8,128)(2,1)S(1)}, bf16[16,4096]{1,0:T(8,128)(2,1)S(1)}, bf16[16,4096]{1,0:T(8,128)(2,1)S(1)}) custom-call(f32[80,512]{1,0:T(8,128)S(1)} %project.6.gate_ref, f32[80,512]{1,0:T(8,128)S(1)} %collective-permute-done.11.gate_other_ref, ...), custom_call_target="tpu_custom_call" | custom-call | flops 335544320 | tf_op jit(solution)/shard_map/down/pallas_call | solution.py:15
  26.9 1.6 %collective-permute-start.13 = (bf16[16,4096]{1,0:T(8,128)(2,1)S(1)}, bf16[16,4096]{1,0:T(8,128)(2,1)S(1)}, u32[]{:S(2)}, u32[]{:S(2)}) collective-permute-start(bf16[16,4096]{1,0:T(8,128)(2,1)S(1)} %get-tuple-element.36), channel_id=1, source_target_pairs={{0,4},{2,6},{4,0},{6,2},{8,12},{10,14},{12,8},{14,10},{1,5},{3,7},... | collective-permute-start | bytes 393224 | tf_op jit(solution)/shard_map/ppermute | solution.py:113
  28.5 0.5 %collective-permute-start.14 = (bf16[16,4096]{1,0:T(8,128)(2,1)S(1)}, bf16[16,4096]{1,0:T(8,128)(2,1)S(1)}, u32[]{:S(2)}, u32[]{:S(2)}) collective-permute-start(bf16[16,4096]{1,0:T(8,128)(2,1)S(1)} %get-tuple-element.37), channel_id=1, source_target_pairs={{0,6},{2,4},{4,2},{6,0},{8,14},{10,12},{12,10},{14,8},{1,7},{3,5},... | collective-permute-start | bytes 393224 | tf_op jit(solution)/shard_map/ppermute | solution.py:113
  29.0 1.4 %collective-permute-start.15 = (bf16[16,4096]{1,0:T(8,128)(2,1)S(1)}, bf16[16,4096]{1,0:T(8,128)(2,1)S(1)}, u32[]{:S(2)}, u32[]{:S(2)}) collective-permute-start(bf16[16,4096]{1,0:T(8,128)(2,1)S(1)} %get-tuple-element.38), channel_id=1, source_target_pairs={{0,2},{2,0},{4,6},{6,4},{8,10},{10,8},{12,14},{14,12},{1,3},{3,1},... | collective-permute-start | bytes 393224 | tf_op jit(solution)/shard_map/ppermute | solution.py:113
  30.4 0.0 collective-permute-done.4.refs_0_
  30.4 1.5 %collective-permute-done.5.refs_1_ = bf16[16,4096]{1,0:T(8,128)(2,1)S(1)} collective-permute-done((bf16[16,4096]{1,0:T(8,128)(2,1)S(1)}, bf16[16,4096]{1,0:T(8,128)(2,1)S(1)}, u32[]{:S(2)}, u32[]{:S(2)}) %collective-permute-start.5) | collective-permute-done | bytes 131104 | tf_op jit(solution)/shard_map/ppermute | solution.py:113
  32.0 2.8 %collective-permute-done.13.refs_0_ = bf16[16,4096]{1,0:T(8,128)(2,1)S(1)} collective-permute-done((bf16[16,4096]{1,0:T(8,128)(2,1)S(1)}, bf16[16,4096]{1,0:T(8,128)(2,1)S(1)}, u32[]{:S(2)}, u32[]{:S(2)}) %collective-permute-start.13) | collective-permute-done | bytes 131104 | tf_op jit(solution)/shard_map/ppermute | solution.py:113
  34.8 1.8 %collective-permute-done.14.refs_1_ = bf16[16,4096]{1,0:T(8,128)(2,1)S(1)} collective-permute-done((bf16[16,4096]{1,0:T(8,128)(2,1)S(1)}, bf16[16,4096]{1,0:T(8,128)(2,1)S(1)}, u32[]{:S(2)}, u32[]{:S(2)}) %collective-permute-start.14) | collective-permute-done | bytes 131104 | tf_op jit(solution)/shard_map/ppermute | solution.py:113
  36.6 0.4 collective-permute-done.15.refs_2_
  37.0 0.1 add.5
  37.1 1.9 %collective-permute-start.16 = (bf16[16,4096]{1,0:T(8,128)(2,1)S(1)}, bf16[16,4096]{1,0:T(8,128)(2,1)S(1)}, u32[]{:S(2)}, u32[]{:S(2)}) collective-permute-start(bf16[16,4096]{1,0:T(8,128)(2,1)S(1)} %add.5), channel_id=1, source_target_pairs={{0,8},{2,10},{4,12},{6,14},{8,0},{10,2},{12,4},{14,6},{1,9},{3,11}... | collective-permute-start | bytes 393224 | tf_op jit(solution)/shard_map/ppermute | solution.py:113
  39.0 1.8 %collective-permute-start.17 = (bf16[16,4096]{1,0:T(8,128)(2,1)S(1)}, bf16[16,4096]{1,0:T(8,128)(2,1)S(1)}, u32[]{:S(2)}, u32[]{:S(2)}) collective-permute-start(bf16[16,4096]{1,0:T(8,128)(2,1)S(1)} %get-tuple-element.40), channel_id=1, source_target_pairs={{0,6},{2,4},{4,2},{6,0},{8,14},{10,12},{12,10},{14,8},{1,7},{3,5},... | collective-permute-start | bytes 393224 | tf_op jit(solution)/shard_map/ppermute | solution.py:113
  40.8 4.1 %collective-permute-done.16.refs_0_ = bf16[16,4096]{1,0:T(8,128)(2,1)S(1)} collective-permute-done((bf16[16,4096]{1,0:T(8,128)(2,1)S(1)}, bf16[16,4096]{1,0:T(8,128)(2,1)S(1)}, u32[]{:S(2)}, u32[]{:S(2)}) %collective-permute-start.16) | collective-permute-done | bytes 131104 | tf_op jit(solution)/shard_map/ppermute | solution.py:113
  44.9 1.0 %collective-permute-done.17.refs_0_ = bf16[16,4096]{1,0:T(8,128)(2,1)S(1)} collective-permute-done((bf16[16,4096]{1,0:T(8,128)(2,1)S(1)}, bf16[16,4096]{1,0:T(8,128)(2,1)S(1)}, u32[]{:S(2)}, u32[]{:S(2)}) %collective-permute-start.17) | collective-permute-done | bytes 131104 | tf_op jit(solution)/shard_map/ppermute | solution.py:113
  46.0 0.7 %add.7 = bf16[16,4096]{1,0:T(8,128)(2,1)} custom-call(f32[16,4096]{1,0:T(8,128)S(1)} %add.6.own_ref, bf16[16,4096]{1,0:T(8,128)(2,1)S(1)} %collective-permute-done.17.refs_0_), custom_call_target="tpu_custom_call" | custom-call | flops 1000000 | tf_op jit(solution)/shard_map/add/pallas_call | solution.py:15
  (3 shorter events, 0.1 us)
Async XLA Ops:
  0.0 11.2 %copy-start.1 = (bf16[16,4096]{1,0:T(8,128)(2,1)S(1)}, bf16[16,4096]{1,0:T(8,128)(2,1)}, u32[]{:S(2)}) copy-start(bf16[16,4096]{1,0:T(8,128)(2,1)} %refs_0_.5) | copy-start | bytes 393220
  0.0 10.6 %collective-permute-start = (bf16[16,4096]{1,0:T(8,128)(2,1)}, bf16[16,4096]{1,0:T(8,128)(2,1)S(1)}, u32[]{:S(2)}, u32[]{:S(2)}) collective-permute-start(bf16[16,4096]{1,0:T(8,128)(2,1)} %refs_0_.5), channel_id=1, source_target_pairs={{0,2},{2,0},{4,6},{6,4},{8,10},{10,8},{12,14},{14,12},{1,3},{3,1},... | collective-permute-start | bytes 393224 | tf_op jit(solution)/shard_map/ppermute | solution.py:113
  3.0 7.7 %collective-permute-start.1 = (bf16[16,4096]{1,0:T(8,128)(2,1)}, bf16[16,4096]{1,0:T(8,128)(2,1)S(1)}, u32[]{:S(2)}, u32[]{:S(2)}) collective-permute-start(bf16[16,4096]{1,0:T(8,128)(2,1)} %refs_0_.5), channel_id=1, source_target_pairs={{0,4},{2,6},{4,0},{6,2},{8,12},{10,14},{12,8},{14,10},{1,5},{3,7},... | collective-permute-start | bytes 393224 | tf_op jit(solution)/shard_map/ppermute | solution.py:113
  4.5 8.7 %collective-permute-start.7 = (bf16[16,4096]{1,0:T(8,128)(2,1)}, bf16[16,4096]{1,0:T(8,128)(2,1)S(1)}, u32[]{:S(2)}, u32[]{:S(2)}) collective-permute-start(bf16[16,4096]{1,0:T(8,128)(2,1)} %refs_0_.5), channel_id=1, source_target_pairs={{0,8},{2,10},{4,12},{6,14},{8,0},{10,2},{12,4},{14,6},{1,9},{3,11}... | collective-permute-start | bytes 393224 | tf_op jit(solution)/shard_map/ppermute | solution.py:113
  10.6 9.1 %collective-permute-start.6 = (bf16[16,4096]{1,0:T(8,128)(2,1)S(1)}, bf16[16,4096]{1,0:T(8,128)(2,1)S(1)}, u32[]{:S(2)}, u32[]{:S(2)}) collective-permute-start(bf16[16,4096]{1,0:T(8,128)(2,1)S(1)} %collective-permute-done.1.refs_2_), channel_id=1, source_target_pairs={{0,2},{2,0},{4,6},{6,4},{8,10},{10,8},{12,14},{14,12},{1,3},{3,1},... | collective-permute-start | bytes 393224 | tf_op jit(solution)/shard_map/ppermute | solution.py:113
  12.0 6.9 %copy-start = (bf16[512,4096]{1,0:T(8,128)(2,1)S(1)}, bf16[512,4096]{1,0:T(8,128)(2,1)}, u32[]{:S(2)}) copy-start(bf16[512,4096]{1,0:T(8,128)(2,1)} %weight_ref.3) | copy-start | bytes 12582916
  12.0 5.5 %collective-permute-start.2 = (f32[48,512]{1,0:T(8,128)S(1)}, f32[48,512]{1,0:T(8,128)S(1)}, u32[]{:S(2)}, u32[]{:S(2)}) collective-permute-start(f32[48,512]{1,0:T(8,128)S(1)} %project.4.gate_ref), channel_id=1, source_target_pairs={{0,1},{1,0},{2,3},{3,2},{4,5},{5,4},{6,7},{7,6},{8,9},{9,8},{10,11... | collective-permute-start | bytes 294920 | tf_op jit(solution)/shard_map/ppermute | solution.py:116
  13.2 7.2 %collective-permute-start.8 = (bf16[16,4096]{1,0:T(8,128)(2,1)S(1)}, bf16[16,4096]{1,0:T(8,128)(2,1)S(1)}, u32[]{:S(2)}, u32[]{:S(2)}) collective-permute-start(bf16[16,4096]{1,0:T(8,128)(2,1)S(1)} %collective-permute-done.7.refs_1_), channel_id=1, source_target_pairs={{0,6},{2,4},{4,2},{6,0},{8,14},{10,12},{12,10},{14,8},{1,7},{3,5},... | collective-permute-start | bytes 393224 | tf_op jit(solution)/shard_map/ppermute | solution.py:113
  13.6 8.2 %collective-permute-start.9 = (bf16[16,4096]{1,0:T(8,128)(2,1)S(1)}, bf16[16,4096]{1,0:T(8,128)(2,1)S(1)}, u32[]{:S(2)}, u32[]{:S(2)}) collective-permute-start(bf16[16,4096]{1,0:T(8,128)(2,1)S(1)} %collective-permute-done.7.refs_1_), channel_id=1, source_target_pairs={{0,4},{2,6},{4,0},{6,2},{8,12},{10,14},{12,8},{14,10},{1,5},{3,7},... | collective-permute-start | bytes 393224 | tf_op jit(solution)/shard_map/ppermute | solution.py:113
  15.2 6.7 %collective-permute-start.10 = (bf16[16,4096]{1,0:T(8,128)(2,1)S(1)}, bf16[16,4096]{1,0:T(8,128)(2,1)S(1)}, u32[]{:S(2)}, u32[]{:S(2)}) collective-permute-start(bf16[16,4096]{1,0:T(8,128)(2,1)S(1)} %collective-permute-done.7.refs_1_), channel_id=1, source_target_pairs={{0,2},{2,0},{4,6},{6,4},{8,10},{10,8},{12,14},{14,12},{1,3},{3,1},... | collective-permute-start | bytes 393224 | tf_op jit(solution)/shard_map/ppermute | solution.py:113
  17.5 1.4 %collective-permute-start.3 = (f32[48,512]{1,0:T(8,128)S(1)}, f32[48,512]{1,0:T(8,128)S(1)}, u32[]{:S(2)}, u32[]{:S(2)}) collective-permute-start(f32[48,512]{1,0:T(8,128)S(1)} %project.5.up_ref), channel_id=1, source_target_pairs={{0,1},{1,0},{2,3},{3,2},{4,5},{5,4},{6,7},{7,6},{8,9},{9,8},{10,11... | collective-permute-start | bytes 294920 | tf_op jit(solution)/shard_map/ppermute | solution.py:116
  22.7 3.3 %collective-permute-start.11 = (f32[80,512]{1,0:T(8,128)S(1)}, f32[80,512]{1,0:T(8,128)S(1)}, u32[]{:S(2)}, u32[]{:S(2)}) collective-permute-start(f32[80,512]{1,0:T(8,128)S(1)} %project.6.gate_ref), channel_id=1, source_target_pairs={{0,1},{1,0},{2,3},{3,2},{4,5},{5,4},{6,7},{7,6},{8,9},{9,8},{10,11... | collective-permute-start | bytes 491528 | tf_op jit(solution)/shard_map/ppermute | solution.py:116
  23.6 2.4 %collective-permute-start.12 = (f32[80,512]{1,0:T(8,128)S(1)}, f32[80,512]{1,0:T(8,128)S(1)}, u32[]{:S(2)}, u32[]{:S(2)}) collective-permute-start(f32[80,512]{1,0:T(8,128)S(1)} %project.7.up_ref), channel_id=1, source_target_pairs={{0,1},{1,0},{2,3},{3,2},{4,5},{5,4},{6,7},{7,6},{8,9},{9,8},{10,11... | collective-permute-start | bytes 491528 | tf_op jit(solution)/shard_map/ppermute | solution.py:116
  24.2 6.3 %collective-permute-start.4 = (bf16[16,4096]{1,0:T(8,128)(2,1)S(1)}, bf16[16,4096]{1,0:T(8,128)(2,1)S(1)}, u32[]{:S(2)}, u32[]{:S(2)}) collective-permute-start(bf16[16,4096]{1,0:T(8,128)(2,1)S(1)} %get-tuple-element.31), channel_id=1, source_target_pairs={{0,2},{2,0},{4,6},{6,4},{8,10},{10,8},{12,14},{14,12},{1,3},{3,1},... | collective-permute-start | bytes 393224 | tf_op jit(solution)/shard_map/ppermute | solution.py:113
  25.6 6.4 %collective-permute-start.5 = (bf16[16,4096]{1,0:T(8,128)(2,1)S(1)}, bf16[16,4096]{1,0:T(8,128)(2,1)S(1)}, u32[]{:S(2)}, u32[]{:S(2)}) collective-permute-start(bf16[16,4096]{1,0:T(8,128)(2,1)S(1)} %get-tuple-element.32), channel_id=1, source_target_pairs={{0,4},{2,6},{4,0},{6,2},{8,12},{10,14},{12,8},{14,10},{1,5},{3,7},... | collective-permute-start | bytes 393224 | tf_op jit(solution)/shard_map/ppermute | solution.py:113
  26.9 7.9 %collective-permute-start.13 = (bf16[16,4096]{1,0:T(8,128)(2,1)S(1)}, bf16[16,4096]{1,0:T(8,128)(2,1)S(1)}, u32[]{:S(2)}, u32[]{:S(2)}) collective-permute-start(bf16[16,4096]{1,0:T(8,128)(2,1)S(1)} %get-tuple-element.36), channel_id=1, source_target_pairs={{0,4},{2,6},{4,0},{6,2},{8,12},{10,14},{12,8},{14,10},{1,5},{3,7},... | collective-permute-start | bytes 393224 | tf_op jit(solution)/shard_map/ppermute | solution.py:113
  28.5 8.0 %collective-permute-start.14 = (bf16[16,4096]{1,0:T(8,128)(2,1)S(1)}, bf16[16,4096]{1,0:T(8,128)(2,1)S(1)}, u32[]{:S(2)}, u32[]{:S(2)}) collective-permute-start(bf16[16,4096]{1,0:T(8,128)(2,1)S(1)} %get-tuple-element.37), channel_id=1, source_target_pairs={{0,6},{2,4},{4,2},{6,0},{8,14},{10,12},{12,10},{14,8},{1,7},{3,5},... | collective-permute-start | bytes 393224 | tf_op jit(solution)/shard_map/ppermute | solution.py:113
  29.0 8.0 %collective-permute-start.15 = (bf16[16,4096]{1,0:T(8,128)(2,1)S(1)}, bf16[16,4096]{1,0:T(8,128)(2,1)S(1)}, u32[]{:S(2)}, u32[]{:S(2)}) collective-permute-start(bf16[16,4096]{1,0:T(8,128)(2,1)S(1)} %get-tuple-element.38), channel_id=1, source_target_pairs={{0,2},{2,0},{4,6},{6,4},{8,10},{10,8},{12,14},{14,12},{1,3},{3,1},... | collective-permute-start | bytes 393224 | tf_op jit(solution)/shard_map/ppermute | solution.py:113
  37.1 7.8 %collective-permute-start.16 = (bf16[16,4096]{1,0:T(8,128)(2,1)S(1)}, bf16[16,4096]{1,0:T(8,128)(2,1)S(1)}, u32[]{:S(2)}, u32[]{:S(2)}) collective-permute-start(bf16[16,4096]{1,0:T(8,128)(2,1)S(1)} %add.5), channel_id=1, source_target_pairs={{0,8},{2,10},{4,12},{6,14},{8,0},{10,2},{12,4},{14,6},{1,9},{3,11}... | collective-permute-start | bytes 393224 | tf_op jit(solution)/shard_map/ppermute | solution.py:113
  39.0 7.0 %collective-permute-start.17 = (bf16[16,4096]{1,0:T(8,128)(2,1)S(1)}, bf16[16,4096]{1,0:T(8,128)(2,1)S(1)}, u32[]{:S(2)}, u32[]{:S(2)}) collective-permute-start(bf16[16,4096]{1,0:T(8,128)(2,1)S(1)} %get-tuple-element.40), channel_id=1, source_target_pairs={{0,6},{2,4},{4,2},{6,0},{8,14},{10,12},{12,10},{14,8},{1,7},{3,5},... | collective-permute-start | bytes 393224 | tf_op jit(solution)/shard_map/ppermute | solution.py:113

commit v13 on v9

--- a/solution.py
+++ b/solution.py
@@ -163,8 +163,9 @@
             sums.append(add(part[far], quad, BF16))
         arrived = [swap(value, far) for value, far in zip(sums, fars)]
         pair = add(part[2], [swap(part[3], 1)], BF16, after=sums)
+        part[1], pair = lax.optimization_barrier((part[1], pair))
         total = add(part[0], arrived, F32, 1500000000)
-        return add(total, [swap(part[1], 1), swap(pair, 2)], BF16)
+        return add(total, [swap(pair, 2), swap(part[1], 1)], BF16)
 
     return local
 

time: 44.8 us -> 44.8 us (level)
  transfers between devices with their start and end apart: 16 -> 16, of which waited for: 10 -> 11; matrix products, arithmetic and copies ran while one was open for 0% -> 0% of each run, Pallas kernels for 10% -> 10%
where the time goes in v13:
time: 44.8 us; the launch traced here: 44.7 us
  starting transfers between devices  20.4 us (46%)
  waiting for transfers between devices  17.7 us (40%)
  Pallas kernels  6.48 us (14%)
    ppermute x14, starting transfers between devices, swap(): return lax.ppermute(value, 'wide', [(i, i ^ bits) for i in range(wide)])  19.7 us
    ppermute x14, waiting for transfers between devices, swap(): return lax.ppermute(value, 'wide', [(i, i ^ bits) for i in range(wide)])  16.5 us
    pallas_call x1, Pallas kernels, fetch(): pl.pallas_call(functools.partial(fetch_kernel, pieces, count), in_specs=[...  3.47 us
    pallas_call x4, Pallas kernels, call(): pl.pallas_call(kernel, out_shape=out_shape, compiler_params=pltpu.Compile...  2.2 us
    ppermute x2, waiting for transfers between devices, across_cores(): lax.ppermute(value, 'narrow', [(i, (i + 1) % narrow) for i in range(narro...  1.16 us
  transfers between devices with their start and end apart: 16, of which 11 were waited for; matrix products, arithmetic and copies ran while one was open for 0% of the time, Pallas kernels for 10%

profile of v13, /device:TPU:0, one launch (start us, length us, event | category | flops | bytes accessed | tf_op | source)
XLA Modules:
  0.0 44.7 jit_solution(17694510298029879618)
XLA Ops:
  0.0 0.0 copy-start.1
  0.0 3.0 %collective-permute-start = (bf16[16,4096]{1,0:T(8,128)(2,1)}, bf16[16,4096]{1,0:T(8,128)(2,1)S(1)}, u32[]{:S(2)}, u32[]{:S(2)}) collective-permute-start(bf16[16,4096]{1,0:T(8,128)(2,1)} %refs_0_.3), channel_id=1, source_target_pairs={{0,2},{2,0},{4,6},{6,4},{8,10},{10,8},{12,14},{14,12},{1,3},{3,1},... | collective-permute-start | bytes 393224 | tf_op jit(solution)/shard_map/ppermute | solution.py:129
  3.0 1.6 %collective-permute-start.1 = (bf16[16,4096]{1,0:T(8,128)(2,1)}, bf16[16,4096]{1,0:T(8,128)(2,1)S(1)}, u32[]{:S(2)}, u32[]{:S(2)}) collective-permute-start(bf16[16,4096]{1,0:T(8,128)(2,1)} %refs_0_.3), channel_id=1, source_target_pairs={{0,4},{2,6},{4,0},{6,2},{8,12},{10,14},{12,8},{14,10},{1,5},{3,7},... | collective-permute-start | bytes 393224 | tf_op jit(solution)/shard_map/ppermute | solution.py:129
  4.5 2.6 %collective-permute-start.3 = (bf16[16,4096]{1,0:T(8,128)(2,1)}, bf16[16,4096]{1,0:T(8,128)(2,1)S(1)}, u32[]{:S(2)}, u32[]{:S(2)}) collective-permute-start(bf16[16,4096]{1,0:T(8,128)(2,1)} %refs_0_.3), channel_id=1, source_target_pairs={{0,8},{2,10},{4,12},{6,14},{8,0},{10,2},{12,4},{14,6},{1,9},{3,11}... | collective-permute-start | bytes 393224 | tf_op jit(solution)/shard_map/ppermute | solution.py:129
  7.1 3.5 %fetch.1 = (bf16[4096,512]{1,0:T(8,128)(2,1)S(1)}, bf16[4096,512]{1,0:T(8,128)(2,1)S(1)}) custom-call(bf16[4096,512]{1,0:T(8,128)(2,1)} %refs_0_.2, bf16[4096,512]{1,0:T(8,128)(2,1)} %refs_1_.1), custom_call_target="tpu_custom_call" | custom-call | flops 4000000000 | tf_op jit(solution)/shard_map/fetch/pallas_call | solution.py:41
  10.6 0.0 collective-permute-done.refs_2_
  10.6 0.0 collective-permute-done.1.refs_1_
  10.6 0.6 %collective-permute-start.2 = (bf16[16,4096]{1,0:T(8,128)(2,1)S(1)}, bf16[16,4096]{1,0:T(8,128)(2,1)S(1)}, u32[]{:S(2)}, u32[]{:S(2)}) collective-permute-start(bf16[16,4096]{1,0:T(8,128)(2,1)S(1)} %collective-permute-done.1.refs_1_), channel_id=1, source_target_pairs={{0,2},{2,0},{4,6},{6,4},{8,10},{10,8},{12,14},{14,12},{1,3},{3,1},... | collective-permute-start | bytes 393224 | tf_op jit(solution)/shard_map/ppermute | solution.py:129
  11.2 2.0 %collective-permute-done.3.refs_1_ = bf16[16,4096]{1,0:T(8,128)(2,1)S(1)} collective-permute-done((bf16[16,4096]{1,0:T(8,128)(2,1)}, bf16[16,4096]{1,0:T(8,128)(2,1)S(1)}, u32[]{:S(2)}, u32[]{:S(2)}) %collective-permute-start.3) | collective-permute-done | bytes 131104 | tf_op jit(solution)/shard_map/ppermute | solution.py:129
  13.2 0.3 collective-permute-start.4
  13.5 1.7 %collective-permute-start.5 = (bf16[16,4096]{1,0:T(8,128)(2,1)S(1)}, bf16[16,4096]{1,0:T(8,128)(2,1)S(1)}, u32[]{:S(2)}, u32[]{:S(2)}) collective-permute-start(bf16[16,4096]{1,0:T(8,128)(2,1)S(1)} %collective-permute-done.3.refs_1_), channel_id=1, source_target_pairs={{0,4},{2,6},{4,0},{6,2},{8,12},{10,14},{12,8},{14,10},{1,5},{3,7},... | collective-permute-start | bytes 393224 | tf_op jit(solution)/shard_map/ppermute | solution.py:129
  15.2 1.5 %collective-permute-start.6 = (bf16[16,4096]{1,0:T(8,128)(2,1)S(1)}, bf16[16,4096]{1,0:T(8,128)(2,1)S(1)}, u32[]{:S(2)}, u32[]{:S(2)}) collective-permute-start(bf16[16,4096]{1,0:T(8,128)(2,1)S(1)} %collective-permute-done.3.refs_1_), channel_id=1, source_target_pairs={{0,2},{2,0},{4,6},{6,4},{8,10},{10,8},{12,14},{14,12},{1,3},{3,1},... | collective-permute-start | bytes 393224 | tf_op jit(solution)/shard_map/ppermute | solution.py:129
  16.7 2.5 %collective-permute-done.2.refs_3_ = bf16[16,4096]{1,0:T(8,128)(2,1)S(1)} collective-permute-done((bf16[16,4096]{1,0:T(8,128)(2,1)S(1)}, bf16[16,4096]{1,0:T(8,128)(2,1)S(1)}, u32[]{:S(2)}, u32[]{:S(2)}) %collective-permute-start.2) | collective-permute-done | bytes 131104 | tf_op jit(solution)/shard_map/ppermute | solution.py:129
  19.2 0.0 copy-done.1
  19.2 0.0 copy-start
  19.3 0.0 collective-permute-done.4.refs_2_
  19.3 0.3 collective-permute-done.5.refs_3_
  19.6 1.2 %collective-permute-done.6.refs_4_ = bf16[16,4096]{1,0:T(8,128)(2,1)S(1)} collective-permute-done((bf16[16,4096]{1,0:T(8,128)(2,1)S(1)}, bf16[16,4096]{1,0:T(8,128)(2,1)S(1)}, u32[]{:S(2)}, u32[]{:S(2)}) %collective-permute-start.6) | collective-permute-done | bytes 131104 | tf_op jit(solution)/shard_map/ppermute | solution.py:129
  20.7 0.7 %project.3.up_ref = f32[128,512]{1,0:T(8,128)S(1)} custom-call(bf16[64,4096]{1,0:T(8,128)(2,1)S(1)} %pack.1.refs_0_, bf16[16,4096]{1,0:T(8,128)(2,1)S(1)} %collective-permute-done.3.refs_1_, bf16[16,4096]{1,0:T(8,128)(2,1)S(1)} %collective-permute-done.4.refs_2_, bf16[16,4096]{1,0:T(8,128)(2,1)S(1)} %collective-permute-done.5.refs_3_, ...), custom_call_target="tpu_custom_call" | custom-call | flops 400000000 | tf_op jit(solution)/shard_map/project/pallas_call | solution.py:15
  21.4 0.1 collective-permute-start.8
  21.5 0.7 %project.2.gate_ref = f32[128,512]{1,0:T(8,128)S(1)} custom-call(bf16[64,4096]{1,0:T(8,128)(2,1)S(1)} %pack.1.refs_0_, bf16[16,4096]{1,0:T(8,128)(2,1)S(1)} %collective-permute-done.3.refs_1_, bf16[16,4096]{1,0:T(8,128)(2,1)S(1)} %collective-permute-done.4.refs_2_, bf16[16,4096]{1,0:T(8,128)(2,1)S(1)} %collective-permute-done.5.refs_3_, ...), custom_call_target="tpu_custom_call" | custom-call | flops 400000000 | tf_op jit(solution)/shard_map/project/pallas_call | solution.py:15
  22.2 0.6 %collective-permute-start.7 = (f32[128,512]{1,0:T(8,128)S(1)}, f32[128,512]{1,0:T(8,128)S(1)}, u32[]{:S(2)}, u32[]{:S(2)}) collective-permute-start(f32[128,512]{1,0:T(8,128)S(1)} %project.2.gate_ref), channel_id=1, source_target_pairs={{0,1},{1,0},{2,3},{3,2},{4,5},{5,4},{6,7},{7,6},{8,9},{9,8},{10,11... | collective-permute-start | bytes 786440 | tf_op jit(solution)/shard_map/ppermute | solution.py:132
  22.8 0.2 collective-permute-done.8.up_other_ref
  23.0 0.9 %collective-permute-done.7.gate_other_ref = f32[128,512]{1,0:T(8,128)S(1)} collective-permute-done((f32[128,512]{1,0:T(8,128)S(1)}, f32[128,512]{1,0:T(8,128)S(1)}, u32[]{:S(2)}, u32[]{:S(2)}) %collective-permute-start.7) | collective-permute-done | bytes 262176 | tf_op jit(solution)/shard_map/ppermute | solution.py:132
  24.0 0.0 copy-done
  24.0 0.7 %down.1 = (f32[16,4096]{1,0:T(8,128)S(1)}, f32[16,4096]{1,0:T(8,128)S(1)}, bf16[16,4096]{1,0:T(8,128)(2,1)S(1)}, bf16[16,4096]{1,0:T(8,128)(2,1)S(1)}, f32[16,40...) custom-call(f32[128,512]{1,0:T(8,128)S(1)} %project.2.gate_ref, ...), custom_call_target="tpu_custom_call" | custom-call | flops 536870912 | tf_op jit(solution)/shard_map/down/pallas_call | solution.py:15
  24.7 1.0 %collective-permute-start.10 = (bf16[16,4096]{1,0:T(8,128)(2,1)S(1)}, bf16[16,4096]{1,0:T(8,128)(2,1)S(1)}, u32[]{:S(2)}, u32[]{:S(2)}) collective-permute-start(bf16[16,4096]{1,0:T(8,128)(2,1)S(1)} %get-tuple-element.30), channel_id=1, source_target_pairs={{0,6},{2,4},{4,2},{6,0},{8,14},{10,12},{12,10},{14,8},{1,7},{3,5},... | collective-permute-start | bytes 393224 | tf_op jit(solution)/shard_map/ppermute | solution.py:129
  25.8 1.5 %collective-permute-start.11 = (bf16[16,4096]{1,0:T(8,128)(2,1)S(1)}, bf16[16,4096]{1,0:T(8,128)(2,1)S(1)}, u32[]{:S(2)}, u32[]{:S(2)}) collective-permute-start(bf16[16,4096]{1,0:T(8,128)(2,1)S(1)} %get-tuple-element.31), channel_id=1, source_target_pairs={{0,2},{2,0},{4,6},{6,4},{8,10},{10,8},{12,14},{14,12},{1,3},{3,1},... | collective-permute-start | bytes 393224 | tf_op jit(solution)/shard_map/ppermute | solution.py:129
  27.3 1.0 %collective-permute-start.9 = (bf16[16,4096]{1,0:T(8,128)(2,1)S(1)}, bf16[16,4096]{1,0:T(8,128)(2,1)S(1)}, u32[]{:S(2)}, u32[]{:S(2)}) collective-permute-start(bf16[16,4096]{1,0:T(8,128)(2,1)S(1)} %get-tuple-element.29), channel_id=1, source_target_pairs={{0,4},{2,6},{4,0},{6,2},{8,12},{10,14},{12,8},{14,10},{1,5},{3,7},... | collective-permute-start | bytes 393224 | tf_op jit(solution)/shard_map/ppermute | solution.py:129
  28.3 1.1 %collective-permute-start.13 = (bf16[16,4096]{1,0:T(8,128)(2,1)S(1)}, bf16[16,4096]{1,0:T(8,128)(2,1)S(1)}, u32[]{:S(2)}, u32[]{:S(2)}) collective-permute-start(bf16[16,4096]{1,0:T(8,128)(2,1)S(1)} %get-tuple-element.34), channel_id=1, source_target_pairs={{0,2},{2,0},{4,6},{6,4},{8,10},{10,8},{12,14},{14,12},{1,3},{3,1},... | collective-permute-start | bytes 393224 | tf_op jit(solution)/shard_map/ppermute | solution.py:129
  29.4 2.7 %collective-permute-done.10.refs_1_ = bf16[16,4096]{1,0:T(8,128)(2,1)S(1)} collective-permute-done((bf16[16,4096]{1,0:T(8,128)(2,1)S(1)}, bf16[16,4096]{1,0:T(8,128)(2,1)S(1)}, u32[]{:S(2)}, u32[]{:S(2)}) %collective-permute-start.10) | collective-permute-done | bytes 131104 | tf_op jit(solution)/shard_map/ppermute | solution.py:129
  32.0 2.3 %collective-permute-done.11.refs_2_ = bf16[16,4096]{1,0:T(8,128)(2,1)S(1)} collective-permute-done((bf16[16,4096]{1,0:T(8,128)(2,1)S(1)}, bf16[16,4096]{1,0:T(8,128)(2,1)S(1)}, u32[]{:S(2)}, u32[]{:S(2)}) %collective-permute-start.11) | collective-permute-done | bytes 131104 | tf_op jit(solution)/shard_map/ppermute | solution.py:129
  34.4 0.0 collective-permute-done.9.refs_0_
  34.4 0.1 add.4.refs_1_
  34.4 2.1 %collective-permute-start.12 = (bf16[16,4096]{1,0:T(8,128)(2,1)S(1)}, bf16[16,4096]{1,0:T(8,128)(2,1)S(1)}, u32[]{:S(2)}, u32[]{:S(2)}) collective-permute-start(bf16[16,4096]{1,0:T(8,128)(2,1)S(1)} %add.4.refs_1_), channel_id=1, source_target_pairs={{0,8},{2,10},{4,12},{6,14},{8,0},{10,2},{12,4},{14,6},{1,9},{3,11}... | collective-permute-start | bytes 393224 | tf_op jit(solution)/shard_map/ppermute | solution.py:129
  36.5 0.4 collective-permute-done.13.refs_0_
  36.9 1.3 %collective-permute-start.14 = (bf16[16,4096]{1,0:T(8,128)(2,1)S(1)}, bf16[16,4096]{1,0:T(8,128)(2,1)S(1)}, u32[]{:S(2)}, u32[]{:S(2)}) collective-permute-start(bf16[16,4096]{1,0:T(8,128)(2,1)S(1)} %add.6), channel_id=1, source_target_pairs={{0,4},{2,6},{4,0},{6,2},{8,12},{10,14},{12,8},{14,10},{1,5},{3,7},... | collective-permute-start | bytes 393224 | tf_op jit(solution)/shard_map/ppermute | solution.py:129
  38.2 0.6 %collective-permute-start.15 = (bf16[16,4096]{1,0:T(8,128)(2,1)S(1)}, bf16[16,4096]{1,0:T(8,128)(2,1)S(1)}, u32[]{:S(2)}, u32[]{:S(2)}) collective-permute-start(bf16[16,4096]{1,0:T(8,128)(2,1)S(1)} %get-tuple-element.36), channel_id=1, source_target_pairs={{0,2},{2,0},{4,6},{6,4},{8,10},{10,8},{12,14},{14,12},{1,3},{3,1},... | collective-permute-start | bytes 393224 | tf_op jit(solution)/shard_map/ppermute | solution.py:129
  38.7 4.5 %collective-permute-done.12.refs_0_ = bf16[16,4096]{1,0:T(8,128)(2,1)S(1)} collective-permute-done((bf16[16,4096]{1,0:T(8,128)(2,1)S(1)}, bf16[16,4096]{1,0:T(8,128)(2,1)S(1)}, u32[]{:S(2)}, u32[]{:S(2)}) %collective-permute-start.12) | collective-permute-done | bytes 131104 | tf_op jit(solution)/shard_map/ppermute | solution.py:129
  43.2 0.7 %collective-permute-done.14.refs_0_ = bf16[16,4096]{1,0:T(8,128)(2,1)S(1)} collective-permute-done((bf16[16,4096]{1,0:T(8,128)(2,1)S(1)}, bf16[16,4096]{1,0:T(8,128)(2,1)S(1)}, u32[]{:S(2)}, u32[]{:S(2)}) %collective-permute-start.14) | collective-permute-done | bytes 131104 | tf_op jit(solution)/shard_map/ppermute | solution.py:129
  44.0 0.0 collective-permute-done.15.refs_1_
  44.0 0.7 %add.7 = bf16[16,4096]{1,0:T(8,128)(2,1)} custom-call(f32[16,4096]{1,0:T(8,128)S(1)} %add.5.own_ref, bf16[16,4096]{1,0:T(8,128)(2,1)S(1)} %collective-permute-done.14.refs_0_, bf16[16,4096]{1,0:T(8,128)(2,1)S(1)} %collective-permute-done.15.refs_1_), custom_call_target="tpu_custom_call" | custom-call | flops 1000000 | tf_op jit(solution)/shard_map/add/pallas_call | solution.py:114
  (3 shorter events, 0.1 us)
Async XLA Ops:
  0.0 19.2 %copy-start.1 = (bf16[16,4096]{1,0:T(8,128)(2,1)S(1)}, bf16[16,4096]{1,0:T(8,128)(2,1)}, u32[]{:S(2)}) copy-start(bf16[16,4096]{1,0:T(8,128)(2,1)} %refs_0_.3) | copy-start | bytes 393220
  0.0 10.6 %collective-permute-start = (bf16[16,4096]{1,0:T(8,128)(2,1)}, bf16[16,4096]{1,0:T(8,128)(2,1)S(1)}, u32[]{:S(2)}, u32[]{:S(2)}) collective-permute-start(bf16[16,4096]{1,0:T(8,128)(2,1)} %refs_0_.3), channel_id=1, source_target_pairs={{0,2},{2,0},{4,6},{6,4},{8,10},{10,8},{12,14},{14,12},{1,3},{3,1},... | collective-permute-start | bytes 393224 | tf_op jit(solution)/shard_map/ppermute | solution.py:129
  3.0 7.7 %collective-permute-start.1 = (bf16[16,4096]{1,0:T(8,128)(2,1)}, bf16[16,4096]{1,0:T(8,128)(2,1)S(1)}, u32[]{:S(2)}, u32[]{:S(2)}) collective-permute-start(bf16[16,4096]{1,0:T(8,128)(2,1)} %refs_0_.3), channel_id=1, source_target_pairs={{0,4},{2,6},{4,0},{6,2},{8,12},{10,14},{12,8},{14,10},{1,5},{3,7},... | collective-permute-start | bytes 393224 | tf_op jit(solution)/shard_map/ppermute | solution.py:129
  4.5 8.7 %collective-permute-start.3 = (bf16[16,4096]{1,0:T(8,128)(2,1)}, bf16[16,4096]{1,0:T(8,128)(2,1)S(1)}, u32[]{:S(2)}, u32[]{:S(2)}) collective-permute-start(bf16[16,4096]{1,0:T(8,128)(2,1)} %refs_0_.3), channel_id=1, source_target_pairs={{0,8},{2,10},{4,12},{6,14},{8,0},{10,2},{12,4},{14,6},{1,9},{3,11}... | collective-permute-start | bytes 393224 | tf_op jit(solution)/shard_map/ppermute | solution.py:129
  10.6 8.6 %collective-permute-start.2 = (bf16[16,4096]{1,0:T(8,128)(2,1)S(1)}, bf16[16,4096]{1,0:T(8,128)(2,1)S(1)}, u32[]{:S(2)}, u32[]{:S(2)}) collective-permute-start(bf16[16,4096]{1,0:T(8,128)(2,1)S(1)} %collective-permute-done.1.refs_1_), channel_id=1, source_target_pairs={{0,2},{2,0},{4,6},{6,4},{8,10},{10,8},{12,14},{14,12},{1,3},{3,1},... | collective-permute-start | bytes 393224 | tf_op jit(solution)/shard_map/ppermute | solution.py:129
  13.2 6.0 %collective-permute-start.4 = (bf16[16,4096]{1,0:T(8,128)(2,1)S(1)}, bf16[16,4096]{1,0:T(8,128)(2,1)S(1)}, u32[]{:S(2)}, u32[]{:S(2)}) collective-permute-start(bf16[16,4096]{1,0:T(8,128)(2,1)S(1)} %collective-permute-done.3.refs_1_), channel_id=1, source_target_pairs={{0,6},{2,4},{4,2},{6,0},{8,14},{10,12},{12,10},{14,8},{1,7},{3,5},... | collective-permute-start | bytes 393224 | tf_op jit(solution)/shard_map/ppermute | solution.py:129
  13.5 6.1 %collective-permute-start.5 = (bf16[16,4096]{1,0:T(8,128)(2,1)S(1)}, bf16[16,4096]{1,0:T(8,128)(2,1)S(1)}, u32[]{:S(2)}, u32[]{:S(2)}) collective-permute-start(bf16[16,4096]{1,0:T(8,128)(2,1)S(1)} %collective-permute-done.3.refs_1_), channel_id=1, source_target_pairs={{0,4},{2,6},{4,0},{6,2},{8,12},{10,14},{12,8},{14,10},{1,5},{3,7},... | collective-permute-start | bytes 393224 | tf_op jit(solution)/shard_map/ppermute | solution.py:129
  15.2 5.5 %collective-permute-start.6 = (bf16[16,4096]{1,0:T(8,128)(2,1)S(1)}, bf16[16,4096]{1,0:T(8,128)(2,1)S(1)}, u32[]{:S(2)}, u32[]{:S(2)}) collective-permute-start(bf16[16,4096]{1,0:T(8,128)(2,1)S(1)} %collective-permute-done.3.refs_1_), channel_id=1, source_target_pairs={{0,2},{2,0},{4,6},{6,4},{8,10},{10,8},{12,14},{14,12},{1,3},{3,1},... | collective-permute-start | bytes 393224 | tf_op jit(solution)/shard_map/ppermute | solution.py:129
  19.2 4.7 %copy-start = (bf16[512,4096]{1,0:T(8,128)(2,1)S(1)}, bf16[512,4096]{1,0:T(8,128)(2,1)}, u32[]{:S(2)}) copy-start(bf16[512,4096]{1,0:T(8,128)(2,1)} %weight_ref.1) | copy-start | bytes 12582916
  21.4 1.6 %collective-permute-start.8 = (f32[128,512]{1,0:T(8,128)S(1)}, f32[128,512]{1,0:T(8,128)S(1)}, u32[]{:S(2)}, u32[]{:S(2)}) collective-permute-start(f32[128,512]{1,0:T(8,128)S(1)} %project.3.up_ref), channel_id=1, source_target_pairs={{0,1},{1,0},{2,3},{3,2},{4,5},{5,4},{6,7},{7,6},{8,9},{9,8},{10,11... | collective-permute-start | bytes 786440 | tf_op jit(solution)/shard_map/ppermute | solution.py:132
  22.2 1.7 %collective-permute-start.7 = (f32[128,512]{1,0:T(8,128)S(1)}, f32[128,512]{1,0:T(8,128)S(1)}, u32[]{:S(2)}, u32[]{:S(2)}) collective-permute-start(f32[128,512]{1,0:T(8,128)S(1)} %project.2.gate_ref), channel_id=1, source_target_pairs={{0,1},{1,0},{2,3},{3,2},{4,5},{5,4},{6,7},{7,6},{8,9},{9,8},{10,11... | collective-permute-start | bytes 786440 | tf_op jit(solution)/shard_map/ppermute | solution.py:132
  24.7 7.3 %collective-permute-start.10 = (bf16[16,4096]{1,0:T(8,128)(2,1)S(1)}, bf16[16,4096]{1,0:T(8,128)(2,1)S(1)}, u32[]{:S(2)}, u32[]{:S(2)}) collective-permute-start(bf16[16,4096]{1,0:T(8,128)(2,1)S(1)} %get-tuple-element.30), channel_id=1, source_target_pairs={{0,6},{2,4},{4,2},{6,0},{8,14},{10,12},{12,10},{14,8},{1,7},{3,5},... | collective-permute-start | bytes 393224 | tf_op jit(solution)/shard_map/ppermute | solution.py:129
  25.8 8.6 %collective-permute-start.11 = (bf16[16,4096]{1,0:T(8,128)(2,1)S(1)}, bf16[16,4096]{1,0:T(8,128)(2,1)S(1)}, u32[]{:S(2)}, u32[]{:S(2)}) collective-permute-start(bf16[16,4096]{1,0:T(8,128)(2,1)S(1)} %get-tuple-element.31), channel_id=1, source_target_pairs={{0,2},{2,0},{4,6},{6,4},{8,10},{10,8},{12,14},{14,12},{1,3},{3,1},... | collective-permute-start | bytes 393224 | tf_op jit(solution)/shard_map/ppermute | solution.py:129
  27.3 7.1 %collective-permute-start.9 = (bf16[16,4096]{1,0:T(8,128)(2,1)S(1)}, bf16[16,4096]{1,0:T(8,128)(2,1)S(1)}, u32[]{:S(2)}, u32[]{:S(2)}) collective-permute-start(bf16[16,4096]{1,0:T(8,128)(2,1)S(1)} %get-tuple-element.29), channel_id=1, source_target_pairs={{0,4},{2,6},{4,0},{6,2},{8,12},{10,14},{12,8},{14,10},{1,5},{3,7},... | collective-permute-start | bytes 393224 | tf_op jit(solution)/shard_map/ppermute | solution.py:129
  28.3 8.6 %collective-permute-start.13 = (bf16[16,4096]{1,0:T(8,128)(2,1)S(1)}, bf16[16,4096]{1,0:T(8,128)(2,1)S(1)}, u32[]{:S(2)}, u32[]{:S(2)}) collective-permute-start(bf16[16,4096]{1,0:T(8,128)(2,1)S(1)} %get-tuple-element.34), channel_id=1, source_target_pairs={{0,2},{2,0},{4,6},{6,4},{8,10},{10,8},{12,14},{14,12},{1,3},{3,1},... | collective-permute-start | bytes 393224 | tf_op jit(solution)/shard_map/ppermute | solution.py:129
  34.4 8.8 %collective-permute-start.12 = (bf16[16,4096]{1,0:T(8,128)(2,1)S(1)}, bf16[16,4096]{1,0:T(8,128)(2,1)S(1)}, u32[]{:S(2)}, u32[]{:S(2)}) collective-permute-start(bf16[16,4096]{1,0:T(8,128)(2,1)S(1)} %add.4.refs_1_), channel_id=1, source_target_pairs={{0,8},{2,10},{4,12},{6,14},{8,0},{10,2},{12,4},{14,6},{1,9},{3,11}... | collective-permute-start | bytes 393224 | tf_op jit(solution)/shard_map/ppermute | solution.py:129
  36.9 7.1 %collective-permute-start.14 = (bf16[16,4096]{1,0:T(8,128)(2,1)S(1)}, bf16[16,4096]{1,0:T(8,128)(2,1)S(1)}, u32[]{:S(2)}, u32[]{:S(2)}) collective-permute-start(bf16[16,4096]{1,0:T(8,128)(2,1)S(1)} %add.6), channel_id=1, source_target_pairs={{0,4},{2,6},{4,0},{6,2},{8,12},{10,14},{12,8},{14,10},{1,5},{3,7},... | collective-permute-start | bytes 393224 | tf_op jit(solution)/shard_map/ppermute | solution.py:129
  38.2 5.8 %collective-permute-start.15 = (bf16[16,4096]{1,0:T(8,128)(2,1)S(1)}, bf16[16,4096]{1,0:T(8,128)(2,1)S(1)}, u32[]{:S(2)}, u32[]{:S(2)}) collective-permute-start(bf16[16,4096]{1,0:T(8,128)(2,1)S(1)} %get-tuple-element.36), channel_id=1, source_target_pairs={{0,2},{2,0},{4,6},{6,4},{8,10},{10,8},{12,14},{14,12},{1,3},{3,1},... | collective-permute-start | bytes 393224 | tf_op jit(solution)/shard_map/ppermute | solution.py:129

commit v14 on v9

--- a/solution.py
+++ b/solution.py
@@ -146,7 +146,7 @@
         for far in fars:
             for near in (2, 3, 1):
                 block[far + near] = swap(block[far], near)
-        stay = [0, 2] + fars
+        stay = [0] + fars
         near_blocks = pack([block[b] for b in (0, 2, 1, 3)])
         order = [0, 2, 1, 3] + [far + near for far in fars for near in (0, 3, 2, 1)]
         far_blocks = [block[b] for b in order[4:]]
@@ -162,9 +162,9 @@
             quad = [swap(part[far + near], near) for near in (2, 3, 1)]
             sums.append(add(part[far], quad, BF16))
         arrived = [swap(value, far) for value, far in zip(sums, fars)]
-        pair = add(part[2], [swap(part[3], 1)], BF16, after=sums)
-        total = add(part[0], arrived, F32, 1500000000)
-        return add(total, [swap(part[1], 1), swap(pair, 2)], BF16)
+        part[1], part[3], sums[0] = lax.optimization_barrier((part[1], part[3], sums[0]))
+        total = add(part[0], [swap(part[2], 2)] + arrived, F32, 1500000000)
+        return add(total, [swap(part[3], 3), swap(part[1], 1)], BF16)
 
     return local
 

time: 44.8 us -> 45.5 us (1.016)
  waiting for transfers between devices: 17.3 us -> 17.8 us
    ppermute x14, waiting for transfers between devices: 16.2 us -> 16.6 us  [swap(): return lax.ppermute(value, 'wide', [(i, i ^ bits) for i in range(wide)])]
  transfers between devices with their start and end apart: 16 -> 16, of which waited for: 10 -> 12; matrix products, arithmetic and copies ran while one was open for 0% -> 0% of each run, Pallas kernels for 10% -> 10%
where the time goes in v14:
time: 45.5 us; the launch traced here: 45.4 us
  starting transfers between devices  21 us (46%)
  waiting for transfers between devices  17.8 us (39%)
  Pallas kernels  6.46 us (14%)
    ppermute x14, starting transfers between devices, swap(): return lax.ppermute(value, 'wide', [(i, i ^ bits) for i in range(wide)])  20.4 us
    ppermute x14, waiting for transfers between devices, swap(): return lax.ppermute(value, 'wide', [(i, i ^ bits) for i in range(wide)])  16.6 us
    pallas_call x1, Pallas kernels, fetch(): pl.pallas_call(functools.partial(fetch_kernel, pieces, count), in_specs=[...  3.47 us
    pallas_call x4, Pallas kernels, call(): pl.pallas_call(kernel, out_shape=out_shape, compiler_params=pltpu.Compile...  2.2 us
    ppermute x2, waiting for transfers between devices, across_cores(): lax.ppermute(value, 'narrow', [(i, (i + 1) % narrow) for i in range(narro...  1.16 us
  transfers between devices with their start and end apart: 16, of which 12 were waited for; matrix products, arithmetic and copies ran while one was open for 0% of the time, Pallas kernels for 10%

profile of v14, /device:TPU:0, one launch (start us, length us, event | category | flops | bytes accessed | tf_op | source)
XLA Modules:
  0.0 45.4 jit_solution(6603009820038663400)
XLA Ops:
  0.0 0.0 copy-start.1
  0.0 3.0 %collective-permute-start = (bf16[16,4096]{1,0:T(8,128)(2,1)}, bf16[16,4096]{1,0:T(8,128)(2,1)S(1)}, u32[]{:S(2)}, u32[]{:S(2)}) collective-permute-start(bf16[16,4096]{1,0:T(8,128)(2,1)} %refs_0_.3), channel_id=1, source_target_pairs={{0,2},{2,0},{4,6},{6,4},{8,10},{10,8},{12,14},{14,12},{1,3},{3,1},... | collective-permute-start | bytes 393224 | tf_op jit(solution)/shard_map/ppermute | solution.py:129
  3.0 1.6 %collective-permute-start.1 = (bf16[16,4096]{1,0:T(8,128)(2,1)}, bf16[16,4096]{1,0:T(8,128)(2,1)S(1)}, u32[]{:S(2)}, u32[]{:S(2)}) collective-permute-start(bf16[16,4096]{1,0:T(8,128)(2,1)} %refs_0_.3), channel_id=1, source_target_pairs={{0,4},{2,6},{4,0},{6,2},{8,12},{10,14},{12,8},{14,10},{1,5},{3,7},... | collective-permute-start | bytes 393224 | tf_op jit(solution)/shard_map/ppermute | solution.py:129
  4.5 2.6 %collective-permute-start.3 = (bf16[16,4096]{1,0:T(8,128)(2,1)}, bf16[16,4096]{1,0:T(8,128)(2,1)S(1)}, u32[]{:S(2)}, u32[]{:S(2)}) collective-permute-start(bf16[16,4096]{1,0:T(8,128)(2,1)} %refs_0_.3), channel_id=1, source_target_pairs={{0,8},{2,10},{4,12},{6,14},{8,0},{10,2},{12,4},{14,6},{1,9},{3,11}... | collective-permute-start | bytes 393224 | tf_op jit(solution)/shard_map/ppermute | solution.py:129
  7.1 3.5 %fetch.1 = (bf16[4096,512]{1,0:T(8,128)(2,1)S(1)}, bf16[4096,512]{1,0:T(8,128)(2,1)S(1)}) custom-call(bf16[4096,512]{1,0:T(8,128)(2,1)} %refs_0_.2, bf16[4096,512]{1,0:T(8,128)(2,1)} %refs_1_.1), custom_call_target="tpu_custom_call" | custom-call | flops 4000000000 | tf_op jit(solution)/shard_map/fetch/pallas_call | solution.py:41
  10.6 0.0 collective-permute-done.refs_2_
  10.6 0.0 collective-permute-done.1.refs_1_
  10.6 0.6 %collective-permute-start.2 = (bf16[16,4096]{1,0:T(8,128)(2,1)S(1)}, bf16[16,4096]{1,0:T(8,128)(2,1)S(1)}, u32[]{:S(2)}, u32[]{:S(2)}) collective-permute-start(bf16[16,4096]{1,0:T(8,128)(2,1)S(1)} %collective-permute-done.1.refs_1_), channel_id=1, source_target_pairs={{0,2},{2,0},{4,6},{6,4},{8,10},{10,8},{12,14},{14,12},{1,3},{3,1},... | collective-permute-start | bytes 393224 | tf_op jit(solution)/shard_map/ppermute | solution.py:129
  11.2 2.0 %collective-permute-done.3.refs_1_ = bf16[16,4096]{1,0:T(8,128)(2,1)S(1)} collective-permute-done((bf16[16,4096]{1,0:T(8,128)(2,1)}, bf16[16,4096]{1,0:T(8,128)(2,1)S(1)}, u32[]{:S(2)}, u32[]{:S(2)}) %collective-permute-start.3) | collective-permute-done | bytes 131104 | tf_op jit(solution)/shard_map/ppermute | solution.py:129
  13.2 0.3 collective-permute-start.4
  13.5 1.7 %collective-permute-start.5 = (bf16[16,4096]{1,0:T(8,128)(2,1)S(1)}, bf16[16,4096]{1,0:T(8,128)(2,1)S(1)}, u32[]{:S(2)}, u32[]{:S(2)}) collective-permute-start(bf16[16,4096]{1,0:T(8,128)(2,1)S(1)} %collective-permute-done.3.refs_1_), channel_id=1, source_target_pairs={{0,4},{2,6},{4,0},{6,2},{8,12},{10,14},{12,8},{14,10},{1,5},{3,7},... | collective-permute-start | bytes 393224 | tf_op jit(solution)/shard_map/ppermute | solution.py:129
  15.2 1.5 %collective-permute-start.6 = (bf16[16,4096]{1,0:T(8,128)(2,1)S(1)}, bf16[16,4096]{1,0:T(8,128)(2,1)S(1)}, u32[]{:S(2)}, u32[]{:S(2)}) collective-permute-start(bf16[16,4096]{1,0:T(8,128)(2,1)S(1)} %collective-permute-done.3.refs_1_), channel_id=1, source_target_pairs={{0,2},{2,0},{4,6},{6,4},{8,10},{10,8},{12,14},{14,12},{1,3},{3,1},... | collective-permute-start | bytes 393224 | tf_op jit(solution)/shard_map/ppermute | solution.py:129
  16.7 2.5 %collective-permute-done.2.refs_3_ = bf16[16,4096]{1,0:T(8,128)(2,1)S(1)} collective-permute-done((bf16[16,4096]{1,0:T(8,128)(2,1)S(1)}, bf16[16,4096]{1,0:T(8,128)(2,1)S(1)}, u32[]{:S(2)}, u32[]{:S(2)}) %collective-permute-start.2) | collective-permute-done | bytes 131104 | tf_op jit(solution)/shard_map/ppermute | solution.py:129
  19.2 0.0 copy-done.1
  19.2 0.0 copy-start
  19.3 0.0 collective-permute-done.4.refs_2_
  19.3 0.3 collective-permute-done.5.refs_3_
  19.6 1.2 %collective-permute-done.6.refs_4_ = bf16[16,4096]{1,0:T(8,128)(2,1)S(1)} collective-permute-done((bf16[16,4096]{1,0:T(8,128)(2,1)S(1)}, bf16[16,4096]{1,0:T(8,128)(2,1)S(1)}, u32[]{:S(2)}, u32[]{:S(2)}) %collective-permute-start.6) | collective-permute-done | bytes 131104 | tf_op jit(solution)/shard_map/ppermute | solution.py:129
  20.7 0.7 %project.3.up_ref = f32[128,512]{1,0:T(8,128)S(1)} custom-call(bf16[64,4096]{1,0:T(8,128)(2,1)S(1)} %pack.1.refs_0_, bf16[16,4096]{1,0:T(8,128)(2,1)S(1)} %collective-permute-done.3.refs_1_, bf16[16,4096]{1,0:T(8,128)(2,1)S(1)} %collective-permute-done.4.refs_2_, bf16[16,4096]{1,0:T(8,128)(2,1)S(1)} %collective-permute-done.5.refs_3_, ...), custom_call_target="tpu_custom_call" | custom-call | flops 400000000 | tf_op jit(solution)/shard_map/project/pallas_call | solution.py:15
  21.4 0.1 collective-permute-start.8
  21.5 0.7 %project.2.gate_ref = f32[128,512]{1,0:T(8,128)S(1)} custom-call(bf16[64,4096]{1,0:T(8,128)(2,1)S(1)} %pack.1.refs_0_, bf16[16,4096]{1,0:T(8,128)(2,1)S(1)} %collective-permute-done.3.refs_1_, bf16[16,4096]{1,0:T(8,128)(2,1)S(1)} %collective-permute-done.4.refs_2_, bf16[16,4096]{1,0:T(8,128)(2,1)S(1)} %collective-permute-done.5.refs_3_, ...), custom_call_target="tpu_custom_call" | custom-call | flops 400000000 | tf_op jit(solution)/shard_map/project/pallas_call | solution.py:15
  22.2 0.6 %collective-permute-start.7 = (f32[128,512]{1,0:T(8,128)S(1)}, f32[128,512]{1,0:T(8,128)S(1)}, u32[]{:S(2)}, u32[]{:S(2)}) collective-permute-start(f32[128,512]{1,0:T(8,128)S(1)} %project.2.gate_ref), channel_id=1, source_target_pairs={{0,1},{1,0},{2,3},{3,2},{4,5},{5,4},{6,7},{7,6},{8,9},{9,8},{10,11... | collective-permute-start | bytes 786440 | tf_op jit(solution)/shard_map/ppermute | solution.py:132
  22.8 0.2 collective-permute-done.8.up_other_ref
  23.0 0.9 %collective-permute-done.7.gate_other_ref = f32[128,512]{1,0:T(8,128)S(1)} collective-permute-done((f32[128,512]{1,0:T(8,128)S(1)}, f32[128,512]{1,0:T(8,128)S(1)}, u32[]{:S(2)}, u32[]{:S(2)}) %collective-permute-start.7) | collective-permute-done | bytes 262176 | tf_op jit(solution)/shard_map/ppermute | solution.py:132
  24.0 0.0 copy-done
  24.0 0.7 %down.1 = (f32[16,4096]{1,0:T(8,128)S(1)}, bf16[16,4096]{1,0:T(8,128)(2,1)S(1)}, bf16[16,4096]{1,0:T(8,128)(2,1)S(1)}, bf16[16,4096]{1,0:T(8,128)(2,1)S(1)}, f32...) custom-call(f32[128,512]{1,0:T(8,128)S(1)} %project.2.gate_ref, ...), custom_call_target="tpu_custom_call" | custom-call | flops 536870912 | tf_op jit(solution)/shard_map/down/pallas_call | solution.py:15
  24.7 1.1 %collective-permute-start.10 = (bf16[16,4096]{1,0:T(8,128)(2,1)S(1)}, bf16[16,4096]{1,0:T(8,128)(2,1)S(1)}, u32[]{:S(2)}, u32[]{:S(2)}) collective-permute-start(bf16[16,4096]{1,0:T(8,128)(2,1)S(1)} %get-tuple-element.30), channel_id=1, source_target_pairs={{0,4},{2,6},{4,0},{6,2},{8,12},{10,14},{12,8},{14,10},{1,5},{3,7},... | collective-permute-start | bytes 393224 | tf_op jit(solution)/shard_map/ppermute | solution.py:129
  25.8 1.5 %collective-permute-start.11 = (bf16[16,4096]{1,0:T(8,128)(2,1)S(1)}, bf16[16,4096]{1,0:T(8,128)(2,1)S(1)}, u32[]{:S(2)}, u32[]{:S(2)}) collective-permute-start(bf16[16,4096]{1,0:T(8,128)(2,1)S(1)} %get-tuple-element.31), channel_id=1, source_target_pairs={{0,6},{2,4},{4,2},{6,0},{8,14},{10,12},{12,10},{14,8},{1,7},{3,5},... | collective-permute-start | bytes 393224 | tf_op jit(solution)/shard_map/ppermute | solution.py:129
  27.3 0.9 %collective-permute-start.12 = (bf16[16,4096]{1,0:T(8,128)(2,1)S(1)}, bf16[16,4096]{1,0:T(8,128)(2,1)S(1)}, u32[]{:S(2)}, u32[]{:S(2)}) collective-permute-start(bf16[16,4096]{1,0:T(8,128)(2,1)S(1)} %get-tuple-element.32), channel_id=1, source_target_pairs={{0,2},{2,0},{4,6},{6,4},{8,10},{10,8},{12,14},{14,12},{1,3},{3,1},... | collective-permute-start | bytes 393224 | tf_op jit(solution)/shard_map/ppermute | solution.py:129
  28.3 1.0 %collective-permute-start.9 = (bf16[16,4096]{1,0:T(8,128)(2,1)S(1)}, bf16[16,4096]{1,0:T(8,128)(2,1)S(1)}, u32[]{:S(2)}, u32[]{:S(2)}) collective-permute-start(bf16[16,4096]{1,0:T(8,128)(2,1)S(1)} %get-tuple-element.28), channel_id=1, source_target_pairs={{0,4},{2,6},{4,0},{6,2},{8,12},{10,14},{12,8},{14,10},{1,5},{3,7},... | collective-permute-start | bytes 393224 | tf_op jit(solution)/shard_map/ppermute | solution.py:129
  29.3 1.8 %collective-permute-done.10.refs_0_ = bf16[16,4096]{1,0:T(8,128)(2,1)S(1)} collective-permute-done((bf16[16,4096]{1,0:T(8,128)(2,1)S(1)}, bf16[16,4096]{1,0:T(8,128)(2,1)S(1)}, u32[]{:S(2)}, u32[]{:S(2)}) %collective-permute-start.10) | collective-permute-done | bytes 131104 | tf_op jit(solution)/shard_map/ppermute | solution.py:129
  31.1 3.4 %collective-permute-done.11.refs_1_ = bf16[16,4096]{1,0:T(8,128)(2,1)S(1)} collective-permute-done((bf16[16,4096]{1,0:T(8,128)(2,1)S(1)}, bf16[16,4096]{1,0:T(8,128)(2,1)S(1)}, u32[]{:S(2)}, u32[]{:S(2)}) %collective-permute-start.11) | collective-permute-done | bytes 131104 | tf_op jit(solution)/shard_map/ppermute | solution.py:129
  34.5 0.9 %collective-permute-done.12.refs_2_ = bf16[16,4096]{1,0:T(8,128)(2,1)S(1)} collective-permute-done((bf16[16,4096]{1,0:T(8,128)(2,1)S(1)}, bf16[16,4096]{1,0:T(8,128)(2,1)S(1)}, u32[]{:S(2)}, u32[]{:S(2)}) %collective-permute-start.12) | collective-permute-done | bytes 131104 | tf_op jit(solution)/shard_map/ppermute | solution.py:129
  35.3 0.1 add.3
  35.4 1.5 %collective-permute-start.13 = (bf16[16,4096]{1,0:T(8,128)(2,1)S(1)}, bf16[16,4096]{1,0:T(8,128)(2,1)S(1)}, u32[]{:S(2)}, u32[]{:S(2)}) collective-permute-start(bf16[16,4096]{1,0:T(8,128)(2,1)S(1)} %add.3), channel_id=1, source_target_pairs={{0,8},{2,10},{4,12},{6,14},{8,0},{10,2},{12,4},{14,6},{1,9},{3,11}... | collective-permute-start | bytes 393224 | tf_op jit(solution)/shard_map/ppermute | solution.py:129
  36.9 1.9 %collective-permute-start.14 = (bf16[16,4096]{1,0:T(8,128)(2,1)S(1)}, bf16[16,4096]{1,0:T(8,128)(2,1)S(1)}, u32[]{:S(2)}, u32[]{:S(2)}) collective-permute-start(bf16[16,4096]{1,0:T(8,128)(2,1)S(1)} %get-tuple-element.35), channel_id=1, source_target_pairs={{0,6},{2,4},{4,2},{6,0},{8,14},{10,12},{12,10},{14,8},{1,7},{3,5},... | collective-permute-start | bytes 393224 | tf_op jit(solution)/shard_map/ppermute | solution.py:129
  38.8 1.2 %collective-permute-start.15 = (bf16[16,4096]{1,0:T(8,128)(2,1)S(1)}, bf16[16,4096]{1,0:T(8,128)(2,1)S(1)}, u32[]{:S(2)}, u32[]{:S(2)}) collective-permute-start(bf16[16,4096]{1,0:T(8,128)(2,1)S(1)} %get-tuple-element.36), channel_id=1, source_target_pairs={{0,2},{2,0},{4,6},{6,4},{8,10},{10,8},{12,14},{14,12},{1,3},{3,1},... | collective-permute-start | bytes 393224 | tf_op jit(solution)/shard_map/ppermute | solution.py:129
  40.0 0.0 collective-permute-done.9.refs_0_
  40.0 3.4 %collective-permute-done.13.refs_1_ = bf16[16,4096]{1,0:T(8,128)(2,1)S(1)} collective-permute-done((bf16[16,4096]{1,0:T(8,128)(2,1)S(1)}, bf16[16,4096]{1,0:T(8,128)(2,1)S(1)}, u32[]{:S(2)}, u32[]{:S(2)}) %collective-permute-start.13) | collective-permute-done | bytes 131104 | tf_op jit(solution)/shard_map/ppermute | solution.py:129
  43.5 0.8 %collective-permute-done.14.refs_0_ = bf16[16,4096]{1,0:T(8,128)(2,1)S(1)} collective-permute-done((bf16[16,4096]{1,0:T(8,128)(2,1)S(1)}, bf16[16,4096]{1,0:T(8,128)(2,1)S(1)}, u32[]{:S(2)}, u32[]{:S(2)}) %collective-permute-start.14) | collective-permute-done | bytes 131104 | tf_op jit(solution)/shard_map/ppermute | solution.py:129
  44.3 0.4 collective-permute-done.15.refs_1_
  44.7 0.7 %add.5 = bf16[16,4096]{1,0:T(8,128)(2,1)} custom-call(f32[16,4096]{1,0:T(8,128)S(1)} %add.4.own_ref, bf16[16,4096]{1,0:T(8,128)(2,1)S(1)} %collective-permute-done.14.refs_0_, bf16[16,4096]{1,0:T(8,128)(2,1)S(1)} %collective-permute-done.15.refs_1_), custom_call_target="tpu_custom_call" | custom-call | flops 1000000 | tf_op jit(solution)/shard_map/add/pallas_call | solution.py:114
  (2 shorter events, 0.1 us)
Async XLA Ops:
  0.0 19.2 %copy-start.1 = (bf16[16,4096]{1,0:T(8,128)(2,1)S(1)}, bf16[16,4096]{1,0:T(8,128)(2,1)}, u32[]{:S(2)}) copy-start(bf16[16,4096]{1,0:T(8,128)(2,1)} %refs_0_.3) | copy-start | bytes 393220
  0.0 10.6 %collective-permute-start = (bf16[16,4096]{1,0:T(8,128)(2,1)}, bf16[16,4096]{1,0:T(8,128)(2,1)S(1)}, u32[]{:S(2)}, u32[]{:S(2)}) collective-permute-start(bf16[16,4096]{1,0:T(8,128)(2,1)} %refs_0_.3), channel_id=1, source_target_pairs={{0,2},{2,0},{4,6},{6,4},{8,10},{10,8},{12,14},{14,12},{1,3},{3,1},... | collective-permute-start | bytes 393224 | tf_op jit(solution)/shard_map/ppermute | solution.py:129
  3.0 7.7 %collective-permute-start.1 = (bf16[16,4096]{1,0:T(8,128)(2,1)}, bf16[16,4096]{1,0:T(8,128)(2,1)S(1)}, u32[]{:S(2)}, u32[]{:S(2)}) collective-permute-start(bf16[16,4096]{1,0:T(8,128)(2,1)} %refs_0_.3), channel_id=1, source_target_pairs={{0,4},{2,6},{4,0},{6,2},{8,12},{10,14},{12,8},{14,10},{1,5},{3,7},... | collective-permute-start | bytes 393224 | tf_op jit(solution)/shard_map/ppermute | solution.py:129
  4.5 8.7 %collective-permute-start.3 = (bf16[16,4096]{1,0:T(8,128)(2,1)}, bf16[16,4096]{1,0:T(8,128)(2,1)S(1)}, u32[]{:S(2)}, u32[]{:S(2)}) collective-permute-start(bf16[16,4096]{1,0:T(8,128)(2,1)} %refs_0_.3), channel_id=1, source_target_pairs={{0,8},{2,10},{4,12},{6,14},{8,0},{10,2},{12,4},{14,6},{1,9},{3,11}... | collective-permute-start | bytes 393224 | tf_op jit(solution)/shard_map/ppermute | solution.py:129
  10.6 8.6 %collective-permute-start.2 = (bf16[16,4096]{1,0:T(8,128)(2,1)S(1)}, bf16[16,4096]{1,0:T(8,128)(2,1)S(1)}, u32[]{:S(2)}, u32[]{:S(2)}) collective-permute-start(bf16[16,4096]{1,0:T(8,128)(2,1)S(1)} %collective-permute-done.1.refs_1_), channel_id=1, source_target_pairs={{0,2},{2,0},{4,6},{6,4},{8,10},{10,8},{12,14},{14,12},{1,3},{3,1},... | collective-permute-start | bytes 393224 | tf_op jit(solution)/shard_map/ppermute | solution.py:129
  13.2 6.0 %collective-permute-start.4 = (bf16[16,4096]{1,0:T(8,128)(2,1)S(1)}, bf16[16,4096]{1,0:T(8,128)(2,1)S(1)}, u32[]{:S(2)}, u32[]{:S(2)}) collective-permute-start(bf16[16,4096]{1,0:T(8,128)(2,1)S(1)} %collective-permute-done.3.refs_1_), channel_id=1, source_target_pairs={{0,6},{2,4},{4,2},{6,0},{8,14},{10,12},{12,10},{14,8},{1,7},{3,5},... | collective-permute-start | bytes 393224 | tf_op jit(solution)/shard_map/ppermute | solution.py:129
  13.5 6.1 %collective-permute-start.5 = (bf16[16,4096]{1,0:T(8,128)(2,1)S(1)}, bf16[16,4096]{1,0:T(8,128)(2,1)S(1)}, u32[]{:S(2)}, u32[]{:S(2)}) collective-permute-start(bf16[16,4096]{1,0:T(8,128)(2,1)S(1)} %collective-permute-done.3.refs_1_), channel_id=1, source_target_pairs={{0,4},{2,6},{4,0},{6,2},{8,12},{10,14},{12,8},{14,10},{1,5},{3,7},... | collective-permute-start | bytes 393224 | tf_op jit(solution)/shard_map/ppermute | solution.py:129
  15.2 5.5 %collective-permute-start.6 = (bf16[16,4096]{1,0:T(8,128)(2,1)S(1)}, bf16[16,4096]{1,0:T(8,128)(2,1)S(1)}, u32[]{:S(2)}, u32[]{:S(2)}) collective-permute-start(bf16[16,4096]{1,0:T(8,128)(2,1)S(1)} %collective-permute-done.3.refs_1_), channel_id=1, source_target_pairs={{0,2},{2,0},{4,6},{6,4},{8,10},{10,8},{12,14},{14,12},{1,3},{3,1},... | collective-permute-start | bytes 393224 | tf_op jit(solution)/shard_map/ppermute | solution.py:129
  19.2 4.7 %copy-start = (bf16[512,4096]{1,0:T(8,128)(2,1)S(1)}, bf16[512,4096]{1,0:T(8,128)(2,1)}, u32[]{:S(2)}) copy-start(bf16[512,4096]{1,0:T(8,128)(2,1)} %weight_ref.1) | copy-start | bytes 12582916
  21.4 1.6 %collective-permute-start.8 = (f32[128,512]{1,0:T(8,128)S(1)}, f32[128,512]{1,0:T(8,128)S(1)}, u32[]{:S(2)}, u32[]{:S(2)}) collective-permute-start(f32[128,512]{1,0:T(8,128)S(1)} %project.3.up_ref), channel_id=1, source_target_pairs={{0,1},{1,0},{2,3},{3,2},{4,5},{5,4},{6,7},{7,6},{8,9},{9,8},{10,11... | collective-permute-start | bytes 786440 | tf_op jit(solution)/shard_map/ppermute | solution.py:132
  22.2 1.7 %collective-permute-start.7 = (f32[128,512]{1,0:T(8,128)S(1)}, f32[128,512]{1,0:T(8,128)S(1)}, u32[]{:S(2)}, u32[]{:S(2)}) collective-permute-start(f32[128,512]{1,0:T(8,128)S(1)} %project.2.gate_ref), channel_id=1, source_target_pairs={{0,1},{1,0},{2,3},{3,2},{4,5},{5,4},{6,7},{7,6},{8,9},{9,8},{10,11... | collective-permute-start | bytes 786440 | tf_op jit(solution)/shard_map/ppermute | solution.py:132
  24.7 6.4 %collective-permute-start.10 = (bf16[16,4096]{1,0:T(8,128)(2,1)S(1)}, bf16[16,4096]{1,0:T(8,128)(2,1)S(1)}, u32[]{:S(2)}, u32[]{:S(2)}) collective-permute-start(bf16[16,4096]{1,0:T(8,128)(2,1)S(1)} %get-tuple-element.30), channel_id=1, source_target_pairs={{0,4},{2,6},{4,0},{6,2},{8,12},{10,14},{12,8},{14,10},{1,5},{3,7},... | collective-permute-start | bytes 393224 | tf_op jit(solution)/shard_map/ppermute | solution.py:129
  25.8 8.7 %collective-permute-start.11 = (bf16[16,4096]{1,0:T(8,128)(2,1)S(1)}, bf16[16,4096]{1,0:T(8,128)(2,1)S(1)}, u32[]{:S(2)}, u32[]{:S(2)}) collective-permute-start(bf16[16,4096]{1,0:T(8,128)(2,1)S(1)} %get-tuple-element.31), channel_id=1, source_target_pairs={{0,6},{2,4},{4,2},{6,0},{8,14},{10,12},{12,10},{14,8},{1,7},{3,5},... | collective-permute-start | bytes 393224 | tf_op jit(solution)/shard_map/ppermute | solution.py:129
  27.3 8.0 %collective-permute-start.12 = (bf16[16,4096]{1,0:T(8,128)(2,1)S(1)}, bf16[16,4096]{1,0:T(8,128)(2,1)S(1)}, u32[]{:S(2)}, u32[]{:S(2)}) collective-permute-start(bf16[16,4096]{1,0:T(8,128)(2,1)S(1)} %get-tuple-element.32), channel_id=1, source_target_pairs={{0,2},{2,0},{4,6},{6,4},{8,10},{10,8},{12,14},{14,12},{1,3},{3,1},... | collective-permute-start | bytes 393224 | tf_op jit(solution)/shard_map/ppermute | solution.py:129
  28.3 11.7 %collective-permute-start.9 = (bf16[16,4096]{1,0:T(8,128)(2,1)S(1)}, bf16[16,4096]{1,0:T(8,128)(2,1)S(1)}, u32[]{:S(2)}, u32[]{:S(2)}) collective-permute-start(bf16[16,4096]{1,0:T(8,128)(2,1)S(1)} %get-tuple-element.28), channel_id=1, source_target_pairs={{0,4},{2,6},{4,0},{6,2},{8,12},{10,14},{12,8},{14,10},{1,5},{3,7},... | collective-permute-start | bytes 393224 | tf_op jit(solution)/shard_map/ppermute | solution.py:129
  35.4 8.0 %collective-permute-start.13 = (bf16[16,4096]{1,0:T(8,128)(2,1)S(1)}, bf16[16,4096]{1,0:T(8,128)(2,1)S(1)}, u32[]{:S(2)}, u32[]{:S(2)}) collective-permute-start(bf16[16,4096]{1,0:T(8,128)(2,1)S(1)} %add.3), channel_id=1, source_target_pairs={{0,8},{2,10},{4,12},{6,14},{8,0},{10,2},{12,4},{14,6},{1,9},{3,11}... | collective-permute-start | bytes 393224 | tf_op jit(solution)/shard_map/ppermute | solution.py:129
  36.9 7.4 %collective-permute-start.14 = (bf16[16,4096]{1,0:T(8,128)(2,1)S(1)}, bf16[16,4096]{1,0:T(8,128)(2,1)S(1)}, u32[]{:S(2)}, u32[]{:S(2)}) collective-permute-start(bf16[16,4096]{1,0:T(8,128)(2,1)S(1)} %get-tuple-element.35), channel_id=1, source_target_pairs={{0,6},{2,4},{4,2},{6,0},{8,14},{10,12},{12,10},{14,8},{1,7},{3,5},... | collective-permute-start | bytes 393224 | tf_op jit(solution)/shard_map/ppermute | solution.py:129
  38.8 5.9 %collective-permute-start.15 = (bf16[16,4096]{1,0:T(8,128)(2,1)S(1)}, bf16[16,4096]{1,0:T(8,128)(2,1)S(1)}, u32[]{:S(2)}, u32[]{:S(2)}) collective-permute-start(bf16[16,4096]{1,0:T(8,128)(2,1)S(1)} %get-tuple-element.36), channel_id=1, source_target_pairs={{0,2},{2,0},{4,6},{6,4},{8,10},{10,8},{12,14},{14,12},{1,3},{3,1},... | collective-permute-start | bytes 393224 | tf_op jit(solution)/shard_map/ppermute | solution.py:129

commit v15 on v13

--- a/solution.py
+++ b/solution.py
@@ -48,19 +48,6 @@
         cost_estimate=pl.CostEstimate(flops=4000000000, bytes_accessed=0, transcendentals=0),
         name="fetch",
     )(*weights)
-
-
-def pack_kernel(*refs):
-    *block_refs, out_ref = refs
-    rows = block_refs[0].shape[0]
-    for k, ref in enumerate(block_refs):
-        out_ref[k * rows:(k + 1) * rows, :] = ref[...]
-
-
-def pack(blocks):
-    rows, width = blocks[0].shape
-    out = jax.ShapeDtypeStruct((len(blocks) * rows, width), BF16)
-    return call(pack_kernel, "pack", out, 4000000000, 2 << 20, *blocks)
 
 
 def project_kernel(*refs):
@@ -139,19 +126,20 @@
         block[2] = swap(tokens, 2)
         block[1] = swap(tokens, 1)
         gate_held, up_held = fetch([gate_weight, up_weight])
-        block[1], block[2], gate_held, up_held = lax.optimization_barrier(
-            (block[1], block[2], gate_held, up_held)
+        first = [1, 2] + fars
+        *hops, gate_held, up_held = lax.optimization_barrier(
+            [block[b] for b in first] + [gate_held, up_held]
         )
+        block.update(zip(first, hops))
         block[3] = swap(block[2], 1)
         for far in fars:
             for near in (2, 3, 1):
                 block[far + near] = swap(block[far], near)
         stay = [0, 2] + fars
-        near_blocks = pack([block[b] for b in (0, 2, 1, 3)])
-        order = [0, 2, 1, 3] + [far + near for far in fars for near in (0, 3, 2, 1)]
-        far_blocks = [block[b] for b in order[4:]]
-        gate_part = project([near_blocks] + far_blocks, gate_held)
-        up_part = project([near_blocks] + far_blocks, up_held)
+        order = list(range(wide))
+        blocks = [block[b] for b in order]
+        gate_part = project(blocks, gate_held)
+        up_part = project(blocks, up_held)
         outs = down(
             gate_part, across_cores(gate_part), up_part, across_cores(up_part),
             down_weight, rows, [F32 if b in stay else BF16 for b in order],

time: 44.8 us -> 47.9 us (1.069)
  starting transfers between devices: 20.4 us -> 23.1 us
    ppermute x14, starting transfers between devices: 19.7 us -> 22.5 us  [swap(): return lax.ppermute(value, 'wide', [(i, i ^ bits) for i in range(wide)])]
    pallas_call x4 -> x3, Pallas kernels: 2.2 us -> 2.17 us  [call(): pl.pallas_call(kernel, out_shape=out_shape, compiler_params=pltpu.Compile...]
  transfers between devices with their start and end apart: 16 -> 16, of which waited for: 11 -> 12; matrix products, arithmetic and copies ran while one was open for 0% -> 0% of each run, Pallas kernels for 10% -> 9%
where the time goes in v15:
time: 47.9 us; the launch traced here: 47.7 us
  starting transfers between devices  23.1 us (48%)
  waiting for transfers between devices  18.1 us (38%)
  Pallas kernels  6.44 us (13%)
    ppermute x14, starting transfers between devices, swap(): return lax.ppermute(value, 'wide', [(i, i ^ bits) for i in range(wide)])  22.5 us
    ppermute x14, waiting for transfers between devices, swap(): return lax.ppermute(value, 'wide', [(i, i ^ bits) for i in range(wide)])  16.9 us
    pallas_call x1, Pallas kernels, fetch(): pl.pallas_call(functools.partial(fetch_kernel, pieces, count), in_specs=[...  3.47 us
    pallas_call x3, Pallas kernels, call(): pl.pallas_call(kernel, out_shape=out_shape, compiler_params=pltpu.Compile...  2.17 us
    ppermute x2, waiting for transfers between devices, across_cores(): lax.ppermute(value, 'narrow', [(i, (i + 1) % narrow) for i in range(narro...  1.16 us
  transfers between devices with their start and end apart: 16, of which 12 were waited for; matrix products, arithmetic and copies ran while one was open for 0% of the time, Pallas kernels for 9%

profile of v15, /device:TPU:0, one launch (start us, length us, event | category | flops | bytes accessed | tf_op | source)
XLA Modules:
  0.0 47.7 jit_solution(3355873462842679696)
XLA Ops:
  0.0 0.0 copy-start.1
  0.0 4.0 %collective-permute-start.2 = (bf16[16,4096]{1,0:T(8,128)(2,1)}, bf16[16,4096]{1,0:T(8,128)(2,1)S(1)}, u32[]{:S(2)}, u32[]{:S(2)}) collective-permute-start(bf16[16,4096]{1,0:T(8,128)(2,1)} %refs_0_.5), channel_id=1, source_target_pairs={{0,8},{2,10},{4,12},{6,14},{8,0},{10,2},{12,4},{14,6},{1,9},{3,11}... | collective-permute-start | bytes 393224 | tf_op jit(solution)/shard_map/ppermute | solution.py:116
  4.0 1.6 %collective-permute-start.1 = (bf16[16,4096]{1,0:T(8,128)(2,1)}, bf16[16,4096]{1,0:T(8,128)(2,1)S(1)}, u32[]{:S(2)}, u32[]{:S(2)}) collective-permute-start(bf16[16,4096]{1,0:T(8,128)(2,1)} %refs_0_.5), channel_id=1, source_target_pairs={{0,4},{2,6},{4,0},{6,2},{8,12},{10,14},{12,8},{14,10},{1,5},{3,7},... | collective-permute-start | bytes 393224 | tf_op jit(solution)/shard_map/ppermute | solution.py:116
  5.6 1.5 %collective-permute-start = (bf16[16,4096]{1,0:T(8,128)(2,1)}, bf16[16,4096]{1,0:T(8,128)(2,1)S(1)}, u32[]{:S(2)}, u32[]{:S(2)}) collective-permute-start(bf16[16,4096]{1,0:T(8,128)(2,1)} %refs_0_.5), channel_id=1, source_target_pairs={{0,2},{2,0},{4,6},{6,4},{8,10},{10,8},{12,14},{14,12},{1,3},{3,1},... | collective-permute-start | bytes 393224 | tf_op jit(solution)/shard_map/ppermute | solution.py:116
  7.1 3.5 %fetch.1 = (bf16[4096,512]{1,0:T(8,128)(2,1)S(1)}, bf16[4096,512]{1,0:T(8,128)(2,1)S(1)}) custom-call(bf16[4096,512]{1,0:T(8,128)(2,1)} %refs_0_.3, bf16[4096,512]{1,0:T(8,128)(2,1)} %refs_1_.1), custom_call_target="tpu_custom_call" | custom-call | flops 4000000000 | tf_op jit(solution)/shard_map/fetch/pallas_call | solution.py:41
  10.6 0.1 collective-permute-done.2.refs_4_
  10.7 0.2 collective-permute-done.1.refs_2_
  10.9 0.0 collective-permute-done.refs_1_
  10.9 0.0 copy-start
  10.9 1.5 %collective-permute-start.3 = (bf16[16,4096]{1,0:T(8,128)(2,1)S(1)}, bf16[16,4096]{1,0:T(8,128)(2,1)S(1)}, u32[]{:S(2)}, u32[]{:S(2)}) collective-permute-start(bf16[16,4096]{1,0:T(8,128)(2,1)S(1)} %collective-permute-done.1.refs_2_), channel_id=1, source_target_pairs={{0,2},{2,0},{4,6},{6,4},{8,10},{10,8},{12,14},{14,12},{1,3},{3,1},... | collective-permute-start | bytes 393224 | tf_op jit(solution)/shard_map/ppermute | solution.py:116
  12.4 1.3 %collective-permute-start.6 = (bf16[16,4096]{1,0:T(8,128)(2,1)S(1)}, bf16[16,4096]{1,0:T(8,128)(2,1)S(1)}, u32[]{:S(2)}, u32[]{:S(2)}) collective-permute-start(bf16[16,4096]{1,0:T(8,128)(2,1)S(1)} %collective-permute-done.2.refs_4_), channel_id=1, source_target_pairs={{0,6},{2,4},{4,2},{6,0},{8,14},{10,12},{12,10},{14,8},{1,7},{3,5},... | collective-permute-start | bytes 393224 | tf_op jit(solution)/shard_map/ppermute | solution.py:116
  13.8 0.6 %collective-permute-start.5 = (bf16[16,4096]{1,0:T(8,128)(2,1)S(1)}, bf16[16,4096]{1,0:T(8,128)(2,1)S(1)}, u32[]{:S(2)}, u32[]{:S(2)}) collective-permute-start(bf16[16,4096]{1,0:T(8,128)(2,1)S(1)} %collective-permute-done.2.refs_4_), channel_id=1, source_target_pairs={{0,4},{2,6},{4,0},{6,2},{8,12},{10,14},{12,8},{14,10},{1,5},{3,7},... | collective-permute-start | bytes 393224 | tf_op jit(solution)/shard_map/ppermute | solution.py:116
  14.4 1.5 %collective-permute-start.4 = (bf16[16,4096]{1,0:T(8,128)(2,1)S(1)}, bf16[16,4096]{1,0:T(8,128)(2,1)S(1)}, u32[]{:S(2)}, u32[]{:S(2)}) collective-permute-start(bf16[16,4096]{1,0:T(8,128)(2,1)S(1)} %collective-permute-done.2.refs_4_), channel_id=1, source_target_pairs={{0,2},{2,0},{4,6},{6,4},{8,10},{10,8},{12,14},{14,12},{1,3},{3,1},... | collective-permute-start | bytes 393224 | tf_op jit(solution)/shard_map/ppermute | solution.py:116
  15.9 3.6 %collective-permute-done.3.refs_3_ = bf16[16,4096]{1,0:T(8,128)(2,1)S(1)} collective-permute-done((bf16[16,4096]{1,0:T(8,128)(2,1)S(1)}, bf16[16,4096]{1,0:T(8,128)(2,1)S(1)}, u32[]{:S(2)}, u32[]{:S(2)}) %collective-permute-start.3) | collective-permute-done | bytes 131104 | tf_op jit(solution)/shard_map/ppermute | solution.py:116
  19.5 0.0 collective-permute-done.6.refs_7_
  19.5 0.0 collective-permute-done.5.refs_6_
  19.5 1.5 %collective-permute-done.4.refs_5_ = bf16[16,4096]{1,0:T(8,128)(2,1)S(1)} collective-permute-done((bf16[16,4096]{1,0:T(8,128)(2,1)S(1)}, bf16[16,4096]{1,0:T(8,128)(2,1)S(1)}, u32[]{:S(2)}, u32[]{:S(2)}) %collective-permute-start.4) | collective-permute-done | bytes 131104 | tf_op jit(solution)/shard_map/ppermute | solution.py:116
  21.0 0.0 copy-done.1
  21.0 0.7 %project.2.gate_ref = f32[128,512]{1,0:T(8,128)S(1)} custom-call(bf16[16,4096]{1,0:T(8,128)(2,1)S(1)} %copy-done.1, bf16[16,4096]{1,0:T(8,128)(2,1)S(1)} %collective-permute-done.refs_1_, bf16[16,4096]{1,0:T(8,128)(2,1)S(1)} %collective-permute-done.1.refs_2_, bf16[16,4096]{1,0:T(8,128)(2,1)S(1)} %collective-permute-done.3.refs_3_, ...), custom_call_target="tpu_custom_call" | custom-call | flops 400000000 | tf_op jit(solution)/shard_map/project/pallas_call | solution.py:15
  21.7 0.1 collective-permute-start.7
  21.8 0.7 %project.3.up_ref = f32[128,512]{1,0:T(8,128)S(1)} custom-call(bf16[16,4096]{1,0:T(8,128)(2,1)S(1)} %copy-done.1, bf16[16,4096]{1,0:T(8,128)(2,1)S(1)} %collective-permute-done.refs_1_, bf16[16,4096]{1,0:T(8,128)(2,1)S(1)} %collective-permute-done.1.refs_2_, bf16[16,4096]{1,0:T(8,128)(2,1)S(1)} %collective-permute-done.3.refs_3_, ...), custom_call_target="tpu_custom_call" | custom-call | flops 400000000 | tf_op jit(solution)/shard_map/project/pallas_call | solution.py:15
  22.5 0.6 %collective-permute-start.8 = (f32[128,512]{1,0:T(8,128)S(1)}, f32[128,512]{1,0:T(8,128)S(1)}, u32[]{:S(2)}, u32[]{:S(2)}) collective-permute-start(f32[128,512]{1,0:T(8,128)S(1)} %project.3.up_ref), channel_id=1, source_target_pairs={{0,1},{1,0},{2,3},{3,2},{4,5},{5,4},{6,7},{7,6},{8,9},{9,8},{10,11... | collective-permute-start | bytes 786440 | tf_op jit(solution)/shard_map/ppermute | solution.py:119
  23.1 0.2 collective-permute-done.7.gate_other_ref
  23.3 0.9 %collective-permute-done.8.up_other_ref = f32[128,512]{1,0:T(8,128)S(1)} collective-permute-done((f32[128,512]{1,0:T(8,128)S(1)}, f32[128,512]{1,0:T(8,128)S(1)}, u32[]{:S(2)}, u32[]{:S(2)}) %collective-permute-start.8) | collective-permute-done | bytes 262176 | tf_op jit(solution)/shard_map/ppermute | solution.py:119
  24.2 0.0 copy-done
  24.2 0.7 %down.1 = (f32[16,4096]{1,0:T(8,128)S(1)}, bf16[16,4096]{1,0:T(8,128)(2,1)S(1)}, f32[16,4096]{1,0:T(8,128)S(1)}, bf16[16,4096]{1,0:T(8,128)(2,1)S(1)}, f32[16,40...) custom-call(f32[128,512]{1,0:T(8,128)S(1)} %project.2.gate_ref, ...), custom_call_target="tpu_custom_call" | custom-call | flops 536870912 | tf_op jit(solution)/shard_map/down/pallas_call | solution.py:15
  25.0 2.0 %collective-permute-start.9 = (bf16[16,4096]{1,0:T(8,128)(2,1)S(1)}, bf16[16,4096]{1,0:T(8,128)(2,1)S(1)}, u32[]{:S(2)}, u32[]{:S(2)}) collective-permute-start(bf16[16,4096]{1,0:T(8,128)(2,1)S(1)} %get-tuple-element.31), channel_id=1, source_target_pairs={{0,4},{2,6},{4,0},{6,2},{8,12},{10,14},{12,8},{14,10},{1,5},{3,7},... | collective-permute-start | bytes 393224 | tf_op jit(solution)/shard_map/ppermute | solution.py:116
  27.0 0.7 %collective-permute-start.10 = (bf16[16,4096]{1,0:T(8,128)(2,1)S(1)}, bf16[16,4096]{1,0:T(8,128)(2,1)S(1)}, u32[]{:S(2)}, u32[]{:S(2)}) collective-permute-start(bf16[16,4096]{1,0:T(8,128)(2,1)S(1)} %get-tuple-element.32), channel_id=1, source_target_pairs={{0,6},{2,4},{4,2},{6,0},{8,14},{10,12},{12,10},{14,8},{1,7},{3,5},... | collective-permute-start | bytes 393224 | tf_op jit(solution)/shard_map/ppermute | solution.py:116
  27.6 0.9 %collective-permute-start.11 = (bf16[16,4096]{1,0:T(8,128)(2,1)S(1)}, bf16[16,4096]{1,0:T(8,128)(2,1)S(1)}, u32[]{:S(2)}, u32[]{:S(2)}) collective-permute-start(bf16[16,4096]{1,0:T(8,128)(2,1)S(1)} %get-tuple-element.33), channel_id=1, source_target_pairs={{0,2},{2,0},{4,6},{6,4},{8,10},{10,8},{12,14},{14,12},{1,3},{3,1},... | collective-permute-start | bytes 393224 | tf_op jit(solution)/shard_map/ppermute | solution.py:116
  28.5 1.1 %collective-permute-start.13 = (bf16[16,4096]{1,0:T(8,128)(2,1)S(1)}, bf16[16,4096]{1,0:T(8,128)(2,1)S(1)}, u32[]{:S(2)}, u32[]{:S(2)}) collective-permute-start(bf16[16,4096]{1,0:T(8,128)(2,1)S(1)} %get-tuple-element.36), channel_id=1, source_target_pairs={{0,2},{2,0},{4,6},{6,4},{8,10},{10,8},{12,14},{14,12},{1,3},{3,1},... | collective-permute-start | bytes 393224 | tf_op jit(solution)/shard_map/ppermute | solution.py:116
  29.6 1.7 %collective-permute-done.9.refs_0_ = bf16[16,4096]{1,0:T(8,128)(2,1)S(1)} collective-permute-done((bf16[16,4096]{1,0:T(8,128)(2,1)S(1)}, bf16[16,4096]{1,0:T(8,128)(2,1)S(1)}, u32[]{:S(2)}, u32[]{:S(2)}) %collective-permute-start.9) | collective-permute-done | bytes 131104 | tf_op jit(solution)/shard_map/ppermute | solution.py:116
  31.3 3.1 %collective-permute-done.10.refs_1_ = bf16[16,4096]{1,0:T(8,128)(2,1)S(1)} collective-permute-done((bf16[16,4096]{1,0:T(8,128)(2,1)S(1)}, bf16[16,4096]{1,0:T(8,128)(2,1)S(1)}, u32[]{:S(2)}, u32[]{:S(2)}) %collective-permute-start.10) | collective-permute-done | bytes 131104 | tf_op jit(solution)/shard_map/ppermute | solution.py:116
  34.5 2.3 %collective-permute-done.11.refs_2_ = bf16[16,4096]{1,0:T(8,128)(2,1)S(1)} collective-permute-done((bf16[16,4096]{1,0:T(8,128)(2,1)S(1)}, bf16[16,4096]{1,0:T(8,128)(2,1)S(1)}, u32[]{:S(2)}, u32[]{:S(2)}) %collective-permute-start.11) | collective-permute-done | bytes 131104 | tf_op jit(solution)/shard_map/ppermute | solution.py:116
  36.8 0.1 add.4.refs_1_
  36.8 3.3 %collective-permute-start.12 = (bf16[16,4096]{1,0:T(8,128)(2,1)S(1)}, bf16[16,4096]{1,0:T(8,128)(2,1)S(1)}, u32[]{:S(2)}, u32[]{:S(2)}) collective-permute-start(bf16[16,4096]{1,0:T(8,128)(2,1)S(1)} %add.4.refs_1_), channel_id=1, source_target_pairs={{0,8},{2,10},{4,12},{6,14},{8,0},{10,2},{12,4},{14,6},{1,9},{3,11}... | collective-permute-start | bytes 393224 | tf_op jit(solution)/shard_map/ppermute | solution.py:116
  40.2 0.0 collective-permute-done.13.refs_0_
  40.2 1.9 %collective-permute-start.14 = (bf16[16,4096]{1,0:T(8,128)(2,1)S(1)}, bf16[16,4096]{1,0:T(8,128)(2,1)S(1)}, u32[]{:S(2)}, u32[]{:S(2)}) collective-permute-start(bf16[16,4096]{1,0:T(8,128)(2,1)S(1)} %add.6), channel_id=1, source_target_pairs={{0,4},{2,6},{4,0},{6,2},{8,12},{10,14},{12,8},{14,10},{1,5},{3,7},... | collective-permute-start | bytes 393224 | tf_op jit(solution)/shard_map/ppermute | solution.py:116
  42.1 0.5 %collective-permute-start.15 = (bf16[16,4096]{1,0:T(8,128)(2,1)S(1)}, bf16[16,4096]{1,0:T(8,128)(2,1)S(1)}, u32[]{:S(2)}, u32[]{:S(2)}) collective-permute-start(bf16[16,4096]{1,0:T(8,128)(2,1)S(1)} %get-tuple-element.38), channel_id=1, source_target_pairs={{0,2},{2,0},{4,6},{6,4},{8,10},{10,8},{12,14},{14,12},{1,3},{3,1},... | collective-permute-start | bytes 393224 | tf_op jit(solution)/shard_map/ppermute | solution.py:116
  42.6 2.1 %collective-permute-done.12.refs_0_ = bf16[16,4096]{1,0:T(8,128)(2,1)S(1)} collective-permute-done((bf16[16,4096]{1,0:T(8,128)(2,1)S(1)}, bf16[16,4096]{1,0:T(8,128)(2,1)S(1)}, u32[]{:S(2)}, u32[]{:S(2)}) %collective-permute-start.12) | collective-permute-done | bytes 131104 | tf_op jit(solution)/shard_map/ppermute | solution.py:116
  44.7 1.0 %collective-permute-done.14.refs_0_ = bf16[16,4096]{1,0:T(8,128)(2,1)S(1)} collective-permute-done((bf16[16,4096]{1,0:T(8,128)(2,1)S(1)}, bf16[16,4096]{1,0:T(8,128)(2,1)S(1)}, u32[]{:S(2)}, u32[]{:S(2)}) %collective-permute-start.14) | collective-permute-done | bytes 131104 | tf_op jit(solution)/shard_map/ppermute | solution.py:116
  45.6 1.4 %collective-permute-done.15.refs_1_ = bf16[16,4096]{1,0:T(8,128)(2,1)S(1)} collective-permute-done((bf16[16,4096]{1,0:T(8,128)(2,1)S(1)}, bf16[16,4096]{1,0:T(8,128)(2,1)S(1)}, u32[]{:S(2)}, u32[]{:S(2)}) %collective-permute-start.15) | collective-permute-done | bytes 131104 | tf_op jit(solution)/shard_map/ppermute | solution.py:116
  47.0 0.7 %add.7 = bf16[16,4096]{1,0:T(8,128)(2,1)} custom-call(f32[16,4096]{1,0:T(8,128)S(1)} %add.5.own_ref, bf16[16,4096]{1,0:T(8,128)(2,1)S(1)} %collective-permute-done.14.refs_0_, bf16[16,4096]{1,0:T(8,128)(2,1)S(1)} %collective-permute-done.15.refs_1_), custom_call_target="tpu_custom_call" | custom-call | flops 1000000 | tf_op jit(solution)/shard_map/add/pallas_call | solution.py:101
  (2 shorter events, 0.0 us)
Async XLA Ops:
  0.0 21.0 %copy-start.1 = (bf16[16,4096]{1,0:T(8,128)(2,1)S(1)}, bf16[16,4096]{1,0:T(8,128)(2,1)}, u32[]{:S(2)}) copy-start(bf16[16,4096]{1,0:T(8,128)(2,1)} %refs_0_.5) | copy-start | bytes 393220
  0.0 10.7 %collective-permute-start.2 = (bf16[16,4096]{1,0:T(8,128)(2,1)}, bf16[16,4096]{1,0:T(8,128)(2,1)S(1)}, u32[]{:S(2)}, u32[]{:S(2)}) collective-permute-start(bf16[16,4096]{1,0:T(8,128)(2,1)} %refs_0_.5), channel_id=1, source_target_pairs={{0,8},{2,10},{4,12},{6,14},{8,0},{10,2},{12,4},{14,6},{1,9},{3,11}... | collective-permute-start | bytes 393224 | tf_op jit(solution)/shard_map/ppermute | solution.py:116
  4.0 6.9 %collective-permute-start.1 = (bf16[16,4096]{1,0:T(8,128)(2,1)}, bf16[16,4096]{1,0:T(8,128)(2,1)S(1)}, u32[]{:S(2)}, u32[]{:S(2)}) collective-permute-start(bf16[16,4096]{1,0:T(8,128)(2,1)} %refs_0_.5), channel_id=1, source_target_pairs={{0,4},{2,6},{4,0},{6,2},{8,12},{10,14},{12,8},{14,10},{1,5},{3,7},... | collective-permute-start | bytes 393224 | tf_op jit(solution)/shard_map/ppermute | solution.py:116
  5.6 5.3 %collective-permute-start = (bf16[16,4096]{1,0:T(8,128)(2,1)}, bf16[16,4096]{1,0:T(8,128)(2,1)S(1)}, u32[]{:S(2)}, u32[]{:S(2)}) collective-permute-start(bf16[16,4096]{1,0:T(8,128)(2,1)} %refs_0_.5), channel_id=1, source_target_pairs={{0,2},{2,0},{4,6},{6,4},{8,10},{10,8},{12,14},{14,12},{1,3},{3,1},... | collective-permute-start | bytes 393224 | tf_op jit(solution)/shard_map/ppermute | solution.py:116
  10.9 13.3 %copy-start = (bf16[512,4096]{1,0:T(8,128)(2,1)S(1)}, bf16[512,4096]{1,0:T(8,128)(2,1)}, u32[]{:S(2)}) copy-start(bf16[512,4096]{1,0:T(8,128)(2,1)} %weight_ref.1) | copy-start | bytes 12582916
  10.9 8.6 %collective-permute-start.3 = (bf16[16,4096]{1,0:T(8,128)(2,1)S(1)}, bf16[16,4096]{1,0:T(8,128)(2,1)S(1)}, u32[]{:S(2)}, u32[]{:S(2)}) collective-permute-start(bf16[16,4096]{1,0:T(8,128)(2,1)S(1)} %collective-permute-done.1.refs_2_), channel_id=1, source_target_pairs={{0,2},{2,0},{4,6},{6,4},{8,10},{10,8},{12,14},{14,12},{1,3},{3,1},... | collective-permute-start | bytes 393224 | tf_op jit(solution)/shard_map/ppermute | solution.py:116
  12.4 7.1 %collective-permute-start.6 = (bf16[16,4096]{1,0:T(8,128)(2,1)S(1)}, bf16[16,4096]{1,0:T(8,128)(2,1)S(1)}, u32[]{:S(2)}, u32[]{:S(2)}) collective-permute-start(bf16[16,4096]{1,0:T(8,128)(2,1)S(1)} %collective-permute-done.2.refs_4_), channel_id=1, source_target_pairs={{0,6},{2,4},{4,2},{6,0},{8,14},{10,12},{12,10},{14,8},{1,7},{3,5},... | collective-permute-start | bytes 393224 | tf_op jit(solution)/shard_map/ppermute | solution.py:116
  13.8 5.8 %collective-permute-start.5 = (bf16[16,4096]{1,0:T(8,128)(2,1)S(1)}, bf16[16,4096]{1,0:T(8,128)(2,1)S(1)}, u32[]{:S(2)}, u32[]{:S(2)}) collective-permute-start(bf16[16,4096]{1,0:T(8,128)(2,1)S(1)} %collective-permute-done.2.refs_4_), channel_id=1, source_target_pairs={{0,4},{2,6},{4,0},{6,2},{8,12},{10,14},{12,8},{14,10},{1,5},{3,7},... | collective-permute-start | bytes 393224 | tf_op jit(solution)/shard_map/ppermute | solution.py:116
  14.4 6.6 %collective-permute-start.4 = (bf16[16,4096]{1,0:T(8,128)(2,1)S(1)}, bf16[16,4096]{1,0:T(8,128)(2,1)S(1)}, u32[]{:S(2)}, u32[]{:S(2)}) collective-permute-start(bf16[16,4096]{1,0:T(8,128)(2,1)S(1)} %collective-permute-done.2.refs_4_), channel_id=1, source_target_pairs={{0,2},{2,0},{4,6},{6,4},{8,10},{10,8},{12,14},{14,12},{1,3},{3,1},... | collective-permute-start | bytes 393224 | tf_op jit(solution)/shard_map/ppermute | solution.py:116
  21.7 1.6 %collective-permute-start.7 = (f32[128,512]{1,0:T(8,128)S(1)}, f32[128,512]{1,0:T(8,128)S(1)}, u32[]{:S(2)}, u32[]{:S(2)}) collective-permute-start(f32[128,512]{1,0:T(8,128)S(1)} %project.2.gate_ref), channel_id=1, source_target_pairs={{0,1},{1,0},{2,3},{3,2},{4,5},{5,4},{6,7},{7,6},{8,9},{9,8},{10,11... | collective-permute-start | bytes 786440 | tf_op jit(solution)/shard_map/ppermute | solution.py:119
  22.5 1.7 %collective-permute-start.8 = (f32[128,512]{1,0:T(8,128)S(1)}, f32[128,512]{1,0:T(8,128)S(1)}, u32[]{:S(2)}, u32[]{:S(2)}) collective-permute-start(f32[128,512]{1,0:T(8,128)S(1)} %project.3.up_ref), channel_id=1, source_target_pairs={{0,1},{1,0},{2,3},{3,2},{4,5},{5,4},{6,7},{7,6},{8,9},{9,8},{10,11... | collective-permute-start | bytes 786440 | tf_op jit(solution)/shard_map/ppermute | solution.py:119
  25.0 6.4 %collective-permute-start.9 = (bf16[16,4096]{1,0:T(8,128)(2,1)S(1)}, bf16[16,4096]{1,0:T(8,128)(2,1)S(1)}, u32[]{:S(2)}, u32[]{:S(2)}) collective-permute-start(bf16[16,4096]{1,0:T(8,128)(2,1)S(1)} %get-tuple-element.31), channel_id=1, source_target_pairs={{0,4},{2,6},{4,0},{6,2},{8,12},{10,14},{12,8},{14,10},{1,5},{3,7},... | collective-permute-start | bytes 393224 | tf_op jit(solution)/shard_map/ppermute | solution.py:116
  27.0 7.5 %collective-permute-start.10 = (bf16[16,4096]{1,0:T(8,128)(2,1)S(1)}, bf16[16,4096]{1,0:T(8,128)(2,1)S(1)}, u32[]{:S(2)}, u32[]{:S(2)}) collective-permute-start(bf16[16,4096]{1,0:T(8,128)(2,1)S(1)} %get-tuple-element.32), channel_id=1, source_target_pairs={{0,6},{2,4},{4,2},{6,0},{8,14},{10,12},{12,10},{14,8},{1,7},{3,5},... | collective-permute-start | bytes 393224 | tf_op jit(solution)/shard_map/ppermute | solution.py:116
  27.6 9.2 %collective-permute-start.11 = (bf16[16,4096]{1,0:T(8,128)(2,1)S(1)}, bf16[16,4096]{1,0:T(8,128)(2,1)S(1)}, u32[]{:S(2)}, u32[]{:S(2)}) collective-permute-start(bf16[16,4096]{1,0:T(8,128)(2,1)S(1)} %get-tuple-element.33), channel_id=1, source_target_pairs={{0,2},{2,0},{4,6},{6,4},{8,10},{10,8},{12,14},{14,12},{1,3},{3,1},... | collective-permute-start | bytes 393224 | tf_op jit(solution)/shard_map/ppermute | solution.py:116
  28.5 11.6 %collective-permute-start.13 = (bf16[16,4096]{1,0:T(8,128)(2,1)S(1)}, bf16[16,4096]{1,0:T(8,128)(2,1)S(1)}, u32[]{:S(2)}, u32[]{:S(2)}) collective-permute-start(bf16[16,4096]{1,0:T(8,128)(2,1)S(1)} %get-tuple-element.36), channel_id=1, source_target_pairs={{0,2},{2,0},{4,6},{6,4},{8,10},{10,8},{12,14},{14,12},{1,3},{3,1},... | collective-permute-start | bytes 393224 | tf_op jit(solution)/shard_map/ppermute | solution.py:116
  36.8 7.8 %collective-permute-start.12 = (bf16[16,4096]{1,0:T(8,128)(2,1)S(1)}, bf16[16,4096]{1,0:T(8,128)(2,1)S(1)}, u32[]{:S(2)}, u32[]{:S(2)}) collective-permute-start(bf16[16,4096]{1,0:T(8,128)(2,1)S(1)} %add.4.refs_1_), channel_id=1, source_target_pairs={{0,8},{2,10},{4,12},{6,14},{8,0},{10,2},{12,4},{14,6},{1,9},{3,11}... | collective-permute-start | bytes 393224 | tf_op jit(solution)/shard_map/ppermute | solution.py:116
  40.2 5.4 %collective-permute-start.14 = (bf16[16,4096]{1,0:T(8,128)(2,1)S(1)}, bf16[16,4096]{1,0:T(8,128)(2,1)S(1)}, u32[]{:S(2)}, u32[]{:S(2)}) collective-permute-start(bf16[16,4096]{1,0:T(8,128)(2,1)S(1)} %add.6), channel_id=1, source_target_pairs={{0,4},{2,6},{4,0},{6,2},{8,12},{10,14},{12,8},{14,10},{1,5},{3,7},... | collective-permute-start | bytes 393224 | tf_op jit(solution)/shard_map/ppermute | solution.py:116
  42.1 5.0 %collective-permute-start.15 = (bf16[16,4096]{1,0:T(8,128)(2,1)S(1)}, bf16[16,4096]{1,0:T(8,128)(2,1)S(1)}, u32[]{:S(2)}, u32[]{:S(2)}) collective-permute-start(bf16[16,4096]{1,0:T(8,128)(2,1)S(1)} %get-tuple-element.38), channel_id=1, source_target_pairs={{0,2},{2,0},{4,6},{6,4},{8,10},{10,8},{12,14},{14,12},{1,3},{3,1},... | collective-permute-start | bytes 393224 | tf_op jit(solution)/shard_map/ppermute | solution.py:116

commit v16 on v15

--- a/solution.py
+++ b/solution.py
@@ -123,20 +123,18 @@
         block = {0: tokens}
         for far in fars:
             block[far] = swap(tokens, far)
-        block[2] = swap(tokens, 2)
-        block[1] = swap(tokens, 1)
+        for near in (1, 2, 3):
+            block[near] = swap(tokens, near)
         gate_held, up_held = fetch([gate_weight, up_weight])
-        first = [1, 2] + fars
-        *hops, gate_held, up_held = lax.optimization_barrier(
-            [block[b] for b in first] + [gate_held, up_held]
+        *crossed, gate_held, up_held = lax.optimization_barrier(
+            [block[far] for far in fars] + [gate_held, up_held]
         )
-        block.update(zip(first, hops))
-        block[3] = swap(block[2], 1)
+        block.update(zip(fars, crossed))
         for far in fars:
             for near in (2, 3, 1):
                 block[far + near] = swap(block[far], near)
         stay = [0, 2] + fars
-        order = list(range(wide))
+        order = [0, 3, 1, 2] + [far + near for far in fars for near in (0, 2, 1, 3)]
         blocks = [block[b] for b in order]
         gate_part = project(blocks, gate_held)
         up_part = project(blocks, up_held)
@@ -147,7 +145,7 @@
         part = dict(zip(order, outs))
         sums = []
         for far in fars:
-            quad = [swap(part[far + near], near) for near in (2, 3, 1)]
+            quad = [swap(part[far + near], near) for near in (3, 1, 2)]
             sums.append(add(part[far], quad, BF16))
         arrived = [swap(value, far) for value, far in zip(sums, fars)]
         pair = add(part[2], [swap(part[3], 1)], BF16, after=sums)

time: 47.9 us -> 45.2 us (0.944)
  starting transfers between devices: 23.1 us -> 19.8 us
  waiting for transfers between devices: 18.1 us -> 18.7 us
    ppermute x14, starting transfers between devices: 22.5 us -> 19.2 us  [swap(): return lax.ppermute(value, 'wide', [(i, i ^ bits) for i in range(wide)])]
    ppermute x14, waiting for transfers between devices: 16.9 us -> 17.5 us  [swap(): return lax.ppermute(value, 'wide', [(i, i ^ bits) for i in range(wide)])]
  transfers between devices with their start and end apart: 16 -> 16, of which waited for: 12 -> 10; matrix products, arithmetic and copies ran while one was open for 0% -> 0% of each run, Pallas kernels for 9% -> 10%
where the time goes in v16:
time: 45.2 us; the launch traced here: 45 us
  starting transfers between devices  19.8 us (44%)
  waiting for transfers between devices  18.7 us (41%)
  Pallas kernels  6.45 us (14%)
    ppermute x14, starting transfers between devices, swap(): return lax.ppermute(value, 'wide', [(i, i ^ bits) for i in range(wide)])  19.2 us
    ppermute x14, waiting for transfers between devices, swap(): return lax.ppermute(value, 'wide', [(i, i ^ bits) for i in range(wide)])  17.5 us
    pallas_call x1, Pallas kernels, fetch(): pl.pallas_call(functools.partial(fetch_kernel, pieces, count), in_specs=[...  3.47 us
    pallas_call x3, Pallas kernels, call(): pl.pallas_call(kernel, out_shape=out_shape, compiler_params=pltpu.Compile...  2.17 us
    ppermute x2, waiting for transfers between devices, across_cores(): lax.ppermute(value, 'narrow', [(i, (i + 1) % narrow) for i in range(narro...  1.16 us
  transfers between devices with their start and end apart: 16, of which 10 were waited for; matrix products, arithmetic and copies ran while one was open for 0% of the time, Pallas kernels for 10%

profile of v16, /device:TPU:0, one launch (start us, length us, event | category | flops | bytes accessed | tf_op | source)
XLA Modules:
  0.0 45.0 jit_solution(17695612180519332401)
XLA Ops:
  0.0 0.0 copy-start.1
  0.0 4.0 %collective-permute-start.3 = (bf16[16,4096]{1,0:T(8,128)(2,1)}, bf16[16,4096]{1,0:T(8,128)(2,1)S(1)}, u32[]{:S(2)}, u32[]{:S(2)}) collective-permute-start(bf16[16,4096]{1,0:T(8,128)(2,1)} %refs_0_.5), channel_id=1, source_target_pairs={{0,8},{2,10},{4,12},{6,14},{8,0},{10,2},{12,4},{14,6},{1,9},{3,11}... | collective-permute-start | bytes 393224 | tf_op jit(solution)/shard_map/ppermute | solution.py:116
  4.0 1.6 %collective-permute-start.2 = (bf16[16,4096]{1,0:T(8,128)(2,1)}, bf16[16,4096]{1,0:T(8,128)(2,1)S(1)}, u32[]{:S(2)}, u32[]{:S(2)}) collective-permute-start(bf16[16,4096]{1,0:T(8,128)(2,1)} %refs_0_.5), channel_id=1, source_target_pairs={{0,4},{2,6},{4,0},{6,2},{8,12},{10,14},{12,8},{14,10},{1,5},{3,7},... | collective-permute-start | bytes 393224 | tf_op jit(solution)/shard_map/ppermute | solution.py:116
  5.6 1.5 %collective-permute-start.1 = (bf16[16,4096]{1,0:T(8,128)(2,1)}, bf16[16,4096]{1,0:T(8,128)(2,1)S(1)}, u32[]{:S(2)}, u32[]{:S(2)}) collective-permute-start(bf16[16,4096]{1,0:T(8,128)(2,1)} %refs_0_.5), channel_id=1, source_target_pairs={{0,2},{2,0},{4,6},{6,4},{8,10},{10,8},{12,14},{14,12},{1,3},{3,1},... | collective-permute-start | bytes 393224 | tf_op jit(solution)/shard_map/ppermute | solution.py:116
  7.1 0.4 collective-permute-start
  7.5 3.5 %fetch.1 = (bf16[4096,512]{1,0:T(8,128)(2,1)S(1)}, bf16[4096,512]{1,0:T(8,128)(2,1)S(1)}) custom-call(bf16[4096,512]{1,0:T(8,128)(2,1)} %refs_0_.3, bf16[4096,512]{1,0:T(8,128)(2,1)} %refs_1_.1), custom_call_target="tpu_custom_call" | custom-call | flops 4000000000 | tf_op jit(solution)/shard_map/fetch/pallas_call | solution.py:41
  11.0 0.0 collective-permute-done.3.refs_4_
  11.0 0.0 copy-start
  11.0 2.6 %collective-permute-start.6 = (bf16[16,4096]{1,0:T(8,128)(2,1)S(1)}, bf16[16,4096]{1,0:T(8,128)(2,1)S(1)}, u32[]{:S(2)}, u32[]{:S(2)}) collective-permute-start(bf16[16,4096]{1,0:T(8,128)(2,1)S(1)} %collective-permute-done.3.refs_4_), channel_id=1, source_target_pairs={{0,6},{2,4},{4,2},{6,0},{8,14},{10,12},{12,10},{14,8},{1,7},{3,5},... | collective-permute-start | bytes 393224 | tf_op jit(solution)/shard_map/ppermute | solution.py:116
  13.6 0.5 %collective-permute-start.5 = (bf16[16,4096]{1,0:T(8,128)(2,1)S(1)}, bf16[16,4096]{1,0:T(8,128)(2,1)S(1)}, u32[]{:S(2)}, u32[]{:S(2)}) collective-permute-start(bf16[16,4096]{1,0:T(8,128)(2,1)S(1)} %collective-permute-done.3.refs_4_), channel_id=1, source_target_pairs={{0,2},{2,0},{4,6},{6,4},{8,10},{10,8},{12,14},{14,12},{1,3},{3,1},... | collective-permute-start | bytes 393224 | tf_op jit(solution)/shard_map/ppermute | solution.py:116
  14.1 0.0 collective-permute-done.2.refs_3_
  14.1 0.5 collective-permute-start.4
  14.6 0.0 collective-permute-done.1.refs_2_
  14.6 1.0 %collective-permute-done.refs_1_ = bf16[16,4096]{1,0:T(8,128)(2,1)S(1)} collective-permute-done((bf16[16,4096]{1,0:T(8,128)(2,1)}, bf16[16,4096]{1,0:T(8,128)(2,1)S(1)}, u32[]{:S(2)}, u32[]{:S(2)}) %collective-permute-start) | collective-permute-done | bytes 131104 | tf_op jit(solution)/shard_map/ppermute | solution.py:116
  15.6 2.9 %collective-permute-done.6.refs_7_ = bf16[16,4096]{1,0:T(8,128)(2,1)S(1)} collective-permute-done((bf16[16,4096]{1,0:T(8,128)(2,1)S(1)}, bf16[16,4096]{1,0:T(8,128)(2,1)S(1)}, u32[]{:S(2)}, u32[]{:S(2)}) %collective-permute-start.6) | collective-permute-done | bytes 131104 | tf_op jit(solution)/shard_map/ppermute | solution.py:116
  18.5 1.8 %collective-permute-done.5.refs_6_ = bf16[16,4096]{1,0:T(8,128)(2,1)S(1)} collective-permute-done((bf16[16,4096]{1,0:T(8,128)(2,1)S(1)}, bf16[16,4096]{1,0:T(8,128)(2,1)S(1)}, u32[]{:S(2)}, u32[]{:S(2)}) %collective-permute-start.5) | collective-permute-done | bytes 131104 | tf_op jit(solution)/shard_map/ppermute | solution.py:116
  20.3 0.0 collective-permute-done.4.refs_5_
  20.3 0.0 copy-done.1
  20.3 0.7 %project.2.gate_ref = f32[128,512]{1,0:T(8,128)S(1)} custom-call(bf16[16,4096]{1,0:T(8,128)(2,1)S(1)} %copy-done.1, bf16[16,4096]{1,0:T(8,128)(2,1)S(1)} %collective-permute-done.refs_1_, bf16[16,4096]{1,0:T(8,128)(2,1)S(1)} %collective-permute-done.1.refs_2_, bf16[16,4096]{1,0:T(8,128)(2,1)S(1)} %collective-permute-done.2.refs_3_, ...), custom_call_target="tpu_custom_call" | custom-call | flops 400000000 | tf_op jit(solution)/shard_map/project/pallas_call | solution.py:15
  21.0 0.1 collective-permute-start.7
  21.1 0.7 %project.3.up_ref = f32[128,512]{1,0:T(8,128)S(1)} custom-call(bf16[16,4096]{1,0:T(8,128)(2,1)S(1)} %copy-done.1, bf16[16,4096]{1,0:T(8,128)(2,1)S(1)} %collective-permute-done.refs_1_, bf16[16,4096]{1,0:T(8,128)(2,1)S(1)} %collective-permute-done.1.refs_2_, bf16[16,4096]{1,0:T(8,128)(2,1)S(1)} %collective-permute-done.2.refs_3_, ...), custom_call_target="tpu_custom_call" | custom-call | flops 400000000 | tf_op jit(solution)/shard_map/project/pallas_call | solution.py:15
  21.8 0.6 %collective-permute-start.8 = (f32[128,512]{1,0:T(8,128)S(1)}, f32[128,512]{1,0:T(8,128)S(1)}, u32[]{:S(2)}, u32[]{:S(2)}) collective-permute-start(f32[128,512]{1,0:T(8,128)S(1)} %project.3.up_ref), channel_id=1, source_target_pairs={{0,1},{1,0},{2,3},{3,2},{4,5},{5,4},{6,7},{7,6},{8,9},{9,8},{10,11... | collective-permute-start | bytes 786440 | tf_op jit(solution)/shard_map/ppermute | solution.py:119
  22.4 0.2 collective-permute-done.7.gate_other_ref
  22.6 0.9 %collective-permute-done.8.up_other_ref = f32[128,512]{1,0:T(8,128)S(1)} collective-permute-done((f32[128,512]{1,0:T(8,128)S(1)}, f32[128,512]{1,0:T(8,128)S(1)}, u32[]{:S(2)}, u32[]{:S(2)}) %collective-permute-start.8) | collective-permute-done | bytes 262176 | tf_op jit(solution)/shard_map/ppermute | solution.py:119
  23.5 0.0 copy-done
  23.5 0.7 %down.1 = (f32[16,4096]{1,0:T(8,128)S(1)}, bf16[16,4096]{1,0:T(8,128)(2,1)S(1)}, bf16[16,4096]{1,0:T(8,128)(2,1)S(1)}, f32[16,4096]{1,0:T(8,128)S(1)}, f32[16,40...) custom-call(f32[128,512]{1,0:T(8,128)S(1)} %project.2.gate_ref, ...), custom_call_target="tpu_custom_call" | custom-call | flops 536870912 | tf_op jit(solution)/shard_map/down/pallas_call | solution.py:15
  24.3 1.5 %collective-permute-start.9 = (bf16[16,4096]{1,0:T(8,128)(2,1)S(1)}, bf16[16,4096]{1,0:T(8,128)(2,1)S(1)}, u32[]{:S(2)}, u32[]{:S(2)}) collective-permute-start(bf16[16,4096]{1,0:T(8,128)(2,1)S(1)} %get-tuple-element.27), channel_id=1, source_target_pairs={{0,6},{2,4},{4,2},{6,0},{8,14},{10,12},{12,10},{14,8},{1,7},{3,5},... | collective-permute-start | bytes 393224 | tf_op jit(solution)/shard_map/ppermute | solution.py:116
  25.8 1.4 %collective-permute-start.10 = (bf16[16,4096]{1,0:T(8,128)(2,1)S(1)}, bf16[16,4096]{1,0:T(8,128)(2,1)S(1)}, u32[]{:S(2)}, u32[]{:S(2)}) collective-permute-start(bf16[16,4096]{1,0:T(8,128)(2,1)S(1)} %get-tuple-element.28), channel_id=1, source_target_pairs={{0,2},{2,0},{4,6},{6,4},{8,10},{10,8},{12,14},{14,12},{1,3},{3,1},... | collective-permute-start | bytes 393224 | tf_op jit(solution)/shard_map/ppermute | solution.py:116
  27.2 0.6 %collective-permute-start.11 = (bf16[16,4096]{1,0:T(8,128)(2,1)S(1)}, bf16[16,4096]{1,0:T(8,128)(2,1)S(1)}, u32[]{:S(2)}, u32[]{:S(2)}) collective-permute-start(bf16[16,4096]{1,0:T(8,128)(2,1)S(1)} %get-tuple-element.29), channel_id=1, source_target_pairs={{0,4},{2,6},{4,0},{6,2},{8,12},{10,14},{12,8},{14,10},{1,5},{3,7},... | collective-permute-start | bytes 393224 | tf_op jit(solution)/shard_map/ppermute | solution.py:116
  27.9 0.6 %collective-permute-start.13 = (bf16[16,4096]{1,0:T(8,128)(2,1)S(1)}, bf16[16,4096]{1,0:T(8,128)(2,1)S(1)}, u32[]{:S(2)}, u32[]{:S(2)}) collective-permute-start(bf16[16,4096]{1,0:T(8,128)(2,1)S(1)} %get-tuple-element.32), channel_id=1, source_target_pairs={{0,2},{2,0},{4,6},{6,4},{8,10},{10,8},{12,14},{14,12},{1,3},{3,1},... | collective-permute-start | bytes 393224 | tf_op jit(solution)/shard_map/ppermute | solution.py:116
  28.5 3.2 %collective-permute-done.9.refs_0_ = bf16[16,4096]{1,0:T(8,128)(2,1)S(1)} collective-permute-done((bf16[16,4096]{1,0:T(8,128)(2,1)S(1)}, bf16[16,4096]{1,0:T(8,128)(2,1)S(1)}, u32[]{:S(2)}, u32[]{:S(2)}) %collective-permute-start.9) | collective-permute-done | bytes 131104 | tf_op jit(solution)/shard_map/ppermute | solution.py:116
  31.6 2.3 %collective-permute-done.10.refs_1_ = bf16[16,4096]{1,0:T(8,128)(2,1)S(1)} collective-permute-done((bf16[16,4096]{1,0:T(8,128)(2,1)S(1)}, bf16[16,4096]{1,0:T(8,128)(2,1)S(1)}, u32[]{:S(2)}, u32[]{:S(2)}) %collective-permute-start.10) | collective-permute-done | bytes 131104 | tf_op jit(solution)/shard_map/ppermute | solution.py:116
  33.9 0.0 collective-permute-done.11.refs_2_
  33.9 0.1 add.4.refs_1_
  34.0 1.9 %collective-permute-start.12 = (bf16[16,4096]{1,0:T(8,128)(2,1)S(1)}, bf16[16,4096]{1,0:T(8,128)(2,1)S(1)}, u32[]{:S(2)}, u32[]{:S(2)}) collective-permute-start(bf16[16,4096]{1,0:T(8,128)(2,1)S(1)} %add.4.refs_1_), channel_id=1, source_target_pairs={{0,8},{2,10},{4,12},{6,14},{8,0},{10,2},{12,4},{14,6},{1,9},{3,11}... | collective-permute-start | bytes 393224 | tf_op jit(solution)/shard_map/ppermute | solution.py:116
  35.9 0.7 %collective-permute-done.13.refs_0_ = bf16[16,4096]{1,0:T(8,128)(2,1)S(1)} collective-permute-done((bf16[16,4096]{1,0:T(8,128)(2,1)S(1)}, bf16[16,4096]{1,0:T(8,128)(2,1)S(1)}, u32[]{:S(2)}, u32[]{:S(2)}) %collective-permute-start.13) | collective-permute-done | bytes 131104 | tf_op jit(solution)/shard_map/ppermute | solution.py:116
  36.7 1.0 %collective-permute-start.14 = (bf16[16,4096]{1,0:T(8,128)(2,1)S(1)}, bf16[16,4096]{1,0:T(8,128)(2,1)S(1)}, u32[]{:S(2)}, u32[]{:S(2)}) collective-permute-start(bf16[16,4096]{1,0:T(8,128)(2,1)S(1)} %add.6), channel_id=1, source_target_pairs={{0,4},{2,6},{4,0},{6,2},{8,12},{10,14},{12,8},{14,10},{1,5},{3,7},... | collective-permute-start | bytes 393224 | tf_op jit(solution)/shard_map/ppermute | solution.py:116
  37.6 1.1 %collective-permute-start.15 = (bf16[16,4096]{1,0:T(8,128)(2,1)S(1)}, bf16[16,4096]{1,0:T(8,128)(2,1)S(1)}, u32[]{:S(2)}, u32[]{:S(2)}) collective-permute-start(bf16[16,4096]{1,0:T(8,128)(2,1)S(1)} %get-tuple-element.34), channel_id=1, source_target_pairs={{0,2},{2,0},{4,6},{6,4},{8,10},{10,8},{12,14},{14,12},{1,3},{3,1},... | collective-permute-start | bytes 393224 | tf_op jit(solution)/shard_map/ppermute | solution.py:116
  38.7 4.3 %collective-permute-done.12.refs_0_ = bf16[16,4096]{1,0:T(8,128)(2,1)S(1)} collective-permute-done((bf16[16,4096]{1,0:T(8,128)(2,1)S(1)}, bf16[16,4096]{1,0:T(8,128)(2,1)S(1)}, u32[]{:S(2)}, u32[]{:S(2)}) %collective-permute-start.12) | collective-permute-done | bytes 131104 | tf_op jit(solution)/shard_map/ppermute | solution.py:116
  43.1 1.3 %collective-permute-done.14.refs_0_ = bf16[16,4096]{1,0:T(8,128)(2,1)S(1)} collective-permute-done((bf16[16,4096]{1,0:T(8,128)(2,1)S(1)}, bf16[16,4096]{1,0:T(8,128)(2,1)S(1)}, u32[]{:S(2)}, u32[]{:S(2)}) %collective-permute-start.14) | collective-permute-done | bytes 131104 | tf_op jit(solution)/shard_map/ppermute | solution.py:116
  44.3 0.0 collective-permute-done.15.refs_1_
  44.3 0.7 %add.7 = bf16[16,4096]{1,0:T(8,128)(2,1)} custom-call(f32[16,4096]{1,0:T(8,128)S(1)} %add.5.own_ref, bf16[16,4096]{1,0:T(8,128)(2,1)S(1)} %collective-permute-done.14.refs_0_, bf16[16,4096]{1,0:T(8,128)(2,1)S(1)} %collective-permute-done.15.refs_1_), custom_call_target="tpu_custom_call" | custom-call | flops 1000000 | tf_op jit(solution)/shard_map/add/pallas_call | solution.py:101
  (2 shorter events, 0.0 us)
Async XLA Ops:
  0.0 20.3 %copy-start.1 = (bf16[16,4096]{1,0:T(8,128)(2,1)S(1)}, bf16[16,4096]{1,0:T(8,128)(2,1)}, u32[]{:S(2)}) copy-start(bf16[16,4096]{1,0:T(8,128)(2,1)} %refs_0_.5) | copy-start | bytes 393220
  0.0 11.0 %collective-permute-start.3 = (bf16[16,4096]{1,0:T(8,128)(2,1)}, bf16[16,4096]{1,0:T(8,128)(2,1)S(1)}, u32[]{:S(2)}, u32[]{:S(2)}) collective-permute-start(bf16[16,4096]{1,0:T(8,128)(2,1)} %refs_0_.5), channel_id=1, source_target_pairs={{0,8},{2,10},{4,12},{6,14},{8,0},{10,2},{12,4},{14,6},{1,9},{3,11}... | collective-permute-start | bytes 393224 | tf_op jit(solution)/shard_map/ppermute | solution.py:116
  4.0 10.1 %collective-permute-start.2 = (bf16[16,4096]{1,0:T(8,128)(2,1)}, bf16[16,4096]{1,0:T(8,128)(2,1)S(1)}, u32[]{:S(2)}, u32[]{:S(2)}) collective-permute-start(bf16[16,4096]{1,0:T(8,128)(2,1)} %refs_0_.5), channel_id=1, source_target_pairs={{0,4},{2,6},{4,0},{6,2},{8,12},{10,14},{12,8},{14,10},{1,5},{3,7},... | collective-permute-start | bytes 393224 | tf_op jit(solution)/shard_map/ppermute | solution.py:116
  5.6 9.0 %collective-permute-start.1 = (bf16[16,4096]{1,0:T(8,128)(2,1)}, bf16[16,4096]{1,0:T(8,128)(2,1)S(1)}, u32[]{:S(2)}, u32[]{:S(2)}) collective-permute-start(bf16[16,4096]{1,0:T(8,128)(2,1)} %refs_0_.5), channel_id=1, source_target_pairs={{0,2},{2,0},{4,6},{6,4},{8,10},{10,8},{12,14},{14,12},{1,3},{3,1},... | collective-permute-start | bytes 393224 | tf_op jit(solution)/shard_map/ppermute | solution.py:116
  7.1 8.4 %collective-permute-start = (bf16[16,4096]{1,0:T(8,128)(2,1)}, bf16[16,4096]{1,0:T(8,128)(2,1)S(1)}, u32[]{:S(2)}, u32[]{:S(2)}) collective-permute-start(bf16[16,4096]{1,0:T(8,128)(2,1)} %refs_0_.5), channel_id=1, source_target_pairs={{0,6},{2,4},{4,2},{6,0},{8,14},{10,12},{12,10},{14,8},{1,7},{3,5},... | collective-permute-start | bytes 393224 | tf_op jit(solution)/shard_map/ppermute | solution.py:116
  11.0 12.5 %copy-start = (bf16[512,4096]{1,0:T(8,128)(2,1)S(1)}, bf16[512,4096]{1,0:T(8,128)(2,1)}, u32[]{:S(2)}) copy-start(bf16[512,4096]{1,0:T(8,128)(2,1)} %weight_ref.1) | copy-start | bytes 12582916
  11.0 7.4 %collective-permute-start.6 = (bf16[16,4096]{1,0:T(8,128)(2,1)S(1)}, bf16[16,4096]{1,0:T(8,128)(2,1)S(1)}, u32[]{:S(2)}, u32[]{:S(2)}) collective-permute-start(bf16[16,4096]{1,0:T(8,128)(2,1)S(1)} %collective-permute-done.3.refs_4_), channel_id=1, source_target_pairs={{0,6},{2,4},{4,2},{6,0},{8,14},{10,12},{12,10},{14,8},{1,7},{3,5},... | collective-permute-start | bytes 393224 | tf_op jit(solution)/shard_map/ppermute | solution.py:116
  13.6 6.7 %collective-permute-start.5 = (bf16[16,4096]{1,0:T(8,128)(2,1)S(1)}, bf16[16,4096]{1,0:T(8,128)(2,1)S(1)}, u32[]{:S(2)}, u32[]{:S(2)}) collective-permute-start(bf16[16,4096]{1,0:T(8,128)(2,1)S(1)} %collective-permute-done.3.refs_4_), channel_id=1, source_target_pairs={{0,2},{2,0},{4,6},{6,4},{8,10},{10,8},{12,14},{14,12},{1,3},{3,1},... | collective-permute-start | bytes 393224 | tf_op jit(solution)/shard_map/ppermute | solution.py:116
  14.1 6.2 %collective-permute-start.4 = (bf16[16,4096]{1,0:T(8,128)(2,1)S(1)}, bf16[16,4096]{1,0:T(8,128)(2,1)S(1)}, u32[]{:S(2)}, u32[]{:S(2)}) collective-permute-start(bf16[16,4096]{1,0:T(8,128)(2,1)S(1)} %collective-permute-done.3.refs_4_), channel_id=1, source_target_pairs={{0,4},{2,6},{4,0},{6,2},{8,12},{10,14},{12,8},{14,10},{1,5},{3,7},... | collective-permute-start | bytes 393224 | tf_op jit(solution)/shard_map/ppermute | solution.py:116
  21.0 1.6 %collective-permute-start.7 = (f32[128,512]{1,0:T(8,128)S(1)}, f32[128,512]{1,0:T(8,128)S(1)}, u32[]{:S(2)}, u32[]{:S(2)}) collective-permute-start(f32[128,512]{1,0:T(8,128)S(1)} %project.2.gate_ref), channel_id=1, source_target_pairs={{0,1},{1,0},{2,3},{3,2},{4,5},{5,4},{6,7},{7,6},{8,9},{9,8},{10,11... | collective-permute-start | bytes 786440 | tf_op jit(solution)/shard_map/ppermute | solution.py:119
  21.8 1.7 %collective-permute-start.8 = (f32[128,512]{1,0:T(8,128)S(1)}, f32[128,512]{1,0:T(8,128)S(1)}, u32[]{:S(2)}, u32[]{:S(2)}) collective-permute-start(f32[128,512]{1,0:T(8,128)S(1)} %project.3.up_ref), channel_id=1, source_target_pairs={{0,1},{1,0},{2,3},{3,2},{4,5},{5,4},{6,7},{7,6},{8,9},{9,8},{10,11... | collective-permute-start | bytes 786440 | tf_op jit(solution)/shard_map/ppermute | solution.py:119
  24.3 7.3 %collective-permute-start.9 = (bf16[16,4096]{1,0:T(8,128)(2,1)S(1)}, bf16[16,4096]{1,0:T(8,128)(2,1)S(1)}, u32[]{:S(2)}, u32[]{:S(2)}) collective-permute-start(bf16[16,4096]{1,0:T(8,128)(2,1)S(1)} %get-tuple-element.27), channel_id=1, source_target_pairs={{0,6},{2,4},{4,2},{6,0},{8,14},{10,12},{12,10},{14,8},{1,7},{3,5},... | collective-permute-start | bytes 393224 | tf_op jit(solution)/shard_map/ppermute | solution.py:116
  25.8 8.1 %collective-permute-start.10 = (bf16[16,4096]{1,0:T(8,128)(2,1)S(1)}, bf16[16,4096]{1,0:T(8,128)(2,1)S(1)}, u32[]{:S(2)}, u32[]{:S(2)}) collective-permute-start(bf16[16,4096]{1,0:T(8,128)(2,1)S(1)} %get-tuple-element.28), channel_id=1, source_target_pairs={{0,2},{2,0},{4,6},{6,4},{8,10},{10,8},{12,14},{14,12},{1,3},{3,1},... | collective-permute-start | bytes 393224 | tf_op jit(solution)/shard_map/ppermute | solution.py:116
  27.2 6.7 %collective-permute-start.11 = (bf16[16,4096]{1,0:T(8,128)(2,1)S(1)}, bf16[16,4096]{1,0:T(8,128)(2,1)S(1)}, u32[]{:S(2)}, u32[]{:S(2)}) collective-permute-start(bf16[16,4096]{1,0:T(8,128)(2,1)S(1)} %get-tuple-element.29), channel_id=1, source_target_pairs={{0,4},{2,6},{4,0},{6,2},{8,12},{10,14},{12,8},{14,10},{1,5},{3,7},... | collective-permute-start | bytes 393224 | tf_op jit(solution)/shard_map/ppermute | solution.py:116
  27.9 8.8 %collective-permute-start.13 = (bf16[16,4096]{1,0:T(8,128)(2,1)S(1)}, bf16[16,4096]{1,0:T(8,128)(2,1)S(1)}, u32[]{:S(2)}, u32[]{:S(2)}) collective-permute-start(bf16[16,4096]{1,0:T(8,128)(2,1)S(1)} %get-tuple-element.32), channel_id=1, source_target_pairs={{0,2},{2,0},{4,6},{6,4},{8,10},{10,8},{12,14},{14,12},{1,3},{3,1},... | collective-permute-start | bytes 393224 | tf_op jit(solution)/shard_map/ppermute | solution.py:116
  34.0 9.0 %collective-permute-start.12 = (bf16[16,4096]{1,0:T(8,128)(2,1)S(1)}, bf16[16,4096]{1,0:T(8,128)(2,1)S(1)}, u32[]{:S(2)}, u32[]{:S(2)}) collective-permute-start(bf16[16,4096]{1,0:T(8,128)(2,1)S(1)} %add.4.refs_1_), channel_id=1, source_target_pairs={{0,8},{2,10},{4,12},{6,14},{8,0},{10,2},{12,4},{14,6},{1,9},{3,11}... | collective-permute-start | bytes 393224 | tf_op jit(solution)/shard_map/ppermute | solution.py:116
  36.7 7.7 %collective-permute-start.14 = (bf16[16,4096]{1,0:T(8,128)(2,1)S(1)}, bf16[16,4096]{1,0:T(8,128)(2,1)S(1)}, u32[]{:S(2)}, u32[]{:S(2)}) collective-permute-start(bf16[16,4096]{1,0:T(8,128)(2,1)S(1)} %add.6), channel_id=1, source_target_pairs={{0,4},{2,6},{4,0},{6,2},{8,12},{10,14},{12,8},{14,10},{1,5},{3,7},... | collective-permute-start | bytes 393224 | tf_op jit(solution)/shard_map/ppermute | solution.py:116
  37.6 6.7 %collective-permute-start.15 = (bf16[16,4096]{1,0:T(8,128)(2,1)S(1)}, bf16[16,4096]{1,0:T(8,128)(2,1)S(1)}, u32[]{:S(2)}, u32[]{:S(2)}) collective-permute-start(bf16[16,4096]{1,0:T(8,128)(2,1)S(1)} %get-tuple-element.34), channel_id=1, source_target_pairs={{0,2},{2,0},{4,6},{6,4},{8,10},{10,8},{12,14},{14,12},{1,3},{3,1},... | collective-permute-start | bytes 393224 | tf_op jit(solution)/shard_map/ppermute | solution.py:116

commit v17 on v16

--- a/solution.py
+++ b/solution.py
@@ -51,20 +51,22 @@
 
 
 def project_kernel(*refs):
-    *block_refs, weight_ref, out_ref = refs
+    *block_refs, weight_ref, out_ref, sent_ref = refs
     rows = jnp.concatenate([ref[...] for ref in block_refs], axis=0)
-    out_ref[...] = jnp.dot(rows, weight_ref[...], preferred_element_type=F32)
+    partial = jnp.dot(rows, weight_ref[...], preferred_element_type=F32)
+    out_ref[...] = partial
+    sent_ref[...] = partial.astype(BF16)
 
 
 def project(blocks, weight):
-    rows = sum(block.shape[0] for block in blocks)
-    out = jax.ShapeDtypeStruct((rows, weight.shape[1]), F32)
-    return call(project_kernel, "project", out, 400000000, 4 << 20, *blocks, weight)
+    shape = (sum(block.shape[0] for block in blocks), weight.shape[1])
+    outs = [jax.ShapeDtypeStruct(shape, F32), jax.ShapeDtypeStruct(shape, BF16)]
+    return call(project_kernel, "project", outs, 400000000, 4 << 20, *blocks, weight)
 
 
 def down_kernel(gate_ref, gate_other_ref, up_ref, up_other_ref, weight_ref, *out_refs):
-    gate_sum = gate_ref[...] + gate_other_ref[...]
-    up_sum = up_ref[...] + up_other_ref[...]
+    gate_sum = gate_ref[...] + gate_other_ref[...].astype(F32)
+    up_sum = up_ref[...] + up_other_ref[...].astype(F32)
     hidden = (jax.nn.silu(gate_sum) * up_sum).astype(BF16)
     width = weight_ref.shape[1]
     tile = min(512, width)
@@ -136,10 +138,10 @@
         stay = [0, 2] + fars
         order = [0, 3, 1, 2] + [far + near for far in fars for near in (0, 2, 1, 3)]
         blocks = [block[b] for b in order]
-        gate_part = project(blocks, gate_held)
-        up_part = project(blocks, up_held)
+        gate_part, gate_sent = project(blocks, gate_held)
+        up_part, up_sent = project(blocks, up_held)
         outs = down(
-            gate_part, across_cores(gate_part), up_part, across_cores(up_part),
+            gate_part, across_cores(gate_sent), up_part, across_cores(up_sent),
             down_weight, rows, [F32 if b in stay else BF16 for b in order],
         )
         part = dict(zip(order, outs))

time: 45.2 us -> 45 us (level)
  transfers between devices with their start and end apart: 16 -> 16, of which waited for: 10 -> 9; matrix products, arithmetic and copies ran while one was open for 0% -> 0% of each run, Pallas kernels for 10% -> 10%
where the time goes in v17:
time: 45 us; the launch traced here: 44.9 us
  starting transfers between devices  19.8 us (44%)
  waiting for transfers between devices  18.5 us (41%)
  Pallas kernels  6.45 us (14%)
    ppermute x14, starting transfers between devices, swap(): return lax.ppermute(value, 'wide', [(i, i ^ bits) for i in range(wide)])  19.2 us
    ppermute x14, waiting for transfers between devices, swap(): return lax.ppermute(value, 'wide', [(i, i ^ bits) for i in range(wide)])  17.5 us
    pallas_call x1, Pallas kernels, fetch(): pl.pallas_call(functools.partial(fetch_kernel, pieces, count), in_specs=[...  3.47 us
    pallas_call x3, Pallas kernels, call(): pl.pallas_call(kernel, out_shape=out_shape, compiler_params=pltpu.Compile...  2.17 us
    ppermute x2, waiting for transfers between devices, across_cores(): lax.ppermute(value, 'narrow', [(i, (i + 1) % narrow) for i in range(narro...  0.99 us
  transfers between devices with their start and end apart: 16, of which 9 were waited for; matrix products, arithmetic and copies ran while one was open for 0% of the time, Pallas kernels for 10%

profile of v17, /device:TPU:0, one launch (start us, length us, event | category | flops | bytes accessed | tf_op | source)
XLA Modules:
  0.0 44.9 jit_solution(6062414033147760683)
XLA Ops:
  0.0 0.0 copy-start.1
  0.0 4.0 %collective-permute-start.3 = (bf16[16,4096]{1,0:T(8,128)(2,1)}, bf16[16,4096]{1,0:T(8,128)(2,1)S(1)}, u32[]{:S(2)}, u32[]{:S(2)}) collective-permute-start(bf16[16,4096]{1,0:T(8,128)(2,1)} %refs_0_.5), channel_id=1, source_target_pairs={{0,8},{2,10},{4,12},{6,14},{8,0},{10,2},{12,4},{14,6},{1,9},{3,11}... | collective-permute-start | bytes 393224 | tf_op jit(solution)/shard_map/ppermute | solution.py:118
  4.0 1.6 %collective-permute-start.2 = (bf16[16,4096]{1,0:T(8,128)(2,1)}, bf16[16,4096]{1,0:T(8,128)(2,1)S(1)}, u32[]{:S(2)}, u32[]{:S(2)}) collective-permute-start(bf16[16,4096]{1,0:T(8,128)(2,1)} %refs_0_.5), channel_id=1, source_target_pairs={{0,4},{2,6},{4,0},{6,2},{8,12},{10,14},{12,8},{14,10},{1,5},{3,7},... | collective-permute-start | bytes 393224 | tf_op jit(solution)/shard_map/ppermute | solution.py:118
  5.6 1.5 %collective-permute-start.1 = (bf16[16,4096]{1,0:T(8,128)(2,1)}, bf16[16,4096]{1,0:T(8,128)(2,1)S(1)}, u32[]{:S(2)}, u32[]{:S(2)}) collective-permute-start(bf16[16,4096]{1,0:T(8,128)(2,1)} %refs_0_.5), channel_id=1, source_target_pairs={{0,2},{2,0},{4,6},{6,4},{8,10},{10,8},{12,14},{14,12},{1,3},{3,1},... | collective-permute-start | bytes 393224 | tf_op jit(solution)/shard_map/ppermute | solution.py:118
  7.1 0.4 collective-permute-start
  7.5 3.5 %fetch.1 = (bf16[4096,512]{1,0:T(8,128)(2,1)S(1)}, bf16[4096,512]{1,0:T(8,128)(2,1)S(1)}) custom-call(bf16[4096,512]{1,0:T(8,128)(2,1)} %refs_0_.3, bf16[4096,512]{1,0:T(8,128)(2,1)} %refs_1_.1), custom_call_target="tpu_custom_call" | custom-call | flops 4000000000 | tf_op jit(solution)/shard_map/fetch/pallas_call | solution.py:41
  11.0 0.0 collective-permute-done.3.refs_4_
  11.0 0.0 copy-start
  11.0 2.6 %collective-permute-start.6 = (bf16[16,4096]{1,0:T(8,128)(2,1)S(1)}, bf16[16,4096]{1,0:T(8,128)(2,1)S(1)}, u32[]{:S(2)}, u32[]{:S(2)}) collective-permute-start(bf16[16,4096]{1,0:T(8,128)(2,1)S(1)} %collective-permute-done.3.refs_4_), channel_id=1, source_target_pairs={{0,6},{2,4},{4,2},{6,0},{8,14},{10,12},{12,10},{14,8},{1,7},{3,5},... | collective-permute-start | bytes 393224 | tf_op jit(solution)/shard_map/ppermute | solution.py:118
  13.6 0.5 %collective-permute-start.5 = (bf16[16,4096]{1,0:T(8,128)(2,1)S(1)}, bf16[16,4096]{1,0:T(8,128)(2,1)S(1)}, u32[]{:S(2)}, u32[]{:S(2)}) collective-permute-start(bf16[16,4096]{1,0:T(8,128)(2,1)S(1)} %collective-permute-done.3.refs_4_), channel_id=1, source_target_pairs={{0,2},{2,0},{4,6},{6,4},{8,10},{10,8},{12,14},{14,12},{1,3},{3,1},... | collective-permute-start | bytes 393224 | tf_op jit(solution)/shard_map/ppermute | solution.py:118
  14.1 0.0 collective-permute-done.2.refs_3_
  14.1 0.5 %collective-permute-start.4 = (bf16[16,4096]{1,0:T(8,128)(2,1)S(1)}, bf16[16,4096]{1,0:T(8,128)(2,1)S(1)}, u32[]{:S(2)}, u32[]{:S(2)}) collective-permute-start(bf16[16,4096]{1,0:T(8,128)(2,1)S(1)} %collective-permute-done.3.refs_4_), channel_id=1, source_target_pairs={{0,4},{2,6},{4,0},{6,2},{8,12},{10,14},{12,8},{14,10},{1,5},{3,7},... | collective-permute-start | bytes 393224 | tf_op jit(solution)/shard_map/ppermute | solution.py:118
  14.6 0.0 collective-permute-done.1.refs_2_
  14.6 1.0 %collective-permute-done.refs_1_ = bf16[16,4096]{1,0:T(8,128)(2,1)S(1)} collective-permute-done((bf16[16,4096]{1,0:T(8,128)(2,1)}, bf16[16,4096]{1,0:T(8,128)(2,1)S(1)}, u32[]{:S(2)}, u32[]{:S(2)}) %collective-permute-start) | collective-permute-done | bytes 131104 | tf_op jit(solution)/shard_map/ppermute | solution.py:118
  15.6 2.9 %collective-permute-done.6.refs_7_ = bf16[16,4096]{1,0:T(8,128)(2,1)S(1)} collective-permute-done((bf16[16,4096]{1,0:T(8,128)(2,1)S(1)}, bf16[16,4096]{1,0:T(8,128)(2,1)S(1)}, u32[]{:S(2)}, u32[]{:S(2)}) %collective-permute-start.6) | collective-permute-done | bytes 131104 | tf_op jit(solution)/shard_map/ppermute | solution.py:118
  18.5 1.8 %collective-permute-done.5.refs_6_ = bf16[16,4096]{1,0:T(8,128)(2,1)S(1)} collective-permute-done((bf16[16,4096]{1,0:T(8,128)(2,1)S(1)}, bf16[16,4096]{1,0:T(8,128)(2,1)S(1)}, u32[]{:S(2)}, u32[]{:S(2)}) %collective-permute-start.5) | collective-permute-done | bytes 131104 | tf_op jit(solution)/shard_map/ppermute | solution.py:118
  20.3 0.0 collective-permute-done.4.refs_5_
  20.3 0.0 copy-done.1
  20.3 0.7 %project.3 = (f32[128,512]{1,0:T(8,128)S(1)}, bf16[128,512]{1,0:T(8,128)(2,1)S(1)}) custom-call(bf16[16,4096]{1,0:T(8,128)(2,1)S(1)} %copy-done.1, bf16[16,4096]{1,0:T(8,128)(2,1)S(1)} %collective-permute-done.refs_1_, bf16[16,4096]{1,0:T(8,128)(2,1)S(1)} %collective-permute-done.1.refs_2_, bf16[16,4096]{1,0:T(8,128)(2,1)S(1)} %collective-permute-done.2.refs_3_, ...), custom_call_target="tpu_custom_call" | custom-call | flops 400000000 | tf_op jit(solution)/shard_map/project/pallas_call | solution.py:15
  21.0 0.1 collective-permute-start.8
  21.1 0.7 %project.2 = (f32[128,512]{1,0:T(8,128)S(1)}, bf16[128,512]{1,0:T(8,128)(2,1)S(1)}) custom-call(bf16[16,4096]{1,0:T(8,128)(2,1)S(1)} %copy-done.1, bf16[16,4096]{1,0:T(8,128)(2,1)S(1)} %collective-permute-done.refs_1_, bf16[16,4096]{1,0:T(8,128)(2,1)S(1)} %collective-permute-done.1.refs_2_, bf16[16,4096]{1,0:T(8,128)(2,1)S(1)} %collective-permute-done.2.refs_3_, ...), custom_call_target="tpu_custom_call" | custom-call | flops 400000000 | tf_op jit(solution)/shard_map/project/pallas_call | solution.py:15
  21.8 0.6 %collective-permute-start.7 = (bf16[128,512]{1,0:T(8,128)(2,1)S(1)}, bf16[128,512]{1,0:T(8,128)(2,1)S(1)}, u32[]{:S(2)}, u32[]{:S(2)}) collective-permute-start(bf16[128,512]{1,0:T(8,128)(2,1)S(1)} %get-tuple-element.29), channel_id=1, source_target_pairs={{0,1},{1,0},{2,3},{3,2},{4,5},{5,4},{6,7},{7,6},{8,9},{9,8},{10,11... | collective-permute-start | bytes 393224 | tf_op jit(solution)/shard_map/ppermute | solution.py:121
  22.4 0.1 collective-permute-done.8.up_other_ref
  22.4 0.9 %collective-permute-done.7.gate_other_ref = bf16[128,512]{1,0:T(8,128)(2,1)S(1)} collective-permute-done((bf16[128,512]{1,0:T(8,128)(2,1)S(1)}, bf16[128,512]{1,0:T(8,128)(2,1)S(1)}, u32[]{:S(2)}, u32[]{:S(2)}) %collective-permute-start.7) | collective-permute-done | bytes 131104 | tf_op jit(solution)/shard_map/ppermute | solution.py:121
  23.4 0.0 copy-done
  23.4 0.7 %down.1 = (f32[16,4096]{1,0:T(8,128)S(1)}, bf16[16,4096]{1,0:T(8,128)(2,1)S(1)}, bf16[16,4096]{1,0:T(8,128)(2,1)S(1)}, f32[16,4096]{1,0:T(8,128)S(1)}, f32[16,40...) custom-call(f32[128,512]{1,0:T(8,128)S(1)} %get-tuple-element.28.gate, ...), custom_call_target="tpu_custom_call" | custom-call | flops 536870912 | tf_op jit(solution)/shard_map/down/pallas_call | solution.py:15
  24.1 1.5 %collective-permute-start.9 = (bf16[16,4096]{1,0:T(8,128)(2,1)S(1)}, bf16[16,4096]{1,0:T(8,128)(2,1)S(1)}, u32[]{:S(2)}, u32[]{:S(2)}) collective-permute-start(bf16[16,4096]{1,0:T(8,128)(2,1)S(1)} %get-tuple-element.35), channel_id=1, source_target_pairs={{0,6},{2,4},{4,2},{6,0},{8,14},{10,12},{12,10},{14,8},{1,7},{3,5},... | collective-permute-start | bytes 393224 | tf_op jit(solution)/shard_map/ppermute | solution.py:118
  25.6 1.4 %collective-permute-start.10 = (bf16[16,4096]{1,0:T(8,128)(2,1)S(1)}, bf16[16,4096]{1,0:T(8,128)(2,1)S(1)}, u32[]{:S(2)}, u32[]{:S(2)}) collective-permute-start(bf16[16,4096]{1,0:T(8,128)(2,1)S(1)} %get-tuple-element.36), channel_id=1, source_target_pairs={{0,2},{2,0},{4,6},{6,4},{8,10},{10,8},{12,14},{14,12},{1,3},{3,1},... | collective-permute-start | bytes 393224 | tf_op jit(solution)/shard_map/ppermute | solution.py:118
  27.0 0.6 %collective-permute-start.11 = (bf16[16,4096]{1,0:T(8,128)(2,1)S(1)}, bf16[16,4096]{1,0:T(8,128)(2,1)S(1)}, u32[]{:S(2)}, u32[]{:S(2)}) collective-permute-start(bf16[16,4096]{1,0:T(8,128)(2,1)S(1)} %get-tuple-element.37), channel_id=1, source_target_pairs={{0,4},{2,6},{4,0},{6,2},{8,12},{10,14},{12,8},{14,10},{1,5},{3,7},... | collective-permute-start | bytes 393224 | tf_op jit(solution)/shard_map/ppermute | solution.py:118
  27.7 0.6 %collective-permute-start.13 = (bf16[16,4096]{1,0:T(8,128)(2,1)S(1)}, bf16[16,4096]{1,0:T(8,128)(2,1)S(1)}, u32[]{:S(2)}, u32[]{:S(2)}) collective-permute-start(bf16[16,4096]{1,0:T(8,128)(2,1)S(1)} %get-tuple-element.40), channel_id=1, source_target_pairs={{0,2},{2,0},{4,6},{6,4},{8,10},{10,8},{12,14},{14,12},{1,3},{3,1},... | collective-permute-start | bytes 393224 | tf_op jit(solution)/shard_map/ppermute | solution.py:118
  28.3 3.2 %collective-permute-done.9.refs_0_ = bf16[16,4096]{1,0:T(8,128)(2,1)S(1)} collective-permute-done((bf16[16,4096]{1,0:T(8,128)(2,1)S(1)}, bf16[16,4096]{1,0:T(8,128)(2,1)S(1)}, u32[]{:S(2)}, u32[]{:S(2)}) %collective-permute-start.9) | collective-permute-done | bytes 131104 | tf_op jit(solution)/shard_map/ppermute | solution.py:118
  31.5 2.3 %collective-permute-done.10.refs_1_ = bf16[16,4096]{1,0:T(8,128)(2,1)S(1)} collective-permute-done((bf16[16,4096]{1,0:T(8,128)(2,1)S(1)}, bf16[16,4096]{1,0:T(8,128)(2,1)S(1)}, u32[]{:S(2)}, u32[]{:S(2)}) %collective-permute-start.10) | collective-permute-done | bytes 131104 | tf_op jit(solution)/shard_map/ppermute | solution.py:118
  33.7 0.0 collective-permute-done.11.refs_2_
  33.7 0.1 add.4.refs_1_
  33.8 1.9 %collective-permute-start.12 = (bf16[16,4096]{1,0:T(8,128)(2,1)S(1)}, bf16[16,4096]{1,0:T(8,128)(2,1)S(1)}, u32[]{:S(2)}, u32[]{:S(2)}) collective-permute-start(bf16[16,4096]{1,0:T(8,128)(2,1)S(1)} %add.4.refs_1_), channel_id=1, source_target_pairs={{0,8},{2,10},{4,12},{6,14},{8,0},{10,2},{12,4},{14,6},{1,9},{3,11}... | collective-permute-start | bytes 393224 | tf_op jit(solution)/shard_map/ppermute | solution.py:118
  35.7 0.7 %collective-permute-done.13.refs_0_ = bf16[16,4096]{1,0:T(8,128)(2,1)S(1)} collective-permute-done((bf16[16,4096]{1,0:T(8,128)(2,1)S(1)}, bf16[16,4096]{1,0:T(8,128)(2,1)S(1)}, u32[]{:S(2)}, u32[]{:S(2)}) %collective-permute-start.13) | collective-permute-done | bytes 131104 | tf_op jit(solution)/shard_map/ppermute | solution.py:118
  36.5 1.0 %collective-permute-start.14 = (bf16[16,4096]{1,0:T(8,128)(2,1)S(1)}, bf16[16,4096]{1,0:T(8,128)(2,1)S(1)}, u32[]{:S(2)}, u32[]{:S(2)}) collective-permute-start(bf16[16,4096]{1,0:T(8,128)(2,1)S(1)} %add.6), channel_id=1, source_target_pairs={{0,4},{2,6},{4,0},{6,2},{8,12},{10,14},{12,8},{14,10},{1,5},{3,7},... | collective-permute-start | bytes 393224 | tf_op jit(solution)/shard_map/ppermute | solution.py:118
  37.5 1.1 %collective-permute-start.15 = (bf16[16,4096]{1,0:T(8,128)(2,1)S(1)}, bf16[16,4096]{1,0:T(8,128)(2,1)S(1)}, u32[]{:S(2)}, u32[]{:S(2)}) collective-permute-start(bf16[16,4096]{1,0:T(8,128)(2,1)S(1)} %get-tuple-element.42), channel_id=1, source_target_pairs={{0,2},{2,0},{4,6},{6,4},{8,10},{10,8},{12,14},{14,12},{1,3},{3,1},... | collective-permute-start | bytes 393224 | tf_op jit(solution)/shard_map/ppermute | solution.py:118
  38.5 4.3 %collective-permute-done.12.refs_0_ = bf16[16,4096]{1,0:T(8,128)(2,1)S(1)} collective-permute-done((bf16[16,4096]{1,0:T(8,128)(2,1)S(1)}, bf16[16,4096]{1,0:T(8,128)(2,1)S(1)}, u32[]{:S(2)}, u32[]{:S(2)}) %collective-permute-start.12) | collective-permute-done | bytes 131104 | tf_op jit(solution)/shard_map/ppermute | solution.py:118
  42.9 1.3 %collective-permute-done.14.refs_0_ = bf16[16,4096]{1,0:T(8,128)(2,1)S(1)} collective-permute-done((bf16[16,4096]{1,0:T(8,128)(2,1)S(1)}, bf16[16,4096]{1,0:T(8,128)(2,1)S(1)}, u32[]{:S(2)}, u32[]{:S(2)}) %collective-permute-start.14) | collective-permute-done | bytes 131104 | tf_op jit(solution)/shard_map/ppermute | solution.py:118
  44.1 0.0 collective-permute-done.15.refs_1_
  44.2 0.7 %add.7 = bf16[16,4096]{1,0:T(8,128)(2,1)} custom-call(f32[16,4096]{1,0:T(8,128)S(1)} %add.5.own_ref, bf16[16,4096]{1,0:T(8,128)(2,1)S(1)} %collective-permute-done.14.refs_0_, bf16[16,4096]{1,0:T(8,128)(2,1)S(1)} %collective-permute-done.15.refs_1_), custom_call_target="tpu_custom_call" | custom-call | flops 1000000 | tf_op jit(solution)/shard_map/add/pallas_call | solution.py:103
  (2 shorter events, 0.0 us)
Async XLA Ops:
  0.0 20.3 %copy-start.1 = (bf16[16,4096]{1,0:T(8,128)(2,1)S(1)}, bf16[16,4096]{1,0:T(8,128)(2,1)}, u32[]{:S(2)}) copy-start(bf16[16,4096]{1,0:T(8,128)(2,1)} %refs_0_.5) | copy-start | bytes 393220
  0.0 11.0 %collective-permute-start.3 = (bf16[16,4096]{1,0:T(8,128)(2,1)}, bf16[16,4096]{1,0:T(8,128)(2,1)S(1)}, u32[]{:S(2)}, u32[]{:S(2)}) collective-permute-start(bf16[16,4096]{1,0:T(8,128)(2,1)} %refs_0_.5), channel_id=1, source_target_pairs={{0,8},{2,10},{4,12},{6,14},{8,0},{10,2},{12,4},{14,6},{1,9},{3,11}... | collective-permute-start | bytes 393224 | tf_op jit(solution)/shard_map/ppermute | solution.py:118
  4.0 10.1 %collective-permute-start.2 = (bf16[16,4096]{1,0:T(8,128)(2,1)}, bf16[16,4096]{1,0:T(8,128)(2,1)S(1)}, u32[]{:S(2)}, u32[]{:S(2)}) collective-permute-start(bf16[16,4096]{1,0:T(8,128)(2,1)} %refs_0_.5), channel_id=1, source_target_pairs={{0,4},{2,6},{4,0},{6,2},{8,12},{10,14},{12,8},{14,10},{1,5},{3,7},... | collective-permute-start | bytes 393224 | tf_op jit(solution)/shard_map/ppermute | solution.py:118
  5.6 9.0 %collective-permute-start.1 = (bf16[16,4096]{1,0:T(8,128)(2,1)}, bf16[16,4096]{1,0:T(8,128)(2,1)S(1)}, u32[]{:S(2)}, u32[]{:S(2)}) collective-permute-start(bf16[16,4096]{1,0:T(8,128)(2,1)} %refs_0_.5), channel_id=1, source_target_pairs={{0,2},{2,0},{4,6},{6,4},{8,10},{10,8},{12,14},{14,12},{1,3},{3,1},... | collective-permute-start | bytes 393224 | tf_op jit(solution)/shard_map/ppermute | solution.py:118
  7.1 8.4 %collective-permute-start = (bf16[16,4096]{1,0:T(8,128)(2,1)}, bf16[16,4096]{1,0:T(8,128)(2,1)S(1)}, u32[]{:S(2)}, u32[]{:S(2)}) collective-permute-start(bf16[16,4096]{1,0:T(8,128)(2,1)} %refs_0_.5), channel_id=1, source_target_pairs={{0,6},{2,4},{4,2},{6,0},{8,14},{10,12},{12,10},{14,8},{1,7},{3,5},... | collective-permute-start | bytes 393224 | tf_op jit(solution)/shard_map/ppermute | solution.py:118
  11.0 12.4 %copy-start = (bf16[512,4096]{1,0:T(8,128)(2,1)S(1)}, bf16[512,4096]{1,0:T(8,128)(2,1)}, u32[]{:S(2)}) copy-start(bf16[512,4096]{1,0:T(8,128)(2,1)} %weight_ref.1) | copy-start | bytes 12582916
  11.0 7.4 %collective-permute-start.6 = (bf16[16,4096]{1,0:T(8,128)(2,1)S(1)}, bf16[16,4096]{1,0:T(8,128)(2,1)S(1)}, u32[]{:S(2)}, u32[]{:S(2)}) collective-permute-start(bf16[16,4096]{1,0:T(8,128)(2,1)S(1)} %collective-permute-done.3.refs_4_), channel_id=1, source_target_pairs={{0,6},{2,4},{4,2},{6,0},{8,14},{10,12},{12,10},{14,8},{1,7},{3,5},... | collective-permute-start | bytes 393224 | tf_op jit(solution)/shard_map/ppermute | solution.py:118
  13.6 6.7 %collective-permute-start.5 = (bf16[16,4096]{1,0:T(8,128)(2,1)S(1)}, bf16[16,4096]{1,0:T(8,128)(2,1)S(1)}, u32[]{:S(2)}, u32[]{:S(2)}) collective-permute-start(bf16[16,4096]{1,0:T(8,128)(2,1)S(1)} %collective-permute-done.3.refs_4_), channel_id=1, source_target_pairs={{0,2},{2,0},{4,6},{6,4},{8,10},{10,8},{12,14},{14,12},{1,3},{3,1},... | collective-permute-start | bytes 393224 | tf_op jit(solution)/shard_map/ppermute | solution.py:118
  14.1 6.2 %collective-permute-start.4 = (bf16[16,4096]{1,0:T(8,128)(2,1)S(1)}, bf16[16,4096]{1,0:T(8,128)(2,1)S(1)}, u32[]{:S(2)}, u32[]{:S(2)}) collective-permute-start(bf16[16,4096]{1,0:T(8,128)(2,1)S(1)} %collective-permute-done.3.refs_4_), channel_id=1, source_target_pairs={{0,4},{2,6},{4,0},{6,2},{8,12},{10,14},{12,8},{14,10},{1,5},{3,7},... | collective-permute-start | bytes 393224 | tf_op jit(solution)/shard_map/ppermute | solution.py:118
  21.0 1.4 %collective-permute-start.8 = (bf16[128,512]{1,0:T(8,128)(2,1)S(1)}, bf16[128,512]{1,0:T(8,128)(2,1)S(1)}, u32[]{:S(2)}, u32[]{:S(2)}) collective-permute-start(bf16[128,512]{1,0:T(8,128)(2,1)S(1)} %get-tuple-element.32), channel_id=1, source_target_pairs={{0,1},{1,0},{2,3},{3,2},{4,5},{5,4},{6,7},{7,6},{8,9},{9,8},{10,11... | collective-permute-start | bytes 393224 | tf_op jit(solution)/shard_map/ppermute | solution.py:121
  21.8 1.5 %collective-permute-start.7 = (bf16[128,512]{1,0:T(8,128)(2,1)S(1)}, bf16[128,512]{1,0:T(8,128)(2,1)S(1)}, u32[]{:S(2)}, u32[]{:S(2)}) collective-permute-start(bf16[128,512]{1,0:T(8,128)(2,1)S(1)} %get-tuple-element.29), channel_id=1, source_target_pairs={{0,1},{1,0},{2,3},{3,2},{4,5},{5,4},{6,7},{7,6},{8,9},{9,8},{10,11... | collective-permute-start | bytes 393224 | tf_op jit(solution)/shard_map/ppermute | solution.py:121
  24.1 7.3 %collective-permute-start.9 = (bf16[16,4096]{1,0:T(8,128)(2,1)S(1)}, bf16[16,4096]{1,0:T(8,128)(2,1)S(1)}, u32[]{:S(2)}, u32[]{:S(2)}) collective-permute-start(bf16[16,4096]{1,0:T(8,128)(2,1)S(1)} %get-tuple-element.35), channel_id=1, source_target_pairs={{0,6},{2,4},{4,2},{6,0},{8,14},{10,12},{12,10},{14,8},{1,7},{3,5},... | collective-permute-start | bytes 393224 | tf_op jit(solution)/shard_map/ppermute | solution.py:118
  25.6 8.1 %collective-permute-start.10 = (bf16[16,4096]{1,0:T(8,128)(2,1)S(1)}, bf16[16,4096]{1,0:T(8,128)(2,1)S(1)}, u32[]{:S(2)}, u32[]{:S(2)}) collective-permute-start(bf16[16,4096]{1,0:T(8,128)(2,1)S(1)} %get-tuple-element.36), channel_id=1, source_target_pairs={{0,2},{2,0},{4,6},{6,4},{8,10},{10,8},{12,14},{14,12},{1,3},{3,1},... | collective-permute-start | bytes 393224 | tf_op jit(solution)/shard_map/ppermute | solution.py:118
  27.0 6.7 %collective-permute-start.11 = (bf16[16,4096]{1,0:T(8,128)(2,1)S(1)}, bf16[16,4096]{1,0:T(8,128)(2,1)S(1)}, u32[]{:S(2)}, u32[]{:S(2)}) collective-permute-start(bf16[16,4096]{1,0:T(8,128)(2,1)S(1)} %get-tuple-element.37), channel_id=1, source_target_pairs={{0,4},{2,6},{4,0},{6,2},{8,12},{10,14},{12,8},{14,10},{1,5},{3,7},... | collective-permute-start | bytes 393224 | tf_op jit(solution)/shard_map/ppermute | solution.py:118
  27.7 8.8 %collective-permute-start.13 = (bf16[16,4096]{1,0:T(8,128)(2,1)S(1)}, bf16[16,4096]{1,0:T(8,128)(2,1)S(1)}, u32[]{:S(2)}, u32[]{:S(2)}) collective-permute-start(bf16[16,4096]{1,0:T(8,128)(2,1)S(1)} %get-tuple-element.40), channel_id=1, source_target_pairs={{0,2},{2,0},{4,6},{6,4},{8,10},{10,8},{12,14},{14,12},{1,3},{3,1},... | collective-permute-start | bytes 393224 | tf_op jit(solution)/shard_map/ppermute | solution.py:118
  33.8 9.0 %collective-permute-start.12 = (bf16[16,4096]{1,0:T(8,128)(2,1)S(1)}, bf16[16,4096]{1,0:T(8,128)(2,1)S(1)}, u32[]{:S(2)}, u32[]{:S(2)}) collective-permute-start(bf16[16,4096]{1,0:T(8,128)(2,1)S(1)} %add.4.refs_1_), channel_id=1, source_target_pairs={{0,8},{2,10},{4,12},{6,14},{8,0},{10,2},{12,4},{14,6},{1,9},{3,11}... | collective-permute-start | bytes 393224 | tf_op jit(solution)/shard_map/ppermute | solution.py:118
  36.5 7.7 %collective-permute-start.14 = (bf16[16,4096]{1,0:T(8,128)(2,1)S(1)}, bf16[16,4096]{1,0:T(8,128)(2,1)S(1)}, u32[]{:S(2)}, u32[]{:S(2)}) collective-permute-start(bf16[16,4096]{1,0:T(8,128)(2,1)S(1)} %add.6), channel_id=1, source_target_pairs={{0,4},{2,6},{4,0},{6,2},{8,12},{10,14},{12,8},{14,10},{1,5},{3,7},... | collective-permute-start | bytes 393224 | tf_op jit(solution)/shard_map/ppermute | solution.py:118
  37.5 6.7 %collective-permute-start.15 = (bf16[16,4096]{1,0:T(8,128)(2,1)S(1)}, bf16[16,4096]{1,0:T(8,128)(2,1)S(1)}, u32[]{:S(2)}, u32[]{:S(2)}) collective-permute-start(bf16[16,4096]{1,0:T(8,128)(2,1)S(1)} %get-tuple-element.42), channel_id=1, source_target_pairs={{0,2},{2,0},{4,6},{6,4},{8,10},{10,8},{12,14},{14,12},{1,3},{3,1},... | collective-permute-start | bytes 393224 | tf_op jit(solution)/shard_map/ppermute | solution.py:118

commit v18 on v16

--- a/solution.py
+++ b/solution.py
@@ -133,7 +133,7 @@
         for far in fars:
             for near in (2, 3, 1):
                 block[far + near] = swap(block[far], near)
-        stay = [0, 2] + fars
+        stay = [0, 1] + fars
         order = [0, 3, 1, 2] + [far + near for far in fars for near in (0, 2, 1, 3)]
         blocks = [block[b] for b in order]
         gate_part = project(blocks, gate_held)
@@ -148,10 +148,9 @@
             quad = [swap(part[far + near], near) for near in (3, 1, 2)]
             sums.append(add(part[far], quad, BF16))
         arrived = [swap(value, far) for value, far in zip(sums, fars)]
-        pair = add(part[2], [swap(part[3], 1)], BF16, after=sums)
-        part[1], pair = lax.optimization_barrier((part[1], pair))
-        total = add(part[0], arrived, F32, 1500000000)
-        return add(total, [swap(pair, 2), swap(part[1], 1)], BF16)
+        pair = add(part[1], [swap(part[3], 2)], BF16, after=sums)
+        total = add(part[0], [swap(part[2], 2)], F32, 1500000000, after=[pair])
+        return add(total, [swap(pair, 1)] + arrived, BF16)
 
     return local
 

time: 45.2 us -> 44 us (0.973)
  waiting for transfers between devices: 18.7 us -> 16.5 us
  starting transfers between devices: 19.8 us -> 20.8 us
    ppermute x14, waiting for transfers between devices: 17.5 us -> 15.3 us  [swap(): return lax.ppermute(value, 'wide', [(i, i ^ bits) for i in range(wide)])]
    ppermute x14, starting transfers between devices: 19.2 us -> 20.2 us  [swap(): return lax.ppermute(value, 'wide', [(i, i ^ bits) for i in range(wide)])]
  transfers between devices with their start and end apart: 16 -> 16, of which waited for: 10 -> 11; matrix products, arithmetic and copies ran while one was open for 0% -> 0% of each run, Pallas kernels for 10% -> 10%
where the time goes in v18:
time: 44 us; the launch traced here: 43.9 us
  starting transfers between devices  20.8 us (47%)
  waiting for transfers between devices  16.5 us (38%)
  Pallas kernels  6.45 us (15%)
    ppermute x14, starting transfers between devices, swap(): return lax.ppermute(value, 'wide', [(i, i ^ bits) for i in range(wide)])  20.2 us
    ppermute x14, waiting for transfers between devices, swap(): return lax.ppermute(value, 'wide', [(i, i ^ bits) for i in range(wide)])  15.3 us
    pallas_call x1, Pallas kernels, fetch(): pl.pallas_call(functools.partial(fetch_kernel, pieces, count), in_specs=[...  3.47 us
    pallas_call x3, Pallas kernels, call(): pl.pallas_call(kernel, out_shape=out_shape, compiler_params=pltpu.Compile...  2.17 us
    ppermute x2, waiting for transfers between devices, across_cores(): lax.ppermute(value, 'narrow', [(i, (i + 1) % narrow) for i in range(narro...  1.16 us
  transfers between devices with their start and end apart: 16, of which 11 were waited for; matrix products, arithmetic and copies ran while one was open for 0% of the time, Pallas kernels for 10%

profile of v18, /device:TPU:0, one launch (start us, length us, event | category | flops | bytes accessed | tf_op | source)
XLA Modules:
  0.0 43.9 jit_solution(7679468561813321738)
XLA Ops:
  0.0 0.0 copy-start.1
  0.0 4.0 %collective-permute-start.3 = (bf16[16,4096]{1,0:T(8,128)(2,1)}, bf16[16,4096]{1,0:T(8,128)(2,1)S(1)}, u32[]{:S(2)}, u32[]{:S(2)}) collective-permute-start(bf16[16,4096]{1,0:T(8,128)(2,1)} %refs_0_.5), channel_id=1, source_target_pairs={{0,8},{2,10},{4,12},{6,14},{8,0},{10,2},{12,4},{14,6},{1,9},{3,11}... | collective-permute-start | bytes 393224 | tf_op jit(solution)/shard_map/ppermute | solution.py:116
  4.0 1.6 %collective-permute-start.2 = (bf16[16,4096]{1,0:T(8,128)(2,1)}, bf16[16,4096]{1,0:T(8,128)(2,1)S(1)}, u32[]{:S(2)}, u32[]{:S(2)}) collective-permute-start(bf16[16,4096]{1,0:T(8,128)(2,1)} %refs_0_.5), channel_id=1, source_target_pairs={{0,4},{2,6},{4,0},{6,2},{8,12},{10,14},{12,8},{14,10},{1,5},{3,7},... | collective-permute-start | bytes 393224 | tf_op jit(solution)/shard_map/ppermute | solution.py:116
  5.6 1.5 %collective-permute-start.1 = (bf16[16,4096]{1,0:T(8,128)(2,1)}, bf16[16,4096]{1,0:T(8,128)(2,1)S(1)}, u32[]{:S(2)}, u32[]{:S(2)}) collective-permute-start(bf16[16,4096]{1,0:T(8,128)(2,1)} %refs_0_.5), channel_id=1, source_target_pairs={{0,2},{2,0},{4,6},{6,4},{8,10},{10,8},{12,14},{14,12},{1,3},{3,1},... | collective-permute-start | bytes 393224 | tf_op jit(solution)/shard_map/ppermute | solution.py:116
  7.1 0.4 collective-permute-start
  7.5 3.5 %fetch.1 = (bf16[4096,512]{1,0:T(8,128)(2,1)S(1)}, bf16[4096,512]{1,0:T(8,128)(2,1)S(1)}) custom-call(bf16[4096,512]{1,0:T(8,128)(2,1)} %refs_0_.3, bf16[4096,512]{1,0:T(8,128)(2,1)} %refs_1_.1), custom_call_target="tpu_custom_call" | custom-call | flops 4000000000 | tf_op jit(solution)/shard_map/fetch/pallas_call | solution.py:41
  11.0 0.0 collective-permute-done.3.refs_4_
  11.0 0.0 copy-start
  11.0 2.6 %collective-permute-start.6 = (bf16[16,4096]{1,0:T(8,128)(2,1)S(1)}, bf16[16,4096]{1,0:T(8,128)(2,1)S(1)}, u32[]{:S(2)}, u32[]{:S(2)}) collective-permute-start(bf16[16,4096]{1,0:T(8,128)(2,1)S(1)} %collective-permute-done.3.refs_4_), channel_id=1, source_target_pairs={{0,6},{2,4},{4,2},{6,0},{8,14},{10,12},{12,10},{14,8},{1,7},{3,5},... | collective-permute-start | bytes 393224 | tf_op jit(solution)/shard_map/ppermute | solution.py:116
  13.6 0.5 %collective-permute-start.5 = (bf16[16,4096]{1,0:T(8,128)(2,1)S(1)}, bf16[16,4096]{1,0:T(8,128)(2,1)S(1)}, u32[]{:S(2)}, u32[]{:S(2)}) collective-permute-start(bf16[16,4096]{1,0:T(8,128)(2,1)S(1)} %collective-permute-done.3.refs_4_), channel_id=1, source_target_pairs={{0,2},{2,0},{4,6},{6,4},{8,10},{10,8},{12,14},{14,12},{1,3},{3,1},... | collective-permute-start | bytes 393224 | tf_op jit(solution)/shard_map/ppermute | solution.py:116
  14.1 0.0 collective-permute-done.2.refs_3_
  14.1 0.5 %collective-permute-start.4 = (bf16[16,4096]{1,0:T(8,128)(2,1)S(1)}, bf16[16,4096]{1,0:T(8,128)(2,1)S(1)}, u32[]{:S(2)}, u32[]{:S(2)}) collective-permute-start(bf16[16,4096]{1,0:T(8,128)(2,1)S(1)} %collective-permute-done.3.refs_4_), channel_id=1, source_target_pairs={{0,4},{2,6},{4,0},{6,2},{8,12},{10,14},{12,8},{14,10},{1,5},{3,7},... | collective-permute-start | bytes 393224 | tf_op jit(solution)/shard_map/ppermute | solution.py:116
  14.6 0.0 collective-permute-done.1.refs_2_
  14.6 1.0 %collective-permute-done.refs_1_ = bf16[16,4096]{1,0:T(8,128)(2,1)S(1)} collective-permute-done((bf16[16,4096]{1,0:T(8,128)(2,1)}, bf16[16,4096]{1,0:T(8,128)(2,1)S(1)}, u32[]{:S(2)}, u32[]{:S(2)}) %collective-permute-start) | collective-permute-done | bytes 131104 | tf_op jit(solution)/shard_map/ppermute | solution.py:116
  15.6 2.9 %collective-permute-done.6.refs_7_ = bf16[16,4096]{1,0:T(8,128)(2,1)S(1)} collective-permute-done((bf16[16,4096]{1,0:T(8,128)(2,1)S(1)}, bf16[16,4096]{1,0:T(8,128)(2,1)S(1)}, u32[]{:S(2)}, u32[]{:S(2)}) %collective-permute-start.6) | collective-permute-done | bytes 131104 | tf_op jit(solution)/shard_map/ppermute | solution.py:116
  18.5 1.8 %collective-permute-done.5.refs_6_ = bf16[16,4096]{1,0:T(8,128)(2,1)S(1)} collective-permute-done((bf16[16,4096]{1,0:T(8,128)(2,1)S(1)}, bf16[16,4096]{1,0:T(8,128)(2,1)S(1)}, u32[]{:S(2)}, u32[]{:S(2)}) %collective-permute-start.5) | collective-permute-done | bytes 131104 | tf_op jit(solution)/shard_map/ppermute | solution.py:116
  20.3 0.0 collective-permute-done.4.refs_5_
  20.3 0.0 copy-done.1
  20.3 0.7 %project.2.gate_ref = f32[128,512]{1,0:T(8,128)S(1)} custom-call(bf16[16,4096]{1,0:T(8,128)(2,1)S(1)} %copy-done.1, bf16[16,4096]{1,0:T(8,128)(2,1)S(1)} %collective-permute-done.refs_1_, bf16[16,4096]{1,0:T(8,128)(2,1)S(1)} %collective-permute-done.1.refs_2_, bf16[16,4096]{1,0:T(8,128)(2,1)S(1)} %collective-permute-done.2.refs_3_, ...), custom_call_target="tpu_custom_call" | custom-call | flops 400000000 | tf_op jit(solution)/shard_map/project/pallas_call | solution.py:15
  21.0 0.1 collective-permute-start.7
  21.1 0.7 %project.3.up_ref = f32[128,512]{1,0:T(8,128)S(1)} custom-call(bf16[16,4096]{1,0:T(8,128)(2,1)S(1)} %copy-done.1, bf16[16,4096]{1,0:T(8,128)(2,1)S(1)} %collective-permute-done.refs_1_, bf16[16,4096]{1,0:T(8,128)(2,1)S(1)} %collective-permute-done.1.refs_2_, bf16[16,4096]{1,0:T(8,128)(2,1)S(1)} %collective-permute-done.2.refs_3_, ...), custom_call_target="tpu_custom_call" | custom-call | flops 400000000 | tf_op jit(solution)/shard_map/project/pallas_call | solution.py:15
  21.8 0.6 %collective-permute-start.8 = (f32[128,512]{1,0:T(8,128)S(1)}, f32[128,512]{1,0:T(8,128)S(1)}, u32[]{:S(2)}, u32[]{:S(2)}) collective-permute-start(f32[128,512]{1,0:T(8,128)S(1)} %project.3.up_ref), channel_id=1, source_target_pairs={{0,1},{1,0},{2,3},{3,2},{4,5},{5,4},{6,7},{7,6},{8,9},{9,8},{10,11... | collective-permute-start | bytes 786440 | tf_op jit(solution)/shard_map/ppermute | solution.py:119
  22.4 0.2 collective-permute-done.7.gate_other_ref
  22.6 0.9 %collective-permute-done.8.up_other_ref = f32[128,512]{1,0:T(8,128)S(1)} collective-permute-done((f32[128,512]{1,0:T(8,128)S(1)}, f32[128,512]{1,0:T(8,128)S(1)}, u32[]{:S(2)}, u32[]{:S(2)}) %collective-permute-start.8) | collective-permute-done | bytes 262176 | tf_op jit(solution)/shard_map/ppermute | solution.py:119
  23.5 0.0 copy-done
  23.5 0.7 %down.1 = (f32[16,4096]{1,0:T(8,128)S(1)}, bf16[16,4096]{1,0:T(8,128)(2,1)S(1)}, f32[16,4096]{1,0:T(8,128)S(1)}, bf16[16,4096]{1,0:T(8,128)(2,1)S(1)}, f32[16,40...) custom-call(f32[128,512]{1,0:T(8,128)S(1)} %project.2.gate_ref, ...), custom_call_target="tpu_custom_call" | custom-call | flops 536870912 | tf_op jit(solution)/shard_map/down/pallas_call | solution.py:15
  24.3 1.5 %collective-permute-start.11 = (bf16[16,4096]{1,0:T(8,128)(2,1)S(1)}, bf16[16,4096]{1,0:T(8,128)(2,1)S(1)}, u32[]{:S(2)}, u32[]{:S(2)}) collective-permute-start(bf16[16,4096]{1,0:T(8,128)(2,1)S(1)} %get-tuple-element.28), channel_id=1, source_target_pairs={{0,6},{2,4},{4,2},{6,0},{8,14},{10,12},{12,10},{14,8},{1,7},{3,5},... | collective-permute-start | bytes 393224 | tf_op jit(solution)/shard_map/ppermute | solution.py:116
  25.8 1.4 %collective-permute-start.12 = (bf16[16,4096]{1,0:T(8,128)(2,1)S(1)}, bf16[16,4096]{1,0:T(8,128)(2,1)S(1)}, u32[]{:S(2)}, u32[]{:S(2)}) collective-permute-start(bf16[16,4096]{1,0:T(8,128)(2,1)S(1)} %get-tuple-element.29), channel_id=1, source_target_pairs={{0,2},{2,0},{4,6},{6,4},{8,10},{10,8},{12,14},{14,12},{1,3},{3,1},... | collective-permute-start | bytes 393224 | tf_op jit(solution)/shard_map/ppermute | solution.py:116
  27.2 0.6 %collective-permute-start.13 = (bf16[16,4096]{1,0:T(8,128)(2,1)S(1)}, bf16[16,4096]{1,0:T(8,128)(2,1)S(1)}, u32[]{:S(2)}, u32[]{:S(2)}) collective-permute-start(bf16[16,4096]{1,0:T(8,128)(2,1)S(1)} %get-tuple-element.30), channel_id=1, source_target_pairs={{0,4},{2,6},{4,0},{6,2},{8,12},{10,14},{12,8},{14,10},{1,5},{3,7},... | collective-permute-start | bytes 393224 | tf_op jit(solution)/shard_map/ppermute | solution.py:116
  27.9 1.4 %collective-permute-start.10 = (bf16[16,4096]{1,0:T(8,128)(2,1)S(1)}, bf16[16,4096]{1,0:T(8,128)(2,1)S(1)}, u32[]{:S(2)}, u32[]{:S(2)}) collective-permute-start(bf16[16,4096]{1,0:T(8,128)(2,1)S(1)} %get-tuple-element.26), channel_id=1, source_target_pairs={{0,4},{2,6},{4,0},{6,2},{8,12},{10,14},{12,8},{14,10},{1,5},{3,7},... | collective-permute-start | bytes 393224 | tf_op jit(solution)/shard_map/ppermute | solution.py:116
  29.3 0.6 %collective-permute-start.9 = (bf16[16,4096]{1,0:T(8,128)(2,1)S(1)}, bf16[16,4096]{1,0:T(8,128)(2,1)S(1)}, u32[]{:S(2)}, u32[]{:S(2)}) collective-permute-start(bf16[16,4096]{1,0:T(8,128)(2,1)S(1)} %get-tuple-element.24), channel_id=1, source_target_pairs={{0,4},{2,6},{4,0},{6,2},{8,12},{10,14},{12,8},{14,10},{1,5},{3,7},... | collective-permute-start | bytes 393224 | tf_op jit(solution)/shard_map/ppermute | solution.py:116
  29.9 1.7 %collective-permute-done.11.refs_0_ = bf16[16,4096]{1,0:T(8,128)(2,1)S(1)} collective-permute-done((bf16[16,4096]{1,0:T(8,128)(2,1)S(1)}, bf16[16,4096]{1,0:T(8,128)(2,1)S(1)}, u32[]{:S(2)}, u32[]{:S(2)}) %collective-permute-start.11) | collective-permute-done | bytes 131104 | tf_op jit(solution)/shard_map/ppermute | solution.py:116
  31.6 2.2 %collective-permute-done.12.refs_1_ = bf16[16,4096]{1,0:T(8,128)(2,1)S(1)} collective-permute-done((bf16[16,4096]{1,0:T(8,128)(2,1)S(1)}, bf16[16,4096]{1,0:T(8,128)(2,1)S(1)}, u32[]{:S(2)}, u32[]{:S(2)}) %collective-permute-start.12) | collective-permute-done | bytes 131104 | tf_op jit(solution)/shard_map/ppermute | solution.py:116
  33.8 0.0 collective-permute-done.13.refs_2_
  33.8 0.1 add.4.refs_1_
  33.9 2.1 %collective-permute-start.15 = (bf16[16,4096]{1,0:T(8,128)(2,1)S(1)}, bf16[16,4096]{1,0:T(8,128)(2,1)S(1)}, u32[]{:S(2)}, u32[]{:S(2)}) collective-permute-start(bf16[16,4096]{1,0:T(8,128)(2,1)S(1)} %add.4.refs_1_), channel_id=1, source_target_pairs={{0,8},{2,10},{4,12},{6,14},{8,0},{10,2},{12,4},{14,6},{1,9},{3,11}... | collective-permute-start | bytes 393224 | tf_op jit(solution)/shard_map/ppermute | solution.py:116
  36.0 0.4 collective-permute-done.10.refs_0_
  36.5 1.5 %collective-permute-start.14 = (bf16[16,4096]{1,0:T(8,128)(2,1)S(1)}, bf16[16,4096]{1,0:T(8,128)(2,1)S(1)}, u32[]{:S(2)}, u32[]{:S(2)}) collective-permute-start(bf16[16,4096]{1,0:T(8,128)(2,1)S(1)} %add.5.refs_1_), channel_id=1, source_target_pairs={{0,2},{2,0},{4,6},{6,4},{8,10},{10,8},{12,14},{14,12},{1,3},{3,1},... | collective-permute-start | bytes 393224 | tf_op jit(solution)/shard_map/ppermute | solution.py:116
  37.9 3.1 %collective-permute-done.9.refs_0_ = bf16[16,4096]{1,0:T(8,128)(2,1)S(1)} collective-permute-done((bf16[16,4096]{1,0:T(8,128)(2,1)S(1)}, bf16[16,4096]{1,0:T(8,128)(2,1)S(1)}, u32[]{:S(2)}, u32[]{:S(2)}) %collective-permute-start.9) | collective-permute-done | bytes 131104 | tf_op jit(solution)/shard_map/ppermute | solution.py:116
  41.1 0.4 collective-permute-done.14.refs_0_
  41.5 1.7 %collective-permute-done.15.refs_1_ = bf16[16,4096]{1,0:T(8,128)(2,1)S(1)} collective-permute-done((bf16[16,4096]{1,0:T(8,128)(2,1)S(1)}, bf16[16,4096]{1,0:T(8,128)(2,1)S(1)}, u32[]{:S(2)}, u32[]{:S(2)}) %collective-permute-start.15) | collective-permute-done | bytes 131104 | tf_op jit(solution)/shard_map/ppermute | solution.py:116
  43.2 0.7 %add.7 = bf16[16,4096]{1,0:T(8,128)(2,1)} custom-call(f32[16,4096]{1,0:T(8,128)S(1)} %add.6.own_ref, bf16[16,4096]{1,0:T(8,128)(2,1)S(1)} %collective-permute-done.14.refs_0_, bf16[16,4096]{1,0:T(8,128)(2,1)S(1)} %collective-permute-done.15.refs_1_), custom_call_target="tpu_custom_call" | custom-call | flops 1000000 | tf_op jit(solution)/shard_map/add/pallas_call | solution.py:101
  (2 shorter events, 0.0 us)
Async XLA Ops:
  0.0 20.3 %copy-start.1 = (bf16[16,4096]{1,0:T(8,128)(2,1)S(1)}, bf16[16,4096]{1,0:T(8,128)(2,1)}, u32[]{:S(2)}) copy-start(bf16[16,4096]{1,0:T(8,128)(2,1)} %refs_0_.5) | copy-start | bytes 393220
  0.0 11.0 %collective-permute-start.3 = (bf16[16,4096]{1,0:T(8,128)(2,1)}, bf16[16,4096]{1,0:T(8,128)(2,1)S(1)}, u32[]{:S(2)}, u32[]{:S(2)}) collective-permute-start(bf16[16,4096]{1,0:T(8,128)(2,1)} %refs_0_.5), channel_id=1, source_target_pairs={{0,8},{2,10},{4,12},{6,14},{8,0},{10,2},{12,4},{14,6},{1,9},{3,11}... | collective-permute-start | bytes 393224 | tf_op jit(solution)/shard_map/ppermute | solution.py:116
  4.0 10.1 %collective-permute-start.2 = (bf16[16,4096]{1,0:T(8,128)(2,1)}, bf16[16,4096]{1,0:T(8,128)(2,1)S(1)}, u32[]{:S(2)}, u32[]{:S(2)}) collective-permute-start(bf16[16,4096]{1,0:T(8,128)(2,1)} %refs_0_.5), channel_id=1, source_target_pairs={{0,4},{2,6},{4,0},{6,2},{8,12},{10,14},{12,8},{14,10},{1,5},{3,7},... | collective-permute-start | bytes 393224 | tf_op jit(solution)/shard_map/ppermute | solution.py:116
  5.6 9.0 %collective-permute-start.1 = (bf16[16,4096]{1,0:T(8,128)(2,1)}, bf16[16,4096]{1,0:T(8,128)(2,1)S(1)}, u32[]{:S(2)}, u32[]{:S(2)}) collective-permute-start(bf16[16,4096]{1,0:T(8,128)(2,1)} %refs_0_.5), channel_id=1, source_target_pairs={{0,2},{2,0},{4,6},{6,4},{8,10},{10,8},{12,14},{14,12},{1,3},{3,1},... | collective-permute-start | bytes 393224 | tf_op jit(solution)/shard_map/ppermute | solution.py:116
  7.1 8.4 %collective-permute-start = (bf16[16,4096]{1,0:T(8,128)(2,1)}, bf16[16,4096]{1,0:T(8,128)(2,1)S(1)}, u32[]{:S(2)}, u32[]{:S(2)}) collective-permute-start(bf16[16,4096]{1,0:T(8,128)(2,1)} %refs_0_.5), channel_id=1, source_target_pairs={{0,6},{2,4},{4,2},{6,0},{8,14},{10,12},{12,10},{14,8},{1,7},{3,5},... | collective-permute-start | bytes 393224 | tf_op jit(solution)/shard_map/ppermute | solution.py:116
  11.0 12.5 %copy-start = (bf16[512,4096]{1,0:T(8,128)(2,1)S(1)}, bf16[512,4096]{1,0:T(8,128)(2,1)}, u32[]{:S(2)}) copy-start(bf16[512,4096]{1,0:T(8,128)(2,1)} %weight_ref.1) | copy-start | bytes 12582916
  11.0 7.4 %collective-permute-start.6 = (bf16[16,4096]{1,0:T(8,128)(2,1)S(1)}, bf16[16,4096]{1,0:T(8,128)(2,1)S(1)}, u32[]{:S(2)}, u32[]{:S(2)}) collective-permute-start(bf16[16,4096]{1,0:T(8,128)(2,1)S(1)} %collective-permute-done.3.refs_4_), channel_id=1, source_target_pairs={{0,6},{2,4},{4,2},{6,0},{8,14},{10,12},{12,10},{14,8},{1,7},{3,5},... | collective-permute-start | bytes 393224 | tf_op jit(solution)/shard_map/ppermute | solution.py:116
  13.6 6.7 %collective-permute-start.5 = (bf16[16,4096]{1,0:T(8,128)(2,1)S(1)}, bf16[16,4096]{1,0:T(8,128)(2,1)S(1)}, u32[]{:S(2)}, u32[]{:S(2)}) collective-permute-start(bf16[16,4096]{1,0:T(8,128)(2,1)S(1)} %collective-permute-done.3.refs_4_), channel_id=1, source_target_pairs={{0,2},{2,0},{4,6},{6,4},{8,10},{10,8},{12,14},{14,12},{1,3},{3,1},... | collective-permute-start | bytes 393224 | tf_op jit(solution)/shard_map/ppermute | solution.py:116
  14.1 6.2 %collective-permute-start.4 = (bf16[16,4096]{1,0:T(8,128)(2,1)S(1)}, bf16[16,4096]{1,0:T(8,128)(2,1)S(1)}, u32[]{:S(2)}, u32[]{:S(2)}) collective-permute-start(bf16[16,4096]{1,0:T(8,128)(2,1)S(1)} %collective-permute-done.3.refs_4_), channel_id=1, source_target_pairs={{0,4},{2,6},{4,0},{6,2},{8,12},{10,14},{12,8},{14,10},{1,5},{3,7},... | collective-permute-start | bytes 393224 | tf_op jit(solution)/shard_map/ppermute | solution.py:116
  21.0 1.6 %collective-permute-start.7 = (f32[128,512]{1,0:T(8,128)S(1)}, f32[128,512]{1,0:T(8,128)S(1)}, u32[]{:S(2)}, u32[]{:S(2)}) collective-permute-start(f32[128,512]{1,0:T(8,128)S(1)} %project.2.gate_ref), channel_id=1, source_target_pairs={{0,1},{1,0},{2,3},{3,2},{4,5},{5,4},{6,7},{7,6},{8,9},{9,8},{10,11... | collective-permute-start | bytes 786440 | tf_op jit(solution)/shard_map/ppermute | solution.py:119
  21.8 1.7 %collective-permute-start.8 = (f32[128,512]{1,0:T(8,128)S(1)}, f32[128,512]{1,0:T(8,128)S(1)}, u32[]{:S(2)}, u32[]{:S(2)}) collective-permute-start(f32[128,512]{1,0:T(8,128)S(1)} %project.3.up_ref), channel_id=1, source_target_pairs={{0,1},{1,0},{2,3},{3,2},{4,5},{5,4},{6,7},{7,6},{8,9},{9,8},{10,11... | collective-permute-start | bytes 786440 | tf_op jit(solution)/shard_map/ppermute | solution.py:119
  24.3 7.3 %collective-permute-start.11 = (bf16[16,4096]{1,0:T(8,128)(2,1)S(1)}, bf16[16,4096]{1,0:T(8,128)(2,1)S(1)}, u32[]{:S(2)}, u32[]{:S(2)}) collective-permute-start(bf16[16,4096]{1,0:T(8,128)(2,1)S(1)} %get-tuple-element.28), channel_id=1, source_target_pairs={{0,6},{2,4},{4,2},{6,0},{8,14},{10,12},{12,10},{14,8},{1,7},{3,5},... | collective-permute-start | bytes 393224 | tf_op jit(solution)/shard_map/ppermute | solution.py:116
  25.8 8.0 %collective-permute-start.12 = (bf16[16,4096]{1,0:T(8,128)(2,1)S(1)}, bf16[16,4096]{1,0:T(8,128)(2,1)S(1)}, u32[]{:S(2)}, u32[]{:S(2)}) collective-permute-start(bf16[16,4096]{1,0:T(8,128)(2,1)S(1)} %get-tuple-element.29), channel_id=1, source_target_pairs={{0,2},{2,0},{4,6},{6,4},{8,10},{10,8},{12,14},{14,12},{1,3},{3,1},... | collective-permute-start | bytes 393224 | tf_op jit(solution)/shard_map/ppermute | solution.py:116
  27.2 6.6 %collective-permute-start.13 = (bf16[16,4096]{1,0:T(8,128)(2,1)S(1)}, bf16[16,4096]{1,0:T(8,128)(2,1)S(1)}, u32[]{:S(2)}, u32[]{:S(2)}) collective-permute-start(bf16[16,4096]{1,0:T(8,128)(2,1)S(1)} %get-tuple-element.30), channel_id=1, source_target_pairs={{0,4},{2,6},{4,0},{6,2},{8,12},{10,14},{12,8},{14,10},{1,5},{3,7},... | collective-permute-start | bytes 393224 | tf_op jit(solution)/shard_map/ppermute | solution.py:116
  27.9 8.6 %collective-permute-start.10 = (bf16[16,4096]{1,0:T(8,128)(2,1)S(1)}, bf16[16,4096]{1,0:T(8,128)(2,1)S(1)}, u32[]{:S(2)}, u32[]{:S(2)}) collective-permute-start(bf16[16,4096]{1,0:T(8,128)(2,1)S(1)} %get-tuple-element.26), channel_id=1, source_target_pairs={{0,4},{2,6},{4,0},{6,2},{8,12},{10,14},{12,8},{14,10},{1,5},{3,7},... | collective-permute-start | bytes 393224 | tf_op jit(solution)/shard_map/ppermute | solution.py:116
  29.3 11.8 %collective-permute-start.9 = (bf16[16,4096]{1,0:T(8,128)(2,1)S(1)}, bf16[16,4096]{1,0:T(8,128)(2,1)S(1)}, u32[]{:S(2)}, u32[]{:S(2)}) collective-permute-start(bf16[16,4096]{1,0:T(8,128)(2,1)S(1)} %get-tuple-element.24), channel_id=1, source_target_pairs={{0,4},{2,6},{4,0},{6,2},{8,12},{10,14},{12,8},{14,10},{1,5},{3,7},... | collective-permute-start | bytes 393224 | tf_op jit(solution)/shard_map/ppermute | solution.py:116
  33.9 9.2 %collective-permute-start.15 = (bf16[16,4096]{1,0:T(8,128)(2,1)S(1)}, bf16[16,4096]{1,0:T(8,128)(2,1)S(1)}, u32[]{:S(2)}, u32[]{:S(2)}) collective-permute-start(bf16[16,4096]{1,0:T(8,128)(2,1)S(1)} %add.4.refs_1_), channel_id=1, source_target_pairs={{0,8},{2,10},{4,12},{6,14},{8,0},{10,2},{12,4},{14,6},{1,9},{3,11}... | collective-permute-start | bytes 393224 | tf_op jit(solution)/shard_map/ppermute | solution.py:116
  36.5 5.0 %collective-permute-start.14 = (bf16[16,4096]{1,0:T(8,128)(2,1)S(1)}, bf16[16,4096]{1,0:T(8,128)(2,1)S(1)}, u32[]{:S(2)}, u32[]{:S(2)}) collective-permute-start(bf16[16,4096]{1,0:T(8,128)(2,1)S(1)} %add.5.refs_1_), channel_id=1, source_target_pairs={{0,2},{2,0},{4,6},{6,4},{8,10},{10,8},{12,14},{14,12},{1,3},{3,1},... | collective-permute-start | bytes 393224 | tf_op jit(solution)/shard_map/ppermute | solution.py:116

commit v19 on v18

--- a/solution.py
+++ b/solution.py
@@ -9,6 +9,7 @@
 
 F32 = jnp.float32
 BF16 = jnp.bfloat16
+HALVES = 2
 
 
 def call(kernel, name, out_shape, flops, vmem, *operands):
@@ -62,30 +63,28 @@
     return call(project_kernel, "project", out, 400000000, 4 << 20, *blocks, weight)
 
 
-def down_kernel(gate_ref, gate_other_ref, up_ref, up_other_ref, weight_ref, *out_refs):
+def down_kernel(pieces, gate_ref, gate_other_ref, up_ref, up_other_ref, weight_ref, *out_refs):
     gate_sum = gate_ref[...] + gate_other_ref[...]
     up_sum = up_ref[...] + up_other_ref[...]
     hidden = (jax.nn.silu(gate_sum) * up_sum).astype(BF16)
     width = weight_ref.shape[1]
-    tile = min(512, width)
+    tile = min(512, width // HALVES)
     rows = out_refs[0].shape[0]
-
-    def column_tile(step, carry):
-        columns = pl.ds(pl.multiple_of(step * tile, tile), tile)
-        partial = jnp.dot(hidden, weight_ref[:, columns], preferred_element_type=F32)
-        for k, out_ref in enumerate(out_refs):
-            out_ref[:, columns] = partial[k * rows:(k + 1) * rows].astype(out_ref.dtype)
-        return carry
-
-    lax.fori_loop(0, width // tile, column_tile, 0, unroll=True)
-
-
-def down(gate, gate_other, up, up_other, weight, rows, dtypes):
-    width = weight.shape[1]
-    outs = [jax.ShapeDtypeStruct((rows, width), dtype) for dtype in dtypes]
-    flops = 2 * gate.shape[0] * weight.shape[0] * width
+    for first in range(0, width, tile):
+        partial = jnp.dot(hidden, weight_ref[:, first:first + tile], preferred_element_type=F32)
+        for (row_block, start, size), out_ref in zip(pieces, out_refs):
+            if start <= first < start + size:
+                piece = partial[row_block * rows:(row_block + 1) * rows]
+                out_ref[:, first - start:first - start + tile] = piece.astype(out_ref.dtype)
+
+
+def down(gate, gate_other, up, up_other, weight, rows, wanted):
+    outs = [jax.ShapeDtypeStruct((rows, size), dtype) for _, _, size, dtype in wanted]
+    pieces = [piece[:3] for piece in wanted]
+    hint = 2 * gate.shape[0] * weight.shape[0] * weight.shape[1]
     return call(
-        down_kernel, "down", outs, flops, 4 << 20, gate, gate_other, up, up_other, weight
+        functools.partial(down_kernel, pieces), "down", outs, hint, 4 << 20,
+        gate, gate_other, up, up_other, weight,
     )
 
 
@@ -107,6 +106,32 @@
         cost_estimate=pl.CostEstimate(flops=hint, bytes_accessed=0, transcendentals=0),
         name="add",
     )(own, *arrived, *after)
+
+
+def early_kernel(near_ref, *refs):
+    *far_refs, out_ref = refs
+    total = near_ref[:, :out_ref.shape[1]]
+    for ref in far_refs:
+        total = total + ref[...].astype(F32)
+    out_ref[...] = total
+
+
+def join_kernel(early_ref, near_ref, pair_ref, *refs):
+    *far_refs, out_ref = refs
+    size = early_ref.shape[1]
+    out_ref[:, :size] = (early_ref[...] + pair_ref[:, :size].astype(F32)).astype(out_ref.dtype)
+    total = near_ref[:, size:] + pair_ref[:, size:].astype(F32)
+    for ref in far_refs:
+        total = total + ref[...].astype(F32)
+    out_ref[:, size:] = total.astype(out_ref.dtype)
+
+
+def join(near, pair, first_halves, second_halves):
+    rows, width = near.shape
+    early = jax.ShapeDtypeStruct((rows, width // HALVES), F32)
+    early = call(early_kernel, "early", early, 3000000000, 2 << 20, near, *first_halves)
+    out = jax.ShapeDtypeStruct(near.shape, BF16)
+    return call(join_kernel, "join", out, 1000000, 2 << 20, early, near, pair, *second_halves)
 
 
 def make_local(wide, narrow):
@@ -138,19 +163,33 @@
         blocks = [block[b] for b in order]
         gate_part = project(blocks, gate_held)
         up_part = project(blocks, up_held)
+        width = down_weight.shape[1]
+        size = width // HALVES
+        names, wanted = [], []
+        for at, b in enumerate(order):
+            dtype = F32 if b in stay else BF16
+            if b < 4:
+                names.append((b, 0))
+                wanted.append((at, 0, width, dtype))
+                continue
+            for half in range(HALVES):
+                names.append((b, half))
+                wanted.append((at, half * size, size, dtype))
         outs = down(
             gate_part, across_cores(gate_part), up_part, across_cores(up_part),
-            down_weight, rows, [F32 if b in stay else BF16 for b in order],
+            down_weight, rows, wanted,
         )
-        part = dict(zip(order, outs))
+        part = dict(zip(names, outs))
         sums = []
         for far in fars:
-            quad = [swap(part[far + near], near) for near in (3, 1, 2)]
-            sums.append(add(part[far], quad, BF16))
-        arrived = [swap(value, far) for value, far in zip(sums, fars)]
-        pair = add(part[1], [swap(part[3], 2)], BF16, after=sums)
-        total = add(part[0], [swap(part[2], 2)], F32, 1500000000, after=[pair])
-        return add(total, [swap(pair, 1)] + arrived, BF16)
+            for half in range(HALVES):
+                quad = [swap(part[far + near, half], near) for near in (3, 1, 2)]
+                sums.append(add(part[far, half], quad, BF16, 3000000000))
+        part[2, 0], sums[0] = lax.optimization_barrier((part[2, 0], sums[0]))
+        arrived = [swap(value, far) for value, far in zip(sums, [f for f in fars for _ in range(HALVES)])]
+        pair = add(part[1, 0], [swap(part[3, 0], 2)], BF16, after=sums[:1])
+        total = add(part[0, 0], [swap(part[2, 0], 2)], F32, 1500000000, after=sums)
+        return join(total, swap(pair, 1), arrived[::2], arrived[1::2])
 
     return local
 

time: 44 us -> 46.4 us (1.055)
  starting transfers between devices: 20.8 us -> 25.4 us
  waiting for transfers between devices: 16.5 us -> 14.3 us
    ppermute x14 -> x18, starting transfers between devices: 20.2 us -> 24.8 us  [swap(): return lax.ppermute(value, 'wide', [(i, i ^ bits) for i in range(wide)])]
    ppermute x14 -> x18, waiting for transfers between devices: 15.3 us -> 13.1 us  [swap(): return lax.ppermute(value, 'wide', [(i, i ^ bits) for i in range(wide)])]
    pallas_call x3 -> x5, Pallas kernels: 2.17 us -> 2.88 us  [call(): pl.pallas_call(kernel, out_shape=out_shape, compiler_params=pltpu.Compile...]
    pallas_call x4, Pallas kernels: 0.81 us -> 0.11 us  [add(): pl.pallas_call(functools.partial(add_kernel, count), in_specs=[pl.BlockSp...]
  transfers between devices with their start and end apart: 16 -> 20, of which waited for: 11 -> 9; matrix products, arithmetic and copies ran while one was open for 0% -> 0% of each run, Pallas kernels for 10% -> 9%
where the time goes in v19:
time: 46.4 us; the launch traced here: 46.3 us
  starting transfers between devices  25.4 us (55%)
  waiting for transfers between devices  14.3 us (31%)
  Pallas kernels  6.46 us (14%)
    ppermute x18, starting transfers between devices, swap(): return lax.ppermute(value, 'wide', [(i, i ^ bits) for i in range(wide)])  24.8 us
    ppermute x18, waiting for transfers between devices, swap(): return lax.ppermute(value, 'wide', [(i, i ^ bits) for i in range(wide)])  13.1 us
    pallas_call x1, Pallas kernels, fetch(): pl.pallas_call(functools.partial(fetch_kernel, pieces, count), in_specs=[...  3.47 us
    pallas_call x5, Pallas kernels, call(): pl.pallas_call(kernel, out_shape=out_shape, compiler_params=pltpu.Compile...  2.88 us
    ppermute x2, waiting for transfers between devices, across_cores(): lax.ppermute(value, 'narrow', [(i, (i + 1) % narrow) for i in range(narro...  1.16 us
  transfers between devices with their start and end apart: 20, of which 9 were waited for; matrix products, arithmetic and copies ran while one was open for 0% of the time, Pallas kernels for 9%

profile of v19, /device:TPU:0, one launch (start us, length us, event | category | flops | bytes accessed | tf_op | source)
XLA Modules:
  0.0 46.3 jit_solution(5220329766366641953)
XLA Ops:
  0.0 4.0 %collective-permute-start.3 = (bf16[16,4096]{1,0:T(8,128)(2,1)}, bf16[16,4096]{1,0:T(8,128)(2,1)S(1)}, u32[]{:S(2)}, u32[]{:S(2)}) collective-permute-start(bf16[16,4096]{1,0:T(8,128)(2,1)} %refs_0_.5), channel_id=1, source_target_pairs={{0,8},{2,10},{4,12},{6,14},{8,0},{10,2},{12,4},{14,6},{1,9},{3,11}... | collective-permute-start | bytes 393224 | tf_op jit(solution)/shard_map/ppermute | solution.py:141
  4.0 1.6 %collective-permute-start.2 = (bf16[16,4096]{1,0:T(8,128)(2,1)}, bf16[16,4096]{1,0:T(8,128)(2,1)S(1)}, u32[]{:S(2)}, u32[]{:S(2)}) collective-permute-start(bf16[16,4096]{1,0:T(8,128)(2,1)} %refs_0_.5), channel_id=1, source_target_pairs={{0,4},{2,6},{4,0},{6,2},{8,12},{10,14},{12,8},{14,10},{1,5},{3,7},... | collective-permute-start | bytes 393224 | tf_op jit(solution)/shard_map/ppermute | solution.py:141
  5.6 1.5 %collective-permute-start.1 = (bf16[16,4096]{1,0:T(8,128)(2,1)}, bf16[16,4096]{1,0:T(8,128)(2,1)S(1)}, u32[]{:S(2)}, u32[]{:S(2)}) collective-permute-start(bf16[16,4096]{1,0:T(8,128)(2,1)} %refs_0_.5), channel_id=1, source_target_pairs={{0,2},{2,0},{4,6},{6,4},{8,10},{10,8},{12,14},{14,12},{1,3},{3,1},... | collective-permute-start | bytes 393224 | tf_op jit(solution)/shard_map/ppermute | solution.py:141
  7.1 0.4 collective-permute-start
  7.5 3.5 %fetch.1 = (bf16[4096,512]{1,0:T(8,128)(2,1)S(1)}, bf16[4096,512]{1,0:T(8,128)(2,1)S(1)}) custom-call(bf16[4096,512]{1,0:T(8,128)(2,1)} %refs_0_.3, bf16[4096,512]{1,0:T(8,128)(2,1)} %refs_1_.1), custom_call_target="tpu_custom_call" | custom-call | flops 4000000000 | tf_op jit(solution)/shard_map/fetch/pallas_call | solution.py:42
  11.0 0.0 collective-permute-done.3.refs_4_
  11.0 0.0 copy-start
  11.0 2.6 %collective-permute-start.6 = (bf16[16,4096]{1,0:T(8,128)(2,1)S(1)}, bf16[16,4096]{1,0:T(8,128)(2,1)S(1)}, u32[]{:S(2)}, u32[]{:S(2)}) collective-permute-start(bf16[16,4096]{1,0:T(8,128)(2,1)S(1)} %collective-permute-done.3.refs_4_), channel_id=1, source_target_pairs={{0,6},{2,4},{4,2},{6,0},{8,14},{10,12},{12,10},{14,8},{1,7},{3,5},... | collective-permute-start | bytes 393224 | tf_op jit(solution)/shard_map/ppermute | solution.py:141
  13.6 0.5 %collective-permute-start.5 = (bf16[16,4096]{1,0:T(8,128)(2,1)S(1)}, bf16[16,4096]{1,0:T(8,128)(2,1)S(1)}, u32[]{:S(2)}, u32[]{:S(2)}) collective-permute-start(bf16[16,4096]{1,0:T(8,128)(2,1)S(1)} %collective-permute-done.3.refs_4_), channel_id=1, source_target_pairs={{0,2},{2,0},{4,6},{6,4},{8,10},{10,8},{12,14},{14,12},{1,3},{3,1},... | collective-permute-start | bytes 393224 | tf_op jit(solution)/shard_map/ppermute | solution.py:141
  14.1 0.0 collective-permute-done.2.refs_3_
  14.1 0.5 collective-permute-start.4
  14.6 0.0 collective-permute-done.1.refs_2_
  14.6 1.0 %collective-permute-done.refs_1_ = bf16[16,4096]{1,0:T(8,128)(2,1)S(1)} collective-permute-done((bf16[16,4096]{1,0:T(8,128)(2,1)}, bf16[16,4096]{1,0:T(8,128)(2,1)S(1)}, u32[]{:S(2)}, u32[]{:S(2)}) %collective-permute-start) | collective-permute-done | bytes 131104 | tf_op jit(solution)/shard_map/ppermute | solution.py:141
  15.6 2.9 %collective-permute-done.6.refs_7_ = bf16[16,4096]{1,0:T(8,128)(2,1)S(1)} collective-permute-done((bf16[16,4096]{1,0:T(8,128)(2,1)S(1)}, bf16[16,4096]{1,0:T(8,128)(2,1)S(1)}, u32[]{:S(2)}, u32[]{:S(2)}) %collective-permute-start.6) | collective-permute-done | bytes 131104 | tf_op jit(solution)/shard_map/ppermute | solution.py:141
  18.5 1.8 %collective-permute-done.5.refs_6_ = bf16[16,4096]{1,0:T(8,128)(2,1)S(1)} collective-permute-done((bf16[16,4096]{1,0:T(8,128)(2,1)S(1)}, bf16[16,4096]{1,0:T(8,128)(2,1)S(1)}, u32[]{:S(2)}, u32[]{:S(2)}) %collective-permute-start.5) | collective-permute-done | bytes 131104 | tf_op jit(solution)/shard_map/ppermute | solution.py:141
  20.3 0.0 collective-permute-done.4.refs_5_
  20.3 0.0 copy-done.1
  20.3 0.7 %project.2.gate_ref = f32[128,512]{1,0:T(8,128)S(1)} custom-call(bf16[16,4096]{1,0:T(8,128)(2,1)S(1)} %copy-done.1, bf16[16,4096]{1,0:T(8,128)(2,1)S(1)} %collective-permute-done.refs_1_, bf16[16,4096]{1,0:T(8,128)(2,1)S(1)} %collective-permute-done.1.refs_2_, bf16[16,4096]{1,0:T(8,128)(2,1)S(1)} %collective-permute-done.2.refs_3_, ...), custom_call_target="tpu_custom_call" | custom-call | flops 400000000 | tf_op jit(solution)/shard_map/project/pallas_call | solution.py:16
  21.0 0.1 collective-permute-start.7
  21.1 0.7 %project.3.up_ref = f32[128,512]{1,0:T(8,128)S(1)} custom-call(bf16[16,4096]{1,0:T(8,128)(2,1)S(1)} %copy-done.1, bf16[16,4096]{1,0:T(8,128)(2,1)S(1)} %collective-permute-done.refs_1_, bf16[16,4096]{1,0:T(8,128)(2,1)S(1)} %collective-permute-done.1.refs_2_, bf16[16,4096]{1,0:T(8,128)(2,1)S(1)} %collective-permute-done.2.refs_3_, ...), custom_call_target="tpu_custom_call" | custom-call | flops 400000000 | tf_op jit(solution)/shard_map/project/pallas_call | solution.py:16
  21.8 0.6 %collective-permute-start.8 = (f32[128,512]{1,0:T(8,128)S(1)}, f32[128,512]{1,0:T(8,128)S(1)}, u32[]{:S(2)}, u32[]{:S(2)}) collective-permute-start(f32[128,512]{1,0:T(8,128)S(1)} %project.3.up_ref), channel_id=1, source_target_pairs={{0,1},{1,0},{2,3},{3,2},{4,5},{5,4},{6,7},{7,6},{8,9},{9,8},{10,11... | collective-permute-start | bytes 786440 | tf_op jit(solution)/shard_map/ppermute | solution.py:144
  22.4 0.2 collective-permute-done.7.gate_other_ref
  22.6 0.9 %collective-permute-done.8.up_other_ref = f32[128,512]{1,0:T(8,128)S(1)} collective-permute-done((f32[128,512]{1,0:T(8,128)S(1)}, f32[128,512]{1,0:T(8,128)S(1)}, u32[]{:S(2)}, u32[]{:S(2)}) %collective-permute-start.8) | collective-permute-done | bytes 262176 | tf_op jit(solution)/shard_map/ppermute | solution.py:144
  23.5 0.0 copy-done
  23.5 0.7 %down.1 = (f32[16,4096]{1,0:T(8,128)S(1)}, bf16[16,4096]{1,0:T(8,128)(2,1)S(1)}, f32[16,4096]{1,0:T(8,128)S(1)}, bf16[16,4096]{1,0:T(8,128)(2,1)S(1)}, f32[16,20...) custom-call(f32[128,512]{1,0:T(8,128)S(1)} %project.2.gate_ref, ...), custom_call_target="tpu_custom_call" | custom-call | flops 536870912 | tf_op jit(solution)/shard_map/down/pallas_call | solution.py:16
  24.3 1.5 %collective-permute-start.9 = (bf16[16,2048]{1,0:T(8,128)(2,1)S(1)}, bf16[16,2048]{1,0:T(8,128)(2,1)S(1)}, u32[]{:S(2)}, u32[]{:S(2)}) collective-permute-start(bf16[16,2048]{1,0:T(8,128)(2,1)S(1)} %get-tuple-element.32), channel_id=1, source_target_pairs={{0,6},{2,4},{4,2},{6,0},{8,14},{10,12},{12,10},{14,8},{1,7},{3,5},... | collective-permute-start | bytes 196616 | tf_op jit(solution)/shard_map/ppermute | solution.py:141
  25.8 1.4 %collective-permute-start.10 = (bf16[16,2048]{1,0:T(8,128)(2,1)S(1)}, bf16[16,2048]{1,0:T(8,128)(2,1)S(1)}, u32[]{:S(2)}, u32[]{:S(2)}) collective-permute-start(bf16[16,2048]{1,0:T(8,128)(2,1)S(1)} %get-tuple-element.33), channel_id=1, source_target_pairs={{0,2},{2,0},{4,6},{6,4},{8,10},{10,8},{12,14},{14,12},{1,3},{3,1},... | collective-permute-start | bytes 196616 | tf_op jit(solution)/shard_map/ppermute | solution.py:141
  27.2 0.6 %collective-permute-start.11 = (bf16[16,2048]{1,0:T(8,128)(2,1)S(1)}, bf16[16,2048]{1,0:T(8,128)(2,1)S(1)}, u32[]{:S(2)}, u32[]{:S(2)}) collective-permute-start(bf16[16,2048]{1,0:T(8,128)(2,1)S(1)} %get-tuple-element.34), channel_id=1, source_target_pairs={{0,4},{2,6},{4,0},{6,2},{8,12},{10,14},{12,8},{14,10},{1,5},{3,7},... | collective-permute-start | bytes 196616 | tf_op jit(solution)/shard_map/ppermute | solution.py:141
  27.9 1.4 %collective-permute-start.13 = (bf16[16,2048]{1,0:T(8,128)(2,1)S(1)}, bf16[16,2048]{1,0:T(8,128)(2,1)S(1)}, u32[]{:S(2)}, u32[]{:S(2)}) collective-permute-start(bf16[16,2048]{1,0:T(8,128)(2,1)S(1)} %get-tuple-element.38), channel_id=1, source_target_pairs={{0,6},{2,4},{4,2},{6,0},{8,14},{10,12},{12,10},{14,8},{1,7},{3,5},... | collective-permute-start | bytes 196616 | tf_op jit(solution)/shard_map/ppermute | solution.py:141
  29.3 1.4 %collective-permute-start.14 = (bf16[16,2048]{1,0:T(8,128)(2,1)S(1)}, bf16[16,2048]{1,0:T(8,128)(2,1)S(1)}, u32[]{:S(2)}, u32[]{:S(2)}) collective-permute-start(bf16[16,2048]{1,0:T(8,128)(2,1)S(1)} %get-tuple-element.39), channel_id=1, source_target_pairs={{0,2},{2,0},{4,6},{6,4},{8,10},{10,8},{12,14},{14,12},{1,3},{3,1},... | collective-permute-start | bytes 196616 | tf_op jit(solution)/shard_map/ppermute | solution.py:141
  30.7 0.0 collective-permute-done.9.refs_0_
  30.7 0.9 %collective-permute-start.15 = (bf16[16,2048]{1,0:T(8,128)(2,1)S(1)}, bf16[16,2048]{1,0:T(8,128)(2,1)S(1)}, u32[]{:S(2)}, u32[]{:S(2)}) collective-permute-start(bf16[16,2048]{1,0:T(8,128)(2,1)S(1)} %get-tuple-element.40), channel_id=1, source_target_pairs={{0,4},{2,6},{4,0},{6,2},{8,12},{10,14},{12,8},{14,10},{1,5},{3,7},... | collective-permute-start | bytes 196616 | tf_op jit(solution)/shard_map/ppermute | solution.py:141
  31.6 0.0 collective-permute-done.10.refs_1_
  31.6 1.2 %collective-permute-start.17 = (bf16[16,4096]{1,0:T(8,128)(2,1)S(1)}, bf16[16,4096]{1,0:T(8,128)(2,1)S(1)}, u32[]{:S(2)}, u32[]{:S(2)}) collective-permute-start(bf16[16,4096]{1,0:T(8,128)(2,1)S(1)} %get-tuple-element.42), channel_id=1, source_target_pairs={{0,4},{2,6},{4,0},{6,2},{8,12},{10,14},{12,8},{14,10},{1,5},{3,7},... | collective-permute-start | bytes 393224 | tf_op jit(solution)/shard_map/ppermute | solution.py:141
  32.8 0.0 collective-permute-done.11.refs_2_
  32.8 2.3 %collective-permute-start.16 = (bf16[16,2048]{1,0:T(8,128)(2,1)S(1)}, bf16[16,2048]{1,0:T(8,128)(2,1)S(1)}, u32[]{:S(2)}, u32[]{:S(2)}) collective-permute-start(bf16[16,2048]{1,0:T(8,128)(2,1)S(1)} %add.4.refs_1_), channel_id=1, source_target_pairs={{0,8},{2,10},{4,12},{6,14},{8,0},{10,2},{12,4},{14,6},{1,9},{3,11}... | collective-permute-start | bytes 196616 | tf_op jit(solution)/shard_map/ppermute | solution.py:141
  35.1 0.0 collective-permute-done.13.refs_0_
  35.1 0.9 %collective-permute-start.12 = (bf16[16,4096]{1,0:T(8,128)(2,1)S(1)}, bf16[16,4096]{1,0:T(8,128)(2,1)S(1)}, u32[]{:S(2)}, u32[]{:S(2)}) collective-permute-start(bf16[16,4096]{1,0:T(8,128)(2,1)S(1)} %get-tuple-element.35), channel_id=1, source_target_pairs={{0,4},{2,6},{4,0},{6,2},{8,12},{10,14},{12,8},{14,10},{1,5},{3,7},... | collective-permute-start | bytes 393224 | tf_op jit(solution)/shard_map/ppermute | solution.py:141
  36.0 0.0 collective-permute-done.14.refs_1_
  36.0 0.4 collective-permute-done.15.refs_2_
  36.4 1.7 %collective-permute-start.19 = (bf16[16,2048]{1,0:T(8,128)(2,1)S(1)}, bf16[16,2048]{1,0:T(8,128)(2,1)S(1)}, u32[]{:S(2)}, u32[]{:S(2)}) collective-permute-start(bf16[16,2048]{1,0:T(8,128)(2,1)S(1)} %add.5.refs_2_), channel_id=1, source_target_pairs={{0,8},{2,10},{4,12},{6,14},{8,0},{10,2},{12,4},{14,6},{1,9},{3,11}... | collective-permute-start | bytes 196616 | tf_op jit(solution)/shard_map/ppermute | solution.py:141
  38.0 2.5 %collective-permute-done.17.refs_0_ = bf16[16,4096]{1,0:T(8,128)(2,1)S(1)} collective-permute-done((bf16[16,4096]{1,0:T(8,128)(2,1)S(1)}, bf16[16,4096]{1,0:T(8,128)(2,1)S(1)}, u32[]{:S(2)}, u32[]{:S(2)}) %collective-permute-start.17) | collective-permute-done | bytes 131104 | tf_op jit(solution)/shard_map/ppermute | solution.py:141
  40.6 0.4 collective-permute-start.18
  41.0 1.9 %collective-permute-done.12.refs_0_ = bf16[16,4096]{1,0:T(8,128)(2,1)S(1)} collective-permute-done((bf16[16,4096]{1,0:T(8,128)(2,1)S(1)}, bf16[16,4096]{1,0:T(8,128)(2,1)S(1)}, u32[]{:S(2)}, u32[]{:S(2)}) %collective-permute-start.12) | collective-permute-done | bytes 131104 | tf_op jit(solution)/shard_map/ppermute | solution.py:141
  42.9 0.0 collective-permute-done.16.refs_0_
  42.9 0.0 collective-permute-done.19.refs_0_
  42.9 2.7 %collective-permute-done.18.pair_ref = bf16[16,4096]{1,0:T(8,128)(2,1)S(1)} collective-permute-done((bf16[16,4096]{1,0:T(8,128)(2,1)S(1)}, bf16[16,4096]{1,0:T(8,128)(2,1)S(1)}, u32[]{:S(2)}, u32[]{:S(2)}) %collective-permute-start.18) | collective-permute-done | bytes 131104 | tf_op jit(solution)/shard_map/ppermute | solution.py:141
  45.6 0.7 %join.1 = bf16[16,4096]{1,0:T(8,128)(2,1)} custom-call(f32[16,2048]{1,0:T(8,128)S(1)} %early.1.early_ref, f32[16,4096]{1,0:T(8,128)S(1)} %add.6.near_ref, bf16[16,4096]{1,0:T(8,128)(2,1)S(1)} %collective-permute-done.18.pair_ref, bf16[16,2048]{1,0:T(8,128)(2,1)S(1)} %collective-permute-done.19.refs_0_), custom_call_target="tpu_custom_call" | custom-call | flops 1000000 | tf_op jit(solution)/shard_map/join/pallas_call | solution.py:16
  (6 shorter events, 0.1 us)
Async XLA Ops:
  0.0 20.3 %copy-start.1 = (bf16[16,4096]{1,0:T(8,128)(2,1)S(1)}, bf16[16,4096]{1,0:T(8,128)(2,1)}, u32[]{:S(2)}) copy-start(bf16[16,4096]{1,0:T(8,128)(2,1)} %refs_0_.5) | copy-start | bytes 393220
  0.0 11.0 %collective-permute-start.3 = (bf16[16,4096]{1,0:T(8,128)(2,1)}, bf16[16,4096]{1,0:T(8,128)(2,1)S(1)}, u32[]{:S(2)}, u32[]{:S(2)}) collective-permute-start(bf16[16,4096]{1,0:T(8,128)(2,1)} %refs_0_.5), channel_id=1, source_target_pairs={{0,8},{2,10},{4,12},{6,14},{8,0},{10,2},{12,4},{14,6},{1,9},{3,11}... | collective-permute-start | bytes 393224 | tf_op jit(solution)/shard_map/ppermute | solution.py:141
  4.0 10.1 %collective-permute-start.2 = (bf16[16,4096]{1,0:T(8,128)(2,1)}, bf16[16,4096]{1,0:T(8,128)(2,1)S(1)}, u32[]{:S(2)}, u32[]{:S(2)}) collective-permute-start(bf16[16,4096]{1,0:T(8,128)(2,1)} %refs_0_.5), channel_id=1, source_target_pairs={{0,4},{2,6},{4,0},{6,2},{8,12},{10,14},{12,8},{14,10},{1,5},{3,7},... | collective-permute-start | bytes 393224 | tf_op jit(solution)/shard_map/ppermute | solution.py:141
  5.6 9.0 %collective-permute-start.1 = (bf16[16,4096]{1,0:T(8,128)(2,1)}, bf16[16,4096]{1,0:T(8,128)(2,1)S(1)}, u32[]{:S(2)}, u32[]{:S(2)}) collective-permute-start(bf16[16,4096]{1,0:T(8,128)(2,1)} %refs_0_.5), channel_id=1, source_target_pairs={{0,2},{2,0},{4,6},{6,4},{8,10},{10,8},{12,14},{14,12},{1,3},{3,1},... | collective-permute-start | bytes 393224 | tf_op jit(solution)/shard_map/ppermute | solution.py:141
  7.1 8.4 %collective-permute-start = (bf16[16,4096]{1,0:T(8,128)(2,1)}, bf16[16,4096]{1,0:T(8,128)(2,1)S(1)}, u32[]{:S(2)}, u32[]{:S(2)}) collective-permute-start(bf16[16,4096]{1,0:T(8,128)(2,1)} %refs_0_.5), channel_id=1, source_target_pairs={{0,6},{2,4},{4,2},{6,0},{8,14},{10,12},{12,10},{14,8},{1,7},{3,5},... | collective-permute-start | bytes 393224 | tf_op jit(solution)/shard_map/ppermute | solution.py:141
  11.0 12.5 %copy-start = (bf16[512,4096]{1,0:T(8,128)(2,1)S(1)}, bf16[512,4096]{1,0:T(8,128)(2,1)}, u32[]{:S(2)}) copy-start(bf16[512,4096]{1,0:T(8,128)(2,1)} %weight_ref.1) | copy-start | bytes 12582916
  11.0 7.4 %collective-permute-start.6 = (bf16[16,4096]{1,0:T(8,128)(2,1)S(1)}, bf16[16,4096]{1,0:T(8,128)(2,1)S(1)}, u32[]{:S(2)}, u32[]{:S(2)}) collective-permute-start(bf16[16,4096]{1,0:T(8,128)(2,1)S(1)} %collective-permute-done.3.refs_4_), channel_id=1, source_target_pairs={{0,6},{2,4},{4,2},{6,0},{8,14},{10,12},{12,10},{14,8},{1,7},{3,5},... | collective-permute-start | bytes 393224 | tf_op jit(solution)/shard_map/ppermute | solution.py:141
  13.6 6.7 %collective-permute-start.5 = (bf16[16,4096]{1,0:T(8,128)(2,1)S(1)}, bf16[16,4096]{1,0:T(8,128)(2,1)S(1)}, u32[]{:S(2)}, u32[]{:S(2)}) collective-permute-start(bf16[16,4096]{1,0:T(8,128)(2,1)S(1)} %collective-permute-done.3.refs_4_), channel_id=1, source_target_pairs={{0,2},{2,0},{4,6},{6,4},{8,10},{10,8},{12,14},{14,12},{1,3},{3,1},... | collective-permute-start | bytes 393224 | tf_op jit(solution)/shard_map/ppermute | solution.py:141
  14.1 6.2 %collective-permute-start.4 = (bf16[16,4096]{1,0:T(8,128)(2,1)S(1)}, bf16[16,4096]{1,0:T(8,128)(2,1)S(1)}, u32[]{:S(2)}, u32[]{:S(2)}) collective-permute-start(bf16[16,4096]{1,0:T(8,128)(2,1)S(1)} %collective-permute-done.3.refs_4_), channel_id=1, source_target_pairs={{0,4},{2,6},{4,0},{6,2},{8,12},{10,14},{12,8},{14,10},{1,5},{3,7},... | collective-permute-start | bytes 393224 | tf_op jit(solution)/shard_map/ppermute | solution.py:141
  21.0 1.6 %collective-permute-start.7 = (f32[128,512]{1,0:T(8,128)S(1)}, f32[128,512]{1,0:T(8,128)S(1)}, u32[]{:S(2)}, u32[]{:S(2)}) collective-permute-start(f32[128,512]{1,0:T(8,128)S(1)} %project.2.gate_ref), channel_id=1, source_target_pairs={{0,1},{1,0},{2,3},{3,2},{4,5},{5,4},{6,7},{7,6},{8,9},{9,8},{10,11... | collective-permute-start | bytes 786440 | tf_op jit(solution)/shard_map/ppermute | solution.py:144
  21.8 1.7 %collective-permute-start.8 = (f32[128,512]{1,0:T(8,128)S(1)}, f32[128,512]{1,0:T(8,128)S(1)}, u32[]{:S(2)}, u32[]{:S(2)}) collective-permute-start(f32[128,512]{1,0:T(8,128)S(1)} %project.3.up_ref), channel_id=1, source_target_pairs={{0,1},{1,0},{2,3},{3,2},{4,5},{5,4},{6,7},{7,6},{8,9},{9,8},{10,11... | collective-permute-start | bytes 786440 | tf_op jit(solution)/shard_map/ppermute | solution.py:144
  24.3 6.4 %collective-permute-start.9 = (bf16[16,2048]{1,0:T(8,128)(2,1)S(1)}, bf16[16,2048]{1,0:T(8,128)(2,1)S(1)}, u32[]{:S(2)}, u32[]{:S(2)}) collective-permute-start(bf16[16,2048]{1,0:T(8,128)(2,1)S(1)} %get-tuple-element.32), channel_id=1, source_target_pairs={{0,6},{2,4},{4,2},{6,0},{8,14},{10,12},{12,10},{14,8},{1,7},{3,5},... | collective-permute-start | bytes 196616 | tf_op jit(solution)/shard_map/ppermute | solution.py:141
  25.8 5.8 %collective-permute-start.10 = (bf16[16,2048]{1,0:T(8,128)(2,1)S(1)}, bf16[16,2048]{1,0:T(8,128)(2,1)S(1)}, u32[]{:S(2)}, u32[]{:S(2)}) collective-permute-start(bf16[16,2048]{1,0:T(8,128)(2,1)S(1)} %get-tuple-element.33), channel_id=1, source_target_pairs={{0,2},{2,0},{4,6},{6,4},{8,10},{10,8},{12,14},{14,12},{1,3},{3,1},... | collective-permute-start | bytes 196616 | tf_op jit(solution)/shard_map/ppermute | solution.py:141
  27.2 5.5 %collective-permute-start.11 = (bf16[16,2048]{1,0:T(8,128)(2,1)S(1)}, bf16[16,2048]{1,0:T(8,128)(2,1)S(1)}, u32[]{:S(2)}, u32[]{:S(2)}) collective-permute-start(bf16[16,2048]{1,0:T(8,128)(2,1)S(1)} %get-tuple-element.34), channel_id=1, source_target_pairs={{0,4},{2,6},{4,0},{6,2},{8,12},{10,14},{12,8},{14,10},{1,5},{3,7},... | collective-permute-start | bytes 196616 | tf_op jit(solution)/shard_map/ppermute | solution.py:141
  27.9 7.2 %collective-permute-start.13 = (bf16[16,2048]{1,0:T(8,128)(2,1)S(1)}, bf16[16,2048]{1,0:T(8,128)(2,1)S(1)}, u32[]{:S(2)}, u32[]{:S(2)}) collective-permute-start(bf16[16,2048]{1,0:T(8,128)(2,1)S(1)} %get-tuple-element.38), channel_id=1, source_target_pairs={{0,6},{2,4},{4,2},{6,0},{8,14},{10,12},{12,10},{14,8},{1,7},{3,5},... | collective-permute-start | bytes 196616 | tf_op jit(solution)/shard_map/ppermute | solution.py:141
  29.3 6.7 %collective-permute-start.14 = (bf16[16,2048]{1,0:T(8,128)(2,1)S(1)}, bf16[16,2048]{1,0:T(8,128)(2,1)S(1)}, u32[]{:S(2)}, u32[]{:S(2)}) collective-permute-start(bf16[16,2048]{1,0:T(8,128)(2,1)S(1)} %get-tuple-element.39), channel_id=1, source_target_pairs={{0,2},{2,0},{4,6},{6,4},{8,10},{10,8},{12,14},{14,12},{1,3},{3,1},... | collective-permute-start | bytes 196616 | tf_op jit(solution)/shard_map/ppermute | solution.py:141
  30.7 5.6 %collective-permute-start.15 = (bf16[16,2048]{1,0:T(8,128)(2,1)S(1)}, bf16[16,2048]{1,0:T(8,128)(2,1)S(1)}, u32[]{:S(2)}, u32[]{:S(2)}) collective-permute-start(bf16[16,2048]{1,0:T(8,128)(2,1)S(1)} %get-tuple-element.40), channel_id=1, source_target_pairs={{0,4},{2,6},{4,0},{6,2},{8,12},{10,14},{12,8},{14,10},{1,5},{3,7},... | collective-permute-start | bytes 196616 | tf_op jit(solution)/shard_map/ppermute | solution.py:141
  31.6 9.0 %collective-permute-start.17 = (bf16[16,4096]{1,0:T(8,128)(2,1)S(1)}, bf16[16,4096]{1,0:T(8,128)(2,1)S(1)}, u32[]{:S(2)}, u32[]{:S(2)}) collective-permute-start(bf16[16,4096]{1,0:T(8,128)(2,1)S(1)} %get-tuple-element.42), channel_id=1, source_target_pairs={{0,4},{2,6},{4,0},{6,2},{8,12},{10,14},{12,8},{14,10},{1,5},{3,7},... | collective-permute-start | bytes 393224 | tf_op jit(solution)/shard_map/ppermute | solution.py:141
  32.8 10.1 %collective-permute-start.16 = (bf16[16,2048]{1,0:T(8,128)(2,1)S(1)}, bf16[16,2048]{1,0:T(8,128)(2,1)S(1)}, u32[]{:S(2)}, u32[]{:S(2)}) collective-permute-start(bf16[16,2048]{1,0:T(8,128)(2,1)S(1)} %add.4.refs_1_), channel_id=1, source_target_pairs={{0,8},{2,10},{4,12},{6,14},{8,0},{10,2},{12,4},{14,6},{1,9},{3,11}... | collective-permute-start | bytes 196616 | tf_op jit(solution)/shard_map/ppermute | solution.py:141
  35.1 7.8 %collective-permute-start.12 = (bf16[16,4096]{1,0:T(8,128)(2,1)S(1)}, bf16[16,4096]{1,0:T(8,128)(2,1)S(1)}, u32[]{:S(2)}, u32[]{:S(2)}) collective-permute-start(bf16[16,4096]{1,0:T(8,128)(2,1)S(1)} %get-tuple-element.35), channel_id=1, source_target_pairs={{0,4},{2,6},{4,0},{6,2},{8,12},{10,14},{12,8},{14,10},{1,5},{3,7},... | collective-permute-start | bytes 393224 | tf_op jit(solution)/shard_map/ppermute | solution.py:141
  36.4 6.6 %collective-permute-start.19 = (bf16[16,2048]{1,0:T(8,128)(2,1)S(1)}, bf16[16,2048]{1,0:T(8,128)(2,1)S(1)}, u32[]{:S(2)}, u32[]{:S(2)}) collective-permute-start(bf16[16,2048]{1,0:T(8,128)(2,1)S(1)} %add.5.refs_2_), channel_id=1, source_target_pairs={{0,8},{2,10},{4,12},{6,14},{8,0},{10,2},{12,4},{14,6},{1,9},{3,11}... | collective-permute-start | bytes 196616 | tf_op jit(solution)/shard_map/ppermute | solution.py:141
  40.6 5.0 %collective-permute-start.18 = (bf16[16,4096]{1,0:T(8,128)(2,1)S(1)}, bf16[16,4096]{1,0:T(8,128)(2,1)S(1)}, u32[]{:S(2)}, u32[]{:S(2)}) collective-permute-start(bf16[16,4096]{1,0:T(8,128)(2,1)S(1)} %add.7), channel_id=1, source_target_pairs={{0,2},{2,0},{4,6},{6,4},{8,10},{10,8},{12,14},{14,12},{1,3},{3,1},... | collective-permute-start | bytes 393224 | tf_op jit(solution)/shard_map/ppermute | solution.py:141

commit v20 on v18

--- a/solution.py
+++ b/solution.py
@@ -21,33 +21,29 @@
     )(*operands)
 
 
-def fetch_kernel(pieces, count, *refs):
-    sems = refs[-1]
+def fetch_kernel(pieces, source, target, sems):
+    step = source.shape[0] // pieces
     copies = []
-    for n in range(count):
-        source, target = refs[n], refs[count + n]
-        step = source.shape[0] // pieces
-        for i in range(pieces):
-            part = pl.ds(i * step, step)
-            copies.append(pltpu.make_async_copy(source.at[part], target.at[part], sems.at[n, i]))
+    for i in range(pieces):
+        part = pl.ds(i * step, step)
+        copies.append(pltpu.make_async_copy(source.at[part], target.at[part], sems.at[i]))
     for copy in copies:
         copy.start()
     for copy in copies:
         copy.wait()
 
 
-def fetch(weights, pieces=4):
-    count = len(weights)
+def fetch(weight, grant, hint, pieces=8):
     return pl.pallas_call(
-        functools.partial(fetch_kernel, pieces, count),
-        in_specs=[pl.BlockSpec(memory_space=pl.ANY)] * count,
-        out_specs=[pl.BlockSpec(memory_space=pltpu.VMEM)] * count,
-        out_shape=[jax.ShapeDtypeStruct(w.shape, w.dtype) for w in weights],
-        scratch_shapes=[pltpu.SemaphoreType.DMA((count, pieces))],
-        compiler_params=pltpu.CompilerParams(vmem_limit_bytes=43 << 20),
-        cost_estimate=pl.CostEstimate(flops=4000000000, bytes_accessed=0, transcendentals=0),
+        functools.partial(fetch_kernel, pieces),
+        in_specs=[pl.BlockSpec(memory_space=pl.ANY)],
+        out_specs=pl.BlockSpec(memory_space=pltpu.VMEM),
+        out_shape=jax.ShapeDtypeStruct(weight.shape, weight.dtype),
+        scratch_shapes=[pltpu.SemaphoreType.DMA((pieces,))],
+        compiler_params=pltpu.CompilerParams(vmem_limit_bytes=grant << 20),
+        cost_estimate=pl.CostEstimate(flops=hint, bytes_accessed=0, transcendentals=0),
         name="fetch",
-    )(*weights)
+    )(weight)
 
 
 def project_kernel(*refs):
@@ -125,10 +121,9 @@
             block[far] = swap(tokens, far)
         for near in (1, 2, 3):
             block[near] = swap(tokens, near)
-        gate_held, up_held = fetch([gate_weight, up_weight])
-        *crossed, gate_held, up_held = lax.optimization_barrier(
-            [block[far] for far in fars] + [gate_held, up_held]
-        )
+        gate_held = fetch(gate_weight, 48, 2000000000)
+        up_held = fetch(up_weight, 48, 2000000000)
+        *crossed, gate_held = lax.optimization_barrier([block[far] for far in fars] + [gate_held])
         block.update(zip(fars, crossed))
         for far in fars:
             for near in (2, 3, 1):

time: 44 us -> 44 us (level)
  Pallas kernels: 6.45 us -> 7.4 us
  waiting for transfers between devices: 16.5 us -> 15.6 us
    pallas_call x1 -> x2, Pallas kernels: 3.47 us -> 4.43 us  [fetch(): pl.pallas_call(functools.partial(fetch_kernel, pieces), in_specs=[pl.Bloc...]
    ppermute x14, waiting for transfers between devices: 15.3 us -> 14.4 us  [swap(): return lax.ppermute(value, 'wide', [(i, i ^ bits) for i in range(wide)])]
  transfers between devices with their start and end apart: 16 -> 16, of which waited for: 11 -> 11; matrix products, arithmetic and copies ran while one was open for 0% -> 0% of each run, Pallas kernels for 10% -> 12%
where the time goes in v20:
time: 44 us; the launch traced here: 43.9 us
  starting transfers between devices  20.7 us (47%)
  waiting for transfers between devices  15.6 us (35%)
  Pallas kernels  7.4 us (17%)
    ppermute x14, starting transfers between devices, swap(): return lax.ppermute(value, 'wide', [(i, i ^ bits) for i in range(wide)])  20.1 us
    ppermute x14, waiting for transfers between devices, swap(): return lax.ppermute(value, 'wide', [(i, i ^ bits) for i in range(wide)])  14.4 us
    pallas_call x2, Pallas kernels, fetch(): pl.pallas_call(functools.partial(fetch_kernel, pieces), in_specs=[pl.Bloc...  4.43 us
    pallas_call x3, Pallas kernels, call(): pl.pallas_call(kernel, out_shape=out_shape, compiler_params=pltpu.Compile...  2.16 us
    ppermute x2, waiting for transfers between devices, across_cores(): lax.ppermute(value, 'narrow', [(i, (i + 1) % narrow) for i in range(narro...  1.16 us
  transfers between devices with their start and end apart: 16, of which 11 were waited for; matrix products, arithmetic and copies ran while one was open for 0% of the time, Pallas kernels for 12%

profile of v20, /device:TPU:0, one launch (start us, length us, event | category | flops | bytes accessed | tf_op | source)
XLA Modules:
  0.0 43.9 jit_solution(10852116792136962393)
XLA Ops:
  0.0 4.0 %collective-permute-start.3 = (bf16[16,4096]{1,0:T(8,128)(2,1)}, bf16[16,4096]{1,0:T(8,128)(2,1)S(1)}, u32[]{:S(2)}, u32[]{:S(2)}) collective-permute-start(bf16[16,4096]{1,0:T(8,128)(2,1)} %refs_0_.3), channel_id=1, source_target_pairs={{0,8},{2,10},{4,12},{6,14},{8,0},{10,2},{12,4},{14,6},{1,9},{3,11}... | collective-permute-start | bytes 393224 | tf_op jit(solution)/shard_map/ppermute | solution.py:112
  4.0 1.6 %collective-permute-start.2 = (bf16[16,4096]{1,0:T(8,128)(2,1)}, bf16[16,4096]{1,0:T(8,128)(2,1)S(1)}, u32[]{:S(2)}, u32[]{:S(2)}) collective-permute-start(bf16[16,4096]{1,0:T(8,128)(2,1)} %refs_0_.3), channel_id=1, source_target_pairs={{0,4},{2,6},{4,0},{6,2},{8,12},{10,14},{12,8},{14,10},{1,5},{3,7},... | collective-permute-start | bytes 393224 | tf_op jit(solution)/shard_map/ppermute | solution.py:112
  5.6 1.5 %collective-permute-start.1 = (bf16[16,4096]{1,0:T(8,128)(2,1)}, bf16[16,4096]{1,0:T(8,128)(2,1)S(1)}, u32[]{:S(2)}, u32[]{:S(2)}) collective-permute-start(bf16[16,4096]{1,0:T(8,128)(2,1)} %refs_0_.3), channel_id=1, source_target_pairs={{0,2},{2,0},{4,6},{6,4},{8,10},{10,8},{12,14},{14,12},{1,3},{3,1},... | collective-permute-start | bytes 393224 | tf_op jit(solution)/shard_map/ppermute | solution.py:112
  7.1 0.4 collective-permute-start
  7.5 2.2 %fetch.2.refs_8_ = bf16[4096,512]{1,0:T(8,128)(2,1)S(1)} custom-call(bf16[4096,512]{1,0:T(8,128)(2,1)} %source.2), custom_call_target="tpu_custom_call" | custom-call | flops 2000000000 | tf_op jit(solution)/shard_map/fetch/pallas_call | solution.py:37
  9.7 0.0 copy-start.1
  9.8 0.9 %collective-permute-done.3.refs_4_ = bf16[16,4096]{1,0:T(8,128)(2,1)S(1)} collective-permute-done((bf16[16,4096]{1,0:T(8,128)(2,1)}, bf16[16,4096]{1,0:T(8,128)(2,1)S(1)}, u32[]{:S(2)}, u32[]{:S(2)}) %collective-permute-start.3) | collective-permute-done | bytes 131104 | tf_op jit(solution)/shard_map/ppermute | solution.py:112
  10.7 1.7 %collective-permute-start.6 = (bf16[16,4096]{1,0:T(8,128)(2,1)S(1)}, bf16[16,4096]{1,0:T(8,128)(2,1)S(1)}, u32[]{:S(2)}, u32[]{:S(2)}) collective-permute-start(bf16[16,4096]{1,0:T(8,128)(2,1)S(1)} %collective-permute-done.3.refs_4_), channel_id=1, source_target_pairs={{0,6},{2,4},{4,2},{6,0},{8,14},{10,12},{12,10},{14,8},{1,7},{3,5},... | collective-permute-start | bytes 393224 | tf_op jit(solution)/shard_map/ppermute | solution.py:112
  12.4 0.5 %collective-permute-start.5 = (bf16[16,4096]{1,0:T(8,128)(2,1)S(1)}, bf16[16,4096]{1,0:T(8,128)(2,1)S(1)}, u32[]{:S(2)}, u32[]{:S(2)}) collective-permute-start(bf16[16,4096]{1,0:T(8,128)(2,1)S(1)} %collective-permute-done.3.refs_4_), channel_id=1, source_target_pairs={{0,2},{2,0},{4,6},{6,4},{8,10},{10,8},{12,14},{14,12},{1,3},{3,1},... | collective-permute-start | bytes 393224 | tf_op jit(solution)/shard_map/ppermute | solution.py:112
  12.9 0.0 collective-permute-done.2.refs_3_
  12.9 1.3 %collective-permute-start.4 = (bf16[16,4096]{1,0:T(8,128)(2,1)S(1)}, bf16[16,4096]{1,0:T(8,128)(2,1)S(1)}, u32[]{:S(2)}, u32[]{:S(2)}) collective-permute-start(bf16[16,4096]{1,0:T(8,128)(2,1)S(1)} %collective-permute-done.3.refs_4_), channel_id=1, source_target_pairs={{0,4},{2,6},{4,0},{6,2},{8,12},{10,14},{12,8},{14,10},{1,5},{3,7},... | collective-permute-start | bytes 393224 | tf_op jit(solution)/shard_map/ppermute | solution.py:112
  14.1 2.2 %fetch.3.refs_8_ = bf16[4096,512]{1,0:T(8,128)(2,1)S(1)} custom-call(bf16[4096,512]{1,0:T(8,128)(2,1)} %source.3), custom_call_target="tpu_custom_call" | custom-call | flops 2000000000 | tf_op jit(solution)/shard_map/fetch/pallas_call | solution.py:37
  16.4 0.0 copy-start
  16.4 0.0 collective-permute-done.1.refs_2_
  16.4 0.0 collective-permute-done.refs_1_
  16.4 2.0 %collective-permute-done.6.refs_7_ = bf16[16,4096]{1,0:T(8,128)(2,1)S(1)} collective-permute-done((bf16[16,4096]{1,0:T(8,128)(2,1)S(1)}, bf16[16,4096]{1,0:T(8,128)(2,1)S(1)}, u32[]{:S(2)}, u32[]{:S(2)}) %collective-permute-start.6) | collective-permute-done | bytes 131104 | tf_op jit(solution)/shard_map/ppermute | solution.py:112
  18.4 1.9 %collective-permute-done.5.refs_6_ = bf16[16,4096]{1,0:T(8,128)(2,1)S(1)} collective-permute-done((bf16[16,4096]{1,0:T(8,128)(2,1)S(1)}, bf16[16,4096]{1,0:T(8,128)(2,1)S(1)}, u32[]{:S(2)}, u32[]{:S(2)}) %collective-permute-start.5) | collective-permute-done | bytes 131104 | tf_op jit(solution)/shard_map/ppermute | solution.py:112
  20.3 0.0 collective-permute-done.4.refs_5_
  20.3 0.0 copy-done.1
  20.3 0.7 %project.2.gate_ref = f32[128,512]{1,0:T(8,128)S(1)} custom-call(bf16[16,4096]{1,0:T(8,128)(2,1)S(1)} %copy-done.1, bf16[16,4096]{1,0:T(8,128)(2,1)S(1)} %collective-permute-done.refs_1_, bf16[16,4096]{1,0:T(8,128)(2,1)S(1)} %collective-permute-done.1.refs_2_, bf16[16,4096]{1,0:T(8,128)(2,1)S(1)} %collective-permute-done.2.refs_3_, ...), custom_call_target="tpu_custom_call" | custom-call | flops 400000000 | tf_op jit(solution)/shard_map/project/pallas_call | solution.py:15
  21.0 0.1 collective-permute-start.7
  21.1 0.7 %project.3.up_ref = f32[128,512]{1,0:T(8,128)S(1)} custom-call(bf16[16,4096]{1,0:T(8,128)(2,1)S(1)} %copy-done.1, bf16[16,4096]{1,0:T(8,128)(2,1)S(1)} %collective-permute-done.refs_1_, bf16[16,4096]{1,0:T(8,128)(2,1)S(1)} %collective-permute-done.1.refs_2_, bf16[16,4096]{1,0:T(8,128)(2,1)S(1)} %collective-permute-done.2.refs_3_, ...), custom_call_target="tpu_custom_call" | custom-call | flops 400000000 | tf_op jit(solution)/shard_map/project/pallas_call | solution.py:15
  21.8 0.6 %collective-permute-start.8 = (f32[128,512]{1,0:T(8,128)S(1)}, f32[128,512]{1,0:T(8,128)S(1)}, u32[]{:S(2)}, u32[]{:S(2)}) collective-permute-start(f32[128,512]{1,0:T(8,128)S(1)} %project.3.up_ref), channel_id=1, source_target_pairs={{0,1},{1,0},{2,3},{3,2},{4,5},{5,4},{6,7},{7,6},{8,9},{9,8},{10,11... | collective-permute-start | bytes 786440 | tf_op jit(solution)/shard_map/ppermute | solution.py:115
  22.4 0.2 collective-permute-done.7.gate_other_ref
  22.6 0.9 %collective-permute-done.8.up_other_ref = f32[128,512]{1,0:T(8,128)S(1)} collective-permute-done((f32[128,512]{1,0:T(8,128)S(1)}, f32[128,512]{1,0:T(8,128)S(1)}, u32[]{:S(2)}, u32[]{:S(2)}) %collective-permute-start.8) | collective-permute-done | bytes 262176 | tf_op jit(solution)/shard_map/ppermute | solution.py:115
  23.5 0.0 copy-done
  23.5 0.7 %down.1 = (f32[16,4096]{1,0:T(8,128)S(1)}, bf16[16,4096]{1,0:T(8,128)(2,1)S(1)}, f32[16,4096]{1,0:T(8,128)S(1)}, bf16[16,4096]{1,0:T(8,128)(2,1)S(1)}, f32[16,40...) custom-call(f32[128,512]{1,0:T(8,128)S(1)} %project.2.gate_ref, ...), custom_call_target="tpu_custom_call" | custom-call | flops 536870912 | tf_op jit(solution)/shard_map/down/pallas_call | solution.py:15
  24.3 1.5 %collective-permute-start.11 = (bf16[16,4096]{1,0:T(8,128)(2,1)S(1)}, bf16[16,4096]{1,0:T(8,128)(2,1)S(1)}, u32[]{:S(2)}, u32[]{:S(2)}) collective-permute-start(bf16[16,4096]{1,0:T(8,128)(2,1)S(1)} %get-tuple-element.22), channel_id=1, source_target_pairs={{0,6},{2,4},{4,2},{6,0},{8,14},{10,12},{12,10},{14,8},{1,7},{3,5},... | collective-permute-start | bytes 393224 | tf_op jit(solution)/shard_map/ppermute | solution.py:112
  25.8 1.4 %collective-permute-start.12 = (bf16[16,4096]{1,0:T(8,128)(2,1)S(1)}, bf16[16,4096]{1,0:T(8,128)(2,1)S(1)}, u32[]{:S(2)}, u32[]{:S(2)}) collective-permute-start(bf16[16,4096]{1,0:T(8,128)(2,1)S(1)} %get-tuple-element.23), channel_id=1, source_target_pairs={{0,2},{2,0},{4,6},{6,4},{8,10},{10,8},{12,14},{14,12},{1,3},{3,1},... | collective-permute-start | bytes 393224 | tf_op jit(solution)/shard_map/ppermute | solution.py:112
  27.2 0.6 %collective-permute-start.13 = (bf16[16,4096]{1,0:T(8,128)(2,1)S(1)}, bf16[16,4096]{1,0:T(8,128)(2,1)S(1)}, u32[]{:S(2)}, u32[]{:S(2)}) collective-permute-start(bf16[16,4096]{1,0:T(8,128)(2,1)S(1)} %get-tuple-element.24), channel_id=1, source_target_pairs={{0,4},{2,6},{4,0},{6,2},{8,12},{10,14},{12,8},{14,10},{1,5},{3,7},... | collective-permute-start | bytes 393224 | tf_op jit(solution)/shard_map/ppermute | solution.py:112
  27.9 1.4 %collective-permute-start.10 = (bf16[16,4096]{1,0:T(8,128)(2,1)S(1)}, bf16[16,4096]{1,0:T(8,128)(2,1)S(1)}, u32[]{:S(2)}, u32[]{:S(2)}) collective-permute-start(bf16[16,4096]{1,0:T(8,128)(2,1)S(1)} %get-tuple-element.20), channel_id=1, source_target_pairs={{0,4},{2,6},{4,0},{6,2},{8,12},{10,14},{12,8},{14,10},{1,5},{3,7},... | collective-permute-start | bytes 393224 | tf_op jit(solution)/shard_map/ppermute | solution.py:112
  29.2 0.6 %collective-permute-start.9 = (bf16[16,4096]{1,0:T(8,128)(2,1)S(1)}, bf16[16,4096]{1,0:T(8,128)(2,1)S(1)}, u32[]{:S(2)}, u32[]{:S(2)}) collective-permute-start(bf16[16,4096]{1,0:T(8,128)(2,1)S(1)} %get-tuple-element.18), channel_id=1, source_target_pairs={{0,4},{2,6},{4,0},{6,2},{8,12},{10,14},{12,8},{14,10},{1,5},{3,7},... | collective-permute-start | bytes 393224 | tf_op jit(solution)/shard_map/ppermute | solution.py:112
  29.9 1.7 %collective-permute-done.11.refs_0_ = bf16[16,4096]{1,0:T(8,128)(2,1)S(1)} collective-permute-done((bf16[16,4096]{1,0:T(8,128)(2,1)S(1)}, bf16[16,4096]{1,0:T(8,128)(2,1)S(1)}, u32[]{:S(2)}, u32[]{:S(2)}) %collective-permute-start.11) | collective-permute-done | bytes 131104 | tf_op jit(solution)/shard_map/ppermute | solution.py:112
  31.6 2.2 %collective-permute-done.12.refs_1_ = bf16[16,4096]{1,0:T(8,128)(2,1)S(1)} collective-permute-done((bf16[16,4096]{1,0:T(8,128)(2,1)S(1)}, bf16[16,4096]{1,0:T(8,128)(2,1)S(1)}, u32[]{:S(2)}, u32[]{:S(2)}) %collective-permute-start.12) | collective-permute-done | bytes 131104 | tf_op jit(solution)/shard_map/ppermute | solution.py:112
  33.8 0.0 collective-permute-done.13.refs_2_
  33.8 0.1 add.4.refs_1_
  33.9 2.1 %collective-permute-start.15 = (bf16[16,4096]{1,0:T(8,128)(2,1)S(1)}, bf16[16,4096]{1,0:T(8,128)(2,1)S(1)}, u32[]{:S(2)}, u32[]{:S(2)}) collective-permute-start(bf16[16,4096]{1,0:T(8,128)(2,1)S(1)} %add.4.refs_1_), channel_id=1, source_target_pairs={{0,8},{2,10},{4,12},{6,14},{8,0},{10,2},{12,4},{14,6},{1,9},{3,11}... | collective-permute-start | bytes 393224 | tf_op jit(solution)/shard_map/ppermute | solution.py:112
  36.0 0.5 %collective-permute-done.10.refs_0_ = bf16[16,4096]{1,0:T(8,128)(2,1)S(1)} collective-permute-done((bf16[16,4096]{1,0:T(8,128)(2,1)S(1)}, bf16[16,4096]{1,0:T(8,128)(2,1)S(1)}, u32[]{:S(2)}, u32[]{:S(2)}) %collective-permute-start.10) | collective-permute-done | bytes 131104 | tf_op jit(solution)/shard_map/ppermute | solution.py:112
  36.5 1.4 %collective-permute-start.14 = (bf16[16,4096]{1,0:T(8,128)(2,1)S(1)}, bf16[16,4096]{1,0:T(8,128)(2,1)S(1)}, u32[]{:S(2)}, u32[]{:S(2)}) collective-permute-start(bf16[16,4096]{1,0:T(8,128)(2,1)S(1)} %add.5.refs_1_), channel_id=1, source_target_pairs={{0,2},{2,0},{4,6},{6,4},{8,10},{10,8},{12,14},{14,12},{1,3},{3,1},... | collective-permute-start | bytes 393224 | tf_op jit(solution)/shard_map/ppermute | solution.py:112
  37.9 3.1 %collective-permute-done.9.refs_0_ = bf16[16,4096]{1,0:T(8,128)(2,1)S(1)} collective-permute-done((bf16[16,4096]{1,0:T(8,128)(2,1)S(1)}, bf16[16,4096]{1,0:T(8,128)(2,1)S(1)}, u32[]{:S(2)}, u32[]{:S(2)}) %collective-permute-start.9) | collective-permute-done | bytes 131104 | tf_op jit(solution)/shard_map/ppermute | solution.py:112
  41.1 0.4 %collective-permute-done.14.refs_0_ = bf16[16,4096]{1,0:T(8,128)(2,1)S(1)} collective-permute-done((bf16[16,4096]{1,0:T(8,128)(2,1)S(1)}, bf16[16,4096]{1,0:T(8,128)(2,1)S(1)}, u32[]{:S(2)}, u32[]{:S(2)}) %collective-permute-start.14) | collective-permute-done | bytes 131104 | tf_op jit(solution)/shard_map/ppermute | solution.py:112
  41.5 1.6 %collective-permute-done.15.refs_1_ = bf16[16,4096]{1,0:T(8,128)(2,1)S(1)} collective-permute-done((bf16[16,4096]{1,0:T(8,128)(2,1)S(1)}, bf16[16,4096]{1,0:T(8,128)(2,1)S(1)}, u32[]{:S(2)}, u32[]{:S(2)}) %collective-permute-start.15) | collective-permute-done | bytes 131104 | tf_op jit(solution)/shard_map/ppermute | solution.py:112
  43.2 0.7 %add.7 = bf16[16,4096]{1,0:T(8,128)(2,1)} custom-call(f32[16,4096]{1,0:T(8,128)S(1)} %add.6.own_ref, bf16[16,4096]{1,0:T(8,128)(2,1)S(1)} %collective-permute-done.14.refs_0_, bf16[16,4096]{1,0:T(8,128)(2,1)S(1)} %collective-permute-done.15.refs_1_), custom_call_target="tpu_custom_call" | custom-call | flops 1000000 | tf_op jit(solution)/shard_map/add/pallas_call | solution.py:97
  (2 shorter events, 0.0 us)
Async XLA Ops:
  0.0 10.7 %collective-permute-start.3 = (bf16[16,4096]{1,0:T(8,128)(2,1)}, bf16[16,4096]{1,0:T(8,128)(2,1)S(1)}, u32[]{:S(2)}, u32[]{:S(2)}) collective-permute-start(bf16[16,4096]{1,0:T(8,128)(2,1)} %refs_0_.3), channel_id=1, source_target_pairs={{0,8},{2,10},{4,12},{6,14},{8,0},{10,2},{12,4},{14,6},{1,9},{3,11}... | collective-permute-start | bytes 393224 | tf_op jit(solution)/shard_map/ppermute | solution.py:112
  4.0 8.9 %collective-permute-start.2 = (bf16[16,4096]{1,0:T(8,128)(2,1)}, bf16[16,4096]{1,0:T(8,128)(2,1)S(1)}, u32[]{:S(2)}, u32[]{:S(2)}) collective-permute-start(bf16[16,4096]{1,0:T(8,128)(2,1)} %refs_0_.3), channel_id=1, source_target_pairs={{0,4},{2,6},{4,0},{6,2},{8,12},{10,14},{12,8},{14,10},{1,5},{3,7},... | collective-permute-start | bytes 393224 | tf_op jit(solution)/shard_map/ppermute | solution.py:112
  5.6 10.8 %collective-permute-start.1 = (bf16[16,4096]{1,0:T(8,128)(2,1)}, bf16[16,4096]{1,0:T(8,128)(2,1)S(1)}, u32[]{:S(2)}, u32[]{:S(2)}) collective-permute-start(bf16[16,4096]{1,0:T(8,128)(2,1)} %refs_0_.3), channel_id=1, source_target_pairs={{0,2},{2,0},{4,6},{6,4},{8,10},{10,8},{12,14},{14,12},{1,3},{3,1},... | collective-permute-start | bytes 393224 | tf_op jit(solution)/shard_map/ppermute | solution.py:112
  7.1 9.3 %collective-permute-start = (bf16[16,4096]{1,0:T(8,128)(2,1)}, bf16[16,4096]{1,0:T(8,128)(2,1)S(1)}, u32[]{:S(2)}, u32[]{:S(2)}) collective-permute-start(bf16[16,4096]{1,0:T(8,128)(2,1)} %refs_0_.3), channel_id=1, source_target_pairs={{0,6},{2,4},{4,2},{6,0},{8,14},{10,12},{12,10},{14,8},{1,7},{3,5},... | collective-permute-start | bytes 393224 | tf_op jit(solution)/shard_map/ppermute | solution.py:112
  9.7 10.6 %copy-start.1 = (bf16[16,4096]{1,0:T(8,128)(2,1)S(1)}, bf16[16,4096]{1,0:T(8,128)(2,1)}, u32[]{:S(2)}) copy-start(bf16[16,4096]{1,0:T(8,128)(2,1)} %refs_0_.3) | copy-start | bytes 393220
  10.7 7.7 %collective-permute-start.6 = (bf16[16,4096]{1,0:T(8,128)(2,1)S(1)}, bf16[16,4096]{1,0:T(8,128)(2,1)S(1)}, u32[]{:S(2)}, u32[]{:S(2)}) collective-permute-start(bf16[16,4096]{1,0:T(8,128)(2,1)S(1)} %collective-permute-done.3.refs_4_), channel_id=1, source_target_pairs={{0,6},{2,4},{4,2},{6,0},{8,14},{10,12},{12,10},{14,8},{1,7},{3,5},... | collective-permute-start | bytes 393224 | tf_op jit(solution)/shard_map/ppermute | solution.py:112
  12.4 7.9 %collective-permute-start.5 = (bf16[16,4096]{1,0:T(8,128)(2,1)S(1)}, bf16[16,4096]{1,0:T(8,128)(2,1)S(1)}, u32[]{:S(2)}, u32[]{:S(2)}) collective-permute-start(bf16[16,4096]{1,0:T(8,128)(2,1)S(1)} %collective-permute-done.3.refs_4_), channel_id=1, source_target_pairs={{0,2},{2,0},{4,6},{6,4},{8,10},{10,8},{12,14},{14,12},{1,3},{3,1},... | collective-permute-start | bytes 393224 | tf_op jit(solution)/shard_map/ppermute | solution.py:112
  12.9 7.4 %collective-permute-start.4 = (bf16[16,4096]{1,0:T(8,128)(2,1)S(1)}, bf16[16,4096]{1,0:T(8,128)(2,1)S(1)}, u32[]{:S(2)}, u32[]{:S(2)}) collective-permute-start(bf16[16,4096]{1,0:T(8,128)(2,1)S(1)} %collective-permute-done.3.refs_4_), channel_id=1, source_target_pairs={{0,4},{2,6},{4,0},{6,2},{8,12},{10,14},{12,8},{14,10},{1,5},{3,7},... | collective-permute-start | bytes 393224 | tf_op jit(solution)/shard_map/ppermute | solution.py:112
  16.4 7.2 %copy-start = (bf16[512,4096]{1,0:T(8,128)(2,1)S(1)}, bf16[512,4096]{1,0:T(8,128)(2,1)}, u32[]{:S(2)}) copy-start(bf16[512,4096]{1,0:T(8,128)(2,1)} %weight_ref.1) | copy-start | bytes 12582916
  21.0 1.6 %collective-permute-start.7 = (f32[128,512]{1,0:T(8,128)S(1)}, f32[128,512]{1,0:T(8,128)S(1)}, u32[]{:S(2)}, u32[]{:S(2)}) collective-permute-start(f32[128,512]{1,0:T(8,128)S(1)} %project.2.gate_ref), channel_id=1, source_target_pairs={{0,1},{1,0},{2,3},{3,2},{4,5},{5,4},{6,7},{7,6},{8,9},{9,8},{10,11... | collective-permute-start | bytes 786440 | tf_op jit(solution)/shard_map/ppermute | solution.py:115
  21.8 1.7 %collective-permute-start.8 = (f32[128,512]{1,0:T(8,128)S(1)}, f32[128,512]{1,0:T(8,128)S(1)}, u32[]{:S(2)}, u32[]{:S(2)}) collective-permute-start(f32[128,512]{1,0:T(8,128)S(1)} %project.3.up_ref), channel_id=1, source_target_pairs={{0,1},{1,0},{2,3},{3,2},{4,5},{5,4},{6,7},{7,6},{8,9},{9,8},{10,11... | collective-permute-start | bytes 786440 | tf_op jit(solution)/shard_map/ppermute | solution.py:115
  24.3 7.3 %collective-permute-start.11 = (bf16[16,4096]{1,0:T(8,128)(2,1)S(1)}, bf16[16,4096]{1,0:T(8,128)(2,1)S(1)}, u32[]{:S(2)}, u32[]{:S(2)}) collective-permute-start(bf16[16,4096]{1,0:T(8,128)(2,1)S(1)} %get-tuple-element.22), channel_id=1, source_target_pairs={{0,6},{2,4},{4,2},{6,0},{8,14},{10,12},{12,10},{14,8},{1,7},{3,5},... | collective-permute-start | bytes 393224 | tf_op jit(solution)/shard_map/ppermute | solution.py:112
  25.8 8.0 %collective-permute-start.12 = (bf16[16,4096]{1,0:T(8,128)(2,1)S(1)}, bf16[16,4096]{1,0:T(8,128)(2,1)S(1)}, u32[]{:S(2)}, u32[]{:S(2)}) collective-permute-start(bf16[16,4096]{1,0:T(8,128)(2,1)S(1)} %get-tuple-element.23), channel_id=1, source_target_pairs={{0,2},{2,0},{4,6},{6,4},{8,10},{10,8},{12,14},{14,12},{1,3},{3,1},... | collective-permute-start | bytes 393224 | tf_op jit(solution)/shard_map/ppermute | solution.py:112
  27.2 6.6 %collective-permute-start.13 = (bf16[16,4096]{1,0:T(8,128)(2,1)S(1)}, bf16[16,4096]{1,0:T(8,128)(2,1)S(1)}, u32[]{:S(2)}, u32[]{:S(2)}) collective-permute-start(bf16[16,4096]{1,0:T(8,128)(2,1)S(1)} %get-tuple-element.24), channel_id=1, source_target_pairs={{0,4},{2,6},{4,0},{6,2},{8,12},{10,14},{12,8},{14,10},{1,5},{3,7},... | collective-permute-start | bytes 393224 | tf_op jit(solution)/shard_map/ppermute | solution.py:112
  27.9 8.6 %collective-permute-start.10 = (bf16[16,4096]{1,0:T(8,128)(2,1)S(1)}, bf16[16,4096]{1,0:T(8,128)(2,1)S(1)}, u32[]{:S(2)}, u32[]{:S(2)}) collective-permute-start(bf16[16,4096]{1,0:T(8,128)(2,1)S(1)} %get-tuple-element.20), channel_id=1, source_target_pairs={{0,4},{2,6},{4,0},{6,2},{8,12},{10,14},{12,8},{14,10},{1,5},{3,7},... | collective-permute-start | bytes 393224 | tf_op jit(solution)/shard_map/ppermute | solution.py:112
  29.2 11.8 %collective-permute-start.9 = (bf16[16,4096]{1,0:T(8,128)(2,1)S(1)}, bf16[16,4096]{1,0:T(8,128)(2,1)S(1)}, u32[]{:S(2)}, u32[]{:S(2)}) collective-permute-start(bf16[16,4096]{1,0:T(8,128)(2,1)S(1)} %get-tuple-element.18), channel_id=1, source_target_pairs={{0,4},{2,6},{4,0},{6,2},{8,12},{10,14},{12,8},{14,10},{1,5},{3,7},... | collective-permute-start | bytes 393224 | tf_op jit(solution)/shard_map/ppermute | solution.py:112
  33.9 9.3 %collective-permute-start.15 = (bf16[16,4096]{1,0:T(8,128)(2,1)S(1)}, bf16[16,4096]{1,0:T(8,128)(2,1)S(1)}, u32[]{:S(2)}, u32[]{:S(2)}) collective-permute-start(bf16[16,4096]{1,0:T(8,128)(2,1)S(1)} %add.4.refs_1_), channel_id=1, source_target_pairs={{0,8},{2,10},{4,12},{6,14},{8,0},{10,2},{12,4},{14,6},{1,9},{3,11}... | collective-permute-start | bytes 393224 | tf_op jit(solution)/shard_map/ppermute | solution.py:112
  36.5 5.0 %collective-permute-start.14 = (bf16[16,4096]{1,0:T(8,128)(2,1)S(1)}, bf16[16,4096]{1,0:T(8,128)(2,1)S(1)}, u32[]{:S(2)}, u32[]{:S(2)}) collective-permute-start(bf16[16,4096]{1,0:T(8,128)(2,1)S(1)} %add.5.refs_1_), channel_id=1, source_target_pairs={{0,2},{2,0},{4,6},{6,4},{8,10},{10,8},{12,14},{14,12},{1,3},{3,1},... | collective-permute-start | bytes 393224 | tf_op jit(solution)/shard_map/ppermute | solution.py:112

commit v21 on v20

--- a/solution.py
+++ b/solution.py
@@ -105,11 +105,50 @@
     )(own, *arrived, *after)
 
 
+def add_in_turn_kernel(count, core_ref, own_ref, other_ref, *refs):
+    first_ref, second_ref = refs[-2:]
+    total = own_ref[...]
+    for ref in refs[:count]:
+        total = total + ref[...].astype(F32)
+    total = total.astype(first_ref.dtype)
+
+    @pl.when(core_ref[0] == 0)
+    def _():
+        first_ref[...] = total
+        second_ref[...] = other_ref[...]
+
+    @pl.when(core_ref[0] != 0)
+    def _():
+        first_ref[...] = other_ref[...]
+        second_ref[...] = total
+
+
+def add_in_turn(core, own, arrived, other):
+    out = jax.ShapeDtypeStruct(own.shape, BF16)
+    return pl.pallas_call(
+        functools.partial(add_in_turn_kernel, len(arrived)),
+        in_specs=[pl.BlockSpec(memory_space=pltpu.SMEM)]
+        + [pl.BlockSpec(memory_space=pltpu.VMEM)] * (2 + len(arrived)),
+        out_shape=[out, out],
+        compiler_params=pltpu.CompilerParams(vmem_limit_bytes=2 << 20),
+        cost_estimate=pl.CostEstimate(flops=1000000, bytes_accessed=0, transcendentals=0),
+        name="add_in_turn",
+    )(core, own, other, *arrived)
+
+
 def make_local(wide, narrow):
     fars = list(range(4, wide, 4))
 
     def swap(value, bits):
         return lax.ppermute(value, "wide", [(i, i ^ bits) for i in range(wide)])
+
+    def swap_by_core(value, bits, other_bits):
+        pairs = []
+        for i in range(wide):
+            for core in range(narrow):
+                target = i ^ (other_bits if core else bits)
+                pairs.append((i * narrow + core, target * narrow + core))
+        return lax.ppermute(value, ("wide", "narrow"), pairs)
 
     def across_cores(value):
         return lax.ppermute(value, "narrow", [(i, (i + 1) % narrow) for i in range(narrow)])
@@ -138,14 +177,19 @@
             down_weight, rows, [F32 if b in stay else BF16 for b in order],
         )
         part = dict(zip(order, outs))
-        sums = []
+        core = lax.axis_index("narrow").reshape(1)
+        sums, arrived = [], []
         for far in fars:
-            quad = [swap(part[far + near], near) for near in (3, 1, 2)]
-            sums.append(add(part[far], quad, BF16))
-        arrived = [swap(value, far) for value, far in zip(sums, fars)]
+            quad = [swap(part[far + near], near) for near in (2, 3, 1)]
+            if sums:
+                sums.append(add(part[far], quad, BF16))
+                arrived.append(swap(sums[-1], far))
+                continue
+            sums = list(add_in_turn(core, part[far], quad, part[2]))
+            arrived = [swap_by_core(sums[0], far, 2), swap_by_core(sums[1], 2, far)]
         pair = add(part[1], [swap(part[3], 2)], BF16, after=sums)
-        total = add(part[0], [swap(part[2], 2)], F32, 1500000000, after=[pair])
-        return add(total, [swap(pair, 1)] + arrived, BF16)
+        total = add(part[0], arrived, F32, 3000000000)
+        return add(total, [swap(pair, 1)], BF16)
 
     return local
 

time: 44 us -> 45.1 us (1.025)
  waiting for transfers between devices: 15.6 us -> 16.4 us
    ppermute x0 -> x2, waiting for transfers between devices: none -> 5.42 us  [swap_by_core(): return lax.ppermute(value, ('wide', 'narrow'), pairs)]
    ppermute x14 -> x12, waiting for transfers between devices: 14.4 us -> 9.86 us  [swap(): return lax.ppermute(value, 'wide', [(i, i ^ bits) for i in range(wide)])]
    ppermute x0 -> x2, starting transfers between devices: none -> 3.13 us  [swap_by_core(): return lax.ppermute(value, ('wide', 'narrow'), pairs)]
    ppermute x14 -> x12, starting transfers between devices: 20.1 us -> 17.2 us  [swap(): return lax.ppermute(value, 'wide', [(i, i ^ bits) for i in range(wide)])]
  transfers between devices with their start and end apart: 16 -> 16, of which waited for: 11 -> 9; matrix products, arithmetic and copies ran while one was open for 0% -> 0% of each run, Pallas kernels for 12% -> 12%
where the time goes in v21:
time: 45.1 us; the launch traced here: 45 us
  starting transfers between devices  21 us (47%)
  waiting for transfers between devices  16.4 us (36%)
  Pallas kernels  7.42 us (16%)
    ppermute x12, starting transfers between devices, swap(): return lax.ppermute(value, 'wide', [(i, i ^ bits) for i in range(wide)])  17.2 us
    ppermute x12, waiting for transfers between devices, swap(): return lax.ppermute(value, 'wide', [(i, i ^ bits) for i in range(wide)])  9.86 us
    ppermute x2, waiting for transfers between devices, swap_by_core(): return lax.ppermute(value, ('wide', 'narrow'), pairs)  5.42 us
    pallas_call x2, Pallas kernels, fetch(): pl.pallas_call(functools.partial(fetch_kernel, pieces), in_specs=[pl.Bloc...  4.43 us
    ppermute x2, starting transfers between devices, swap_by_core(): return lax.ppermute(value, ('wide', 'narrow'), pairs)  3.13 us
    pallas_call x3, Pallas kernels, call(): pl.pallas_call(kernel, out_shape=out_shape, compiler_params=pltpu.Compile...  2.17 us
    ppermute x2, waiting for transfers between devices, across_cores(): lax.ppermute(value, 'narrow', [(i, (i + 1) % narrow) for i in range(narro...  1.16 us
  transfers between devices with their start and end apart: 16, of which 9 were waited for; matrix products, arithmetic and copies ran while one was open for 0% of the time, Pallas kernels for 12%

profile of v21, /device:TPU:0, one launch (start us, length us, event | category | flops | bytes accessed | tf_op | source)
XLA Modules:
  0.0 45.0 jit_solution(8576170165760168409)
XLA Ops:
  0.0 4.0 %collective-permute-start.3 = (bf16[16,4096]{1,0:T(8,128)(2,1)}, bf16[16,4096]{1,0:T(8,128)(2,1)S(1)}, u32[]{:S(2)}, u32[]{:S(2)}) collective-permute-start(bf16[16,4096]{1,0:T(8,128)(2,1)} %refs_0_.3), channel_id=1, source_target_pairs={{0,8},{2,10},{4,12},{6,14},{8,0},{10,2},{12,4},{14,6},{1,9},{3,11}... | collective-permute-start | bytes 393224 | tf_op jit(solution)/shard_map/ppermute | solution.py:143
  4.0 2.5 %collective-permute-start = (bf16[16,4096]{1,0:T(8,128)(2,1)}, bf16[16,4096]{1,0:T(8,128)(2,1)S(1)}, u32[]{:S(2)}, u32[]{:S(2)}) collective-permute-start(bf16[16,4096]{1,0:T(8,128)(2,1)} %refs_0_.3), channel_id=1, source_target_pairs={{0,6},{2,4},{4,2},{6,0},{8,14},{10,12},{12,10},{14,8},{1,7},{3,5},... | collective-permute-start | bytes 393224 | tf_op jit(solution)/shard_map/ppermute | solution.py:143
  6.6 0.5 %collective-permute-start.1 = (bf16[16,4096]{1,0:T(8,128)(2,1)}, bf16[16,4096]{1,0:T(8,128)(2,1)S(1)}, u32[]{:S(2)}, u32[]{:S(2)}) collective-permute-start(bf16[16,4096]{1,0:T(8,128)(2,1)} %refs_0_.3), channel_id=1, source_target_pairs={{0,2},{2,0},{4,6},{6,4},{8,10},{10,8},{12,14},{14,12},{1,3},{3,1},... | collective-permute-start | bytes 393224 | tf_op jit(solution)/shard_map/ppermute | solution.py:143
  7.1 0.4 collective-permute-start.2
  7.5 2.2 %fetch.2.refs_8_ = bf16[4096,512]{1,0:T(8,128)(2,1)S(1)} custom-call(bf16[4096,512]{1,0:T(8,128)(2,1)} %source.2), custom_call_target="tpu_custom_call" | custom-call | flops 2000000000 | tf_op jit(solution)/shard_map/fetch/pallas_call | solution.py:37
  9.7 0.0 copy-start.1
  9.8 0.9 %collective-permute-done.3.refs_4_ = bf16[16,4096]{1,0:T(8,128)(2,1)S(1)} collective-permute-done((bf16[16,4096]{1,0:T(8,128)(2,1)}, bf16[16,4096]{1,0:T(8,128)(2,1)S(1)}, u32[]{:S(2)}, u32[]{:S(2)}) %collective-permute-start.3) | collective-permute-done | bytes 131104 | tf_op jit(solution)/shard_map/ppermute | solution.py:143
  10.6 0.8 %collective-permute-start.4 = (bf16[16,4096]{1,0:T(8,128)(2,1)S(1)}, bf16[16,4096]{1,0:T(8,128)(2,1)S(1)}, u32[]{:S(2)}, u32[]{:S(2)}) collective-permute-start(bf16[16,4096]{1,0:T(8,128)(2,1)S(1)} %collective-permute-done.3.refs_4_), channel_id=1, source_target_pairs={{0,4},{2,6},{4,0},{6,2},{8,12},{10,14},{12,8},{14,10},{1,5},{3,7},... | collective-permute-start | bytes 393224 | tf_op jit(solution)/shard_map/ppermute | solution.py:143
  11.4 1.5 %collective-permute-start.5 = (bf16[16,4096]{1,0:T(8,128)(2,1)S(1)}, bf16[16,4096]{1,0:T(8,128)(2,1)S(1)}, u32[]{:S(2)}, u32[]{:S(2)}) collective-permute-start(bf16[16,4096]{1,0:T(8,128)(2,1)S(1)} %collective-permute-done.3.refs_4_), channel_id=1, source_target_pairs={{0,2},{2,0},{4,6},{6,4},{8,10},{10,8},{12,14},{14,12},{1,3},{3,1},... | collective-permute-start | bytes 393224 | tf_op jit(solution)/shard_map/ppermute | solution.py:143
  12.9 0.0 collective-permute-done.refs_1_
  13.0 1.2 %collective-permute-start.6 = (bf16[16,4096]{1,0:T(8,128)(2,1)S(1)}, bf16[16,4096]{1,0:T(8,128)(2,1)S(1)}, u32[]{:S(2)}, u32[]{:S(2)}) collective-permute-start(bf16[16,4096]{1,0:T(8,128)(2,1)S(1)} %collective-permute-done.3.refs_4_), channel_id=1, source_target_pairs={{0,6},{2,4},{4,2},{6,0},{8,14},{10,12},{12,10},{14,8},{1,7},{3,5},... | collective-permute-start | bytes 393224 | tf_op jit(solution)/shard_map/ppermute | solution.py:143
  14.2 2.2 %fetch.3.refs_8_ = bf16[4096,512]{1,0:T(8,128)(2,1)S(1)} custom-call(bf16[4096,512]{1,0:T(8,128)(2,1)} %source.3), custom_call_target="tpu_custom_call" | custom-call | flops 2000000000 | tf_op jit(solution)/shard_map/fetch/pallas_call | solution.py:37
  16.4 0.0 copy-start
  16.4 0.0 collective-permute-done.1.refs_2_
  16.4 0.0 collective-permute-done.2.refs_3_
  16.4 2.0 %collective-permute-done.4.refs_5_ = bf16[16,4096]{1,0:T(8,128)(2,1)S(1)} collective-permute-done((bf16[16,4096]{1,0:T(8,128)(2,1)S(1)}, bf16[16,4096]{1,0:T(8,128)(2,1)S(1)}, u32[]{:S(2)}, u32[]{:S(2)}) %collective-permute-start.4) | collective-permute-done | bytes 131104 | tf_op jit(solution)/shard_map/ppermute | solution.py:143
  18.4 0.0 collective-permute-done.5.refs_6_
  18.4 1.8 %collective-permute-done.6.refs_7_ = bf16[16,4096]{1,0:T(8,128)(2,1)S(1)} collective-permute-done((bf16[16,4096]{1,0:T(8,128)(2,1)S(1)}, bf16[16,4096]{1,0:T(8,128)(2,1)S(1)}, u32[]{:S(2)}, u32[]{:S(2)}) %collective-permute-start.6) | collective-permute-done | bytes 131104 | tf_op jit(solution)/shard_map/ppermute | solution.py:143
  20.2 0.0 copy-done.1
  20.2 0.7 %project.2.gate_ref = f32[128,512]{1,0:T(8,128)S(1)} custom-call(bf16[16,4096]{1,0:T(8,128)(2,1)S(1)} %copy-done.1, bf16[16,4096]{1,0:T(8,128)(2,1)S(1)} %collective-permute-done.refs_1_, bf16[16,4096]{1,0:T(8,128)(2,1)S(1)} %collective-permute-done.1.refs_2_, bf16[16,4096]{1,0:T(8,128)(2,1)S(1)} %collective-permute-done.2.refs_3_, ...), custom_call_target="tpu_custom_call" | custom-call | flops 400000000 | tf_op jit(solution)/shard_map/project/pallas_call | solution.py:15
  21.0 0.1 collective-permute-start.7
  21.0 0.7 %project.3.up_ref = f32[128,512]{1,0:T(8,128)S(1)} custom-call(bf16[16,4096]{1,0:T(8,128)(2,1)S(1)} %copy-done.1, bf16[16,4096]{1,0:T(8,128)(2,1)S(1)} %collective-permute-done.refs_1_, bf16[16,4096]{1,0:T(8,128)(2,1)S(1)} %collective-permute-done.1.refs_2_, bf16[16,4096]{1,0:T(8,128)(2,1)S(1)} %collective-permute-done.2.refs_3_, ...), custom_call_target="tpu_custom_call" | custom-call | flops 400000000 | tf_op jit(solution)/shard_map/project/pallas_call | solution.py:15
  21.8 0.6 %collective-permute-start.8 = (f32[128,512]{1,0:T(8,128)S(1)}, f32[128,512]{1,0:T(8,128)S(1)}, u32[]{:S(2)}, u32[]{:S(2)}) collective-permute-start(f32[128,512]{1,0:T(8,128)S(1)} %project.3.up_ref), channel_id=1, source_target_pairs={{0,1},{1,0},{2,3},{3,2},{4,5},{5,4},{6,7},{7,6},{8,9},{9,8},{10,11... | collective-permute-start | bytes 786440 | tf_op jit(solution)/shard_map/ppermute | solution.py:154
  22.3 0.2 collective-permute-done.7.gate_other_ref
  22.6 0.9 %collective-permute-done.8.up_other_ref = f32[128,512]{1,0:T(8,128)S(1)} collective-permute-done((f32[128,512]{1,0:T(8,128)S(1)}, f32[128,512]{1,0:T(8,128)S(1)}, u32[]{:S(2)}, u32[]{:S(2)}) %collective-permute-start.8) | collective-permute-done | bytes 262176 | tf_op jit(solution)/shard_map/ppermute | solution.py:154
  23.5 0.0 copy-done
  23.5 0.7 %down.1 = (f32[16,4096]{1,0:T(8,128)S(1)}, bf16[16,4096]{1,0:T(8,128)(2,1)S(1)}, f32[16,4096]{1,0:T(8,128)S(1)}, bf16[16,4096]{1,0:T(8,128)(2,1)S(1)}, f32[16,40...) custom-call(f32[128,512]{1,0:T(8,128)S(1)} %project.2.gate_ref, ...), custom_call_target="tpu_custom_call" | custom-call | flops 536870912 | tf_op jit(solution)/shard_map/down/pallas_call | solution.py:15
  24.2 1.6 %collective-permute-start.10 = (bf16[16,4096]{1,0:T(8,128)(2,1)S(1)}, bf16[16,4096]{1,0:T(8,128)(2,1)S(1)}, u32[]{:S(2)}, u32[]{:S(2)}) collective-permute-start(bf16[16,4096]{1,0:T(8,128)(2,1)S(1)} %get-tuple-element.23), channel_id=1, source_target_pairs={{0,6},{2,4},{4,2},{6,0},{8,14},{10,12},{12,10},{14,8},{1,7},{3,5},... | collective-permute-start | bytes 393224 | tf_op jit(solution)/shard_map/ppermute | solution.py:143
  25.8 1.4 %collective-permute-start.11 = (bf16[16,4096]{1,0:T(8,128)(2,1)S(1)}, bf16[16,4096]{1,0:T(8,128)(2,1)S(1)}, u32[]{:S(2)}, u32[]{:S(2)}) collective-permute-start(bf16[16,4096]{1,0:T(8,128)(2,1)S(1)} %get-tuple-element.24), channel_id=1, source_target_pairs={{0,2},{2,0},{4,6},{6,4},{8,10},{10,8},{12,14},{14,12},{1,3},{3,1},... | collective-permute-start | bytes 393224 | tf_op jit(solution)/shard_map/ppermute | solution.py:143
  27.2 0.6 %collective-permute-start.9 = (bf16[16,4096]{1,0:T(8,128)(2,1)S(1)}, bf16[16,4096]{1,0:T(8,128)(2,1)S(1)}, u32[]{:S(2)}, u32[]{:S(2)}) collective-permute-start(bf16[16,4096]{1,0:T(8,128)(2,1)S(1)} %get-tuple-element.22), channel_id=1, source_target_pairs={{0,4},{2,6},{4,0},{6,2},{8,12},{10,14},{12,8},{14,10},{1,5},{3,7},... | collective-permute-start | bytes 393224 | tf_op jit(solution)/shard_map/ppermute | solution.py:143
  27.8 1.4 %collective-permute-start.14 = (bf16[16,4096]{1,0:T(8,128)(2,1)S(1)}, bf16[16,4096]{1,0:T(8,128)(2,1)S(1)}, u32[]{:S(2)}, u32[]{:S(2)}) collective-permute-start(bf16[16,4096]{1,0:T(8,128)(2,1)S(1)} %get-tuple-element.28), channel_id=1, source_target_pairs={{0,4},{2,6},{4,0},{6,2},{8,12},{10,14},{12,8},{14,10},{1,5},{3,7},... | collective-permute-start | bytes 393224 | tf_op jit(solution)/shard_map/ppermute | solution.py:143
  29.2 2.3 %collective-permute-done.10.refs_1_ = bf16[16,4096]{1,0:T(8,128)(2,1)S(1)} collective-permute-done((bf16[16,4096]{1,0:T(8,128)(2,1)S(1)}, bf16[16,4096]{1,0:T(8,128)(2,1)S(1)}, u32[]{:S(2)}, u32[]{:S(2)}) %collective-permute-start.10) | collective-permute-done | bytes 131104 | tf_op jit(solution)/shard_map/ppermute | solution.py:143
  31.6 2.2 %collective-permute-done.11.refs_2_ = bf16[16,4096]{1,0:T(8,128)(2,1)S(1)} collective-permute-done((bf16[16,4096]{1,0:T(8,128)(2,1)S(1)}, bf16[16,4096]{1,0:T(8,128)(2,1)S(1)}, u32[]{:S(2)}, u32[]{:S(2)}) %collective-permute-start.11) | collective-permute-done | bytes 131104 | tf_op jit(solution)/shard_map/ppermute | solution.py:143
  33.8 0.6 %collective-permute-done.9.refs_0_ = bf16[16,4096]{1,0:T(8,128)(2,1)S(1)} collective-permute-done((bf16[16,4096]{1,0:T(8,128)(2,1)S(1)}, bf16[16,4096]{1,0:T(8,128)(2,1)S(1)}, u32[]{:S(2)}, u32[]{:S(2)}) %collective-permute-start.9) | collective-permute-done | bytes 131104 | tf_op jit(solution)/shard_map/ppermute | solution.py:143
  34.4 0.1 add_in_turn.1
  34.5 2.6 %collective-permute-start.12 = (bf16[16,4096]{1,0:T(8,128)(2,1)S(1)}, bf16[16,4096]{1,0:T(8,128)(2,1)S(1)}, u32[]{:S(2)}, u32[]{:S(2)}) collective-permute-start(bf16[16,4096]{1,0:T(8,128)(2,1)S(1)} %get-tuple-element.25.refs_1_), channel_id=1, source_target_pairs={{0,8},{1,5},{2,10},{3,7},{4,12},{5,1},{6,14},{7,3},{8,0},{9,13},{1... | collective-permute-start | bytes 393224 | tf_op jit(solution)/shard_map/ppermute | solution.py:151
  37.0 0.6 %collective-permute-start.13 = (bf16[16,4096]{1,0:T(8,128)(2,1)S(1)}, bf16[16,4096]{1,0:T(8,128)(2,1)S(1)}, u32[]{:S(2)}, u32[]{:S(2)}) collective-permute-start(bf16[16,4096]{1,0:T(8,128)(2,1)S(1)} %get-tuple-element.26.refs_2_), channel_id=1, source_target_pairs={{0,4},{1,9},{2,6},{3,11},{4,0},{5,13},{6,2},{7,15},{8,12},{9,1},{1... | collective-permute-start | bytes 393224 | tf_op jit(solution)/shard_map/ppermute | solution.py:151
  37.6 0.0 collective-permute-done.14.refs_0_
  37.6 1.2 %collective-permute-start.15 = (bf16[16,4096]{1,0:T(8,128)(2,1)S(1)}, bf16[16,4096]{1,0:T(8,128)(2,1)S(1)}, u32[]{:S(2)}, u32[]{:S(2)}) collective-permute-start(bf16[16,4096]{1,0:T(8,128)(2,1)S(1)} %add.4), channel_id=1, source_target_pairs={{0,2},{2,0},{4,6},{6,4},{8,10},{10,8},{12,14},{14,12},{1,3},{3,1},... | collective-permute-start | bytes 393224 | tf_op jit(solution)/shard_map/ppermute | solution.py:143
  38.8 5.4 %collective-permute-done.12.refs_0_ = bf16[16,4096]{1,0:T(8,128)(2,1)S(1)} collective-permute-done((bf16[16,4096]{1,0:T(8,128)(2,1)S(1)}, bf16[16,4096]{1,0:T(8,128)(2,1)S(1)}, u32[]{:S(2)}, u32[]{:S(2)}) %collective-permute-start.12) | collective-permute-done | bytes 131104 | tf_op jit(solution)/shard_map/ppermute | solution.py:151
  44.2 0.0 collective-permute-done.13.refs_1_
  44.3 0.0 collective-permute-done.15.refs_0_
  44.3 0.7 %add.5 = bf16[16,4096]{1,0:T(8,128)(2,1)} custom-call(f32[16,4096]{1,0:T(8,128)S(1)} %add.3.own_ref, bf16[16,4096]{1,0:T(8,128)(2,1)S(1)} %collective-permute-done.15.refs_0_), custom_call_target="tpu_custom_call" | custom-call | flops 1000000 | tf_op jit(solution)/shard_map/add/pallas_call | solution.py:97
  (2 shorter events, 0.1 us)
Async XLA Ops:
  0.0 10.6 %collective-permute-start.3 = (bf16[16,4096]{1,0:T(8,128)(2,1)}, bf16[16,4096]{1,0:T(8,128)(2,1)S(1)}, u32[]{:S(2)}, u32[]{:S(2)}) collective-permute-start(bf16[16,4096]{1,0:T(8,128)(2,1)} %refs_0_.3), channel_id=1, source_target_pairs={{0,8},{2,10},{4,12},{6,14},{8,0},{10,2},{12,4},{14,6},{1,9},{3,11}... | collective-permute-start | bytes 393224 | tf_op jit(solution)/shard_map/ppermute | solution.py:143
  4.0 8.9 %collective-permute-start = (bf16[16,4096]{1,0:T(8,128)(2,1)}, bf16[16,4096]{1,0:T(8,128)(2,1)S(1)}, u32[]{:S(2)}, u32[]{:S(2)}) collective-permute-start(bf16[16,4096]{1,0:T(8,128)(2,1)} %refs_0_.3), channel_id=1, source_target_pairs={{0,6},{2,4},{4,2},{6,0},{8,14},{10,12},{12,10},{14,8},{1,7},{3,5},... | collective-permute-start | bytes 393224 | tf_op jit(solution)/shard_map/ppermute | solution.py:143
  6.6 9.8 %collective-permute-start.1 = (bf16[16,4096]{1,0:T(8,128)(2,1)}, bf16[16,4096]{1,0:T(8,128)(2,1)S(1)}, u32[]{:S(2)}, u32[]{:S(2)}) collective-permute-start(bf16[16,4096]{1,0:T(8,128)(2,1)} %refs_0_.3), channel_id=1, source_target_pairs={{0,2},{2,0},{4,6},{6,4},{8,10},{10,8},{12,14},{14,12},{1,3},{3,1},... | collective-permute-start | bytes 393224 | tf_op jit(solution)/shard_map/ppermute | solution.py:143
  7.1 9.3 %collective-permute-start.2 = (bf16[16,4096]{1,0:T(8,128)(2,1)}, bf16[16,4096]{1,0:T(8,128)(2,1)S(1)}, u32[]{:S(2)}, u32[]{:S(2)}) collective-permute-start(bf16[16,4096]{1,0:T(8,128)(2,1)} %refs_0_.3), channel_id=1, source_target_pairs={{0,4},{2,6},{4,0},{6,2},{8,12},{10,14},{12,8},{14,10},{1,5},{3,7},... | collective-permute-start | bytes 393224 | tf_op jit(solution)/shard_map/ppermute | solution.py:143
  9.7 10.5 %copy-start.1 = (bf16[16,4096]{1,0:T(8,128)(2,1)S(1)}, bf16[16,4096]{1,0:T(8,128)(2,1)}, u32[]{:S(2)}) copy-start(bf16[16,4096]{1,0:T(8,128)(2,1)} %refs_0_.3) | copy-start | bytes 393220
  10.6 7.8 %collective-permute-start.4 = (bf16[16,4096]{1,0:T(8,128)(2,1)S(1)}, bf16[16,4096]{1,0:T(8,128)(2,1)S(1)}, u32[]{:S(2)}, u32[]{:S(2)}) collective-permute-start(bf16[16,4096]{1,0:T(8,128)(2,1)S(1)} %collective-permute-done.3.refs_4_), channel_id=1, source_target_pairs={{0,4},{2,6},{4,0},{6,2},{8,12},{10,14},{12,8},{14,10},{1,5},{3,7},... | collective-permute-start | bytes 393224 | tf_op jit(solution)/shard_map/ppermute | solution.py:143
  11.4 7.0 %collective-permute-start.5 = (bf16[16,4096]{1,0:T(8,128)(2,1)S(1)}, bf16[16,4096]{1,0:T(8,128)(2,1)S(1)}, u32[]{:S(2)}, u32[]{:S(2)}) collective-permute-start(bf16[16,4096]{1,0:T(8,128)(2,1)S(1)} %collective-permute-done.3.refs_4_), channel_id=1, source_target_pairs={{0,2},{2,0},{4,6},{6,4},{8,10},{10,8},{12,14},{14,12},{1,3},{3,1},... | collective-permute-start | bytes 393224 | tf_op jit(solution)/shard_map/ppermute | solution.py:143
  13.0 7.3 %collective-permute-start.6 = (bf16[16,4096]{1,0:T(8,128)(2,1)S(1)}, bf16[16,4096]{1,0:T(8,128)(2,1)S(1)}, u32[]{:S(2)}, u32[]{:S(2)}) collective-permute-start(bf16[16,4096]{1,0:T(8,128)(2,1)S(1)} %collective-permute-done.3.refs_4_), channel_id=1, source_target_pairs={{0,6},{2,4},{4,2},{6,0},{8,14},{10,12},{12,10},{14,8},{1,7},{3,5},... | collective-permute-start | bytes 393224 | tf_op jit(solution)/shard_map/ppermute | solution.py:143
  16.4 7.1 %copy-start = (bf16[512,4096]{1,0:T(8,128)(2,1)S(1)}, bf16[512,4096]{1,0:T(8,128)(2,1)}, u32[]{:S(2)}) copy-start(bf16[512,4096]{1,0:T(8,128)(2,1)} %weight_ref.1) | copy-start | bytes 12582916
  21.0 1.6 %collective-permute-start.7 = (f32[128,512]{1,0:T(8,128)S(1)}, f32[128,512]{1,0:T(8,128)S(1)}, u32[]{:S(2)}, u32[]{:S(2)}) collective-permute-start(f32[128,512]{1,0:T(8,128)S(1)} %project.2.gate_ref), channel_id=1, source_target_pairs={{0,1},{1,0},{2,3},{3,2},{4,5},{5,4},{6,7},{7,6},{8,9},{9,8},{10,11... | collective-permute-start | bytes 786440 | tf_op jit(solution)/shard_map/ppermute | solution.py:154
  21.8 1.7 %collective-permute-start.8 = (f32[128,512]{1,0:T(8,128)S(1)}, f32[128,512]{1,0:T(8,128)S(1)}, u32[]{:S(2)}, u32[]{:S(2)}) collective-permute-start(f32[128,512]{1,0:T(8,128)S(1)} %project.3.up_ref), channel_id=1, source_target_pairs={{0,1},{1,0},{2,3},{3,2},{4,5},{5,4},{6,7},{7,6},{8,9},{9,8},{10,11... | collective-permute-start | bytes 786440 | tf_op jit(solution)/shard_map/ppermute | solution.py:154
  24.2 7.3 %collective-permute-start.10 = (bf16[16,4096]{1,0:T(8,128)(2,1)S(1)}, bf16[16,4096]{1,0:T(8,128)(2,1)S(1)}, u32[]{:S(2)}, u32[]{:S(2)}) collective-permute-start(bf16[16,4096]{1,0:T(8,128)(2,1)S(1)} %get-tuple-element.23), channel_id=1, source_target_pairs={{0,6},{2,4},{4,2},{6,0},{8,14},{10,12},{12,10},{14,8},{1,7},{3,5},... | collective-permute-start | bytes 393224 | tf_op jit(solution)/shard_map/ppermute | solution.py:143
  25.8 8.0 %collective-permute-start.11 = (bf16[16,4096]{1,0:T(8,128)(2,1)S(1)}, bf16[16,4096]{1,0:T(8,128)(2,1)S(1)}, u32[]{:S(2)}, u32[]{:S(2)}) collective-permute-start(bf16[16,4096]{1,0:T(8,128)(2,1)S(1)} %get-tuple-element.24), channel_id=1, source_target_pairs={{0,2},{2,0},{4,6},{6,4},{8,10},{10,8},{12,14},{14,12},{1,3},{3,1},... | collective-permute-start | bytes 393224 | tf_op jit(solution)/shard_map/ppermute | solution.py:143
  27.2 7.2 %collective-permute-start.9 = (bf16[16,4096]{1,0:T(8,128)(2,1)S(1)}, bf16[16,4096]{1,0:T(8,128)(2,1)S(1)}, u32[]{:S(2)}, u32[]{:S(2)}) collective-permute-start(bf16[16,4096]{1,0:T(8,128)(2,1)S(1)} %get-tuple-element.22), channel_id=1, source_target_pairs={{0,4},{2,6},{4,0},{6,2},{8,12},{10,14},{12,8},{14,10},{1,5},{3,7},... | collective-permute-start | bytes 393224 | tf_op jit(solution)/shard_map/ppermute | solution.py:143
  27.8 9.8 %collective-permute-start.14 = (bf16[16,4096]{1,0:T(8,128)(2,1)S(1)}, bf16[16,4096]{1,0:T(8,128)(2,1)S(1)}, u32[]{:S(2)}, u32[]{:S(2)}) collective-permute-start(bf16[16,4096]{1,0:T(8,128)(2,1)S(1)} %get-tuple-element.28), channel_id=1, source_target_pairs={{0,4},{2,6},{4,0},{6,2},{8,12},{10,14},{12,8},{14,10},{1,5},{3,7},... | collective-permute-start | bytes 393224 | tf_op jit(solution)/shard_map/ppermute | solution.py:143
  34.5 9.8 %collective-permute-start.12 = (bf16[16,4096]{1,0:T(8,128)(2,1)S(1)}, bf16[16,4096]{1,0:T(8,128)(2,1)S(1)}, u32[]{:S(2)}, u32[]{:S(2)}) collective-permute-start(bf16[16,4096]{1,0:T(8,128)(2,1)S(1)} %get-tuple-element.25.refs_1_), channel_id=1, source_target_pairs={{0,8},{1,5},{2,10},{3,7},{4,12},{5,1},{6,14},{7,3},{8,0},{9,13},{1... | collective-permute-start | bytes 393224 | tf_op jit(solution)/shard_map/ppermute | solution.py:151
  37.0 7.2 %collective-permute-start.13 = (bf16[16,4096]{1,0:T(8,128)(2,1)S(1)}, bf16[16,4096]{1,0:T(8,128)(2,1)S(1)}, u32[]{:S(2)}, u32[]{:S(2)}) collective-permute-start(bf16[16,4096]{1,0:T(8,128)(2,1)S(1)} %get-tuple-element.26.refs_2_), channel_id=1, source_target_pairs={{0,4},{1,9},{2,6},{3,11},{4,0},{5,13},{6,2},{7,15},{8,12},{9,1},{1... | collective-permute-start | bytes 393224 | tf_op jit(solution)/shard_map/ppermute | solution.py:151
  37.6 6.7 %collective-permute-start.15 = (bf16[16,4096]{1,0:T(8,128)(2,1)S(1)}, bf16[16,4096]{1,0:T(8,128)(2,1)S(1)}, u32[]{:S(2)}, u32[]{:S(2)}) collective-permute-start(bf16[16,4096]{1,0:T(8,128)(2,1)S(1)} %add.4), channel_id=1, source_target_pairs={{0,2},{2,0},{4,6},{6,4},{8,10},{10,8},{12,14},{14,12},{1,3},{3,1},... | collective-permute-start | bytes 393224 | tf_op jit(solution)/shard_map/ppermute | solution.py:143

commit v22 on v20

--- a/solution.py
+++ b/solution.py
@@ -119,10 +119,12 @@
         block = {0: tokens}
         for far in fars:
             block[far] = swap(tokens, far)
-        for near in (1, 2, 3):
+        for near in (1, 2):
             block[near] = swap(tokens, near)
         gate_held = fetch(gate_weight, 48, 2000000000)
         up_held = fetch(up_weight, 48, 2000000000)
+        own, gate_held = lax.optimization_barrier((tokens, gate_held))
+        block[3] = swap(own, 3)
         *crossed, gate_held = lax.optimization_barrier([block[far] for far in fars] + [gate_held])
         block.update(zip(fars, crossed))
         for far in fars:

time: 44 us -> 44 us (level)
  no operation moved by 1% of the time
where the time goes in v22:
time: 44 us; the launch traced here: 43.9 us
  starting transfers between devices  20.6 us (47%)
  waiting for transfers between devices  15.8 us (36%)
  Pallas kernels  7.39 us (17%)
    ppermute x14, starting transfers between devices, swap(): return lax.ppermute(value, 'wide', [(i, i ^ bits) for i in range(wide)])  20 us
    ppermute x14, waiting for transfers between devices, swap(): return lax.ppermute(value, 'wide', [(i, i ^ bits) for i in range(wide)])  14.6 us
    pallas_call x2, Pallas kernels, fetch(): pl.pallas_call(functools.partial(fetch_kernel, pieces), in_specs=[pl.Bloc...  4.43 us
    pallas_call x3, Pallas kernels, call(): pl.pallas_call(kernel, out_shape=out_shape, compiler_params=pltpu.Compile...  2.16 us
    ppermute x2, waiting for transfers between devices, across_cores(): lax.ppermute(value, 'narrow', [(i, (i + 1) % narrow) for i in range(narro...  1.16 us
  transfers between devices with their start and end apart: 16, of which 11 were waited for; matrix products, arithmetic and copies ran while one was open for 0% of the time, Pallas kernels for 12%

profile of v22, /device:TPU:0, one launch (start us, length us, event | category | flops | bytes accessed | tf_op | source)
XLA Modules:
  0.0 43.9 jit_solution(2765549454093762483)
XLA Ops:
  0.0 0.0 copy-start.1
  0.0 4.0 %collective-permute-start.3 = (bf16[16,4096]{1,0:T(8,128)(2,1)}, bf16[16,4096]{1,0:T(8,128)(2,1)S(1)}, u32[]{:S(2)}, u32[]{:S(2)}) collective-permute-start(bf16[16,4096]{1,0:T(8,128)(2,1)} %refs_0_.3), channel_id=1, source_target_pairs={{0,8},{2,10},{4,12},{6,14},{8,0},{10,2},{12,4},{14,6},{1,9},{3,11}... | collective-permute-start | bytes 393224 | tf_op jit(solution)/shard_map/ppermute | solution.py:112
  4.0 1.6 %collective-permute-start.2 = (bf16[16,4096]{1,0:T(8,128)(2,1)}, bf16[16,4096]{1,0:T(8,128)(2,1)S(1)}, u32[]{:S(2)}, u32[]{:S(2)}) collective-permute-start(bf16[16,4096]{1,0:T(8,128)(2,1)} %refs_0_.3), channel_id=1, source_target_pairs={{0,4},{2,6},{4,0},{6,2},{8,12},{10,14},{12,8},{14,10},{1,5},{3,7},... | collective-permute-start | bytes 393224 | tf_op jit(solution)/shard_map/ppermute | solution.py:112
  5.6 1.5 %collective-permute-start.1 = (bf16[16,4096]{1,0:T(8,128)(2,1)}, bf16[16,4096]{1,0:T(8,128)(2,1)S(1)}, u32[]{:S(2)}, u32[]{:S(2)}) collective-permute-start(bf16[16,4096]{1,0:T(8,128)(2,1)} %refs_0_.3), channel_id=1, source_target_pairs={{0,2},{2,0},{4,6},{6,4},{8,10},{10,8},{12,14},{14,12},{1,3},{3,1},... | collective-permute-start | bytes 393224 | tf_op jit(solution)/shard_map/ppermute | solution.py:112
  7.1 2.2 %fetch.2.refs_8_ = bf16[4096,512]{1,0:T(8,128)(2,1)S(1)} custom-call(bf16[4096,512]{1,0:T(8,128)(2,1)} %source.2), custom_call_target="tpu_custom_call" | custom-call | flops 2000000000 | tf_op jit(solution)/shard_map/fetch/pallas_call | solution.py:37
  9.4 0.0 copy-done.1
  9.4 0.5 %collective-permute-start = (bf16[16,4096]{1,0:T(8,128)(2,1)S(1)}, bf16[16,4096]{1,0:T(8,128)(2,1)S(1)}, u32[]{:S(2)}, u32[]{:S(2)}) collective-permute-start(bf16[16,4096]{1,0:T(8,128)(2,1)S(1)} %copy-done.1), channel_id=1, source_target_pairs={{0,6},{2,4},{4,2},{6,0},{8,14},{10,12},{12,10},{14,8},{1,7},{3,5},... | collective-permute-start | bytes 393224 | tf_op jit(solution)/shard_map/ppermute | solution.py:112
  9.8 0.9 %collective-permute-done.3.refs_4_ = bf16[16,4096]{1,0:T(8,128)(2,1)S(1)} collective-permute-done((bf16[16,4096]{1,0:T(8,128)(2,1)}, bf16[16,4096]{1,0:T(8,128)(2,1)S(1)}, u32[]{:S(2)}, u32[]{:S(2)}) %collective-permute-start.3) | collective-permute-done | bytes 131104 | tf_op jit(solution)/shard_map/ppermute | solution.py:112
  10.7 1.7 %collective-permute-start.6 = (bf16[16,4096]{1,0:T(8,128)(2,1)S(1)}, bf16[16,4096]{1,0:T(8,128)(2,1)S(1)}, u32[]{:S(2)}, u32[]{:S(2)}) collective-permute-start(bf16[16,4096]{1,0:T(8,128)(2,1)S(1)} %collective-permute-done.3.refs_4_), channel_id=1, source_target_pairs={{0,6},{2,4},{4,2},{6,0},{8,14},{10,12},{12,10},{14,8},{1,7},{3,5},... | collective-permute-start | bytes 393224 | tf_op jit(solution)/shard_map/ppermute | solution.py:112
  12.4 0.5 %collective-permute-start.5 = (bf16[16,4096]{1,0:T(8,128)(2,1)S(1)}, bf16[16,4096]{1,0:T(8,128)(2,1)S(1)}, u32[]{:S(2)}, u32[]{:S(2)}) collective-permute-start(bf16[16,4096]{1,0:T(8,128)(2,1)S(1)} %collective-permute-done.3.refs_4_), channel_id=1, source_target_pairs={{0,2},{2,0},{4,6},{6,4},{8,10},{10,8},{12,14},{14,12},{1,3},{3,1},... | collective-permute-start | bytes 393224 | tf_op jit(solution)/shard_map/ppermute | solution.py:112
  12.9 0.0 collective-permute-done.2.refs_3_
  12.9 1.3 %collective-permute-start.4 = (bf16[16,4096]{1,0:T(8,128)(2,1)S(1)}, bf16[16,4096]{1,0:T(8,128)(2,1)S(1)}, u32[]{:S(2)}, u32[]{:S(2)}) collective-permute-start(bf16[16,4096]{1,0:T(8,128)(2,1)S(1)} %collective-permute-done.3.refs_4_), channel_id=1, source_target_pairs={{0,4},{2,6},{4,0},{6,2},{8,12},{10,14},{12,8},{14,10},{1,5},{3,7},... | collective-permute-start | bytes 393224 | tf_op jit(solution)/shard_map/ppermute | solution.py:112
  14.2 2.2 %fetch.3.refs_8_ = bf16[4096,512]{1,0:T(8,128)(2,1)S(1)} custom-call(bf16[4096,512]{1,0:T(8,128)(2,1)} %source.3), custom_call_target="tpu_custom_call" | custom-call | flops 2000000000 | tf_op jit(solution)/shard_map/fetch/pallas_call | solution.py:37
  16.4 0.0 copy-start
  16.5 0.0 collective-permute-done.1.refs_2_
  16.5 0.0 collective-permute-done.refs_1_
  16.5 2.5 %collective-permute-done.6.refs_7_ = bf16[16,4096]{1,0:T(8,128)(2,1)S(1)} collective-permute-done((bf16[16,4096]{1,0:T(8,128)(2,1)S(1)}, bf16[16,4096]{1,0:T(8,128)(2,1)S(1)}, u32[]{:S(2)}, u32[]{:S(2)}) %collective-permute-start.6) | collective-permute-done | bytes 131104 | tf_op jit(solution)/shard_map/ppermute | solution.py:112
  19.0 1.4 %collective-permute-done.5.refs_6_ = bf16[16,4096]{1,0:T(8,128)(2,1)S(1)} collective-permute-done((bf16[16,4096]{1,0:T(8,128)(2,1)S(1)}, bf16[16,4096]{1,0:T(8,128)(2,1)S(1)}, u32[]{:S(2)}, u32[]{:S(2)}) %collective-permute-start.5) | collective-permute-done | bytes 131104 | tf_op jit(solution)/shard_map/ppermute | solution.py:112
  20.3 0.0 collective-permute-done.4.refs_5_
  20.4 0.7 %project.2.gate_ref = f32[128,512]{1,0:T(8,128)S(1)} custom-call(bf16[16,4096]{1,0:T(8,128)(2,1)S(1)} %copy-done.1, bf16[16,4096]{1,0:T(8,128)(2,1)S(1)} %collective-permute-done.refs_1_, bf16[16,4096]{1,0:T(8,128)(2,1)S(1)} %collective-permute-done.1.refs_2_, bf16[16,4096]{1,0:T(8,128)(2,1)S(1)} %collective-permute-done.2.refs_3_, ...), custom_call_target="tpu_custom_call" | custom-call | flops 400000000 | tf_op jit(solution)/shard_map/project/pallas_call | solution.py:15
  21.1 0.1 collective-permute-start.7
  21.2 0.7 %project.3.up_ref = f32[128,512]{1,0:T(8,128)S(1)} custom-call(bf16[16,4096]{1,0:T(8,128)(2,1)S(1)} %copy-done.1, bf16[16,4096]{1,0:T(8,128)(2,1)S(1)} %collective-permute-done.refs_1_, bf16[16,4096]{1,0:T(8,128)(2,1)S(1)} %collective-permute-done.1.refs_2_, bf16[16,4096]{1,0:T(8,128)(2,1)S(1)} %collective-permute-done.2.refs_3_, ...), custom_call_target="tpu_custom_call" | custom-call | flops 400000000 | tf_op jit(solution)/shard_map/project/pallas_call | solution.py:15
  21.9 0.6 %collective-permute-start.8 = (f32[128,512]{1,0:T(8,128)S(1)}, f32[128,512]{1,0:T(8,128)S(1)}, u32[]{:S(2)}, u32[]{:S(2)}) collective-permute-start(f32[128,512]{1,0:T(8,128)S(1)} %project.3.up_ref), channel_id=1, source_target_pairs={{0,1},{1,0},{2,3},{3,2},{4,5},{5,4},{6,7},{7,6},{8,9},{9,8},{10,11... | collective-permute-start | bytes 786440 | tf_op jit(solution)/shard_map/ppermute | solution.py:115
  22.4 0.2 collective-permute-done.7.gate_other_ref
  22.7 0.9 %collective-permute-done.8.up_other_ref = f32[128,512]{1,0:T(8,128)S(1)} collective-permute-done((f32[128,512]{1,0:T(8,128)S(1)}, f32[128,512]{1,0:T(8,128)S(1)}, u32[]{:S(2)}, u32[]{:S(2)}) %collective-permute-start.8) | collective-permute-done | bytes 262176 | tf_op jit(solution)/shard_map/ppermute | solution.py:115
  23.6 0.0 copy-done
  23.6 0.7 %down.1 = (f32[16,4096]{1,0:T(8,128)S(1)}, bf16[16,4096]{1,0:T(8,128)(2,1)S(1)}, f32[16,4096]{1,0:T(8,128)S(1)}, bf16[16,4096]{1,0:T(8,128)(2,1)S(1)}, f32[16,40...) custom-call(f32[128,512]{1,0:T(8,128)S(1)} %project.2.gate_ref, ...), custom_call_target="tpu_custom_call" | custom-call | flops 536870912 | tf_op jit(solution)/shard_map/down/pallas_call | solution.py:15
  24.3 1.5 %collective-permute-start.11 = (bf16[16,4096]{1,0:T(8,128)(2,1)S(1)}, bf16[16,4096]{1,0:T(8,128)(2,1)S(1)}, u32[]{:S(2)}, u32[]{:S(2)}) collective-permute-start(bf16[16,4096]{1,0:T(8,128)(2,1)S(1)} %get-tuple-element.26), channel_id=1, source_target_pairs={{0,6},{2,4},{4,2},{6,0},{8,14},{10,12},{12,10},{14,8},{1,7},{3,5},... | collective-permute-start | bytes 393224 | tf_op jit(solution)/shard_map/ppermute | solution.py:112
  25.8 1.4 %collective-permute-start.12 = (bf16[16,4096]{1,0:T(8,128)(2,1)S(1)}, bf16[16,4096]{1,0:T(8,128)(2,1)S(1)}, u32[]{:S(2)}, u32[]{:S(2)}) collective-permute-start(bf16[16,4096]{1,0:T(8,128)(2,1)S(1)} %get-tuple-element.27), channel_id=1, source_target_pairs={{0,2},{2,0},{4,6},{6,4},{8,10},{10,8},{12,14},{14,12},{1,3},{3,1},... | collective-permute-start | bytes 393224 | tf_op jit(solution)/shard_map/ppermute | solution.py:112
  27.2 0.7 %collective-permute-start.13 = (bf16[16,4096]{1,0:T(8,128)(2,1)S(1)}, bf16[16,4096]{1,0:T(8,128)(2,1)S(1)}, u32[]{:S(2)}, u32[]{:S(2)}) collective-permute-start(bf16[16,4096]{1,0:T(8,128)(2,1)S(1)} %get-tuple-element.28), channel_id=1, source_target_pairs={{0,4},{2,6},{4,0},{6,2},{8,12},{10,14},{12,8},{14,10},{1,5},{3,7},... | collective-permute-start | bytes 393224 | tf_op jit(solution)/shard_map/ppermute | solution.py:112
  27.9 1.3 %collective-permute-start.10 = (bf16[16,4096]{1,0:T(8,128)(2,1)S(1)}, bf16[16,4096]{1,0:T(8,128)(2,1)S(1)}, u32[]{:S(2)}, u32[]{:S(2)}) collective-permute-start(bf16[16,4096]{1,0:T(8,128)(2,1)S(1)} %get-tuple-element.24), channel_id=1, source_target_pairs={{0,4},{2,6},{4,0},{6,2},{8,12},{10,14},{12,8},{14,10},{1,5},{3,7},... | collective-permute-start | bytes 393224 | tf_op jit(solution)/shard_map/ppermute | solution.py:112
  29.2 0.7 %collective-permute-start.9 = (bf16[16,4096]{1,0:T(8,128)(2,1)S(1)}, bf16[16,4096]{1,0:T(8,128)(2,1)S(1)}, u32[]{:S(2)}, u32[]{:S(2)}) collective-permute-start(bf16[16,4096]{1,0:T(8,128)(2,1)S(1)} %get-tuple-element.22), channel_id=1, source_target_pairs={{0,4},{2,6},{4,0},{6,2},{8,12},{10,14},{12,8},{14,10},{1,5},{3,7},... | collective-permute-start | bytes 393224 | tf_op jit(solution)/shard_map/ppermute | solution.py:112
  29.9 1.7 %collective-permute-done.11.refs_0_ = bf16[16,4096]{1,0:T(8,128)(2,1)S(1)} collective-permute-done((bf16[16,4096]{1,0:T(8,128)(2,1)S(1)}, bf16[16,4096]{1,0:T(8,128)(2,1)S(1)}, u32[]{:S(2)}, u32[]{:S(2)}) %collective-permute-start.11) | collective-permute-done | bytes 131104 | tf_op jit(solution)/shard_map/ppermute | solution.py:112
  31.7 2.2 %collective-permute-done.12.refs_1_ = bf16[16,4096]{1,0:T(8,128)(2,1)S(1)} collective-permute-done((bf16[16,4096]{1,0:T(8,128)(2,1)S(1)}, bf16[16,4096]{1,0:T(8,128)(2,1)S(1)}, u32[]{:S(2)}, u32[]{:S(2)}) %collective-permute-start.12) | collective-permute-done | bytes 131104 | tf_op jit(solution)/shard_map/ppermute | solution.py:112
  33.9 0.0 collective-permute-done.13.refs_2_
  33.9 0.1 add.4.refs_1_
  34.0 2.0 %collective-permute-start.15 = (bf16[16,4096]{1,0:T(8,128)(2,1)S(1)}, bf16[16,4096]{1,0:T(8,128)(2,1)S(1)}, u32[]{:S(2)}, u32[]{:S(2)}) collective-permute-start(bf16[16,4096]{1,0:T(8,128)(2,1)S(1)} %add.4.refs_1_), channel_id=1, source_target_pairs={{0,8},{2,10},{4,12},{6,14},{8,0},{10,2},{12,4},{14,6},{1,9},{3,11}... | collective-permute-start | bytes 393224 | tf_op jit(solution)/shard_map/ppermute | solution.py:112
  36.0 0.6 %collective-permute-done.10.refs_0_ = bf16[16,4096]{1,0:T(8,128)(2,1)S(1)} collective-permute-done((bf16[16,4096]{1,0:T(8,128)(2,1)S(1)}, bf16[16,4096]{1,0:T(8,128)(2,1)S(1)}, u32[]{:S(2)}, u32[]{:S(2)}) %collective-permute-start.10) | collective-permute-done | bytes 131104 | tf_op jit(solution)/shard_map/ppermute | solution.py:112
  36.7 1.3 %collective-permute-start.14 = (bf16[16,4096]{1,0:T(8,128)(2,1)S(1)}, bf16[16,4096]{1,0:T(8,128)(2,1)S(1)}, u32[]{:S(2)}, u32[]{:S(2)}) collective-permute-start(bf16[16,4096]{1,0:T(8,128)(2,1)S(1)} %add.5.refs_1_), channel_id=1, source_target_pairs={{0,2},{2,0},{4,6},{6,4},{8,10},{10,8},{12,14},{14,12},{1,3},{3,1},... | collective-permute-start | bytes 393224 | tf_op jit(solution)/shard_map/ppermute | solution.py:112
  38.0 3.3 %collective-permute-done.9.refs_0_ = bf16[16,4096]{1,0:T(8,128)(2,1)S(1)} collective-permute-done((bf16[16,4096]{1,0:T(8,128)(2,1)S(1)}, bf16[16,4096]{1,0:T(8,128)(2,1)S(1)}, u32[]{:S(2)}, u32[]{:S(2)}) %collective-permute-start.9) | collective-permute-done | bytes 131104 | tf_op jit(solution)/shard_map/ppermute | solution.py:112
  41.3 0.4 collective-permute-done.14.refs_0_
  41.7 1.5 %collective-permute-done.15.refs_1_ = bf16[16,4096]{1,0:T(8,128)(2,1)S(1)} collective-permute-done((bf16[16,4096]{1,0:T(8,128)(2,1)S(1)}, bf16[16,4096]{1,0:T(8,128)(2,1)S(1)}, u32[]{:S(2)}, u32[]{:S(2)}) %collective-permute-start.15) | collective-permute-done | bytes 131104 | tf_op jit(solution)/shard_map/ppermute | solution.py:112
  43.2 0.7 %add.7 = bf16[16,4096]{1,0:T(8,128)(2,1)} custom-call(f32[16,4096]{1,0:T(8,128)S(1)} %add.6.own_ref, bf16[16,4096]{1,0:T(8,128)(2,1)S(1)} %collective-permute-done.14.refs_0_, bf16[16,4096]{1,0:T(8,128)(2,1)S(1)} %collective-permute-done.15.refs_1_), custom_call_target="tpu_custom_call" | custom-call | flops 1000000 | tf_op jit(solution)/shard_map/add/pallas_call | solution.py:97
  (2 shorter events, 0.0 us)
Async XLA Ops:
  0.0 9.4 %copy-start.1 = (bf16[16,4096]{1,0:T(8,128)(2,1)S(1)}, bf16[16,4096]{1,0:T(8,128)(2,1)}, u32[]{:S(2)}) copy-start(bf16[16,4096]{1,0:T(8,128)(2,1)} %refs_0_.3) | copy-start | bytes 393220
  0.0 10.7 %collective-permute-start.3 = (bf16[16,4096]{1,0:T(8,128)(2,1)}, bf16[16,4096]{1,0:T(8,128)(2,1)S(1)}, u32[]{:S(2)}, u32[]{:S(2)}) collective-permute-start(bf16[16,4096]{1,0:T(8,128)(2,1)} %refs_0_.3), channel_id=1, source_target_pairs={{0,8},{2,10},{4,12},{6,14},{8,0},{10,2},{12,4},{14,6},{1,9},{3,11}... | collective-permute-start | bytes 393224 | tf_op jit(solution)/shard_map/ppermute | solution.py:112
  4.0 8.9 %collective-permute-start.2 = (bf16[16,4096]{1,0:T(8,128)(2,1)}, bf16[16,4096]{1,0:T(8,128)(2,1)S(1)}, u32[]{:S(2)}, u32[]{:S(2)}) collective-permute-start(bf16[16,4096]{1,0:T(8,128)(2,1)} %refs_0_.3), channel_id=1, source_target_pairs={{0,4},{2,6},{4,0},{6,2},{8,12},{10,14},{12,8},{14,10},{1,5},{3,7},... | collective-permute-start | bytes 393224 | tf_op jit(solution)/shard_map/ppermute | solution.py:112
  5.6 10.8 %collective-permute-start.1 = (bf16[16,4096]{1,0:T(8,128)(2,1)}, bf16[16,4096]{1,0:T(8,128)(2,1)S(1)}, u32[]{:S(2)}, u32[]{:S(2)}) collective-permute-start(bf16[16,4096]{1,0:T(8,128)(2,1)} %refs_0_.3), channel_id=1, source_target_pairs={{0,2},{2,0},{4,6},{6,4},{8,10},{10,8},{12,14},{14,12},{1,3},{3,1},... | collective-permute-start | bytes 393224 | tf_op jit(solution)/shard_map/ppermute | solution.py:112
  9.4 7.1 %collective-permute-start = (bf16[16,4096]{1,0:T(8,128)(2,1)S(1)}, bf16[16,4096]{1,0:T(8,128)(2,1)S(1)}, u32[]{:S(2)}, u32[]{:S(2)}) collective-permute-start(bf16[16,4096]{1,0:T(8,128)(2,1)S(1)} %copy-done.1), channel_id=1, source_target_pairs={{0,6},{2,4},{4,2},{6,0},{8,14},{10,12},{12,10},{14,8},{1,7},{3,5},... | collective-permute-start | bytes 393224 | tf_op jit(solution)/shard_map/ppermute | solution.py:112
  10.7 8.2 %collective-permute-start.6 = (bf16[16,4096]{1,0:T(8,128)(2,1)S(1)}, bf16[16,4096]{1,0:T(8,128)(2,1)S(1)}, u32[]{:S(2)}, u32[]{:S(2)}) collective-permute-start(bf16[16,4096]{1,0:T(8,128)(2,1)S(1)} %collective-permute-done.3.refs_4_), channel_id=1, source_target_pairs={{0,6},{2,4},{4,2},{6,0},{8,14},{10,12},{12,10},{14,8},{1,7},{3,5},... | collective-permute-start | bytes 393224 | tf_op jit(solution)/shard_map/ppermute | solution.py:112
  12.4 8.0 %collective-permute-start.5 = (bf16[16,4096]{1,0:T(8,128)(2,1)S(1)}, bf16[16,4096]{1,0:T(8,128)(2,1)S(1)}, u32[]{:S(2)}, u32[]{:S(2)}) collective-permute-start(bf16[16,4096]{1,0:T(8,128)(2,1)S(1)} %collective-permute-done.3.refs_4_), channel_id=1, source_target_pairs={{0,2},{2,0},{4,6},{6,4},{8,10},{10,8},{12,14},{14,12},{1,3},{3,1},... | collective-permute-start | bytes 393224 | tf_op jit(solution)/shard_map/ppermute | solution.py:112
  12.9 7.5 %collective-permute-start.4 = (bf16[16,4096]{1,0:T(8,128)(2,1)S(1)}, bf16[16,4096]{1,0:T(8,128)(2,1)S(1)}, u32[]{:S(2)}, u32[]{:S(2)}) collective-permute-start(bf16[16,4096]{1,0:T(8,128)(2,1)S(1)} %collective-permute-done.3.refs_4_), channel_id=1, source_target_pairs={{0,4},{2,6},{4,0},{6,2},{8,12},{10,14},{12,8},{14,10},{1,5},{3,7},... | collective-permute-start | bytes 393224 | tf_op jit(solution)/shard_map/ppermute | solution.py:112
  16.4 7.1 %copy-start = (bf16[512,4096]{1,0:T(8,128)(2,1)S(1)}, bf16[512,4096]{1,0:T(8,128)(2,1)}, u32[]{:S(2)}) copy-start(bf16[512,4096]{1,0:T(8,128)(2,1)} %weight_ref.1) | copy-start | bytes 12582916
  21.1 1.6 %collective-permute-start.7 = (f32[128,512]{1,0:T(8,128)S(1)}, f32[128,512]{1,0:T(8,128)S(1)}, u32[]{:S(2)}, u32[]{:S(2)}) collective-permute-start(f32[128,512]{1,0:T(8,128)S(1)} %project.2.gate_ref), channel_id=1, source_target_pairs={{0,1},{1,0},{2,3},{3,2},{4,5},{5,4},{6,7},{7,6},{8,9},{9,8},{10,11... | collective-permute-start | bytes 786440 | tf_op jit(solution)/shard_map/ppermute | solution.py:115
  21.9 1.7 %collective-permute-start.8 = (f32[128,512]{1,0:T(8,128)S(1)}, f32[128,512]{1,0:T(8,128)S(1)}, u32[]{:S(2)}, u32[]{:S(2)}) collective-permute-start(f32[128,512]{1,0:T(8,128)S(1)} %project.3.up_ref), channel_id=1, source_target_pairs={{0,1},{1,0},{2,3},{3,2},{4,5},{5,4},{6,7},{7,6},{8,9},{9,8},{10,11... | collective-permute-start | bytes 786440 | tf_op jit(solution)/shard_map/ppermute | solution.py:115
  24.3 7.3 %collective-permute-start.11 = (bf16[16,4096]{1,0:T(8,128)(2,1)S(1)}, bf16[16,4096]{1,0:T(8,128)(2,1)S(1)}, u32[]{:S(2)}, u32[]{:S(2)}) collective-permute-start(bf16[16,4096]{1,0:T(8,128)(2,1)S(1)} %get-tuple-element.26), channel_id=1, source_target_pairs={{0,6},{2,4},{4,2},{6,0},{8,14},{10,12},{12,10},{14,8},{1,7},{3,5},... | collective-permute-start | bytes 393224 | tf_op jit(solution)/shard_map/ppermute | solution.py:112
  25.8 8.1 %collective-permute-start.12 = (bf16[16,4096]{1,0:T(8,128)(2,1)S(1)}, bf16[16,4096]{1,0:T(8,128)(2,1)S(1)}, u32[]{:S(2)}, u32[]{:S(2)}) collective-permute-start(bf16[16,4096]{1,0:T(8,128)(2,1)S(1)} %get-tuple-element.27), channel_id=1, source_target_pairs={{0,2},{2,0},{4,6},{6,4},{8,10},{10,8},{12,14},{14,12},{1,3},{3,1},... | collective-permute-start | bytes 393224 | tf_op jit(solution)/shard_map/ppermute | solution.py:112
  27.2 6.7 %collective-permute-start.13 = (bf16[16,4096]{1,0:T(8,128)(2,1)S(1)}, bf16[16,4096]{1,0:T(8,128)(2,1)S(1)}, u32[]{:S(2)}, u32[]{:S(2)}) collective-permute-start(bf16[16,4096]{1,0:T(8,128)(2,1)S(1)} %get-tuple-element.28), channel_id=1, source_target_pairs={{0,4},{2,6},{4,0},{6,2},{8,12},{10,14},{12,8},{14,10},{1,5},{3,7},... | collective-permute-start | bytes 393224 | tf_op jit(solution)/shard_map/ppermute | solution.py:112
  27.9 8.7 %collective-permute-start.10 = (bf16[16,4096]{1,0:T(8,128)(2,1)S(1)}, bf16[16,4096]{1,0:T(8,128)(2,1)S(1)}, u32[]{:S(2)}, u32[]{:S(2)}) collective-permute-start(bf16[16,4096]{1,0:T(8,128)(2,1)S(1)} %get-tuple-element.24), channel_id=1, source_target_pairs={{0,4},{2,6},{4,0},{6,2},{8,12},{10,14},{12,8},{14,10},{1,5},{3,7},... | collective-permute-start | bytes 393224 | tf_op jit(solution)/shard_map/ppermute | solution.py:112
  29.2 12.0 %collective-permute-start.9 = (bf16[16,4096]{1,0:T(8,128)(2,1)S(1)}, bf16[16,4096]{1,0:T(8,128)(2,1)S(1)}, u32[]{:S(2)}, u32[]{:S(2)}) collective-permute-start(bf16[16,4096]{1,0:T(8,128)(2,1)S(1)} %get-tuple-element.22), channel_id=1, source_target_pairs={{0,4},{2,6},{4,0},{6,2},{8,12},{10,14},{12,8},{14,10},{1,5},{3,7},... | collective-permute-start | bytes 393224 | tf_op jit(solution)/shard_map/ppermute | solution.py:112
  34.0 9.2 %collective-permute-start.15 = (bf16[16,4096]{1,0:T(8,128)(2,1)S(1)}, bf16[16,4096]{1,0:T(8,128)(2,1)S(1)}, u32[]{:S(2)}, u32[]{:S(2)}) collective-permute-start(bf16[16,4096]{1,0:T(8,128)(2,1)S(1)} %add.4.refs_1_), channel_id=1, source_target_pairs={{0,8},{2,10},{4,12},{6,14},{8,0},{10,2},{12,4},{14,6},{1,9},{3,11}... | collective-permute-start | bytes 393224 | tf_op jit(solution)/shard_map/ppermute | solution.py:112
  36.7 5.0 %collective-permute-start.14 = (bf16[16,4096]{1,0:T(8,128)(2,1)S(1)}, bf16[16,4096]{1,0:T(8,128)(2,1)S(1)}, u32[]{:S(2)}, u32[]{:S(2)}) collective-permute-start(bf16[16,4096]{1,0:T(8,128)(2,1)S(1)} %add.5.refs_1_), channel_id=1, source_target_pairs={{0,2},{2,0},{4,6},{6,4},{8,10},{10,8},{12,14},{14,12},{1,3},{3,1},... | collective-permute-start | bytes 393224 | tf_op jit(solution)/shard_map/ppermute | solution.py:112

commit v23 on v22

--- a/solution.py
+++ b/solution.py
@@ -140,13 +140,13 @@
             down_weight, rows, [F32 if b in stay else BF16 for b in order],
         )
         part = dict(zip(order, outs))
-        sums = []
+        sums, direct = [], []
         for far in fars:
-            quad = [swap(part[far + near], near) for near in (3, 1, 2)]
-            sums.append(add(part[far], quad, BF16))
+            sums.append(add(part[far], [swap(part[far + near], near) for near in (1, 2)], BF16))
+            direct.append(swap(part[far + 3], far + 3))
         arrived = [swap(value, far) for value, far in zip(sums, fars)]
         pair = add(part[1], [swap(part[3], 2)], BF16, after=sums)
-        total = add(part[0], [swap(part[2], 2)], F32, 1500000000, after=[pair])
+        total = add(part[0], direct + [swap(part[2], 2)], F32, 1500000000, after=[pair])
         return add(total, [swap(pair, 1)] + arrived, BF16)
 
     return local

time: 44 us -> 45.8 us (1.041)
  starting transfers between devices: 20.6 us -> 23 us
  waiting for transfers between devices: 15.8 us -> 15.2 us
    ppermute x14, starting transfers between devices: 20 us -> 22.3 us  [swap(): return lax.ppermute(value, 'wide', [(i, i ^ bits) for i in range(wide)])]
    ppermute x14, waiting for transfers between devices: 14.6 us -> 14 us  [swap(): return lax.ppermute(value, 'wide', [(i, i ^ bits) for i in range(wide)])]
  transfers between devices with their start and end apart: 16 -> 16, of which waited for: 11 -> 9; matrix products, arithmetic and copies ran while one was open for 0% -> 0% of each run, Pallas kernels for 12% -> 11%
where the time goes in v23:
time: 45.8 us; the launch traced here: 45.6 us
  starting transfers between devices  23 us (50%)
  waiting for transfers between devices  15.2 us (33%)
  Pallas kernels  7.39 us (16%)
    ppermute x14, starting transfers between devices, swap(): return lax.ppermute(value, 'wide', [(i, i ^ bits) for i in range(wide)])  22.3 us
    ppermute x14, waiting for transfers between devices, swap(): return lax.ppermute(value, 'wide', [(i, i ^ bits) for i in range(wide)])  14 us
    pallas_call x2, Pallas kernels, fetch(): pl.pallas_call(functools.partial(fetch_kernel, pieces), in_specs=[pl.Bloc...  4.43 us
    pallas_call x3, Pallas kernels, call(): pl.pallas_call(kernel, out_shape=out_shape, compiler_params=pltpu.Compile...  2.16 us
    ppermute x2, waiting for transfers between devices, across_cores(): lax.ppermute(value, 'narrow', [(i, (i + 1) % narrow) for i in range(narro...  1.16 us
  transfers between devices with their start and end apart: 16, of which 9 were waited for; matrix products, arithmetic and copies ran while one was open for 0% of the time, Pallas kernels for 11%

profile of v23, /device:TPU:0, one launch (start us, length us, event | category | flops | bytes accessed | tf_op | source)
XLA Modules:
  0.0 45.6 jit_solution(4407918088227476884)
XLA Ops:
  0.0 0.0 copy-start.1
  0.0 4.0 %collective-permute-start.3 = (bf16[16,4096]{1,0:T(8,128)(2,1)}, bf16[16,4096]{1,0:T(8,128)(2,1)S(1)}, u32[]{:S(2)}, u32[]{:S(2)}) collective-permute-start(bf16[16,4096]{1,0:T(8,128)(2,1)} %refs_0_.3), channel_id=1, source_target_pairs={{0,8},{2,10},{4,12},{6,14},{8,0},{10,2},{12,4},{14,6},{1,9},{3,11}... | collective-permute-start | bytes 393224 | tf_op jit(solution)/shard_map/ppermute | solution.py:112
  4.0 1.6 %collective-permute-start.2 = (bf16[16,4096]{1,0:T(8,128)(2,1)}, bf16[16,4096]{1,0:T(8,128)(2,1)S(1)}, u32[]{:S(2)}, u32[]{:S(2)}) collective-permute-start(bf16[16,4096]{1,0:T(8,128)(2,1)} %refs_0_.3), channel_id=1, source_target_pairs={{0,4},{2,6},{4,0},{6,2},{8,12},{10,14},{12,8},{14,10},{1,5},{3,7},... | collective-permute-start | bytes 393224 | tf_op jit(solution)/shard_map/ppermute | solution.py:112
  5.6 1.5 %collective-permute-start.1 = (bf16[16,4096]{1,0:T(8,128)(2,1)}, bf16[16,4096]{1,0:T(8,128)(2,1)S(1)}, u32[]{:S(2)}, u32[]{:S(2)}) collective-permute-start(bf16[16,4096]{1,0:T(8,128)(2,1)} %refs_0_.3), channel_id=1, source_target_pairs={{0,2},{2,0},{4,6},{6,4},{8,10},{10,8},{12,14},{14,12},{1,3},{3,1},... | collective-permute-start | bytes 393224 | tf_op jit(solution)/shard_map/ppermute | solution.py:112
  7.1 2.2 %fetch.2.refs_8_ = bf16[4096,512]{1,0:T(8,128)(2,1)S(1)} custom-call(bf16[4096,512]{1,0:T(8,128)(2,1)} %source.2), custom_call_target="tpu_custom_call" | custom-call | flops 2000000000 | tf_op jit(solution)/shard_map/fetch/pallas_call | solution.py:37
  9.4 0.0 copy-done.1
  9.4 0.5 %collective-permute-start = (bf16[16,4096]{1,0:T(8,128)(2,1)S(1)}, bf16[16,4096]{1,0:T(8,128)(2,1)S(1)}, u32[]{:S(2)}, u32[]{:S(2)}) collective-permute-start(bf16[16,4096]{1,0:T(8,128)(2,1)S(1)} %copy-done.1), channel_id=1, source_target_pairs={{0,6},{2,4},{4,2},{6,0},{8,14},{10,12},{12,10},{14,8},{1,7},{3,5},... | collective-permute-start | bytes 393224 | tf_op jit(solution)/shard_map/ppermute | solution.py:112
  9.8 0.9 %collective-permute-done.3.refs_4_ = bf16[16,4096]{1,0:T(8,128)(2,1)S(1)} collective-permute-done((bf16[16,4096]{1,0:T(8,128)(2,1)}, bf16[16,4096]{1,0:T(8,128)(2,1)S(1)}, u32[]{:S(2)}, u32[]{:S(2)}) %collective-permute-start.3) | collective-permute-done | bytes 131104 | tf_op jit(solution)/shard_map/ppermute | solution.py:112
  10.7 1.7 %collective-permute-start.6 = (bf16[16,4096]{1,0:T(8,128)(2,1)S(1)}, bf16[16,4096]{1,0:T(8,128)(2,1)S(1)}, u32[]{:S(2)}, u32[]{:S(2)}) collective-permute-start(bf16[16,4096]{1,0:T(8,128)(2,1)S(1)} %collective-permute-done.3.refs_4_), channel_id=1, source_target_pairs={{0,6},{2,4},{4,2},{6,0},{8,14},{10,12},{12,10},{14,8},{1,7},{3,5},... | collective-permute-start | bytes 393224 | tf_op jit(solution)/shard_map/ppermute | solution.py:112
  12.4 0.5 %collective-permute-start.5 = (bf16[16,4096]{1,0:T(8,128)(2,1)S(1)}, bf16[16,4096]{1,0:T(8,128)(2,1)S(1)}, u32[]{:S(2)}, u32[]{:S(2)}) collective-permute-start(bf16[16,4096]{1,0:T(8,128)(2,1)S(1)} %collective-permute-done.3.refs_4_), channel_id=1, source_target_pairs={{0,2},{2,0},{4,6},{6,4},{8,10},{10,8},{12,14},{14,12},{1,3},{3,1},... | collective-permute-start | bytes 393224 | tf_op jit(solution)/shard_map/ppermute | solution.py:112
  12.9 0.0 collective-permute-done.2.refs_3_
  12.9 1.3 %collective-permute-start.4 = (bf16[16,4096]{1,0:T(8,128)(2,1)S(1)}, bf16[16,4096]{1,0:T(8,128)(2,1)S(1)}, u32[]{:S(2)}, u32[]{:S(2)}) collective-permute-start(bf16[16,4096]{1,0:T(8,128)(2,1)S(1)} %collective-permute-done.3.refs_4_), channel_id=1, source_target_pairs={{0,4},{2,6},{4,0},{6,2},{8,12},{10,14},{12,8},{14,10},{1,5},{3,7},... | collective-permute-start | bytes 393224 | tf_op jit(solution)/shard_map/ppermute | solution.py:112
  14.2 2.2 %fetch.3.refs_8_ = bf16[4096,512]{1,0:T(8,128)(2,1)S(1)} custom-call(bf16[4096,512]{1,0:T(8,128)(2,1)} %source.3), custom_call_target="tpu_custom_call" | custom-call | flops 2000000000 | tf_op jit(solution)/shard_map/fetch/pallas_call | solution.py:37
  16.4 0.0 copy-start
  16.5 0.0 collective-permute-done.1.refs_2_
  16.5 0.0 collective-permute-done.refs_1_
  16.5 2.5 %collective-permute-done.6.refs_7_ = bf16[16,4096]{1,0:T(8,128)(2,1)S(1)} collective-permute-done((bf16[16,4096]{1,0:T(8,128)(2,1)S(1)}, bf16[16,4096]{1,0:T(8,128)(2,1)S(1)}, u32[]{:S(2)}, u32[]{:S(2)}) %collective-permute-start.6) | collective-permute-done | bytes 131104 | tf_op jit(solution)/shard_map/ppermute | solution.py:112
  19.0 1.4 %collective-permute-done.5.refs_6_ = bf16[16,4096]{1,0:T(8,128)(2,1)S(1)} collective-permute-done((bf16[16,4096]{1,0:T(8,128)(2,1)S(1)}, bf16[16,4096]{1,0:T(8,128)(2,1)S(1)}, u32[]{:S(2)}, u32[]{:S(2)}) %collective-permute-start.5) | collective-permute-done | bytes 131104 | tf_op jit(solution)/shard_map/ppermute | solution.py:112
  20.3 0.0 collective-permute-done.4.refs_5_
  20.4 0.7 %project.2.gate_ref = f32[128,512]{1,0:T(8,128)S(1)} custom-call(bf16[16,4096]{1,0:T(8,128)(2,1)S(1)} %copy-done.1, bf16[16,4096]{1,0:T(8,128)(2,1)S(1)} %collective-permute-done.refs_1_, bf16[16,4096]{1,0:T(8,128)(2,1)S(1)} %collective-permute-done.1.refs_2_, bf16[16,4096]{1,0:T(8,128)(2,1)S(1)} %collective-permute-done.2.refs_3_, ...), custom_call_target="tpu_custom_call" | custom-call | flops 400000000 | tf_op jit(solution)/shard_map/project/pallas_call | solution.py:15
  21.1 0.1 collective-permute-start.7
  21.2 0.7 %project.3.up_ref = f32[128,512]{1,0:T(8,128)S(1)} custom-call(bf16[16,4096]{1,0:T(8,128)(2,1)S(1)} %copy-done.1, bf16[16,4096]{1,0:T(8,128)(2,1)S(1)} %collective-permute-done.refs_1_, bf16[16,4096]{1,0:T(8,128)(2,1)S(1)} %collective-permute-done.1.refs_2_, bf16[16,4096]{1,0:T(8,128)(2,1)S(1)} %collective-permute-done.2.refs_3_, ...), custom_call_target="tpu_custom_call" | custom-call | flops 400000000 | tf_op jit(solution)/shard_map/project/pallas_call | solution.py:15
  21.9 0.6 %collective-permute-start.8 = (f32[128,512]{1,0:T(8,128)S(1)}, f32[128,512]{1,0:T(8,128)S(1)}, u32[]{:S(2)}, u32[]{:S(2)}) collective-permute-start(f32[128,512]{1,0:T(8,128)S(1)} %project.3.up_ref), channel_id=1, source_target_pairs={{0,1},{1,0},{2,3},{3,2},{4,5},{5,4},{6,7},{7,6},{8,9},{9,8},{10,11... | collective-permute-start | bytes 786440 | tf_op jit(solution)/shard_map/ppermute | solution.py:115
  22.4 0.2 collective-permute-done.7.gate_other_ref
  22.7 0.9 %collective-permute-done.8.up_other_ref = f32[128,512]{1,0:T(8,128)S(1)} collective-permute-done((f32[128,512]{1,0:T(8,128)S(1)}, f32[128,512]{1,0:T(8,128)S(1)}, u32[]{:S(2)}, u32[]{:S(2)}) %collective-permute-start.8) | collective-permute-done | bytes 262176 | tf_op jit(solution)/shard_map/ppermute | solution.py:115
  23.6 0.0 copy-done
  23.6 0.7 %down.1 = (f32[16,4096]{1,0:T(8,128)S(1)}, bf16[16,4096]{1,0:T(8,128)(2,1)S(1)}, f32[16,4096]{1,0:T(8,128)S(1)}, bf16[16,4096]{1,0:T(8,128)(2,1)S(1)}, f32[16,40...) custom-call(f32[128,512]{1,0:T(8,128)S(1)} %project.2.gate_ref, ...), custom_call_target="tpu_custom_call" | custom-call | flops 536870912 | tf_op jit(solution)/shard_map/down/pallas_call | solution.py:15
  24.3 0.9 %collective-permute-start.12 = (bf16[16,4096]{1,0:T(8,128)(2,1)S(1)}, bf16[16,4096]{1,0:T(8,128)(2,1)S(1)}, u32[]{:S(2)}, u32[]{:S(2)}) collective-permute-start(bf16[16,4096]{1,0:T(8,128)(2,1)S(1)} %get-tuple-element.27), channel_id=1, source_target_pairs={{0,2},{2,0},{4,6},{6,4},{8,10},{10,8},{12,14},{14,12},{1,3},{3,1},... | collective-permute-start | bytes 393224 | tf_op jit(solution)/shard_map/ppermute | solution.py:112
  25.3 1.1 %collective-permute-start.13 = (bf16[16,4096]{1,0:T(8,128)(2,1)S(1)}, bf16[16,4096]{1,0:T(8,128)(2,1)S(1)}, u32[]{:S(2)}, u32[]{:S(2)}) collective-permute-start(bf16[16,4096]{1,0:T(8,128)(2,1)S(1)} %get-tuple-element.28), channel_id=1, source_target_pairs={{0,4},{2,6},{4,0},{6,2},{8,12},{10,14},{12,8},{14,10},{1,5},{3,7},... | collective-permute-start | bytes 393224 | tf_op jit(solution)/shard_map/ppermute | solution.py:112
  26.4 0.9 %collective-permute-start.11 = (bf16[16,4096]{1,0:T(8,128)(2,1)S(1)}, bf16[16,4096]{1,0:T(8,128)(2,1)S(1)}, u32[]{:S(2)}, u32[]{:S(2)}) collective-permute-start(bf16[16,4096]{1,0:T(8,128)(2,1)S(1)} %get-tuple-element.25), channel_id=1, source_target_pairs={{0,4},{2,6},{4,0},{6,2},{8,12},{10,14},{12,8},{14,10},{1,5},{3,7},... | collective-permute-start | bytes 393224 | tf_op jit(solution)/shard_map/ppermute | solution.py:112
  27.3 3.6 %collective-permute-start.9 = (bf16[16,4096]{1,0:T(8,128)(2,1)S(1)}, bf16[16,4096]{1,0:T(8,128)(2,1)S(1)}, u32[]{:S(2)}, u32[]{:S(2)}) collective-permute-start(bf16[16,4096]{1,0:T(8,128)(2,1)S(1)} %get-tuple-element.22), channel_id=1, source_target_pairs={{0,14},{2,12},{4,10},{6,8},{8,6},{10,4},{12,2},{14,0},{1,15},{3,13... | collective-permute-start | bytes 393224 | tf_op jit(solution)/shard_map/ppermute | solution.py:112
  30.9 0.0 collective-permute-start.10
  30.9 0.0 collective-permute-done.12.refs_0_
  30.9 0.7 %collective-permute-done.13.refs_1_ = bf16[16,4096]{1,0:T(8,128)(2,1)S(1)} collective-permute-done((bf16[16,4096]{1,0:T(8,128)(2,1)S(1)}, bf16[16,4096]{1,0:T(8,128)(2,1)S(1)}, u32[]{:S(2)}, u32[]{:S(2)}) %collective-permute-start.13) | collective-permute-done | bytes 131104 | tf_op jit(solution)/shard_map/ppermute | solution.py:112
  31.7 3.2 %collective-permute-start.15 = (bf16[16,4096]{1,0:T(8,128)(2,1)S(1)}, bf16[16,4096]{1,0:T(8,128)(2,1)S(1)}, u32[]{:S(2)}, u32[]{:S(2)}) collective-permute-start(bf16[16,4096]{1,0:T(8,128)(2,1)S(1)} %add.4.refs_1_), channel_id=1, source_target_pairs={{0,8},{2,10},{4,12},{6,14},{8,0},{10,2},{12,4},{14,6},{1,9},{3,11}... | collective-permute-start | bytes 393224 | tf_op jit(solution)/shard_map/ppermute | solution.py:112
  34.9 5.0 %collective-permute-done.11.refs_0_ = bf16[16,4096]{1,0:T(8,128)(2,1)S(1)} collective-permute-done((bf16[16,4096]{1,0:T(8,128)(2,1)S(1)}, bf16[16,4096]{1,0:T(8,128)(2,1)S(1)}, u32[]{:S(2)}, u32[]{:S(2)}) %collective-permute-start.11) | collective-permute-done | bytes 131104 | tf_op jit(solution)/shard_map/ppermute | solution.py:112
  39.9 1.4 %collective-permute-start.14 = (bf16[16,4096]{1,0:T(8,128)(2,1)S(1)}, bf16[16,4096]{1,0:T(8,128)(2,1)S(1)}, u32[]{:S(2)}, u32[]{:S(2)}) collective-permute-start(bf16[16,4096]{1,0:T(8,128)(2,1)S(1)} %add.5.refs_2_), channel_id=1, source_target_pairs={{0,2},{2,0},{4,6},{6,4},{8,10},{10,8},{12,14},{14,12},{1,3},{3,1},... | collective-permute-start | bytes 393224 | tf_op jit(solution)/shard_map/ppermute | solution.py:112
  41.3 0.0 collective-permute-done.9.refs_0_
  41.3 0.6 %collective-permute-done.10.refs_1_ = bf16[16,4096]{1,0:T(8,128)(2,1)S(1)} collective-permute-done((bf16[16,4096]{1,0:T(8,128)(2,1)S(1)}, bf16[16,4096]{1,0:T(8,128)(2,1)S(1)}, u32[]{:S(2)}, u32[]{:S(2)}) %collective-permute-start.10) | collective-permute-done | bytes 131104 | tf_op jit(solution)/shard_map/ppermute | solution.py:112
  42.0 2.9 %collective-permute-done.14.refs_0_ = bf16[16,4096]{1,0:T(8,128)(2,1)S(1)} collective-permute-done((bf16[16,4096]{1,0:T(8,128)(2,1)S(1)}, bf16[16,4096]{1,0:T(8,128)(2,1)S(1)}, u32[]{:S(2)}, u32[]{:S(2)}) %collective-permute-start.14) | collective-permute-done | bytes 131104 | tf_op jit(solution)/shard_map/ppermute | solution.py:112
  44.9 0.0 collective-permute-done.15.refs_1_
  44.9 0.7 %add.7 = bf16[16,4096]{1,0:T(8,128)(2,1)} custom-call(f32[16,4096]{1,0:T(8,128)S(1)} %add.6.own_ref, bf16[16,4096]{1,0:T(8,128)(2,1)S(1)} %collective-permute-done.14.refs_0_, bf16[16,4096]{1,0:T(8,128)(2,1)S(1)} %collective-permute-done.15.refs_1_), custom_call_target="tpu_custom_call" | custom-call | flops 1000000 | tf_op jit(solution)/shard_map/add/pallas_call | solution.py:97
  (3 shorter events, 0.1 us)
Async XLA Ops:
  0.0 9.4 %copy-start.1 = (bf16[16,4096]{1,0:T(8,128)(2,1)S(1)}, bf16[16,4096]{1,0:T(8,128)(2,1)}, u32[]{:S(2)}) copy-start(bf16[16,4096]{1,0:T(8,128)(2,1)} %refs_0_.3) | copy-start | bytes 393220
  0.0 10.7 %collective-permute-start.3 = (bf16[16,4096]{1,0:T(8,128)(2,1)}, bf16[16,4096]{1,0:T(8,128)(2,1)S(1)}, u32[]{:S(2)}, u32[]{:S(2)}) collective-permute-start(bf16[16,4096]{1,0:T(8,128)(2,1)} %refs_0_.3), channel_id=1, source_target_pairs={{0,8},{2,10},{4,12},{6,14},{8,0},{10,2},{12,4},{14,6},{1,9},{3,11}... | collective-permute-start | bytes 393224 | tf_op jit(solution)/shard_map/ppermute | solution.py:112
  4.0 8.9 %collective-permute-start.2 = (bf16[16,4096]{1,0:T(8,128)(2,1)}, bf16[16,4096]{1,0:T(8,128)(2,1)S(1)}, u32[]{:S(2)}, u32[]{:S(2)}) collective-permute-start(bf16[16,4096]{1,0:T(8,128)(2,1)} %refs_0_.3), channel_id=1, source_target_pairs={{0,4},{2,6},{4,0},{6,2},{8,12},{10,14},{12,8},{14,10},{1,5},{3,7},... | collective-permute-start | bytes 393224 | tf_op jit(solution)/shard_map/ppermute | solution.py:112
  5.6 10.8 %collective-permute-start.1 = (bf16[16,4096]{1,0:T(8,128)(2,1)}, bf16[16,4096]{1,0:T(8,128)(2,1)S(1)}, u32[]{:S(2)}, u32[]{:S(2)}) collective-permute-start(bf16[16,4096]{1,0:T(8,128)(2,1)} %refs_0_.3), channel_id=1, source_target_pairs={{0,2},{2,0},{4,6},{6,4},{8,10},{10,8},{12,14},{14,12},{1,3},{3,1},... | collective-permute-start | bytes 393224 | tf_op jit(solution)/shard_map/ppermute | solution.py:112
  9.4 7.1 %collective-permute-start = (bf16[16,4096]{1,0:T(8,128)(2,1)S(1)}, bf16[16,4096]{1,0:T(8,128)(2,1)S(1)}, u32[]{:S(2)}, u32[]{:S(2)}) collective-permute-start(bf16[16,4096]{1,0:T(8,128)(2,1)S(1)} %copy-done.1), channel_id=1, source_target_pairs={{0,6},{2,4},{4,2},{6,0},{8,14},{10,12},{12,10},{14,8},{1,7},{3,5},... | collective-permute-start | bytes 393224 | tf_op jit(solution)/shard_map/ppermute | solution.py:112
  10.7 8.2 %collective-permute-start.6 = (bf16[16,4096]{1,0:T(8,128)(2,1)S(1)}, bf16[16,4096]{1,0:T(8,128)(2,1)S(1)}, u32[]{:S(2)}, u32[]{:S(2)}) collective-permute-start(bf16[16,4096]{1,0:T(8,128)(2,1)S(1)} %collective-permute-done.3.refs_4_), channel_id=1, source_target_pairs={{0,6},{2,4},{4,2},{6,0},{8,14},{10,12},{12,10},{14,8},{1,7},{3,5},... | collective-permute-start | bytes 393224 | tf_op jit(solution)/shard_map/ppermute | solution.py:112
  12.4 8.0 %collective-permute-start.5 = (bf16[16,4096]{1,0:T(8,128)(2,1)S(1)}, bf16[16,4096]{1,0:T(8,128)(2,1)S(1)}, u32[]{:S(2)}, u32[]{:S(2)}) collective-permute-start(bf16[16,4096]{1,0:T(8,128)(2,1)S(1)} %collective-permute-done.3.refs_4_), channel_id=1, source_target_pairs={{0,2},{2,0},{4,6},{6,4},{8,10},{10,8},{12,14},{14,12},{1,3},{3,1},... | collective-permute-start | bytes 393224 | tf_op jit(solution)/shard_map/ppermute | solution.py:112
  12.9 7.5 %collective-permute-start.4 = (bf16[16,4096]{1,0:T(8,128)(2,1)S(1)}, bf16[16,4096]{1,0:T(8,128)(2,1)S(1)}, u32[]{:S(2)}, u32[]{:S(2)}) collective-permute-start(bf16[16,4096]{1,0:T(8,128)(2,1)S(1)} %collective-permute-done.3.refs_4_), channel_id=1, source_target_pairs={{0,4},{2,6},{4,0},{6,2},{8,12},{10,14},{12,8},{14,10},{1,5},{3,7},... | collective-permute-start | bytes 393224 | tf_op jit(solution)/shard_map/ppermute | solution.py:112
  16.4 7.1 %copy-start = (bf16[512,4096]{1,0:T(8,128)(2,1)S(1)}, bf16[512,4096]{1,0:T(8,128)(2,1)}, u32[]{:S(2)}) copy-start(bf16[512,4096]{1,0:T(8,128)(2,1)} %weight_ref.1) | copy-start | bytes 12582916
  21.1 1.6 %collective-permute-start.7 = (f32[128,512]{1,0:T(8,128)S(1)}, f32[128,512]{1,0:T(8,128)S(1)}, u32[]{:S(2)}, u32[]{:S(2)}) collective-permute-start(f32[128,512]{1,0:T(8,128)S(1)} %project.2.gate_ref), channel_id=1, source_target_pairs={{0,1},{1,0},{2,3},{3,2},{4,5},{5,4},{6,7},{7,6},{8,9},{9,8},{10,11... | collective-permute-start | bytes 786440 | tf_op jit(solution)/shard_map/ppermute | solution.py:115
  21.9 1.7 %collective-permute-start.8 = (f32[128,512]{1,0:T(8,128)S(1)}, f32[128,512]{1,0:T(8,128)S(1)}, u32[]{:S(2)}, u32[]{:S(2)}) collective-permute-start(f32[128,512]{1,0:T(8,128)S(1)} %project.3.up_ref), channel_id=1, source_target_pairs={{0,1},{1,0},{2,3},{3,2},{4,5},{5,4},{6,7},{7,6},{8,9},{9,8},{10,11... | collective-permute-start | bytes 786440 | tf_op jit(solution)/shard_map/ppermute | solution.py:115
  24.3 6.6 %collective-permute-start.12 = (bf16[16,4096]{1,0:T(8,128)(2,1)S(1)}, bf16[16,4096]{1,0:T(8,128)(2,1)S(1)}, u32[]{:S(2)}, u32[]{:S(2)}) collective-permute-start(bf16[16,4096]{1,0:T(8,128)(2,1)S(1)} %get-tuple-element.27), channel_id=1, source_target_pairs={{0,2},{2,0},{4,6},{6,4},{8,10},{10,8},{12,14},{14,12},{1,3},{3,1},... | collective-permute-start | bytes 393224 | tf_op jit(solution)/shard_map/ppermute | solution.py:112
  25.3 6.4 %collective-permute-start.13 = (bf16[16,4096]{1,0:T(8,128)(2,1)S(1)}, bf16[16,4096]{1,0:T(8,128)(2,1)S(1)}, u32[]{:S(2)}, u32[]{:S(2)}) collective-permute-start(bf16[16,4096]{1,0:T(8,128)(2,1)S(1)} %get-tuple-element.28), channel_id=1, source_target_pairs={{0,4},{2,6},{4,0},{6,2},{8,12},{10,14},{12,8},{14,10},{1,5},{3,7},... | collective-permute-start | bytes 393224 | tf_op jit(solution)/shard_map/ppermute | solution.py:112
  26.4 13.5 %collective-permute-start.11 = (bf16[16,4096]{1,0:T(8,128)(2,1)S(1)}, bf16[16,4096]{1,0:T(8,128)(2,1)S(1)}, u32[]{:S(2)}, u32[]{:S(2)}) collective-permute-start(bf16[16,4096]{1,0:T(8,128)(2,1)S(1)} %get-tuple-element.25), channel_id=1, source_target_pairs={{0,4},{2,6},{4,0},{6,2},{8,12},{10,14},{12,8},{14,10},{1,5},{3,7},... | collective-permute-start | bytes 393224 | tf_op jit(solution)/shard_map/ppermute | solution.py:112
  27.3 14.0 %collective-permute-start.9 = (bf16[16,4096]{1,0:T(8,128)(2,1)S(1)}, bf16[16,4096]{1,0:T(8,128)(2,1)S(1)}, u32[]{:S(2)}, u32[]{:S(2)}) collective-permute-start(bf16[16,4096]{1,0:T(8,128)(2,1)S(1)} %get-tuple-element.22), channel_id=1, source_target_pairs={{0,14},{2,12},{4,10},{6,8},{8,6},{10,4},{12,2},{14,0},{1,15},{3,13... | collective-permute-start | bytes 393224 | tf_op jit(solution)/shard_map/ppermute | solution.py:112
  30.9 11.0 %collective-permute-start.10 = (bf16[16,4096]{1,0:T(8,128)(2,1)S(1)}, bf16[16,4096]{1,0:T(8,128)(2,1)S(1)}, u32[]{:S(2)}, u32[]{:S(2)}) collective-permute-start(bf16[16,4096]{1,0:T(8,128)(2,1)S(1)} %get-tuple-element.23), channel_id=1, source_target_pairs={{0,4},{2,6},{4,0},{6,2},{8,12},{10,14},{12,8},{14,10},{1,5},{3,7},... | collective-permute-start | bytes 393224 | tf_op jit(solution)/shard_map/ppermute | solution.py:112
  31.7 13.3 %collective-permute-start.15 = (bf16[16,4096]{1,0:T(8,128)(2,1)S(1)}, bf16[16,4096]{1,0:T(8,128)(2,1)S(1)}, u32[]{:S(2)}, u32[]{:S(2)}) collective-permute-start(bf16[16,4096]{1,0:T(8,128)(2,1)S(1)} %add.4.refs_1_), channel_id=1, source_target_pairs={{0,8},{2,10},{4,12},{6,14},{8,0},{10,2},{12,4},{14,6},{1,9},{3,11}... | collective-permute-start | bytes 393224 | tf_op jit(solution)/shard_map/ppermute | solution.py:112
  39.9 5.0 %collective-permute-start.14 = (bf16[16,4096]{1,0:T(8,128)(2,1)S(1)}, bf16[16,4096]{1,0:T(8,128)(2,1)S(1)}, u32[]{:S(2)}, u32[]{:S(2)}) collective-permute-start(bf16[16,4096]{1,0:T(8,128)(2,1)S(1)} %add.5.refs_2_), channel_id=1, source_target_pairs={{0,2},{2,0},{4,6},{6,4},{8,10},{10,8},{12,14},{14,12},{1,3},{3,1},... | collective-permute-start | bytes 393224 | tf_op jit(solution)/shard_map/ppermute | solution.py:112

commit v24 on v23

--- a/solution.py
+++ b/solution.py
@@ -130,7 +130,7 @@
         for far in fars:
             for near in (2, 3, 1):
                 block[far + near] = swap(block[far], near)
-        stay = [0, 1] + fars
+        stay = [0, 2] + fars
         order = [0, 3, 1, 2] + [far + near for far in fars for near in (0, 2, 1, 3)]
         blocks = [block[b] for b in order]
         gate_part = project(blocks, gate_held)
@@ -145,9 +145,9 @@
             sums.append(add(part[far], [swap(part[far + near], near) for near in (1, 2)], BF16))
             direct.append(swap(part[far + 3], far + 3))
         arrived = [swap(value, far) for value, far in zip(sums, fars)]
-        pair = add(part[1], [swap(part[3], 2)], BF16, after=sums)
-        total = add(part[0], direct + [swap(part[2], 2)], F32, 1500000000, after=[pair])
-        return add(total, [swap(pair, 1)] + arrived, BF16)
+        pair = add(part[2], [swap(part[3], 1)], BF16, after=sums)
+        total = add(part[0], direct + [swap(part[1], 1)], F32, 1500000000, after=[pair])
+        return add(total, [swap(pair, 2)] + arrived, BF16)
 
     return local
 

time: 45.8 us -> 43.8 us (0.956)
  starting transfers between devices: 23 us -> 20.3 us
  waiting for transfers between devices: 15.2 us -> 15.9 us
    ppermute x14, starting transfers between devices: 22.3 us -> 19.7 us  [swap(): return lax.ppermute(value, 'wide', [(i, i ^ bits) for i in range(wide)])]
    ppermute x14, waiting for transfers between devices: 14 us -> 14.7 us  [swap(): return lax.ppermute(value, 'wide', [(i, i ^ bits) for i in range(wide)])]
  transfers between devices with their start and end apart: 16 -> 16, of which waited for: 9 -> 8; matrix products, arithmetic and copies ran while one was open for 0% -> 0% of each run, Pallas kernels for 11% -> 12%
where the time goes in v24:
time: 43.8 us; the launch traced here: 43.7 us
  starting transfers between devices  20.3 us (46%)
  waiting for transfers between devices  15.9 us (36%)
  Pallas kernels  7.39 us (17%)
    ppermute x14, starting transfers between devices, swap(): return lax.ppermute(value, 'wide', [(i, i ^ bits) for i in range(wide)])  19.7 us
    ppermute x14, waiting for transfers between devices, swap(): return lax.ppermute(value, 'wide', [(i, i ^ bits) for i in range(wide)])  14.7 us
    pallas_call x2, Pallas kernels, fetch(): pl.pallas_call(functools.partial(fetch_kernel, pieces), in_specs=[pl.Bloc...  4.43 us
    pallas_call x3, Pallas kernels, call(): pl.pallas_call(kernel, out_shape=out_shape, compiler_params=pltpu.Compile...  2.16 us
    ppermute x2, waiting for transfers between devices, across_cores(): lax.ppermute(value, 'narrow', [(i, (i + 1) % narrow) for i in range(narro...  1.16 us
  transfers between devices with their start and end apart: 16, of which 8 were waited for; matrix products, arithmetic and copies ran while one was open for 0% of the time, Pallas kernels for 12%

profile of v24, /device:TPU:0, one launch (start us, length us, event | category | flops | bytes accessed | tf_op | source)
XLA Modules:
  0.0 43.7 jit_solution(2812410935701085399)
XLA Ops:
  0.0 0.0 copy-start.1
  0.0 4.0 %collective-permute-start.3 = (bf16[16,4096]{1,0:T(8,128)(2,1)}, bf16[16,4096]{1,0:T(8,128)(2,1)S(1)}, u32[]{:S(2)}, u32[]{:S(2)}) collective-permute-start(bf16[16,4096]{1,0:T(8,128)(2,1)} %refs_0_.3), channel_id=1, source_target_pairs={{0,8},{2,10},{4,12},{6,14},{8,0},{10,2},{12,4},{14,6},{1,9},{3,11}... | collective-permute-start | bytes 393224 | tf_op jit(solution)/shard_map/ppermute | solution.py:112
  4.0 1.6 %collective-permute-start.2 = (bf16[16,4096]{1,0:T(8,128)(2,1)}, bf16[16,4096]{1,0:T(8,128)(2,1)S(1)}, u32[]{:S(2)}, u32[]{:S(2)}) collective-permute-start(bf16[16,4096]{1,0:T(8,128)(2,1)} %refs_0_.3), channel_id=1, source_target_pairs={{0,4},{2,6},{4,0},{6,2},{8,12},{10,14},{12,8},{14,10},{1,5},{3,7},... | collective-permute-start | bytes 393224 | tf_op jit(solution)/shard_map/ppermute | solution.py:112
  5.6 1.5 %collective-permute-start.1 = (bf16[16,4096]{1,0:T(8,128)(2,1)}, bf16[16,4096]{1,0:T(8,128)(2,1)S(1)}, u32[]{:S(2)}, u32[]{:S(2)}) collective-permute-start(bf16[16,4096]{1,0:T(8,128)(2,1)} %refs_0_.3), channel_id=1, source_target_pairs={{0,2},{2,0},{4,6},{6,4},{8,10},{10,8},{12,14},{14,12},{1,3},{3,1},... | collective-permute-start | bytes 393224 | tf_op jit(solution)/shard_map/ppermute | solution.py:112
  7.1 2.2 %fetch.2.refs_8_ = bf16[4096,512]{1,0:T(8,128)(2,1)S(1)} custom-call(bf16[4096,512]{1,0:T(8,128)(2,1)} %source.2), custom_call_target="tpu_custom_call" | custom-call | flops 2000000000 | tf_op jit(solution)/shard_map/fetch/pallas_call | solution.py:37
  9.4 0.0 copy-done.1
  9.4 0.5 %collective-permute-start = (bf16[16,4096]{1,0:T(8,128)(2,1)S(1)}, bf16[16,4096]{1,0:T(8,128)(2,1)S(1)}, u32[]{:S(2)}, u32[]{:S(2)}) collective-permute-start(bf16[16,4096]{1,0:T(8,128)(2,1)S(1)} %copy-done.1), channel_id=1, source_target_pairs={{0,6},{2,4},{4,2},{6,0},{8,14},{10,12},{12,10},{14,8},{1,7},{3,5},... | collective-permute-start | bytes 393224 | tf_op jit(solution)/shard_map/ppermute | solution.py:112
  9.8 0.9 %collective-permute-done.3.refs_4_ = bf16[16,4096]{1,0:T(8,128)(2,1)S(1)} collective-permute-done((bf16[16,4096]{1,0:T(8,128)(2,1)}, bf16[16,4096]{1,0:T(8,128)(2,1)S(1)}, u32[]{:S(2)}, u32[]{:S(2)}) %collective-permute-start.3) | collective-permute-done | bytes 131104 | tf_op jit(solution)/shard_map/ppermute | solution.py:112
  10.7 1.7 %collective-permute-start.6 = (bf16[16,4096]{1,0:T(8,128)(2,1)S(1)}, bf16[16,4096]{1,0:T(8,128)(2,1)S(1)}, u32[]{:S(2)}, u32[]{:S(2)}) collective-permute-start(bf16[16,4096]{1,0:T(8,128)(2,1)S(1)} %collective-permute-done.3.refs_4_), channel_id=1, source_target_pairs={{0,6},{2,4},{4,2},{6,0},{8,14},{10,12},{12,10},{14,8},{1,7},{3,5},... | collective-permute-start | bytes 393224 | tf_op jit(solution)/shard_map/ppermute | solution.py:112
  12.4 0.5 %collective-permute-start.5 = (bf16[16,4096]{1,0:T(8,128)(2,1)S(1)}, bf16[16,4096]{1,0:T(8,128)(2,1)S(1)}, u32[]{:S(2)}, u32[]{:S(2)}) collective-permute-start(bf16[16,4096]{1,0:T(8,128)(2,1)S(1)} %collective-permute-done.3.refs_4_), channel_id=1, source_target_pairs={{0,2},{2,0},{4,6},{6,4},{8,10},{10,8},{12,14},{14,12},{1,3},{3,1},... | collective-permute-start | bytes 393224 | tf_op jit(solution)/shard_map/ppermute | solution.py:112
  12.9 0.0 collective-permute-done.2.refs_3_
  12.9 1.3 %collective-permute-start.4 = (bf16[16,4096]{1,0:T(8,128)(2,1)S(1)}, bf16[16,4096]{1,0:T(8,128)(2,1)S(1)}, u32[]{:S(2)}, u32[]{:S(2)}) collective-permute-start(bf16[16,4096]{1,0:T(8,128)(2,1)S(1)} %collective-permute-done.3.refs_4_), channel_id=1, source_target_pairs={{0,4},{2,6},{4,0},{6,2},{8,12},{10,14},{12,8},{14,10},{1,5},{3,7},... | collective-permute-start | bytes 393224 | tf_op jit(solution)/shard_map/ppermute | solution.py:112
  14.2 2.2 %fetch.3.refs_8_ = bf16[4096,512]{1,0:T(8,128)(2,1)S(1)} custom-call(bf16[4096,512]{1,0:T(8,128)(2,1)} %source.3), custom_call_target="tpu_custom_call" | custom-call | flops 2000000000 | tf_op jit(solution)/shard_map/fetch/pallas_call | solution.py:37
  16.4 0.0 copy-start
  16.5 0.0 collective-permute-done.1.refs_2_
  16.5 0.0 collective-permute-done.refs_1_
  16.5 2.5 %collective-permute-done.6.refs_7_ = bf16[16,4096]{1,0:T(8,128)(2,1)S(1)} collective-permute-done((bf16[16,4096]{1,0:T(8,128)(2,1)S(1)}, bf16[16,4096]{1,0:T(8,128)(2,1)S(1)}, u32[]{:S(2)}, u32[]{:S(2)}) %collective-permute-start.6) | collective-permute-done | bytes 131104 | tf_op jit(solution)/shard_map/ppermute | solution.py:112
  19.0 1.4 %collective-permute-done.5.refs_6_ = bf16[16,4096]{1,0:T(8,128)(2,1)S(1)} collective-permute-done((bf16[16,4096]{1,0:T(8,128)(2,1)S(1)}, bf16[16,4096]{1,0:T(8,128)(2,1)S(1)}, u32[]{:S(2)}, u32[]{:S(2)}) %collective-permute-start.5) | collective-permute-done | bytes 131104 | tf_op jit(solution)/shard_map/ppermute | solution.py:112
  20.3 0.0 collective-permute-done.4.refs_5_
  20.4 0.7 %project.2.gate_ref = f32[128,512]{1,0:T(8,128)S(1)} custom-call(bf16[16,4096]{1,0:T(8,128)(2,1)S(1)} %copy-done.1, bf16[16,4096]{1,0:T(8,128)(2,1)S(1)} %collective-permute-done.refs_1_, bf16[16,4096]{1,0:T(8,128)(2,1)S(1)} %collective-permute-done.1.refs_2_, bf16[16,4096]{1,0:T(8,128)(2,1)S(1)} %collective-permute-done.2.refs_3_, ...), custom_call_target="tpu_custom_call" | custom-call | flops 400000000 | tf_op jit(solution)/shard_map/project/pallas_call | solution.py:15
  21.1 0.1 collective-permute-start.7
  21.2 0.7 %project.3.up_ref = f32[128,512]{1,0:T(8,128)S(1)} custom-call(bf16[16,4096]{1,0:T(8,128)(2,1)S(1)} %copy-done.1, bf16[16,4096]{1,0:T(8,128)(2,1)S(1)} %collective-permute-done.refs_1_, bf16[16,4096]{1,0:T(8,128)(2,1)S(1)} %collective-permute-done.1.refs_2_, bf16[16,4096]{1,0:T(8,128)(2,1)S(1)} %collective-permute-done.2.refs_3_, ...), custom_call_target="tpu_custom_call" | custom-call | flops 400000000 | tf_op jit(solution)/shard_map/project/pallas_call | solution.py:15
  21.9 0.6 %collective-permute-start.8 = (f32[128,512]{1,0:T(8,128)S(1)}, f32[128,512]{1,0:T(8,128)S(1)}, u32[]{:S(2)}, u32[]{:S(2)}) collective-permute-start(f32[128,512]{1,0:T(8,128)S(1)} %project.3.up_ref), channel_id=1, source_target_pairs={{0,1},{1,0},{2,3},{3,2},{4,5},{5,4},{6,7},{7,6},{8,9},{9,8},{10,11... | collective-permute-start | bytes 786440 | tf_op jit(solution)/shard_map/ppermute | solution.py:115
  22.4 0.2 collective-permute-done.7.gate_other_ref
  22.7 0.9 %collective-permute-done.8.up_other_ref = f32[128,512]{1,0:T(8,128)S(1)} collective-permute-done((f32[128,512]{1,0:T(8,128)S(1)}, f32[128,512]{1,0:T(8,128)S(1)}, u32[]{:S(2)}, u32[]{:S(2)}) %collective-permute-start.8) | collective-permute-done | bytes 262176 | tf_op jit(solution)/shard_map/ppermute | solution.py:115
  23.6 0.0 copy-done
  23.6 0.7 %down.1 = (f32[16,4096]{1,0:T(8,128)S(1)}, bf16[16,4096]{1,0:T(8,128)(2,1)S(1)}, bf16[16,4096]{1,0:T(8,128)(2,1)S(1)}, f32[16,4096]{1,0:T(8,128)S(1)}, f32[16,40...) custom-call(f32[128,512]{1,0:T(8,128)S(1)} %project.2.gate_ref, ...), custom_call_target="tpu_custom_call" | custom-call | flops 536870912 | tf_op jit(solution)/shard_map/down/pallas_call | solution.py:15
  24.3 0.9 %collective-permute-start.12 = (bf16[16,4096]{1,0:T(8,128)(2,1)S(1)}, bf16[16,4096]{1,0:T(8,128)(2,1)S(1)}, u32[]{:S(2)}, u32[]{:S(2)}) collective-permute-start(bf16[16,4096]{1,0:T(8,128)(2,1)S(1)} %get-tuple-element.27), channel_id=1, source_target_pairs={{0,2},{2,0},{4,6},{6,4},{8,10},{10,8},{12,14},{14,12},{1,3},{3,1},... | collective-permute-start | bytes 393224 | tf_op jit(solution)/shard_map/ppermute | solution.py:112
  25.3 1.1 %collective-permute-start.13 = (bf16[16,4096]{1,0:T(8,128)(2,1)S(1)}, bf16[16,4096]{1,0:T(8,128)(2,1)S(1)}, u32[]{:S(2)}, u32[]{:S(2)}) collective-permute-start(bf16[16,4096]{1,0:T(8,128)(2,1)S(1)} %get-tuple-element.28), channel_id=1, source_target_pairs={{0,4},{2,6},{4,0},{6,2},{8,12},{10,14},{12,8},{14,10},{1,5},{3,7},... | collective-permute-start | bytes 393224 | tf_op jit(solution)/shard_map/ppermute | solution.py:112
  26.4 1.4 %collective-permute-start.11 = (bf16[16,4096]{1,0:T(8,128)(2,1)S(1)}, bf16[16,4096]{1,0:T(8,128)(2,1)S(1)}, u32[]{:S(2)}, u32[]{:S(2)}) collective-permute-start(bf16[16,4096]{1,0:T(8,128)(2,1)S(1)} %get-tuple-element.25), channel_id=1, source_target_pairs={{0,2},{2,0},{4,6},{6,4},{8,10},{10,8},{12,14},{14,12},{1,3},{3,1},... | collective-permute-start | bytes 393224 | tf_op jit(solution)/shard_map/ppermute | solution.py:112
  27.8 1.9 %collective-permute-start.9 = (bf16[16,4096]{1,0:T(8,128)(2,1)S(1)}, bf16[16,4096]{1,0:T(8,128)(2,1)S(1)}, u32[]{:S(2)}, u32[]{:S(2)}) collective-permute-start(bf16[16,4096]{1,0:T(8,128)(2,1)S(1)} %get-tuple-element.22), channel_id=1, source_target_pairs={{0,14},{2,12},{4,10},{6,8},{8,6},{10,4},{12,2},{14,0},{1,15},{3,13... | collective-permute-start | bytes 393224 | tf_op jit(solution)/shard_map/ppermute | solution.py:112
  29.7 1.5 %collective-permute-start.10 = (bf16[16,4096]{1,0:T(8,128)(2,1)S(1)}, bf16[16,4096]{1,0:T(8,128)(2,1)S(1)}, u32[]{:S(2)}, u32[]{:S(2)}) collective-permute-start(bf16[16,4096]{1,0:T(8,128)(2,1)S(1)} %get-tuple-element.23), channel_id=1, source_target_pairs={{0,2},{2,0},{4,6},{6,4},{8,10},{10,8},{12,14},{14,12},{1,3},{3,1},... | collective-permute-start | bytes 393224 | tf_op jit(solution)/shard_map/ppermute | solution.py:112
  31.2 0.0 collective-permute-done.12.refs_0_
  31.2 0.0 collective-permute-done.13.refs_1_
  31.2 1.4 %collective-permute-start.15 = (bf16[16,4096]{1,0:T(8,128)(2,1)S(1)}, bf16[16,4096]{1,0:T(8,128)(2,1)S(1)}, u32[]{:S(2)}, u32[]{:S(2)}) collective-permute-start(bf16[16,4096]{1,0:T(8,128)(2,1)S(1)} %add.4.refs_1_), channel_id=1, source_target_pairs={{0,8},{2,10},{4,12},{6,14},{8,0},{10,2},{12,4},{14,6},{1,9},{3,11}... | collective-permute-start | bytes 393224 | tf_op jit(solution)/shard_map/ppermute | solution.py:112
  32.6 3.7 %collective-permute-done.11.refs_0_ = bf16[16,4096]{1,0:T(8,128)(2,1)S(1)} collective-permute-done((bf16[16,4096]{1,0:T(8,128)(2,1)S(1)}, bf16[16,4096]{1,0:T(8,128)(2,1)S(1)}, u32[]{:S(2)}, u32[]{:S(2)}) %collective-permute-start.11) | collective-permute-done | bytes 131104 | tf_op jit(solution)/shard_map/ppermute | solution.py:112
  36.4 0.4 collective-permute-start.14
  36.8 0.0 collective-permute-done.9.refs_0_
  36.8 1.9 %collective-permute-done.10.refs_1_ = bf16[16,4096]{1,0:T(8,128)(2,1)S(1)} collective-permute-done((bf16[16,4096]{1,0:T(8,128)(2,1)S(1)}, bf16[16,4096]{1,0:T(8,128)(2,1)S(1)}, u32[]{:S(2)}, u32[]{:S(2)}) %collective-permute-start.10) | collective-permute-done | bytes 131104 | tf_op jit(solution)/shard_map/ppermute | solution.py:112
  38.7 4.3 %collective-permute-done.14.refs_0_ = bf16[16,4096]{1,0:T(8,128)(2,1)S(1)} collective-permute-done((bf16[16,4096]{1,0:T(8,128)(2,1)S(1)}, bf16[16,4096]{1,0:T(8,128)(2,1)S(1)}, u32[]{:S(2)}, u32[]{:S(2)}) %collective-permute-start.14) | collective-permute-done | bytes 131104 | tf_op jit(solution)/shard_map/ppermute | solution.py:112
  43.0 0.0 collective-permute-done.15.refs_1_
  43.0 0.7 %add.7 = bf16[16,4096]{1,0:T(8,128)(2,1)} custom-call(f32[16,4096]{1,0:T(8,128)S(1)} %add.6.own_ref, bf16[16,4096]{1,0:T(8,128)(2,1)S(1)} %collective-permute-done.14.refs_0_, bf16[16,4096]{1,0:T(8,128)(2,1)S(1)} %collective-permute-done.15.refs_1_), custom_call_target="tpu_custom_call" | custom-call | flops 1000000 | tf_op jit(solution)/shard_map/add/pallas_call | solution.py:97
  (3 shorter events, 0.1 us)
Async XLA Ops:
  0.0 9.4 %copy-start.1 = (bf16[16,4096]{1,0:T(8,128)(2,1)S(1)}, bf16[16,4096]{1,0:T(8,128)(2,1)}, u32[]{:S(2)}) copy-start(bf16[16,4096]{1,0:T(8,128)(2,1)} %refs_0_.3) | copy-start | bytes 393220
  0.0 10.7 %collective-permute-start.3 = (bf16[16,4096]{1,0:T(8,128)(2,1)}, bf16[16,4096]{1,0:T(8,128)(2,1)S(1)}, u32[]{:S(2)}, u32[]{:S(2)}) collective-permute-start(bf16[16,4096]{1,0:T(8,128)(2,1)} %refs_0_.3), channel_id=1, source_target_pairs={{0,8},{2,10},{4,12},{6,14},{8,0},{10,2},{12,4},{14,6},{1,9},{3,11}... | collective-permute-start | bytes 393224 | tf_op jit(solution)/shard_map/ppermute | solution.py:112
  4.0 8.9 %collective-permute-start.2 = (bf16[16,4096]{1,0:T(8,128)(2,1)}, bf16[16,4096]{1,0:T(8,128)(2,1)S(1)}, u32[]{:S(2)}, u32[]{:S(2)}) collective-permute-start(bf16[16,4096]{1,0:T(8,128)(2,1)} %refs_0_.3), channel_id=1, source_target_pairs={{0,4},{2,6},{4,0},{6,2},{8,12},{10,14},{12,8},{14,10},{1,5},{3,7},... | collective-permute-start | bytes 393224 | tf_op jit(solution)/shard_map/ppermute | solution.py:112
  5.6 10.8 %collective-permute-start.1 = (bf16[16,4096]{1,0:T(8,128)(2,1)}, bf16[16,4096]{1,0:T(8,128)(2,1)S(1)}, u32[]{:S(2)}, u32[]{:S(2)}) collective-permute-start(bf16[16,4096]{1,0:T(8,128)(2,1)} %refs_0_.3), channel_id=1, source_target_pairs={{0,2},{2,0},{4,6},{6,4},{8,10},{10,8},{12,14},{14,12},{1,3},{3,1},... | collective-permute-start | bytes 393224 | tf_op jit(solution)/shard_map/ppermute | solution.py:112
  9.4 7.1 %collective-permute-start = (bf16[16,4096]{1,0:T(8,128)(2,1)S(1)}, bf16[16,4096]{1,0:T(8,128)(2,1)S(1)}, u32[]{:S(2)}, u32[]{:S(2)}) collective-permute-start(bf16[16,4096]{1,0:T(8,128)(2,1)S(1)} %copy-done.1), channel_id=1, source_target_pairs={{0,6},{2,4},{4,2},{6,0},{8,14},{10,12},{12,10},{14,8},{1,7},{3,5},... | collective-permute-start | bytes 393224 | tf_op jit(solution)/shard_map/ppermute | solution.py:112
  10.7 8.2 %collective-permute-start.6 = (bf16[16,4096]{1,0:T(8,128)(2,1)S(1)}, bf16[16,4096]{1,0:T(8,128)(2,1)S(1)}, u32[]{:S(2)}, u32[]{:S(2)}) collective-permute-start(bf16[16,4096]{1,0:T(8,128)(2,1)S(1)} %collective-permute-done.3.refs_4_), channel_id=1, source_target_pairs={{0,6},{2,4},{4,2},{6,0},{8,14},{10,12},{12,10},{14,8},{1,7},{3,5},... | collective-permute-start | bytes 393224 | tf_op jit(solution)/shard_map/ppermute | solution.py:112
  12.4 8.0 %collective-permute-start.5 = (bf16[16,4096]{1,0:T(8,128)(2,1)S(1)}, bf16[16,4096]{1,0:T(8,128)(2,1)S(1)}, u32[]{:S(2)}, u32[]{:S(2)}) collective-permute-start(bf16[16,4096]{1,0:T(8,128)(2,1)S(1)} %collective-permute-done.3.refs_4_), channel_id=1, source_target_pairs={{0,2},{2,0},{4,6},{6,4},{8,10},{10,8},{12,14},{14,12},{1,3},{3,1},... | collective-permute-start | bytes 393224 | tf_op jit(solution)/shard_map/ppermute | solution.py:112
  12.9 7.5 %collective-permute-start.4 = (bf16[16,4096]{1,0:T(8,128)(2,1)S(1)}, bf16[16,4096]{1,0:T(8,128)(2,1)S(1)}, u32[]{:S(2)}, u32[]{:S(2)}) collective-permute-start(bf16[16,4096]{1,0:T(8,128)(2,1)S(1)} %collective-permute-done.3.refs_4_), channel_id=1, source_target_pairs={{0,4},{2,6},{4,0},{6,2},{8,12},{10,14},{12,8},{14,10},{1,5},{3,7},... | collective-permute-start | bytes 393224 | tf_op jit(solution)/shard_map/ppermute | solution.py:112
  16.4 7.1 %copy-start = (bf16[512,4096]{1,0:T(8,128)(2,1)S(1)}, bf16[512,4096]{1,0:T(8,128)(2,1)}, u32[]{:S(2)}) copy-start(bf16[512,4096]{1,0:T(8,128)(2,1)} %weight_ref.1) | copy-start | bytes 12582916
  21.1 1.6 %collective-permute-start.7 = (f32[128,512]{1,0:T(8,128)S(1)}, f32[128,512]{1,0:T(8,128)S(1)}, u32[]{:S(2)}, u32[]{:S(2)}) collective-permute-start(f32[128,512]{1,0:T(8,128)S(1)} %project.2.gate_ref), channel_id=1, source_target_pairs={{0,1},{1,0},{2,3},{3,2},{4,5},{5,4},{6,7},{7,6},{8,9},{9,8},{10,11... | collective-permute-start | bytes 786440 | tf_op jit(solution)/shard_map/ppermute | solution.py:115
  21.9 1.7 %collective-permute-start.8 = (f32[128,512]{1,0:T(8,128)S(1)}, f32[128,512]{1,0:T(8,128)S(1)}, u32[]{:S(2)}, u32[]{:S(2)}) collective-permute-start(f32[128,512]{1,0:T(8,128)S(1)} %project.3.up_ref), channel_id=1, source_target_pairs={{0,1},{1,0},{2,3},{3,2},{4,5},{5,4},{6,7},{7,6},{8,9},{9,8},{10,11... | collective-permute-start | bytes 786440 | tf_op jit(solution)/shard_map/ppermute | solution.py:115
  24.3 6.8 %collective-permute-start.12 = (bf16[16,4096]{1,0:T(8,128)(2,1)S(1)}, bf16[16,4096]{1,0:T(8,128)(2,1)S(1)}, u32[]{:S(2)}, u32[]{:S(2)}) collective-permute-start(bf16[16,4096]{1,0:T(8,128)(2,1)S(1)} %get-tuple-element.27), channel_id=1, source_target_pairs={{0,2},{2,0},{4,6},{6,4},{8,10},{10,8},{12,14},{14,12},{1,3},{3,1},... | collective-permute-start | bytes 393224 | tf_op jit(solution)/shard_map/ppermute | solution.py:112
  25.3 5.9 %collective-permute-start.13 = (bf16[16,4096]{1,0:T(8,128)(2,1)S(1)}, bf16[16,4096]{1,0:T(8,128)(2,1)S(1)}, u32[]{:S(2)}, u32[]{:S(2)}) collective-permute-start(bf16[16,4096]{1,0:T(8,128)(2,1)S(1)} %get-tuple-element.28), channel_id=1, source_target_pairs={{0,4},{2,6},{4,0},{6,2},{8,12},{10,14},{12,8},{14,10},{1,5},{3,7},... | collective-permute-start | bytes 393224 | tf_op jit(solution)/shard_map/ppermute | solution.py:112
  26.4 10.0 %collective-permute-start.11 = (bf16[16,4096]{1,0:T(8,128)(2,1)S(1)}, bf16[16,4096]{1,0:T(8,128)(2,1)S(1)}, u32[]{:S(2)}, u32[]{:S(2)}) collective-permute-start(bf16[16,4096]{1,0:T(8,128)(2,1)S(1)} %get-tuple-element.25), channel_id=1, source_target_pairs={{0,2},{2,0},{4,6},{6,4},{8,10},{10,8},{12,14},{14,12},{1,3},{3,1},... | collective-permute-start | bytes 393224 | tf_op jit(solution)/shard_map/ppermute | solution.py:112
  27.8 9.0 %collective-permute-start.9 = (bf16[16,4096]{1,0:T(8,128)(2,1)S(1)}, bf16[16,4096]{1,0:T(8,128)(2,1)S(1)}, u32[]{:S(2)}, u32[]{:S(2)}) collective-permute-start(bf16[16,4096]{1,0:T(8,128)(2,1)S(1)} %get-tuple-element.22), channel_id=1, source_target_pairs={{0,14},{2,12},{4,10},{6,8},{8,6},{10,4},{12,2},{14,0},{1,15},{3,13... | collective-permute-start | bytes 393224 | tf_op jit(solution)/shard_map/ppermute | solution.py:112
  29.7 8.9 %collective-permute-start.10 = (bf16[16,4096]{1,0:T(8,128)(2,1)S(1)}, bf16[16,4096]{1,0:T(8,128)(2,1)S(1)}, u32[]{:S(2)}, u32[]{:S(2)}) collective-permute-start(bf16[16,4096]{1,0:T(8,128)(2,1)S(1)} %get-tuple-element.23), channel_id=1, source_target_pairs={{0,2},{2,0},{4,6},{6,4},{8,10},{10,8},{12,14},{14,12},{1,3},{3,1},... | collective-permute-start | bytes 393224 | tf_op jit(solution)/shard_map/ppermute | solution.py:112
  31.2 11.8 %collective-permute-start.15 = (bf16[16,4096]{1,0:T(8,128)(2,1)S(1)}, bf16[16,4096]{1,0:T(8,128)(2,1)S(1)}, u32[]{:S(2)}, u32[]{:S(2)}) collective-permute-start(bf16[16,4096]{1,0:T(8,128)(2,1)S(1)} %add.4.refs_1_), channel_id=1, source_target_pairs={{0,8},{2,10},{4,12},{6,14},{8,0},{10,2},{12,4},{14,6},{1,9},{3,11}... | collective-permute-start | bytes 393224 | tf_op jit(solution)/shard_map/ppermute | solution.py:112
  36.4 6.6 %collective-permute-start.14 = (bf16[16,4096]{1,0:T(8,128)(2,1)S(1)}, bf16[16,4096]{1,0:T(8,128)(2,1)S(1)}, u32[]{:S(2)}, u32[]{:S(2)}) collective-permute-start(bf16[16,4096]{1,0:T(8,128)(2,1)S(1)} %add.5.refs_2_), channel_id=1, source_target_pairs={{0,4},{2,6},{4,0},{6,2},{8,12},{10,14},{12,8},{14,10},{1,5},{3,7},... | collective-permute-start | bytes 393224 | tf_op jit(solution)/shard_map/ppermute | solution.py:112

commit v25 on v24

--- a/solution.py
+++ b/solution.py
@@ -144,10 +144,11 @@
         for far in fars:
             sums.append(add(part[far], [swap(part[far + near], near) for near in (1, 2)], BF16))
             direct.append(swap(part[far + 3], far + 3))
+        pair = add(part[2], [swap(part[3], 1)], BF16, after=sums)
+        part[1], sums[0] = lax.optimization_barrier((part[1], sums[0]))
         arrived = [swap(value, far) for value, far in zip(sums, fars)]
-        pair = add(part[2], [swap(part[3], 1)], BF16, after=sums)
-        total = add(part[0], direct + [swap(part[1], 1)], F32, 1500000000, after=[pair])
-        return add(total, [swap(pair, 2)] + arrived, BF16)
+        total = add(part[0], direct, F32, 1500000000, after=[pair])
+        return add(total, arrived + [swap(pair, 2), swap(part[1], 1)], BF16)
 
     return local
 

time: 43.8 us -> 43.6 us (level)
  waiting for transfers between devices: 15.9 us -> 15 us
  starting transfers between devices: 20.3 us -> 20.9 us
    ppermute x14, waiting for transfers between devices: 14.7 us -> 13.9 us  [swap(): return lax.ppermute(value, 'wide', [(i, i ^ bits) for i in range(wide)])]
    ppermute x14, starting transfers between devices: 19.7 us -> 20.2 us  [swap(): return lax.ppermute(value, 'wide', [(i, i ^ bits) for i in range(wide)])]
  transfers between devices with their start and end apart: 16 -> 16, of which waited for: 8 -> 9; matrix products, arithmetic and copies ran while one was open for 0% -> 0% of each run, Pallas kernels for 12% -> 12%
where the time goes in v25:
time: 43.6 us; the launch traced here: 43.4 us
  starting transfers between devices  20.9 us (48%)
  waiting for transfers between devices  15 us (34%)
  Pallas kernels  7.39 us (17%)
    ppermute x14, starting transfers between devices, swap(): return lax.ppermute(value, 'wide', [(i, i ^ bits) for i in range(wide)])  20.2 us
    ppermute x14, waiting for transfers between devices, swap(): return lax.ppermute(value, 'wide', [(i, i ^ bits) for i in range(wide)])  13.9 us
    pallas_call x2, Pallas kernels, fetch(): pl.pallas_call(functools.partial(fetch_kernel, pieces), in_specs=[pl.Bloc...  4.43 us
    pallas_call x3, Pallas kernels, call(): pl.pallas_call(kernel, out_shape=out_shape, compiler_params=pltpu.Compile...  2.16 us
    ppermute x2, waiting for transfers between devices, across_cores(): lax.ppermute(value, 'narrow', [(i, (i + 1) % narrow) for i in range(narro...  1.16 us
  transfers between devices with their start and end apart: 16, of which 9 were waited for; matrix products, arithmetic and copies ran while one was open for 0% of the time, Pallas kernels for 12%

profile of v25, /device:TPU:0, one launch (start us, length us, event | category | flops | bytes accessed | tf_op | source)
XLA Modules:
  0.0 43.4 jit_solution(18394497787350120973)
XLA Ops:
  0.0 0.0 copy-start.1
  0.0 4.0 %collective-permute-start.3 = (bf16[16,4096]{1,0:T(8,128)(2,1)}, bf16[16,4096]{1,0:T(8,128)(2,1)S(1)}, u32[]{:S(2)}, u32[]{:S(2)}) collective-permute-start(bf16[16,4096]{1,0:T(8,128)(2,1)} %refs_0_.3), channel_id=1, source_target_pairs={{0,8},{2,10},{4,12},{6,14},{8,0},{10,2},{12,4},{14,6},{1,9},{3,11}... | collective-permute-start | bytes 393224 | tf_op jit(solution)/shard_map/ppermute | solution.py:112
  4.0 1.6 %collective-permute-start.2 = (bf16[16,4096]{1,0:T(8,128)(2,1)}, bf16[16,4096]{1,0:T(8,128)(2,1)S(1)}, u32[]{:S(2)}, u32[]{:S(2)}) collective-permute-start(bf16[16,4096]{1,0:T(8,128)(2,1)} %refs_0_.3), channel_id=1, source_target_pairs={{0,4},{2,6},{4,0},{6,2},{8,12},{10,14},{12,8},{14,10},{1,5},{3,7},... | collective-permute-start | bytes 393224 | tf_op jit(solution)/shard_map/ppermute | solution.py:112
  5.6 1.5 %collective-permute-start.1 = (bf16[16,4096]{1,0:T(8,128)(2,1)}, bf16[16,4096]{1,0:T(8,128)(2,1)S(1)}, u32[]{:S(2)}, u32[]{:S(2)}) collective-permute-start(bf16[16,4096]{1,0:T(8,128)(2,1)} %refs_0_.3), channel_id=1, source_target_pairs={{0,2},{2,0},{4,6},{6,4},{8,10},{10,8},{12,14},{14,12},{1,3},{3,1},... | collective-permute-start | bytes 393224 | tf_op jit(solution)/shard_map/ppermute | solution.py:112
  7.1 2.2 %fetch.2.refs_8_ = bf16[4096,512]{1,0:T(8,128)(2,1)S(1)} custom-call(bf16[4096,512]{1,0:T(8,128)(2,1)} %source.2), custom_call_target="tpu_custom_call" | custom-call | flops 2000000000 | tf_op jit(solution)/shard_map/fetch/pallas_call | solution.py:37
  9.4 0.0 copy-done.1
  9.4 0.5 %collective-permute-start = (bf16[16,4096]{1,0:T(8,128)(2,1)S(1)}, bf16[16,4096]{1,0:T(8,128)(2,1)S(1)}, u32[]{:S(2)}, u32[]{:S(2)}) collective-permute-start(bf16[16,4096]{1,0:T(8,128)(2,1)S(1)} %copy-done.1), channel_id=1, source_target_pairs={{0,6},{2,4},{4,2},{6,0},{8,14},{10,12},{12,10},{14,8},{1,7},{3,5},... | collective-permute-start | bytes 393224 | tf_op jit(solution)/shard_map/ppermute | solution.py:112
  9.8 0.9 %collective-permute-done.3.refs_4_ = bf16[16,4096]{1,0:T(8,128)(2,1)S(1)} collective-permute-done((bf16[16,4096]{1,0:T(8,128)(2,1)}, bf16[16,4096]{1,0:T(8,128)(2,1)S(1)}, u32[]{:S(2)}, u32[]{:S(2)}) %collective-permute-start.3) | collective-permute-done | bytes 131104 | tf_op jit(solution)/shard_map/ppermute | solution.py:112
  10.7 1.7 %collective-permute-start.6 = (bf16[16,4096]{1,0:T(8,128)(2,1)S(1)}, bf16[16,4096]{1,0:T(8,128)(2,1)S(1)}, u32[]{:S(2)}, u32[]{:S(2)}) collective-permute-start(bf16[16,4096]{1,0:T(8,128)(2,1)S(1)} %collective-permute-done.3.refs_4_), channel_id=1, source_target_pairs={{0,6},{2,4},{4,2},{6,0},{8,14},{10,12},{12,10},{14,8},{1,7},{3,5},... | collective-permute-start | bytes 393224 | tf_op jit(solution)/shard_map/ppermute | solution.py:112
  12.4 0.5 %collective-permute-start.5 = (bf16[16,4096]{1,0:T(8,128)(2,1)S(1)}, bf16[16,4096]{1,0:T(8,128)(2,1)S(1)}, u32[]{:S(2)}, u32[]{:S(2)}) collective-permute-start(bf16[16,4096]{1,0:T(8,128)(2,1)S(1)} %collective-permute-done.3.refs_4_), channel_id=1, source_target_pairs={{0,2},{2,0},{4,6},{6,4},{8,10},{10,8},{12,14},{14,12},{1,3},{3,1},... | collective-permute-start | bytes 393224 | tf_op jit(solution)/shard_map/ppermute | solution.py:112
  12.9 0.0 collective-permute-done.2.refs_3_
  12.9 1.3 %collective-permute-start.4 = (bf16[16,4096]{1,0:T(8,128)(2,1)S(1)}, bf16[16,4096]{1,0:T(8,128)(2,1)S(1)}, u32[]{:S(2)}, u32[]{:S(2)}) collective-permute-start(bf16[16,4096]{1,0:T(8,128)(2,1)S(1)} %collective-permute-done.3.refs_4_), channel_id=1, source_target_pairs={{0,4},{2,6},{4,0},{6,2},{8,12},{10,14},{12,8},{14,10},{1,5},{3,7},... | collective-permute-start | bytes 393224 | tf_op jit(solution)/shard_map/ppermute | solution.py:112
  14.2 2.2 %fetch.3.refs_8_ = bf16[4096,512]{1,0:T(8,128)(2,1)S(1)} custom-call(bf16[4096,512]{1,0:T(8,128)(2,1)} %source.3), custom_call_target="tpu_custom_call" | custom-call | flops 2000000000 | tf_op jit(solution)/shard_map/fetch/pallas_call | solution.py:37
  16.4 0.0 copy-start
  16.5 0.0 collective-permute-done.1.refs_2_
  16.5 0.0 collective-permute-done.refs_1_
  16.5 2.5 %collective-permute-done.6.refs_7_ = bf16[16,4096]{1,0:T(8,128)(2,1)S(1)} collective-permute-done((bf16[16,4096]{1,0:T(8,128)(2,1)S(1)}, bf16[16,4096]{1,0:T(8,128)(2,1)S(1)}, u32[]{:S(2)}, u32[]{:S(2)}) %collective-permute-start.6) | collective-permute-done | bytes 131104 | tf_op jit(solution)/shard_map/ppermute | solution.py:112
  19.0 1.4 %collective-permute-done.5.refs_6_ = bf16[16,4096]{1,0:T(8,128)(2,1)S(1)} collective-permute-done((bf16[16,4096]{1,0:T(8,128)(2,1)S(1)}, bf16[16,4096]{1,0:T(8,128)(2,1)S(1)}, u32[]{:S(2)}, u32[]{:S(2)}) %collective-permute-start.5) | collective-permute-done | bytes 131104 | tf_op jit(solution)/shard_map/ppermute | solution.py:112
  20.3 0.0 collective-permute-done.4.refs_5_
  20.4 0.7 %project.2.gate_ref = f32[128,512]{1,0:T(8,128)S(1)} custom-call(bf16[16,4096]{1,0:T(8,128)(2,1)S(1)} %copy-done.1, bf16[16,4096]{1,0:T(8,128)(2,1)S(1)} %collective-permute-done.refs_1_, bf16[16,4096]{1,0:T(8,128)(2,1)S(1)} %collective-permute-done.1.refs_2_, bf16[16,4096]{1,0:T(8,128)(2,1)S(1)} %collective-permute-done.2.refs_3_, ...), custom_call_target="tpu_custom_call" | custom-call | flops 400000000 | tf_op jit(solution)/shard_map/project/pallas_call | solution.py:15
  21.1 0.1 collective-permute-start.7
  21.2 0.7 %project.3.up_ref = f32[128,512]{1,0:T(8,128)S(1)} custom-call(bf16[16,4096]{1,0:T(8,128)(2,1)S(1)} %copy-done.1, bf16[16,4096]{1,0:T(8,128)(2,1)S(1)} %collective-permute-done.refs_1_, bf16[16,4096]{1,0:T(8,128)(2,1)S(1)} %collective-permute-done.1.refs_2_, bf16[16,4096]{1,0:T(8,128)(2,1)S(1)} %collective-permute-done.2.refs_3_, ...), custom_call_target="tpu_custom_call" | custom-call | flops 400000000 | tf_op jit(solution)/shard_map/project/pallas_call | solution.py:15
  21.9 0.6 %collective-permute-start.8 = (f32[128,512]{1,0:T(8,128)S(1)}, f32[128,512]{1,0:T(8,128)S(1)}, u32[]{:S(2)}, u32[]{:S(2)}) collective-permute-start(f32[128,512]{1,0:T(8,128)S(1)} %project.3.up_ref), channel_id=1, source_target_pairs={{0,1},{1,0},{2,3},{3,2},{4,5},{5,4},{6,7},{7,6},{8,9},{9,8},{10,11... | collective-permute-start | bytes 786440 | tf_op jit(solution)/shard_map/ppermute | solution.py:115
  22.4 0.2 collective-permute-done.7.gate_other_ref
  22.7 0.9 %collective-permute-done.8.up_other_ref = f32[128,512]{1,0:T(8,128)S(1)} collective-permute-done((f32[128,512]{1,0:T(8,128)S(1)}, f32[128,512]{1,0:T(8,128)S(1)}, u32[]{:S(2)}, u32[]{:S(2)}) %collective-permute-start.8) | collective-permute-done | bytes 262176 | tf_op jit(solution)/shard_map/ppermute | solution.py:115
  23.6 0.0 copy-done
  23.6 0.7 %down.1 = (f32[16,4096]{1,0:T(8,128)S(1)}, bf16[16,4096]{1,0:T(8,128)(2,1)S(1)}, bf16[16,4096]{1,0:T(8,128)(2,1)S(1)}, f32[16,4096]{1,0:T(8,128)S(1)}, f32[16,40...) custom-call(f32[128,512]{1,0:T(8,128)S(1)} %project.2.gate_ref, ...), custom_call_target="tpu_custom_call" | custom-call | flops 536870912 | tf_op jit(solution)/shard_map/down/pallas_call | solution.py:15
  24.3 0.9 %collective-permute-start.11 = (bf16[16,4096]{1,0:T(8,128)(2,1)S(1)}, bf16[16,4096]{1,0:T(8,128)(2,1)S(1)}, u32[]{:S(2)}, u32[]{:S(2)}) collective-permute-start(bf16[16,4096]{1,0:T(8,128)(2,1)S(1)} %get-tuple-element.28), channel_id=1, source_target_pairs={{0,2},{2,0},{4,6},{6,4},{8,10},{10,8},{12,14},{14,12},{1,3},{3,1},... | collective-permute-start | bytes 393224 | tf_op jit(solution)/shard_map/ppermute | solution.py:112
  25.3 1.1 %collective-permute-start.12 = (bf16[16,4096]{1,0:T(8,128)(2,1)S(1)}, bf16[16,4096]{1,0:T(8,128)(2,1)S(1)}, u32[]{:S(2)}, u32[]{:S(2)}) collective-permute-start(bf16[16,4096]{1,0:T(8,128)(2,1)S(1)} %get-tuple-element.29), channel_id=1, source_target_pairs={{0,4},{2,6},{4,0},{6,2},{8,12},{10,14},{12,8},{14,10},{1,5},{3,7},... | collective-permute-start | bytes 393224 | tf_op jit(solution)/shard_map/ppermute | solution.py:112
  26.4 1.4 %collective-permute-start.10 = (bf16[16,4096]{1,0:T(8,128)(2,1)S(1)}, bf16[16,4096]{1,0:T(8,128)(2,1)S(1)}, u32[]{:S(2)}, u32[]{:S(2)}) collective-permute-start(bf16[16,4096]{1,0:T(8,128)(2,1)S(1)} %get-tuple-element.26), channel_id=1, source_target_pairs={{0,2},{2,0},{4,6},{6,4},{8,10},{10,8},{12,14},{14,12},{1,3},{3,1},... | collective-permute-start | bytes 393224 | tf_op jit(solution)/shard_map/ppermute | solution.py:112
  27.8 1.9 %collective-permute-start.9 = (bf16[16,4096]{1,0:T(8,128)(2,1)S(1)}, bf16[16,4096]{1,0:T(8,128)(2,1)S(1)}, u32[]{:S(2)}, u32[]{:S(2)}) collective-permute-start(bf16[16,4096]{1,0:T(8,128)(2,1)S(1)} %get-tuple-element.24), channel_id=1, source_target_pairs={{0,14},{2,12},{4,10},{6,8},{8,6},{10,4},{12,2},{14,0},{1,15},{3,13... | collective-permute-start | bytes 393224 | tf_op jit(solution)/shard_map/ppermute | solution.py:112
  29.7 1.0 %collective-permute-done.11.refs_0_ = bf16[16,4096]{1,0:T(8,128)(2,1)S(1)} collective-permute-done((bf16[16,4096]{1,0:T(8,128)(2,1)S(1)}, bf16[16,4096]{1,0:T(8,128)(2,1)S(1)}, u32[]{:S(2)}, u32[]{:S(2)}) %collective-permute-start.11) | collective-permute-done | bytes 131104 | tf_op jit(solution)/shard_map/ppermute | solution.py:112
  30.7 0.0 collective-permute-done.12.refs_1_
  30.8 1.9 %collective-permute-start.13 = (bf16[16,4096]{1,0:T(8,128)(2,1)S(1)}, bf16[16,4096]{1,0:T(8,128)(2,1)S(1)}, u32[]{:S(2)}, u32[]{:S(2)}) collective-permute-start(bf16[16,4096]{1,0:T(8,128)(2,1)S(1)} %add.4.refs_1_), channel_id=1, source_target_pairs={{0,8},{2,10},{4,12},{6,14},{8,0},{10,2},{12,4},{14,6},{1,9},{3,11}... | collective-permute-start | bytes 393224 | tf_op jit(solution)/shard_map/ppermute | solution.py:112
  32.6 1.2 %collective-permute-start.15 = (bf16[16,4096]{1,0:T(8,128)(2,1)S(1)}, bf16[16,4096]{1,0:T(8,128)(2,1)S(1)}, u32[]{:S(2)}, u32[]{:S(2)}) collective-permute-start(bf16[16,4096]{1,0:T(8,128)(2,1)S(1)} %get-tuple-element.32), channel_id=1, source_target_pairs={{0,2},{2,0},{4,6},{6,4},{8,10},{10,8},{12,14},{14,12},{1,3},{3,1},... | collective-permute-start | bytes 393224 | tf_op jit(solution)/shard_map/ppermute | solution.py:112
  33.9 1.9 %collective-permute-done.10.refs_0_ = bf16[16,4096]{1,0:T(8,128)(2,1)S(1)} collective-permute-done((bf16[16,4096]{1,0:T(8,128)(2,1)S(1)}, bf16[16,4096]{1,0:T(8,128)(2,1)S(1)}, u32[]{:S(2)}, u32[]{:S(2)}) %collective-permute-start.10) | collective-permute-done | bytes 131104 | tf_op jit(solution)/shard_map/ppermute | solution.py:112
  35.8 0.7 %collective-permute-start.14 = (bf16[16,4096]{1,0:T(8,128)(2,1)S(1)}, bf16[16,4096]{1,0:T(8,128)(2,1)S(1)}, u32[]{:S(2)}, u32[]{:S(2)}) collective-permute-start(bf16[16,4096]{1,0:T(8,128)(2,1)S(1)} %add.5.refs_1_), channel_id=1, source_target_pairs={{0,4},{2,6},{4,0},{6,2},{8,12},{10,14},{12,8},{14,10},{1,5},{3,7},... | collective-permute-start | bytes 393224 | tf_op jit(solution)/shard_map/ppermute | solution.py:112
  36.5 0.0 collective-permute-done.9.refs_0_
  36.5 5.3 %collective-permute-done.13.refs_0_ = bf16[16,4096]{1,0:T(8,128)(2,1)S(1)} collective-permute-done((bf16[16,4096]{1,0:T(8,128)(2,1)S(1)}, bf16[16,4096]{1,0:T(8,128)(2,1)S(1)}, u32[]{:S(2)}, u32[]{:S(2)}) %collective-permute-start.13) | collective-permute-done | bytes 131104 | tf_op jit(solution)/shard_map/ppermute | solution.py:112
  41.8 0.0 collective-permute-done.15.refs_2_
  41.8 0.9 %collective-permute-done.14.refs_1_ = bf16[16,4096]{1,0:T(8,128)(2,1)S(1)} collective-permute-done((bf16[16,4096]{1,0:T(8,128)(2,1)S(1)}, bf16[16,4096]{1,0:T(8,128)(2,1)S(1)}, u32[]{:S(2)}, u32[]{:S(2)}) %collective-permute-start.14) | collective-permute-done | bytes 131104 | tf_op jit(solution)/shard_map/ppermute | solution.py:112
  42.7 0.7 %add.7 = bf16[16,4096]{1,0:T(8,128)(2,1)} custom-call(f32[16,4096]{1,0:T(8,128)S(1)} %add.6.own_ref, bf16[16,4096]{1,0:T(8,128)(2,1)S(1)} %collective-permute-done.13.refs_0_, bf16[16,4096]{1,0:T(8,128)(2,1)S(1)} %collective-permute-done.14.refs_1_, bf16[16,4096]{1,0:T(8,128)(2,1)S(1)} %collective-permute-done.15.refs_2_), custom_call_target="tpu_custom_call" | custom-call | flops 1000000 | tf_op jit(solution)/shard_map/add/pallas_call | solution.py:97
  (3 shorter events, 0.1 us)
Async XLA Ops:
  0.0 9.4 %copy-start.1 = (bf16[16,4096]{1,0:T(8,128)(2,1)S(1)}, bf16[16,4096]{1,0:T(8,128)(2,1)}, u32[]{:S(2)}) copy-start(bf16[16,4096]{1,0:T(8,128)(2,1)} %refs_0_.3) | copy-start | bytes 393220
  0.0 10.7 %collective-permute-start.3 = (bf16[16,4096]{1,0:T(8,128)(2,1)}, bf16[16,4096]{1,0:T(8,128)(2,1)S(1)}, u32[]{:S(2)}, u32[]{:S(2)}) collective-permute-start(bf16[16,4096]{1,0:T(8,128)(2,1)} %refs_0_.3), channel_id=1, source_target_pairs={{0,8},{2,10},{4,12},{6,14},{8,0},{10,2},{12,4},{14,6},{1,9},{3,11}... | collective-permute-start | bytes 393224 | tf_op jit(solution)/shard_map/ppermute | solution.py:112
  4.0 8.9 %collective-permute-start.2 = (bf16[16,4096]{1,0:T(8,128)(2,1)}, bf16[16,4096]{1,0:T(8,128)(2,1)S(1)}, u32[]{:S(2)}, u32[]{:S(2)}) collective-permute-start(bf16[16,4096]{1,0:T(8,128)(2,1)} %refs_0_.3), channel_id=1, source_target_pairs={{0,4},{2,6},{4,0},{6,2},{8,12},{10,14},{12,8},{14,10},{1,5},{3,7},... | collective-permute-start | bytes 393224 | tf_op jit(solution)/shard_map/ppermute | solution.py:112
  5.6 10.8 %collective-permute-start.1 = (bf16[16,4096]{1,0:T(8,128)(2,1)}, bf16[16,4096]{1,0:T(8,128)(2,1)S(1)}, u32[]{:S(2)}, u32[]{:S(2)}) collective-permute-start(bf16[16,4096]{1,0:T(8,128)(2,1)} %refs_0_.3), channel_id=1, source_target_pairs={{0,2},{2,0},{4,6},{6,4},{8,10},{10,8},{12,14},{14,12},{1,3},{3,1},... | collective-permute-start | bytes 393224 | tf_op jit(solution)/shard_map/ppermute | solution.py:112
  9.4 7.1 %collective-permute-start = (bf16[16,4096]{1,0:T(8,128)(2,1)S(1)}, bf16[16,4096]{1,0:T(8,128)(2,1)S(1)}, u32[]{:S(2)}, u32[]{:S(2)}) collective-permute-start(bf16[16,4096]{1,0:T(8,128)(2,1)S(1)} %copy-done.1), channel_id=1, source_target_pairs={{0,6},{2,4},{4,2},{6,0},{8,14},{10,12},{12,10},{14,8},{1,7},{3,5},... | collective-permute-start | bytes 393224 | tf_op jit(solution)/shard_map/ppermute | solution.py:112
  10.7 8.2 %collective-permute-start.6 = (bf16[16,4096]{1,0:T(8,128)(2,1)S(1)}, bf16[16,4096]{1,0:T(8,128)(2,1)S(1)}, u32[]{:S(2)}, u32[]{:S(2)}) collective-permute-start(bf16[16,4096]{1,0:T(8,128)(2,1)S(1)} %collective-permute-done.3.refs_4_), channel_id=1, source_target_pairs={{0,6},{2,4},{4,2},{6,0},{8,14},{10,12},{12,10},{14,8},{1,7},{3,5},... | collective-permute-start | bytes 393224 | tf_op jit(solution)/shard_map/ppermute | solution.py:112
  12.4 8.0 %collective-permute-start.5 = (bf16[16,4096]{1,0:T(8,128)(2,1)S(1)}, bf16[16,4096]{1,0:T(8,128)(2,1)S(1)}, u32[]{:S(2)}, u32[]{:S(2)}) collective-permute-start(bf16[16,4096]{1,0:T(8,128)(2,1)S(1)} %collective-permute-done.3.refs_4_), channel_id=1, source_target_pairs={{0,2},{2,0},{4,6},{6,4},{8,10},{10,8},{12,14},{14,12},{1,3},{3,1},... | collective-permute-start | bytes 393224 | tf_op jit(solution)/shard_map/ppermute | solution.py:112
  12.9 7.5 %collective-permute-start.4 = (bf16[16,4096]{1,0:T(8,128)(2,1)S(1)}, bf16[16,4096]{1,0:T(8,128)(2,1)S(1)}, u32[]{:S(2)}, u32[]{:S(2)}) collective-permute-start(bf16[16,4096]{1,0:T(8,128)(2,1)S(1)} %collective-permute-done.3.refs_4_), channel_id=1, source_target_pairs={{0,4},{2,6},{4,0},{6,2},{8,12},{10,14},{12,8},{14,10},{1,5},{3,7},... | collective-permute-start | bytes 393224 | tf_op jit(solution)/shard_map/ppermute | solution.py:112
  16.4 7.1 %copy-start = (bf16[512,4096]{1,0:T(8,128)(2,1)S(1)}, bf16[512,4096]{1,0:T(8,128)(2,1)}, u32[]{:S(2)}) copy-start(bf16[512,4096]{1,0:T(8,128)(2,1)} %weight_ref.1) | copy-start | bytes 12582916
  21.1 1.6 %collective-permute-start.7 = (f32[128,512]{1,0:T(8,128)S(1)}, f32[128,512]{1,0:T(8,128)S(1)}, u32[]{:S(2)}, u32[]{:S(2)}) collective-permute-start(f32[128,512]{1,0:T(8,128)S(1)} %project.2.gate_ref), channel_id=1, source_target_pairs={{0,1},{1,0},{2,3},{3,2},{4,5},{5,4},{6,7},{7,6},{8,9},{9,8},{10,11... | collective-permute-start | bytes 786440 | tf_op jit(solution)/shard_map/ppermute | solution.py:115
  21.9 1.7 %collective-permute-start.8 = (f32[128,512]{1,0:T(8,128)S(1)}, f32[128,512]{1,0:T(8,128)S(1)}, u32[]{:S(2)}, u32[]{:S(2)}) collective-permute-start(f32[128,512]{1,0:T(8,128)S(1)} %project.3.up_ref), channel_id=1, source_target_pairs={{0,1},{1,0},{2,3},{3,2},{4,5},{5,4},{6,7},{7,6},{8,9},{9,8},{10,11... | collective-permute-start | bytes 786440 | tf_op jit(solution)/shard_map/ppermute | solution.py:115
  24.3 6.4 %collective-permute-start.11 = (bf16[16,4096]{1,0:T(8,128)(2,1)S(1)}, bf16[16,4096]{1,0:T(8,128)(2,1)S(1)}, u32[]{:S(2)}, u32[]{:S(2)}) collective-permute-start(bf16[16,4096]{1,0:T(8,128)(2,1)S(1)} %get-tuple-element.28), channel_id=1, source_target_pairs={{0,2},{2,0},{4,6},{6,4},{8,10},{10,8},{12,14},{14,12},{1,3},{3,1},... | collective-permute-start | bytes 393224 | tf_op jit(solution)/shard_map/ppermute | solution.py:112
  25.3 5.5 %collective-permute-start.12 = (bf16[16,4096]{1,0:T(8,128)(2,1)S(1)}, bf16[16,4096]{1,0:T(8,128)(2,1)S(1)}, u32[]{:S(2)}, u32[]{:S(2)}) collective-permute-start(bf16[16,4096]{1,0:T(8,128)(2,1)S(1)} %get-tuple-element.29), channel_id=1, source_target_pairs={{0,4},{2,6},{4,0},{6,2},{8,12},{10,14},{12,8},{14,10},{1,5},{3,7},... | collective-permute-start | bytes 393224 | tf_op jit(solution)/shard_map/ppermute | solution.py:112
  26.4 9.4 %collective-permute-start.10 = (bf16[16,4096]{1,0:T(8,128)(2,1)S(1)}, bf16[16,4096]{1,0:T(8,128)(2,1)S(1)}, u32[]{:S(2)}, u32[]{:S(2)}) collective-permute-start(bf16[16,4096]{1,0:T(8,128)(2,1)S(1)} %get-tuple-element.26), channel_id=1, source_target_pairs={{0,2},{2,0},{4,6},{6,4},{8,10},{10,8},{12,14},{14,12},{1,3},{3,1},... | collective-permute-start | bytes 393224 | tf_op jit(solution)/shard_map/ppermute | solution.py:112
  27.8 8.7 %collective-permute-start.9 = (bf16[16,4096]{1,0:T(8,128)(2,1)S(1)}, bf16[16,4096]{1,0:T(8,128)(2,1)S(1)}, u32[]{:S(2)}, u32[]{:S(2)}) collective-permute-start(bf16[16,4096]{1,0:T(8,128)(2,1)S(1)} %get-tuple-element.24), channel_id=1, source_target_pairs={{0,14},{2,12},{4,10},{6,8},{8,6},{10,4},{12,2},{14,0},{1,15},{3,13... | collective-permute-start | bytes 393224 | tf_op jit(solution)/shard_map/ppermute | solution.py:112
  30.8 11.0 %collective-permute-start.13 = (bf16[16,4096]{1,0:T(8,128)(2,1)S(1)}, bf16[16,4096]{1,0:T(8,128)(2,1)S(1)}, u32[]{:S(2)}, u32[]{:S(2)}) collective-permute-start(bf16[16,4096]{1,0:T(8,128)(2,1)S(1)} %add.4.refs_1_), channel_id=1, source_target_pairs={{0,8},{2,10},{4,12},{6,14},{8,0},{10,2},{12,4},{14,6},{1,9},{3,11}... | collective-permute-start | bytes 393224 | tf_op jit(solution)/shard_map/ppermute | solution.py:112
  32.6 9.1 %collective-permute-start.15 = (bf16[16,4096]{1,0:T(8,128)(2,1)S(1)}, bf16[16,4096]{1,0:T(8,128)(2,1)S(1)}, u32[]{:S(2)}, u32[]{:S(2)}) collective-permute-start(bf16[16,4096]{1,0:T(8,128)(2,1)S(1)} %get-tuple-element.32), channel_id=1, source_target_pairs={{0,2},{2,0},{4,6},{6,4},{8,10},{10,8},{12,14},{14,12},{1,3},{3,1},... | collective-permute-start | bytes 393224 | tf_op jit(solution)/shard_map/ppermute | solution.py:112
  35.8 6.9 %collective-permute-start.14 = (bf16[16,4096]{1,0:T(8,128)(2,1)S(1)}, bf16[16,4096]{1,0:T(8,128)(2,1)S(1)}, u32[]{:S(2)}, u32[]{:S(2)}) collective-permute-start(bf16[16,4096]{1,0:T(8,128)(2,1)S(1)} %add.5.refs_1_), channel_id=1, source_target_pairs={{0,4},{2,6},{4,0},{6,2},{8,12},{10,14},{12,8},{14,10},{1,5},{3,7},... | collective-permute-start | bytes 393224 | tf_op jit(solution)/shard_map/ppermute | solution.py:112

commit v26 on v25

--- a/solution.py
+++ b/solution.py
@@ -125,10 +125,12 @@
         up_held = fetch(up_weight, 48, 2000000000)
         own, gate_held = lax.optimization_barrier((tokens, gate_held))
         block[3] = swap(own, 3)
+        for far in fars:
+            block[far + 3] = swap(own, far + 3)
         *crossed, gate_held = lax.optimization_barrier([block[far] for far in fars] + [gate_held])
         block.update(zip(fars, crossed))
         for far in fars:
-            for near in (2, 3, 1):
+            for near in (2, 1):
                 block[far + near] = swap(block[far], near)
         stay = [0, 2] + fars
         order = [0, 3, 1, 2] + [far + near for far in fars for near in (0, 2, 1, 3)]

time: 43.6 us -> 44.3 us (1.016)
  starting transfers between devices: 20.9 us -> 25.1 us
  waiting for transfers between devices: 15 us -> 11.6 us
    ppermute x14, starting transfers between devices: 20.2 us -> 24.5 us  [swap(): return lax.ppermute(value, 'wide', [(i, i ^ bits) for i in range(wide)])]
    ppermute x14, waiting for transfers between devices: 13.9 us -> 10.4 us  [swap(): return lax.ppermute(value, 'wide', [(i, i ^ bits) for i in range(wide)])]
  transfers between devices with their start and end apart: 16 -> 16, of which waited for: 9 -> 8; matrix products, arithmetic and copies ran while one was open for 0% -> 0% of each run, Pallas kernels for 12% -> 12%
where the time goes in v26:
time: 44.3 us; the launch traced here: 44.2 us
  starting transfers between devices  25.1 us (57%)
  waiting for transfers between devices  11.6 us (26%)
  Pallas kernels  7.4 us (17%)
    ppermute x14, starting transfers between devices, swap(): return lax.ppermute(value, 'wide', [(i, i ^ bits) for i in range(wide)])  24.5 us
    ppermute x14, waiting for transfers between devices, swap(): return lax.ppermute(value, 'wide', [(i, i ^ bits) for i in range(wide)])  10.4 us
    pallas_call x2, Pallas kernels, fetch(): pl.pallas_call(functools.partial(fetch_kernel, pieces), in_specs=[pl.Bloc...  4.43 us
    pallas_call x3, Pallas kernels, call(): pl.pallas_call(kernel, out_shape=out_shape, compiler_params=pltpu.Compile...  2.17 us
    ppermute x2, waiting for transfers between devices, across_cores(): lax.ppermute(value, 'narrow', [(i, (i + 1) % narrow) for i in range(narro...  1.16 us
  transfers between devices with their start and end apart: 16, of which 8 were waited for; matrix products, arithmetic and copies ran while one was open for 0% of the time, Pallas kernels for 12%

profile of v26, /device:TPU:0, one launch (start us, length us, event | category | flops | bytes accessed | tf_op | source)
XLA Modules:
  0.0 44.2 jit_solution(14630272917574403904)
XLA Ops:
  0.0 0.0 copy-start.1
  0.0 4.0 %collective-permute-start.3 = (bf16[16,4096]{1,0:T(8,128)(2,1)}, bf16[16,4096]{1,0:T(8,128)(2,1)S(1)}, u32[]{:S(2)}, u32[]{:S(2)}) collective-permute-start(bf16[16,4096]{1,0:T(8,128)(2,1)} %refs_0_.3), channel_id=1, source_target_pairs={{0,8},{2,10},{4,12},{6,14},{8,0},{10,2},{12,4},{14,6},{1,9},{3,11}... | collective-permute-start | bytes 393224 | tf_op jit(solution)/shard_map/ppermute | solution.py:112
  4.0 1.6 %collective-permute-start.2 = (bf16[16,4096]{1,0:T(8,128)(2,1)}, bf16[16,4096]{1,0:T(8,128)(2,1)S(1)}, u32[]{:S(2)}, u32[]{:S(2)}) collective-permute-start(bf16[16,4096]{1,0:T(8,128)(2,1)} %refs_0_.3), channel_id=1, source_target_pairs={{0,4},{2,6},{4,0},{6,2},{8,12},{10,14},{12,8},{14,10},{1,5},{3,7},... | collective-permute-start | bytes 393224 | tf_op jit(solution)/shard_map/ppermute | solution.py:112
  5.6 1.5 %collective-permute-start.1 = (bf16[16,4096]{1,0:T(8,128)(2,1)}, bf16[16,4096]{1,0:T(8,128)(2,1)S(1)}, u32[]{:S(2)}, u32[]{:S(2)}) collective-permute-start(bf16[16,4096]{1,0:T(8,128)(2,1)} %refs_0_.3), channel_id=1, source_target_pairs={{0,2},{2,0},{4,6},{6,4},{8,10},{10,8},{12,14},{14,12},{1,3},{3,1},... | collective-permute-start | bytes 393224 | tf_op jit(solution)/shard_map/ppermute | solution.py:112
  7.1 2.2 %fetch.2.refs_8_ = bf16[4096,512]{1,0:T(8,128)(2,1)S(1)} custom-call(bf16[4096,512]{1,0:T(8,128)(2,1)} %source.2), custom_call_target="tpu_custom_call" | custom-call | flops 2000000000 | tf_op jit(solution)/shard_map/fetch/pallas_call | solution.py:37
  9.4 0.0 copy-done.1
  9.4 0.1 collective-permute-start.6
  9.4 1.8 %collective-permute-start = (bf16[16,4096]{1,0:T(8,128)(2,1)S(1)}, bf16[16,4096]{1,0:T(8,128)(2,1)S(1)}, u32[]{:S(2)}, u32[]{:S(2)}) collective-permute-start(bf16[16,4096]{1,0:T(8,128)(2,1)S(1)} %copy-done.1), channel_id=1, source_target_pairs={{0,6},{2,4},{4,2},{6,0},{8,14},{10,12},{12,10},{14,8},{1,7},{3,5},... | collective-permute-start | bytes 393224 | tf_op jit(solution)/shard_map/ppermute | solution.py:112
  11.2 0.0 collective-permute-done.3.refs_4_
  11.2 1.0 %collective-permute-start.5 = (bf16[16,4096]{1,0:T(8,128)(2,1)S(1)}, bf16[16,4096]{1,0:T(8,128)(2,1)S(1)}, u32[]{:S(2)}, u32[]{:S(2)}) collective-permute-start(bf16[16,4096]{1,0:T(8,128)(2,1)S(1)} %collective-permute-done.3.refs_4_), channel_id=1, source_target_pairs={{0,2},{2,0},{4,6},{6,4},{8,10},{10,8},{12,14},{14,12},{1,3},{3,1},... | collective-permute-start | bytes 393224 | tf_op jit(solution)/shard_map/ppermute | solution.py:112
  12.3 0.0 collective-permute-done.2.refs_3_
  12.3 1.5 %collective-permute-start.4 = (bf16[16,4096]{1,0:T(8,128)(2,1)S(1)}, bf16[16,4096]{1,0:T(8,128)(2,1)S(1)}, u32[]{:S(2)}, u32[]{:S(2)}) collective-permute-start(bf16[16,4096]{1,0:T(8,128)(2,1)S(1)} %collective-permute-done.3.refs_4_), channel_id=1, source_target_pairs={{0,4},{2,6},{4,0},{6,2},{8,12},{10,14},{12,8},{14,10},{1,5},{3,7},... | collective-permute-start | bytes 393224 | tf_op jit(solution)/shard_map/ppermute | solution.py:112
  13.8 2.2 %fetch.3.refs_8_ = bf16[4096,512]{1,0:T(8,128)(2,1)S(1)} custom-call(bf16[4096,512]{1,0:T(8,128)(2,1)} %source.3), custom_call_target="tpu_custom_call" | custom-call | flops 2000000000 | tf_op jit(solution)/shard_map/fetch/pallas_call | solution.py:37
  16.0 0.0 copy-start
  16.0 0.0 collective-permute-done.1.refs_2_
  16.0 2.5 %collective-permute-done.6.refs_7_ = bf16[16,4096]{1,0:T(8,128)(2,1)S(1)} collective-permute-done((bf16[16,4096]{1,0:T(8,128)(2,1)S(1)}, bf16[16,4096]{1,0:T(8,128)(2,1)S(1)}, u32[]{:S(2)}, u32[]{:S(2)}) %collective-permute-start.6) | collective-permute-done | bytes 131104 | tf_op jit(solution)/shard_map/ppermute | solution.py:112
  18.6 0.8 %collective-permute-done.refs_1_ = bf16[16,4096]{1,0:T(8,128)(2,1)S(1)} collective-permute-done((bf16[16,4096]{1,0:T(8,128)(2,1)S(1)}, bf16[16,4096]{1,0:T(8,128)(2,1)S(1)}, u32[]{:S(2)}, u32[]{:S(2)}) %collective-permute-start) | collective-permute-done | bytes 131104 | tf_op jit(solution)/shard_map/ppermute | solution.py:112
  19.3 1.1 %collective-permute-done.5.refs_6_ = bf16[16,4096]{1,0:T(8,128)(2,1)S(1)} collective-permute-done((bf16[16,4096]{1,0:T(8,128)(2,1)S(1)}, bf16[16,4096]{1,0:T(8,128)(2,1)S(1)}, u32[]{:S(2)}, u32[]{:S(2)}) %collective-permute-start.5) | collective-permute-done | bytes 131104 | tf_op jit(solution)/shard_map/ppermute | solution.py:112
  20.4 0.0 collective-permute-done.4.refs_5_
  20.4 0.7 %project.2.gate_ref = f32[128,512]{1,0:T(8,128)S(1)} custom-call(bf16[16,4096]{1,0:T(8,128)(2,1)S(1)} %copy-done.1, bf16[16,4096]{1,0:T(8,128)(2,1)S(1)} %collective-permute-done.refs_1_, bf16[16,4096]{1,0:T(8,128)(2,1)S(1)} %collective-permute-done.1.refs_2_, bf16[16,4096]{1,0:T(8,128)(2,1)S(1)} %collective-permute-done.2.refs_3_, ...), custom_call_target="tpu_custom_call" | custom-call | flops 400000000 | tf_op jit(solution)/shard_map/project/pallas_call | solution.py:15
  21.1 0.1 collective-permute-start.7
  21.2 0.7 %project.3.up_ref = f32[128,512]{1,0:T(8,128)S(1)} custom-call(bf16[16,4096]{1,0:T(8,128)(2,1)S(1)} %copy-done.1, bf16[16,4096]{1,0:T(8,128)(2,1)S(1)} %collective-permute-done.refs_1_, bf16[16,4096]{1,0:T(8,128)(2,1)S(1)} %collective-permute-done.1.refs_2_, bf16[16,4096]{1,0:T(8,128)(2,1)S(1)} %collective-permute-done.2.refs_3_, ...), custom_call_target="tpu_custom_call" | custom-call | flops 400000000 | tf_op jit(solution)/shard_map/project/pallas_call | solution.py:15
  21.9 0.6 %collective-permute-start.8 = (f32[128,512]{1,0:T(8,128)S(1)}, f32[128,512]{1,0:T(8,128)S(1)}, u32[]{:S(2)}, u32[]{:S(2)}) collective-permute-start(f32[128,512]{1,0:T(8,128)S(1)} %project.3.up_ref), channel_id=1, source_target_pairs={{0,1},{1,0},{2,3},{3,2},{4,5},{5,4},{6,7},{7,6},{8,9},{9,8},{10,11... | collective-permute-start | bytes 786440 | tf_op jit(solution)/shard_map/ppermute | solution.py:115
  22.5 0.2 collective-permute-done.7.gate_other_ref
  22.8 0.9 %collective-permute-done.8.up_other_ref = f32[128,512]{1,0:T(8,128)S(1)} collective-permute-done((f32[128,512]{1,0:T(8,128)S(1)}, f32[128,512]{1,0:T(8,128)S(1)}, u32[]{:S(2)}, u32[]{:S(2)}) %collective-permute-start.8) | collective-permute-done | bytes 262176 | tf_op jit(solution)/shard_map/ppermute | solution.py:115
  23.7 0.0 copy-done
  23.7 0.7 %down.1 = (f32[16,4096]{1,0:T(8,128)S(1)}, bf16[16,4096]{1,0:T(8,128)(2,1)S(1)}, bf16[16,4096]{1,0:T(8,128)(2,1)S(1)}, f32[16,4096]{1,0:T(8,128)S(1)}, f32[16,40...) custom-call(f32[128,512]{1,0:T(8,128)S(1)} %project.2.gate_ref, ...), custom_call_target="tpu_custom_call" | custom-call | flops 536870912 | tf_op jit(solution)/shard_map/down/pallas_call | solution.py:15
  24.4 1.3 %collective-permute-start.11 = (bf16[16,4096]{1,0:T(8,128)(2,1)S(1)}, bf16[16,4096]{1,0:T(8,128)(2,1)S(1)}, u32[]{:S(2)}, u32[]{:S(2)}) collective-permute-start(bf16[16,4096]{1,0:T(8,128)(2,1)S(1)} %get-tuple-element.28), channel_id=1, source_target_pairs={{0,2},{2,0},{4,6},{6,4},{8,10},{10,8},{12,14},{14,12},{1,3},{3,1},... | collective-permute-start | bytes 393224 | tf_op jit(solution)/shard_map/ppermute | solution.py:112
  25.8 1.0 %collective-permute-start.12 = (bf16[16,4096]{1,0:T(8,128)(2,1)S(1)}, bf16[16,4096]{1,0:T(8,128)(2,1)S(1)}, u32[]{:S(2)}, u32[]{:S(2)}) collective-permute-start(bf16[16,4096]{1,0:T(8,128)(2,1)S(1)} %get-tuple-element.29), channel_id=1, source_target_pairs={{0,4},{2,6},{4,0},{6,2},{8,12},{10,14},{12,8},{14,10},{1,5},{3,7},... | collective-permute-start | bytes 393224 | tf_op jit(solution)/shard_map/ppermute | solution.py:112
  26.8 0.6 %collective-permute-start.10 = (bf16[16,4096]{1,0:T(8,128)(2,1)S(1)}, bf16[16,4096]{1,0:T(8,128)(2,1)S(1)}, u32[]{:S(2)}, u32[]{:S(2)}) collective-permute-start(bf16[16,4096]{1,0:T(8,128)(2,1)S(1)} %get-tuple-element.26), channel_id=1, source_target_pairs={{0,2},{2,0},{4,6},{6,4},{8,10},{10,8},{12,14},{14,12},{1,3},{3,1},... | collective-permute-start | bytes 393224 | tf_op jit(solution)/shard_map/ppermute | solution.py:112
  27.4 4.1 %collective-permute-start.9 = (bf16[16,4096]{1,0:T(8,128)(2,1)S(1)}, bf16[16,4096]{1,0:T(8,128)(2,1)S(1)}, u32[]{:S(2)}, u32[]{:S(2)}) collective-permute-start(bf16[16,4096]{1,0:T(8,128)(2,1)S(1)} %get-tuple-element.24), channel_id=1, source_target_pairs={{0,14},{2,12},{4,10},{6,8},{8,6},{10,4},{12,2},{14,0},{1,15},{3,13... | collective-permute-start | bytes 393224 | tf_op jit(solution)/shard_map/ppermute | solution.py:112
  31.5 0.0 collective-permute-done.11.refs_0_
  31.5 0.0 collective-permute-done.12.refs_1_
  31.6 5.1 %collective-permute-start.13 = (bf16[16,4096]{1,0:T(8,128)(2,1)S(1)}, bf16[16,4096]{1,0:T(8,128)(2,1)S(1)}, u32[]{:S(2)}, u32[]{:S(2)}) collective-permute-start(bf16[16,4096]{1,0:T(8,128)(2,1)S(1)} %add.4.refs_1_), channel_id=1, source_target_pairs={{0,8},{2,10},{4,12},{6,14},{8,0},{10,2},{12,4},{14,6},{1,9},{3,11}... | collective-permute-start | bytes 393224 | tf_op jit(solution)/shard_map/ppermute | solution.py:112
  36.7 0.5 %collective-permute-start.15 = (bf16[16,4096]{1,0:T(8,128)(2,1)S(1)}, bf16[16,4096]{1,0:T(8,128)(2,1)S(1)}, u32[]{:S(2)}, u32[]{:S(2)}) collective-permute-start(bf16[16,4096]{1,0:T(8,128)(2,1)S(1)} %get-tuple-element.32), channel_id=1, source_target_pairs={{0,2},{2,0},{4,6},{6,4},{8,10},{10,8},{12,14},{14,12},{1,3},{3,1},... | collective-permute-start | bytes 393224 | tf_op jit(solution)/shard_map/ppermute | solution.py:112
  37.2 0.0 collective-permute-done.10.refs_0_
  37.2 0.3 collective-permute-start.14
  37.5 0.8 %collective-permute-done.9.refs_0_ = bf16[16,4096]{1,0:T(8,128)(2,1)S(1)} collective-permute-done((bf16[16,4096]{1,0:T(8,128)(2,1)S(1)}, bf16[16,4096]{1,0:T(8,128)(2,1)S(1)}, u32[]{:S(2)}, u32[]{:S(2)}) %collective-permute-start.9) | collective-permute-done | bytes 131104 | tf_op jit(solution)/shard_map/ppermute | solution.py:112
  38.3 3.9 %collective-permute-done.13.refs_0_ = bf16[16,4096]{1,0:T(8,128)(2,1)S(1)} collective-permute-done((bf16[16,4096]{1,0:T(8,128)(2,1)S(1)}, bf16[16,4096]{1,0:T(8,128)(2,1)S(1)}, u32[]{:S(2)}, u32[]{:S(2)}) %collective-permute-start.13) | collective-permute-done | bytes 131104 | tf_op jit(solution)/shard_map/ppermute | solution.py:112
  42.2 0.0 collective-permute-done.15.refs_2_
  42.2 1.3 %collective-permute-done.14.refs_1_ = bf16[16,4096]{1,0:T(8,128)(2,1)S(1)} collective-permute-done((bf16[16,4096]{1,0:T(8,128)(2,1)S(1)}, bf16[16,4096]{1,0:T(8,128)(2,1)S(1)}, u32[]{:S(2)}, u32[]{:S(2)}) %collective-permute-start.14) | collective-permute-done | bytes 131104 | tf_op jit(solution)/shard_map/ppermute | solution.py:112
  43.5 0.7 %add.7 = bf16[16,4096]{1,0:T(8,128)(2,1)} custom-call(f32[16,4096]{1,0:T(8,128)S(1)} %add.6.own_ref, bf16[16,4096]{1,0:T(8,128)(2,1)S(1)} %collective-permute-done.13.refs_0_, bf16[16,4096]{1,0:T(8,128)(2,1)S(1)} %collective-permute-done.14.refs_1_, bf16[16,4096]{1,0:T(8,128)(2,1)S(1)} %collective-permute-done.15.refs_2_), custom_call_target="tpu_custom_call" | custom-call | flops 1000000 | tf_op jit(solution)/shard_map/add/pallas_call | solution.py:97
  (3 shorter events, 0.1 us)
Async XLA Ops:
  0.0 9.4 %copy-start.1 = (bf16[16,4096]{1,0:T(8,128)(2,1)S(1)}, bf16[16,4096]{1,0:T(8,128)(2,1)}, u32[]{:S(2)}) copy-start(bf16[16,4096]{1,0:T(8,128)(2,1)} %refs_0_.3) | copy-start | bytes 393220
  0.0 11.2 %collective-permute-start.3 = (bf16[16,4096]{1,0:T(8,128)(2,1)}, bf16[16,4096]{1,0:T(8,128)(2,1)S(1)}, u32[]{:S(2)}, u32[]{:S(2)}) collective-permute-start(bf16[16,4096]{1,0:T(8,128)(2,1)} %refs_0_.3), channel_id=1, source_target_pairs={{0,8},{2,10},{4,12},{6,14},{8,0},{10,2},{12,4},{14,6},{1,9},{3,11}... | collective-permute-start | bytes 393224 | tf_op jit(solution)/shard_map/ppermute | solution.py:112
  4.0 8.2 %collective-permute-start.2 = (bf16[16,4096]{1,0:T(8,128)(2,1)}, bf16[16,4096]{1,0:T(8,128)(2,1)S(1)}, u32[]{:S(2)}, u32[]{:S(2)}) collective-permute-start(bf16[16,4096]{1,0:T(8,128)(2,1)} %refs_0_.3), channel_id=1, source_target_pairs={{0,4},{2,6},{4,0},{6,2},{8,12},{10,14},{12,8},{14,10},{1,5},{3,7},... | collective-permute-start | bytes 393224 | tf_op jit(solution)/shard_map/ppermute | solution.py:112
  5.6 10.4 %collective-permute-start.1 = (bf16[16,4096]{1,0:T(8,128)(2,1)}, bf16[16,4096]{1,0:T(8,128)(2,1)S(1)}, u32[]{:S(2)}, u32[]{:S(2)}) collective-permute-start(bf16[16,4096]{1,0:T(8,128)(2,1)} %refs_0_.3), channel_id=1, source_target_pairs={{0,2},{2,0},{4,6},{6,4},{8,10},{10,8},{12,14},{14,12},{1,3},{3,1},... | collective-permute-start | bytes 393224 | tf_op jit(solution)/shard_map/ppermute | solution.py:112
  9.4 9.2 %collective-permute-start.6 = (bf16[16,4096]{1,0:T(8,128)(2,1)S(1)}, bf16[16,4096]{1,0:T(8,128)(2,1)S(1)}, u32[]{:S(2)}, u32[]{:S(2)}) collective-permute-start(bf16[16,4096]{1,0:T(8,128)(2,1)S(1)} %copy-done.1), channel_id=1, source_target_pairs={{0,14},{2,12},{4,10},{6,8},{8,6},{10,4},{12,2},{14,0},{1,15},{3,13... | collective-permute-start | bytes 393224 | tf_op jit(solution)/shard_map/ppermute | solution.py:112
  9.4 9.9 %collective-permute-start = (bf16[16,4096]{1,0:T(8,128)(2,1)S(1)}, bf16[16,4096]{1,0:T(8,128)(2,1)S(1)}, u32[]{:S(2)}, u32[]{:S(2)}) collective-permute-start(bf16[16,4096]{1,0:T(8,128)(2,1)S(1)} %copy-done.1), channel_id=1, source_target_pairs={{0,6},{2,4},{4,2},{6,0},{8,14},{10,12},{12,10},{14,8},{1,7},{3,5},... | collective-permute-start | bytes 393224 | tf_op jit(solution)/shard_map/ppermute | solution.py:112
  11.2 9.2 %collective-permute-start.5 = (bf16[16,4096]{1,0:T(8,128)(2,1)S(1)}, bf16[16,4096]{1,0:T(8,128)(2,1)S(1)}, u32[]{:S(2)}, u32[]{:S(2)}) collective-permute-start(bf16[16,4096]{1,0:T(8,128)(2,1)S(1)} %collective-permute-done.3.refs_4_), channel_id=1, source_target_pairs={{0,2},{2,0},{4,6},{6,4},{8,10},{10,8},{12,14},{14,12},{1,3},{3,1},... | collective-permute-start | bytes 393224 | tf_op jit(solution)/shard_map/ppermute | solution.py:112
  12.3 8.2 %collective-permute-start.4 = (bf16[16,4096]{1,0:T(8,128)(2,1)S(1)}, bf16[16,4096]{1,0:T(8,128)(2,1)S(1)}, u32[]{:S(2)}, u32[]{:S(2)}) collective-permute-start(bf16[16,4096]{1,0:T(8,128)(2,1)S(1)} %collective-permute-done.3.refs_4_), channel_id=1, source_target_pairs={{0,4},{2,6},{4,0},{6,2},{8,12},{10,14},{12,8},{14,10},{1,5},{3,7},... | collective-permute-start | bytes 393224 | tf_op jit(solution)/shard_map/ppermute | solution.py:112
  16.0 7.7 %copy-start = (bf16[512,4096]{1,0:T(8,128)(2,1)S(1)}, bf16[512,4096]{1,0:T(8,128)(2,1)}, u32[]{:S(2)}) copy-start(bf16[512,4096]{1,0:T(8,128)(2,1)} %weight_ref.1) | copy-start | bytes 12582916
  21.1 1.6 %collective-permute-start.7 = (f32[128,512]{1,0:T(8,128)S(1)}, f32[128,512]{1,0:T(8,128)S(1)}, u32[]{:S(2)}, u32[]{:S(2)}) collective-permute-start(f32[128,512]{1,0:T(8,128)S(1)} %project.2.gate_ref), channel_id=1, source_target_pairs={{0,1},{1,0},{2,3},{3,2},{4,5},{5,4},{6,7},{7,6},{8,9},{9,8},{10,11... | collective-permute-start | bytes 786440 | tf_op jit(solution)/shard_map/ppermute | solution.py:115
  21.9 1.7 %collective-permute-start.8 = (f32[128,512]{1,0:T(8,128)S(1)}, f32[128,512]{1,0:T(8,128)S(1)}, u32[]{:S(2)}, u32[]{:S(2)}) collective-permute-start(f32[128,512]{1,0:T(8,128)S(1)} %project.3.up_ref), channel_id=1, source_target_pairs={{0,1},{1,0},{2,3},{3,2},{4,5},{5,4},{6,7},{7,6},{8,9},{9,8},{10,11... | collective-permute-start | bytes 786440 | tf_op jit(solution)/shard_map/ppermute | solution.py:115
  24.4 7.1 %collective-permute-start.11 = (bf16[16,4096]{1,0:T(8,128)(2,1)S(1)}, bf16[16,4096]{1,0:T(8,128)(2,1)S(1)}, u32[]{:S(2)}, u32[]{:S(2)}) collective-permute-start(bf16[16,4096]{1,0:T(8,128)(2,1)S(1)} %get-tuple-element.28), channel_id=1, source_target_pairs={{0,2},{2,0},{4,6},{6,4},{8,10},{10,8},{12,14},{14,12},{1,3},{3,1},... | collective-permute-start | bytes 393224 | tf_op jit(solution)/shard_map/ppermute | solution.py:112
  25.8 5.8 %collective-permute-start.12 = (bf16[16,4096]{1,0:T(8,128)(2,1)S(1)}, bf16[16,4096]{1,0:T(8,128)(2,1)S(1)}, u32[]{:S(2)}, u32[]{:S(2)}) collective-permute-start(bf16[16,4096]{1,0:T(8,128)(2,1)S(1)} %get-tuple-element.29), channel_id=1, source_target_pairs={{0,4},{2,6},{4,0},{6,2},{8,12},{10,14},{12,8},{14,10},{1,5},{3,7},... | collective-permute-start | bytes 393224 | tf_op jit(solution)/shard_map/ppermute | solution.py:112
  26.8 10.4 %collective-permute-start.10 = (bf16[16,4096]{1,0:T(8,128)(2,1)S(1)}, bf16[16,4096]{1,0:T(8,128)(2,1)S(1)}, u32[]{:S(2)}, u32[]{:S(2)}) collective-permute-start(bf16[16,4096]{1,0:T(8,128)(2,1)S(1)} %get-tuple-element.26), channel_id=1, source_target_pairs={{0,2},{2,0},{4,6},{6,4},{8,10},{10,8},{12,14},{14,12},{1,3},{3,1},... | collective-permute-start | bytes 393224 | tf_op jit(solution)/shard_map/ppermute | solution.py:112
  27.4 10.8 %collective-permute-start.9 = (bf16[16,4096]{1,0:T(8,128)(2,1)S(1)}, bf16[16,4096]{1,0:T(8,128)(2,1)S(1)}, u32[]{:S(2)}, u32[]{:S(2)}) collective-permute-start(bf16[16,4096]{1,0:T(8,128)(2,1)S(1)} %get-tuple-element.24), channel_id=1, source_target_pairs={{0,14},{2,12},{4,10},{6,8},{8,6},{10,4},{12,2},{14,0},{1,15},{3,13... | collective-permute-start | bytes 393224 | tf_op jit(solution)/shard_map/ppermute | solution.py:112
  31.6 10.6 %collective-permute-start.13 = (bf16[16,4096]{1,0:T(8,128)(2,1)S(1)}, bf16[16,4096]{1,0:T(8,128)(2,1)S(1)}, u32[]{:S(2)}, u32[]{:S(2)}) collective-permute-start(bf16[16,4096]{1,0:T(8,128)(2,1)S(1)} %add.4.refs_1_), channel_id=1, source_target_pairs={{0,8},{2,10},{4,12},{6,14},{8,0},{10,2},{12,4},{14,6},{1,9},{3,11}... | collective-permute-start | bytes 393224 | tf_op jit(solution)/shard_map/ppermute | solution.py:112
  36.7 5.5 %collective-permute-start.15 = (bf16[16,4096]{1,0:T(8,128)(2,1)S(1)}, bf16[16,4096]{1,0:T(8,128)(2,1)S(1)}, u32[]{:S(2)}, u32[]{:S(2)}) collective-permute-start(bf16[16,4096]{1,0:T(8,128)(2,1)S(1)} %get-tuple-element.32), channel_id=1, source_target_pairs={{0,2},{2,0},{4,6},{6,4},{8,10},{10,8},{12,14},{14,12},{1,3},{3,1},... | collective-permute-start | bytes 393224 | tf_op jit(solution)/shard_map/ppermute | solution.py:112
  37.2 6.3 %collective-permute-start.14 = (bf16[16,4096]{1,0:T(8,128)(2,1)S(1)}, bf16[16,4096]{1,0:T(8,128)(2,1)S(1)}, u32[]{:S(2)}, u32[]{:S(2)}) collective-permute-start(bf16[16,4096]{1,0:T(8,128)(2,1)S(1)} %add.5.refs_1_), channel_id=1, source_target_pairs={{0,4},{2,6},{4,0},{6,2},{8,12},{10,14},{12,8},{14,10},{1,5},{3,7},... | collective-permute-start | bytes 393224 | tf_op jit(solution)/shard_map/ppermute | solution.py:112

commit v27 on v26

--- a/solution.py
+++ b/solution.py
@@ -124,7 +124,7 @@
         gate_held = fetch(gate_weight, 48, 2000000000)
         up_held = fetch(up_weight, 48, 2000000000)
         own, gate_held = lax.optimization_barrier((tokens, gate_held))
-        block[3] = swap(own, 3)
+        block[3] = swap(block[2], 1)
         for far in fars:
             block[far + 3] = swap(own, far + 3)
         *crossed, gate_held = lax.optimization_barrier([block[far] for far in fars] + [gate_held])

time: 44.3 us -> 44.3 us (level)
  starting transfers between devices: 25.1 us -> 23.5 us
  waiting for transfers between devices: 11.6 us -> 13.2 us
    ppermute x14, starting transfers between devices: 24.5 us -> 22.9 us  [swap(): return lax.ppermute(value, 'wide', [(i, i ^ bits) for i in range(wide)])]
    ppermute x14, waiting for transfers between devices: 10.4 us -> 12 us  [swap(): return lax.ppermute(value, 'wide', [(i, i ^ bits) for i in range(wide)])]
  transfers between devices with their start and end apart: 16 -> 16, of which waited for: 8 -> 7; matrix products, arithmetic and copies ran while one was open for 0% -> 0% of each run, Pallas kernels for 12% -> 12%
where the time goes in v27:
time: 44.3 us; the launch traced here: 44.2 us
  starting transfers between devices  23.5 us (53%)
  waiting for transfers between devices  13.2 us (30%)
  Pallas kernels  7.4 us (17%)
    ppermute x14, starting transfers between devices, swap(): return lax.ppermute(value, 'wide', [(i, i ^ bits) for i in range(wide)])  22.9 us
    ppermute x14, waiting for transfers between devices, swap(): return lax.ppermute(value, 'wide', [(i, i ^ bits) for i in range(wide)])  12 us
    pallas_call x2, Pallas kernels, fetch(): pl.pallas_call(functools.partial(fetch_kernel, pieces), in_specs=[pl.Bloc...  4.43 us
    pallas_call x3, Pallas kernels, call(): pl.pallas_call(kernel, out_shape=out_shape, compiler_params=pltpu.Compile...  2.17 us
    ppermute x2, waiting for transfers between devices, across_cores(): lax.ppermute(value, 'narrow', [(i, (i + 1) % narrow) for i in range(narro...  1.16 us
  transfers between devices with their start and end apart: 16, of which 7 were waited for; matrix products, arithmetic and copies ran while one was open for 0% of the time, Pallas kernels for 12%

profile of v27, /device:TPU:0, one launch (start us, length us, event | category | flops | bytes accessed | tf_op | source)
XLA Modules:
  0.0 44.2 jit_solution(16440417362742249063)
XLA Ops:
  0.0 0.0 copy-start.1
  0.0 4.0 %collective-permute-start.3 = (bf16[16,4096]{1,0:T(8,128)(2,1)}, bf16[16,4096]{1,0:T(8,128)(2,1)S(1)}, u32[]{:S(2)}, u32[]{:S(2)}) collective-permute-start(bf16[16,4096]{1,0:T(8,128)(2,1)} %refs_0_.3), channel_id=1, source_target_pairs={{0,8},{2,10},{4,12},{6,14},{8,0},{10,2},{12,4},{14,6},{1,9},{3,11}... | collective-permute-start | bytes 393224 | tf_op jit(solution)/shard_map/ppermute | solution.py:112
  4.0 1.5 %collective-permute-start.2 = (bf16[16,4096]{1,0:T(8,128)(2,1)}, bf16[16,4096]{1,0:T(8,128)(2,1)S(1)}, u32[]{:S(2)}, u32[]{:S(2)}) collective-permute-start(bf16[16,4096]{1,0:T(8,128)(2,1)} %refs_0_.3), channel_id=1, source_target_pairs={{0,2},{2,0},{4,6},{6,4},{8,10},{10,8},{12,14},{14,12},{1,3},{3,1},... | collective-permute-start | bytes 393224 | tf_op jit(solution)/shard_map/ppermute | solution.py:112
  5.6 1.6 %collective-permute-start = (bf16[16,4096]{1,0:T(8,128)(2,1)}, bf16[16,4096]{1,0:T(8,128)(2,1)S(1)}, u32[]{:S(2)}, u32[]{:S(2)}) collective-permute-start(bf16[16,4096]{1,0:T(8,128)(2,1)} %refs_0_.3), channel_id=1, source_target_pairs={{0,4},{2,6},{4,0},{6,2},{8,12},{10,14},{12,8},{14,10},{1,5},{3,7},... | collective-permute-start | bytes 393224 | tf_op jit(solution)/shard_map/ppermute | solution.py:112
  7.1 2.2 %fetch.2.refs_8_ = bf16[4096,512]{1,0:T(8,128)(2,1)S(1)} custom-call(bf16[4096,512]{1,0:T(8,128)(2,1)} %source.2), custom_call_target="tpu_custom_call" | custom-call | flops 2000000000 | tf_op jit(solution)/shard_map/fetch/pallas_call | solution.py:37
  9.4 0.0 copy-done.1
  9.4 0.1 collective-permute-start.6
  9.4 1.3 %collective-permute-done.3.refs_4_ = bf16[16,4096]{1,0:T(8,128)(2,1)S(1)} collective-permute-done((bf16[16,4096]{1,0:T(8,128)(2,1)}, bf16[16,4096]{1,0:T(8,128)(2,1)S(1)}, u32[]{:S(2)}, u32[]{:S(2)}) %collective-permute-start.3) | collective-permute-done | bytes 131104 | tf_op jit(solution)/shard_map/ppermute | solution.py:112
  10.7 1.5 %collective-permute-start.5 = (bf16[16,4096]{1,0:T(8,128)(2,1)S(1)}, bf16[16,4096]{1,0:T(8,128)(2,1)S(1)}, u32[]{:S(2)}, u32[]{:S(2)}) collective-permute-start(bf16[16,4096]{1,0:T(8,128)(2,1)S(1)} %collective-permute-done.3.refs_4_), channel_id=1, source_target_pairs={{0,2},{2,0},{4,6},{6,4},{8,10},{10,8},{12,14},{14,12},{1,3},{3,1},... | collective-permute-start | bytes 393224 | tf_op jit(solution)/shard_map/ppermute | solution.py:112
  12.2 1.5 %collective-permute-start.4 = (bf16[16,4096]{1,0:T(8,128)(2,1)S(1)}, bf16[16,4096]{1,0:T(8,128)(2,1)S(1)}, u32[]{:S(2)}, u32[]{:S(2)}) collective-permute-start(bf16[16,4096]{1,0:T(8,128)(2,1)S(1)} %collective-permute-done.3.refs_4_), channel_id=1, source_target_pairs={{0,4},{2,6},{4,0},{6,2},{8,12},{10,14},{12,8},{14,10},{1,5},{3,7},... | collective-permute-start | bytes 393224 | tf_op jit(solution)/shard_map/ppermute | solution.py:112
  13.8 0.0 collective-permute-done.refs_3_
  13.8 0.6 %collective-permute-start.1 = (bf16[16,4096]{1,0:T(8,128)(2,1)S(1)}, bf16[16,4096]{1,0:T(8,128)(2,1)S(1)}, u32[]{:S(2)}, u32[]{:S(2)}) collective-permute-start(bf16[16,4096]{1,0:T(8,128)(2,1)S(1)} %collective-permute-done.refs_3_), channel_id=1, source_target_pairs={{0,2},{2,0},{4,6},{6,4},{8,10},{10,8},{12,14},{14,12},{1,3},{3,1},... | collective-permute-start | bytes 393224 | tf_op jit(solution)/shard_map/ppermute | solution.py:112
  14.4 2.2 %fetch.3.refs_8_ = bf16[4096,512]{1,0:T(8,128)(2,1)S(1)} custom-call(bf16[4096,512]{1,0:T(8,128)(2,1)} %source.3), custom_call_target="tpu_custom_call" | custom-call | flops 2000000000 | tf_op jit(solution)/shard_map/fetch/pallas_call | solution.py:37
  16.7 0.0 copy-start
  16.7 0.0 collective-permute-done.2.refs_2_
  16.7 0.6 %collective-permute-done.6.refs_7_ = bf16[16,4096]{1,0:T(8,128)(2,1)S(1)} collective-permute-done((bf16[16,4096]{1,0:T(8,128)(2,1)S(1)}, bf16[16,4096]{1,0:T(8,128)(2,1)S(1)}, u32[]{:S(2)}, u32[]{:S(2)}) %collective-permute-start.6) | collective-permute-done | bytes 131104 | tf_op jit(solution)/shard_map/ppermute | solution.py:112
  17.3 3.5 %collective-permute-done.1.refs_1_ = bf16[16,4096]{1,0:T(8,128)(2,1)S(1)} collective-permute-done((bf16[16,4096]{1,0:T(8,128)(2,1)S(1)}, bf16[16,4096]{1,0:T(8,128)(2,1)S(1)}, u32[]{:S(2)}, u32[]{:S(2)}) %collective-permute-start.1) | collective-permute-done | bytes 131104 | tf_op jit(solution)/shard_map/ppermute | solution.py:112
  20.9 0.0 collective-permute-done.5.refs_6_
  20.9 0.0 collective-permute-done.4.refs_5_
  20.9 0.7 %project.2.gate_ref = f32[128,512]{1,0:T(8,128)S(1)} custom-call(bf16[16,4096]{1,0:T(8,128)(2,1)S(1)} %copy-done.1, bf16[16,4096]{1,0:T(8,128)(2,1)S(1)} %collective-permute-done.1.refs_1_, bf16[16,4096]{1,0:T(8,128)(2,1)S(1)} %collective-permute-done.2.refs_2_, bf16[16,4096]{1,0:T(8,128)(2,1)S(1)} %collective-permute-done.refs_3_, ...), custom_call_target="tpu_custom_call" | custom-call | flops 400000000 | tf_op jit(solution)/shard_map/project/pallas_call | solution.py:15
  21.6 0.1 collective-permute-start.7
  21.7 0.7 %project.3.up_ref = f32[128,512]{1,0:T(8,128)S(1)} custom-call(bf16[16,4096]{1,0:T(8,128)(2,1)S(1)} %copy-done.1, bf16[16,4096]{1,0:T(8,128)(2,1)S(1)} %collective-permute-done.1.refs_1_, bf16[16,4096]{1,0:T(8,128)(2,1)S(1)} %collective-permute-done.2.refs_2_, bf16[16,4096]{1,0:T(8,128)(2,1)S(1)} %collective-permute-done.refs_3_, ...), custom_call_target="tpu_custom_call" | custom-call | flops 400000000 | tf_op jit(solution)/shard_map/project/pallas_call | solution.py:15
  22.4 0.6 %collective-permute-start.8 = (f32[128,512]{1,0:T(8,128)S(1)}, f32[128,512]{1,0:T(8,128)S(1)}, u32[]{:S(2)}, u32[]{:S(2)}) collective-permute-start(f32[128,512]{1,0:T(8,128)S(1)} %project.3.up_ref), channel_id=1, source_target_pairs={{0,1},{1,0},{2,3},{3,2},{4,5},{5,4},{6,7},{7,6},{8,9},{9,8},{10,11... | collective-permute-start | bytes 786440 | tf_op jit(solution)/shard_map/ppermute | solution.py:115
  22.9 0.2 collective-permute-done.7.gate_other_ref
  23.2 0.9 %collective-permute-done.8.up_other_ref = f32[128,512]{1,0:T(8,128)S(1)} collective-permute-done((f32[128,512]{1,0:T(8,128)S(1)}, f32[128,512]{1,0:T(8,128)S(1)}, u32[]{:S(2)}, u32[]{:S(2)}) %collective-permute-start.8) | collective-permute-done | bytes 262176 | tf_op jit(solution)/shard_map/ppermute | solution.py:115
  24.1 0.0 copy-done
  24.1 0.7 %down.1 = (f32[16,4096]{1,0:T(8,128)S(1)}, bf16[16,4096]{1,0:T(8,128)(2,1)S(1)}, bf16[16,4096]{1,0:T(8,128)(2,1)S(1)}, f32[16,4096]{1,0:T(8,128)S(1)}, f32[16,40...) custom-call(f32[128,512]{1,0:T(8,128)S(1)} %project.2.gate_ref, ...), custom_call_target="tpu_custom_call" | custom-call | flops 536870912 | tf_op jit(solution)/shard_map/down/pallas_call | solution.py:15
  24.9 0.9 %collective-permute-start.11 = (bf16[16,4096]{1,0:T(8,128)(2,1)S(1)}, bf16[16,4096]{1,0:T(8,128)(2,1)S(1)}, u32[]{:S(2)}, u32[]{:S(2)}) collective-permute-start(bf16[16,4096]{1,0:T(8,128)(2,1)S(1)} %get-tuple-element.28), channel_id=1, source_target_pairs={{0,2},{2,0},{4,6},{6,4},{8,10},{10,8},{12,14},{14,12},{1,3},{3,1},... | collective-permute-start | bytes 393224 | tf_op jit(solution)/shard_map/ppermute | solution.py:112
  25.8 1.2 %collective-permute-start.12 = (bf16[16,4096]{1,0:T(8,128)(2,1)S(1)}, bf16[16,4096]{1,0:T(8,128)(2,1)S(1)}, u32[]{:S(2)}, u32[]{:S(2)}) collective-permute-start(bf16[16,4096]{1,0:T(8,128)(2,1)S(1)} %get-tuple-element.29), channel_id=1, source_target_pairs={{0,4},{2,6},{4,0},{6,2},{8,12},{10,14},{12,8},{14,10},{1,5},{3,7},... | collective-permute-start | bytes 393224 | tf_op jit(solution)/shard_map/ppermute | solution.py:112
  27.0 0.7 %collective-permute-start.10 = (bf16[16,4096]{1,0:T(8,128)(2,1)S(1)}, bf16[16,4096]{1,0:T(8,128)(2,1)S(1)}, u32[]{:S(2)}, u32[]{:S(2)}) collective-permute-start(bf16[16,4096]{1,0:T(8,128)(2,1)S(1)} %get-tuple-element.26), channel_id=1, source_target_pairs={{0,2},{2,0},{4,6},{6,4},{8,10},{10,8},{12,14},{14,12},{1,3},{3,1},... | collective-permute-start | bytes 393224 | tf_op jit(solution)/shard_map/ppermute | solution.py:112
  27.7 3.9 %collective-permute-start.9 = (bf16[16,4096]{1,0:T(8,128)(2,1)S(1)}, bf16[16,4096]{1,0:T(8,128)(2,1)S(1)}, u32[]{:S(2)}, u32[]{:S(2)}) collective-permute-start(bf16[16,4096]{1,0:T(8,128)(2,1)S(1)} %get-tuple-element.24), channel_id=1, source_target_pairs={{0,14},{2,12},{4,10},{6,8},{8,6},{10,4},{12,2},{14,0},{1,15},{3,13... | collective-permute-start | bytes 393224 | tf_op jit(solution)/shard_map/ppermute | solution.py:112
  31.6 0.0 collective-permute-done.11.refs_0_
  31.6 0.0 collective-permute-done.12.refs_1_
  31.7 3.5 %collective-permute-start.13 = (bf16[16,4096]{1,0:T(8,128)(2,1)S(1)}, bf16[16,4096]{1,0:T(8,128)(2,1)S(1)}, u32[]{:S(2)}, u32[]{:S(2)}) collective-permute-start(bf16[16,4096]{1,0:T(8,128)(2,1)S(1)} %add.4.refs_1_), channel_id=1, source_target_pairs={{0,8},{2,10},{4,12},{6,14},{8,0},{10,2},{12,4},{14,6},{1,9},{3,11}... | collective-permute-start | bytes 393224 | tf_op jit(solution)/shard_map/ppermute | solution.py:112
  35.2 1.7 %collective-permute-start.15 = (bf16[16,4096]{1,0:T(8,128)(2,1)S(1)}, bf16[16,4096]{1,0:T(8,128)(2,1)S(1)}, u32[]{:S(2)}, u32[]{:S(2)}) collective-permute-start(bf16[16,4096]{1,0:T(8,128)(2,1)S(1)} %get-tuple-element.32), channel_id=1, source_target_pairs={{0,2},{2,0},{4,6},{6,4},{8,10},{10,8},{12,14},{14,12},{1,3},{3,1},... | collective-permute-start | bytes 393224 | tf_op jit(solution)/shard_map/ppermute | solution.py:112
  36.8 0.0 collective-permute-done.10.refs_0_
  36.8 0.1 collective-permute-start.14
  36.9 0.0 collective-permute-done.9.refs_0_
  37.0 5.2 %collective-permute-done.13.refs_0_ = bf16[16,4096]{1,0:T(8,128)(2,1)S(1)} collective-permute-done((bf16[16,4096]{1,0:T(8,128)(2,1)S(1)}, bf16[16,4096]{1,0:T(8,128)(2,1)S(1)}, u32[]{:S(2)}, u32[]{:S(2)}) %collective-permute-start.13) | collective-permute-done | bytes 131104 | tf_op jit(solution)/shard_map/ppermute | solution.py:112
  42.2 0.0 collective-permute-done.15.refs_2_
  42.2 1.3 %collective-permute-done.14.refs_1_ = bf16[16,4096]{1,0:T(8,128)(2,1)S(1)} collective-permute-done((bf16[16,4096]{1,0:T(8,128)(2,1)S(1)}, bf16[16,4096]{1,0:T(8,128)(2,1)S(1)}, u32[]{:S(2)}, u32[]{:S(2)}) %collective-permute-start.14) | collective-permute-done | bytes 131104 | tf_op jit(solution)/shard_map/ppermute | solution.py:112
  43.5 0.7 %add.7 = bf16[16,4096]{1,0:T(8,128)(2,1)} custom-call(f32[16,4096]{1,0:T(8,128)S(1)} %add.6.own_ref, bf16[16,4096]{1,0:T(8,128)(2,1)S(1)} %collective-permute-done.13.refs_0_, bf16[16,4096]{1,0:T(8,128)(2,1)S(1)} %collective-permute-done.14.refs_1_, bf16[16,4096]{1,0:T(8,128)(2,1)S(1)} %collective-permute-done.15.refs_2_), custom_call_target="tpu_custom_call" | custom-call | flops 1000000 | tf_op jit(solution)/shard_map/add/pallas_call | solution.py:97
  (3 shorter events, 0.1 us)
Async XLA Ops:
  0.0 9.4 %copy-start.1 = (bf16[16,4096]{1,0:T(8,128)(2,1)S(1)}, bf16[16,4096]{1,0:T(8,128)(2,1)}, u32[]{:S(2)}) copy-start(bf16[16,4096]{1,0:T(8,128)(2,1)} %refs_0_.3) | copy-start | bytes 393220
  0.0 10.7 %collective-permute-start.3 = (bf16[16,4096]{1,0:T(8,128)(2,1)}, bf16[16,4096]{1,0:T(8,128)(2,1)S(1)}, u32[]{:S(2)}, u32[]{:S(2)}) collective-permute-start(bf16[16,4096]{1,0:T(8,128)(2,1)} %refs_0_.3), channel_id=1, source_target_pairs={{0,8},{2,10},{4,12},{6,14},{8,0},{10,2},{12,4},{14,6},{1,9},{3,11}... | collective-permute-start | bytes 393224 | tf_op jit(solution)/shard_map/ppermute | solution.py:112
  4.0 12.6 %collective-permute-start.2 = (bf16[16,4096]{1,0:T(8,128)(2,1)}, bf16[16,4096]{1,0:T(8,128)(2,1)S(1)}, u32[]{:S(2)}, u32[]{:S(2)}) collective-permute-start(bf16[16,4096]{1,0:T(8,128)(2,1)} %refs_0_.3), channel_id=1, source_target_pairs={{0,2},{2,0},{4,6},{6,4},{8,10},{10,8},{12,14},{14,12},{1,3},{3,1},... | collective-permute-start | bytes 393224 | tf_op jit(solution)/shard_map/ppermute | solution.py:112
  5.6 8.2 %collective-permute-start = (bf16[16,4096]{1,0:T(8,128)(2,1)}, bf16[16,4096]{1,0:T(8,128)(2,1)S(1)}, u32[]{:S(2)}, u32[]{:S(2)}) collective-permute-start(bf16[16,4096]{1,0:T(8,128)(2,1)} %refs_0_.3), channel_id=1, source_target_pairs={{0,4},{2,6},{4,0},{6,2},{8,12},{10,14},{12,8},{14,10},{1,5},{3,7},... | collective-permute-start | bytes 393224 | tf_op jit(solution)/shard_map/ppermute | solution.py:112
  9.4 7.9 %collective-permute-start.6 = (bf16[16,4096]{1,0:T(8,128)(2,1)S(1)}, bf16[16,4096]{1,0:T(8,128)(2,1)S(1)}, u32[]{:S(2)}, u32[]{:S(2)}) collective-permute-start(bf16[16,4096]{1,0:T(8,128)(2,1)S(1)} %copy-done.1), channel_id=1, source_target_pairs={{0,14},{2,12},{4,10},{6,8},{8,6},{10,4},{12,2},{14,0},{1,15},{3,13... | collective-permute-start | bytes 393224 | tf_op jit(solution)/shard_map/ppermute | solution.py:112
  10.7 10.1 %collective-permute-start.5 = (bf16[16,4096]{1,0:T(8,128)(2,1)S(1)}, bf16[16,4096]{1,0:T(8,128)(2,1)S(1)}, u32[]{:S(2)}, u32[]{:S(2)}) collective-permute-start(bf16[16,4096]{1,0:T(8,128)(2,1)S(1)} %collective-permute-done.3.refs_4_), channel_id=1, source_target_pairs={{0,2},{2,0},{4,6},{6,4},{8,10},{10,8},{12,14},{14,12},{1,3},{3,1},... | collective-permute-start | bytes 393224 | tf_op jit(solution)/shard_map/ppermute | solution.py:112
  12.2 8.6 %collective-permute-start.4 = (bf16[16,4096]{1,0:T(8,128)(2,1)S(1)}, bf16[16,4096]{1,0:T(8,128)(2,1)S(1)}, u32[]{:S(2)}, u32[]{:S(2)}) collective-permute-start(bf16[16,4096]{1,0:T(8,128)(2,1)S(1)} %collective-permute-done.3.refs_4_), channel_id=1, source_target_pairs={{0,4},{2,6},{4,0},{6,2},{8,12},{10,14},{12,8},{14,10},{1,5},{3,7},... | collective-permute-start | bytes 393224 | tf_op jit(solution)/shard_map/ppermute | solution.py:112
  13.8 7.1 %collective-permute-start.1 = (bf16[16,4096]{1,0:T(8,128)(2,1)S(1)}, bf16[16,4096]{1,0:T(8,128)(2,1)S(1)}, u32[]{:S(2)}, u32[]{:S(2)}) collective-permute-start(bf16[16,4096]{1,0:T(8,128)(2,1)S(1)} %collective-permute-done.refs_3_), channel_id=1, source_target_pairs={{0,2},{2,0},{4,6},{6,4},{8,10},{10,8},{12,14},{14,12},{1,3},{3,1},... | collective-permute-start | bytes 393224 | tf_op jit(solution)/shard_map/ppermute | solution.py:112
  16.7 7.5 %copy-start = (bf16[512,4096]{1,0:T(8,128)(2,1)S(1)}, bf16[512,4096]{1,0:T(8,128)(2,1)}, u32[]{:S(2)}) copy-start(bf16[512,4096]{1,0:T(8,128)(2,1)} %weight_ref.1) | copy-start | bytes 12582916
  21.6 1.6 %collective-permute-start.7 = (f32[128,512]{1,0:T(8,128)S(1)}, f32[128,512]{1,0:T(8,128)S(1)}, u32[]{:S(2)}, u32[]{:S(2)}) collective-permute-start(f32[128,512]{1,0:T(8,128)S(1)} %project.2.gate_ref), channel_id=1, source_target_pairs={{0,1},{1,0},{2,3},{3,2},{4,5},{5,4},{6,7},{7,6},{8,9},{9,8},{10,11... | collective-permute-start | bytes 786440 | tf_op jit(solution)/shard_map/ppermute | solution.py:115
  22.4 1.7 %collective-permute-start.8 = (f32[128,512]{1,0:T(8,128)S(1)}, f32[128,512]{1,0:T(8,128)S(1)}, u32[]{:S(2)}, u32[]{:S(2)}) collective-permute-start(f32[128,512]{1,0:T(8,128)S(1)} %project.3.up_ref), channel_id=1, source_target_pairs={{0,1},{1,0},{2,3},{3,2},{4,5},{5,4},{6,7},{7,6},{8,9},{9,8},{10,11... | collective-permute-start | bytes 786440 | tf_op jit(solution)/shard_map/ppermute | solution.py:115
  24.9 6.8 %collective-permute-start.11 = (bf16[16,4096]{1,0:T(8,128)(2,1)S(1)}, bf16[16,4096]{1,0:T(8,128)(2,1)S(1)}, u32[]{:S(2)}, u32[]{:S(2)}) collective-permute-start(bf16[16,4096]{1,0:T(8,128)(2,1)S(1)} %get-tuple-element.28), channel_id=1, source_target_pairs={{0,2},{2,0},{4,6},{6,4},{8,10},{10,8},{12,14},{14,12},{1,3},{3,1},... | collective-permute-start | bytes 393224 | tf_op jit(solution)/shard_map/ppermute | solution.py:112
  25.8 5.9 %collective-permute-start.12 = (bf16[16,4096]{1,0:T(8,128)(2,1)S(1)}, bf16[16,4096]{1,0:T(8,128)(2,1)S(1)}, u32[]{:S(2)}, u32[]{:S(2)}) collective-permute-start(bf16[16,4096]{1,0:T(8,128)(2,1)S(1)} %get-tuple-element.29), channel_id=1, source_target_pairs={{0,4},{2,6},{4,0},{6,2},{8,12},{10,14},{12,8},{14,10},{1,5},{3,7},... | collective-permute-start | bytes 393224 | tf_op jit(solution)/shard_map/ppermute | solution.py:112
  27.0 9.9 %collective-permute-start.10 = (bf16[16,4096]{1,0:T(8,128)(2,1)S(1)}, bf16[16,4096]{1,0:T(8,128)(2,1)S(1)}, u32[]{:S(2)}, u32[]{:S(2)}) collective-permute-start(bf16[16,4096]{1,0:T(8,128)(2,1)S(1)} %get-tuple-element.26), channel_id=1, source_target_pairs={{0,2},{2,0},{4,6},{6,4},{8,10},{10,8},{12,14},{14,12},{1,3},{3,1},... | collective-permute-start | bytes 393224 | tf_op jit(solution)/shard_map/ppermute | solution.py:112
  27.7 9.3 %collective-permute-start.9 = (bf16[16,4096]{1,0:T(8,128)(2,1)S(1)}, bf16[16,4096]{1,0:T(8,128)(2,1)S(1)}, u32[]{:S(2)}, u32[]{:S(2)}) collective-permute-start(bf16[16,4096]{1,0:T(8,128)(2,1)S(1)} %get-tuple-element.24), channel_id=1, source_target_pairs={{0,14},{2,12},{4,10},{6,8},{8,6},{10,4},{12,2},{14,0},{1,15},{3,13... | collective-permute-start | bytes 393224 | tf_op jit(solution)/shard_map/ppermute | solution.py:112
  31.7 10.5 %collective-permute-start.13 = (bf16[16,4096]{1,0:T(8,128)(2,1)S(1)}, bf16[16,4096]{1,0:T(8,128)(2,1)S(1)}, u32[]{:S(2)}, u32[]{:S(2)}) collective-permute-start(bf16[16,4096]{1,0:T(8,128)(2,1)S(1)} %add.4.refs_1_), channel_id=1, source_target_pairs={{0,8},{2,10},{4,12},{6,14},{8,0},{10,2},{12,4},{14,6},{1,9},{3,11}... | collective-permute-start | bytes 393224 | tf_op jit(solution)/shard_map/ppermute | solution.py:112
  35.2 7.0 %collective-permute-start.15 = (bf16[16,4096]{1,0:T(8,128)(2,1)S(1)}, bf16[16,4096]{1,0:T(8,128)(2,1)S(1)}, u32[]{:S(2)}, u32[]{:S(2)}) collective-permute-start(bf16[16,4096]{1,0:T(8,128)(2,1)S(1)} %get-tuple-element.32), channel_id=1, source_target_pairs={{0,2},{2,0},{4,6},{6,4},{8,10},{10,8},{12,14},{14,12},{1,3},{3,1},... | collective-permute-start | bytes 393224 | tf_op jit(solution)/shard_map/ppermute | solution.py:112
  36.8 6.6 %collective-permute-start.14 = (bf16[16,4096]{1,0:T(8,128)(2,1)S(1)}, bf16[16,4096]{1,0:T(8,128)(2,1)S(1)}, u32[]{:S(2)}, u32[]{:S(2)}) collective-permute-start(bf16[16,4096]{1,0:T(8,128)(2,1)S(1)} %add.5.refs_1_), channel_id=1, source_target_pairs={{0,4},{2,6},{4,0},{6,2},{8,12},{10,14},{12,8},{14,10},{1,5},{3,7},... | collective-permute-start | bytes 393224 | tf_op jit(solution)/shard_map/ppermute | solution.py:112

commit v28 on v25

--- a/solution.py
+++ b/solution.py
@@ -144,7 +144,7 @@
         for far in fars:
             sums.append(add(part[far], [swap(part[far + near], near) for near in (1, 2)], BF16))
             direct.append(swap(part[far + 3], far + 3))
-        pair = add(part[2], [swap(part[3], 1)], BF16, after=sums)
+        pair = add(part[2], [swap(part[3], 1)], BF16)
         part[1], sums[0] = lax.optimization_barrier((part[1], sums[0]))
         arrived = [swap(value, far) for value, far in zip(sums, fars)]
         total = add(part[0], direct, F32, 1500000000, after=[pair])

time: 43.6 us -> 43.8 us (level)
  starting transfers between devices: 20.9 us -> 23.7 us
  waiting for transfers between devices: 15 us -> 12.5 us
    ppermute x14, starting transfers between devices: 20.2 us -> 23 us  [swap(): return lax.ppermute(value, 'wide', [(i, i ^ bits) for i in range(wide)])]
    ppermute x14, waiting for transfers between devices: 13.9 us -> 11.4 us  [swap(): return lax.ppermute(value, 'wide', [(i, i ^ bits) for i in range(wide)])]
  transfers between devices with their start and end apart: 16 -> 16, of which waited for: 9 -> 8; matrix products, arithmetic and copies ran while one was open for 0% -> 0% of each run, Pallas kernels for 12% -> 12%
where the time goes in v28:
time: 43.8 us; the launch traced here: 43.7 us
  starting transfers between devices  23.7 us (54%)
  waiting for transfers between devices  12.5 us (29%)
  Pallas kernels  7.4 us (17%)
    ppermute x14, starting transfers between devices, swap(): return lax.ppermute(value, 'wide', [(i, i ^ bits) for i in range(wide)])  23 us
    ppermute x14, waiting for transfers between devices, swap(): return lax.ppermute(value, 'wide', [(i, i ^ bits) for i in range(wide)])  11.4 us
    pallas_call x2, Pallas kernels, fetch(): pl.pallas_call(functools.partial(fetch_kernel, pieces), in_specs=[pl.Bloc...  4.43 us
    pallas_call x3, Pallas kernels, call(): pl.pallas_call(kernel, out_shape=out_shape, compiler_params=pltpu.Compile...  2.16 us
    ppermute x2, waiting for transfers between devices, across_cores(): lax.ppermute(value, 'narrow', [(i, (i + 1) % narrow) for i in range(narro...  1.16 us
  transfers between devices with their start and end apart: 16, of which 8 were waited for; matrix products, arithmetic and copies ran while one was open for 0% of the time, Pallas kernels for 12%

profile of v28, /device:TPU:0, one launch (start us, length us, event | category | flops | bytes accessed | tf_op | source)
XLA Modules:
  0.0 43.7 jit_solution(4925411623621983688)
XLA Ops:
  0.0 0.0 copy-start.1
  0.0 4.0 %collective-permute-start.3 = (bf16[16,4096]{1,0:T(8,128)(2,1)}, bf16[16,4096]{1,0:T(8,128)(2,1)S(1)}, u32[]{:S(2)}, u32[]{:S(2)}) collective-permute-start(bf16[16,4096]{1,0:T(8,128)(2,1)} %refs_0_.3), channel_id=1, source_target_pairs={{0,8},{2,10},{4,12},{6,14},{8,0},{10,2},{12,4},{14,6},{1,9},{3,11}... | collective-permute-start | bytes 393224 | tf_op jit(solution)/shard_map/ppermute | solution.py:112
  4.0 1.6 %collective-permute-start.2 = (bf16[16,4096]{1,0:T(8,128)(2,1)}, bf16[16,4096]{1,0:T(8,128)(2,1)S(1)}, u32[]{:S(2)}, u32[]{:S(2)}) collective-permute-start(bf16[16,4096]{1,0:T(8,128)(2,1)} %refs_0_.3), channel_id=1, source_target_pairs={{0,4},{2,6},{4,0},{6,2},{8,12},{10,14},{12,8},{14,10},{1,5},{3,7},... | collective-permute-start | bytes 393224 | tf_op jit(solution)/shard_map/ppermute | solution.py:112
  5.6 1.5 %collective-permute-start.1 = (bf16[16,4096]{1,0:T(8,128)(2,1)}, bf16[16,4096]{1,0:T(8,128)(2,1)S(1)}, u32[]{:S(2)}, u32[]{:S(2)}) collective-permute-start(bf16[16,4096]{1,0:T(8,128)(2,1)} %refs_0_.3), channel_id=1, source_target_pairs={{0,2},{2,0},{4,6},{6,4},{8,10},{10,8},{12,14},{14,12},{1,3},{3,1},... | collective-permute-start | bytes 393224 | tf_op jit(solution)/shard_map/ppermute | solution.py:112
  7.1 2.2 %fetch.2.refs_8_ = bf16[4096,512]{1,0:T(8,128)(2,1)S(1)} custom-call(bf16[4096,512]{1,0:T(8,128)(2,1)} %source.2), custom_call_target="tpu_custom_call" | custom-call | flops 2000000000 | tf_op jit(solution)/shard_map/fetch/pallas_call | solution.py:37
  9.4 0.0 copy-done.1
  9.4 0.5 %collective-permute-start = (bf16[16,4096]{1,0:T(8,128)(2,1)S(1)}, bf16[16,4096]{1,0:T(8,128)(2,1)S(1)}, u32[]{:S(2)}, u32[]{:S(2)}) collective-permute-start(bf16[16,4096]{1,0:T(8,128)(2,1)S(1)} %copy-done.1), channel_id=1, source_target_pairs={{0,6},{2,4},{4,2},{6,0},{8,14},{10,12},{12,10},{14,8},{1,7},{3,5},... | collective-permute-start | bytes 393224 | tf_op jit(solution)/shard_map/ppermute | solution.py:112
  9.8 0.9 %collective-permute-done.3.refs_4_ = bf16[16,4096]{1,0:T(8,128)(2,1)S(1)} collective-permute-done((bf16[16,4096]{1,0:T(8,128)(2,1)}, bf16[16,4096]{1,0:T(8,128)(2,1)S(1)}, u32[]{:S(2)}, u32[]{:S(2)}) %collective-permute-start.3) | collective-permute-done | bytes 131104 | tf_op jit(solution)/shard_map/ppermute | solution.py:112
  10.7 1.7 %collective-permute-start.6 = (bf16[16,4096]{1,0:T(8,128)(2,1)S(1)}, bf16[16,4096]{1,0:T(8,128)(2,1)S(1)}, u32[]{:S(2)}, u32[]{:S(2)}) collective-permute-start(bf16[16,4096]{1,0:T(8,128)(2,1)S(1)} %collective-permute-done.3.refs_4_), channel_id=1, source_target_pairs={{0,6},{2,4},{4,2},{6,0},{8,14},{10,12},{12,10},{14,8},{1,7},{3,5},... | collective-permute-start | bytes 393224 | tf_op jit(solution)/shard_map/ppermute | solution.py:112
  12.4 0.5 %collective-permute-start.5 = (bf16[16,4096]{1,0:T(8,128)(2,1)S(1)}, bf16[16,4096]{1,0:T(8,128)(2,1)S(1)}, u32[]{:S(2)}, u32[]{:S(2)}) collective-permute-start(bf16[16,4096]{1,0:T(8,128)(2,1)S(1)} %collective-permute-done.3.refs_4_), channel_id=1, source_target_pairs={{0,2},{2,0},{4,6},{6,4},{8,10},{10,8},{12,14},{14,12},{1,3},{3,1},... | collective-permute-start | bytes 393224 | tf_op jit(solution)/shard_map/ppermute | solution.py:112
  12.9 0.0 collective-permute-done.2.refs_3_
  12.9 1.3 %collective-permute-start.4 = (bf16[16,4096]{1,0:T(8,128)(2,1)S(1)}, bf16[16,4096]{1,0:T(8,128)(2,1)S(1)}, u32[]{:S(2)}, u32[]{:S(2)}) collective-permute-start(bf16[16,4096]{1,0:T(8,128)(2,1)S(1)} %collective-permute-done.3.refs_4_), channel_id=1, source_target_pairs={{0,4},{2,6},{4,0},{6,2},{8,12},{10,14},{12,8},{14,10},{1,5},{3,7},... | collective-permute-start | bytes 393224 | tf_op jit(solution)/shard_map/ppermute | solution.py:112
  14.2 2.2 %fetch.3.refs_8_ = bf16[4096,512]{1,0:T(8,128)(2,1)S(1)} custom-call(bf16[4096,512]{1,0:T(8,128)(2,1)} %source.3), custom_call_target="tpu_custom_call" | custom-call | flops 2000000000 | tf_op jit(solution)/shard_map/fetch/pallas_call | solution.py:37
  16.4 0.0 copy-start
  16.5 0.0 collective-permute-done.1.refs_2_
  16.5 0.0 collective-permute-done.refs_1_
  16.5 2.5 %collective-permute-done.6.refs_7_ = bf16[16,4096]{1,0:T(8,128)(2,1)S(1)} collective-permute-done((bf16[16,4096]{1,0:T(8,128)(2,1)S(1)}, bf16[16,4096]{1,0:T(8,128)(2,1)S(1)}, u32[]{:S(2)}, u32[]{:S(2)}) %collective-permute-start.6) | collective-permute-done | bytes 131104 | tf_op jit(solution)/shard_map/ppermute | solution.py:112
  19.0 1.4 %collective-permute-done.5.refs_6_ = bf16[16,4096]{1,0:T(8,128)(2,1)S(1)} collective-permute-done((bf16[16,4096]{1,0:T(8,128)(2,1)S(1)}, bf16[16,4096]{1,0:T(8,128)(2,1)S(1)}, u32[]{:S(2)}, u32[]{:S(2)}) %collective-permute-start.5) | collective-permute-done | bytes 131104 | tf_op jit(solution)/shard_map/ppermute | solution.py:112
  20.3 0.0 collective-permute-done.4.refs_5_
  20.4 0.7 %project.2.gate_ref = f32[128,512]{1,0:T(8,128)S(1)} custom-call(bf16[16,4096]{1,0:T(8,128)(2,1)S(1)} %copy-done.1, bf16[16,4096]{1,0:T(8,128)(2,1)S(1)} %collective-permute-done.refs_1_, bf16[16,4096]{1,0:T(8,128)(2,1)S(1)} %collective-permute-done.1.refs_2_, bf16[16,4096]{1,0:T(8,128)(2,1)S(1)} %collective-permute-done.2.refs_3_, ...), custom_call_target="tpu_custom_call" | custom-call | flops 400000000 | tf_op jit(solution)/shard_map/project/pallas_call | solution.py:15
  21.1 0.1 collective-permute-start.7
  21.2 0.7 %project.3.up_ref = f32[128,512]{1,0:T(8,128)S(1)} custom-call(bf16[16,4096]{1,0:T(8,128)(2,1)S(1)} %copy-done.1, bf16[16,4096]{1,0:T(8,128)(2,1)S(1)} %collective-permute-done.refs_1_, bf16[16,4096]{1,0:T(8,128)(2,1)S(1)} %collective-permute-done.1.refs_2_, bf16[16,4096]{1,0:T(8,128)(2,1)S(1)} %collective-permute-done.2.refs_3_, ...), custom_call_target="tpu_custom_call" | custom-call | flops 400000000 | tf_op jit(solution)/shard_map/project/pallas_call | solution.py:15
  21.9 0.6 %collective-permute-start.8 = (f32[128,512]{1,0:T(8,128)S(1)}, f32[128,512]{1,0:T(8,128)S(1)}, u32[]{:S(2)}, u32[]{:S(2)}) collective-permute-start(f32[128,512]{1,0:T(8,128)S(1)} %project.3.up_ref), channel_id=1, source_target_pairs={{0,1},{1,0},{2,3},{3,2},{4,5},{5,4},{6,7},{7,6},{8,9},{9,8},{10,11... | collective-permute-start | bytes 786440 | tf_op jit(solution)/shard_map/ppermute | solution.py:115
  22.4 0.2 collective-permute-done.7.gate_other_ref
  22.7 0.9 %collective-permute-done.8.up_other_ref = f32[128,512]{1,0:T(8,128)S(1)} collective-permute-done((f32[128,512]{1,0:T(8,128)S(1)}, f32[128,512]{1,0:T(8,128)S(1)}, u32[]{:S(2)}, u32[]{:S(2)}) %collective-permute-start.8) | collective-permute-done | bytes 262176 | tf_op jit(solution)/shard_map/ppermute | solution.py:115
  23.6 0.0 copy-done
  23.6 0.7 %down.1 = (f32[16,4096]{1,0:T(8,128)S(1)}, bf16[16,4096]{1,0:T(8,128)(2,1)S(1)}, bf16[16,4096]{1,0:T(8,128)(2,1)S(1)}, f32[16,4096]{1,0:T(8,128)S(1)}, f32[16,40...) custom-call(f32[128,512]{1,0:T(8,128)S(1)} %project.2.gate_ref, ...), custom_call_target="tpu_custom_call" | custom-call | flops 536870912 | tf_op jit(solution)/shard_map/down/pallas_call | solution.py:15
  24.3 0.9 %collective-permute-start.10 = (bf16[16,4096]{1,0:T(8,128)(2,1)S(1)}, bf16[16,4096]{1,0:T(8,128)(2,1)S(1)}, u32[]{:S(2)}, u32[]{:S(2)}) collective-permute-start(bf16[16,4096]{1,0:T(8,128)(2,1)S(1)} %get-tuple-element.26), channel_id=1, source_target_pairs={{0,2},{2,0},{4,6},{6,4},{8,10},{10,8},{12,14},{14,12},{1,3},{3,1},... | collective-permute-start | bytes 393224 | tf_op jit(solution)/shard_map/ppermute | solution.py:112
  25.3 1.2 %collective-permute-start.11 = (bf16[16,4096]{1,0:T(8,128)(2,1)S(1)}, bf16[16,4096]{1,0:T(8,128)(2,1)S(1)}, u32[]{:S(2)}, u32[]{:S(2)}) collective-permute-start(bf16[16,4096]{1,0:T(8,128)(2,1)S(1)} %get-tuple-element.29), channel_id=1, source_target_pairs={{0,2},{2,0},{4,6},{6,4},{8,10},{10,8},{12,14},{14,12},{1,3},{3,1},... | collective-permute-start | bytes 393224 | tf_op jit(solution)/shard_map/ppermute | solution.py:112
  26.4 1.3 %collective-permute-start.12 = (bf16[16,4096]{1,0:T(8,128)(2,1)S(1)}, bf16[16,4096]{1,0:T(8,128)(2,1)S(1)}, u32[]{:S(2)}, u32[]{:S(2)}) collective-permute-start(bf16[16,4096]{1,0:T(8,128)(2,1)S(1)} %get-tuple-element.30), channel_id=1, source_target_pairs={{0,4},{2,6},{4,0},{6,2},{8,12},{10,14},{12,8},{14,10},{1,5},{3,7},... | collective-permute-start | bytes 393224 | tf_op jit(solution)/shard_map/ppermute | solution.py:112
  27.8 1.9 %collective-permute-start.9 = (bf16[16,4096]{1,0:T(8,128)(2,1)S(1)}, bf16[16,4096]{1,0:T(8,128)(2,1)S(1)}, u32[]{:S(2)}, u32[]{:S(2)}) collective-permute-start(bf16[16,4096]{1,0:T(8,128)(2,1)S(1)} %get-tuple-element.24), channel_id=1, source_target_pairs={{0,14},{2,12},{4,10},{6,8},{8,6},{10,4},{12,2},{14,0},{1,15},{3,13... | collective-permute-start | bytes 393224 | tf_op jit(solution)/shard_map/ppermute | solution.py:112
  29.7 1.0 %collective-permute-done.10.refs_0_ = bf16[16,4096]{1,0:T(8,128)(2,1)S(1)} collective-permute-done((bf16[16,4096]{1,0:T(8,128)(2,1)S(1)}, bf16[16,4096]{1,0:T(8,128)(2,1)S(1)}, u32[]{:S(2)}, u32[]{:S(2)}) %collective-permute-start.10) | collective-permute-done | bytes 131104 | tf_op jit(solution)/shard_map/ppermute | solution.py:112
  30.8 3.4 %collective-permute-start.14 = (bf16[16,4096]{1,0:T(8,128)(2,1)S(1)}, bf16[16,4096]{1,0:T(8,128)(2,1)S(1)}, u32[]{:S(2)}, u32[]{:S(2)}) collective-permute-start(bf16[16,4096]{1,0:T(8,128)(2,1)S(1)} %add.4.refs_1_), channel_id=1, source_target_pairs={{0,4},{2,6},{4,0},{6,2},{8,12},{10,14},{12,8},{14,10},{1,5},{3,7},... | collective-permute-start | bytes 393224 | tf_op jit(solution)/shard_map/ppermute | solution.py:112
  34.2 0.0 collective-permute-done.11.refs_0_
  34.2 0.0 collective-permute-done.12.refs_1_
  34.2 1.7 %collective-permute-start.13 = (bf16[16,4096]{1,0:T(8,128)(2,1)S(1)}, bf16[16,4096]{1,0:T(8,128)(2,1)S(1)}, u32[]{:S(2)}, u32[]{:S(2)}) collective-permute-start(bf16[16,4096]{1,0:T(8,128)(2,1)S(1)} %add.6), channel_id=1, source_target_pairs={{0,8},{2,10},{4,12},{6,14},{8,0},{10,2},{12,4},{14,6},{1,9},{3,11}... | collective-permute-start | bytes 393224 | tf_op jit(solution)/shard_map/ppermute | solution.py:112
  36.0 1.4 %collective-permute-start.15 = (bf16[16,4096]{1,0:T(8,128)(2,1)S(1)}, bf16[16,4096]{1,0:T(8,128)(2,1)S(1)}, u32[]{:S(2)}, u32[]{:S(2)}) collective-permute-start(bf16[16,4096]{1,0:T(8,128)(2,1)S(1)} %get-tuple-element.32), channel_id=1, source_target_pairs={{0,2},{2,0},{4,6},{6,4},{8,10},{10,8},{12,14},{14,12},{1,3},{3,1},... | collective-permute-start | bytes 393224 | tf_op jit(solution)/shard_map/ppermute | solution.py:112
  37.4 0.0 collective-permute-done.9.refs_0_
  37.4 2.6 %collective-permute-done.14.refs_1_ = bf16[16,4096]{1,0:T(8,128)(2,1)S(1)} collective-permute-done((bf16[16,4096]{1,0:T(8,128)(2,1)S(1)}, bf16[16,4096]{1,0:T(8,128)(2,1)S(1)}, u32[]{:S(2)}, u32[]{:S(2)}) %collective-permute-start.14) | collective-permute-done | bytes 131104 | tf_op jit(solution)/shard_map/ppermute | solution.py:112
  40.0 3.0 %collective-permute-done.13.refs_0_ = bf16[16,4096]{1,0:T(8,128)(2,1)S(1)} collective-permute-done((bf16[16,4096]{1,0:T(8,128)(2,1)S(1)}, bf16[16,4096]{1,0:T(8,128)(2,1)S(1)}, u32[]{:S(2)}, u32[]{:S(2)}) %collective-permute-start.13) | collective-permute-done | bytes 131104 | tf_op jit(solution)/shard_map/ppermute | solution.py:112
  43.0 0.0 collective-permute-done.15.refs_2_
  43.0 0.7 %add.7 = bf16[16,4096]{1,0:T(8,128)(2,1)} custom-call(f32[16,4096]{1,0:T(8,128)S(1)} %add.5.own_ref, bf16[16,4096]{1,0:T(8,128)(2,1)S(1)} %collective-permute-done.13.refs_0_, bf16[16,4096]{1,0:T(8,128)(2,1)S(1)} %collective-permute-done.14.refs_1_, bf16[16,4096]{1,0:T(8,128)(2,1)S(1)} %collective-permute-done.15.refs_2_), custom_call_target="tpu_custom_call" | custom-call | flops 1000000 | tf_op jit(solution)/shard_map/add/pallas_call | solution.py:97
  (3 shorter events, 0.1 us)
Async XLA Ops:
  0.0 9.4 %copy-start.1 = (bf16[16,4096]{1,0:T(8,128)(2,1)S(1)}, bf16[16,4096]{1,0:T(8,128)(2,1)}, u32[]{:S(2)}) copy-start(bf16[16,4096]{1,0:T(8,128)(2,1)} %refs_0_.3) | copy-start | bytes 393220
  0.0 10.7 %collective-permute-start.3 = (bf16[16,4096]{1,0:T(8,128)(2,1)}, bf16[16,4096]{1,0:T(8,128)(2,1)S(1)}, u32[]{:S(2)}, u32[]{:S(2)}) collective-permute-start(bf16[16,4096]{1,0:T(8,128)(2,1)} %refs_0_.3), channel_id=1, source_target_pairs={{0,8},{2,10},{4,12},{6,14},{8,0},{10,2},{12,4},{14,6},{1,9},{3,11}... | collective-permute-start | bytes 393224 | tf_op jit(solution)/shard_map/ppermute | solution.py:112
  4.0 8.9 %collective-permute-start.2 = (bf16[16,4096]{1,0:T(8,128)(2,1)}, bf16[16,4096]{1,0:T(8,128)(2,1)S(1)}, u32[]{:S(2)}, u32[]{:S(2)}) collective-permute-start(bf16[16,4096]{1,0:T(8,128)(2,1)} %refs_0_.3), channel_id=1, source_target_pairs={{0,4},{2,6},{4,0},{6,2},{8,12},{10,14},{12,8},{14,10},{1,5},{3,7},... | collective-permute-start | bytes 393224 | tf_op jit(solution)/shard_map/ppermute | solution.py:112
  5.6 10.8 %collective-permute-start.1 = (bf16[16,4096]{1,0:T(8,128)(2,1)}, bf16[16,4096]{1,0:T(8,128)(2,1)S(1)}, u32[]{:S(2)}, u32[]{:S(2)}) collective-permute-start(bf16[16,4096]{1,0:T(8,128)(2,1)} %refs_0_.3), channel_id=1, source_target_pairs={{0,2},{2,0},{4,6},{6,4},{8,10},{10,8},{12,14},{14,12},{1,3},{3,1},... | collective-permute-start | bytes 393224 | tf_op jit(solution)/shard_map/ppermute | solution.py:112
  9.4 7.1 %collective-permute-start = (bf16[16,4096]{1,0:T(8,128)(2,1)S(1)}, bf16[16,4096]{1,0:T(8,128)(2,1)S(1)}, u32[]{:S(2)}, u32[]{:S(2)}) collective-permute-start(bf16[16,4096]{1,0:T(8,128)(2,1)S(1)} %copy-done.1), channel_id=1, source_target_pairs={{0,6},{2,4},{4,2},{6,0},{8,14},{10,12},{12,10},{14,8},{1,7},{3,5},... | collective-permute-start | bytes 393224 | tf_op jit(solution)/shard_map/ppermute | solution.py:112
  10.7 8.2 %collective-permute-start.6 = (bf16[16,4096]{1,0:T(8,128)(2,1)S(1)}, bf16[16,4096]{1,0:T(8,128)(2,1)S(1)}, u32[]{:S(2)}, u32[]{:S(2)}) collective-permute-start(bf16[16,4096]{1,0:T(8,128)(2,1)S(1)} %collective-permute-done.3.refs_4_), channel_id=1, source_target_pairs={{0,6},{2,4},{4,2},{6,0},{8,14},{10,12},{12,10},{14,8},{1,7},{3,5},... | collective-permute-start | bytes 393224 | tf_op jit(solution)/shard_map/ppermute | solution.py:112
  12.4 8.0 %collective-permute-start.5 = (bf16[16,4096]{1,0:T(8,128)(2,1)S(1)}, bf16[16,4096]{1,0:T(8,128)(2,1)S(1)}, u32[]{:S(2)}, u32[]{:S(2)}) collective-permute-start(bf16[16,4096]{1,0:T(8,128)(2,1)S(1)} %collective-permute-done.3.refs_4_), channel_id=1, source_target_pairs={{0,2},{2,0},{4,6},{6,4},{8,10},{10,8},{12,14},{14,12},{1,3},{3,1},... | collective-permute-start | bytes 393224 | tf_op jit(solution)/shard_map/ppermute | solution.py:112
  12.9 7.5 %collective-permute-start.4 = (bf16[16,4096]{1,0:T(8,128)(2,1)S(1)}, bf16[16,4096]{1,0:T(8,128)(2,1)S(1)}, u32[]{:S(2)}, u32[]{:S(2)}) collective-permute-start(bf16[16,4096]{1,0:T(8,128)(2,1)S(1)} %collective-permute-done.3.refs_4_), channel_id=1, source_target_pairs={{0,4},{2,6},{4,0},{6,2},{8,12},{10,14},{12,8},{14,10},{1,5},{3,7},... | collective-permute-start | bytes 393224 | tf_op jit(solution)/shard_map/ppermute | solution.py:112
  16.4 7.1 %copy-start = (bf16[512,4096]{1,0:T(8,128)(2,1)S(1)}, bf16[512,4096]{1,0:T(8,128)(2,1)}, u32[]{:S(2)}) copy-start(bf16[512,4096]{1,0:T(8,128)(2,1)} %weight_ref.1) | copy-start | bytes 12582916
  21.1 1.6 %collective-permute-start.7 = (f32[128,512]{1,0:T(8,128)S(1)}, f32[128,512]{1,0:T(8,128)S(1)}, u32[]{:S(2)}, u32[]{:S(2)}) collective-permute-start(f32[128,512]{1,0:T(8,128)S(1)} %project.2.gate_ref), channel_id=1, source_target_pairs={{0,1},{1,0},{2,3},{3,2},{4,5},{5,4},{6,7},{7,6},{8,9},{9,8},{10,11... | collective-permute-start | bytes 786440 | tf_op jit(solution)/shard_map/ppermute | solution.py:115
  21.9 1.7 %collective-permute-start.8 = (f32[128,512]{1,0:T(8,128)S(1)}, f32[128,512]{1,0:T(8,128)S(1)}, u32[]{:S(2)}, u32[]{:S(2)}) collective-permute-start(f32[128,512]{1,0:T(8,128)S(1)} %project.3.up_ref), channel_id=1, source_target_pairs={{0,1},{1,0},{2,3},{3,2},{4,5},{5,4},{6,7},{7,6},{8,9},{9,8},{10,11... | collective-permute-start | bytes 786440 | tf_op jit(solution)/shard_map/ppermute | solution.py:115
  24.3 6.4 %collective-permute-start.10 = (bf16[16,4096]{1,0:T(8,128)(2,1)S(1)}, bf16[16,4096]{1,0:T(8,128)(2,1)S(1)}, u32[]{:S(2)}, u32[]{:S(2)}) collective-permute-start(bf16[16,4096]{1,0:T(8,128)(2,1)S(1)} %get-tuple-element.26), channel_id=1, source_target_pairs={{0,2},{2,0},{4,6},{6,4},{8,10},{10,8},{12,14},{14,12},{1,3},{3,1},... | collective-permute-start | bytes 393224 | tf_op jit(solution)/shard_map/ppermute | solution.py:112
  25.3 8.9 %collective-permute-start.11 = (bf16[16,4096]{1,0:T(8,128)(2,1)S(1)}, bf16[16,4096]{1,0:T(8,128)(2,1)S(1)}, u32[]{:S(2)}, u32[]{:S(2)}) collective-permute-start(bf16[16,4096]{1,0:T(8,128)(2,1)S(1)} %get-tuple-element.29), channel_id=1, source_target_pairs={{0,2},{2,0},{4,6},{6,4},{8,10},{10,8},{12,14},{14,12},{1,3},{3,1},... | collective-permute-start | bytes 393224 | tf_op jit(solution)/shard_map/ppermute | solution.py:112
  26.4 7.7 %collective-permute-start.12 = (bf16[16,4096]{1,0:T(8,128)(2,1)S(1)}, bf16[16,4096]{1,0:T(8,128)(2,1)S(1)}, u32[]{:S(2)}, u32[]{:S(2)}) collective-permute-start(bf16[16,4096]{1,0:T(8,128)(2,1)S(1)} %get-tuple-element.30), channel_id=1, source_target_pairs={{0,4},{2,6},{4,0},{6,2},{8,12},{10,14},{12,8},{14,10},{1,5},{3,7},... | collective-permute-start | bytes 393224 | tf_op jit(solution)/shard_map/ppermute | solution.py:112
  27.8 9.6 %collective-permute-start.9 = (bf16[16,4096]{1,0:T(8,128)(2,1)S(1)}, bf16[16,4096]{1,0:T(8,128)(2,1)S(1)}, u32[]{:S(2)}, u32[]{:S(2)}) collective-permute-start(bf16[16,4096]{1,0:T(8,128)(2,1)S(1)} %get-tuple-element.24), channel_id=1, source_target_pairs={{0,14},{2,12},{4,10},{6,8},{8,6},{10,4},{12,2},{14,0},{1,15},{3,13... | collective-permute-start | bytes 393224 | tf_op jit(solution)/shard_map/ppermute | solution.py:112
  30.8 9.2 %collective-permute-start.14 = (bf16[16,4096]{1,0:T(8,128)(2,1)S(1)}, bf16[16,4096]{1,0:T(8,128)(2,1)S(1)}, u32[]{:S(2)}, u32[]{:S(2)}) collective-permute-start(bf16[16,4096]{1,0:T(8,128)(2,1)S(1)} %add.4.refs_1_), channel_id=1, source_target_pairs={{0,4},{2,6},{4,0},{6,2},{8,12},{10,14},{12,8},{14,10},{1,5},{3,7},... | collective-permute-start | bytes 393224 | tf_op jit(solution)/shard_map/ppermute | solution.py:112
  34.2 8.7 %collective-permute-start.13 = (bf16[16,4096]{1,0:T(8,128)(2,1)S(1)}, bf16[16,4096]{1,0:T(8,128)(2,1)S(1)}, u32[]{:S(2)}, u32[]{:S(2)}) collective-permute-start(bf16[16,4096]{1,0:T(8,128)(2,1)S(1)} %add.6), channel_id=1, source_target_pairs={{0,8},{2,10},{4,12},{6,14},{8,0},{10,2},{12,4},{14,6},{1,9},{3,11}... | collective-permute-start | bytes 393224 | tf_op jit(solution)/shard_map/ppermute | solution.py:112
  36.0 7.0 %collective-permute-start.15 = (bf16[16,4096]{1,0:T(8,128)(2,1)S(1)}, bf16[16,4096]{1,0:T(8,128)(2,1)S(1)}, u32[]{:S(2)}, u32[]{:S(2)}) collective-permute-start(bf16[16,4096]{1,0:T(8,128)(2,1)S(1)} %get-tuple-element.32), channel_id=1, source_target_pairs={{0,2},{2,0},{4,6},{6,4},{8,10},{10,8},{12,14},{14,12},{1,3},{3,1},... | collective-permute-start | bytes 393224 | tf_op jit(solution)/shard_map/ppermute | solution.py:112

commit v29 on v25

--- a/solution.py
+++ b/solution.py
@@ -142,7 +142,7 @@
         part = dict(zip(order, outs))
         sums, direct = [], []
         for far in fars:
-            sums.append(add(part[far], [swap(part[far + near], near) for near in (1, 2)], BF16))
+            sums.append(add(part[far], [swap(part[far + near], near) for near in (2, 1)], BF16))
             direct.append(swap(part[far + 3], far + 3))
         pair = add(part[2], [swap(part[3], 1)], BF16, after=sums)
         part[1], sums[0] = lax.optimization_barrier((part[1], sums[0]))

time: 43.6 us -> 43.9 us (level)
  waiting for transfers between devices: 15 us -> 15.5 us
    ppermute x14, waiting for transfers between devices: 13.9 us -> 14.3 us  [swap(): return lax.ppermute(value, 'wide', [(i, i ^ bits) for i in range(wide)])]
  transfers between devices with their start and end apart: 16 -> 16, of which waited for: 9 -> 10; matrix products, arithmetic and copies ran while one was open for 0% -> 0% of each run, Pallas kernels for 12% -> 12%
where the time goes in v29:
time: 43.9 us; the launch traced here: 43.8 us
  starting transfers between devices  20.8 us (47%)
  waiting for transfers between devices  15.5 us (35%)
  Pallas kernels  7.4 us (17%)
    ppermute x14, starting transfers between devices, swap(): return lax.ppermute(value, 'wide', [(i, i ^ bits) for i in range(wide)])  20.1 us
    ppermute x14, waiting for transfers between devices, swap(): return lax.ppermute(value, 'wide', [(i, i ^ bits) for i in range(wide)])  14.3 us
    pallas_call x2, Pallas kernels, fetch(): pl.pallas_call(functools.partial(fetch_kernel, pieces), in_specs=[pl.Bloc...  4.43 us
    pallas_call x3, Pallas kernels, call(): pl.pallas_call(kernel, out_shape=out_shape, compiler_params=pltpu.Compile...  2.16 us
    ppermute x2, waiting for transfers between devices, across_cores(): lax.ppermute(value, 'narrow', [(i, (i + 1) % narrow) for i in range(narro...  1.16 us
  transfers between devices with their start and end apart: 16, of which 10 were waited for; matrix products, arithmetic and copies ran while one was open for 0% of the time, Pallas kernels for 12%

profile of v29, /device:TPU:0, one launch (start us, length us, event | category | flops | bytes accessed | tf_op | source)
XLA Modules:
  0.0 43.8 jit_solution(17648340071340546113)
XLA Ops:
  0.0 0.0 copy-start.1
  0.0 4.0 %collective-permute-start.3 = (bf16[16,4096]{1,0:T(8,128)(2,1)}, bf16[16,4096]{1,0:T(8,128)(2,1)S(1)}, u32[]{:S(2)}, u32[]{:S(2)}) collective-permute-start(bf16[16,4096]{1,0:T(8,128)(2,1)} %refs_0_.3), channel_id=1, source_target_pairs={{0,8},{2,10},{4,12},{6,14},{8,0},{10,2},{12,4},{14,6},{1,9},{3,11}... | collective-permute-start | bytes 393224 | tf_op jit(solution)/shard_map/ppermute | solution.py:112
  4.0 1.6 %collective-permute-start.2 = (bf16[16,4096]{1,0:T(8,128)(2,1)}, bf16[16,4096]{1,0:T(8,128)(2,1)S(1)}, u32[]{:S(2)}, u32[]{:S(2)}) collective-permute-start(bf16[16,4096]{1,0:T(8,128)(2,1)} %refs_0_.3), channel_id=1, source_target_pairs={{0,4},{2,6},{4,0},{6,2},{8,12},{10,14},{12,8},{14,10},{1,5},{3,7},... | collective-permute-start | bytes 393224 | tf_op jit(solution)/shard_map/ppermute | solution.py:112
  5.6 1.5 %collective-permute-start.1 = (bf16[16,4096]{1,0:T(8,128)(2,1)}, bf16[16,4096]{1,0:T(8,128)(2,1)S(1)}, u32[]{:S(2)}, u32[]{:S(2)}) collective-permute-start(bf16[16,4096]{1,0:T(8,128)(2,1)} %refs_0_.3), channel_id=1, source_target_pairs={{0,2},{2,0},{4,6},{6,4},{8,10},{10,8},{12,14},{14,12},{1,3},{3,1},... | collective-permute-start | bytes 393224 | tf_op jit(solution)/shard_map/ppermute | solution.py:112
  7.1 2.2 %fetch.2.refs_8_ = bf16[4096,512]{1,0:T(8,128)(2,1)S(1)} custom-call(bf16[4096,512]{1,0:T(8,128)(2,1)} %source.2), custom_call_target="tpu_custom_call" | custom-call | flops 2000000000 | tf_op jit(solution)/shard_map/fetch/pallas_call | solution.py:37
  9.4 0.0 copy-done.1
  9.4 0.5 %collective-permute-start = (bf16[16,4096]{1,0:T(8,128)(2,1)S(1)}, bf16[16,4096]{1,0:T(8,128)(2,1)S(1)}, u32[]{:S(2)}, u32[]{:S(2)}) collective-permute-start(bf16[16,4096]{1,0:T(8,128)(2,1)S(1)} %copy-done.1), channel_id=1, source_target_pairs={{0,6},{2,4},{4,2},{6,0},{8,14},{10,12},{12,10},{14,8},{1,7},{3,5},... | collective-permute-start | bytes 393224 | tf_op jit(solution)/shard_map/ppermute | solution.py:112
  9.8 0.9 %collective-permute-done.3.refs_4_ = bf16[16,4096]{1,0:T(8,128)(2,1)S(1)} collective-permute-done((bf16[16,4096]{1,0:T(8,128)(2,1)}, bf16[16,4096]{1,0:T(8,128)(2,1)S(1)}, u32[]{:S(2)}, u32[]{:S(2)}) %collective-permute-start.3) | collective-permute-done | bytes 131104 | tf_op jit(solution)/shard_map/ppermute | solution.py:112
  10.7 1.7 %collective-permute-start.6 = (bf16[16,4096]{1,0:T(8,128)(2,1)S(1)}, bf16[16,4096]{1,0:T(8,128)(2,1)S(1)}, u32[]{:S(2)}, u32[]{:S(2)}) collective-permute-start(bf16[16,4096]{1,0:T(8,128)(2,1)S(1)} %collective-permute-done.3.refs_4_), channel_id=1, source_target_pairs={{0,6},{2,4},{4,2},{6,0},{8,14},{10,12},{12,10},{14,8},{1,7},{3,5},... | collective-permute-start | bytes 393224 | tf_op jit(solution)/shard_map/ppermute | solution.py:112
  12.4 0.5 %collective-permute-start.5 = (bf16[16,4096]{1,0:T(8,128)(2,1)S(1)}, bf16[16,4096]{1,0:T(8,128)(2,1)S(1)}, u32[]{:S(2)}, u32[]{:S(2)}) collective-permute-start(bf16[16,4096]{1,0:T(8,128)(2,1)S(1)} %collective-permute-done.3.refs_4_), channel_id=1, source_target_pairs={{0,2},{2,0},{4,6},{6,4},{8,10},{10,8},{12,14},{14,12},{1,3},{3,1},... | collective-permute-start | bytes 393224 | tf_op jit(solution)/shard_map/ppermute | solution.py:112
  12.9 0.0 collective-permute-done.2.refs_3_
  12.9 1.3 %collective-permute-start.4 = (bf16[16,4096]{1,0:T(8,128)(2,1)S(1)}, bf16[16,4096]{1,0:T(8,128)(2,1)S(1)}, u32[]{:S(2)}, u32[]{:S(2)}) collective-permute-start(bf16[16,4096]{1,0:T(8,128)(2,1)S(1)} %collective-permute-done.3.refs_4_), channel_id=1, source_target_pairs={{0,4},{2,6},{4,0},{6,2},{8,12},{10,14},{12,8},{14,10},{1,5},{3,7},... | collective-permute-start | bytes 393224 | tf_op jit(solution)/shard_map/ppermute | solution.py:112
  14.2 2.2 %fetch.3.refs_8_ = bf16[4096,512]{1,0:T(8,128)(2,1)S(1)} custom-call(bf16[4096,512]{1,0:T(8,128)(2,1)} %source.3), custom_call_target="tpu_custom_call" | custom-call | flops 2000000000 | tf_op jit(solution)/shard_map/fetch/pallas_call | solution.py:37
  16.4 0.0 copy-start
  16.5 0.0 collective-permute-done.1.refs_2_
  16.5 0.0 collective-permute-done.refs_1_
  16.5 2.5 %collective-permute-done.6.refs_7_ = bf16[16,4096]{1,0:T(8,128)(2,1)S(1)} collective-permute-done((bf16[16,4096]{1,0:T(8,128)(2,1)S(1)}, bf16[16,4096]{1,0:T(8,128)(2,1)S(1)}, u32[]{:S(2)}, u32[]{:S(2)}) %collective-permute-start.6) | collective-permute-done | bytes 131104 | tf_op jit(solution)/shard_map/ppermute | solution.py:112
  19.0 1.4 %collective-permute-done.5.refs_6_ = bf16[16,4096]{1,0:T(8,128)(2,1)S(1)} collective-permute-done((bf16[16,4096]{1,0:T(8,128)(2,1)S(1)}, bf16[16,4096]{1,0:T(8,128)(2,1)S(1)}, u32[]{:S(2)}, u32[]{:S(2)}) %collective-permute-start.5) | collective-permute-done | bytes 131104 | tf_op jit(solution)/shard_map/ppermute | solution.py:112
  20.3 0.0 collective-permute-done.4.refs_5_
  20.4 0.7 %project.2.gate_ref = f32[128,512]{1,0:T(8,128)S(1)} custom-call(bf16[16,4096]{1,0:T(8,128)(2,1)S(1)} %copy-done.1, bf16[16,4096]{1,0:T(8,128)(2,1)S(1)} %collective-permute-done.refs_1_, bf16[16,4096]{1,0:T(8,128)(2,1)S(1)} %collective-permute-done.1.refs_2_, bf16[16,4096]{1,0:T(8,128)(2,1)S(1)} %collective-permute-done.2.refs_3_, ...), custom_call_target="tpu_custom_call" | custom-call | flops 400000000 | tf_op jit(solution)/shard_map/project/pallas_call | solution.py:15
  21.1 0.1 collective-permute-start.7
  21.2 0.7 %project.3.up_ref = f32[128,512]{1,0:T(8,128)S(1)} custom-call(bf16[16,4096]{1,0:T(8,128)(2,1)S(1)} %copy-done.1, bf16[16,4096]{1,0:T(8,128)(2,1)S(1)} %collective-permute-done.refs_1_, bf16[16,4096]{1,0:T(8,128)(2,1)S(1)} %collective-permute-done.1.refs_2_, bf16[16,4096]{1,0:T(8,128)(2,1)S(1)} %collective-permute-done.2.refs_3_, ...), custom_call_target="tpu_custom_call" | custom-call | flops 400000000 | tf_op jit(solution)/shard_map/project/pallas_call | solution.py:15
  21.9 0.6 %collective-permute-start.8 = (f32[128,512]{1,0:T(8,128)S(1)}, f32[128,512]{1,0:T(8,128)S(1)}, u32[]{:S(2)}, u32[]{:S(2)}) collective-permute-start(f32[128,512]{1,0:T(8,128)S(1)} %project.3.up_ref), channel_id=1, source_target_pairs={{0,1},{1,0},{2,3},{3,2},{4,5},{5,4},{6,7},{7,6},{8,9},{9,8},{10,11... | collective-permute-start | bytes 786440 | tf_op jit(solution)/shard_map/ppermute | solution.py:115
  22.4 0.2 collective-permute-done.7.gate_other_ref
  22.7 0.9 %collective-permute-done.8.up_other_ref = f32[128,512]{1,0:T(8,128)S(1)} collective-permute-done((f32[128,512]{1,0:T(8,128)S(1)}, f32[128,512]{1,0:T(8,128)S(1)}, u32[]{:S(2)}, u32[]{:S(2)}) %collective-permute-start.8) | collective-permute-done | bytes 262176 | tf_op jit(solution)/shard_map/ppermute | solution.py:115
  23.6 0.0 copy-done
  23.6 0.7 %down.1 = (f32[16,4096]{1,0:T(8,128)S(1)}, bf16[16,4096]{1,0:T(8,128)(2,1)S(1)}, bf16[16,4096]{1,0:T(8,128)(2,1)S(1)}, f32[16,4096]{1,0:T(8,128)S(1)}, f32[16,40...) custom-call(f32[128,512]{1,0:T(8,128)S(1)} %project.2.gate_ref, ...), custom_call_target="tpu_custom_call" | custom-call | flops 536870912 | tf_op jit(solution)/shard_map/down/pallas_call | solution.py:15
  24.3 1.4 %collective-permute-start.11 = (bf16[16,4096]{1,0:T(8,128)(2,1)S(1)}, bf16[16,4096]{1,0:T(8,128)(2,1)S(1)}, u32[]{:S(2)}, u32[]{:S(2)}) collective-permute-start(bf16[16,4096]{1,0:T(8,128)(2,1)S(1)} %get-tuple-element.28), channel_id=1, source_target_pairs={{0,4},{2,6},{4,0},{6,2},{8,12},{10,14},{12,8},{14,10},{1,5},{3,7},... | collective-permute-start | bytes 393224 | tf_op jit(solution)/shard_map/ppermute | solution.py:112
  25.8 0.6 %collective-permute-start.12 = (bf16[16,4096]{1,0:T(8,128)(2,1)S(1)}, bf16[16,4096]{1,0:T(8,128)(2,1)S(1)}, u32[]{:S(2)}, u32[]{:S(2)}) collective-permute-start(bf16[16,4096]{1,0:T(8,128)(2,1)S(1)} %get-tuple-element.29), channel_id=1, source_target_pairs={{0,2},{2,0},{4,6},{6,4},{8,10},{10,8},{12,14},{14,12},{1,3},{3,1},... | collective-permute-start | bytes 393224 | tf_op jit(solution)/shard_map/ppermute | solution.py:112
  26.4 1.4 %collective-permute-start.10 = (bf16[16,4096]{1,0:T(8,128)(2,1)S(1)}, bf16[16,4096]{1,0:T(8,128)(2,1)S(1)}, u32[]{:S(2)}, u32[]{:S(2)}) collective-permute-start(bf16[16,4096]{1,0:T(8,128)(2,1)S(1)} %get-tuple-element.26), channel_id=1, source_target_pairs={{0,2},{2,0},{4,6},{6,4},{8,10},{10,8},{12,14},{14,12},{1,3},{3,1},... | collective-permute-start | bytes 393224 | tf_op jit(solution)/shard_map/ppermute | solution.py:112
  27.8 1.9 %collective-permute-start.9 = (bf16[16,4096]{1,0:T(8,128)(2,1)S(1)}, bf16[16,4096]{1,0:T(8,128)(2,1)S(1)}, u32[]{:S(2)}, u32[]{:S(2)}) collective-permute-start(bf16[16,4096]{1,0:T(8,128)(2,1)S(1)} %get-tuple-element.24), channel_id=1, source_target_pairs={{0,14},{2,12},{4,10},{6,8},{8,6},{10,4},{12,2},{14,0},{1,15},{3,13... | collective-permute-start | bytes 393224 | tf_op jit(solution)/shard_map/ppermute | solution.py:112
  29.7 0.5 %collective-permute-done.11.refs_0_ = bf16[16,4096]{1,0:T(8,128)(2,1)S(1)} collective-permute-done((bf16[16,4096]{1,0:T(8,128)(2,1)S(1)}, bf16[16,4096]{1,0:T(8,128)(2,1)S(1)}, u32[]{:S(2)}, u32[]{:S(2)}) %collective-permute-start.11) | collective-permute-done | bytes 131104 | tf_op jit(solution)/shard_map/ppermute | solution.py:112
  30.2 1.9 %collective-permute-done.12.refs_1_ = bf16[16,4096]{1,0:T(8,128)(2,1)S(1)} collective-permute-done((bf16[16,4096]{1,0:T(8,128)(2,1)S(1)}, bf16[16,4096]{1,0:T(8,128)(2,1)S(1)}, u32[]{:S(2)}, u32[]{:S(2)}) %collective-permute-start.12) | collective-permute-done | bytes 131104 | tf_op jit(solution)/shard_map/ppermute | solution.py:112
  32.2 3.1 %collective-permute-start.13 = (bf16[16,4096]{1,0:T(8,128)(2,1)S(1)}, bf16[16,4096]{1,0:T(8,128)(2,1)S(1)}, u32[]{:S(2)}, u32[]{:S(2)}) collective-permute-start(bf16[16,4096]{1,0:T(8,128)(2,1)S(1)} %add.4.refs_1_), channel_id=1, source_target_pairs={{0,8},{2,10},{4,12},{6,14},{8,0},{10,2},{12,4},{14,6},{1,9},{3,11}... | collective-permute-start | bytes 393224 | tf_op jit(solution)/shard_map/ppermute | solution.py:112
  35.3 0.5 %collective-permute-start.15 = (bf16[16,4096]{1,0:T(8,128)(2,1)S(1)}, bf16[16,4096]{1,0:T(8,128)(2,1)S(1)}, u32[]{:S(2)}, u32[]{:S(2)}) collective-permute-start(bf16[16,4096]{1,0:T(8,128)(2,1)S(1)} %get-tuple-element.32), channel_id=1, source_target_pairs={{0,2},{2,0},{4,6},{6,4},{8,10},{10,8},{12,14},{14,12},{1,3},{3,1},... | collective-permute-start | bytes 393224 | tf_op jit(solution)/shard_map/ppermute | solution.py:112
  35.8 1.9 %collective-permute-done.10.refs_0_ = bf16[16,4096]{1,0:T(8,128)(2,1)S(1)} collective-permute-done((bf16[16,4096]{1,0:T(8,128)(2,1)S(1)}, bf16[16,4096]{1,0:T(8,128)(2,1)S(1)}, u32[]{:S(2)}, u32[]{:S(2)}) %collective-permute-start.10) | collective-permute-done | bytes 131104 | tf_op jit(solution)/shard_map/ppermute | solution.py:112
  37.8 0.1 collective-permute-start.14
  37.8 0.0 collective-permute-done.9.refs_0_
  37.9 3.8 %collective-permute-done.13.refs_0_ = bf16[16,4096]{1,0:T(8,128)(2,1)S(1)} collective-permute-done((bf16[16,4096]{1,0:T(8,128)(2,1)S(1)}, bf16[16,4096]{1,0:T(8,128)(2,1)S(1)}, u32[]{:S(2)}, u32[]{:S(2)}) %collective-permute-start.13) | collective-permute-done | bytes 131104 | tf_op jit(solution)/shard_map/ppermute | solution.py:112
  41.7 0.0 collective-permute-done.15.refs_2_
  41.7 1.4 %collective-permute-done.14.refs_1_ = bf16[16,4096]{1,0:T(8,128)(2,1)S(1)} collective-permute-done((bf16[16,4096]{1,0:T(8,128)(2,1)S(1)}, bf16[16,4096]{1,0:T(8,128)(2,1)S(1)}, u32[]{:S(2)}, u32[]{:S(2)}) %collective-permute-start.14) | collective-permute-done | bytes 131104 | tf_op jit(solution)/shard_map/ppermute | solution.py:112
  43.1 0.7 %add.7 = bf16[16,4096]{1,0:T(8,128)(2,1)} custom-call(f32[16,4096]{1,0:T(8,128)S(1)} %add.6.own_ref, bf16[16,4096]{1,0:T(8,128)(2,1)S(1)} %collective-permute-done.13.refs_0_, bf16[16,4096]{1,0:T(8,128)(2,1)S(1)} %collective-permute-done.14.refs_1_, bf16[16,4096]{1,0:T(8,128)(2,1)S(1)} %collective-permute-done.15.refs_2_), custom_call_target="tpu_custom_call" | custom-call | flops 1000000 | tf_op jit(solution)/shard_map/add/pallas_call | solution.py:97
  (3 shorter events, 0.1 us)
Async XLA Ops:
  0.0 9.4 %copy-start.1 = (bf16[16,4096]{1,0:T(8,128)(2,1)S(1)}, bf16[16,4096]{1,0:T(8,128)(2,1)}, u32[]{:S(2)}) copy-start(bf16[16,4096]{1,0:T(8,128)(2,1)} %refs_0_.3) | copy-start | bytes 393220
  0.0 10.7 %collective-permute-start.3 = (bf16[16,4096]{1,0:T(8,128)(2,1)}, bf16[16,4096]{1,0:T(8,128)(2,1)S(1)}, u32[]{:S(2)}, u32[]{:S(2)}) collective-permute-start(bf16[16,4096]{1,0:T(8,128)(2,1)} %refs_0_.3), channel_id=1, source_target_pairs={{0,8},{2,10},{4,12},{6,14},{8,0},{10,2},{12,4},{14,6},{1,9},{3,11}... | collective-permute-start | bytes 393224 | tf_op jit(solution)/shard_map/ppermute | solution.py:112
  4.0 8.9 %collective-permute-start.2 = (bf16[16,4096]{1,0:T(8,128)(2,1)}, bf16[16,4096]{1,0:T(8,128)(2,1)S(1)}, u32[]{:S(2)}, u32[]{:S(2)}) collective-permute-start(bf16[16,4096]{1,0:T(8,128)(2,1)} %refs_0_.3), channel_id=1, source_target_pairs={{0,4},{2,6},{4,0},{6,2},{8,12},{10,14},{12,8},{14,10},{1,5},{3,7},... | collective-permute-start | bytes 393224 | tf_op jit(solution)/shard_map/ppermute | solution.py:112
  5.6 10.8 %collective-permute-start.1 = (bf16[16,4096]{1,0:T(8,128)(2,1)}, bf16[16,4096]{1,0:T(8,128)(2,1)S(1)}, u32[]{:S(2)}, u32[]{:S(2)}) collective-permute-start(bf16[16,4096]{1,0:T(8,128)(2,1)} %refs_0_.3), channel_id=1, source_target_pairs={{0,2},{2,0},{4,6},{6,4},{8,10},{10,8},{12,14},{14,12},{1,3},{3,1},... | collective-permute-start | bytes 393224 | tf_op jit(solution)/shard_map/ppermute | solution.py:112
  9.4 7.1 %collective-permute-start = (bf16[16,4096]{1,0:T(8,128)(2,1)S(1)}, bf16[16,4096]{1,0:T(8,128)(2,1)S(1)}, u32[]{:S(2)}, u32[]{:S(2)}) collective-permute-start(bf16[16,4096]{1,0:T(8,128)(2,1)S(1)} %copy-done.1), channel_id=1, source_target_pairs={{0,6},{2,4},{4,2},{6,0},{8,14},{10,12},{12,10},{14,8},{1,7},{3,5},... | collective-permute-start | bytes 393224 | tf_op jit(solution)/shard_map/ppermute | solution.py:112
  10.7 8.2 %collective-permute-start.6 = (bf16[16,4096]{1,0:T(8,128)(2,1)S(1)}, bf16[16,4096]{1,0:T(8,128)(2,1)S(1)}, u32[]{:S(2)}, u32[]{:S(2)}) collective-permute-start(bf16[16,4096]{1,0:T(8,128)(2,1)S(1)} %collective-permute-done.3.refs_4_), channel_id=1, source_target_pairs={{0,6},{2,4},{4,2},{6,0},{8,14},{10,12},{12,10},{14,8},{1,7},{3,5},... | collective-permute-start | bytes 393224 | tf_op jit(solution)/shard_map/ppermute | solution.py:112
  12.4 8.0 %collective-permute-start.5 = (bf16[16,4096]{1,0:T(8,128)(2,1)S(1)}, bf16[16,4096]{1,0:T(8,128)(2,1)S(1)}, u32[]{:S(2)}, u32[]{:S(2)}) collective-permute-start(bf16[16,4096]{1,0:T(8,128)(2,1)S(1)} %collective-permute-done.3.refs_4_), channel_id=1, source_target_pairs={{0,2},{2,0},{4,6},{6,4},{8,10},{10,8},{12,14},{14,12},{1,3},{3,1},... | collective-permute-start | bytes 393224 | tf_op jit(solution)/shard_map/ppermute | solution.py:112
  12.9 7.5 %collective-permute-start.4 = (bf16[16,4096]{1,0:T(8,128)(2,1)S(1)}, bf16[16,4096]{1,0:T(8,128)(2,1)S(1)}, u32[]{:S(2)}, u32[]{:S(2)}) collective-permute-start(bf16[16,4096]{1,0:T(8,128)(2,1)S(1)} %collective-permute-done.3.refs_4_), channel_id=1, source_target_pairs={{0,4},{2,6},{4,0},{6,2},{8,12},{10,14},{12,8},{14,10},{1,5},{3,7},... | collective-permute-start | bytes 393224 | tf_op jit(solution)/shard_map/ppermute | solution.py:112
  16.4 7.1 %copy-start = (bf16[512,4096]{1,0:T(8,128)(2,1)S(1)}, bf16[512,4096]{1,0:T(8,128)(2,1)}, u32[]{:S(2)}) copy-start(bf16[512,4096]{1,0:T(8,128)(2,1)} %weight_ref.1) | copy-start | bytes 12582916
  21.1 1.6 %collective-permute-start.7 = (f32[128,512]{1,0:T(8,128)S(1)}, f32[128,512]{1,0:T(8,128)S(1)}, u32[]{:S(2)}, u32[]{:S(2)}) collective-permute-start(f32[128,512]{1,0:T(8,128)S(1)} %project.2.gate_ref), channel_id=1, source_target_pairs={{0,1},{1,0},{2,3},{3,2},{4,5},{5,4},{6,7},{7,6},{8,9},{9,8},{10,11... | collective-permute-start | bytes 786440 | tf_op jit(solution)/shard_map/ppermute | solution.py:115
  21.9 1.7 %collective-permute-start.8 = (f32[128,512]{1,0:T(8,128)S(1)}, f32[128,512]{1,0:T(8,128)S(1)}, u32[]{:S(2)}, u32[]{:S(2)}) collective-permute-start(f32[128,512]{1,0:T(8,128)S(1)} %project.3.up_ref), channel_id=1, source_target_pairs={{0,1},{1,0},{2,3},{3,2},{4,5},{5,4},{6,7},{7,6},{8,9},{9,8},{10,11... | collective-permute-start | bytes 786440 | tf_op jit(solution)/shard_map/ppermute | solution.py:115
  24.3 5.8 %collective-permute-start.11 = (bf16[16,4096]{1,0:T(8,128)(2,1)S(1)}, bf16[16,4096]{1,0:T(8,128)(2,1)S(1)}, u32[]{:S(2)}, u32[]{:S(2)}) collective-permute-start(bf16[16,4096]{1,0:T(8,128)(2,1)S(1)} %get-tuple-element.28), channel_id=1, source_target_pairs={{0,4},{2,6},{4,0},{6,2},{8,12},{10,14},{12,8},{14,10},{1,5},{3,7},... | collective-permute-start | bytes 393224 | tf_op jit(solution)/shard_map/ppermute | solution.py:112
  25.8 6.4 %collective-permute-start.12 = (bf16[16,4096]{1,0:T(8,128)(2,1)S(1)}, bf16[16,4096]{1,0:T(8,128)(2,1)S(1)}, u32[]{:S(2)}, u32[]{:S(2)}) collective-permute-start(bf16[16,4096]{1,0:T(8,128)(2,1)S(1)} %get-tuple-element.29), channel_id=1, source_target_pairs={{0,2},{2,0},{4,6},{6,4},{8,10},{10,8},{12,14},{14,12},{1,3},{3,1},... | collective-permute-start | bytes 393224 | tf_op jit(solution)/shard_map/ppermute | solution.py:112
  26.4 11.4 %collective-permute-start.10 = (bf16[16,4096]{1,0:T(8,128)(2,1)S(1)}, bf16[16,4096]{1,0:T(8,128)(2,1)S(1)}, u32[]{:S(2)}, u32[]{:S(2)}) collective-permute-start(bf16[16,4096]{1,0:T(8,128)(2,1)S(1)} %get-tuple-element.26), channel_id=1, source_target_pairs={{0,2},{2,0},{4,6},{6,4},{8,10},{10,8},{12,14},{14,12},{1,3},{3,1},... | collective-permute-start | bytes 393224 | tf_op jit(solution)/shard_map/ppermute | solution.py:112
  27.8 10.1 %collective-permute-start.9 = (bf16[16,4096]{1,0:T(8,128)(2,1)S(1)}, bf16[16,4096]{1,0:T(8,128)(2,1)S(1)}, u32[]{:S(2)}, u32[]{:S(2)}) collective-permute-start(bf16[16,4096]{1,0:T(8,128)(2,1)S(1)} %get-tuple-element.24), channel_id=1, source_target_pairs={{0,14},{2,12},{4,10},{6,8},{8,6},{10,4},{12,2},{14,0},{1,15},{3,13... | collective-permute-start | bytes 393224 | tf_op jit(solution)/shard_map/ppermute | solution.py:112
  32.2 9.6 %collective-permute-start.13 = (bf16[16,4096]{1,0:T(8,128)(2,1)S(1)}, bf16[16,4096]{1,0:T(8,128)(2,1)S(1)}, u32[]{:S(2)}, u32[]{:S(2)}) collective-permute-start(bf16[16,4096]{1,0:T(8,128)(2,1)S(1)} %add.4.refs_1_), channel_id=1, source_target_pairs={{0,8},{2,10},{4,12},{6,14},{8,0},{10,2},{12,4},{14,6},{1,9},{3,11}... | collective-permute-start | bytes 393224 | tf_op jit(solution)/shard_map/ppermute | solution.py:112
  35.3 6.4 %collective-permute-start.15 = (bf16[16,4096]{1,0:T(8,128)(2,1)S(1)}, bf16[16,4096]{1,0:T(8,128)(2,1)S(1)}, u32[]{:S(2)}, u32[]{:S(2)}) collective-permute-start(bf16[16,4096]{1,0:T(8,128)(2,1)S(1)} %get-tuple-element.32), channel_id=1, source_target_pairs={{0,2},{2,0},{4,6},{6,4},{8,10},{10,8},{12,14},{14,12},{1,3},{3,1},... | collective-permute-start | bytes 393224 | tf_op jit(solution)/shard_map/ppermute | solution.py:112
  37.8 5.3 %collective-permute-start.14 = (bf16[16,4096]{1,0:T(8,128)(2,1)S(1)}, bf16[16,4096]{1,0:T(8,128)(2,1)S(1)}, u32[]{:S(2)}, u32[]{:S(2)}) collective-permute-start(bf16[16,4096]{1,0:T(8,128)(2,1)S(1)} %add.5.refs_1_), channel_id=1, source_target_pairs={{0,4},{2,6},{4,0},{6,2},{8,12},{10,14},{12,8},{14,10},{1,5},{3,7},... | collective-permute-start | bytes 393224 | tf_op jit(solution)/shard_map/ppermute | solution.py:112
